TPU v7x, 32 devices: a whole 2x2x4 slice. The times are simulated.
32 devices in a mesh: node: 4 (over x, core), local: 8 (over z, y).
Axes of the slice: x: 2, y: 2, z: 4, core: 2. Of those that a mesh axis runs over, the one named last changes fastest.
Arguments:
- tokens: bfloat16 [2048, 4096], P('local'), may hold values from -6 to 6
- norm_gain: bfloat16 [4096], replicated, may hold values from 0.099609375 to 1.8984375
- w_quant: bfloat16 [3, 4096, 4096], P(None, 'local', 'node'), may hold values from -1 to 1
- w_scale: bfloat16 [3, 32, 4096], P(None, 'local', 'node'), as said below
- d_out: bfloat16 [2048, 4096], P('local', 'node'), may hold values from -4 to 4
Outputs:
- attn_out: bfloat16 [2048, 4096], P('local', 'node')
- d_tokens: bfloat16 [2048, 4096], P('local', 'node')
- weight_grads: float32 [3, 4096, 4096], P(None, 'local', 'node')
Inputs may be any that keep to these rules, and one draw needn't show every extreme that they name: `w_scale`: positive.
All inputs are finite; a program needn't handle non-finite values. Where the computation divides by a largest or mean magnitude, that divisor is 1e-20 or more.
Results may differ from a plain program's by a relative error of at most 0.017.
Values may be sent and summed in bfloat16 or wider, within the bound.
No kernel may reach another device: no remote copies, remote signals or barrier semaphores. Data moves between devices by JAX's collectives and lax.ppermute only.
A program may use at most 320 MiB of HBM per device.

v0:
```python
import math

import jax
import jax.numpy as jnp
from jax import lax
from jax.sharding import PartitionSpec as P

HEAD_DIM = 128


NORM_EPS = 1e-05
SCALE_EPS = 1e-06


def rope_tables(length, width):
    position = jnp.arange(length).astype(jnp.float32)[:, None]
    frequency = jnp.exp(
        jnp.arange(width // 2).astype(jnp.float32) * (-2.0 * math.log(10000.0) / width)
    )
    angle = position * frequency[None, :]
    return (jnp.cos(angle), jnp.sin(angle))


def rotate(tensor, cosine, sine):
    half = tensor.shape[-1] // 2
    first = tensor[..., :half]
    second = tensor[..., half:]
    cosine = cosine[:, None, :]
    sine = sine[:, None, :]
    return jnp.concatenate(
        [first * cosine - second * sine, second * cosine + first * sine], axis=-1
    )


def attend(query, key_rows, value):
    length = query.shape[0]
    scores = jnp.einsum(
        "shd,thd->hst", query, key_rows, preferred_element_type=jnp.float32
    ) / math.sqrt(query.shape[-1])
    causal = jnp.arange(length)[:, None] >= jnp.arange(length)[None, :]
    scores = jnp.where(causal[None], scores, jnp.float32(-1e30))
    probs = jax.nn.softmax(scores, axis=-1).astype(jnp.bfloat16)
    return jnp.einsum("hst,thd->shd", probs, value, preferred_element_type=jnp.float32).astype(
        jnp.bfloat16
    )


def normed(rows, gain):
    values = rows.astype(jnp.float32)
    inverse_rms = lax.rsqrt(jnp.mean(values * values, axis=-1, keepdims=True) + NORM_EPS)
    return ((values * inverse_rms * gain.astype(jnp.float32)).astype(jnp.bfloat16), inverse_rms)


def expand_blocks(quant, scale):
    widened = quant.astype(jnp.float32) * scale.astype(jnp.float32)[:, :, None, :]
    return widened.reshape(quant.shape[0], quant.shape[1] * quant.shape[2], quant.shape[3])


def quantize(grad, block):
    blocks = grad.reshape(grad.shape[0], grad.shape[1] // block, block, grad.shape[2])
    scale = (jnp.max(jnp.abs(blocks), axis=2) + SCALE_EPS).astype(jnp.bfloat16)
    quant = (blocks / scale.astype(jnp.float32)[:, :, None, :]).astype(jnp.bfloat16)
    return (quant, scale)


def back_term(pre, weights):
    total = jnp.einsum("sc,rc->sr", pre[0], weights[0], preferred_element_type=jnp.float32)
    total = total + jnp.einsum("sc,rc->sr", pre[1], weights[1], preferred_element_type=jnp.float32)
    return total + jnp.einsum("sc,rc->sr", pre[2], weights[2], preferred_element_type=jnp.float32)


def local(tokens, norm_gain, w_quant, w_scale, d_out):
    length = tokens.shape[0]
    width = tokens.shape[1]
    columns = w_quant.shape[2]
    heads_here = columns // HEAD_DIM
    block = w_quant.shape[1] // w_scale.shape[1]
    normed_rows, inverse_rms = normed(tokens, norm_gain)
    cosine, sine = rope_tables(length, HEAD_DIM)
    quant_blocks = w_quant.reshape(3, w_scale.shape[1], block, columns)
    gathered_quant, gathered_scale = (
        lax.all_gather(quant_blocks, "local", axis=1, tiled=True),
        lax.all_gather(w_scale, "local", axis=1, tiled=True),
    )
    weights = expand_blocks(gathered_quant, gathered_scale).astype(jnp.bfloat16)
    proj = [
        jnp.dot(normed_rows, weights[which], preferred_element_type=jnp.float32)
        for which in range(3)
    ]
    query = rotate(proj[0].reshape(length, heads_here, HEAD_DIM), cosine, sine).astype(jnp.bfloat16)
    key_rows = rotate(proj[1].reshape(length, heads_here, HEAD_DIM), cosine, sine).astype(
        jnp.bfloat16
    )
    value = proj[2].reshape(length, heads_here, HEAD_DIM).astype(jnp.bfloat16)
    output, pull = jax.vjp(attend, query, key_rows, value)
    d_query, d_key, d_value = pull(d_out.reshape(length, heads_here, HEAD_DIM))
    pre_query = (
        rotate(d_query.astype(jnp.float32), cosine, -sine)
        .astype(jnp.bfloat16)
        .reshape(length, columns)
    )
    pre_key = (
        rotate(d_key.astype(jnp.float32), cosine, -sine)
        .astype(jnp.bfloat16)
        .reshape(length, columns)
    )
    pre = [pre_query, pre_key, d_value.reshape(length, columns)]
    pre_stack = jnp.stack(pre)
    partial_value = jnp.einsum(
        "sr,msc->mrc", normed_rows, pre_stack, preferred_element_type=jnp.float32
    )
    quant, scale = quantize(partial_value, block)
    received_quant, received_scale = (
        lax.all_to_all(quant, "local", split_axis=1, concat_axis=0, tiled=True),
        lax.all_to_all(scale, "local", split_axis=1, concat_axis=0, tiled=True),
    )
    senders = received_quant.shape[0] // 3
    widened = expand_blocks(received_quant, received_scale).astype(jnp.bfloat16)
    widened = lax.optimization_barrier(widened).astype(jnp.float32)
    weight_grads = jnp.sum(widened.reshape(senders, 3, widened.shape[1], columns), axis=0)
    term = back_term(pre, weights)
    share = width // lax.axis_size("node")
    offset = lax.axis_index("node") * share
    values = tokens.astype(jnp.float32)
    gains = norm_gain.astype(jnp.float32)
    values_part = lax.dynamic_slice_in_dim(values, offset, share, 1)
    gains_part = lax.dynamic_slice_in_dim(gains, offset, share, 0)
    upstream_norm = lax.psum(term.astype(jnp.bfloat16), "node").astype(jnp.float32)
    dots = jnp.sum(gains * upstream_norm * values, axis=-1, keepdims=True)
    upstream_part = lax.dynamic_slice_in_dim(upstream_norm, offset, share, 1)
    d_tokens = (
        inverse_rms * gains_part * upstream_part - values_part * inverse_rms**3 * dots / width
    )
    return (output.reshape(length, columns), d_tokens.astype(jnp.bfloat16), weight_grads)


def solution(mesh):
    placed = (
        P("local", None),
        P(),
        P(None, "local", "node"),
        P(None, "local", "node"),
        P("local", "node"),
    )
    return jax.shard_map(
        local,
        mesh=mesh,
        in_specs=placed,
        out_specs=(P("local", "node"), P("local", "node"), P(None, "local", "node")),
        check_vma=False,
    )
```

profile of v0, /device:TPU:2, one launch (start us, length us, event | category | flops | bytes accessed | tf_op | source)
XLA Modules:
  0.0 1398.6 jit_solution(2126882063957072433)
XLA Ops:
  7.2 0.0 all-gather.2.cloned.1.call-start
  7.2 0.7 all-gather.2.cloned.1.call-update
  7.9 0.7 convert_element_type.250
  8.6 0.8 copy.70
  9.4 2.0 copy.102
  11.4 69.0 %all_gather.7 = bf16[3,32,1024]{2,0,1:T(4,128)(2,1)S(1)} all-gather(bf16[3,4,1024]{2,0,1:T(4,128)(2,1)S(1)} %copy.70), channel_id=1, replica_groups=mesh['node'=4,'local'=8] {'local'}, dimensions={1}, use_global_device_ids=true | all-gather | bytes 221184 | tf_op jit(solution)/shard_map/all_gather | solution.py:83
  80.4 0.7 iota_compare_fusion
  81.1 0.5 multiply_reduce_fusion.1
  81.6 0.6 multiply_multiply_fusion
  82.2 1.0 fusion.27
  83.2 0.8 copy_convert_fusion.1
  84.0 411.5 %all-gather.2.cloned.1.call-done = bf16[3,32,128,1024]{3,2,1,0:T(8,128)(2,1)} async-done(((bf16[3,4,128,1024]{3,2,1,0:T(8,128)(2,1)}), bf16[3,32,128,1024]{3,2,1,0:T(8,128)(2,1)}) %all-gather.2.cloned.1.call-update) | async-done | bytes 25165840 | tf_op jit(solution)/shard_map/all_gather | solution.py:82
  495.5 14.9 %multiply_convert_fusion = bf16[3,32,128,1024]{3,2,1,0:T(8,128)(2,1)S(1)} fusion(bf16[3,32,128,1024]{3,2,1,0:T(8,128)(2,1)} %all-gather.2.cloned.1.call-done, f32[3,32,1024]{2,1,0:T(8,128)} %copy_convert_fusion.1), kind=kLoop, calls=%fused_computation.7 | loop fusion | flops 37748736 | bytes 50724864 | tf_op jit(solution)/shard_map/convert_element_type | solution.py:85
  510.4 8.7 fusion.44
  519.1 11.7 copy.101
  530.9 11.3 copy.100
  542.2 6.0 fusion.39
  548.2 0.0 copy-start.12
  548.2 2.4 fusion.41
  550.6 0.3 subtract_convert_fusion.2
  551.0 2.2 fusion.45
  553.2 11.3 copy.99
  564.5 5.0 convolution_convert_fusion.1
  569.6 0.0 copy-start.8
  569.6 1.3 convolution_convert_fusion.2
  570.9 0.4 fusion.10
  571.4 0.7 fusion.22
  572.1 0.7 fusion.20
  572.8 0.1 copy-done.10
  572.9 0.3 multiply_subtract_fusion
  573.3 0.1 maximum_convert_fusion
  573.4 0.0 copy-start.3
  573.4 20.7 %fusion.13 = f32[3,1024,4096]{2,1,0:T(8,128)} fusion(bf16[1,256,1024]{1,2,0:T(8,128)(2,1)} %bitcast.113, bf16[1,256,1024]{1,2,0:T(8,128)(2,1)S(1)} %bitcast.105, bf16[1,256,1024]{1,2,0:T(8,128)(2,1)S(1)} %bitcast.107, bf16[256,4096]{1,0:T(8,128)(2,1)S(1)} %copy-done, f32[4096]{0:T(1024)S(1)} %convert_element_type.250, f32[256]{0:T(256)S(1)} %get-tuple-element.37), kind=kOutput, calls=%fused_computation.29 | convolution fusion | flops 6448218112 | bytes 54019072 | tf_op jit(solution)/shard_map/sr,msc->mrc/dot_general | solution.py:109
  594.1 40.9 %copy.103 = f32[384,8,32,128]{3,2,1,0:T(8,128)} copy(f32[384,8,32,128]{3,1,2,0:T(8,128)} %bitcast.90) | data formatting | bytes 100663296
  635.0 18.0 %abs_reduce_fusion = f32[3,32,1024]{1,2,0:T(8,128)} fusion(f32[3,32,128,1024]{2,1,3,0:T(8,128)} %bitcast.87), kind=kLoop, calls=%fused_computation.6 | loop fusion | flops 25067520 | bytes 50724864 | tf_op jit(solution)/shard_map/reduce_max | solution.py:61
  653.1 49.6 %copy.85 = f32[3,32,128,1024]{3,2,0,1:T(8,128)} copy(f32[3,32,128,1024]{2,1,3,0:T(8,128)} %bitcast.88) | data formatting | bytes 100663296 | tf_op jit(solution)/shard_map/reshape | solution.py:60
  702.7 1.8 copy.83
  704.6 0.9 copy.88
  705.4 0.2 copy.84
  705.6 4.5 all-to-all-start.1
  710.1 25.2 %divide_convert_fusion = bf16[3,32,128,1024]{3,2,0,1:T(8,128)(2,1)} fusion(f32[3,32,128,1024]{3,2,0,1:T(8,128)} %copy.85, f32[3,32,1024]{2,0,1:T(4,128)S(1)} %copy.84), kind=kLoop, calls=%fused_computation.5 | loop fusion | flops 25165824 | bytes 75890688 | tf_op jit(solution)/shard_map/convert_element_type | solution.py:62
  735.3 0.0 all-to-all-done.1
  735.3 6.6 all-to-all-start
  741.9 0.3 all-reduce.2.cloned.1.call-start
  742.2 0.0 slice-start
  742.2 5.9 fusion.46
  748.2 6.1 convolution_add_fusion.1
  754.3 3.8 fusion.2
  758.1 0.0 all-reduce.2.cloned.1.call-update
  758.1 2.5 convert_element_type.249
  760.6 1.9 convolution_convert_fusion.5
  762.6 1.0 copy.91
  763.6 0.1 copy_convert_fusion
  763.7 0.1 reshape.236
  763.9 46.0 %all-reduce.2.cloned.1.call-done = bf16[256,4096]{1,0:T(8,128)(2,1)} async-done(((bf16[256,4096]{1,0:T(8,128)(2,1)}), bf16[256,4096]{1,0:T(8,128)(2,1)}) %all-reduce.2.cloned.1.call-update) | async-done | bytes 2097168 | tf_op jit(solution)/shard_map/psum | solution.py:128
  809.8 2.2 convert_element_type.276
  812.1 0.8 multiply_reduce_fusion
  812.9 2.3 subtract_convert_fusion
  815.2 469.6 %all-to-all-done = bf16[3,32,128,1024]{3,2,0,1:T(8,128)(2,1)} async-done(((bf16[3,32,128,1024]{3,2,0,1:T(8,128)(2,1)}), bf16[3,32,128,1024]{3,2,0,1:T(8,128)(2,1)}, u32[]{:S(2)}, u32[]{:S(2)}) %all-to-all-start) | async-done | bytes 25165856 | tf_op jit(solution)/shard_map/all_to_all | solution.py:114
  1284.8 12.0 copy.86
  1296.8 16.4 %convert_bitcast_fusion = f32[8,3,4,128,1024]{4,3,2,0,1:T(8,128)} fusion(bf16[3,8,4,128,1024]{4,3,2,1,0:T(8,128)(2,1)S(1)} %bitcast.91), kind=kLoop, calls=%fused_computation.2 | loop fusion | flops 12582912 | bytes 75497472 | tf_op jit(solution)/shard_map/convert_element_type | solution.py:55
  1313.2 34.9 %copy.87 = f32[8,3,4,128,1024]{4,3,2,1,0:T(8,128)} copy(f32[8,3,4,128,1024]{4,3,2,0,1:T(8,128)} %convert_bitcast_fusion) | data formatting | bytes 100663296 | tf_op jit(solution)/shard_map/convert_element_type | solution.py:55
  1348.0 27.4 %fusion.1 = bf16[24,512,1024]{2,1,0:T(8,128)(2,1)} fusion(f32[24,512,1024]{2,1,0:T(8,128)} %bitcast.89, f32[24,4,1024]{2,1,0:T(4,128)S(1)} %bitcast.111), kind=kLoop, calls=%fused_computation.4 | loop fusion | flops 25165824 | bytes 75890688 | tf_op jit(solution)/shard_map/convert_element_type | solution.py:118
  1375.4 16.4 %convert_reduce_fusion = f32[3,512,1024]{2,1,0:T(8,128)} fusion(bf16[8,3,512,1024]{3,2,1,0:T(8,128)(2,1)} %bitcast.92), kind=kLoop, calls=%fused_computation.1 | loop fusion | flops 23592960 | bytes 31457280 | tf_op jit(solution)/shard_map/reduce_sum | solution.py:120
  (37 shorter events, 0.1 us)
Async XLA Ops:
  7.2 73.9 %copy-start = (bf16[256,4096]{1,0:T(8,128)(2,1)S(1)}, bf16[256,4096]{1,0:T(8,128)(2,1)}, u32[]{:S(2)}) copy-start(bf16[256,4096]{1,0:T(8,128)(2,1)} %param.5) | copy-start | bytes 6291460
  7.2 488.3 %all-gather.2.cloned.1.call-start = ((), (), s32[]{:S(2)}) async-start(), calls=%async_computation.2 | async-start | bytes 28311552 | tf_op jit(solution)/shard_map/all_gather | solution.py:82
  542.2 6.0 copy-start.2
  548.2 2.5 copy-start.11
  548.2 2.8 copy-start.12
  564.5 5.1 copy-start.5
  564.5 5.1 copy-start.6
  569.6 1.8 copy-start.8
  572.1 0.8 copy-start.10
  573.4 20.7 %copy-start.3 = (bf16[256,8,128]{0,2,1:T(8,128)(2,1)}, bf16[256,8,128]{0,2,1:T(8,128)(2,1)S(1)}, u32[]{:S(2)}) copy-start(bf16[256,8,128]{0,2,1:T(8,128)(2,1)S(1)} %get-tuple-element.42) | copy-start | bytes 1572868
  705.6 29.7 %all-to-all-start.1 = ((bf16[3,32,1024]{2,0,1:T(4,128)(2,1)}), bf16[3,32,1024]{2,0,1:T(4,128)(2,1)S(1)}, u32[]{:S(2)}, u32[]{:S(2)}) async-start(bf16[3,32,1024]{2,0,1:T(4,128)(2,1)} %copy.88), calls=%async_computation.1 | async-start | bytes 524288 | tf_op jit(solution)/shard_map/all_to_all | solution.py:115
  735.3 6.9 copy-start.4
  735.3 549.4 %all-to-all-start = ((bf16[3,32,128,1024]{3,2,0,1:T(8,128)(2,1)}), bf16[3,32,128,1024]{3,2,0,1:T(8,128)(2,1)}, u32[]{:S(2)}, u32[]{:S(2)}) async-start(bf16[3,32,128,1024]{3,2,0,1:T(8,128)(2,1)} %divide_convert_fusion), calls=%async_computation | async-start | bytes 50331648 | tf_op jit(solution)/shard_map/all_to_all | solution.py:114
  741.9 67.9 %all-reduce.2.cloned.1.call-start = ((), (), s32[]{:S(2)}) async-start(), calls=%async_computation.3 | async-start | bytes 4194304 | tf_op jit(solution)/shard_map/psum | solution.py:128
  742.2 12.0 slice-start
  748.2 6.1 slice-start.1
  748.2 6.1 copy-start.7
  758.1 2.5 copy-start.13
  758.1 2.5 copy-start.9
  763.8 49.0 %copy-start.14 = (f32[256]{0:T(256)S(1)}, f32[256]{0:T(256)}, u32[]{:S(2)}) copy-start(f32[256]{0:T(256)} %get-tuple-element.36) | copy-start | bytes 3076
  809.8 2.2 copy-start.1
Sparse Core Ops, SparseCore 0:
  9.5 485.9 all-gather.1
  758.2 51.5 all-reduce.1
where the time goes:
time: 1400 us
  waiting for transfers between devices  928 us (66%)
  local copies, waits for them, and re-layouts  188 us (13%)
  other arithmetic  131 us (9%)
  blocking collectives  69 us (5%)
  matrix products  57.3 us (4%)
  between operations  14.4 us (1%)
    all_to_all x1, waiting for transfers between devices, local(): lax.all_to_all(quant, 'local', split_axis=1, concat_axis=0, tiled=True)  470 us
    all_gather x1, waiting for transfers between devices, local(): lax.all_gather(quant_blocks, 'local', axis=1, tiled=True)  412 us
    all_gather x1, blocking collectives, local(): lax.all_gather(w_scale, 'local', axis=1, tiled=True)  69 us
    reshape x1, local copies, waits for them, and re-layouts, quantize(): grad.reshape(grad.shape[0], grad.shape[1] // block, block, grad.shape[2])  49.6 us
    psum x1, waiting for transfers between devices, local(): lax.psum(term.astype(jnp.bfloat16), 'node').astype(jnp.float32)  46 us
    unnamed x37, local copies, waits for them, and re-layouts  42.9 us
    convert_element_type x1, local copies, waits for them, and re-layouts, expand_blocks(): quant.astype(jnp.float32) * scale.astype(jnp.float32)[:, :, None, :]  34.9 us
    squeeze x3, local copies, waits for them, and re-layouts, local(): weights[which]  34.4 us
  transfers between devices with their start and end apart: 4, of which 3 were waited for; matrix products, arithmetic and copies ran while one was open for 4% of the time, Pallas kernels for 0%

commit v1 on v0

v1 whole, which is shorter than its diff:
```python
import functools
import math

import jax
import jax.numpy as jnp
from jax import lax
from jax.experimental import pallas as pl
from jax.experimental.pallas import tpu as pltpu
from jax.sharding import PartitionSpec as P

HEAD_DIM = 128
NORM_EPS = 1e-05
CHUNKS = 2
VMEM = 40 * 1024 * 1024


def params(*semantics):
    return pltpu.CompilerParams(dimension_semantics=semantics, vmem_limit_bytes=VMEM)


def cost(flops, moved):
    return pl.CostEstimate(flops=flops, bytes_accessed=moved, transcendentals=0)


def mm(a, b):
    return jnp.dot(a, b, preferred_element_type=jnp.float32)


def mm_nt(a, b):
    return lax.dot_general(a, b, (((1,), (1,)), ((), ())), preferred_element_type=jnp.float32)


def mm_tn(a, b):
    return lax.dot_general(a, b, (((0,), (0,)), ((), ())), preferred_element_type=jnp.float32)


def rope_tables(length, width):
    position = jnp.arange(length).astype(jnp.float32)[:, None]
    frequency = jnp.exp(
        jnp.arange(width // 2).astype(jnp.float32) * (-2.0 * math.log(10000.0) / width)
    )
    angle = position * frequency[None, :]
    cosine, sine = jnp.cos(angle), jnp.sin(angle)
    return (
        jnp.concatenate([cosine, cosine], axis=-1),
        jnp.concatenate([-sine, sine], axis=-1),
    )


def ring_order(size):
    return [*range(0, size, 2), *reversed(range(1, size, 2))]


def sum_first_kernel(idx, rows, weight, right, left):
    half = right.shape[1]
    product = mm(rows[0], weight[0])
    right[0] = product[:half].astype(jnp.bfloat16)
    left[0] = product[half:].astype(jnp.bfloat16)


def sum_step_kernel(idx, rows_r, rows_l, weight, from_left, from_right, right, left):
    length, part = right.shape[1], from_left.shape[1]
    product = mm(rows_r[0], weight[0])
    right[0, :part] = (product[:part] + from_left[0].astype(jnp.float32)).astype(jnp.bfloat16)
    if part < length:
        right[0, part:] = product[part:].astype(jnp.bfloat16)
    product = mm(rows_l[0], weight[0])
    rest = length - part
    left[0, rest:] = (product[rest:] + from_right[0].astype(jnp.float32)).astype(jnp.bfloat16)
    if rest:
        left[0, :rest] = product[:rest].astype(jnp.bfloat16)


def sum_first(seq, rows, weights, chunk, wide):
    _, length, depth = rows.shape
    half = length // 2
    part = jax.ShapeDtypeStruct((3, half, wide), jnp.bfloat16)
    return pl.pallas_call(
        sum_first_kernel,
        grid_spec=pltpu.PrefetchScalarGridSpec(
            num_scalar_prefetch=1,
            grid=(3,),
            in_specs=[
                pl.BlockSpec((1, length, depth), lambda m, idx: (idx[0], 0, 0)),
                pl.BlockSpec((1, depth, wide), lambda m, idx: (m, 0, chunk)),
            ],
            out_specs=[pl.BlockSpec((1, half, wide), lambda m, idx: (m, 0, 0))] * 2,
        ),
        out_shape=[part, part],
        compiler_params=params("arbitrary"),
        cost_estimate=cost(6 * length * depth * wide, 8 * depth * wide),
        name="sum_first",
    )(seq, rows, weights)


def sum_step(seqs, rows, weights, from_left, from_right, chunk, wide):
    _, length, depth = rows.shape
    whole = jax.ShapeDtypeStruct((3, length, wide), jnp.bfloat16)
    part = from_left.shape[1]
    return pl.pallas_call(
        sum_step_kernel,
        grid_spec=pltpu.PrefetchScalarGridSpec(
            num_scalar_prefetch=1,
            grid=(3,),
            in_specs=[
                pl.BlockSpec((1, length, depth), lambda m, idx: (idx[0], 0, 0)),
                pl.BlockSpec((1, length, depth), lambda m, idx: (idx[1], 0, 0)),
                pl.BlockSpec((1, depth, wide), lambda m, idx: (m, 0, chunk)),
                pl.BlockSpec((1, part, wide), lambda m, idx: (m, 0, 0)),
                pl.BlockSpec((1, part, wide), lambda m, idx: (m, 0, 0)),
            ],
            out_specs=[pl.BlockSpec((1, length, wide), lambda m, idx: (m, 0, 0))] * 2,
        ),
        out_shape=[whole, whole],
        compiler_params=params("arbitrary"),
        cost_estimate=cost(12 * length * depth * wide, 12 * depth * wide),
        name="sum_step",
    )(seqs, rows, rows, weights, from_left, from_right)


def attention_kernel(
    idx, rows, weight, from_left, from_right, d_out, cosine, sine, output, pre, dots
):
    length = rows.shape[1]
    proj = [
        mm(rows[0], weight[m])
        + (from_left[m].astype(jnp.float32) + from_right[m].astype(jnp.float32))
        for m in range(3)
    ]
    cos, sin = cosine[...], sine[...]
    half = HEAD_DIM // 2

    def rotate(tensor, angle):
        return tensor * cos + pltpu.roll(tensor, half, 1) * angle

    query = rotate(proj[0], sin).astype(jnp.bfloat16)
    key_rows = rotate(proj[1], sin).astype(jnp.bfloat16)
    value = proj[2].astype(jnp.bfloat16)
    scores = mm_nt(query, key_rows) * (1.0 / math.sqrt(HEAD_DIM))
    causal = lax.broadcasted_iota(jnp.int32, (length, length), 0) >= lax.broadcasted_iota(
        jnp.int32, (length, length), 1
    )
    scores = jnp.where(causal, scores, jnp.float32(-1e30))
    powers = jnp.exp(scores - jnp.max(scores, axis=-1, keepdims=True))
    probs = powers * (1.0 / jnp.sum(powers, axis=-1, keepdims=True))
    probs_low = probs.astype(jnp.bfloat16)
    output[...] = mm(probs_low, value).astype(jnp.bfloat16)
    cotangent = d_out[...]
    d_value = mm_tn(probs_low, cotangent).astype(jnp.bfloat16)
    d_probs = mm_nt(cotangent, value).astype(jnp.bfloat16).astype(jnp.float32)
    inner = jnp.sum(d_probs * probs, axis=-1, keepdims=True)
    d_scores = (probs * (d_probs - inner) * (1.0 / math.sqrt(HEAD_DIM))).astype(jnp.bfloat16)
    d_query = mm(d_scores, key_rows).astype(jnp.bfloat16).astype(jnp.float32)
    d_key = mm_tn(d_scores, query).astype(jnp.bfloat16).astype(jnp.float32)
    pre_query = rotate(d_query, -sin).astype(jnp.bfloat16)
    pre_key = rotate(d_key, -sin).astype(jnp.bfloat16)
    pre[0] = pre_query
    pre[1] = pre_key
    pre[2] = d_value
    product = (
        pre_query.astype(jnp.float32) * proj[0]
        + pre_key.astype(jnp.float32) * proj[1]
        + d_value.astype(jnp.float32) * proj[2]
    )

    @pl.when(pl.program_id(0) == 0)
    def _():
        dots[...] = product

    @pl.when(pl.program_id(0) > 0)
    def _():
        dots[...] += product


def attention(seq, rows, weights, from_left, from_right, d_out, tables, chunk, wide):
    _, length, depth = rows.shape
    heads = wide // HEAD_DIM
    first = chunk * heads
    table = pl.BlockSpec((length, HEAD_DIM), lambda h, idx: (0, 0))
    stack = pl.BlockSpec((3, length, HEAD_DIM), lambda h, idx: (0, 0, h))
    return pl.pallas_call(
        attention_kernel,
        grid_spec=pltpu.PrefetchScalarGridSpec(
            num_scalar_prefetch=1,
            grid=(heads,),
            in_specs=[
                pl.BlockSpec((1, length, depth), lambda h, idx: (idx[0], 0, 0)),
                pl.BlockSpec((3, depth, HEAD_DIM), lambda h, idx: (0, 0, first + h)),
                stack,
                stack,
                pl.BlockSpec((length, HEAD_DIM), lambda h, idx: (0, first + h)),
                table,
                table,
            ],
            out_specs=[
                pl.BlockSpec((length, HEAD_DIM), lambda h, idx: (0, h)),
                stack,
                table,
            ],
        ),
        out_shape=[
            jax.ShapeDtypeStruct((length, wide), jnp.bfloat16),
            jax.ShapeDtypeStruct((3, length, wide), jnp.bfloat16),
            jax.ShapeDtypeStruct((length, HEAD_DIM), jnp.float32),
        ],
        compiler_params=params("arbitrary"),
        cost_estimate=cost(6 * length * depth * wide, 12 * depth * wide),
        name="attention",
    )(seq, rows, weights, from_left, from_right, d_out, *tables)


def grads_kernel(count, idx, rows_t, *refs):
    pieces, far, out = refs[: count - 1], refs[count - 1 : count + 1], refs[-1]
    total = mm(rows_t[idx[0]], pieces[0][0])
    for place in range(1, count - 1):
        total += mm(rows_t[idx[place]], pieces[place][0])
    half = far[0].shape[1]
    last = rows_t[idx[count - 1]]
    total += mm(last[:, :half], far[0][0])
    total += mm(last[:, half:], far[1][0])
    out[0] = total


def grads_chunk(seqs, rows_t, pieces, far, before, chunk, wide, columns):
    size, depth, length = rows_t.shape
    block = pl.BlockSpec((1, length, wide), lambda m, idx: (m, 0, 0))
    half = pl.BlockSpec((1, length // 2, wide), lambda m, idx: (m, 0, 0))
    in_specs = [
        pl.BlockSpec((size, depth, length), lambda m, idx: (0, 0, 0)),
        *[block] * (size - 1),
        half,
        half,
    ]
    operands = [seqs, rows_t, *pieces, *far]
    aliases = {}
    if before is not None:
        aliases = {len(operands): 0}
        operands.append(before)
        in_specs.append(pl.BlockSpec(memory_space=pl.ANY))
    return pl.pallas_call(
        functools.partial(grads_kernel, size),
        grid_spec=pltpu.PrefetchScalarGridSpec(
            num_scalar_prefetch=1,
            grid=(3,),
            in_specs=in_specs,
            out_specs=pl.BlockSpec((1, depth, wide), lambda m, idx: (m, 0, chunk)),
        ),
        out_shape=jax.ShapeDtypeStruct((3, depth, columns), jnp.float32),
        input_output_aliases=aliases,
        compiler_params=params("arbitrary"),
        cost_estimate=cost(6 * size * length * depth * wide, 12 * size * length * wide),
        name="grads",
    )(*operands)


def term_kernel(count, has_before, idx, weight, *refs):
    pieces, far = refs[: count - 1], refs[count - 1 : count + 1]
    before, out = refs[count + 1] if has_before else None, refs[-1]

    def back(piece):
        total = mm_nt(piece[0], weight[0])
        for m in range(1, 3):
            total += mm_nt(piece[m], weight[m])
        return total

    def put(place, low, high, total):
        if has_before:
            total += before[place, low:high]
        out[place, low:high] = total.astype(out.dtype)

    length = pieces[0].shape[1]
    for index in range(count - 1):
        put(idx[index], 0, length, back(pieces[index]))
    put(idx[count - 1], 0, length // 2, back(far[0]))
    put(idx[count - 1], length // 2, length, back(far[1]))


def term_chunk(seqs, weights, pieces, far, before, kind, chunk, wide):
    size = len(pieces) + 1
    length = pieces[0].shape[1]
    depth = weights.shape[1]
    block = pl.BlockSpec((3, length, wide), lambda i, idx: (0, 0, 0))
    half = pl.BlockSpec((3, length // 2, wide), lambda i, idx: (0, 0, 0))
    result = pl.BlockSpec((size, length, depth), lambda i, idx: (0, 0, 0))
    in_specs = [
        pl.BlockSpec((3, depth, wide), lambda i, idx: (0, 0, chunk)),
        *[block] * (size - 1),
        half,
        half,
    ]
    operands = [seqs, weights, *pieces, *far]
    if before is not None:
        operands.append(before)
        in_specs.append(result)
    return pl.pallas_call(
        functools.partial(term_kernel, size, before is not None),
        grid_spec=pltpu.PrefetchScalarGridSpec(
            num_scalar_prefetch=1, grid=(1,), in_specs=in_specs, out_specs=result
        ),
        out_shape=jax.ShapeDtypeStruct((size, length, depth), kind),
        compiler_params=params("arbitrary"),
        cost_estimate=cost(6 * size * length * depth * wide, 12 * size * length * wide),
        name="term",
    )(*operands)


def local(tokens, norm_gain, w_quant, w_scale, d_out):
    length, width = tokens.shape
    depth, columns = w_quant.shape[1:]
    size, nodes = lax.axis_size("local"), lax.axis_size("node")
    here, node = lax.axis_index("local"), lax.axis_index("node")
    wide = columns // CHUNKS
    far = size // 2

    order = ring_order(size)
    to_right = [(order[i], order[(i + 1) % size]) for i in range(size)]
    to_left = [(b, a) for a, b in to_right]
    table = jnp.array(order, jnp.int32)
    place = jnp.where(here % 2 == 0, here // 2, size - (here + 1) // 2)

    def sequence(distance):
        return table[(place + distance + size) % size]

    values = tokens.astype(jnp.float32)
    gains = norm_gain.astype(jnp.float32)
    inverse_rms = lax.rsqrt(jnp.mean(values * values, axis=-1, keepdims=True) + NORM_EPS)
    normed = (values * inverse_rms * gains).astype(jnp.bfloat16)
    core = node % 2
    pairs = [(n, n ^ 1) for n in range(nodes)]
    shares = normed.reshape(length, size, 2, depth // 2)
    mine = lax.dynamic_index_in_dim(shares, core, 2, keepdims=False).transpose(1, 0, 2)
    mine = lax.all_to_all(mine, "local", split_axis=0, concat_axis=0, tiled=True)
    other = lax.ppermute(mine, "node", pairs)
    rows = jnp.where(
        core == 0,
        jnp.concatenate([mine, other], axis=-1),
        jnp.concatenate([other, mine], axis=-1),
    )
    rows_t = rows.transpose(0, 2, 1)

    blocks = w_quant.reshape(3, w_scale.shape[1], -1, columns).astype(jnp.float32)
    weights = (blocks * w_scale.astype(jnp.float32)[:, :, None, :]).astype(jnp.bfloat16)
    weights = weights.reshape(3, depth, columns)

    tables = rope_tables(length, HEAD_DIM)
    arrived = []
    for chunk in range(CHUNKS):
        right, left = sum_first(sequence(far)[None], rows, weights, chunk, wide)
        for distance in range(far - 1, -1, -1):
            from_left = lax.ppermute(right, "local", to_right)
            from_right = lax.ppermute(left, "local", to_left)
            if distance:
                seqs = jnp.stack([sequence(distance), sequence(-distance)])
                right, left = sum_step(seqs, rows, weights, from_left, from_right, chunk, wide)
        arrived.append((from_left, from_right))

    outputs, pres, dots = [], [], 0.0
    for chunk in range(CHUNKS):
        output, pre, product = attention(
            here[None], rows, weights, *arrived[chunk], d_out, tables, chunk, wide
        )
        outputs.append(output)
        pres.append(pre)
        dots += jnp.sum(product, axis=-1, keepdims=True)
    dots = lax.psum(dots, "node")

    distances = [0]
    for step in range(1, far):
        distances += [-step, step]
    distances.append(far)
    seqs = jnp.stack([sequence(distance) for distance in distances])
    grads, term = None, None
    half = length // 2
    for chunk in range(CHUNKS):
        right = left = pres[chunk]
        pieces = [pres[chunk]]
        for step in range(1, far + 1):
            if step == far:
                right, left = right[:, :half], left[:, half:]
            right = lax.ppermute(right, "local", to_right)
            left = lax.ppermute(left, "local", to_left)
            if step < far:
                pieces += [right, left]
        kind = jnp.bfloat16 if chunk == CHUNKS - 1 else jnp.float32
        term = term_chunk(seqs, weights, pieces, (right, left), term, kind, chunk, wide)
        grads = grads_chunk(
            seqs, rows_t, pieces, (right, left), grads, chunk, wide, columns
        )

    group = size // nodes
    summed = lax.all_to_all(
        term.reshape(nodes, group, length, depth), "node", split_axis=0, concat_axis=0, tiled=True
    )
    summed = jnp.sum(summed.astype(jnp.float32), axis=0).astype(jnp.bfloat16)
    came = []
    for turn in range(group):
        block = lax.dynamic_index_in_dim(summed, (here + turn) % group, 0, keepdims=False)
        moves = [
            (n * size + s, (s // group) * size + n * group + (s + turn) % group)
            for n in range(nodes)
            for s in range(size)
        ]
        came.append(lax.ppermute(block, ("node", "local"), moves))
    came = jnp.stack(came)
    upstream = jnp.concatenate(
        [
            lax.dynamic_index_in_dim(came, (here + group - i) % group, 0, keepdims=False)
            for i in range(group)
        ],
        axis=-1,
    ).astype(jnp.float32)
    share = width // nodes
    values_part = lax.dynamic_slice_in_dim(tokens, node * share, share, 1).astype(jnp.float32)
    gains_part = lax.dynamic_slice_in_dim(gains, node * share, share, 0)
    d_tokens = (
        inverse_rms * gains_part * upstream - values_part * inverse_rms**2 * dots / width
    )
    return (jnp.concatenate(outputs, axis=-1), d_tokens.astype(jnp.bfloat16), grads)


def solution(mesh):
    placed = (
        P("local", None),
        P(),
        P(None, "local", "node"),
        P(None, "local", "node"),
        P("local", "node"),
    )
    return jax.shard_map(
        local,
        mesh=mesh,
        in_specs=placed,
        out_specs=(P("local", "node"), P("local", "node"), P(None, "local", "node")),
        check_vma=False,
    )
```

time: 1400 us -> 404 us (0.29)
  waiting for transfers between devices: 928 us -> 157 us
  local copies, waits for them, and re-layouts: 188 us -> 62.2 us
  other arithmetic: 131 us -> 26.2 us
  matrix products: 57.3 us -> 0 us
  Pallas kernels: 0 us -> 54.9 us
  starting transfers between devices: 11.4 us -> 44.2 us
    all_to_all x2 -> x1, waiting for transfers between devices: 470 us -> 0.01 us  [local(): lax.all_to_all(term.reshape(nodes, group, length, depth), 'node', split_a...]
    all_gather x1 -> x0, waiting for transfers between devices: 412 us -> none  [local(): lax.all_gather(quant_blocks, 'local', axis=1, tiled=True)]
    ppermute x0 -> x35, waiting for transfers between devices: none -> 157 us  [the longest x8 72.1 us: local(): left = lax.ppermute(left, 'local', to_left)]
    convert_element_type x11 -> x4, other arithmetic: 90.3 us -> 7.16 us  [the longest x1 4.5 us: local(): (blocks * w_scale.astype(jnp.float32)[:, :, None, :]).astype(jnp.bfloat16)]
    all_gather x1 -> x0, blocking collectives: 69 us -> none  [local(): lax.all_gather(w_scale, 'local', axis=1, tiled=True)]
    dot_general x12 -> x0, matrix products: 55 us -> none  [the longest x1 20.7 us: local(): jnp.einsum('sr,msc->mrc', normed_rows, pre_stack, preferred_element_type=...]
    pallas_call x0 -> x14, Pallas kernels: none -> 54.9 us  [the longest x2 13.3 us: grads_chunk(): pl.pallas_call(functools.partial(grads_kernel, size), grid_spec=pltpu.Pre...]
    reshape x2 -> x1, local copies, waits for them, and re-layouts: 51.7 us -> 3.29 us  [local(): shares = normed.reshape(length, size, 2, depth // 2)]
  transfers between devices with their start and end apart: 4 -> 36, of which waited for: 3 -> 24; matrix products, arithmetic and copies ran while one was open for 4% -> 6% of each run, Pallas kernels for 0% -> 12%
where the time goes in v1:
time: 404 us; the launch traced here: 402 us
  waiting for transfers between devices  157 us (39%)
  local copies, waits for them, and re-layouts  62.2 us (15%)
  blocking collectives  56.2 us (14%)
  Pallas kernels  54.9 us (14%)
  starting transfers between devices  44.2 us (11%)
  other arithmetic  26.2 us (6%)
    ppermute x8, waiting for transfers between devices, local(): left = lax.ppermute(left, 'local', to_left)  72.1 us
    ppermute x8, waiting for transfers between devices, local(): from_left = lax.ppermute(right, 'local', to_right)  69 us
    unnamed x123, local copies, waits for them, and re-layouts  42.4 us
    all_to_all x1, blocking collectives, local(): lax.all_to_all(mine, 'local', split_axis=0, concat_axis=0, tiled=True)  31.4 us
    psum x1, blocking collectives, local(): dots = lax.psum(dots, 'node')  24.8 us
    pallas_call x2, Pallas kernels, grads_chunk(): pl.pallas_call(functools.partial(grads_kernel, size), grid_spec=pltpu.Pre...  13.3 us
    pallas_call x2, Pallas kernels, attention(): pl.pallas_call(attention_kernel, grid_spec=pltpu.PrefetchScalarGridSpec(n...  13.1 us
    pallas_call x2, Pallas kernels, term_chunk(): pl.pallas_call(functools.partial(term_kernel, size, before is not None),...  13 us
  transfers between devices with their start and end apart: 36, of which 24 were waited for; matrix products, arithmetic and copies ran while one was open for 6% of the time, Pallas kernels for 12%

profile of v1, /device:TPU:2, one launch (start us, length us, event | category | flops | bytes accessed | tf_op | source)
XLA Modules:
  0.0 401.9 jit_solution(13583528734942676493)
XLA Ops:
  0.7 2.2 fusion.1
  4.2 1.9 fusion.3
  6.1 3.3 reshape.53
  9.4 3.5 constant_dynamic-slice_fusion
  12.9 4.5 %copy.27 = bf16[256,8,1,256]{0,3,1,2:T(8,128)(2,1)S(1)} copy(bf16[256,8,1,256]{3,2,1,0:T(2,128)(2,1)} %constant_dynamic-slice_fusion) | data formatting | bytes 2097152
  17.4 31.4 %all_to_all.10 = bf16[8,256,256]{1,2,0:T(8,128)(2,1)S(1)} all-to-all(bf16[8,256,256]{1,2,0:T(8,128)(2,1)S(1)} %bitcast.23), channel_id=1, replica_groups=mesh['node'=4,'local'=8] {'local'}, dimensions={0} | all-to-all | bytes 2097152 | tf_op jit(solution)/shard_map/all_to_all | solution.py:332
  48.9 4.5 %fusion.weight = bf16[3,512,1024]{2,1,0:T(8,128)(2,1)} fusion(bf16[3,512,1024]{2,1,0:T(8,128)(2,1)} %param.8, f32[3,4,1024]{2,1,0:T(4,128)S(1)} %convert_element_type.61), kind=kLoop, calls=%fused_computation.1 | loop fusion | flops 4718592 | bytes 6340608 | tf_op jit(solution)/shard_map/convert_element_type | solution.py:342
  54.1 1.8 maximum_select_fusion
  55.9 2.9 copy.18.rows.rows_r.rows_l
  58.8 1.9 copy-done
  60.7 1.7 sum_first.2
  62.4 1.2 collective-permute-start.1
  64.5 1.7 sum_first.3
  66.1 1.2 collective-permute-start.9
  68.2 1.4 pad_add_fusion.2.idx
  69.6 4.7 %collective-permute-done.1.from_left = bf16[3,128,512]{2,1,0:T(8,128)(2,1)S(1)} collective-permute-done((bf16[3,128,512]{2,1,0:T(8,128)(2,1)S(1)}, bf16[3,128,512]{2,1,0:T(8,128)(2,1)S(1)}, u32[]{:S(2)}, u32[]{:S(2)}) %collective-permute-start.1) | collective-permute-done | bytes 393248 | tf_op jit(solution)/shard_map/ppermute | solution.py:350
  75.5 2.0 sum_step.6
  78.1 1.5 collective-permute-start.4
  79.6 3.2 collective-permute-done.9.from_left
  82.8 1.1 collective-permute-done.10.from_right
  83.9 2.0 sum_step.9
  86.5 1.5 collective-permute-start.12
  88.0 1.3 pad_add_fusion.1.idx
  89.3 10.3 %collective-permute-done.3.from_left = bf16[3,256,512]{2,1,0:T(8,128)(2,1)S(1)} collective-permute-done((bf16[3,256,512]{2,1,0:T(8,128)(2,1)S(1)}, bf16[3,256,512]{2,1,0:T(8,128)(2,1)S(1)}, u32[]{:S(2)}, u32[]{:S(2)}) %collective-permute-start.3) | collective-permute-done | bytes 786464 | tf_op jit(solution)/shard_map/ppermute | solution.py:350
  100.8 2.0 sum_step.7
  103.4 1.5 collective-permute-start.6
  104.9 11.6 %collective-permute-done.11.from_left = bf16[3,256,512]{2,1,0:T(8,128)(2,1)S(1)} collective-permute-done((bf16[3,256,512]{2,1,0:T(8,128)(2,1)S(1)}, bf16[3,256,512]{2,1,0:T(8,128)(2,1)S(1)}, u32[]{:S(2)}, u32[]{:S(2)}) %collective-permute-start.11) | collective-permute-done | bytes 786464 | tf_op jit(solution)/shard_map/ppermute | solution.py:350
  117.6 2.0 sum_step.10
  120.2 1.5 collective-permute-start.14
  121.7 1.4 pad_add_fusion.idx
  123.1 10.2 %collective-permute-done.5.from_left = bf16[3,256,512]{2,1,0:T(8,128)(2,1)S(1)} collective-permute-done((bf16[3,256,512]{2,1,0:T(8,128)(2,1)S(1)}, bf16[3,256,512]{2,1,0:T(8,128)(2,1)S(1)}, u32[]{:S(2)}, u32[]{:S(2)}) %collective-permute-start.5) | collective-permute-done | bytes 786464 | tf_op jit(solution)/shard_map/ppermute | solution.py:350
  134.5 2.0 sum_step.8
  137.1 1.5 collective-permute-start.8
  138.6 11.6 %collective-permute-done.13.from_left = bf16[3,256,512]{2,1,0:T(8,128)(2,1)S(1)} collective-permute-done((bf16[3,256,512]{2,1,0:T(8,128)(2,1)S(1)}, bf16[3,256,512]{2,1,0:T(8,128)(2,1)S(1)}, u32[]{:S(2)}, u32[]{:S(2)}) %collective-permute-start.13) | collective-permute-done | bytes 786464 | tf_op jit(solution)/shard_map/ppermute | solution.py:350
  150.2 1.1 collective-permute-done.14.from_right
  151.3 2.0 sum_step.11
  153.9 1.5 collective-permute-start.16
  156.1 10.9 %collective-permute-done.7.from_left = bf16[3,256,512]{2,1,0:T(8,128)(2,1)S(1)} collective-permute-done((bf16[3,256,512]{2,1,0:T(8,128)(2,1)S(1)}, bf16[3,256,512]{2,1,0:T(8,128)(2,1)S(1)}, u32[]{:S(2)}, u32[]{:S(2)}) %collective-permute-start.7) | collective-permute-done | bytes 786464 | tf_op jit(solution)/shard_map/ppermute | solution.py:350
  167.0 1.1 collective-permute-done.8.from_right
  168.2 6.6 %attention.2 = (bf16[256,512]{1,0:T(8,128)(2,1)S(1)}, bf16[3,256,512]{2,1,0:T(8,128)(2,1)S(1)}, f32[256,128]{1,0:T(8,128)S(1)}) custom-call(s32[1]{0:T(128)} %bitcast.idx, bf16[8,256,512]{2,1,0:T(8,128)(2,1)S(1)} %copy.18.rows.rows_r.rows_l, bf16[3,512,1024]{2,1,0:T(8,128)(2,1)S(1)} %copy-done, bf16[3,256,512]{2,1,0:T(8,128)(2,1)S(1)} %collective-permute-done.7.from_left, ...), custom_call_target="tpu_custom_call" | custom-call | flops 402653184 | bytes 3145728 | tf_op jit(solution)/shard_map/attention/pallas_call | solution.py:181
  177.4 6.4 %collective-permute-done.15.from_left = bf16[3,256,512]{2,1,0:T(8,128)(2,1)S(1)} collective-permute-done((bf16[3,256,512]{2,1,0:T(8,128)(2,1)S(1)}, bf16[3,256,512]{2,1,0:T(8,128)(2,1)S(1)}, u32[]{:S(2)}, u32[]{:S(2)}) %collective-permute-start.15) | collective-permute-done | bytes 786464 | tf_op jit(solution)/shard_map/ppermute | solution.py:350
  183.9 1.1 collective-permute-done.16.from_right
  185.0 6.6 %attention.3 = (bf16[256,512]{1,0:T(8,128)(2,1)S(1)}, bf16[3,256,512]{2,1,0:T(8,128)(2,1)S(1)}, f32[256,128]{1,0:T(8,128)S(1)}) custom-call(s32[1]{0:T(128)} %bitcast.idx, bf16[8,256,512]{2,1,0:T(8,128)(2,1)S(1)} %copy.18.rows.rows_r.rows_l, bf16[3,512,1024]{2,1,0:T(8,128)(2,1)S(1)} %copy-done, bf16[3,256,512]{2,1,0:T(8,128)(2,1)S(1)} %collective-permute-done.15.from_left, ...), custom_call_target="tpu_custom_call" | custom-call | flops 402653184 | bytes 3145728 | tf_op jit(solution)/shard_map/attention/pallas_call | solution.py:181
  195.0 6.9 %collective-permute-done.26.refs_2_ = bf16[3,256,512]{2,1,0:T(8,128)(2,1)S(1)} collective-permute-done((bf16[3,256,512]{2,1,0:T(8,128)(2,1)S(1)}, bf16[3,256,512]{2,1,0:T(8,128)(2,1)S(1)}, u32[]{:S(2)}, u32[]{:S(2)}) %collective-permute-start.26) | collective-permute-done | bytes 786464 | tf_op jit(solution)/shard_map/ppermute | solution.py:381
  205.7 13.0 %collective-permute-done.18.refs_2_ = bf16[3,256,512]{2,1,0:T(8,128)(2,1)S(1)} collective-permute-done((bf16[3,256,512]{2,1,0:T(8,128)(2,1)S(1)}, bf16[3,256,512]{2,1,0:T(8,128)(2,1)S(1)}, u32[]{:S(2)}, u32[]{:S(2)}) %collective-permute-start.18) | collective-permute-done | bytes 786464 | tf_op jit(solution)/shard_map/ppermute | solution.py:381
  222.6 13.0 %collective-permute-done.28.refs_4_ = bf16[3,256,512]{2,1,0:T(8,128)(2,1)S(1)} collective-permute-done((bf16[3,256,512]{2,1,0:T(8,128)(2,1)S(1)}, bf16[3,256,512]{2,1,0:T(8,128)(2,1)S(1)}, u32[]{:S(2)}, u32[]{:S(2)}) %collective-permute-start.28) | collective-permute-done | bytes 786464 | tf_op jit(solution)/shard_map/ppermute | solution.py:381
  239.4 13.0 %collective-permute-done.20.refs_4_ = bf16[3,256,512]{2,1,0:T(8,128)(2,1)S(1)} collective-permute-done((bf16[3,256,512]{2,1,0:T(8,128)(2,1)S(1)}, bf16[3,256,512]{2,1,0:T(8,128)(2,1)S(1)}, u32[]{:S(2)}, u32[]{:S(2)}) %collective-permute-start.20) | collective-permute-done | bytes 786464 | tf_op jit(solution)/shard_map/ppermute | solution.py:381
  256.2 13.0 %collective-permute-done.30.refs_6_ = bf16[3,256,512]{2,1,0:T(8,128)(2,1)S(1)} collective-permute-done((bf16[3,256,512]{2,1,0:T(8,128)(2,1)S(1)}, bf16[3,256,512]{2,1,0:T(8,128)(2,1)S(1)}, u32[]{:S(2)}, u32[]{:S(2)}) %collective-permute-start.30) | collective-permute-done | bytes 786464 | tf_op jit(solution)/shard_map/ppermute | solution.py:381
  273.0 13.2 %collective-permute-done.22.refs_6_ = bf16[3,256,512]{2,1,0:T(8,128)(2,1)S(1)} collective-permute-done((bf16[3,256,512]{2,1,0:T(8,128)(2,1)S(1)}, bf16[3,256,512]{2,1,0:T(8,128)(2,1)S(1)}, u32[]{:S(2)}, u32[]{:S(2)}) %collective-permute-start.22) | collective-permute-done | bytes 786464 | tf_op jit(solution)/shard_map/ppermute | solution.py:381
  291.5 5.2 %stack.27.idx = s32[8]{0:T(128)S(1)} concatenate(s32[1]{0:T(128)} %get-tuple-element.56, s32[1]{0:T(128)} %get-tuple-element.61, s32[1]{0:T(128)} %get-tuple-element.62, s32[1]{0:T(128)} %get-tuple-element.59, s32[1]{0:T(128)} %get-tuple-element.60, s32[1]{0:T(128)} %get-tuple-element.57, s32[1]{0:T(128)} %get-tuple-element.58, s32[1]{0:T(128)} %get-tuple-element.63.idx), dimensions={0} | concatenate | bytes 64 | tf_op jit(solution)/shard_map/stack | solution.py:371
  296.8 1.2 copy-done.12
  304.8 6.1 %term.2.refs_9_ = f32[8,256,512]{2,1,0:T(8,128)S(1)} custom-call(s32[8]{0:T(128)S(1)} %stack.27.idx, bf16[3,512,1024]{2,1,0:T(8,128)(2,1)S(1)} %copy-done.1, bf16[3,256,512]{2,1,0:T(8,128)(2,1)S(1)} %copy-done.33, bf16[3,256,512]{2,1,0:T(8,128)(2,1)S(1)} %copy-done.39, bf16[3,256,512]{2,1,0:T(8,128)(2,1)S(1)} %copy-done.36, ...), custom_call_target="tpu_custom_call" | custom-call | flops 3221225472 | bytes 12582912 | tf_op jit(solution)/shard_map/term/pallas_call | solution.py:295
  310.9 2.0 copy-done.3
  313.0 6.9 %term.3 = bf16[8,256,512]{2,1,0:T(8,128)(2,1)S(1)} custom-call(s32[8]{0:T(128)S(1)} %stack.27.idx, bf16[3,512,1024]{2,1,0:T(8,128)(2,1)S(1)} %copy-done.1, bf16[3,256,512]{2,1,0:T(8,128)(2,1)S(1)} %copy-done.18, bf16[3,256,512]{2,1,0:T(8,128)(2,1)S(1)} %copy-done.24, bf16[3,256,512]{2,1,0:T(8,128)(2,1)S(1)} %copy-done.21, ...), custom_call_target="tpu_custom_call" | custom-call | flops 3221225472 | bytes 12582912 | tf_op jit(solution)/shard_map/term/pallas_call | solution.py:295
  319.9 1.3 copy-done.4
  321.3 5.2 %all-to-all-start.1 = ((bf16[4,2,256,512]{3,2,1,0:T(8,128)(2,1)}), bf16[4,2,256,512]{3,2,1,0:T(8,128)(2,1)}, u32[]{:S(2)}, u32[]{:S(2)}) async-start(bf16[4,2,256,512]{3,2,1,0:T(8,128)(2,1)} %bitcast.22), calls=%async_computation.1 | async-start | bytes 4194304 | tf_op jit(solution)/shard_map/all_to_all | solution.py:391
  329.1 24.8 %psum.7 = f32[256]{0:T(256)} all-reduce(f32[256]{0:T(256)} %add.263), channel_id=1, replica_groups=mesh['node'=4,'local'=8] {'node'}, use_global_device_ids=true, to_apply=%region_4.5 | all-reduce | flops 256 | bytes 2048 | tf_op jit(solution)/shard_map/psum | solution.py:365
  353.9 1.8 pad_maximum_fusion
  362.5 6.7 %grads.2.refs_9_ = f32[3,512,1024]{2,1,0:T(8,128)} custom-call(s32[8]{0:T(128)S(1)} %stack.27.idx, bf16[8,512,256]{2,1,0:T(8,128)(2,1)S(1)} %bitcast.20, bf16[3,256,512]{2,1,0:T(8,128)(2,1)S(1)} %copy-done.34, bf16[3,256,512]{2,1,0:T(8,128)(2,1)S(1)} %copy-done.40, bf16[3,256,512]{2,1,0:T(8,128)(2,1)S(1)} %copy-done.37, bf16[3,256,512]{2,1,0:T(8,128)(2,1)S(1)} %copy-done.46, ...), custom_call_target="tpu_custom_call" | custom-call | flops 3221225472 | bytes 12582912 | tf_op jit(solution)/shard_map/grads/pallas_call | solution.py:240
  369.1 2.9 reduce_sum.40
  374.2 5.0 %collective-permute-start.33 = (bf16[256,512]{1,0:T(8,128)(2,1)S(1)}, bf16[256,512]{1,0:T(8,128)(2,1)S(1)}, u32[]{:S(2)}, u32[]{:S(2)}) collective-permute-start(bf16[256,512]{1,0:T(8,128)(2,1)S(1)} %get-tuple-element.50), channel_id=1, source_target_pairs={{0,0},{1,1},{2,8},{3,9},{4,16},{5,17},{6,24},{7,25},{8,2},{9,3},{1... | collective-permute-start | bytes 786440 | tf_op jit(solution)/shard_map/ppermute | solution.py:403
  386.1 6.6 %grads.3 = f32[3,512,1024]{2,1,0:T(8,128)} custom-call(s32[8]{0:T(128)S(1)} %stack.27.idx, bf16[8,512,256]{2,1,0:T(8,128)(2,1)S(1)} %bitcast.21, bf16[3,256,512]{2,1,0:T(8,128)(2,1)S(1)} %copy-done.19, bf16[3,256,512]{2,1,0:T(8,128)(2,1)S(1)} %copy-done.25, bf16[3,256,512]{2,1,0:T(8,128)(2,1)S(1)} %copy-done.22, ...), custom_call_target="tpu_custom_call", output_to_operand_aliasing={{}: (11, {})} | custom-call | flops 3221225472 | bytes 12582912 | tf_op jit(solution)/shard_map/grads/pallas_call | solution.py:240
  393.6 5.9 %collective-permute-done.33 = bf16[256,512]{1,0:T(8,128)(2,1)S(1)} collective-permute-done((bf16[256,512]{1,0:T(8,128)(2,1)S(1)}, bf16[256,512]{1,0:T(8,128)(2,1)S(1)}, u32[]{:S(2)}, u32[]{:S(2)}) %collective-permute-start.33) | collective-permute-done | bytes 262176 | tf_op jit(solution)/shard_map/ppermute | solution.py:403
  399.7 2.2 subtract_convert_fusion
  (179 shorter events, 69.3 us)
Async XLA Ops:
  0.6 3.6 copy-start.53
  12.9 35.9 %copy-start.55 = (bf16[3,4,1024]{2,1,0:T(4,128)(2,1)S(1)}, bf16[3,4,1024]{2,1,0:T(4,128)(2,1)}, u32[]{:S(2)}) copy-start(bf16[3,4,1024]{2,1,0:T(4,128)(2,1)} %param.9) | copy-start | bytes 73732
  48.8 5.3 %collective-permute-start = (bf16[8,256,256]{1,2,0:T(8,128)(2,1)S(1)}, bf16[8,256,256]{1,2,0:T(8,128)(2,1)S(1)}, u32[]{:S(2)}, u32[]{:S(2)}) collective-permute-start(bf16[8,256,256]{1,2,0:T(8,128)(2,1)S(1)} %all_to_all.10), channel_id=1, source_target_pairs={{0,8},{8,0},{16,24},{24,16},{1,9},{9,1},{17,25},{25,17},{2,10},{10... | collective-permute-start | bytes 3145736 | tf_op jit(solution)/shard_map/ppermute | solution.py:333
  48.9 4.5 %copy-start.54 = (s32[8]{0:T(128)S(1)}, s32[8]{0:T(128)}, u32[]{:S(2)}) copy-start(s32[8]{0:T(128)} %constant.178.clone) | copy-start | bytes 100
  58.8 1.9 copy-start
  62.4 12.0 %collective-permute-start.1 = (bf16[3,128,512]{2,1,0:T(8,128)(2,1)S(1)}, bf16[3,128,512]{2,1,0:T(8,128)(2,1)S(1)}, u32[]{:S(2)}, u32[]{:S(2)}) collective-permute-start(bf16[3,128,512]{2,1,0:T(8,128)(2,1)S(1)} %get-tuple-element.25), channel_id=1, source_target_pairs={{0,2},{2,4},{4,6},{6,7},{7,5},{5,3},{3,1},{1,0},{8,10},{10,12},{12... | collective-permute-start | bytes 1179656 | tf_op jit(solution)/shard_map/ppermute | solution.py:350
  63.5 11.9 %collective-permute-start.2 = (bf16[3,128,512]{2,1,0:T(8,128)(2,1)S(1)}, bf16[3,128,512]{2,1,0:T(8,128)(2,1)S(1)}, u32[]{:S(2)}, u32[]{:S(2)}) collective-permute-start(bf16[3,128,512]{2,1,0:T(8,128)(2,1)S(1)} %get-tuple-element.26), channel_id=1, source_target_pairs={{2,0},{4,2},{6,4},{7,6},{5,7},{3,5},{1,3},{0,1},{10,8},{12,10},{14... | collective-permute-start | bytes 1179656 | tf_op jit(solution)/shard_map/ppermute | solution.py:351
  66.1 16.6 %collective-permute-start.9 = (bf16[3,128,512]{2,1,0:T(8,128)(2,1)S(1)}, bf16[3,128,512]{2,1,0:T(8,128)(2,1)S(1)}, u32[]{:S(2)}, u32[]{:S(2)}) collective-permute-start(bf16[3,128,512]{2,1,0:T(8,128)(2,1)S(1)} %get-tuple-element.34), channel_id=1, source_target_pairs={{0,2},{2,4},{4,6},{6,7},{7,5},{5,3},{3,1},{1,0},{8,10},{10,12},{12... | collective-permute-start | bytes 1179656 | tf_op jit(solution)/shard_map/ppermute | solution.py:350
  67.3 16.6 %collective-permute-start.10 = (bf16[3,128,512]{2,1,0:T(8,128)(2,1)S(1)}, bf16[3,128,512]{2,1,0:T(8,128)(2,1)S(1)}, u32[]{:S(2)}, u32[]{:S(2)}) collective-permute-start(bf16[3,128,512]{2,1,0:T(8,128)(2,1)S(1)} %get-tuple-element.35), channel_id=1, source_target_pairs={{2,0},{4,2},{6,4},{7,6},{5,7},{3,5},{1,3},{0,1},{10,8},{12,10},{14... | collective-permute-start | bytes 1179656 | tf_op jit(solution)/shard_map/ppermute | solution.py:351
  77.5 22.1 %collective-permute-start.3 = (bf16[3,256,512]{2,1,0:T(8,128)(2,1)S(1)}, bf16[3,256,512]{2,1,0:T(8,128)(2,1)S(1)}, u32[]{:S(2)}, u32[]{:S(2)}) collective-permute-start(bf16[3,256,512]{2,1,0:T(8,128)(2,1)S(1)} %get-tuple-element.27), channel_id=1, source_target_pairs={{0,2},{2,4},{4,6},{6,7},{7,5},{5,3},{3,1},{1,0},{8,10},{10,12},{12... | collective-permute-start | bytes 2359304 | tf_op jit(solution)/shard_map/ppermute | solution.py:350
  78.1 22.7 %collective-permute-start.4 = (bf16[3,256,512]{2,1,0:T(8,128)(2,1)S(1)}, bf16[3,256,512]{2,1,0:T(8,128)(2,1)S(1)}, u32[]{:S(2)}, u32[]{:S(2)}) collective-permute-start(bf16[3,256,512]{2,1,0:T(8,128)(2,1)S(1)} %get-tuple-element.28), channel_id=1, source_target_pairs={{2,0},{4,2},{6,4},{7,6},{5,7},{3,5},{1,3},{0,1},{10,8},{12,10},{14... | collective-permute-start | bytes 2359304 | tf_op jit(solution)/shard_map/ppermute | solution.py:351
  85.9 30.5 %collective-permute-start.11 = (bf16[3,256,512]{2,1,0:T(8,128)(2,1)S(1)}, bf16[3,256,512]{2,1,0:T(8,128)(2,1)S(1)}, u32[]{:S(2)}, u32[]{:S(2)}) collective-permute-start(bf16[3,256,512]{2,1,0:T(8,128)(2,1)S(1)} %get-tuple-element.36), channel_id=1, source_target_pairs={{0,2},{2,4},{4,6},{6,7},{7,5},{5,3},{3,1},{1,0},{8,10},{10,12},{12... | collective-permute-start | bytes 2359304 | tf_op jit(solution)/shard_map/ppermute | solution.py:350
  86.5 31.1 %collective-permute-start.12 = (bf16[3,256,512]{2,1,0:T(8,128)(2,1)S(1)}, bf16[3,256,512]{2,1,0:T(8,128)(2,1)S(1)}, u32[]{:S(2)}, u32[]{:S(2)}) collective-permute-start(bf16[3,256,512]{2,1,0:T(8,128)(2,1)S(1)} %get-tuple-element.37), channel_id=1, source_target_pairs={{2,0},{4,2},{6,4},{7,6},{5,7},{3,5},{1,3},{0,1},{10,8},{12,10},{14... | collective-permute-start | bytes 2359304 | tf_op jit(solution)/shard_map/ppermute | solution.py:351
  102.8 30.5 %collective-permute-start.5 = (bf16[3,256,512]{2,1,0:T(8,128)(2,1)S(1)}, bf16[3,256,512]{2,1,0:T(8,128)(2,1)S(1)}, u32[]{:S(2)}, u32[]{:S(2)}) collective-permute-start(bf16[3,256,512]{2,1,0:T(8,128)(2,1)S(1)} %get-tuple-element.29), channel_id=1, source_target_pairs={{0,2},{2,4},{4,6},{6,7},{7,5},{5,3},{3,1},{1,0},{8,10},{10,12},{12... | collective-permute-start | bytes 2359304 | tf_op jit(solution)/shard_map/ppermute | solution.py:350
  103.4 31.1 %collective-permute-start.6 = (bf16[3,256,512]{2,1,0:T(8,128)(2,1)S(1)}, bf16[3,256,512]{2,1,0:T(8,128)(2,1)S(1)}, u32[]{:S(2)}, u32[]{:S(2)}) collective-permute-start(bf16[3,256,512]{2,1,0:T(8,128)(2,1)S(1)} %get-tuple-element.30), channel_id=1, source_target_pairs={{2,0},{4,2},{6,4},{7,6},{5,7},{3,5},{1,3},{0,1},{10,8},{12,10},{14... | collective-permute-start | bytes 2359304 | tf_op jit(solution)/shard_map/ppermute | solution.py:351
  119.6 30.5 %collective-permute-start.13 = (bf16[3,256,512]{2,1,0:T(8,128)(2,1)S(1)}, bf16[3,256,512]{2,1,0:T(8,128)(2,1)S(1)}, u32[]{:S(2)}, u32[]{:S(2)}) collective-permute-start(bf16[3,256,512]{2,1,0:T(8,128)(2,1)S(1)} %get-tuple-element.38), channel_id=1, source_target_pairs={{0,2},{2,4},{4,6},{6,7},{7,5},{5,3},{3,1},{1,0},{8,10},{10,12},{12... | collective-permute-start | bytes 2359304 | tf_op jit(solution)/shard_map/ppermute | solution.py:350
  120.2 31.1 %collective-permute-start.14 = (bf16[3,256,512]{2,1,0:T(8,128)(2,1)S(1)}, bf16[3,256,512]{2,1,0:T(8,128)(2,1)S(1)}, u32[]{:S(2)}, u32[]{:S(2)}) collective-permute-start(bf16[3,256,512]{2,1,0:T(8,128)(2,1)S(1)} %get-tuple-element.39), channel_id=1, source_target_pairs={{2,0},{4,2},{6,4},{7,6},{5,7},{3,5},{1,3},{0,1},{10,8},{12,10},{14... | collective-permute-start | bytes 2359304 | tf_op jit(solution)/shard_map/ppermute | solution.py:351
  136.5 30.5 %collective-permute-start.7 = (bf16[3,256,512]{2,1,0:T(8,128)(2,1)S(1)}, bf16[3,256,512]{2,1,0:T(8,128)(2,1)S(1)}, u32[]{:S(2)}, u32[]{:S(2)}) collective-permute-start(bf16[3,256,512]{2,1,0:T(8,128)(2,1)S(1)} %get-tuple-element.31), channel_id=1, source_target_pairs={{0,2},{2,4},{4,6},{6,7},{7,5},{5,3},{3,1},{1,0},{8,10},{10,12},{12... | collective-permute-start | bytes 2359304 | tf_op jit(solution)/shard_map/ppermute | solution.py:350
  137.1 31.1 %copy-start.47 = (bf16[256,1024]{1,0:T(8,128)(2,1)S(1)}, bf16[256,1024]{1,0:T(8,128)(2,1)}, u32[]{:S(2)}) copy-start(bf16[256,1024]{1,0:T(8,128)(2,1)} %d_out.3) | copy-start | bytes 1572868
  137.1 31.1 %collective-permute-start.8 = (bf16[3,256,512]{2,1,0:T(8,128)(2,1)S(1)}, bf16[3,256,512]{2,1,0:T(8,128)(2,1)S(1)}, u32[]{:S(2)}, u32[]{:S(2)}) collective-permute-start(bf16[3,256,512]{2,1,0:T(8,128)(2,1)S(1)} %get-tuple-element.32), channel_id=1, source_target_pairs={{2,0},{4,2},{6,4},{7,6},{5,7},{3,5},{1,3},{0,1},{10,8},{12,10},{14... | collective-permute-start | bytes 2359304 | tf_op jit(solution)/shard_map/ppermute | solution.py:351
  153.3 30.5 %collective-permute-start.15 = (bf16[3,256,512]{2,1,0:T(8,128)(2,1)S(1)}, bf16[3,256,512]{2,1,0:T(8,128)(2,1)S(1)}, u32[]{:S(2)}, u32[]{:S(2)}) collective-permute-start(bf16[3,256,512]{2,1,0:T(8,128)(2,1)S(1)} %get-tuple-element.40), channel_id=1, source_target_pairs={{0,2},{2,4},{4,6},{6,7},{7,5},{5,3},{3,1},{1,0},{8,10},{10,12},{12... | collective-permute-start | bytes 2359304 | tf_op jit(solution)/shard_map/ppermute | solution.py:350
  153.9 31.1 %collective-permute-start.16 = (bf16[3,256,512]{2,1,0:T(8,128)(2,1)S(1)}, bf16[3,256,512]{2,1,0:T(8,128)(2,1)S(1)}, u32[]{:S(2)}, u32[]{:S(2)}) collective-permute-start(bf16[3,256,512]{2,1,0:T(8,128)(2,1)S(1)} %get-tuple-element.41), channel_id=1, source_target_pairs={{2,0},{4,2},{6,4},{7,6},{5,7},{3,5},{1,3},{0,1},{10,8},{12,10},{14... | collective-permute-start | bytes 2359304 | tf_op jit(solution)/shard_map/ppermute | solution.py:351
  175.4 16.2 %copy-start.32 = (bf16[3,256,512]{2,1,0:T(8,128)(2,1)}, bf16[3,256,512]{2,1,0:T(8,128)(2,1)S(1)}, u32[]{:S(2)}) copy-start(bf16[3,256,512]{2,1,0:T(8,128)(2,1)S(1)} %get-tuple-element.44.refs_0_) | copy-start | bytes 2359300
  175.4 16.2 %copy-start.48 = (bf16[256,512]{1,0:T(8,128)(2,1)}, bf16[256,512]{1,0:T(8,128)(2,1)S(1)}, u32[]{:S(2)}) copy-start(bf16[256,512]{1,0:T(8,128)(2,1)S(1)} %get-tuple-element.33) | copy-start | bytes 786436
  175.4 26.5 %collective-permute-start.26 = (bf16[3,256,512]{2,1,0:T(8,128)(2,1)S(1)}, bf16[3,256,512]{2,1,0:T(8,128)(2,1)S(1)}, u32[]{:S(2)}, u32[]{:S(2)}) collective-permute-start(bf16[3,256,512]{2,1,0:T(8,128)(2,1)S(1)} %get-tuple-element.44.refs_0_), channel_id=1, source_target_pairs={{2,0},{4,2},{6,4},{7,6},{5,7},{3,5},{1,3},{0,1},{10,8},{12,10},{14... | collective-permute-start | bytes 2359304 | tf_op jit(solution)/shard_map/ppermute | solution.py:381
  176.3 27.4 %collective-permute-start.25 = (bf16[3,256,512]{2,1,0:T(8,128)(2,1)S(1)}, bf16[3,256,512]{2,1,0:T(8,128)(2,1)S(1)}, u32[]{:S(2)}, u32[]{:S(2)}) collective-permute-start(bf16[3,256,512]{2,1,0:T(8,128)(2,1)S(1)} %get-tuple-element.44.refs_0_), channel_id=1, source_target_pairs={{0,2},{2,4},{4,6},{6,7},{7,5},{5,3},{3,1},{1,0},{8,10},{10,12},{12... | collective-permute-start | bytes 2359304 | tf_op jit(solution)/shard_map/ppermute | solution.py:380
  193.0 98.5 %copy-start.17 = (bf16[3,256,512]{2,1,0:T(8,128)(2,1)}, bf16[3,256,512]{2,1,0:T(8,128)(2,1)S(1)}, u32[]{:S(2)}) copy-start(bf16[3,256,512]{2,1,0:T(8,128)(2,1)S(1)} %get-tuple-element.43.refs_0_) | copy-start | bytes 2359300
  193.0 103.8 %copy-start.1 = (bf16[3,512,1024]{2,1,0:T(8,128)(2,1)S(1)}, bf16[3,512,1024]{2,1,0:T(8,128)(2,1)}, u32[]{:S(2)}) copy-start(bf16[3,512,1024]{2,1,0:T(8,128)(2,1)} %fusion.weight) | copy-start | bytes 9437188
  193.0 25.7 %collective-permute-start.18 = (bf16[3,256,512]{2,1,0:T(8,128)(2,1)S(1)}, bf16[3,256,512]{2,1,0:T(8,128)(2,1)S(1)}, u32[]{:S(2)}, u32[]{:S(2)}) collective-permute-start(bf16[3,256,512]{2,1,0:T(8,128)(2,1)S(1)} %get-tuple-element.43.refs_0_), channel_id=1, source_target_pairs={{2,0},{4,2},{6,4},{7,6},{5,7},{3,5},{1,3},{0,1},{10,8},{12,10},{14... | collective-permute-start | bytes 2359304 | tf_op jit(solution)/shard_map/ppermute | solution.py:381
  193.9 26.6 %collective-permute-start.17 = (bf16[3,256,512]{2,1,0:T(8,128)(2,1)S(1)}, bf16[3,256,512]{2,1,0:T(8,128)(2,1)S(1)}, u32[]{:S(2)}, u32[]{:S(2)}) collective-permute-start(bf16[3,256,512]{2,1,0:T(8,128)(2,1)S(1)} %get-tuple-element.43.refs_0_), channel_id=1, source_target_pairs={{0,2},{2,4},{4,6},{6,7},{7,5},{5,3},{3,1},{1,0},{8,10},{10,12},{12... | collective-permute-start | bytes 2359304 | tf_op jit(solution)/shard_map/ppermute | solution.py:380
  201.9 33.7 %collective-permute-start.28 = (bf16[3,256,512]{2,1,0:T(8,128)(2,1)S(1)}, bf16[3,256,512]{2,1,0:T(8,128)(2,1)S(1)}, u32[]{:S(2)}, u32[]{:S(2)}) collective-permute-start(bf16[3,256,512]{2,1,0:T(8,128)(2,1)S(1)} %collective-permute-done.26.refs_2_), channel_id=1, source_target_pairs={{2,0},{4,2},{6,4},{7,6},{5,7},{3,5},{1,3},{0,1},{10,8},{12,10},{14... | collective-permute-start | bytes 2359304 | tf_op jit(solution)/shard_map/ppermute | solution.py:381
  203.7 33.7 %collective-permute-start.27 = (bf16[3,256,512]{2,1,0:T(8,128)(2,1)S(1)}, bf16[3,256,512]{2,1,0:T(8,128)(2,1)S(1)}, u32[]{:S(2)}, u32[]{:S(2)}) collective-permute-start(bf16[3,256,512]{2,1,0:T(8,128)(2,1)S(1)} %collective-permute-done.25.refs_1_), channel_id=1, source_target_pairs={{0,2},{2,4},{4,6},{6,7},{7,5},{5,3},{3,1},{1,0},{8,10},{10,12},{12... | collective-permute-start | bytes 2359304 | tf_op jit(solution)/shard_map/ppermute | solution.py:380
  218.7 33.7 %collective-permute-start.20 = (bf16[3,256,512]{2,1,0:T(8,128)(2,1)S(1)}, bf16[3,256,512]{2,1,0:T(8,128)(2,1)S(1)}, u32[]{:S(2)}, u32[]{:S(2)}) collective-permute-start(bf16[3,256,512]{2,1,0:T(8,128)(2,1)S(1)} %collective-permute-done.18.refs_2_), channel_id=1, source_target_pairs={{2,0},{4,2},{6,4},{7,6},{5,7},{3,5},{1,3},{0,1},{10,8},{12,10},{14... | collective-permute-start | bytes 2359304 | tf_op jit(solution)/shard_map/ppermute | solution.py:381
  220.5 33.7 %collective-permute-start.19 = (bf16[3,256,512]{2,1,0:T(8,128)(2,1)S(1)}, bf16[3,256,512]{2,1,0:T(8,128)(2,1)S(1)}, u32[]{:S(2)}, u32[]{:S(2)}) collective-permute-start(bf16[3,256,512]{2,1,0:T(8,128)(2,1)S(1)} %collective-permute-done.17.refs_1_), channel_id=1, source_target_pairs={{0,2},{2,4},{4,6},{6,7},{7,5},{5,3},{3,1},{1,0},{8,10},{10,12},{12... | collective-permute-start | bytes 2359304 | tf_op jit(solution)/shard_map/ppermute | solution.py:380
  235.6 33.7 %collective-permute-start.30 = (bf16[3,256,512]{2,1,0:T(8,128)(2,1)S(1)}, bf16[3,256,512]{2,1,0:T(8,128)(2,1)S(1)}, u32[]{:S(2)}, u32[]{:S(2)}) collective-permute-start(bf16[3,256,512]{2,1,0:T(8,128)(2,1)S(1)} %collective-permute-done.28.refs_4_), channel_id=1, source_target_pairs={{2,0},{4,2},{6,4},{7,6},{5,7},{3,5},{1,3},{0,1},{10,8},{12,10},{14... | collective-permute-start | bytes 2359304 | tf_op jit(solution)/shard_map/ppermute | solution.py:381
  237.4 33.6 %collective-permute-start.29 = (bf16[3,256,512]{2,1,0:T(8,128)(2,1)S(1)}, bf16[3,256,512]{2,1,0:T(8,128)(2,1)S(1)}, u32[]{:S(2)}, u32[]{:S(2)}) collective-permute-start(bf16[3,256,512]{2,1,0:T(8,128)(2,1)S(1)} %collective-permute-done.27.refs_3_), channel_id=1, source_target_pairs={{0,2},{2,4},{4,6},{6,7},{7,5},{5,3},{3,1},{1,0},{8,10},{10,12},{12... | collective-permute-start | bytes 2359304 | tf_op jit(solution)/shard_map/ppermute | solution.py:380
  252.4 33.7 %collective-permute-start.22 = (bf16[3,256,512]{2,1,0:T(8,128)(2,1)S(1)}, bf16[3,256,512]{2,1,0:T(8,128)(2,1)S(1)}, u32[]{:S(2)}, u32[]{:S(2)}) collective-permute-start(bf16[3,256,512]{2,1,0:T(8,128)(2,1)S(1)} %collective-permute-done.20.refs_4_), channel_id=1, source_target_pairs={{2,0},{4,2},{6,4},{7,6},{5,7},{3,5},{1,3},{0,1},{10,8},{12,10},{14... | collective-permute-start | bytes 2359304 | tf_op jit(solution)/shard_map/ppermute | solution.py:381
  254.2 34.5 %collective-permute-start.21 = (bf16[3,256,512]{2,1,0:T(8,128)(2,1)S(1)}, bf16[3,256,512]{2,1,0:T(8,128)(2,1)S(1)}, u32[]{:S(2)}, u32[]{:S(2)}) collective-permute-start(bf16[3,256,512]{2,1,0:T(8,128)(2,1)S(1)} %collective-permute-done.19.refs_3_), channel_id=1, source_target_pairs={{0,2},{2,4},{4,6},{6,7},{7,5},{5,3},{3,1},{1,0},{8,10},{10,12},{12... | collective-permute-start | bytes 2359304 | tf_op jit(solution)/shard_map/ppermute | solution.py:380
  269.3 20.2 %copy-start.11 = (bf16[3,256,512]{2,1,0:T(8,128)(2,1)}, bf16[3,256,512]{2,1,0:T(8,128)(2,1)S(1)}, u32[]{:S(2)}) copy-start(bf16[3,256,512]{2,1,0:T(8,128)(2,1)S(1)} %collective-permute-done.30.refs_6_) | copy-start | bytes 2359300
  270.1 26.6 %collective-permute-start.32 = (bf16[3,128,512]{2,1,0:T(8,128)(2,1)}, bf16[3,128,512]{2,1,0:T(8,128)(2,1)}, u32[]{:S(2)}, u32[]{:S(2)}) collective-permute-start(bf16[3,128,512]{2,1,0:T(8,128)(2,1)} %slice.19), channel_id=1, source_target_pairs={{2,0},{4,2},{6,4},{7,6},{5,7},{3,5},{1,3},{0,1},{10,8},{12,10},{14... | collective-permute-start | bytes 1179656 | tf_op jit(solution)/shard_map/ppermute | solution.py:381
  271.0 20.5 %copy-start.14 = (bf16[3,256,512]{2,1,0:T(8,128)(2,1)}, bf16[3,256,512]{2,1,0:T(8,128)(2,1)S(1)}, u32[]{:S(2)}) copy-start(bf16[3,256,512]{2,1,0:T(8,128)(2,1)S(1)} %collective-permute-done.29.refs_5_) | copy-start | bytes 2359300
  271.9 24.9 %collective-permute-start.31 = (bf16[3,128,512]{2,1,0:T(8,128)(2,1)}, bf16[3,128,512]{2,1,0:T(8,128)(2,1)}, u32[]{:S(2)}, u32[]{:S(2)}) collective-permute-start(bf16[3,128,512]{2,1,0:T(8,128)(2,1)} %slice.18), channel_id=1, source_target_pairs={{0,2},{2,4},{4,6},{6,7},{7,5},{5,3},{3,1},{1,0},{8,10},{10,12},{12... | collective-permute-start | bytes 1179656 | tf_op jit(solution)/shard_map/ppermute | solution.py:380
  287.8 25.1 %collective-permute-start.24 = (bf16[3,128,512]{2,1,0:T(8,128)(2,1)}, bf16[3,128,512]{2,1,0:T(8,128)(2,1)S(1)}, u32[]{:S(2)}, u32[]{:S(2)}) collective-permute-start(bf16[3,128,512]{2,1,0:T(8,128)(2,1)} %slice.17), channel_id=1, source_target_pairs={{2,0},{4,2},{6,4},{7,6},{5,7},{3,5},{1,3},{0,1},{10,8},{12,10},{14... | collective-permute-start | bytes 1179656 | tf_op jit(solution)/shard_map/ppermute | solution.py:381
  290.4 22.5 %collective-permute-start.23 = (bf16[3,128,512]{2,1,0:T(8,128)(2,1)}, bf16[3,128,512]{2,1,0:T(8,128)(2,1)}, u32[]{:S(2)}, u32[]{:S(2)}) collective-permute-start(bf16[3,128,512]{2,1,0:T(8,128)(2,1)} %slice.16), channel_id=1, source_target_pairs={{0,2},{2,4},{4,6},{6,7},{7,5},{5,3},{3,1},{1,0},{8,10},{10,12},{12... | collective-permute-start | bytes 1179656 | tf_op jit(solution)/shard_map/ppermute | solution.py:380
  296.7 16.2 %copy-start.6 = (bf16[3,256,512]{2,1,0:T(8,128)(2,1)S(1)}, bf16[3,256,512]{2,1,0:T(8,128)(2,1)}, u32[]{:S(2)}) copy-start(bf16[3,256,512]{2,1,0:T(8,128)(2,1)} %copy-done.5) | copy-start | bytes 2359300
  296.7 16.2 %copy-start.9 = (bf16[3,256,512]{2,1,0:T(8,128)(2,1)S(1)}, bf16[3,256,512]{2,1,0:T(8,128)(2,1)}, u32[]{:S(2)}) copy-start(bf16[3,256,512]{2,1,0:T(8,128)(2,1)} %copy-done.8) | copy-start | bytes 2359300
  304.8 8.1 %copy-start.18 = (bf16[3,256,512]{2,1,0:T(8,128)(2,1)S(1)}, bf16[3,256,512]{2,1,0:T(8,128)(2,1)}, u32[]{:S(2)}) copy-start(bf16[3,256,512]{2,1,0:T(8,128)(2,1)} %copy-done.17) | copy-start | bytes 2359300
  304.8 8.1 %copy-start.21 = (bf16[3,256,512]{2,1,0:T(8,128)(2,1)S(1)}, bf16[3,256,512]{2,1,0:T(8,128)(2,1)}, u32[]{:S(2)}) copy-start(bf16[3,256,512]{2,1,0:T(8,128)(2,1)} %copy-done.20) | copy-start | bytes 2359300
  304.8 8.1 %copy-start.24 = (bf16[3,256,512]{2,1,0:T(8,128)(2,1)S(1)}, bf16[3,256,512]{2,1,0:T(8,128)(2,1)}, u32[]{:S(2)}) copy-start(bf16[3,256,512]{2,1,0:T(8,128)(2,1)} %copy-done.23) | copy-start | bytes 2359300
  304.8 8.1 %copy-start.27 = (bf16[3,256,512]{2,1,0:T(8,128)(2,1)S(1)}, bf16[3,256,512]{2,1,0:T(8,128)(2,1)}, u32[]{:S(2)}) copy-start(bf16[3,256,512]{2,1,0:T(8,128)(2,1)} %copy-done.26) | copy-start | bytes 2359300
  304.8 8.2 %copy-start.30 = (bf16[3,256,512]{2,1,0:T(8,128)(2,1)S(1)}, bf16[3,256,512]{2,1,0:T(8,128)(2,1)}, u32[]{:S(2)}) copy-start(bf16[3,256,512]{2,1,0:T(8,128)(2,1)} %copy-done.29) | copy-start | bytes 2359300
  310.9 2.0 copy-start.3
  319.9 1.3 copy-start.4
  321.2 5.2 %copy-start.56 = (bf16[4096]{0:T(1024)(128)(2,1)S(1)}, bf16[4096]{0:T(1024)(128)(2,1)}, u32[]{:S(2)}) copy-start(bf16[4096]{0:T(1024)(128)(2,1)} %param.7) | copy-start | bytes 24580
  321.3 32.6 %copy-start.49 = (bf16[256,512]{1,0:T(8,128)(2,1)S(1)}, bf16[256,512]{1,0:T(8,128)(2,1)}, u32[]{:S(2)}) copy-start(bf16[256,512]{1,0:T(8,128)(2,1)} %copy-done.48) | copy-start | bytes 786436
  321.3 34.4 %copy-start.2 = (bf16[8,256,512]{1,2,0:T(8,128)(2,1)S(1)}, bf16[8,256,512]{1,2,0:T(8,128)(2,1)}, u32[]{:S(2)}) copy-start(bf16[8,256,512]{1,2,0:T(8,128)(2,1)} %maximum_select_fusion) | copy-start | bytes 6291460
  321.3 34.4 %copy-start.13 = (bf16[3,256,512]{2,1,0:T(8,128)(2,1)S(1)}, bf16[3,256,512]{2,1,0:T(8,128)(2,1)}, u32[]{:S(2)}) copy-start(bf16[3,256,512]{2,1,0:T(8,128)(2,1)} %copy-done.11) | copy-start | bytes 2359300
  321.3 47.9 %all-to-all-start.1 = ((bf16[4,2,256,512]{3,2,1,0:T(8,128)(2,1)}), bf16[4,2,256,512]{3,2,1,0:T(8,128)(2,1)}, u32[]{:S(2)}, u32[]{:S(2)}) async-start(bf16[4,2,256,512]{3,2,1,0:T(8,128)(2,1)} %bitcast.22), calls=%async_computation.1 | async-start | bytes 4194304 | tf_op jit(solution)/shard_map/all_to_all | solution.py:391
  369.1 10.1 %copy-start.7 = (bf16[3,256,512]{2,1,0:T(8,128)(2,1)S(1)}, bf16[3,256,512]{2,1,0:T(8,128)(2,1)}, u32[]{:S(2)}) copy-start(bf16[3,256,512]{2,1,0:T(8,128)(2,1)} %copy-done.5) | copy-start | bytes 2359300
  373.1 20.5 %collective-permute-start.34 = (bf16[256,512]{1,0:T(8,128)(2,1)S(1)}, bf16[256,512]{1,0:T(8,128)(2,1)S(1)}, u32[]{:S(2)}, u32[]{:S(2)}) collective-permute-start(bf16[256,512]{1,0:T(8,128)(2,1)S(1)} %get-tuple-element.49), channel_id=1, source_target_pairs={{0,1},{1,0},{2,9},{3,8},{4,17},{5,16},{6,25},{7,24},{8,3},{9,2},{1... | collective-permute-start | bytes 786440 | tf_op jit(solution)/shard_map/ppermute | solution.py:403
  374.2 25.3 %collective-permute-start.33 = (bf16[256,512]{1,0:T(8,128)(2,1)S(1)}, bf16[256,512]{1,0:T(8,128)(2,1)S(1)}, u32[]{:S(2)}, u32[]{:S(2)}) collective-permute-start(bf16[256,512]{1,0:T(8,128)(2,1)S(1)} %get-tuple-element.50), channel_id=1, source_target_pairs={{0,0},{1,1},{2,8},{3,9},{4,16},{5,17},{6,24},{7,25},{8,2},{9,3},{1... | collective-permute-start | bytes 786440 | tf_op jit(solution)/shard_map/ppermute | solution.py:403
  386.1 13.6 %copy-start.58 = (f32[256]{0:T(256)S(1)}, f32[256]{0:T(256)}, u32[]{:S(2)}) copy-start(f32[256]{0:T(256)} %copy-done.57) | copy-start | bytes 3076
  386.1 13.6 %copy-start.59 = (f32[256]{0:T(256)S(1)}, f32[256]{0:T(256)}, u32[]{:S(2)}) copy-start(f32[256]{0:T(256)} %get-tuple-element.54) | copy-start | bytes 3076
  386.1 13.7 %copy-start.60 = (f32[256]{0:T(256)S(1)}, f32[256]{0:T(256)}, u32[]{:S(2)}) copy-start(f32[256]{0:T(256)} %psum.7) | copy-start | bytes 3076
  (33 other events, 33.4 us)

commit v2 on v1

v2 whole, which is shorter than its diff:
```python
import functools
import math

import jax
import jax.numpy as jnp
from jax import lax
from jax.experimental import pallas as pl
from jax.experimental.pallas import tpu as pltpu
from jax.sharding import PartitionSpec as P

HEAD_DIM = 128
NORM_EPS = 1e-05
VMEM = 60 * 1024 * 1024


def params(*semantics):
    return pltpu.CompilerParams(dimension_semantics=semantics, vmem_limit_bytes=VMEM)


def cost(flops, moved):
    return pl.CostEstimate(flops=flops, bytes_accessed=moved, transcendentals=0)


def mm(a, b):
    return jnp.dot(a, b, preferred_element_type=jnp.float32)


def mm_nt(a, b):
    return lax.dot_general(a, b, (((1,), (1,)), ((), ())), preferred_element_type=jnp.float32)


def mm_tn(a, b):
    return lax.dot_general(a, b, (((0,), (0,)), ((), ())), preferred_element_type=jnp.float32)


def rope_tables(length, width):
    position = jnp.arange(length).astype(jnp.float32)[:, None]
    frequency = jnp.exp(
        jnp.arange(width // 2).astype(jnp.float32) * (-2.0 * math.log(10000.0) / width)
    )
    angle = position * frequency[None, :]
    cosine, sine = jnp.cos(angle), jnp.sin(angle)
    return (
        jnp.concatenate([cosine, cosine], axis=-1),
        jnp.concatenate([-sine, sine], axis=-1),
    )


def ring_order(size):
    return [*range(0, size, 2), *reversed(range(1, size, 2))]


def normed_kernel(idx, tokens, gain, *outs):
    width, part = tokens.shape[1], outs[0].shape[1]
    values = tokens[...].astype(jnp.float32)
    inverse = lax.rsqrt(jnp.mean(values * values, axis=-1, keepdims=True) + NORM_EPS)
    size = len(outs) - 1
    for distance in range(size):
        start = pl.multiple_of(idx[distance] * (width // size) + idx[size] * part, part)
        block = tokens[:, pl.ds(start, part)].astype(jnp.float32)
        scale = gain[:, pl.ds(start, part)]
        outs[distance][...] = (block * inverse * scale).astype(jnp.bfloat16)
    outs[size][...] = jnp.broadcast_to(inverse, outs[size].shape)


def normed_blocks(idx, tokens, gain, size, part):
    length, width = tokens.shape
    tile = length // 4
    block = pl.BlockSpec((tile, part), lambda i, idx: (i, 0))
    *blocks, inverse = pl.pallas_call(
        normed_kernel,
        grid_spec=pltpu.PrefetchScalarGridSpec(
            num_scalar_prefetch=1,
            grid=(4,),
            in_specs=[
                pl.BlockSpec((tile, width), lambda i, idx: (i, 0)),
                pl.BlockSpec((1, width), lambda i, idx: (0, 0)),
            ],
            out_specs=[block] * size + [pl.BlockSpec((tile, 128), lambda i, idx: (i, 0))],
        ),
        out_shape=[jax.ShapeDtypeStruct((length, part), jnp.bfloat16)] * size
        + [jax.ShapeDtypeStruct((length, 128), jnp.float32)],
        compiler_params=params("arbitrary"),
        cost_estimate=cost(8 * length * width, 4 * length * width),
        name="normed_blocks",
    )(idx, tokens, gain)
    return blocks, inverse[:, :1]


def sum_first_kernel(core, mine, other, weight, weight_other, right, left):
    half = right.shape[1]
    product = mm(mine[...], weight[0]) + mm(other[...], weight_other[0])
    right[0] = product[:half].astype(jnp.bfloat16)
    left[0] = product[half:].astype(jnp.bfloat16)


def sum_step_kernel(
    core, mine_r, other_r, mine_l, other_l, weight, weight_other, from_left, from_right, right, left
):
    length, part = right.shape[1], from_left.shape[1]
    product = mm(mine_r[...], weight[0]) + mm(other_r[...], weight_other[0])
    right[0, :part] = (product[:part] + from_left[0].astype(jnp.float32)).astype(jnp.bfloat16)
    if part < length:
        right[0, part:] = product[part:].astype(jnp.bfloat16)
    product = mm(mine_l[...], weight[0]) + mm(other_l[...], weight_other[0])
    rest = length - part
    left[0, rest:] = (product[rest:] + from_right[0].astype(jnp.float32)).astype(jnp.bfloat16)
    if rest:
        left[0, :rest] = product[:rest].astype(jnp.bfloat16)


def weight_halves(depth, wide, chunk):
    return [
        pl.BlockSpec((1, depth // 2, wide), lambda m, core: (m, core[0], chunk)),
        pl.BlockSpec((1, depth // 2, wide), lambda m, core: (m, 1 - core[0], chunk)),
    ]


def sum_first(core, rows, weights, chunk, wide):
    length, part = rows[0].shape
    half = length // 2
    block = pl.BlockSpec((length, part), lambda m, core: (0, 0))
    result = jax.ShapeDtypeStruct((3, half, wide), jnp.bfloat16)
    return pl.pallas_call(
        sum_first_kernel,
        grid_spec=pltpu.PrefetchScalarGridSpec(
            num_scalar_prefetch=1,
            grid=(3,),
            in_specs=[block, block, *weight_halves(2 * part, wide, chunk)],
            out_specs=[pl.BlockSpec((1, half, wide), lambda m, core: (m, 0, 0))] * 2,
        ),
        out_shape=[result, result],
        compiler_params=params("arbitrary"),
        cost_estimate=cost(12 * length * part * wide, 16 * part * wide),
        name="sum_first",
    )(core, *rows, weights, weights)


def sum_step(core, rows_r, rows_l, weights, from_left, from_right, chunk, wide):
    length, part = rows_r[0].shape
    block = pl.BlockSpec((length, part), lambda m, core: (0, 0))
    whole = jax.ShapeDtypeStruct((3, length, wide), jnp.bfloat16)
    came = from_left.shape[1]
    return pl.pallas_call(
        sum_step_kernel,
        grid_spec=pltpu.PrefetchScalarGridSpec(
            num_scalar_prefetch=1,
            grid=(3,),
            in_specs=[
                *[block] * 4,
                *weight_halves(2 * part, wide, chunk),
                pl.BlockSpec((1, came, wide), lambda m, core: (m, 0, 0)),
                pl.BlockSpec((1, came, wide), lambda m, core: (m, 0, 0)),
            ],
            out_specs=[pl.BlockSpec((1, length, wide), lambda m, core: (m, 0, 0))] * 2,
        ),
        out_shape=[whole, whole],
        compiler_params=params("arbitrary"),
        cost_estimate=cost(24 * length * part * wide, 24 * part * wide),
        name="sum_step",
    )(core, *rows_r, *rows_l, weights, weights, from_left, from_right)


def attention_kernel(
    core, mine, other, weight, weight_other, from_left, from_right, d_out, cosine, sine,
    output, pre, dots,
):
    length = mine.shape[0]
    proj = [
        mm(mine[...], weight[m])
        + mm(other[...], weight_other[m])
        + (from_left[m].astype(jnp.float32) + from_right[m].astype(jnp.float32))
        for m in range(3)
    ]
    cos, sin = cosine[...], sine[...]
    half = HEAD_DIM // 2

    def rotate(tensor, angle):
        return tensor * cos + pltpu.roll(tensor, half, 1) * angle

    query = rotate(proj[0], sin).astype(jnp.bfloat16)
    key_rows = rotate(proj[1], sin).astype(jnp.bfloat16)
    value = proj[2].astype(jnp.bfloat16)
    scores = mm_nt(query, key_rows) * (1.0 / math.sqrt(HEAD_DIM))
    causal = lax.broadcasted_iota(jnp.int32, (length, length), 0) >= lax.broadcasted_iota(
        jnp.int32, (length, length), 1
    )
    scores = jnp.where(causal, scores, jnp.float32(-1e30))
    powers = jnp.exp(scores - jnp.max(scores, axis=-1, keepdims=True))
    probs = powers * (1.0 / jnp.sum(powers, axis=-1, keepdims=True))
    probs_low = probs.astype(jnp.bfloat16)
    output[...] = mm(probs_low, value).astype(jnp.bfloat16)
    cotangent = d_out[...]
    d_value = mm_tn(probs_low, cotangent).astype(jnp.bfloat16)
    d_probs = mm_nt(cotangent, value).astype(jnp.bfloat16).astype(jnp.float32)
    inner = jnp.sum(d_probs * probs, axis=-1, keepdims=True)
    d_scores = (probs * (d_probs - inner) * (1.0 / math.sqrt(HEAD_DIM))).astype(jnp.bfloat16)
    d_query = mm(d_scores, key_rows).astype(jnp.bfloat16).astype(jnp.float32)
    d_key = mm_tn(d_scores, query).astype(jnp.bfloat16).astype(jnp.float32)
    pre_query = rotate(d_query, -sin).astype(jnp.bfloat16)
    pre_key = rotate(d_key, -sin).astype(jnp.bfloat16)
    pre[0] = pre_query
    pre[1] = pre_key
    pre[2] = d_value
    product = (
        pre_query.astype(jnp.float32) * proj[0]
        + pre_key.astype(jnp.float32) * proj[1]
        + d_value.astype(jnp.float32) * proj[2]
    )

    @pl.when(pl.program_id(0) == 0)
    def _():
        dots[...] = product

    @pl.when(pl.program_id(0) > 0)
    def _():
        dots[...] += product


def attention(core, rows, weights, from_left, from_right, d_out, tables, chunk, wide):
    length, part = rows[0].shape
    heads = wide // HEAD_DIM
    first = chunk * heads
    block = pl.BlockSpec((length, part), lambda h, core: (0, 0))
    table = pl.BlockSpec((length, HEAD_DIM), lambda h, core: (0, 0))
    stack = pl.BlockSpec((3, length, HEAD_DIM), lambda h, core: (0, 0, h))
    return pl.pallas_call(
        attention_kernel,
        grid_spec=pltpu.PrefetchScalarGridSpec(
            num_scalar_prefetch=1,
            grid=(heads,),
            in_specs=[
                block,
                block,
                pl.BlockSpec((3, part, HEAD_DIM), lambda h, core: (0, core[0], first + h)),
                pl.BlockSpec((3, part, HEAD_DIM), lambda h, core: (0, 1 - core[0], first + h)),
                stack,
                stack,
                pl.BlockSpec((length, HEAD_DIM), lambda h, core: (0, first + h)),
                table,
                table,
            ],
            out_specs=[
                pl.BlockSpec((length, HEAD_DIM), lambda h, core: (0, h)),
                stack,
                table,
            ],
        ),
        out_shape=[
            jax.ShapeDtypeStruct((length, wide), jnp.bfloat16),
            jax.ShapeDtypeStruct((3, length, wide), jnp.bfloat16),
            jax.ShapeDtypeStruct((length, HEAD_DIM), jnp.float32),
        ],
        compiler_params=params("arbitrary"),
        cost_estimate=cost(12 * length * part * wide, 24 * part * wide),
        name="attention",
    )(core, *rows, weights, weights, from_left, from_right, d_out, *tables)


def grads_kernel(count, sets, core, *refs):
    mine, other = refs[:count], refs[count : 2 * count]
    pieces, out, turned = refs[2 * count : -2], refs[-2], refs[-1]
    length, part = mine[0].shape

    @pl.when(pl.program_id(0) == 0)
    def _():
        for place in range(count):
            span = slice(place * length, (place + 1) * length)
            turned[:part, span] = mine[place][...].T
            turned[part:, span] = other[place][...].T

    totals = [None, None]
    start = 0
    for position in range(sets):
        group = pieces[position * (count + 1) : (position + 1) * (count + 1)]
        rows = group[0].shape[1]
        for place in range(count):
            if place < count - 1:
                block = group[place][0]
            else:
                block = jnp.concatenate([group[place][0], group[place + 1][0]], axis=0)
            low = place * length + start
            for side in range(2):
                product = mm(turned[side * part : (side + 1) * part, low : low + rows], block)
                totals[side] = product if totals[side] is None else totals[side] + product
        start += rows
    out[0, pl.ds(pl.multiple_of(core[0] * part, part), part)] = totals[0]
    out[0, pl.ds(pl.multiple_of((1 - core[0]) * part, part), part)] = totals[1]


def grads_chunk(core, mine, other, gathered, before, chunk, wide, columns):
    count = len(mine)
    length, part = mine[0].shape
    block = pl.BlockSpec((length, part), lambda m, core: (0, 0))
    in_specs = [block] * (2 * count)
    operands = [core, *mine, *other]
    for pieces in gathered:
        for piece in pieces:
            in_specs.append(pl.BlockSpec((1, *piece.shape[1:]), lambda m, core: (m, 0, 0)))
            operands.append(piece)
    aliases = {}
    kernel = functools.partial(grads_kernel, count, len(gathered))
    if before is not None:
        aliases = {len(operands): 0}
        operands.append(before)
        in_specs.append(pl.BlockSpec(memory_space=pl.ANY))
        inner = kernel

        def kernel(*refs):
            inner(*refs[:-3], *refs[-2:])

    return pl.pallas_call(
        kernel,
        grid_spec=pltpu.PrefetchScalarGridSpec(
            num_scalar_prefetch=1,
            grid=(3,),
            in_specs=in_specs,
            out_specs=pl.BlockSpec((1, 2 * part, wide), lambda m, core: (m, 0, chunk)),
            scratch_shapes=[pltpu.VMEM((2 * part, count * length), jnp.bfloat16)],
        ),
        out_shape=jax.ShapeDtypeStruct((3, 2 * part, columns), jnp.float32),
        input_output_aliases=aliases,
        compiler_params=params("arbitrary"),
        cost_estimate=cost(12 * count * length * part * wide, 12 * count * length * wide),
        name="grads",
    )(*operands)


def back(pieces, weight, place, count):
    def one(piece):
        total = mm_nt(piece[0], weight[0])
        for m in range(1, 3):
            total += mm_nt(piece[m], weight[m])
        return total

    if place < count - 1:
        return one(pieces[place])
    return jnp.concatenate([one(pieces[place]), one(pieces[place + 1])], axis=0)


def term_first_kernel(count, idx, weight, *refs):
    for place in range(count):
        refs[-1][idx[place]] = back(refs, weight, place, count)


def term_first(seqs, weights, pieces, chunk, wide):
    count = len(pieces) - 1
    length = pieces[0].shape[1]
    depth = weights.shape[1]
    return pl.pallas_call(
        functools.partial(term_first_kernel, count),
        grid_spec=pltpu.PrefetchScalarGridSpec(
            num_scalar_prefetch=1,
            grid=(1,),
            in_specs=[
                pl.BlockSpec((3, depth, wide), lambda i, idx: (0, 0, chunk)),
                *[pl.BlockSpec(piece.shape, lambda i, idx: (0, 0, 0)) for piece in pieces],
            ],
            out_specs=pl.BlockSpec((count, length, depth), lambda i, idx: (0, 0, 0)),
        ),
        out_shape=jax.ShapeDtypeStruct((count, length, depth), jnp.float32),
        compiler_params=params("arbitrary"),
        cost_estimate=cost(6 * count * length * depth * wide, 6 * count * length * wide),
        name="term_first",
    )(seqs, weights, *pieces)


def term_last_kernel(count, idx, weight, before, *refs):
    keep, send = refs[-2], refs[-1]
    for place in range(count):
        total = back(refs, weight, place, count) + before[idx[place]]

        @pl.when(idx[count + place] == 0)
        def _():
            keep[idx[2 * count + place]] = total.astype(jnp.bfloat16).astype(jnp.float32)

        @pl.when(idx[count + place] == 1)
        def _():
            send[idx[2 * count + place]] = total.astype(jnp.bfloat16)


def term_last(idx, weights, before, pieces, part, chunk, wide):
    count, _, depth = before.shape
    rows = pieces[0].shape[1]
    result = pl.BlockSpec((count // 2, rows, depth), lambda i, idx: (0, 0, 0))
    return pl.pallas_call(
        functools.partial(term_last_kernel, count),
        grid_spec=pltpu.PrefetchScalarGridSpec(
            num_scalar_prefetch=1,
            grid=(1,),
            in_specs=[
                pl.BlockSpec((3, depth, wide), lambda i, idx: (0, 0, chunk)),
                pl.BlockSpec((count, rows, depth), lambda i, idx: (0, part, 0)),
                *[pl.BlockSpec(piece.shape, lambda i, idx: (0, 0, 0)) for piece in pieces],
            ],
            out_specs=[result, result],
        ),
        out_shape=[
            jax.ShapeDtypeStruct((count // 2, rows, depth), jnp.float32),
            jax.ShapeDtypeStruct((count // 2, rows, depth), jnp.bfloat16),
        ],
        compiler_params=params("arbitrary"),
        cost_estimate=cost(6 * count * rows * depth * wide, 6 * count * rows * wide),
        name="term_last",
    )(idx, weights, before, *pieces)


def after(first, *arrays):
    tied = lax.optimization_barrier((first, *arrays))
    return tied[1:]


def local(tokens, norm_gain, w_quant, w_scale, d_out):
    length, width = tokens.shape
    depth, columns = w_quant.shape[1:]
    size, nodes = lax.axis_size("local"), lax.axis_size("node")
    here, node = lax.axis_index("local"), lax.axis_index("node")
    wide = columns // 2
    far = size // 2
    group = size // nodes
    core = node % 2

    order = ring_order(size)
    table = jnp.array(order, jnp.int32)
    place = jnp.where(here % 2 == 0, here // 2, size - (here + 1) // 2)

    def shift(array, distance):
        moves = [(order[i], order[(i + distance) % size]) for i in range(size)]
        return lax.ppermute(array, "local", moves)

    def swap(array, bit):
        return lax.ppermute(array, "node", [(n, n ^ bit) for n in range(nodes)])

    def sequence(distance):
        return table[(place + distance + size) % size]

    targets = jnp.stack([sequence(distance) for distance in range(size)] + [core])
    gains = norm_gain.astype(jnp.float32)
    blocks, inverse_rms = normed_blocks(
        targets.astype(jnp.int32), tokens, gains[None], size, depth // 2
    )
    mine, other = {0: blocks[0]}, {}
    mine[far] = shift(blocks[far], far)
    other[far] = swap(mine[far], 1)
    previous = mine[far]
    for distance in range(far - 1, 0, -1):
        tied = after(previous, blocks[distance], blocks[size - distance])
        mine[-distance] = shift(tied[0], distance)
        mine[distance] = shift(tied[1], -distance)
        for sign in (-1, 1):
            other[sign * distance] = swap(mine[sign * distance], 1)
        previous = mine[distance]
    other[0] = swap(mine[0], 1)

    scaled = w_quant.reshape(3, w_scale.shape[1], -1, columns).astype(jnp.float32)
    weights = (scaled * w_scale.astype(jnp.float32)[:, :, None, :]).astype(jnp.bfloat16)
    weights = weights.reshape(3, depth, columns)

    tables = rope_tables(length, HEAD_DIM)
    core_index = core[None].astype(jnp.int32)
    arrived = []
    for chunk in range(2):
        right, left = sum_first(core_index, (mine[far], other[far]), weights, chunk, wide)
        for distance in range(far - 1, -1, -1):
            from_left, from_right = shift(right, 1), shift(left, -1)
            if distance:
                right, left = sum_step(
                    core_index,
                    (mine[distance], other[distance]),
                    (mine[-distance], other[-distance]),
                    weights,
                    from_left,
                    from_right,
                    chunk,
                    wide,
                )
        arrived.append((from_left, from_right))

    outputs, pres, dots = [], [], 0.0
    for chunk in range(2):
        output, pre, product = attention(
            core_index, (mine[0], other[0]), weights, *arrived[chunk], d_out, tables, chunk, wide
        )
        outputs.append(output)
        pres.append(pre)
        dots += jnp.sum(product, axis=-1, keepdims=True)
    bit = 1
    while bit < nodes:
        dots = dots + swap(dots, bit)
        bit *= 2

    half = length // 2
    sets = [pres[0], pres[1][:, :half], pres[1][:, half:]]
    gathered = [[block] for block in sets]
    moving = [(block, block) for block in sets]
    schedule = [(0, 1)]
    for step in range(2, far + 1):
        schedule += [(0, step), (1, step - 1)]
    schedule += [(2, 1), (1, far)] + [(2, step) for step in range(2, far + 1)]

    distances = [0]
    for step in range(1, far):
        distances += [-step, step]
    distances.append(far)
    seqs = jnp.stack([sequence(distance) for distance in distances]).astype(jnp.int32)
    owner = seqs // group
    position = (owner // 2) * group + seqs % group
    idx = jnp.concatenate([seqs, (owner % 2) ^ core, position]).astype(jnp.int32)

    share = width // nodes
    values_part = lax.dynamic_slice_in_dim(tokens, node * share, share, 1).astype(jnp.float32)
    gains_part = lax.dynamic_slice_in_dim(gains, node * share, share, 0)

    def start_term(before, part):
        keep, send = term_last(idx, weights, before, gathered[1 + part], part, 1, wide)
        return keep + swap(send, 1).astype(jnp.float32)

    def end_term(summed, part):
        bit = 2
        while bit < nodes:
            pair = summed.reshape(-1, 2, group, *summed.shape[1:])
            own = (node // bit) % 2
            keep = lax.dynamic_index_in_dim(pair, own, 1, keepdims=False)
            send = lax.dynamic_index_in_dim(pair, 1 - own, 1, keepdims=False)
            summed = keep + swap(send.astype(jnp.bfloat16), bit).astype(jnp.float32)
            summed = summed.reshape(-1, *pair.shape[3:])
            bit *= 2
        summed = summed.astype(jnp.bfloat16)
        came = []
        for turn in range(group):
            block = lax.dynamic_index_in_dim(summed, (here + turn) % group, 0, keepdims=False)
            moves = [
                (n * size + s, (s // group) * size + n * group + (s + turn) % group)
                for n in range(nodes)
                for s in range(size)
            ]
            came.append(lax.ppermute(block, ("node", "local"), moves))
        came = jnp.stack(came)
        upstream = jnp.concatenate(
            [
                lax.dynamic_index_in_dim(came, (here + group - i) % group, 0, keepdims=False)
                for i in range(group)
            ],
            axis=-1,
        ).astype(jnp.float32)
        rows = slice(part * half, (part + 1) * half)
        d_rows = (
            inverse_rms[rows] * gains_part * upstream
            - values_part[rows] * inverse_rms[rows] ** 2 * dots[rows] / width
        )
        return d_rows.astype(jnp.bfloat16)

    term = early = None
    for ring, step in schedule:
        right, left = moving[ring]
        if step == far:
            middle = right.shape[1] // 2
            right, left = right[:, :middle], left[:, middle:]
        if (ring, step) == (1, 1):
            right, left = after(moving[0][0], right, left)
        if (ring, step) == (2, 1):
            right, left = after(moving[0][0], right, left)
        if (ring, step) == (2, min(2, far)):
            right, left = after(term, right, left)
        if (ring, step) == (2, far):
            right, left = after(early, right, left)
        right, left = shift(right, 1), shift(left, -1)
        moving[ring] = right, left
        gathered[ring] += [right, left]
        if (ring, step) == (0, far):
            term = term_first(seqs, weights, gathered[0], 0, wide)
        if (ring, step) == (1, far):
            early = start_term(term, 0)
    late = start_term(term, 1)
    d_tokens = jnp.concatenate([end_term(early, 0), end_term(late, 1)], axis=0)

    rows = [mine[distance] for distance in distances], [other[distance] for distance in distances]
    grads = grads_chunk(core_index, *rows, gathered[:1], None, 0, wide, columns)
    grads = grads_chunk(core_index, *rows, gathered[1:], grads, 1, wide, columns)
    return (jnp.concatenate(outputs, axis=-1), d_tokens, grads)


def solution(mesh):
    placed = (
        P("local", None),
        P(),
        P(None, "local", "node"),
        P(None, "local", "node"),
        P("local", "node"),
    )
    return jax.shard_map(
        local,
        mesh=mesh,
        in_specs=placed,
        out_specs=(P("local", "node"), P("local", "node"), P(None, "local", "node")),
        check_vma=False,
    )
```

time: 404 us -> 393 us (0.973)
  blocking collectives: 56.2 us -> 0 us
  Pallas kernels: 54.9 us -> 104 us
  local copies, waits for them, and re-layouts: 62.2 us -> 34.9 us
  starting transfers between devices: 44.2 us -> 67.9 us
  other arithmetic: 26.2 us -> 17.3 us
  waiting for transfers between devices: 157 us -> 165 us
    all_to_all x1 -> x0, blocking collectives: 31.4 us -> none  [local(): lax.all_to_all(mine, 'local', split_axis=0, concat_axis=0, tiled=True)]
    unnamed x123 -> x128, local copies, waits for them, and re-layouts: 42.4 us -> 12.2 us
    ppermute x35 -> x65, starting transfers between devices: 39 us -> 67.9 us  [the longest x47 53.3 us: shift(): return lax.ppermute(array, 'local', moves)]
    pallas_call x4 -> x6, Pallas kernels: 26.3 us -> 54.7 us  [the longest x2 20.8 us: term_last(): pl.pallas_call(functools.partial(term_last_kernel, count), grid_spec=pltp...]
    psum x1 -> x0, blocking collectives: 24.8 us -> none  [local(): dots = lax.psum(dots, 'node')]
    pallas_call x6, Pallas kernels: 12.1 us -> 26.1 us  [sum_step(): pl.pallas_call(sum_step_kernel, grid_spec=pltpu.PrefetchScalarGridSpec(nu...]
    ppermute x35 -> x65, waiting for transfers between devices: 157 us -> 165 us  [the longest x47 156 us: shift(): return lax.ppermute(array, 'local', moves)]
    another operation x1 -> x2, local copies, waits for them, and re-layouts: 5.19 us -> 10.8 us  [the longest x1 5.77 us: local(): jnp.stack([sequence(distance) for distance in range(size)] + [core])]
  transfers between devices with their start and end apart: 36 -> 65, of which waited for: 24 -> 34; matrix products, arithmetic and copies ran while one was open for 6% -> 8% of each run, Pallas kernels for 12% -> 23%
where the time goes in v2:
time: 393 us; the launch traced here: 390 us
  waiting for transfers between devices  165 us (42%)
  Pallas kernels  104 us (26%)
  starting transfers between devices  67.9 us (17%)
  local copies, waits for them, and re-layouts  34.9 us (9%)
  other arithmetic  17.3 us (4%)
    ppermute x47, waiting for transfers between devices, shift(): return lax.ppermute(array, 'local', moves)  156 us
    ppermute x47, starting transfers between devices, shift(): return lax.ppermute(array, 'local', moves)  53.3 us
    pallas_call x6, Pallas kernels, sum_step(): pl.pallas_call(sum_step_kernel, grid_spec=pltpu.PrefetchScalarGridSpec(nu...  26.1 us
    pallas_call x2, Pallas kernels, term_last(): pl.pallas_call(functools.partial(term_last_kernel, count), grid_spec=pltp...  20.8 us
    pallas_call x2, Pallas kernels, grads_chunk(): pl.pallas_call(kernel, grid_spec=pltpu.PrefetchScalarGridSpec(num_scalar_...  19.5 us
    pallas_call x2, Pallas kernels, attention(): pl.pallas_call(attention_kernel, grid_spec=pltpu.PrefetchScalarGridSpec(n...  16 us
    ppermute x4, starting transfers between devices, end_term(): came.append(lax.ppermute(block, ('node', 'local'), moves))  12.7 us
    unnamed x128, local copies, waits for them, and re-layouts  12.2 us
  transfers between devices with their start and end apart: 65, of which 34 were waited for; matrix products, arithmetic and copies ran while one was open for 8% of the time, Pallas kernels for 23%

profile of v2, /device:TPU:2, one launch (start us, length us, event | category | flops | bytes accessed | tf_op | source)
XLA Modules:
  0.0 390.3 jit_solution(6626666121022185783)
XLA Ops:
  2.2 1.7 fusion.25
  3.9 5.8 %stack.25.idx = s32[9]{0:T(128)} concatenate(s32[1]{0:T(128)} %get-tuple-element.133, s32[1]{0:T(128)} %get-tuple-element.132, s32[1]{0:T(128)} %get-tuple-element.131, s32[1]{0:T(128)} %get-tuple-element.130, s32[1]{0:T(128)} %get-tuple-element.129, s32[1]{0:T(128)} %get-tuple-element.128, s32[1]{0:T(128)} %get-tuple-element.127, s32[1]{0:T(128)} %get-tuple-element.126, ...), dimensions={0} | concatenate | bytes 72 | tf_op jit(solution)/shard_map/stack | solution.py:437
  9.7 4.6 %normed_blocks.1 = (bf16[256,256]{1,0:T(8,128)(2,1)}, bf16[256,256]{1,0:T(8,128)(2,1)}, bf16[256,256]{1,0:T(8,128)(2,1)}, bf16[256,256]{1,0:T(8,128)(2,1)}, bf16...) custom-call(s32[9]{0:T(128)} %stack.25.idx, ...), custom_call_target="tpu_custom_call" | custom-call | flops 8388608 | bytes 4194304 | tf_op jit(solution)/shard_map/normed_blocks/pallas_call | solution.py:70
  14.3 4.6 %collective-permute-start.1 = (bf16[256,256]{1,0:T(8,128)(2,1)}, bf16[256,256]{1,0:T(8,128)(2,1)S(1)}, u32[]{:S(2)}, u32[]{:S(2)}) collective-permute-start(bf16[256,256]{1,0:T(8,128)(2,1)} %get-tuple-element.53), channel_id=1, source_target_pairs={{0,7},{2,5},{4,3},{6,1},{7,0},{5,2},{3,4},{1,6},{8,15},{10,13},{12... | collective-permute-start | bytes 393224 | tf_op jit(solution)/shard_map/ppermute | solution.py:429
  18.9 3.8 collective-permute-done.1.mine.refs_7_.refs_8_
  23.5 4.5 %fusion.weight.weight_other = bf16[3,512,1024]{2,1,0:T(8,128)(2,1)} fusion(bf16[3,512,1024]{2,1,0:T(8,128)(2,1)} %param.8, f32[3,4,1024]{2,1,0:T(4,128)S(1)} %convert_element_type.105), kind=kLoop, calls=%fused_computation.1 | loop fusion | flops 4718592 | bytes 6340608 | tf_op jit(solution)/shard_map/convert_element_type | solution.py:456
  28.6 3.5 sum_first.2
  32.1 2.4 collective-permute-start.15
  34.6 4.0 %collective-permute-start.2 = (bf16[256,256]{1,0:T(8,128)(2,1)S(1)}, bf16[256,256]{1,0:T(8,128)(2,1)S(1)}, u32[]{:S(2)}, u32[]{:S(2)}) collective-permute-start(bf16[256,256]{1,0:T(8,128)(2,1)S(1)} %copy-done.63), channel_id=1, source_target_pairs={{0,5},{2,3},{4,1},{6,0},{7,2},{5,4},{3,6},{1,7},{8,13},{10,11},{12... | collective-permute-start | bytes 393224 | tf_op jit(solution)/shard_map/ppermute | solution.py:429
  38.6 12.2 %collective-permute-done.2.mine_r.refs_6_.refs_7_ = bf16[256,256]{1,0:T(8,128)(2,1)S(1)} collective-permute-done((bf16[256,256]{1,0:T(8,128)(2,1)S(1)}, bf16[256,256]{1,0:T(8,128)(2,1)S(1)}, u32[]{:S(2)}, u32[]{:S(2)}) %collective-permute-start.2) | collective-permute-done | bytes 131104 | tf_op jit(solution)/shard_map/ppermute | solution.py:429
  50.7 4.4 %collective-permute-done.12.mine_l.refs_5_.refs_6_ = bf16[256,256]{1,0:T(8,128)(2,1)S(1)} collective-permute-done((bf16[256,256]{1,0:T(8,128)(2,1)S(1)}, bf16[256,256]{1,0:T(8,128)(2,1)S(1)}, u32[]{:S(2)}, u32[]{:S(2)}) %collective-permute-start.12) | collective-permute-done | bytes 131104 | tf_op jit(solution)/shard_map/ppermute | solution.py:429
  58.0 4.2 %sum_step.6 = (bf16[3,256,512]{2,1,0:T(8,128)(2,1)}, bf16[3,256,512]{2,1,0:T(8,128)(2,1)}) custom-call(s32[1]{0:T(128)} %bitcast.core.refs_0_, bf16[256,256]{1,0:T(8,128)(2,1)} %copy-done.11, bf16[256,256]{1,0:T(8,128)(2,1)} %copy-done.13, bf16[256,256]{1,0:T(8,128)(2,1)} %copy-done.12, bf16[256,256]{1,0:T(8,128)(2,1)} %copy-done.14, ...), custom_call_target="tpu_custom_call" | custom-call | flops 805306368 | bytes 3145728 | tf_op jit(solution)/shard_map/sum_step/pallas_call | solution.py:144
  62.1 2.0 collective-permute-start.18
  67.1 22.0 %collective-permute-done.3.mine_r.refs_4_.refs_5_ = bf16[256,256]{1,0:T(8,128)(2,1)S(1)} collective-permute-done((bf16[256,256]{1,0:T(8,128)(2,1)S(1)}, bf16[256,256]{1,0:T(8,128)(2,1)S(1)}, u32[]{:S(2)}, u32[]{:S(2)}) %collective-permute-start.3) | collective-permute-done | bytes 131104 | tf_op jit(solution)/shard_map/ppermute | solution.py:429
  89.6 3.5 sum_first.3
  97.1 4.4 %sum_step.7 = (bf16[3,256,512]{2,1,0:T(8,128)(2,1)}, bf16[3,256,512]{2,1,0:T(8,128)(2,1)}) custom-call(s32[1]{0:T(128)} %bitcast.core.refs_0_, bf16[256,256]{1,0:T(8,128)(2,1)} %copy-done.15, bf16[256,256]{1,0:T(8,128)(2,1)} %copy-done.17, bf16[256,256]{1,0:T(8,128)(2,1)} %copy-done.16, bf16[256,256]{1,0:T(8,128)(2,1)} %copy-done.18, ...), custom_call_target="tpu_custom_call" | custom-call | flops 805306368 | bytes 3145728 | tf_op jit(solution)/shard_map/sum_step/pallas_call | solution.py:144
  107.4 4.1 %sum_step.9 = (bf16[3,256,512]{2,1,0:T(8,128)(2,1)}, bf16[3,256,512]{2,1,0:T(8,128)(2,1)}) custom-call(s32[1]{0:T(128)} %bitcast.core.refs_0_, bf16[256,256]{1,0:T(8,128)(2,1)} %copy-done.11, bf16[256,256]{1,0:T(8,128)(2,1)} %copy-done.13, bf16[256,256]{1,0:T(8,128)(2,1)} %copy-done.12, bf16[256,256]{1,0:T(8,128)(2,1)} %copy-done.14, ...), custom_call_target="tpu_custom_call" | custom-call | flops 805306368 | bytes 3145728 | tf_op jit(solution)/shard_map/sum_step/pallas_call | solution.py:144
  112.3 13.4 %collective-permute-done.4.mine_r.refs_2_.refs_3_ = bf16[256,256]{1,0:T(8,128)(2,1)S(1)} collective-permute-done((bf16[256,256]{1,0:T(8,128)(2,1)S(1)}, bf16[256,256]{1,0:T(8,128)(2,1)S(1)}, u32[]{:S(2)}, u32[]{:S(2)}) %collective-permute-start.4) | collective-permute-done | bytes 131104 | tf_op jit(solution)/shard_map/ppermute | solution.py:429
  130.5 4.4 %sum_step.8 = (bf16[3,256,512]{2,1,0:T(8,128)(2,1)}, bf16[3,256,512]{2,1,0:T(8,128)(2,1)}) custom-call(s32[1]{0:T(128)} %bitcast.core.refs_0_, bf16[256,256]{1,0:T(8,128)(2,1)} %copy-done.19, bf16[256,256]{1,0:T(8,128)(2,1)} %copy-done.21, bf16[256,256]{1,0:T(8,128)(2,1)} %copy-done.20, bf16[256,256]{1,0:T(8,128)(2,1)} %copy-done.22, ...), custom_call_target="tpu_custom_call" | custom-call | flops 805306368 | bytes 3145728 | tf_op jit(solution)/shard_map/sum_step/pallas_call | solution.py:144
  135.0 1.7 collective-permute-start.21
  137.0 4.8 %collective-permute-done.25.from_left = bf16[3,256,512]{2,1,0:T(8,128)(2,1)S(1)} collective-permute-done((bf16[3,256,512]{2,1,0:T(8,128)(2,1)}, bf16[3,256,512]{2,1,0:T(8,128)(2,1)S(1)}, u32[]{:S(2)}, u32[]{:S(2)}) %collective-permute-start.25) | collective-permute-done | bytes 786464 | tf_op jit(solution)/shard_map/ppermute | solution.py:429
  141.8 4.5 %collective-permute-done.26.from_right = bf16[3,256,512]{2,1,0:T(8,128)(2,1)S(1)} collective-permute-done((bf16[3,256,512]{2,1,0:T(8,128)(2,1)}, bf16[3,256,512]{2,1,0:T(8,128)(2,1)S(1)}, u32[]{:S(2)}, u32[]{:S(2)}) %collective-permute-start.26) | collective-permute-done | bytes 786464 | tf_op jit(solution)/shard_map/ppermute | solution.py:429
  147.3 4.5 %sum_step.10 = (bf16[3,256,512]{2,1,0:T(8,128)(2,1)}, bf16[3,256,512]{2,1,0:T(8,128)(2,1)}) custom-call(s32[1]{0:T(128)} %bitcast.core.refs_0_, bf16[256,256]{1,0:T(8,128)(2,1)} %copy-done.15, bf16[256,256]{1,0:T(8,128)(2,1)} %copy-done.17, bf16[256,256]{1,0:T(8,128)(2,1)} %copy-done.16, bf16[256,256]{1,0:T(8,128)(2,1)} %copy-done.18, ...), custom_call_target="tpu_custom_call" | custom-call | flops 805306368 | bytes 3145728 | tf_op jit(solution)/shard_map/sum_step/pallas_call | solution.py:144
  152.0 1.7 collective-permute-start.28
  155.1 3.6 collective-permute-done.21.from_left
  158.7 4.5 %collective-permute-done.22.from_right = bf16[3,256,512]{2,1,0:T(8,128)(2,1)S(1)} collective-permute-done((bf16[3,256,512]{2,1,0:T(8,128)(2,1)}, bf16[3,256,512]{2,1,0:T(8,128)(2,1)S(1)}, u32[]{:S(2)}, u32[]{:S(2)}) %collective-permute-start.22) | collective-permute-done | bytes 786464 | tf_op jit(solution)/shard_map/ppermute | solution.py:429
  164.2 8.0 %attention.2 = (bf16[256,512]{1,0:T(8,128)(2,1)}, bf16[3,256,512]{2,1,0:T(8,128)(2,1)}, f32[256,128]{1,0:T(8,128)}) custom-call(s32[1]{0:T(128)} %bitcast.core.refs_0_, bf16[256,256]{1,0:T(8,128)(2,1)} %get-tuple-element.52.mine.refs_0_.refs_1_, bf16[256,256]{1,0:T(8,128)(2,1)} %copy-done.23, bf16[3,512,1024]{2,1,0:T(8,128)(2,1)} %fusion.weight.weight_other, ...), custom_call_target="tpu_custom_call" | custom-call | flops 402653184 | bytes 3145728 | tf_op jit(solution)/shard_map/attention/pallas_call | solution.py:227
  172.5 1.7 collective-permute-start.32
  175.5 4.6 %collective-permute-done.28.from_right = bf16[3,256,512]{2,1,0:T(8,128)(2,1)} collective-permute-done((bf16[3,256,512]{2,1,0:T(8,128)(2,1)}, bf16[3,256,512]{2,1,0:T(8,128)(2,1)}, u32[]{:S(2)}, u32[]{:S(2)}) %collective-permute-start.28) | collective-permute-done | bytes 786464 | tf_op jit(solution)/shard_map/ppermute | solution.py:429
  180.1 4.5 %sum_step.11 = (bf16[3,256,512]{2,1,0:T(8,128)(2,1)}, bf16[3,256,512]{2,1,0:T(8,128)(2,1)}) custom-call(s32[1]{0:T(128)} %bitcast.core.refs_0_, bf16[256,256]{1,0:T(8,128)(2,1)} %copy-done.19, bf16[256,256]{1,0:T(8,128)(2,1)} %copy-done.21, bf16[256,256]{1,0:T(8,128)(2,1)} %copy-done.20, bf16[256,256]{1,0:T(8,128)(2,1)} %copy-done.22, ...), custom_call_target="tpu_custom_call" | custom-call | flops 805306368 | bytes 3145728 | tf_op jit(solution)/shard_map/sum_step/pallas_call | solution.py:144
  184.9 1.7 collective-permute-start.30
  186.6 6.3 %collective-permute-done.31.refs_1_.refs_17_ = bf16[3,256,512]{2,1,0:T(8,128)(2,1)S(1)} collective-permute-done((bf16[3,256,512]{2,1,0:T(8,128)(2,1)}, bf16[3,256,512]{2,1,0:T(8,128)(2,1)S(1)}, u32[]{:S(2)}, u32[]{:S(2)}) %collective-permute-start.31) | collective-permute-done | bytes 786464 | tf_op jit(solution)/shard_map/ppermute | solution.py:429
  193.8 3.1 collective-permute-done.32.refs_2_.refs_18_
  197.2 12.6 %collective-permute-done.29.from_left = bf16[3,256,512]{2,1,0:T(8,128)(2,1)S(1)} collective-permute-done((bf16[3,256,512]{2,1,0:T(8,128)(2,1)}, bf16[3,256,512]{2,1,0:T(8,128)(2,1)S(1)}, u32[]{:S(2)}, u32[]{:S(2)}) %collective-permute-start.29) | collective-permute-done | bytes 786464 | tf_op jit(solution)/shard_map/ppermute | solution.py:429
  209.8 4.0 %collective-permute-done.30.from_right = bf16[3,256,512]{2,1,0:T(8,128)(2,1)S(1)} collective-permute-done((bf16[3,256,512]{2,1,0:T(8,128)(2,1)}, bf16[3,256,512]{2,1,0:T(8,128)(2,1)S(1)}, u32[]{:S(2)}, u32[]{:S(2)}) %collective-permute-start.30) | collective-permute-done | bytes 786464 | tf_op jit(solution)/shard_map/ppermute | solution.py:429
  214.7 8.0 %attention.3 = (bf16[256,512]{1,0:T(8,128)(2,1)}, bf16[3,256,512]{2,1,0:T(8,128)(2,1)}, f32[256,128]{1,0:T(8,128)}) custom-call(s32[1]{0:T(128)} %bitcast.core.refs_0_, bf16[256,256]{1,0:T(8,128)(2,1)} %get-tuple-element.52.mine.refs_0_.refs_1_, bf16[256,256]{1,0:T(8,128)(2,1)} %copy-done.23, bf16[3,512,1024]{2,1,0:T(8,128)(2,1)} %fusion.weight.weight_other, ...), custom_call_target="tpu_custom_call" | custom-call | flops 402653184 | bytes 3145728 | tf_op jit(solution)/shard_map/attention/pallas_call | solution.py:227
  225.3 1.8 collective-permute-start.35
  227.1 2.0 collective-permute-done.34.refs_4_.refs_20_
  229.3 1.7 collective-permute-start.39
  231.4 20.9 %collective-permute-done.39.refs_1_.refs_18_ = bf16[3,128,512]{2,1,0:T(8,128)(2,1)S(1)} collective-permute-done((bf16[3,128,512]{2,1,0:T(8,128)(2,1)S(1)}, bf16[3,128,512]{2,1,0:T(8,128)(2,1)S(1)}, u32[]{:S(2)}, u32[]{:S(2)}) %collective-permute-start.39) | collective-permute-done | bytes 393248 | tf_op jit(solution)/shard_map/ppermute | solution.py:429
  252.3 2.5 collective-permute-start.41
  255.9 5.1 %stack.26.idx = s32[8]{0:T(128)S(1)} concatenate(s32[1]{0:T(128)} %get-tuple-element.133, s32[1]{0:T(128)} %get-tuple-element.125, s32[1]{0:T(128)} %get-tuple-element.132, s32[1]{0:T(128)} %get-tuple-element.134, s32[1]{0:T(128)} %get-tuple-element.131, s32[1]{0:T(128)} %get-tuple-element.124, s32[1]{0:T(128)} %get-tuple-element.130, s32[1]{0:T(128)} %get-tuple-element.129), dimensions={0} | concatenate | bytes 64 | tf_op jit(solution)/shard_map/stack | solution.py:505
  261.8 1.7 collective-permute-start.37
  264.6 1.7 collective-permute-start.43
  266.7 5.6 %concatenate.25.idx = s32[24]{0:T(128)} concatenate(s32[1]{0:T(128)} %get-tuple-element.133, s32[1]{0:T(128)} %get-tuple-element.125, s32[1]{0:T(128)} %get-tuple-element.132, s32[1]{0:T(128)} %get-tuple-element.134, s32[1]{0:T(128)} %get-tuple-element.131, s32[1]{0:T(128)} %get-tuple-element.124, s32[1]{0:T(128)} %get-tuple-element.130, s32[1]{0:T(128)} %get-tuple-element.129, ...), dimensions={0} | concatenate | bytes 192 | tf_op jit(solution)/shard_map/concatenate | solution.py:508
  272.3 1.9 collective-permute-done.37.refs_7_.refs_23_
  274.2 1.7 collective-permute-start.53
  276.2 6.3 %collective-permute-done.43.refs_5_.refs_22_ = bf16[3,128,512]{2,1,0:T(8,128)(2,1)S(1)} collective-permute-done((bf16[3,128,512]{2,1,0:T(8,128)(2,1)}, bf16[3,128,512]{2,1,0:T(8,128)(2,1)S(1)}, u32[]{:S(2)}, u32[]{:S(2)}) %collective-permute-start.43) | collective-permute-done | bytes 393248 | tf_op jit(solution)/shard_map/ppermute | solution.py:429
  283.2 1.7 collective-permute-start.45
  286.1 9.9 %term_first.1.before = f32[8,256,512]{2,1,0:T(8,128)} custom-call(s32[8]{0:T(128)} %copy-done.57, bf16[3,512,1024]{2,1,0:T(8,128)(2,1)} %fusion.weight.weight_other, bf16[3,256,512]{2,1,0:T(8,128)(2,1)} %get-tuple-element.85.refs_0_.refs_16_, bf16[3,256,512]{2,1,0:T(8,128)(2,1)} %copy-done.4, bf16[3,256,512]{2,1,0:T(8,128)(2,1)} %copy-done.5, ...), custom_call_target="tpu_custom_call" | custom-call | flops 3221225472 | bytes 6291456 | tf_op jit(solution)/shard_map/term_first/pallas_call | solution.py:350
  297.4 10.4 %term_last.2 = (f32[4,128,512]{2,1,0:T(8,128)}, bf16[4,128,512]{2,1,0:T(8,128)(2,1)}) custom-call(s32[24]{0:T(128)} %concatenate.25.idx, bf16[3,512,1024]{2,1,0:T(8,128)(2,1)} %fusion.weight.weight_other, f32[8,256,512]{2,1,0:T(8,128)} %term_first.1.before, bf16[3,128,512]{2,1,0:T(8,128)(2,1)} %copy-done.2, bf16[3,128,512]{2,1,0:T(8,128)(2,1)} %copy-done.26, ...), custom_call_target="tpu_custom_call" | custom-call | flops 1610612736 | bytes 3145728 | tf_op jit(solution)/shard_map/term_last/pallas_call | solution.py:386
  307.8 1.8 collective-permute-start.55
  311.0 8.5 %collective-permute-done.55.refs_3_.refs_29_ = bf16[3,128,512]{2,1,0:T(8,128)(2,1)S(1)} collective-permute-done((bf16[3,128,512]{2,1,0:T(8,128)(2,1)}, bf16[3,128,512]{2,1,0:T(8,128)(2,1)S(1)}, u32[]{:S(2)}, u32[]{:S(2)}) %collective-permute-start.55) | collective-permute-done | bytes 393248 | tf_op jit(solution)/shard_map/ppermute | solution.py:429
  319.5 1.7 collective-permute-start.57
  326.6 3.7 collective-permute-done.57.refs_5_.refs_31_
  334.1 1.8 pad_maximum_fusion
  339.3 10.4 %term_last.3 = (f32[4,128,512]{2,1,0:T(8,128)}, bf16[4,128,512]{2,1,0:T(8,128)(2,1)}) custom-call(s32[24]{0:T(128)} %concatenate.25.idx, bf16[3,512,1024]{2,1,0:T(8,128)(2,1)} %fusion.weight.weight_other, f32[8,256,512]{2,1,0:T(8,128)} %term_first.1.before, bf16[3,128,512]{2,1,0:T(8,128)(2,1)} %copy-done.3, ...), custom_call_target="tpu_custom_call" | custom-call | flops 1610612736 | bytes 3145728 | tf_op jit(solution)/shard_map/term_last/pallas_call | solution.py:386
  350.8 2.9 collective-permute-start.49
  353.6 3.7 collective-permute-start.50
  358.9 8.5 %grads.2.refs_35_ = f32[3,512,1024]{2,1,0:T(8,128)} custom-call(s32[1]{0:T(128)} %bitcast.core.refs_0_, bf16[256,256]{1,0:T(8,128)(2,1)} %get-tuple-element.52.mine.refs_0_.refs_1_, bf16[256,256]{1,0:T(8,128)(2,1)} %copy-done.20, bf16[256,256]{1,0:T(8,128)(2,1)} %copy-done.19, bf16[256,256]{1,0:T(8,128)(2,1)} %copy-done.16, bf16[256,256]{1,0:T(8,128)(2,1)} %copy-done.15, ...), custom_call_target="tpu_custom_call" | custom-call | flops 3221225472 | bytes 12582912 | tf_op jit(solution)/shard_map/grads/pallas_call | solution.py:312
  368.2 3.4 collective-permute-done.62
  371.7 1.9 collective-permute-start.63
  373.7 4.2 %collective-permute-start.64 = (bf16[128,512]{1,0:T(8,128)(2,1)S(1)}, bf16[128,512]{1,0:T(8,128)(2,1)S(1)}, u32[]{:S(2)}, u32[]{:S(2)}) collective-permute-start(bf16[128,512]{1,0:T(8,128)(2,1)S(1)} %get-tuple-element.117), channel_id=1, source_target_pairs={{0,1},{1,0},{2,9},{3,8},{4,17},{5,16},{6,25},{7,24},{8,3},{9,2},{1... | collective-permute-start | bytes 393224 | tf_op jit(solution)/shard_map/ppermute | solution.py:537
  377.9 11.0 %grads.3 = f32[3,512,1024]{2,1,0:T(8,128)} custom-call(s32[1]{0:T(128)} %bitcast.core.refs_0_, bf16[256,256]{1,0:T(8,128)(2,1)} %get-tuple-element.52.mine.refs_0_.refs_1_, bf16[256,256]{1,0:T(8,128)(2,1)} %copy-done.20, bf16[256,256]{1,0:T(8,128)(2,1)} %copy-done.19, bf16[256,256]{1,0:T(8,128)(2,1)} %copy-done.16, ...), custom_call_target="tpu_custom_call", output_to_operand_aliasing={{}: (35, {})} | custom-call | flops 3221225472 | bytes 12582912 | tf_op jit(solution)/shard_map/grads/pallas_call | solution.py:312
  (252 shorter events, 61.0 us)
Async XLA Ops:
  14.3 8.4 %collective-permute-start.1 = (bf16[256,256]{1,0:T(8,128)(2,1)}, bf16[256,256]{1,0:T(8,128)(2,1)S(1)}, u32[]{:S(2)}, u32[]{:S(2)}) collective-permute-start(bf16[256,256]{1,0:T(8,128)(2,1)} %get-tuple-element.53), channel_id=1, source_target_pairs={{0,7},{2,5},{4,3},{6,1},{7,0},{5,2},{3,4},{1,6},{8,15},{10,13},{12... | collective-permute-start | bytes 393224 | tf_op jit(solution)/shard_map/ppermute | solution.py:429
  22.7 5.2 %collective-permute-start.14 = (bf16[256,256]{1,0:T(8,128)(2,1)S(1)}, bf16[256,256]{1,0:T(8,128)(2,1)S(1)}, u32[]{:S(2)}, u32[]{:S(2)}) collective-permute-start(bf16[256,256]{1,0:T(8,128)(2,1)S(1)} %collective-permute-done.1.mine.refs_7_.refs_8_), channel_id=1, source_target_pairs={{0,8},{8,0},{16,24},{24,16},{1,9},{9,1},{17,25},{25,17},{2,10},{10... | collective-permute-start | bytes 393224 | tf_op jit(solution)/shard_map/ppermute | solution.py:432
  32.1 24.3 %collective-permute-start.15 = (bf16[3,128,512]{2,1,0:T(8,128)(2,1)}, bf16[3,128,512]{2,1,0:T(8,128)(2,1)S(1)}, u32[]{:S(2)}, u32[]{:S(2)}) collective-permute-start(bf16[3,128,512]{2,1,0:T(8,128)(2,1)} %get-tuple-element.66), channel_id=1, source_target_pairs={{0,2},{2,4},{4,6},{6,7},{7,5},{5,3},{3,1},{1,0},{8,10},{10,12},{12... | collective-permute-start | bytes 1179656 | tf_op jit(solution)/shard_map/ppermute | solution.py:429
  34.5 21.9 %collective-permute-start.16 = (bf16[3,128,512]{2,1,0:T(8,128)(2,1)}, bf16[3,128,512]{2,1,0:T(8,128)(2,1)S(1)}, u32[]{:S(2)}, u32[]{:S(2)}) collective-permute-start(bf16[3,128,512]{2,1,0:T(8,128)(2,1)} %get-tuple-element.67), channel_id=1, source_target_pairs={{0,1},{2,0},{4,2},{6,4},{7,6},{5,7},{3,5},{1,3},{8,9},{10,8},{12,1... | collective-permute-start | bytes 1179656 | tf_op jit(solution)/shard_map/ppermute | solution.py:429
  34.6 16.2 %collective-permute-start.2 = (bf16[256,256]{1,0:T(8,128)(2,1)S(1)}, bf16[256,256]{1,0:T(8,128)(2,1)S(1)}, u32[]{:S(2)}, u32[]{:S(2)}) collective-permute-start(bf16[256,256]{1,0:T(8,128)(2,1)S(1)} %copy-done.63), channel_id=1, source_target_pairs={{0,5},{2,3},{4,1},{6,0},{7,2},{5,4},{3,6},{1,7},{8,13},{10,11},{12... | collective-permute-start | bytes 393224 | tf_op jit(solution)/shard_map/ppermute | solution.py:429
  38.5 16.6 %collective-permute-start.12 = (bf16[256,256]{1,0:T(8,128)(2,1)S(1)}, bf16[256,256]{1,0:T(8,128)(2,1)S(1)}, u32[]{:S(2)}, u32[]{:S(2)}) collective-permute-start(bf16[256,256]{1,0:T(8,128)(2,1)S(1)} %copy-done.62), channel_id=1, source_target_pairs={{0,6},{2,7},{4,5},{6,3},{7,1},{5,0},{3,2},{1,4},{8,14},{10,15},{12... | collective-permute-start | bytes 393224 | tf_op jit(solution)/shard_map/ppermute | solution.py:429
  50.7 4.4 %collective-permute-start.11 = (bf16[256,256]{1,0:T(8,128)(2,1)S(1)}, bf16[256,256]{1,0:T(8,128)(2,1)S(1)}, u32[]{:S(2)}, u32[]{:S(2)}) collective-permute-start(bf16[256,256]{1,0:T(8,128)(2,1)S(1)} %collective-permute-done.2.mine_r.refs_6_.refs_7_), channel_id=1, source_target_pairs={{0,8},{8,0},{16,24},{24,16},{1,9},{9,1},{17,25},{25,17},{2,10},{10... | collective-permute-start | bytes 393224 | tf_op jit(solution)/shard_map/ppermute | solution.py:432
  55.1 1.3 collective-permute-start.13
  62.1 33.1 %collective-permute-start.17 = (bf16[3,256,512]{2,1,0:T(8,128)(2,1)}, bf16[3,256,512]{2,1,0:T(8,128)(2,1)S(1)}, u32[]{:S(2)}, u32[]{:S(2)}) collective-permute-start(bf16[3,256,512]{2,1,0:T(8,128)(2,1)} %get-tuple-element.68), channel_id=1, source_target_pairs={{0,2},{2,4},{4,6},{6,7},{7,5},{5,3},{3,1},{1,0},{8,10},{10,12},{12... | collective-permute-start | bytes 2359304 | tf_op jit(solution)/shard_map/ppermute | solution.py:429
  62.1 33.1 %collective-permute-start.18 = (bf16[3,256,512]{2,1,0:T(8,128)(2,1)}, bf16[3,256,512]{2,1,0:T(8,128)(2,1)S(1)}, u32[]{:S(2)}, u32[]{:S(2)}) collective-permute-start(bf16[3,256,512]{2,1,0:T(8,128)(2,1)} %get-tuple-element.69), channel_id=1, source_target_pairs={{0,1},{2,0},{4,2},{6,4},{7,6},{5,7},{3,5},{1,3},{8,9},{10,8},{12,1... | collective-permute-start | bytes 2359304 | tf_op jit(solution)/shard_map/ppermute | solution.py:429
  64.2 24.9 %collective-permute-start.3 = (bf16[256,256]{1,0:T(8,128)(2,1)S(1)}, bf16[256,256]{1,0:T(8,128)(2,1)S(1)}, u32[]{:S(2)}, u32[]{:S(2)}) collective-permute-start(bf16[256,256]{1,0:T(8,128)(2,1)S(1)} %copy-done.61), channel_id=1, source_target_pairs={{0,3},{2,1},{4,0},{6,2},{7,4},{5,6},{3,7},{1,5},{8,11},{10,9},{12,... | collective-permute-start | bytes 393224 | tf_op jit(solution)/shard_map/ppermute | solution.py:429
  65.6 23.6 %collective-permute-start.9 = (bf16[256,256]{1,0:T(8,128)(2,1)S(1)}, bf16[256,256]{1,0:T(8,128)(2,1)S(1)}, u32[]{:S(2)}, u32[]{:S(2)}) collective-permute-start(bf16[256,256]{1,0:T(8,128)(2,1)S(1)} %copy-done.60), channel_id=1, source_target_pairs={{0,4},{2,6},{4,7},{6,5},{7,3},{5,1},{3,0},{1,2},{8,12},{10,14},{12... | collective-permute-start | bytes 393224 | tf_op jit(solution)/shard_map/ppermute | solution.py:429
  89.1 5.4 %collective-permute-start.8 = (bf16[256,256]{1,0:T(8,128)(2,1)S(1)}, bf16[256,256]{1,0:T(8,128)(2,1)S(1)}, u32[]{:S(2)}, u32[]{:S(2)}) collective-permute-start(bf16[256,256]{1,0:T(8,128)(2,1)S(1)} %collective-permute-done.3.mine_r.refs_4_.refs_5_), channel_id=1, source_target_pairs={{0,8},{8,0},{16,24},{24,16},{1,9},{9,1},{17,25},{25,17},{2,10},{10... | collective-permute-start | bytes 393224 | tf_op jit(solution)/shard_map/ppermute | solution.py:432
  89.2 6.0 %collective-permute-start.10 = (bf16[256,256]{1,0:T(8,128)(2,1)S(1)}, bf16[256,256]{1,0:T(8,128)(2,1)S(1)}, u32[]{:S(2)}, u32[]{:S(2)}) collective-permute-start(bf16[256,256]{1,0:T(8,128)(2,1)S(1)} %collective-permute-done.9.mine_l.refs_3_.refs_4_), channel_id=1, source_target_pairs={{0,8},{8,0},{16,24},{24,16},{1,9},{9,1},{17,25},{25,17},{2,10},{10... | collective-permute-start | bytes 393224 | tf_op jit(solution)/shard_map/ppermute | solution.py:432
  93.1 11.8 %collective-permute-start.23 = (bf16[3,128,512]{2,1,0:T(8,128)(2,1)}, bf16[3,128,512]{2,1,0:T(8,128)(2,1)S(1)}, u32[]{:S(2)}, u32[]{:S(2)}) collective-permute-start(bf16[3,128,512]{2,1,0:T(8,128)(2,1)} %get-tuple-element.75), channel_id=1, source_target_pairs={{0,2},{2,4},{4,6},{6,7},{7,5},{5,3},{3,1},{1,0},{8,10},{10,12},{12... | collective-permute-start | bytes 1179656 | tf_op jit(solution)/shard_map/ppermute | solution.py:429
  94.5 12.1 %collective-permute-start.24 = (bf16[3,128,512]{2,1,0:T(8,128)(2,1)}, bf16[3,128,512]{2,1,0:T(8,128)(2,1)S(1)}, u32[]{:S(2)}, u32[]{:S(2)}) collective-permute-start(bf16[3,128,512]{2,1,0:T(8,128)(2,1)} %get-tuple-element.76), channel_id=1, source_target_pairs={{0,1},{2,0},{4,2},{6,4},{7,6},{5,7},{3,5},{1,3},{8,9},{10,8},{12,1... | collective-permute-start | bytes 1179656 | tf_op jit(solution)/shard_map/ppermute | solution.py:429
  101.5 27.1 %collective-permute-start.19 = (bf16[3,256,512]{2,1,0:T(8,128)(2,1)}, bf16[3,256,512]{2,1,0:T(8,128)(2,1)S(1)}, u32[]{:S(2)}, u32[]{:S(2)}) collective-permute-start(bf16[3,256,512]{2,1,0:T(8,128)(2,1)} %get-tuple-element.70), channel_id=1, source_target_pairs={{0,2},{2,4},{4,6},{6,7},{7,5},{5,3},{3,1},{1,0},{8,10},{10,12},{12... | collective-permute-start | bytes 2359304 | tf_op jit(solution)/shard_map/ppermute | solution.py:429
  102.9 25.8 %collective-permute-start.20 = (bf16[3,256,512]{2,1,0:T(8,128)(2,1)}, bf16[3,256,512]{2,1,0:T(8,128)(2,1)S(1)}, u32[]{:S(2)}, u32[]{:S(2)}) collective-permute-start(bf16[3,256,512]{2,1,0:T(8,128)(2,1)} %get-tuple-element.71), channel_id=1, source_target_pairs={{0,1},{2,0},{4,2},{6,4},{7,6},{5,7},{3,5},{1,3},{8,9},{10,8},{12,1... | collective-permute-start | bytes 2359304 | tf_op jit(solution)/shard_map/ppermute | solution.py:429
  103.5 22.1 %collective-permute-start.4 = (bf16[256,256]{1,0:T(8,128)(2,1)S(1)}, bf16[256,256]{1,0:T(8,128)(2,1)S(1)}, u32[]{:S(2)}, u32[]{:S(2)}) collective-permute-start(bf16[256,256]{1,0:T(8,128)(2,1)S(1)} %copy-done.59), channel_id=1, source_target_pairs={{0,1},{2,0},{4,2},{6,4},{7,6},{5,7},{3,5},{1,3},{8,9},{10,8},{12,1... | collective-permute-start | bytes 393224 | tf_op jit(solution)/shard_map/ppermute | solution.py:429
  104.9 21.0 %collective-permute-start.6 = (bf16[256,256]{1,0:T(8,128)(2,1)S(1)}, bf16[256,256]{1,0:T(8,128)(2,1)S(1)}, u32[]{:S(2)}, u32[]{:S(2)}) collective-permute-start(bf16[256,256]{1,0:T(8,128)(2,1)S(1)} %copy-done.58), channel_id=1, source_target_pairs={{0,2},{2,4},{4,6},{6,7},{7,5},{5,3},{3,1},{1,0},{8,10},{10,12},{12... | collective-permute-start | bytes 393224 | tf_op jit(solution)/shard_map/ppermute | solution.py:429
  111.5 30.3 %collective-permute-start.25 = (bf16[3,256,512]{2,1,0:T(8,128)(2,1)}, bf16[3,256,512]{2,1,0:T(8,128)(2,1)S(1)}, u32[]{:S(2)}, u32[]{:S(2)}) collective-permute-start(bf16[3,256,512]{2,1,0:T(8,128)(2,1)} %get-tuple-element.77), channel_id=1, source_target_pairs={{0,2},{2,4},{4,6},{6,7},{7,5},{5,3},{3,1},{1,0},{8,10},{10,12},{12... | collective-permute-start | bytes 2359304 | tf_op jit(solution)/shard_map/ppermute | solution.py:429
  125.6 20.7 %collective-permute-start.26 = (bf16[3,256,512]{2,1,0:T(8,128)(2,1)}, bf16[3,256,512]{2,1,0:T(8,128)(2,1)S(1)}, u32[]{:S(2)}, u32[]{:S(2)}) collective-permute-start(bf16[3,256,512]{2,1,0:T(8,128)(2,1)} %get-tuple-element.78), channel_id=1, source_target_pairs={{0,1},{2,0},{4,2},{6,4},{7,6},{5,7},{3,5},{1,3},{8,9},{10,8},{12,1... | collective-permute-start | bytes 2359304 | tf_op jit(solution)/shard_map/ppermute | solution.py:429
  125.9 1.3 collective-permute-start.5
  127.3 1.3 collective-permute-start.7
  135.0 23.7 %collective-permute-start.21 = (bf16[3,256,512]{2,1,0:T(8,128)(2,1)}, bf16[3,256,512]{2,1,0:T(8,128)(2,1)S(1)}, u32[]{:S(2)}, u32[]{:S(2)}) collective-permute-start(bf16[3,256,512]{2,1,0:T(8,128)(2,1)} %get-tuple-element.72), channel_id=1, source_target_pairs={{0,2},{2,4},{4,6},{6,7},{7,5},{5,3},{3,1},{1,0},{8,10},{10,12},{12... | collective-permute-start | bytes 2359304 | tf_op jit(solution)/shard_map/ppermute | solution.py:429
  136.7 26.5 %collective-permute-start.22 = (bf16[3,256,512]{2,1,0:T(8,128)(2,1)}, bf16[3,256,512]{2,1,0:T(8,128)(2,1)S(1)}, u32[]{:S(2)}, u32[]{:S(2)}) collective-permute-start(bf16[3,256,512]{2,1,0:T(8,128)(2,1)} %get-tuple-element.73), channel_id=1, source_target_pairs={{0,1},{2,0},{4,2},{6,4},{7,6},{5,7},{3,5},{1,3},{8,9},{10,8},{12,1... | collective-permute-start | bytes 2359304 | tf_op jit(solution)/shard_map/ppermute | solution.py:429
  137.0 18.1 %collective-permute-start = (bf16[256,256]{1,0:T(8,128)(2,1)S(1)}, bf16[256,256]{1,0:T(8,128)(2,1)S(1)}, u32[]{:S(2)}, u32[]{:S(2)}) collective-permute-start(bf16[256,256]{1,0:T(8,128)(2,1)S(1)} %copy-done.10), channel_id=1, source_target_pairs={{0,8},{8,0},{16,24},{24,16},{1,9},{9,1},{17,25},{25,17},{2,10},{10... | collective-permute-start | bytes 393224 | tf_op jit(solution)/shard_map/ppermute | solution.py:432
  151.7 23.8 %collective-permute-start.27 = (bf16[3,256,512]{2,1,0:T(8,128)(2,1)}, bf16[3,256,512]{2,1,0:T(8,128)(2,1)S(1)}, u32[]{:S(2)}, u32[]{:S(2)}) collective-permute-start(bf16[3,256,512]{2,1,0:T(8,128)(2,1)} %get-tuple-element.79), channel_id=1, source_target_pairs={{0,2},{2,4},{4,6},{6,7},{7,5},{5,3},{3,1},{1,0},{8,10},{10,12},{12... | collective-permute-start | bytes 2359304 | tf_op jit(solution)/shard_map/ppermute | solution.py:429
  152.0 28.2 %collective-permute-start.28 = (bf16[3,256,512]{2,1,0:T(8,128)(2,1)}, bf16[3,256,512]{2,1,0:T(8,128)(2,1)}, u32[]{:S(2)}, u32[]{:S(2)}) collective-permute-start(bf16[3,256,512]{2,1,0:T(8,128)(2,1)} %get-tuple-element.80), channel_id=1, source_target_pairs={{0,1},{2,0},{4,2},{6,4},{7,6},{5,7},{3,5},{1,3},{8,9},{10,8},{12,1... | collective-permute-start | bytes 2359304 | tf_op jit(solution)/shard_map/ppermute | solution.py:429
  172.2 20.7 %collective-permute-start.31 = (bf16[3,256,512]{2,1,0:T(8,128)(2,1)}, bf16[3,256,512]{2,1,0:T(8,128)(2,1)S(1)}, u32[]{:S(2)}, u32[]{:S(2)}) collective-permute-start(bf16[3,256,512]{2,1,0:T(8,128)(2,1)} %get-tuple-element.85.refs_0_.refs_16_), channel_id=1, source_target_pairs={{0,2},{2,4},{4,6},{6,7},{7,5},{5,3},{3,1},{1,0},{8,10},{10,12},{12... | collective-permute-start | bytes 2359304 | tf_op jit(solution)/shard_map/ppermute | solution.py:429
  172.5 24.4 %collective-permute-start.32 = (bf16[3,256,512]{2,1,0:T(8,128)(2,1)}, bf16[3,256,512]{2,1,0:T(8,128)(2,1)S(1)}, u32[]{:S(2)}, u32[]{:S(2)}) collective-permute-start(bf16[3,256,512]{2,1,0:T(8,128)(2,1)} %get-tuple-element.85.refs_0_.refs_16_), channel_id=1, source_target_pairs={{0,1},{2,0},{4,2},{6,4},{7,6},{5,7},{3,5},{1,3},{8,9},{10,8},{12,1... | collective-permute-start | bytes 2359304 | tf_op jit(solution)/shard_map/ppermute | solution.py:429
  184.6 25.2 %collective-permute-start.29 = (bf16[3,256,512]{2,1,0:T(8,128)(2,1)}, bf16[3,256,512]{2,1,0:T(8,128)(2,1)S(1)}, u32[]{:S(2)}, u32[]{:S(2)}) collective-permute-start(bf16[3,256,512]{2,1,0:T(8,128)(2,1)} %get-tuple-element.81), channel_id=1, source_target_pairs={{0,2},{2,4},{4,6},{6,7},{7,5},{5,3},{3,1},{1,0},{8,10},{10,12},{12... | collective-permute-start | bytes 2359304 | tf_op jit(solution)/shard_map/ppermute | solution.py:429
  184.9 28.9 %collective-permute-start.30 = (bf16[3,256,512]{2,1,0:T(8,128)(2,1)}, bf16[3,256,512]{2,1,0:T(8,128)(2,1)S(1)}, u32[]{:S(2)}, u32[]{:S(2)}) collective-permute-start(bf16[3,256,512]{2,1,0:T(8,128)(2,1)} %get-tuple-element.82), channel_id=1, source_target_pairs={{0,1},{2,0},{4,2},{6,4},{7,6},{5,7},{3,5},{1,3},{8,9},{10,8},{12,1... | collective-permute-start | bytes 2359304 | tf_op jit(solution)/shard_map/ppermute | solution.py:429
  192.9 32.4 %collective-permute-start.33 = (bf16[3,256,512]{2,1,0:T(8,128)(2,1)S(1)}, bf16[3,256,512]{2,1,0:T(8,128)(2,1)}, u32[]{:S(2)}, u32[]{:S(2)}) collective-permute-start(bf16[3,256,512]{2,1,0:T(8,128)(2,1)S(1)} %collective-permute-done.31.refs_1_.refs_17_), channel_id=1, source_target_pairs={{0,2},{2,4},{4,6},{6,7},{7,5},{5,3},{3,1},{1,0},{8,10},{10,12},{12... | collective-permute-start | bytes 2359304 | tf_op jit(solution)/shard_map/ppermute | solution.py:429
  196.9 32.2 %collective-permute-start.34 = (bf16[3,256,512]{2,1,0:T(8,128)(2,1)S(1)}, bf16[3,256,512]{2,1,0:T(8,128)(2,1)}, u32[]{:S(2)}, u32[]{:S(2)}) collective-permute-start(bf16[3,256,512]{2,1,0:T(8,128)(2,1)S(1)} %collective-permute-done.32.refs_2_.refs_18_), channel_id=1, source_target_pairs={{0,1},{2,0},{4,2},{6,4},{7,6},{5,7},{3,5},{1,3},{8,9},{10,8},{12,1... | collective-permute-start | bytes 2359304 | tf_op jit(solution)/shard_map/ppermute | solution.py:429
  225.3 35.6 %collective-permute-start.35 = (bf16[3,256,512]{2,1,0:T(8,128)(2,1)}, bf16[3,256,512]{2,1,0:T(8,128)(2,1)S(1)}, u32[]{:S(2)}, u32[]{:S(2)}) collective-permute-start(bf16[3,256,512]{2,1,0:T(8,128)(2,1)} %collective-permute-done.33.refs_3_.refs_19_), channel_id=1, source_target_pairs={{0,2},{2,4},{4,6},{6,7},{7,5},{5,3},{3,1},{1,0},{8,10},{10,12},{12... | collective-permute-start | bytes 2359304 | tf_op jit(solution)/shard_map/ppermute | solution.py:429
  229.0 34.5 %collective-permute-start.36 = (bf16[3,256,512]{2,1,0:T(8,128)(2,1)}, bf16[3,256,512]{2,1,0:T(8,128)(2,1)S(1)}, u32[]{:S(2)}, u32[]{:S(2)}) collective-permute-start(bf16[3,256,512]{2,1,0:T(8,128)(2,1)} %collective-permute-done.34.refs_4_.refs_20_), channel_id=1, source_target_pairs={{0,1},{2,0},{4,2},{6,4},{7,6},{5,7},{3,5},{1,3},{8,9},{10,8},{12,1... | collective-permute-start | bytes 2359304 | tf_op jit(solution)/shard_map/ppermute | solution.py:429
  229.3 22.9 %collective-permute-start.39 = (bf16[3,128,512]{2,1,0:T(8,128)(2,1)S(1)}, bf16[3,128,512]{2,1,0:T(8,128)(2,1)S(1)}, u32[]{:S(2)}, u32[]{:S(2)}) collective-permute-start(bf16[3,128,512]{2,1,0:T(8,128)(2,1)S(1)} %get-tuple-element.88.refs_0_.refs_17_), channel_id=1, source_target_pairs={{0,2},{2,4},{4,6},{6,7},{7,5},{5,3},{3,1},{1,0},{8,10},{10,12},{12... | collective-permute-start | bytes 1179656 | tf_op jit(solution)/shard_map/ppermute | solution.py:429
  231.1 24.5 %collective-permute-start.40 = (bf16[3,128,512]{2,1,0:T(8,128)(2,1)S(1)}, bf16[3,128,512]{2,1,0:T(8,128)(2,1)S(1)}, u32[]{:S(2)}, u32[]{:S(2)}) collective-permute-start(bf16[3,128,512]{2,1,0:T(8,128)(2,1)S(1)} %get-tuple-element.88.refs_0_.refs_17_), channel_id=1, source_target_pairs={{0,1},{2,0},{4,2},{6,4},{7,6},{5,7},{3,5},{1,3},{8,9},{10,8},{12,1... | collective-permute-start | bytes 1179656 | tf_op jit(solution)/shard_map/ppermute | solution.py:429
  252.3 12.4 %collective-permute-start.41 = (bf16[3,128,512]{2,1,0:T(8,128)(2,1)S(1)}, bf16[3,128,512]{2,1,0:T(8,128)(2,1)}, u32[]{:S(2)}, u32[]{:S(2)}) collective-permute-start(bf16[3,128,512]{2,1,0:T(8,128)(2,1)S(1)} %collective-permute-done.39.refs_1_.refs_18_), channel_id=1, source_target_pairs={{0,2},{2,4},{4,6},{6,7},{7,5},{5,3},{3,1},{1,0},{8,10},{10,12},{12... | collective-permute-start | bytes 1179656 | tf_op jit(solution)/shard_map/ppermute | solution.py:429
  255.6 10.8 %collective-permute-start.42 = (bf16[3,128,512]{2,1,0:T(8,128)(2,1)S(1)}, bf16[3,128,512]{2,1,0:T(8,128)(2,1)}, u32[]{:S(2)}, u32[]{:S(2)}) collective-permute-start(bf16[3,128,512]{2,1,0:T(8,128)(2,1)S(1)} %collective-permute-done.40.refs_2_.refs_19_), channel_id=1, source_target_pairs={{0,1},{2,0},{4,2},{6,4},{7,6},{5,7},{3,5},{1,3},{8,9},{10,8},{12,1... | collective-permute-start | bytes 1179656 | tf_op jit(solution)/shard_map/ppermute | solution.py:429
  261.8 12.4 %collective-permute-start.37 = (bf16[3,128,512]{2,1,0:T(8,128)(2,1)}, bf16[3,128,512]{2,1,0:T(8,128)(2,1)}, u32[]{:S(2)}, u32[]{:S(2)}) collective-permute-start(bf16[3,128,512]{2,1,0:T(8,128)(2,1)} %slice.61), channel_id=1, source_target_pairs={{0,2},{2,4},{4,6},{6,7},{7,5},{5,3},{3,1},{1,0},{8,10},{10,12},{12... | collective-permute-start | bytes 1179656 | tf_op jit(solution)/shard_map/ppermute | solution.py:429
  264.4 21.7 %collective-permute-start.38 = (bf16[3,128,512]{2,1,0:T(8,128)(2,1)}, bf16[3,128,512]{2,1,0:T(8,128)(2,1)}, u32[]{:S(2)}, u32[]{:S(2)}) collective-permute-start(bf16[3,128,512]{2,1,0:T(8,128)(2,1)} %slice.62), channel_id=1, source_target_pairs={{0,1},{2,0},{4,2},{6,4},{7,6},{5,7},{3,5},{1,3},{8,9},{10,8},{12,1... | collective-permute-start | bytes 1179656 | tf_op jit(solution)/shard_map/ppermute | solution.py:429
  264.6 17.8 %collective-permute-start.43 = (bf16[3,128,512]{2,1,0:T(8,128)(2,1)}, bf16[3,128,512]{2,1,0:T(8,128)(2,1)S(1)}, u32[]{:S(2)}, u32[]{:S(2)}) collective-permute-start(bf16[3,128,512]{2,1,0:T(8,128)(2,1)} %collective-permute-done.41.refs_3_.refs_20_), channel_id=1, source_target_pairs={{0,2},{2,4},{4,6},{6,7},{7,5},{5,3},{3,1},{1,0},{8,10},{10,12},{12... | collective-permute-start | bytes 1179656 | tf_op jit(solution)/shard_map/ppermute | solution.py:429
  266.4 18.7 %collective-permute-start.44 = (bf16[3,128,512]{2,1,0:T(8,128)(2,1)}, bf16[3,128,512]{2,1,0:T(8,128)(2,1)S(1)}, u32[]{:S(2)}, u32[]{:S(2)}) collective-permute-start(bf16[3,128,512]{2,1,0:T(8,128)(2,1)} %collective-permute-done.42.refs_4_.refs_21_), channel_id=1, source_target_pairs={{0,1},{2,0},{4,2},{6,4},{7,6},{5,7},{3,5},{1,3},{8,9},{10,8},{12,1... | collective-permute-start | bytes 1179656 | tf_op jit(solution)/shard_map/ppermute | solution.py:429
  274.2 33.6 %collective-permute-start.53 = (bf16[3,128,512]{2,1,0:T(8,128)(2,1)S(1)}, bf16[3,128,512]{2,1,0:T(8,128)(2,1)}, u32[]{:S(2)}, u32[]{:S(2)}) collective-permute-start(bf16[3,128,512]{2,1,0:T(8,128)(2,1)S(1)} %get-tuple-element.94.refs_0_.refs_26_), channel_id=1, source_target_pairs={{0,2},{2,4},{4,6},{6,7},{7,5},{5,3},{3,1},{1,0},{8,10},{10,12},{12... | collective-permute-start | bytes 1179656 | tf_op jit(solution)/shard_map/ppermute | solution.py:429
  275.9 31.9 %collective-permute-start.54 = (bf16[3,128,512]{2,1,0:T(8,128)(2,1)S(1)}, bf16[3,128,512]{2,1,0:T(8,128)(2,1)}, u32[]{:S(2)}, u32[]{:S(2)}) collective-permute-start(bf16[3,128,512]{2,1,0:T(8,128)(2,1)S(1)} %get-tuple-element.94.refs_0_.refs_26_), channel_id=1, source_target_pairs={{0,1},{2,0},{4,2},{6,4},{7,6},{5,7},{3,5},{1,3},{8,9},{10,8},{12,1... | collective-permute-start | bytes 1179656 | tf_op jit(solution)/shard_map/ppermute | solution.py:429
  283.2 12.8 %collective-permute-start.45 = (bf16[3,64,512]{2,1,0:T(8,128)(2,1)}, bf16[3,64,512]{2,1,0:T(8,128)(2,1)S(1)}, u32[]{:S(2)}, u32[]{:S(2)}) collective-permute-start(bf16[3,64,512]{2,1,0:T(8,128)(2,1)} %slice.63), channel_id=1, source_target_pairs={{0,2},{2,4},{4,6},{6,7},{7,5},{5,3},{3,1},{1,0},{8,10},{10,12},{12... | collective-permute-start | bytes 589832 | tf_op jit(solution)/shard_map/ppermute | solution.py:429
  285.8 10.3 %collective-permute-start.46 = (bf16[3,64,512]{2,1,0:T(8,128)(2,1)}, bf16[3,64,512]{2,1,0:T(8,128)(2,1)S(1)}, u32[]{:S(2)}, u32[]{:S(2)}) collective-permute-start(bf16[3,64,512]{2,1,0:T(8,128)(2,1)} %slice.64), channel_id=1, source_target_pairs={{0,1},{2,0},{4,2},{6,4},{7,6},{5,7},{3,5},{1,3},{8,9},{10,8},{12,1... | collective-permute-start | bytes 589832 | tf_op jit(solution)/shard_map/ppermute | solution.py:429
  307.8 16.5 %collective-permute-start.47 = (bf16[4,128,512]{2,1,0:T(8,128)(2,1)}, bf16[4,128,512]{2,1,0:T(8,128)(2,1)S(1)}, u32[]{:S(2)}, u32[]{:S(2)}) collective-permute-start(bf16[4,128,512]{2,1,0:T(8,128)(2,1)} %get-tuple-element.90), channel_id=1, source_target_pairs={{0,8},{8,0},{16,24},{24,16},{1,9},{9,1},{17,25},{25,17},{2,10},{10... | collective-permute-start | bytes 1572872 | tf_op jit(solution)/shard_map/ppermute | solution.py:432
  307.8 11.7 %collective-permute-start.55 = (bf16[3,128,512]{2,1,0:T(8,128)(2,1)}, bf16[3,128,512]{2,1,0:T(8,128)(2,1)S(1)}, u32[]{:S(2)}, u32[]{:S(2)}) collective-permute-start(bf16[3,128,512]{2,1,0:T(8,128)(2,1)} %collective-permute-done.53.refs_1_.refs_27_), channel_id=1, source_target_pairs={{0,2},{2,4},{4,6},{6,7},{7,5},{5,3},{3,1},{1,0},{8,10},{10,12},{12... | collective-permute-start | bytes 1179656 | tf_op jit(solution)/shard_map/ppermute | solution.py:429
  309.6 11.7 %collective-permute-start.56 = (bf16[3,128,512]{2,1,0:T(8,128)(2,1)}, bf16[3,128,512]{2,1,0:T(8,128)(2,1)}, u32[]{:S(2)}, u32[]{:S(2)}) collective-permute-start(bf16[3,128,512]{2,1,0:T(8,128)(2,1)} %collective-permute-done.54.refs_2_.refs_28_), channel_id=1, source_target_pairs={{0,1},{2,0},{4,2},{6,4},{7,6},{5,7},{3,5},{1,3},{8,9},{10,8},{12,1... | collective-permute-start | bytes 1179656 | tf_op jit(solution)/shard_map/ppermute | solution.py:429
  319.5 10.8 %collective-permute-start.57 = (bf16[3,128,512]{2,1,0:T(8,128)(2,1)S(1)}, bf16[3,128,512]{2,1,0:T(8,128)(2,1)S(1)}, u32[]{:S(2)}, u32[]{:S(2)}) collective-permute-start(bf16[3,128,512]{2,1,0:T(8,128)(2,1)S(1)} %collective-permute-done.55.refs_3_.refs_29_), channel_id=1, source_target_pairs={{0,2},{2,4},{4,6},{6,7},{7,5},{5,3},{3,1},{1,0},{8,10},{10,12},{12... | collective-permute-start | bytes 1179656 | tf_op jit(solution)/shard_map/ppermute | solution.py:429
  321.3 10.7 %collective-permute-start.58 = (bf16[3,128,512]{2,1,0:T(8,128)(2,1)}, bf16[3,128,512]{2,1,0:T(8,128)(2,1)S(1)}, u32[]{:S(2)}, u32[]{:S(2)}) collective-permute-start(bf16[3,128,512]{2,1,0:T(8,128)(2,1)} %collective-permute-done.56.refs_4_.refs_30_), channel_id=1, source_target_pairs={{0,1},{2,0},{4,2},{6,4},{7,6},{5,7},{3,5},{1,3},{8,9},{10,8},{12,1... | collective-permute-start | bytes 1179656 | tf_op jit(solution)/shard_map/ppermute | solution.py:429
  323.8 12.1 %collective-permute-start.52 = (f32[256,1]{0,1:T(1,128)S(1)}, f32[256,1]{0,1:T(1,128)S(1)}, u32[]{:S(2)}, u32[]{:S(2)}) collective-permute-start(f32[256,1]{0,1:T(1,128)S(1)} %add.317), channel_id=1, source_target_pairs={{0,16},{8,24},{16,0},{24,8},{1,17},{9,25},{17,1},{25,9},{2,18},{10... | collective-permute-start | bytes 3080 | tf_op jit(solution)/shard_map/ppermute | solution.py:432
  332.0 5.7 %collective-permute-start.59 = (bf16[3,64,512]{2,1,0:T(8,128)(2,1)S(1)}, bf16[3,64,512]{2,1,0:T(8,128)(2,1)S(1)}, u32[]{:S(2)}, u32[]{:S(2)}) collective-permute-start(bf16[3,64,512]{2,1,0:T(8,128)(2,1)S(1)} %slice.67), channel_id=1, source_target_pairs={{0,2},{2,4},{4,6},{6,7},{7,5},{5,3},{3,1},{1,0},{8,10},{10,12},{12... | collective-permute-start | bytes 589832 | tf_op jit(solution)/shard_map/ppermute | solution.py:429
  332.9 5.7 %collective-permute-start.60 = (bf16[3,64,512]{2,1,0:T(8,128)(2,1)S(1)}, bf16[3,64,512]{2,1,0:T(8,128)(2,1)S(1)}, u32[]{:S(2)}, u32[]{:S(2)}) collective-permute-start(bf16[3,64,512]{2,1,0:T(8,128)(2,1)S(1)} %slice.68), channel_id=1, source_target_pairs={{0,1},{2,0},{4,2},{6,4},{7,6},{5,7},{3,5},{1,3},{8,9},{10,8},{12,1... | collective-permute-start | bytes 589832 | tf_op jit(solution)/shard_map/ppermute | solution.py:429
  335.9 13.8 %collective-permute-start.48 = (bf16[1,2,128,512]{3,2,1,0:T(8,128)(2,1)S(1)}, bf16[1,2,128,512]{3,2,1,0:T(8,128)(2,1)}, u32[]{:S(2)}, u32[]{:S(2)}) collective-permute-start(bf16[1,2,128,512]{3,2,1,0:T(8,128)(2,1)S(1)} %fusion.11), channel_id=1, source_target_pairs={{0,16},{8,24},{16,0},{24,8},{1,17},{9,25},{17,1},{25,9},{2,18},{10... | collective-permute-start | bytes 786440 | tf_op jit(solution)/shard_map/ppermute | solution.py:432
  349.7 7.7 %collective-permute-start.61 = (bf16[4,128,512]{2,1,0:T(8,128)(2,1)}, bf16[4,128,512]{2,1,0:T(8,128)(2,1)S(1)}, u32[]{:S(2)}, u32[]{:S(2)}) collective-permute-start(bf16[4,128,512]{2,1,0:T(8,128)(2,1)} %get-tuple-element.100), channel_id=1, source_target_pairs={{0,8},{8,0},{16,24},{24,16},{1,9},{9,1},{17,25},{25,17},{2,10},{10... | collective-permute-start | bytes 1572872 | tf_op jit(solution)/shard_map/ppermute | solution.py:432
  350.8 16.6 %collective-permute-start.49 = (bf16[128,512]{1,0:T(8,128)(2,1)S(1)}, bf16[128,512]{1,0:T(8,128)(2,1)S(1)}, u32[]{:S(2)}, u32[]{:S(2)}) collective-permute-start(bf16[128,512]{1,0:T(8,128)(2,1)S(1)} %get-tuple-element.114), channel_id=1, source_target_pairs={{0,0},{1,1},{2,8},{3,9},{4,16},{5,17},{6,24},{7,25},{8,2},{9,3},{1... | collective-permute-start | bytes 393224 | tf_op jit(solution)/shard_map/ppermute | solution.py:537
  353.6 14.5 %collective-permute-start.50 = (bf16[128,512]{1,0:T(8,128)(2,1)S(1)}, bf16[128,512]{1,0:T(8,128)(2,1)S(1)}, u32[]{:S(2)}, u32[]{:S(2)}) collective-permute-start(bf16[128,512]{1,0:T(8,128)(2,1)S(1)} %get-tuple-element.113), channel_id=1, source_target_pairs={{0,1},{1,0},{2,9},{3,8},{4,17},{5,16},{6,25},{7,24},{8,3},{9,2},{1... | collective-permute-start | bytes 393224 | tf_op jit(solution)/shard_map/ppermute | solution.py:537
  358.8 12.8 %collective-permute-start.62 = (bf16[1,2,128,512]{3,2,1,0:T(8,128)(2,1)S(1)}, bf16[1,2,128,512]{3,2,1,0:T(8,128)(2,1)S(1)}, u32[]{:S(2)}, u32[]{:S(2)}) collective-permute-start(bf16[1,2,128,512]{3,2,1,0:T(8,128)(2,1)S(1)} %fusion.12), channel_id=1, source_target_pairs={{0,16},{8,24},{16,0},{24,8},{1,17},{9,25},{17,1},{25,9},{2,18},{10... | collective-permute-start | bytes 786440 | tf_op jit(solution)/shard_map/ppermute | solution.py:432
  371.7 17.2 %collective-permute-start.63 = (bf16[128,512]{1,0:T(8,128)(2,1)S(1)}, bf16[128,512]{1,0:T(8,128)(2,1)S(1)}, u32[]{:S(2)}, u32[]{:S(2)}) collective-permute-start(bf16[128,512]{1,0:T(8,128)(2,1)S(1)} %get-tuple-element.118), channel_id=1, source_target_pairs={{0,0},{1,1},{2,8},{3,9},{4,16},{5,17},{6,24},{7,25},{8,2},{9,3},{1... | collective-permute-start | bytes 393224 | tf_op jit(solution)/shard_map/ppermute | solution.py:537
  373.7 15.2 %collective-permute-start.64 = (bf16[128,512]{1,0:T(8,128)(2,1)S(1)}, bf16[128,512]{1,0:T(8,128)(2,1)S(1)}, u32[]{:S(2)}, u32[]{:S(2)}) collective-permute-start(bf16[128,512]{1,0:T(8,128)(2,1)S(1)} %get-tuple-element.117), channel_id=1, source_target_pairs={{0,1},{1,0},{2,9},{3,8},{4,17},{5,16},{6,25},{7,24},{8,3},{9,2},{1... | collective-permute-start | bytes 393224 | tf_op jit(solution)/shard_map/ppermute | solution.py:537
  (65 other events, 754.1 us)

commit v3 on v2

v3 whole, which is shorter than its diff:
```python
import functools
import math

import jax
import jax.numpy as jnp
import numpy as np
from jax import lax
from jax.experimental import pallas as pl
from jax.experimental.pallas import tpu as pltpu
from jax.sharding import PartitionSpec as P

HEAD_DIM = 128
NORM_EPS = 1e-05
SMALL, LARGE = 20 * 1024 * 1024, 56 * 1024 * 1024


def params(limit):
    return pltpu.CompilerParams(dimension_semantics=("arbitrary",), vmem_limit_bytes=limit)


def cost(flops, moved):
    return pl.CostEstimate(flops=flops, bytes_accessed=moved, transcendentals=0)


def mm(a, b):
    return jnp.dot(a, b, preferred_element_type=jnp.float32)


def mm_nt(a, b):
    return lax.dot_general(a, b, (((1,), (1,)), ((), ())), preferred_element_type=jnp.float32)


def mm_tn(a, b):
    return lax.dot_general(a, b, (((0,), (0,)), ((), ())), preferred_element_type=jnp.float32)


def rope_tables(length, width):
    position = jnp.arange(length).astype(jnp.float32)[:, None]
    frequency = jnp.exp(
        jnp.arange(width // 2).astype(jnp.float32) * (-2.0 * math.log(10000.0) / width)
    )
    angle = position * frequency[None, :]
    cosine, sine = jnp.cos(angle), jnp.sin(angle)
    return (
        jnp.concatenate([cosine, cosine], axis=-1),
        jnp.concatenate([-sine, sine], axis=-1),
    )


def ring_order(size):
    return [*range(0, size, 2), *reversed(range(1, size, 2))]


def ring_distances(size):
    far = size // 2
    distances = [0]
    for step in range(1, far):
        distances += [-step, step]
    return [*distances, far]


def index_table(size, nodes):
    order, group = ring_order(size), size // nodes
    rows = []
    for node in range(nodes):
        for here in range(size):
            place = order.index(here)
            seqs = [order[(place + distance) % size] for distance in ring_distances(size)]
            owner = [seq // group for seq in seqs]
            rows.append(
                [order[(place + distance) % size] for distance in range(size)]
                + [node % 2]
                + seqs
                + [owner_ % 2 ^ node % 2 for owner_ in owner]
                + [(o // 2) * group + seq % group for o, seq in zip(owner, seqs)]
            )
    return np.array(rows, np.int32)


def weights_kernel(quant, scale, out, turned):
    blocks = scale.shape[1]
    rows = quant.shape[1] // blocks
    scales = scale[0].astype(jnp.float32)
    for block in range(blocks):
        span = slice(block * rows, (block + 1) * rows)
        scaled = (quant[0, span].astype(jnp.float32) * scales[block : block + 1]).astype(jnp.bfloat16)
        out[0, span] = scaled
        turned[0, :, span] = scaled.T


def scaled_weights(w_quant, w_scale):
    _, depth, columns = w_quant.shape
    blocks = w_scale.shape[1]
    return pl.pallas_call(
        weights_kernel,
        grid=(3,),
        in_specs=[
            pl.BlockSpec((1, depth, columns), lambda m: (m, 0, 0)),
            pl.BlockSpec((1, blocks, columns), lambda m: (m, 0, 0)),
        ],
        out_specs=[
            pl.BlockSpec((1, depth, columns), lambda m: (m, 0, 0)),
            pl.BlockSpec((1, columns, depth), lambda m: (m, 0, 0)),
        ],
        out_shape=[
            jax.ShapeDtypeStruct((3, depth, columns), jnp.bfloat16),
            jax.ShapeDtypeStruct((3, columns, depth), jnp.bfloat16),
        ],
        compiler_params=params(SMALL),
        cost_estimate=cost(3 * depth * columns, 18 * depth * columns),
        name="scaled_weights",
    )(w_quant, w_scale)


def normed_kernel(idx, tokens, gain, *refs):
    outs, gains = refs[:-1], refs[-1]
    width, part = tokens.shape[1], outs[0].shape[1]
    gains[...] = gain[...].astype(jnp.float32)
    values = tokens[...].astype(jnp.float32)
    inverse = lax.rsqrt(jnp.mean(values * values, axis=-1, keepdims=True) + NORM_EPS)
    size = len(outs) - 1
    for distance in range(size):
        start = pl.multiple_of(idx[distance] * (width // size) + idx[size] * part, part)
        block = tokens[:, pl.ds(start, part)].astype(jnp.float32)
        scale = gains[:, pl.ds(start, part)]
        outs[distance][...] = (block * inverse * scale).astype(jnp.bfloat16)
    outs[size][...] = jnp.broadcast_to(inverse, outs[size].shape)


def normed_blocks(idx, tokens, gain, size, part):
    length, width = tokens.shape
    tile = length // 4
    block = pl.BlockSpec((tile, part), lambda i, idx: (i, 0))
    *blocks, inverse = pl.pallas_call(
        normed_kernel,
        grid_spec=pltpu.PrefetchScalarGridSpec(
            num_scalar_prefetch=1,
            grid=(4,),
            in_specs=[
                pl.BlockSpec((tile, width), lambda i, idx: (i, 0)),
                pl.BlockSpec((1, width), lambda i, idx: (0, 0)),
            ],
            out_specs=[block] * size + [pl.BlockSpec((tile, 128), lambda i, idx: (i, 0))],
            scratch_shapes=[pltpu.VMEM((1, width), jnp.float32)],
        ),
        out_shape=[jax.ShapeDtypeStruct((length, part), jnp.bfloat16)] * size
        + [jax.ShapeDtypeStruct((length, 128), jnp.float32)],
        compiler_params=params(SMALL),
        cost_estimate=cost(8 * length * width, 4 * length * width),
        name="normed_blocks",
    )(idx, tokens, gain)
    return blocks, inverse


def turn_kernel(count, idx, mine, other, mine_far, other_far, out):
    length, part = mine_far.shape
    for side, near, last in ((0, mine, mine_far), (1, other, other_far)):
        half = idx[count] * (1 - side) + (1 - idx[count]) * side
        rows = pl.ds(pl.multiple_of(half * part, part), part)
        for place in range(count):
            block = near[place] if place < count - 1 else last[...]
            out[rows, place * length : (place + 1) * length] = block.T


def turn(idx, mine, other, mine_far, other_far):
    near, length, part = mine.shape
    count = near + 1
    stack = pl.BlockSpec(mine.shape, lambda i, idx: (0, 0, 0))
    last = pl.BlockSpec((length, part), lambda i, idx: (0, 0))
    shape = (2 * part, count * length)
    return pl.pallas_call(
        functools.partial(turn_kernel, count),
        grid_spec=pltpu.PrefetchScalarGridSpec(
            num_scalar_prefetch=1,
            grid=(1,),
            in_specs=[stack, stack, last, last],
            out_specs=pl.BlockSpec(shape, lambda i, idx: (0, 0)),
        ),
        out_shape=jax.ShapeDtypeStruct(shape, jnp.bfloat16),
        compiler_params=params(SMALL),
        cost_estimate=cost(2 * count * length * part, 8 * count * length * part),
        name="turn",
    )(idx, mine, other, mine_far, other_far)


def sum_first_kernel(idx, mine, other, weight, weight_other, *outs):
    half, wide = outs[0].shape[1:]
    for chunk in range(2):
        span = slice(chunk * wide, (chunk + 1) * wide)
        product = mm(mine[...], weight[0, :, span]) + mm(other[...], weight_other[0, :, span])
        outs[2 * chunk][0] = product[:half].astype(jnp.bfloat16)
        outs[2 * chunk + 1][0] = product[half:].astype(jnp.bfloat16)


def sum_step_kernel(
    idx, mine_r, other_r, mine_l, other_l, weight, weight_other, from_left, from_right, right, left
):
    length, part = right.shape[1], from_left.shape[1]
    product = mm(mine_r[0], weight[0]) + mm(other_r[0], weight_other[0])
    right[0, :part] = (product[:part] + from_left[0].astype(jnp.float32)).astype(jnp.bfloat16)
    if part < length:
        right[0, part:] = product[part:].astype(jnp.bfloat16)
    product = mm(mine_l[0], weight[0]) + mm(other_l[0], weight_other[0])
    rest = length - part
    left[0, rest:] = (product[rest:] + from_right[0].astype(jnp.float32)).astype(jnp.bfloat16)
    if rest:
        left[0, :rest] = product[:rest].astype(jnp.bfloat16)


def weight_halves(size, part, wide, chunk):
    return [
        pl.BlockSpec((1, part, wide), lambda m, idx: (m, idx[size], chunk)),
        pl.BlockSpec((1, part, wide), lambda m, idx: (m, 1 - idx[size], chunk)),
    ]


def sum_first(idx, size, mine, other, weights):
    length, part = mine.shape
    columns = weights.shape[2]
    half, wide = length // 2, columns // 2
    block = pl.BlockSpec((length, part), lambda m, idx: (0, 0))
    result = jax.ShapeDtypeStruct((3, half, wide), jnp.bfloat16)
    return pl.pallas_call(
        sum_first_kernel,
        grid_spec=pltpu.PrefetchScalarGridSpec(
            num_scalar_prefetch=1,
            grid=(3,),
            in_specs=[block, block, *weight_halves(size, part, columns, 0)],
            out_specs=[pl.BlockSpec((1, half, wide), lambda m, idx: (m, 0, 0))] * 4,
        ),
        out_shape=[result] * 4,
        compiler_params=params(SMALL),
        cost_estimate=cost(12 * length * part * columns, 16 * part * columns),
        name="sum_first",
    )(idx, mine, other, weights, weights)


def sum_step(idx, size, mine, other, places, weights, from_left, from_right, chunk, wide):
    _, length, part = mine.shape
    block_r = pl.BlockSpec((1, length, part), lambda m, idx: (places[0], 0, 0))
    block_l = pl.BlockSpec((1, length, part), lambda m, idx: (places[1], 0, 0))
    came = pl.BlockSpec((1, from_left.shape[1], wide), lambda m, idx: (m, 0, 0))
    whole = jax.ShapeDtypeStruct((3, length, wide), jnp.bfloat16)
    return pl.pallas_call(
        sum_step_kernel,
        grid_spec=pltpu.PrefetchScalarGridSpec(
            num_scalar_prefetch=1,
            grid=(3,),
            in_specs=[
                block_r,
                block_r,
                block_l,
                block_l,
                *weight_halves(size, part, wide, chunk),
                came,
                came,
            ],
            out_specs=[pl.BlockSpec((1, length, wide), lambda m, idx: (m, 0, 0))] * 2,
        ),
        out_shape=[whole, whole],
        compiler_params=params(SMALL),
        cost_estimate=cost(24 * length * part * wide, 24 * part * wide),
        name="sum_step",
    )(idx, mine, other, mine, other, weights, weights, from_left, from_right)


def attention_kernel(
    idx, mine, other, weight, weight_other, from_left, from_right, d_out, cosine, sine,
    output, pre, dots,
):
    length = mine.shape[1]
    proj = [
        mm(mine[0], weight[m])
        + mm(other[0], weight_other[m])
        + (from_left[m].astype(jnp.float32) + from_right[m].astype(jnp.float32))
        for m in range(3)
    ]
    cos, sin = cosine[...], sine[...]
    half = HEAD_DIM // 2

    def rotate(tensor, angle):
        return tensor * cos + pltpu.roll(tensor, half, 1) * angle

    query = rotate(proj[0], sin).astype(jnp.bfloat16)
    key_rows = rotate(proj[1], sin).astype(jnp.bfloat16)
    value = proj[2].astype(jnp.bfloat16)
    scores = mm_nt(query, key_rows) * (1.0 / math.sqrt(HEAD_DIM))
    causal = lax.broadcasted_iota(jnp.int32, (length, length), 0) >= lax.broadcasted_iota(
        jnp.int32, (length, length), 1
    )
    scores = jnp.where(causal, scores, jnp.float32(-1e30))
    powers = jnp.exp(scores - jnp.max(scores, axis=-1, keepdims=True))
    probs = powers * (1.0 / jnp.sum(powers, axis=-1, keepdims=True))
    probs_low = probs.astype(jnp.bfloat16)
    output[...] = mm(probs_low, value).astype(jnp.bfloat16)
    cotangent = d_out[...]
    d_value = mm_tn(probs_low, cotangent).astype(jnp.bfloat16)
    d_probs = mm_nt(cotangent, value).astype(jnp.bfloat16).astype(jnp.float32)
    inner = jnp.sum(d_probs * probs, axis=-1, keepdims=True)
    d_scores = (probs * (d_probs - inner) * (1.0 / math.sqrt(HEAD_DIM))).astype(jnp.bfloat16)
    d_query = mm(d_scores, key_rows).astype(jnp.bfloat16).astype(jnp.float32)
    d_key = mm_tn(d_scores, query).astype(jnp.bfloat16).astype(jnp.float32)
    pre_query = rotate(d_query, -sin).astype(jnp.bfloat16)
    pre_key = rotate(d_key, -sin).astype(jnp.bfloat16)
    pre[0] = pre_query
    pre[1] = pre_key
    pre[2] = d_value
    product = (
        pre_query.astype(jnp.float32) * proj[0]
        + pre_key.astype(jnp.float32) * proj[1]
        + d_value.astype(jnp.float32) * proj[2]
    )

    @pl.when(pl.program_id(0) == 0)
    def _():
        dots[...] = product

    @pl.when(pl.program_id(0) > 0)
    def _():
        dots[...] += product


def attention(idx, size, mine, other, weights, from_left, from_right, d_out, tables, chunk, wide):
    _, length, part = mine.shape
    heads = wide // HEAD_DIM
    first = chunk * heads
    block = pl.BlockSpec((1, length, part), lambda h, idx: (0, 0, 0))
    table = pl.BlockSpec((length, HEAD_DIM), lambda h, idx: (0, 0))
    stack = pl.BlockSpec((3, length, HEAD_DIM), lambda h, idx: (0, 0, h))
    return pl.pallas_call(
        attention_kernel,
        grid_spec=pltpu.PrefetchScalarGridSpec(
            num_scalar_prefetch=1,
            grid=(heads,),
            in_specs=[
                block,
                block,
                pl.BlockSpec((3, part, HEAD_DIM), lambda h, idx: (0, idx[size], first + h)),
                pl.BlockSpec((3, part, HEAD_DIM), lambda h, idx: (0, 1 - idx[size], first + h)),
                stack,
                stack,
                pl.BlockSpec((length, HEAD_DIM), lambda h, idx: (0, first + h)),
                table,
                table,
            ],
            out_specs=[
                pl.BlockSpec((length, HEAD_DIM), lambda h, idx: (0, h)),
                stack,
                table,
            ],
        ),
        out_shape=[
            jax.ShapeDtypeStruct((length, wide), jnp.bfloat16),
            jax.ShapeDtypeStruct((3, length, wide), jnp.bfloat16),
            jax.ShapeDtypeStruct((length, HEAD_DIM), jnp.float32),
        ],
        compiler_params=params(SMALL),
        cost_estimate=cost(12 * length * part * wide, 24 * part * wide),
        name="attention",
    )(idx, mine, other, weights, weights, from_left, from_right, d_out, *tables)


def grads_kernel(count, sets, turned, *refs):
    pieces, out = refs[:-1], refs[-1]
    length = turned.shape[1] // count
    total, start = None, 0
    for position in range(sets):
        group = pieces[position * (count + 1) : (position + 1) * (count + 1)]
        rows = group[0].shape[1]
        for place in range(count):
            if place < count - 1:
                block = group[place][0]
            else:
                block = jnp.concatenate([group[place][0], group[place + 1][0]], axis=0)
            low = place * length + start
            product = mm(turned[:, low : low + rows], block)
            total = product if total is None else total + product
        start += rows
    out[0] = total


def grads_chunk(count, turned, gathered, before, chunk, wide, columns):
    depth, span = turned.shape
    in_specs = [pl.BlockSpec((depth, span), lambda m: (0, 0))]
    operands = [turned]
    for pieces in gathered:
        for piece in pieces:
            in_specs.append(pl.BlockSpec((1, *piece.shape[1:]), lambda m: (m, 0, 0)))
            operands.append(piece)
    aliases = {}
    kernel = functools.partial(grads_kernel, count, len(gathered))
    if before is not None:
        aliases = {len(operands): 0}
        operands.append(before)
        in_specs.append(pl.BlockSpec(memory_space=pl.ANY))
        inner = kernel

        def kernel(*refs):
            inner(*refs[:-2], refs[-1])

    return pl.pallas_call(
        kernel,
        grid=(3,),
        in_specs=in_specs,
        out_specs=pl.BlockSpec((1, depth, wide), lambda m: (m, 0, chunk)),
        out_shape=jax.ShapeDtypeStruct((3, depth, columns), jnp.float32),
        input_output_aliases=aliases,
        compiler_params=params(LARGE),
        cost_estimate=cost(6 * span * depth * wide, 6 * span * wide + 12 * depth * wide),
        name="grads",
    )(*operands)


def back(pieces, turned, place, count):
    def one(piece):
        total = mm(piece[0], turned[0])
        for m in range(1, 3):
            total += mm(piece[m], turned[m])
        return total

    if place < count - 1:
        return one(pieces[place])
    return jnp.concatenate([one(pieces[place]), one(pieces[place + 1])], axis=0)


def term_first_kernel(count, idx, turned, *refs):
    for place in range(count):
        refs[-1][idx[count + 1 + place]] = back(refs, turned, place, count)


def term_first(idx, turned, pieces, chunk, wide):
    count = len(pieces) - 1
    length = pieces[0].shape[1]
    depth = turned.shape[2]
    return pl.pallas_call(
        functools.partial(term_first_kernel, count),
        grid_spec=pltpu.PrefetchScalarGridSpec(
            num_scalar_prefetch=1,
            grid=(1,),
            in_specs=[
                pl.BlockSpec((3, wide, depth), lambda i, idx: (0, chunk, 0)),
                *[pl.BlockSpec(piece.shape, lambda i, idx: (0, 0, 0)) for piece in pieces],
            ],
            out_specs=pl.BlockSpec((count, length, depth), lambda i, idx: (0, 0, 0)),
        ),
        out_shape=jax.ShapeDtypeStruct((count, length, depth), jnp.float32),
        compiler_params=params(LARGE),
        cost_estimate=cost(6 * count * length * depth * wide, 6 * count * length * wide),
        name="term_first",
    )(idx, turned, *pieces)


def term_last_kernel(count, idx, turned, before, *refs):
    keep, send = refs[-2], refs[-1]
    for place in range(count):
        total = back(refs, turned, place, count) + before[idx[count + 1 + place]]

        @pl.when(idx[2 * count + 1 + place] == 0)
        def _():
            keep[idx[3 * count + 1 + place]] = total

        @pl.when(idx[2 * count + 1 + place] == 1)
        def _():
            send[idx[3 * count + 1 + place]] = total.astype(jnp.bfloat16)


def term_last(idx, turned, before, pieces, part, chunk, wide):
    count, _, depth = before.shape
    rows = pieces[0].shape[1]
    result = pl.BlockSpec((count // 2, rows, depth), lambda i, idx: (0, 0, 0))
    return pl.pallas_call(
        functools.partial(term_last_kernel, count),
        grid_spec=pltpu.PrefetchScalarGridSpec(
            num_scalar_prefetch=1,
            grid=(1,),
            in_specs=[
                pl.BlockSpec((3, wide, depth), lambda i, idx: (0, chunk, 0)),
                pl.BlockSpec((count, rows, depth), lambda i, idx: (0, part, 0)),
                *[pl.BlockSpec(piece.shape, lambda i, idx: (0, 0, 0)) for piece in pieces],
            ],
            out_specs=[result, result],
        ),
        out_shape=[
            jax.ShapeDtypeStruct((count // 2, rows, depth), jnp.float32),
            jax.ShapeDtypeStruct((count // 2, rows, depth), jnp.bfloat16),
        ],
        compiler_params=params(LARGE),
        cost_estimate=cost(6 * count * rows * depth * wide, 6 * count * rows * wide),
        name="term_last",
    )(idx, turned, before, *pieces)


def after(first, *arrays):
    tied = lax.optimization_barrier((first, *arrays))
    return tied[1:]


def local(tokens, norm_gain, w_quant, w_scale, d_out):
    length, width = tokens.shape
    depth, columns = w_quant.shape[1:]
    size, nodes = lax.axis_size("local"), lax.axis_size("node")
    here, node = lax.axis_index("local"), lax.axis_index("node")
    wide = columns // 2
    far = size // 2
    group = size // nodes
    core = node % 2

    order = ring_order(size)
    distances = ring_distances(size)
    table = jnp.asarray(index_table(size, nodes))
    idx = lax.dynamic_index_in_dim(table, node * size + here, 0, keepdims=False)

    def shift(array, distance):
        moves = [(order[i], order[(i + distance) % size]) for i in range(size)]
        return lax.ppermute(array, "local", moves)

    def swap(array, bit):
        return lax.ppermute(array, "node", [(n, n ^ bit) for n in range(nodes)])

    blocks, inverse_rms = normed_blocks(idx, tokens, norm_gain[None], size, depth // 2)
    mine_far = shift(blocks[far], far)
    other_far = swap(mine_far, 1)
    weights, turned = scaled_weights(w_quant, w_scale)
    firsts = sum_first(idx, size, mine_far, other_far, weights)
    mine = jnp.stack([shift(blocks[-d % size], -d) if d else blocks[0] for d in distances[:-1]])
    other = swap(mine, 1)

    tables = rope_tables(length, HEAD_DIM)
    arrived = []
    for chunk in range(2):
        right, left = firsts[2 * chunk : 2 * chunk + 2]
        for distance in range(far - 1, -1, -1):
            from_left, from_right = shift(right, 1), shift(left, -1)
            if distance:
                places = distances.index(distance), distances.index(-distance)
                right, left = sum_step(
                    idx, size, mine, other, places, weights, from_left, from_right, chunk, wide
                )
        arrived.append((from_left, from_right))

    outputs, pres, dots = [], [], 0.0
    for chunk in range(2):
        output, pre, product = attention(
            idx, size, mine, other, weights, *arrived[chunk], d_out, tables, chunk, wide
        )
        outputs.append(output)
        pres.append(pre)
        dots += jnp.sum(product, axis=-1, keepdims=True)
    bit = 1
    while bit < nodes:
        dots = dots + swap(dots, bit)
        bit *= 2
    rows_turned = turn(idx, mine, other, mine_far, other_far)

    half = length // 2
    sets = [pres[0], pres[1][:, :half], pres[1][:, half:]]
    gathered = [[block] for block in sets]
    moving = [(block, block) for block in sets]
    schedule = [(0, 1)]
    for step in range(2, far + 1):
        schedule += [(0, step), (1, step - 1)]
    schedule += [(2, 1), (1, far)] + [(2, step) for step in range(2, far + 1)]

    share = width // nodes
    values_part = lax.dynamic_slice_in_dim(tokens, node * share, share, 1).astype(jnp.float32)
    gains_part = lax.dynamic_slice_in_dim(norm_gain, node * share, share, 0).astype(jnp.float32)
    inverse_rms = inverse_rms[:, :1]

    def start_term(before, part):
        keep, send = term_last(idx, turned, before, gathered[1 + part], part, 1, wide)
        return keep + swap(send, 1).astype(jnp.float32)

    def end_term(summed, part):
        bit = 2
        while bit < nodes:
            pair = summed.reshape(-1, 2, group, *summed.shape[1:])
            own = (node // bit) % 2
            keep = lax.dynamic_index_in_dim(pair, own, 1, keepdims=False)
            send = lax.dynamic_index_in_dim(pair, 1 - own, 1, keepdims=False)
            summed = keep + swap(send.astype(jnp.bfloat16), bit).astype(jnp.float32)
            summed = summed.reshape(-1, *pair.shape[3:])
            bit *= 2
        summed = summed.astype(jnp.bfloat16)
        came = []
        for turn in range(group):
            block = lax.dynamic_index_in_dim(summed, (here + turn) % group, 0, keepdims=False)
            moves = [
                (n * size + s, (s // group) * size + n * group + (s + turn) % group)
                for n in range(nodes)
                for s in range(size)
            ]
            came.append(lax.ppermute(block, ("node", "local"), moves))
        came = jnp.stack(came)
        upstream = jnp.concatenate(
            [
                lax.dynamic_index_in_dim(came, (here + group - i) % group, 0, keepdims=False)
                for i in range(group)
            ],
            axis=-1,
        ).astype(jnp.float32)
        rows = slice(part * half, (part + 1) * half)
        d_rows = (
            inverse_rms[rows] * gains_part * upstream
            - values_part[rows] * inverse_rms[rows] ** 2 * dots[rows] / width
        )
        return d_rows.astype(jnp.bfloat16)

    term = early = None
    for ring, step in schedule:
        right, left = moving[ring]
        if step == far:
            middle = right.shape[1] // 2
            right, left = right[:, :middle], left[:, middle:]
        if (ring, step) == (1, 1):
            right, left = after(moving[0][0], right, left)
        if (ring, step) == (2, 1):
            right, left = after(moving[0][0], right, left)
        if (ring, step) == (2, min(2, far)):
            right, left = after(term, right, left)
        if (ring, step) == (2, far):
            right, left = after(early, right, left)
        right, left = shift(right, 1), shift(left, -1)
        moving[ring] = right, left
        gathered[ring] += [right, left]
        if (ring, step) == (0, far):
            term = term_first(idx, turned, gathered[0], 0, wide)
        if (ring, step) == (1, far):
            early = start_term(term, 0)
    late = start_term(term, 1)
    d_tokens = jnp.concatenate([end_term(early, 0), end_term(late, 1)], axis=0)

    grads = grads_chunk(size, rows_turned, gathered[:1], None, 0, wide, columns)
    grads = grads_chunk(size, rows_turned, gathered[1:], grads, 1, wide, columns)
    return (jnp.concatenate(outputs, axis=-1), d_tokens, grads)


def solution(mesh):
    placed = (
        P("local", None),
        P(),
        P(None, "local", "node"),
        P(None, "local", "node"),
        P("local", "node"),
    )
    return jax.shard_map(
        local,
        mesh=mesh,
        in_specs=placed,
        out_specs=(P("local", "node"), P("local", "node"), P(None, "local", "node")),
        check_vma=False,
    )
```

time: 393 us -> 364 us (0.926)
  waiting for transfers between devices: 165 us -> 199 us
  Pallas kernels: 104 us -> 76.2 us
  local copies, waits for them, and re-layouts: 34.9 us -> 10.4 us
  other arithmetic: 17.3 us -> 8.87 us
    ppermute x47, waiting for transfers between devices: 156 us -> 193 us  [shift(): return lax.ppermute(array, 'local', moves)]
    pallas_call x6, Pallas kernels: 26.1 us -> 12.3 us  [sum_step(): pl.pallas_call(sum_step_kernel, grid_spec=pltpu.PrefetchScalarGridSpec(nu...]
    another operation x2 -> x1, local copies, waits for them, and re-layouts: 10.8 us -> 0.01 us  [local(): jnp.stack([shift(blocks[-d % size], -d) if d else blocks[0] for d in dist...]
    unnamed x128 -> x62, local copies, waits for them, and re-layouts: 12.2 us -> 5.38 us
    convert_element_type x3 -> x1, other arithmetic: 6.54 us -> 0.68 us  [local(): lax.dynamic_slice_in_dim(norm_gain, node * share, share, 0)]
    concatenate x1 -> x0, local copies, waits for them, and re-layouts: 5.56 us -> none  [local(): idx = jnp.concatenate([seqs, owner % 2 ^ core, position]).astype(jnp.int32)]
    ppermute x14 -> x8, waiting for transfers between devices: 8.35 us -> 2.85 us  [swap(): return lax.ppermute(array, 'node', [(n, n ^ bit) for n in range(nodes)])]
    pallas_call x2 -> x1, Pallas kernels: 6.97 us -> 1.91 us  [sum_first(): pl.pallas_call(sum_first_kernel, grid_spec=pltpu.PrefetchScalarGridSpec(n...]
  transfers between devices with their start and end apart: 65 -> 59, of which waited for: 34 -> 29; matrix products, arithmetic and copies ran while one was open for 8% -> 3% of each run, Pallas kernels for 23% -> 19%
where the time goes in v3:
time: 364 us; the launch traced here: 363 us
  waiting for transfers between devices  199 us (55%)
  Pallas kernels  76.2 us (21%)
  starting transfers between devices  67.5 us (19%)
  local copies, waits for them, and re-layouts  10.4 us (3%)
  other arithmetic  8.87 us (2%)
    ppermute x47, waiting for transfers between devices, shift(): return lax.ppermute(array, 'local', moves)  193 us
    ppermute x47, starting transfers between devices, shift(): return lax.ppermute(array, 'local', moves)  53.5 us
    pallas_call x2, Pallas kernels, grads_chunk(): pl.pallas_call(kernel, grid=(3,), in_specs=in_specs, out_specs=pl.BlockSp...  18.3 us
    pallas_call x2, Pallas kernels, term_last(): pl.pallas_call(functools.partial(term_last_kernel, count), grid_spec=pltp...  16.2 us
    pallas_call x2, Pallas kernels, attention(): pl.pallas_call(attention_kernel, grid_spec=pltpu.PrefetchScalarGridSpec(n...  14.5 us
    ppermute x4, starting transfers between devices, end_term(): came.append(lax.ppermute(block, ('node', 'local'), moves))  12.7 us
    pallas_call x6, Pallas kernels, sum_step(): pl.pallas_call(sum_step_kernel, grid_spec=pltpu.PrefetchScalarGridSpec(nu...  12.3 us
    pallas_call x1, Pallas kernels, term_first(): pl.pallas_call(functools.partial(term_first_kernel, count), grid_spec=plt...  9.31 us
  transfers between devices with their start and end apart: 59, of which 29 were waited for; matrix products, arithmetic and copies ran while one was open for 3% of the time, Pallas kernels for 19%

profile of v3, /device:TPU:2, one launch (start us, length us, event | category | flops | bytes accessed | tf_op | source)
XLA Modules:
  0.0 362.8 jit_solution(12572445748397161051)
XLA Ops:
  2.1 1.6 copy-done.2
  3.7 1.4 normed_blocks.1
  5.1 1.6 collective-permute-start
  7.2 2.6 collective-permute-start.2
  10.1 3.6 collective-permute-start.4
  13.7 1.4 collective-permute-start.5
  15.3 1.4 collective-permute-done.3
  16.7 9.7 %collective-permute-done.4 = bf16[256,256]{1,0:T(8,128)(2,1)S(1)} collective-permute-done((bf16[256,256]{1,0:T(8,128)(2,1)S(1)}, bf16[256,256]{1,0:T(8,128)(2,1)S(1)}, u32[]{:S(2)}, u32[]{:S(2)}) %collective-permute-start.4) | collective-permute-done | bytes 131104 | tf_op jit(solution)/shard_map/ppermute | solution.py:515
  26.5 2.5 collective-permute-start.7
  29.0 6.1 %collective-permute-done.7.mine.mine_far = bf16[256,256]{1,0:T(8,128)(2,1)S(1)} collective-permute-done((bf16[256,256]{1,0:T(8,128)(2,1)S(1)}, bf16[256,256]{1,0:T(8,128)(2,1)S(1)}, u32[]{:S(2)}, u32[]{:S(2)}) %collective-permute-start.7) | collective-permute-done | bytes 131104 | tf_op jit(solution)/shard_map/ppermute | solution.py:515
  36.2 1.6 copy-done
  37.9 1.9 sum_first.1
  39.8 2.0 collective-permute-start.10
  41.9 9.6 %collective-permute-done.9.from_left = bf16[3,128,512]{2,1,0:T(8,128)(2,1)S(1)} collective-permute-done((bf16[3,128,512]{2,1,0:T(8,128)(2,1)S(1)}, bf16[3,128,512]{2,1,0:T(8,128)(2,1)S(1)}, u32[]{:S(2)}, u32[]{:S(2)}) %collective-permute-start.9) | collective-permute-done | bytes 393248 | tf_op jit(solution)/shard_map/ppermute | solution.py:515
  51.5 2.1 sum_step.6
  53.6 1.6 collective-permute-start.11
  55.6 17.2 %collective-permute-done.11.from_left = bf16[3,256,512]{2,1,0:T(8,128)(2,1)S(1)} collective-permute-done((bf16[3,256,512]{2,1,0:T(8,128)(2,1)S(1)}, bf16[3,256,512]{2,1,0:T(8,128)(2,1)S(1)}, u32[]{:S(2)}, u32[]{:S(2)}) %collective-permute-start.11) | collective-permute-done | bytes 786464 | tf_op jit(solution)/shard_map/ppermute | solution.py:515
  74.1 2.1 sum_step.7
  76.1 1.5 collective-permute-start.13
  78.2 1.4 collective-permute-start.17
  80.2 22.3 %collective-permute-done.17.from_left = bf16[3,128,512]{2,1,0:T(8,128)(2,1)S(1)} collective-permute-done((bf16[3,128,512]{2,1,0:T(8,128)(2,1)S(1)}, bf16[3,128,512]{2,1,0:T(8,128)(2,1)S(1)}, u32[]{:S(2)}, u32[]{:S(2)}) %collective-permute-start.17) | collective-permute-done | bytes 393248 | tf_op jit(solution)/shard_map/ppermute | solution.py:515
  103.4 2.1 sum_step.9
  106.3 1.2 collective-permute-start.20
  107.5 2.1 sum_step.8
  110.4 1.2 collective-permute-start.16
  112.2 13.7 %collective-permute-done.19.from_left = bf16[3,256,512]{2,1,0:T(8,128)(2,1)S(1)} collective-permute-done((bf16[3,256,512]{2,1,0:T(8,128)(2,1)S(1)}, bf16[3,256,512]{2,1,0:T(8,128)(2,1)S(1)}, u32[]{:S(2)}, u32[]{:S(2)}) %collective-permute-start.19) | collective-permute-done | bytes 786464 | tf_op jit(solution)/shard_map/ppermute | solution.py:515
  126.8 2.1 sum_step.10
  129.5 1.4 collective-permute-start.22
  131.1 11.8 %collective-permute-done.15.from_left = bf16[3,256,512]{2,1,0:T(8,128)(2,1)S(1)} collective-permute-done((bf16[3,256,512]{2,1,0:T(8,128)(2,1)S(1)}, bf16[3,256,512]{2,1,0:T(8,128)(2,1)S(1)}, u32[]{:S(2)}, u32[]{:S(2)}) %collective-permute-start.15) | collective-permute-done | bytes 786464 | tf_op jit(solution)/shard_map/ppermute | solution.py:515
  143.6 7.2 %attention.2 = (bf16[256,512]{1,0:T(8,128)(2,1)S(1)}, bf16[3,256,512]{2,1,0:T(8,128)(2,1)S(1)}, f32[256,128]{1,0:T(8,128)S(1)}) custom-call(s32[33]{0:T(128)S(1)} %fusion.21.idx, bf16[7,256,256]{2,1,0:T(8,128)(2,1)S(1)} %bitcast_dynamic-update-slice_fusion.mine_r.mine_l.mine, bf16[7,256,256]{2,1,0:T(8,128)(2,1)S(1)} %collective-permute-done.6.other_r.other_l.other, ...), custom_call_target="tpu_custom_call" | custom-call | flops 402653184 | bytes 3145728 | tf_op jit(solution)/shard_map/attention/pallas_call | solution.py:330
  151.5 1.4 collective-permute-start.26
  152.9 6.7 %collective-permute-done.21.from_left = bf16[3,256,512]{2,1,0:T(8,128)(2,1)S(1)} collective-permute-done((bf16[3,256,512]{2,1,0:T(8,128)(2,1)S(1)}, bf16[3,256,512]{2,1,0:T(8,128)(2,1)S(1)}, u32[]{:S(2)}, u32[]{:S(2)}) %collective-permute-start.21) | collective-permute-done | bytes 786464 | tf_op jit(solution)/shard_map/ppermute | solution.py:515
  160.5 2.1 sum_step.11
  163.2 1.4 collective-permute-start.24
  164.6 11.9 %collective-permute-done.25.refs_1_ = bf16[3,256,512]{2,1,0:T(8,128)(2,1)S(1)} collective-permute-done((bf16[3,256,512]{2,1,0:T(8,128)(2,1)S(1)}, bf16[3,256,512]{2,1,0:T(8,128)(2,1)S(1)}, u32[]{:S(2)}, u32[]{:S(2)}) %collective-permute-start.25) | collective-permute-done | bytes 786464 | tf_op jit(solution)/shard_map/ppermute | solution.py:515
  178.6 14.8 %collective-permute-done.23.from_left = bf16[3,256,512]{2,1,0:T(8,128)(2,1)S(1)} collective-permute-done((bf16[3,256,512]{2,1,0:T(8,128)(2,1)S(1)}, bf16[3,256,512]{2,1,0:T(8,128)(2,1)S(1)}, u32[]{:S(2)}, u32[]{:S(2)}) %collective-permute-start.23) | collective-permute-done | bytes 786464 | tf_op jit(solution)/shard_map/ppermute | solution.py:515
  194.2 7.3 %attention.3 = (bf16[256,512]{1,0:T(8,128)(2,1)S(1)}, bf16[3,256,512]{2,1,0:T(8,128)(2,1)S(1)}, f32[256,128]{1,0:T(8,128)S(1)}) custom-call(s32[33]{0:T(128)S(1)} %fusion.21.idx, bf16[7,256,256]{2,1,0:T(8,128)(2,1)S(1)} %bitcast_dynamic-update-slice_fusion.mine_r.mine_l.mine, bf16[7,256,256]{2,1,0:T(8,128)(2,1)S(1)} %collective-permute-done.6.other_r.other_l.other, ...), custom_call_target="tpu_custom_call" | custom-call | flops 402653184 | bytes 3145728 | tf_op jit(solution)/shard_map/attention/pallas_call | solution.py:330
  201.5 6.0 %collective-permute-done.27.refs_3_ = bf16[3,256,512]{2,1,0:T(8,128)(2,1)S(1)} collective-permute-done((bf16[3,256,512]{2,1,0:T(8,128)(2,1)S(1)}, bf16[3,256,512]{2,1,0:T(8,128)(2,1)S(1)}, u32[]{:S(2)}, u32[]{:S(2)}) %collective-permute-start.27) | collective-permute-done | bytes 786464 | tf_op jit(solution)/shard_map/ppermute | solution.py:515
  209.0 1.4 collective-permute-start.34
  211.7 21.9 %collective-permute-done.33.refs_1_.refs_2_ = bf16[3,128,512]{2,1,0:T(8,128)(2,1)S(1)} collective-permute-done((bf16[3,128,512]{2,1,0:T(8,128)(2,1)S(1)}, bf16[3,128,512]{2,1,0:T(8,128)(2,1)S(1)}, u32[]{:S(2)}, u32[]{:S(2)}) %collective-permute-start.33) | collective-permute-done | bytes 393248 | tf_op jit(solution)/shard_map/ppermute | solution.py:515
  236.5 9.1 %collective-permute-done.35.refs_3_.refs_4_ = bf16[3,128,512]{2,1,0:T(8,128)(2,1)S(1)} collective-permute-done((bf16[3,128,512]{2,1,0:T(8,128)(2,1)S(1)}, bf16[3,128,512]{2,1,0:T(8,128)(2,1)S(1)}, u32[]{:S(2)}, u32[]{:S(2)}) %collective-permute-start.35) | collective-permute-done | bytes 393248 | tf_op jit(solution)/shard_map/ppermute | solution.py:515
  246.5 1.3 collective-permute-start.38
  248.7 5.3 %collective-permute-done.31.refs_7_ = bf16[3,128,512]{2,1,0:T(8,128)(2,1)S(1)} collective-permute-done((bf16[3,128,512]{2,1,0:T(8,128)(2,1)S(1)}, bf16[3,128,512]{2,1,0:T(8,128)(2,1)S(1)}, u32[]{:S(2)}, u32[]{:S(2)}) %collective-permute-start.31) | collective-permute-done | bytes 393248 | tf_op jit(solution)/shard_map/ppermute | solution.py:515
  256.1 6.4 %collective-permute-done.37.refs_5_.refs_6_ = bf16[3,128,512]{2,1,0:T(8,128)(2,1)S(1)} collective-permute-done((bf16[3,128,512]{2,1,0:T(8,128)(2,1)S(1)}, bf16[3,128,512]{2,1,0:T(8,128)(2,1)S(1)}, u32[]{:S(2)}, u32[]{:S(2)}) %collective-permute-start.37) | collective-permute-done | bytes 393248 | tf_op jit(solution)/shard_map/ppermute | solution.py:515
  266.0 9.3 %term_first.1.before = f32[8,256,512]{2,1,0:T(8,128)} custom-call(s32[33]{0:T(128)} %copy-done.6, bf16[3,1024,512]{2,1,0:T(8,128)(2,1)} %copy-done, bf16[3,256,512]{2,1,0:T(8,128)(2,1)} %copy-done.3, bf16[3,256,512]{2,1,0:T(8,128)(2,1)} %copy-done.14, bf16[3,256,512]{2,1,0:T(8,128)(2,1)} %copy-done.15, bf16[3,256,512]{2,1,0:T(8,128)(2,1)} %copy-done.16, ...), custom_call_target="tpu_custom_call" | custom-call | flops 3221225472 | bytes 6291456 | tf_op jit(solution)/shard_map/term_first/pallas_call | solution.py:435
  275.4 8.1 %term_last.2 = (f32[4,128,512]{2,1,0:T(8,128)}, bf16[4,128,512]{2,1,0:T(8,128)(2,1)}) custom-call(s32[33]{0:T(128)} %copy-done.6, bf16[3,1024,512]{2,1,0:T(8,128)(2,1)} %copy-done, f32[8,256,512]{2,1,0:T(8,128)} %term_first.1.before, bf16[3,128,512]{2,1,0:T(8,128)(2,1)} %copy-done.12, bf16[3,128,512]{2,1,0:T(8,128)(2,1)} %copy-done.20, ...), custom_call_target="tpu_custom_call" | custom-call | flops 1610612736 | bytes 3145728 | tf_op jit(solution)/shard_map/term_last/pallas_call | solution.py:471
  284.4 1.2 collective-permute-start.50
  285.8 2.1 dynamic-slice_convert_fusion.1
  287.9 7.5 %collective-permute-done.49.refs_3_.refs_13_ = bf16[3,128,512]{2,1,0:T(8,128)(2,1)} collective-permute-done((bf16[3,128,512]{2,1,0:T(8,128)(2,1)}, bf16[3,128,512]{2,1,0:T(8,128)(2,1)}, u32[]{:S(2)}, u32[]{:S(2)}) %collective-permute-start.49) | collective-permute-done | bytes 393248 | tf_op jit(solution)/shard_map/ppermute | solution.py:515
  296.2 1.2 collective-permute-start.52
  299.7 1.3 copy-done.1
  301.6 1.2 convert_add_fusion.1
  302.8 3.6 collective-permute-done.51.refs_5_.refs_15_
  311.9 2.1 collective-permute-done.53.refs_7_.refs_17_
  315.5 8.1 %term_last.3 = (f32[4,128,512]{2,1,0:T(8,128)}, bf16[4,128,512]{2,1,0:T(8,128)(2,1)}) custom-call(s32[33]{0:T(128)} %copy-done.6, bf16[3,1024,512]{2,1,0:T(8,128)(2,1)} %copy-done, f32[8,256,512]{2,1,0:T(8,128)} %term_first.1.before, bf16[3,128,512]{2,1,0:T(8,128)(2,1)} %copy-done.13, bf16[3,128,512]{2,1,0:T(8,128)(2,1)} %collective-permute-done.47.refs_1_.refs_11_, ...), custom_call_target="tpu_custom_call" | custom-call | flops 1610612736 | bytes 3145728 | tf_op jit(solution)/shard_map/term_last/pallas_call | solution.py:471
  323.7 3.7 %collective-permute-start.43 = (bf16[128,512]{1,0:T(8,128)(2,1)S(1)}, bf16[128,512]{1,0:T(8,128)(2,1)S(1)}, u32[]{:S(2)}, u32[]{:S(2)}) collective-permute-start(bf16[128,512]{1,0:T(8,128)(2,1)S(1)} %get-tuple-element.104), channel_id=1, source_target_pairs={{0,0},{1,1},{2,8},{3,9},{4,16},{5,17},{6,24},{7,25},{8,2},{9,3},{1... | collective-permute-start | bytes 393224 | tf_op jit(solution)/shard_map/ppermute | solution.py:592
  327.4 2.8 collective-permute-start.44
  330.2 1.4 convert_add_fusion
  331.7 7.9 %grads.2.refs_19_ = f32[3,512,1024]{2,1,0:T(8,128)} custom-call(bf16[512,2048]{1,0:T(8,128)(2,1)} %copy-done.1, bf16[3,256,512]{2,1,0:T(8,128)(2,1)} %copy-done.3, bf16[3,256,512]{2,1,0:T(8,128)(2,1)} %copy-done.14, bf16[3,256,512]{2,1,0:T(8,128)(2,1)} %copy-done.15, bf16[3,256,512]{2,1,0:T(8,128)(2,1)} %copy-done.16, bf16[3,256,512]{2,1,0:T(8,128)(2,1)} %copy-done.17, ...), custom_call_target="tpu_custom_call" | custom-call | flops 3221225472 | bytes 9437184 | tf_op jit(solution)/shard_map/grads/pallas_call | solution.py:401
  339.6 2.2 collective-permute-done.44
  341.9 2.8 collective-permute-done.56
  344.8 1.9 collective-permute-start.57
  346.8 4.3 %collective-permute-start.58 = (bf16[128,512]{1,0:T(8,128)(2,1)S(1)}, bf16[128,512]{1,0:T(8,128)(2,1)S(1)}, u32[]{:S(2)}, u32[]{:S(2)}) collective-permute-start(bf16[128,512]{1,0:T(8,128)(2,1)S(1)} %get-tuple-element.107), channel_id=1, source_target_pairs={{0,1},{1,0},{2,9},{3,8},{4,17},{5,16},{6,25},{7,24},{8,3},{9,2},{1... | collective-permute-start | bytes 393224 | tf_op jit(solution)/shard_map/ppermute | solution.py:592
  351.1 10.4 %grads.3 = f32[3,512,1024]{2,1,0:T(8,128)} custom-call(bf16[512,2048]{1,0:T(8,128)(2,1)} %copy-done.1, bf16[3,128,512]{2,1,0:T(8,128)(2,1)} %copy-done.12, bf16[3,128,512]{2,1,0:T(8,128)(2,1)} %copy-done.20, bf16[3,128,512]{2,1,0:T(8,128)(2,1)} %copy-done.21, bf16[3,128,512]{2,1,0:T(8,128)(2,1)} %copy-done.22, ...), custom_call_target="tpu_custom_call", output_to_operand_aliasing={{}: (19, {})} | custom-call | flops 3221225472 | bytes 9437184 | tf_op jit(solution)/shard_map/grads/pallas_call | solution.py:401
  (169 shorter events, 43.3 us)
Async XLA Ops:
  3.7 190.5 %copy-start.6 = (s32[33]{0:T(128)}, s32[33]{0:T(128)S(1)}, u32[]{:S(2)}) copy-start(s32[33]{0:T(128)S(1)} %fusion.21.idx) | copy-start | bytes 400
  5.1 8.6 %collective-permute-start = (bf16[256,256]{1,0:T(8,128)(2,1)S(1)}, bf16[256,256]{1,0:T(8,128)(2,1)S(1)}, u32[]{:S(2)}, u32[]{:S(2)}) collective-permute-start(bf16[256,256]{1,0:T(8,128)(2,1)S(1)} %get-tuple-element.49), channel_id=1, source_target_pairs={{0,2},{2,4},{4,6},{6,7},{7,5},{5,3},{3,1},{1,0},{8,10},{10,12},{12... | collective-permute-start | bytes 393224 | tf_op jit(solution)/shard_map/ppermute | solution.py:515
  6.7 8.4 %collective-permute-start.1 = (bf16[256,256]{1,0:T(8,128)(2,1)S(1)}, bf16[256,256]{1,0:T(8,128)(2,1)S(1)}, u32[]{:S(2)}, u32[]{:S(2)}) collective-permute-start(bf16[256,256]{1,0:T(8,128)(2,1)S(1)} %get-tuple-element.50), channel_id=1, source_target_pairs={{0,1},{2,0},{4,2},{6,4},{7,6},{5,7},{3,5},{1,3},{8,9},{10,8},{12,1... | collective-permute-start | bytes 393224 | tf_op jit(solution)/shard_map/ppermute | solution.py:515
  7.2 8.1 %collective-permute-start.2 = (bf16[256,256]{1,0:T(8,128)(2,1)S(1)}, bf16[256,256]{1,0:T(8,128)(2,1)S(1)}, u32[]{:S(2)}, u32[]{:S(2)}) collective-permute-start(bf16[256,256]{1,0:T(8,128)(2,1)S(1)} %get-tuple-element.51), channel_id=1, source_target_pairs={{0,4},{2,6},{4,7},{6,5},{7,3},{5,1},{3,0},{1,2},{8,12},{10,14},{12... | collective-permute-start | bytes 393224 | tf_op jit(solution)/shard_map/ppermute | solution.py:515
  9.8 6.9 %collective-permute-start.3 = (bf16[256,256]{1,0:T(8,128)(2,1)S(1)}, bf16[256,256]{1,0:T(8,128)(2,1)S(1)}, u32[]{:S(2)}, u32[]{:S(2)}) collective-permute-start(bf16[256,256]{1,0:T(8,128)(2,1)S(1)} %get-tuple-element.52), channel_id=1, source_target_pairs={{0,3},{2,1},{4,0},{6,2},{7,4},{5,6},{3,7},{1,5},{8,11},{10,9},{12,... | collective-permute-start | bytes 393224 | tf_op jit(solution)/shard_map/ppermute | solution.py:515
  10.1 16.3 %collective-permute-start.4 = (bf16[256,256]{1,0:T(8,128)(2,1)S(1)}, bf16[256,256]{1,0:T(8,128)(2,1)S(1)}, u32[]{:S(2)}, u32[]{:S(2)}) collective-permute-start(bf16[256,256]{1,0:T(8,128)(2,1)S(1)} %get-tuple-element.53), channel_id=1, source_target_pairs={{0,6},{2,7},{4,5},{6,3},{7,1},{5,0},{3,2},{1,4},{8,14},{10,15},{12... | collective-permute-start | bytes 393224 | tf_op jit(solution)/shard_map/ppermute | solution.py:515
  13.7 12.7 %collective-permute-start.5 = (bf16[256,256]{1,0:T(8,128)(2,1)S(1)}, bf16[256,256]{1,0:T(8,128)(2,1)S(1)}, u32[]{:S(2)}, u32[]{:S(2)}) collective-permute-start(bf16[256,256]{1,0:T(8,128)(2,1)S(1)} %get-tuple-element.54), channel_id=1, source_target_pairs={{0,5},{2,3},{4,1},{6,0},{7,2},{5,4},{3,6},{1,7},{8,13},{10,11},{12... | collective-permute-start | bytes 393224 | tf_op jit(solution)/shard_map/ppermute | solution.py:515
  26.4 25.1 %collective-permute-start.6 = (bf16[7,256,256]{2,1,0:T(8,128)(2,1)S(1)}, bf16[7,256,256]{2,1,0:T(8,128)(2,1)S(1)}, u32[]{:S(2)}, u32[]{:S(2)}) collective-permute-start(bf16[7,256,256]{2,1,0:T(8,128)(2,1)S(1)} %bitcast_dynamic-update-slice_fusion.mine_r.mine_l.mine), channel_id=1, source_target_pairs={{0,8},{8,0},{16,24},{24,16},{1,9},{9,1},{17,25},{25,17},{2,10},{10... | collective-permute-start | bytes 2752520 | tf_op jit(solution)/shard_map/ppermute | solution.py:518
  26.5 8.6 %collective-permute-start.7 = (bf16[256,256]{1,0:T(8,128)(2,1)S(1)}, bf16[256,256]{1,0:T(8,128)(2,1)S(1)}, u32[]{:S(2)}, u32[]{:S(2)}) collective-permute-start(bf16[256,256]{1,0:T(8,128)(2,1)S(1)} %get-tuple-element.56), channel_id=1, source_target_pairs={{0,7},{2,5},{4,3},{6,1},{7,0},{5,2},{3,4},{1,6},{8,15},{10,13},{12... | collective-permute-start | bytes 393224 | tf_op jit(solution)/shard_map/ppermute | solution.py:515
  35.1 2.7 collective-permute-start.8
  39.8 11.7 %collective-permute-start.9 = (bf16[3,128,512]{2,1,0:T(8,128)(2,1)S(1)}, bf16[3,128,512]{2,1,0:T(8,128)(2,1)S(1)}, u32[]{:S(2)}, u32[]{:S(2)}) collective-permute-start(bf16[3,128,512]{2,1,0:T(8,128)(2,1)S(1)} %get-tuple-element.57), channel_id=1, source_target_pairs={{0,2},{2,4},{4,6},{6,7},{7,5},{5,3},{3,1},{1,0},{8,10},{10,12},{12... | collective-permute-start | bytes 1179656 | tf_op jit(solution)/shard_map/ppermute | solution.py:515
  39.8 11.7 %collective-permute-start.10 = (bf16[3,128,512]{2,1,0:T(8,128)(2,1)S(1)}, bf16[3,128,512]{2,1,0:T(8,128)(2,1)S(1)}, u32[]{:S(2)}, u32[]{:S(2)}) collective-permute-start(bf16[3,128,512]{2,1,0:T(8,128)(2,1)S(1)} %get-tuple-element.58), channel_id=1, source_target_pairs={{0,1},{2,0},{4,2},{6,4},{7,6},{5,7},{3,5},{1,3},{8,9},{10,8},{12,1... | collective-permute-start | bytes 1179656 | tf_op jit(solution)/shard_map/ppermute | solution.py:515
  53.6 19.3 %collective-permute-start.11 = (bf16[3,256,512]{2,1,0:T(8,128)(2,1)S(1)}, bf16[3,256,512]{2,1,0:T(8,128)(2,1)S(1)}, u32[]{:S(2)}, u32[]{:S(2)}) collective-permute-start(bf16[3,256,512]{2,1,0:T(8,128)(2,1)S(1)} %get-tuple-element.59), channel_id=1, source_target_pairs={{0,2},{2,4},{4,6},{6,7},{7,5},{5,3},{3,1},{1,0},{8,10},{10,12},{12... | collective-permute-start | bytes 2359304 | tf_op jit(solution)/shard_map/ppermute | solution.py:515
  55.2 18.9 %collective-permute-start.12 = (bf16[3,256,512]{2,1,0:T(8,128)(2,1)S(1)}, bf16[3,256,512]{2,1,0:T(8,128)(2,1)S(1)}, u32[]{:S(2)}, u32[]{:S(2)}) collective-permute-start(bf16[3,256,512]{2,1,0:T(8,128)(2,1)S(1)} %get-tuple-element.60), channel_id=1, source_target_pairs={{0,1},{2,0},{4,2},{6,4},{7,6},{5,7},{3,5},{1,3},{8,9},{10,8},{12,1... | collective-permute-start | bytes 2359304 | tf_op jit(solution)/shard_map/ppermute | solution.py:515
  76.1 31.4 %collective-permute-start.13 = (bf16[3,256,512]{2,1,0:T(8,128)(2,1)S(1)}, bf16[3,256,512]{2,1,0:T(8,128)(2,1)S(1)}, u32[]{:S(2)}, u32[]{:S(2)}) collective-permute-start(bf16[3,256,512]{2,1,0:T(8,128)(2,1)S(1)} %get-tuple-element.61), channel_id=1, source_target_pairs={{0,2},{2,4},{4,6},{6,7},{7,5},{5,3},{3,1},{1,0},{8,10},{10,12},{12... | collective-permute-start | bytes 2359304 | tf_op jit(solution)/shard_map/ppermute | solution.py:515
  77.6 29.9 %collective-permute-start.14 = (bf16[3,256,512]{2,1,0:T(8,128)(2,1)S(1)}, bf16[3,256,512]{2,1,0:T(8,128)(2,1)S(1)}, u32[]{:S(2)}, u32[]{:S(2)}) collective-permute-start(bf16[3,256,512]{2,1,0:T(8,128)(2,1)S(1)} %get-tuple-element.62), channel_id=1, source_target_pairs={{0,1},{2,0},{4,2},{6,4},{7,6},{5,7},{3,5},{1,3},{8,9},{10,8},{12,1... | collective-permute-start | bytes 2359304 | tf_op jit(solution)/shard_map/ppermute | solution.py:515
  78.2 24.4 %collective-permute-start.17 = (bf16[3,128,512]{2,1,0:T(8,128)(2,1)S(1)}, bf16[3,128,512]{2,1,0:T(8,128)(2,1)S(1)}, u32[]{:S(2)}, u32[]{:S(2)}) collective-permute-start(bf16[3,128,512]{2,1,0:T(8,128)(2,1)S(1)} %get-tuple-element.66), channel_id=1, source_target_pairs={{0,2},{2,4},{4,6},{6,7},{7,5},{5,3},{3,1},{1,0},{8,10},{10,12},{12... | collective-permute-start | bytes 1179656 | tf_op jit(solution)/shard_map/ppermute | solution.py:515
  79.6 23.7 %collective-permute-start.18 = (bf16[3,128,512]{2,1,0:T(8,128)(2,1)S(1)}, bf16[3,128,512]{2,1,0:T(8,128)(2,1)S(1)}, u32[]{:S(2)}, u32[]{:S(2)}) collective-permute-start(bf16[3,128,512]{2,1,0:T(8,128)(2,1)S(1)} %get-tuple-element.67), channel_id=1, source_target_pairs={{0,1},{2,0},{4,2},{6,4},{7,6},{5,7},{3,5},{1,3},{8,9},{10,8},{12,1... | collective-permute-start | bytes 1179656 | tf_op jit(solution)/shard_map/ppermute | solution.py:515
  105.4 20.5 %collective-permute-start.19 = (bf16[3,256,512]{2,1,0:T(8,128)(2,1)S(1)}, bf16[3,256,512]{2,1,0:T(8,128)(2,1)S(1)}, u32[]{:S(2)}, u32[]{:S(2)}) collective-permute-start(bf16[3,256,512]{2,1,0:T(8,128)(2,1)S(1)} %get-tuple-element.68), channel_id=1, source_target_pairs={{0,2},{2,4},{4,6},{6,7},{7,5},{5,3},{3,1},{1,0},{8,10},{10,12},{12... | collective-permute-start | bytes 2359304 | tf_op jit(solution)/shard_map/ppermute | solution.py:515
  106.3 20.5 %collective-permute-start.20 = (bf16[3,256,512]{2,1,0:T(8,128)(2,1)S(1)}, bf16[3,256,512]{2,1,0:T(8,128)(2,1)S(1)}, u32[]{:S(2)}, u32[]{:S(2)}) collective-permute-start(bf16[3,256,512]{2,1,0:T(8,128)(2,1)S(1)} %get-tuple-element.69), channel_id=1, source_target_pairs={{0,1},{2,0},{4,2},{6,4},{7,6},{5,7},{3,5},{1,3},{8,9},{10,8},{12,1... | collective-permute-start | bytes 2359304 | tf_op jit(solution)/shard_map/ppermute | solution.py:515
  109.6 33.2 %collective-permute-start.15 = (bf16[3,256,512]{2,1,0:T(8,128)(2,1)S(1)}, bf16[3,256,512]{2,1,0:T(8,128)(2,1)S(1)}, u32[]{:S(2)}, u32[]{:S(2)}) collective-permute-start(bf16[3,256,512]{2,1,0:T(8,128)(2,1)S(1)} %get-tuple-element.63), channel_id=1, source_target_pairs={{0,2},{2,4},{4,6},{6,7},{7,5},{5,3},{3,1},{1,0},{8,10},{10,12},{12... | collective-permute-start | bytes 2359304 | tf_op jit(solution)/shard_map/ppermute | solution.py:515
  110.4 33.2 %collective-permute-start.16 = (bf16[3,256,512]{2,1,0:T(8,128)(2,1)S(1)}, bf16[3,256,512]{2,1,0:T(8,128)(2,1)S(1)}, u32[]{:S(2)}, u32[]{:S(2)}) collective-permute-start(bf16[3,256,512]{2,1,0:T(8,128)(2,1)S(1)} %get-tuple-element.64), channel_id=1, source_target_pairs={{0,1},{2,0},{4,2},{6,4},{7,6},{5,7},{3,5},{1,3},{8,9},{10,8},{12,1... | collective-permute-start | bytes 2359304 | tf_op jit(solution)/shard_map/ppermute | solution.py:515
  128.8 30.8 %collective-permute-start.21 = (bf16[3,256,512]{2,1,0:T(8,128)(2,1)S(1)}, bf16[3,256,512]{2,1,0:T(8,128)(2,1)S(1)}, u32[]{:S(2)}, u32[]{:S(2)}) collective-permute-start(bf16[3,256,512]{2,1,0:T(8,128)(2,1)S(1)} %get-tuple-element.70), channel_id=1, source_target_pairs={{0,2},{2,4},{4,6},{6,7},{7,5},{5,3},{3,1},{1,0},{8,10},{10,12},{12... | collective-permute-start | bytes 2359304 | tf_op jit(solution)/shard_map/ppermute | solution.py:515
  129.5 31.0 %collective-permute-start.22 = (bf16[3,256,512]{2,1,0:T(8,128)(2,1)S(1)}, bf16[3,256,512]{2,1,0:T(8,128)(2,1)S(1)}, u32[]{:S(2)}, u32[]{:S(2)}) collective-permute-start(bf16[3,256,512]{2,1,0:T(8,128)(2,1)S(1)} %get-tuple-element.71), channel_id=1, source_target_pairs={{0,1},{2,0},{4,2},{6,4},{7,6},{5,7},{3,5},{1,3},{8,9},{10,8},{12,1... | collective-permute-start | bytes 2359304 | tf_op jit(solution)/shard_map/ppermute | solution.py:515
  150.9 25.7 %collective-permute-start.25 = (bf16[3,256,512]{2,1,0:T(8,128)(2,1)S(1)}, bf16[3,256,512]{2,1,0:T(8,128)(2,1)S(1)}, u32[]{:S(2)}, u32[]{:S(2)}) collective-permute-start(bf16[3,256,512]{2,1,0:T(8,128)(2,1)S(1)} %get-tuple-element.77.refs_0_), channel_id=1, source_target_pairs={{0,2},{2,4},{4,6},{6,7},{7,5},{5,3},{3,1},{1,0},{8,10},{10,12},{12... | collective-permute-start | bytes 2359304 | tf_op jit(solution)/shard_map/ppermute | solution.py:515
  151.5 25.8 %collective-permute-start.26 = (bf16[3,256,512]{2,1,0:T(8,128)(2,1)S(1)}, bf16[3,256,512]{2,1,0:T(8,128)(2,1)S(1)}, u32[]{:S(2)}, u32[]{:S(2)}) collective-permute-start(bf16[3,256,512]{2,1,0:T(8,128)(2,1)S(1)} %get-tuple-element.77.refs_0_), channel_id=1, source_target_pairs={{0,1},{2,0},{4,2},{6,4},{7,6},{5,7},{3,5},{1,3},{8,9},{10,8},{12,1... | collective-permute-start | bytes 2359304 | tf_op jit(solution)/shard_map/ppermute | solution.py:515
  162.6 30.8 %collective-permute-start.23 = (bf16[3,256,512]{2,1,0:T(8,128)(2,1)S(1)}, bf16[3,256,512]{2,1,0:T(8,128)(2,1)S(1)}, u32[]{:S(2)}, u32[]{:S(2)}) collective-permute-start(bf16[3,256,512]{2,1,0:T(8,128)(2,1)S(1)} %get-tuple-element.72), channel_id=1, source_target_pairs={{0,2},{2,4},{4,6},{6,7},{7,5},{5,3},{3,1},{1,0},{8,10},{10,12},{12... | collective-permute-start | bytes 2359304 | tf_op jit(solution)/shard_map/ppermute | solution.py:515
  163.2 31.0 %collective-permute-start.24 = (bf16[3,256,512]{2,1,0:T(8,128)(2,1)S(1)}, bf16[3,256,512]{2,1,0:T(8,128)(2,1)S(1)}, u32[]{:S(2)}, u32[]{:S(2)}) collective-permute-start(bf16[3,256,512]{2,1,0:T(8,128)(2,1)S(1)} %get-tuple-element.73), channel_id=1, source_target_pairs={{0,1},{2,0},{4,2},{6,4},{7,6},{5,7},{3,5},{1,3},{8,9},{10,8},{12,1... | collective-permute-start | bytes 2359304 | tf_op jit(solution)/shard_map/ppermute | solution.py:515
  176.5 30.9 %collective-permute-start.27 = (bf16[3,256,512]{2,1,0:T(8,128)(2,1)S(1)}, bf16[3,256,512]{2,1,0:T(8,128)(2,1)S(1)}, u32[]{:S(2)}, u32[]{:S(2)}) collective-permute-start(bf16[3,256,512]{2,1,0:T(8,128)(2,1)S(1)} %collective-permute-done.25.refs_1_), channel_id=1, source_target_pairs={{0,2},{2,4},{4,6},{6,7},{7,5},{5,3},{3,1},{1,0},{8,10},{10,12},{12... | collective-permute-start | bytes 2359304 | tf_op jit(solution)/shard_map/ppermute | solution.py:515
  177.3 33.1 %collective-permute-start.28 = (bf16[3,256,512]{2,1,0:T(8,128)(2,1)S(1)}, bf16[3,256,512]{2,1,0:T(8,128)(2,1)S(1)}, u32[]{:S(2)}, u32[]{:S(2)}) collective-permute-start(bf16[3,256,512]{2,1,0:T(8,128)(2,1)S(1)} %collective-permute-done.26.refs_2_), channel_id=1, source_target_pairs={{0,1},{2,0},{4,2},{6,4},{7,6},{5,7},{3,5},{1,3},{8,9},{10,8},{12,1... | collective-permute-start | bytes 2359304 | tf_op jit(solution)/shard_map/ppermute | solution.py:515
  207.4 58.6 %copy-start.16 = (bf16[3,256,512]{2,1,0:T(8,128)(2,1)}, bf16[3,256,512]{2,1,0:T(8,128)(2,1)S(1)}, u32[]{:S(2)}) copy-start(bf16[3,256,512]{2,1,0:T(8,128)(2,1)S(1)} %collective-permute-done.27.refs_3_) | copy-start | bytes 2359300
  207.5 28.2 %collective-permute-start.29 = (bf16[3,256,512]{2,1,0:T(8,128)(2,1)S(1)}, bf16[3,256,512]{2,1,0:T(8,128)(2,1)S(1)}, u32[]{:S(2)}, u32[]{:S(2)}) collective-permute-start(bf16[3,256,512]{2,1,0:T(8,128)(2,1)S(1)} %collective-permute-done.27.refs_3_), channel_id=1, source_target_pairs={{0,2},{2,4},{4,6},{6,7},{7,5},{5,3},{3,1},{1,0},{8,10},{10,12},{12... | collective-permute-start | bytes 2359304 | tf_op jit(solution)/shard_map/ppermute | solution.py:515
  208.3 67.0 %copy-start.12 = (bf16[3,128,512]{2,1,0:T(8,128)(2,1)}, bf16[3,128,512]{2,1,0:T(8,128)(2,1)S(1)}, u32[]{:S(2)}) copy-start(bf16[3,128,512]{2,1,0:T(8,128)(2,1)S(1)} %get-tuple-element.80.refs_0_.refs_1_) | copy-start | bytes 1179652
  208.4 67.0 %copy-start.13 = (bf16[3,128,512]{2,1,0:T(8,128)(2,1)}, bf16[3,128,512]{2,1,0:T(8,128)(2,1)S(1)}, u32[]{:S(2)}) copy-start(bf16[3,128,512]{2,1,0:T(8,128)(2,1)S(1)} %get-tuple-element.86.refs_0_.refs_10_) | copy-start | bytes 1179652
  208.4 25.2 %collective-permute-start.33 = (bf16[3,128,512]{2,1,0:T(8,128)(2,1)S(1)}, bf16[3,128,512]{2,1,0:T(8,128)(2,1)S(1)}, u32[]{:S(2)}, u32[]{:S(2)}) collective-permute-start(bf16[3,128,512]{2,1,0:T(8,128)(2,1)S(1)} %get-tuple-element.80.refs_0_.refs_1_), channel_id=1, source_target_pairs={{0,2},{2,4},{4,6},{6,7},{7,5},{5,3},{3,1},{1,0},{8,10},{10,12},{12... | collective-permute-start | bytes 1179656 | tf_op jit(solution)/shard_map/ppermute | solution.py:515
  209.0 25.4 %collective-permute-start.34 = (bf16[3,128,512]{2,1,0:T(8,128)(2,1)S(1)}, bf16[3,128,512]{2,1,0:T(8,128)(2,1)S(1)}, u32[]{:S(2)}, u32[]{:S(2)}) collective-permute-start(bf16[3,128,512]{2,1,0:T(8,128)(2,1)S(1)} %get-tuple-element.80.refs_0_.refs_1_), channel_id=1, source_target_pairs={{0,1},{2,0},{4,2},{6,4},{7,6},{5,7},{3,5},{1,3},{8,9},{10,8},{12,1... | collective-permute-start | bytes 1179656 | tf_op jit(solution)/shard_map/ppermute | solution.py:515
  210.5 43.6 %copy-start.17 = (bf16[3,256,512]{2,1,0:T(8,128)(2,1)}, bf16[3,256,512]{2,1,0:T(8,128)(2,1)S(1)}, u32[]{:S(2)}) copy-start(bf16[3,256,512]{2,1,0:T(8,128)(2,1)S(1)} %collective-permute-done.28.refs_4_) | copy-start | bytes 2359300
  210.5 37.3 %collective-permute-start.30 = (bf16[3,256,512]{2,1,0:T(8,128)(2,1)S(1)}, bf16[3,256,512]{2,1,0:T(8,128)(2,1)S(1)}, u32[]{:S(2)}, u32[]{:S(2)}) collective-permute-start(bf16[3,256,512]{2,1,0:T(8,128)(2,1)S(1)} %collective-permute-done.28.refs_4_), channel_id=1, source_target_pairs={{0,1},{2,0},{4,2},{6,4},{7,6},{5,7},{3,5},{1,3},{8,9},{10,8},{12,1... | collective-permute-start | bytes 2359304 | tf_op jit(solution)/shard_map/ppermute | solution.py:515
  233.6 12.1 %collective-permute-start.35 = (bf16[3,128,512]{2,1,0:T(8,128)(2,1)S(1)}, bf16[3,128,512]{2,1,0:T(8,128)(2,1)S(1)}, u32[]{:S(2)}, u32[]{:S(2)}) collective-permute-start(bf16[3,128,512]{2,1,0:T(8,128)(2,1)S(1)} %collective-permute-done.33.refs_1_.refs_2_), channel_id=1, source_target_pairs={{0,2},{2,4},{4,6},{6,7},{7,5},{5,3},{3,1},{1,0},{8,10},{10,12},{12... | collective-permute-start | bytes 1179656 | tf_op jit(solution)/shard_map/ppermute | solution.py:515
  234.4 12.1 %collective-permute-start.36 = (bf16[3,128,512]{2,1,0:T(8,128)(2,1)S(1)}, bf16[3,128,512]{2,1,0:T(8,128)(2,1)S(1)}, u32[]{:S(2)}, u32[]{:S(2)}) collective-permute-start(bf16[3,128,512]{2,1,0:T(8,128)(2,1)S(1)} %collective-permute-done.34.refs_2_.refs_3_), channel_id=1, source_target_pairs={{0,1},{2,0},{4,2},{6,4},{7,6},{5,7},{3,5},{1,3},{8,9},{10,8},{12,1... | collective-permute-start | bytes 1179656 | tf_op jit(solution)/shard_map/ppermute | solution.py:515
  235.7 18.4 %collective-permute-start.31 = (bf16[3,128,512]{2,1,0:T(8,128)(2,1)S(1)}, bf16[3,128,512]{2,1,0:T(8,128)(2,1)S(1)}, u32[]{:S(2)}, u32[]{:S(2)}) collective-permute-start(bf16[3,128,512]{2,1,0:T(8,128)(2,1)S(1)} %slice.61), channel_id=1, source_target_pairs={{0,2},{2,4},{4,6},{6,7},{7,5},{5,3},{3,1},{1,0},{8,10},{10,12},{12... | collective-permute-start | bytes 1179656 | tf_op jit(solution)/shard_map/ppermute | solution.py:515
  245.6 16.9 %collective-permute-start.37 = (bf16[3,128,512]{2,1,0:T(8,128)(2,1)S(1)}, bf16[3,128,512]{2,1,0:T(8,128)(2,1)S(1)}, u32[]{:S(2)}, u32[]{:S(2)}) collective-permute-start(bf16[3,128,512]{2,1,0:T(8,128)(2,1)S(1)} %collective-permute-done.35.refs_3_.refs_4_), channel_id=1, source_target_pairs={{0,2},{2,4},{4,6},{6,7},{7,5},{5,3},{3,1},{1,0},{8,10},{10,12},{12... | collective-permute-start | bytes 1179656 | tf_op jit(solution)/shard_map/ppermute | solution.py:515
  246.5 17.6 %collective-permute-start.38 = (bf16[3,128,512]{2,1,0:T(8,128)(2,1)S(1)}, bf16[3,128,512]{2,1,0:T(8,128)(2,1)S(1)}, u32[]{:S(2)}, u32[]{:S(2)}) collective-permute-start(bf16[3,128,512]{2,1,0:T(8,128)(2,1)S(1)} %collective-permute-done.36.refs_4_.refs_5_), channel_id=1, source_target_pairs={{0,1},{2,0},{4,2},{6,4},{7,6},{5,7},{3,5},{1,3},{8,9},{10,8},{12,1... | collective-permute-start | bytes 1179656 | tf_op jit(solution)/shard_map/ppermute | solution.py:515
  247.8 18.2 %collective-permute-start.32 = (bf16[3,128,512]{2,1,0:T(8,128)(2,1)S(1)}, bf16[3,128,512]{2,1,0:T(8,128)(2,1)}, u32[]{:S(2)}, u32[]{:S(2)}) collective-permute-start(bf16[3,128,512]{2,1,0:T(8,128)(2,1)S(1)} %slice.62), channel_id=1, source_target_pairs={{0,1},{2,0},{4,2},{6,4},{7,6},{5,7},{3,5},{1,3},{8,9},{10,8},{12,1... | collective-permute-start | bytes 1179656 | tf_op jit(solution)/shard_map/ppermute | solution.py:515
  254.1 29.5 %collective-permute-start.47 = (bf16[3,128,512]{2,1,0:T(8,128)(2,1)S(1)}, bf16[3,128,512]{2,1,0:T(8,128)(2,1)}, u32[]{:S(2)}, u32[]{:S(2)}) collective-permute-start(bf16[3,128,512]{2,1,0:T(8,128)(2,1)S(1)} %get-tuple-element.86.refs_0_.refs_10_), channel_id=1, source_target_pairs={{0,2},{2,4},{4,6},{6,7},{7,5},{5,3},{3,1},{1,0},{8,10},{10,12},{12... | collective-permute-start | bytes 1179656 | tf_op jit(solution)/shard_map/ppermute | solution.py:515
  254.9 28.7 %collective-permute-start.48 = (bf16[3,128,512]{2,1,0:T(8,128)(2,1)S(1)}, bf16[3,128,512]{2,1,0:T(8,128)(2,1)}, u32[]{:S(2)}, u32[]{:S(2)}) collective-permute-start(bf16[3,128,512]{2,1,0:T(8,128)(2,1)S(1)} %get-tuple-element.86.refs_0_.refs_10_), channel_id=1, source_target_pairs={{0,1},{2,0},{4,2},{6,4},{7,6},{5,7},{3,5},{1,3},{8,9},{10,8},{12,1... | collective-permute-start | bytes 1179656 | tf_op jit(solution)/shard_map/ppermute | solution.py:515
  263.2 12.1 %collective-permute-start.39 = (bf16[3,64,512]{2,1,0:T(8,128)(2,1)}, bf16[3,64,512]{2,1,0:T(8,128)(2,1)}, u32[]{:S(2)}, u32[]{:S(2)}) collective-permute-start(bf16[3,64,512]{2,1,0:T(8,128)(2,1)} %slice.63), channel_id=1, source_target_pairs={{0,2},{2,4},{4,6},{6,7},{7,5},{5,3},{3,1},{1,0},{8,10},{10,12},{12... | collective-permute-start | bytes 589832 | tf_op jit(solution)/shard_map/ppermute | solution.py:515
  264.8 10.6 %collective-permute-start.40 = (bf16[3,64,512]{2,1,0:T(8,128)(2,1)}, bf16[3,64,512]{2,1,0:T(8,128)(2,1)}, u32[]{:S(2)}, u32[]{:S(2)}) collective-permute-start(bf16[3,64,512]{2,1,0:T(8,128)(2,1)} %slice.64), channel_id=1, source_target_pairs={{0,1},{2,0},{4,2},{6,4},{7,6},{5,7},{3,5},{1,3},{8,9},{10,8},{12,1... | collective-permute-start | bytes 589832 | tf_op jit(solution)/shard_map/ppermute | solution.py:515
  283.5 18.0 %collective-permute-start.41 = (bf16[4,128,512]{2,1,0:T(8,128)(2,1)}, bf16[4,128,512]{2,1,0:T(8,128)(2,1)}, u32[]{:S(2)}, u32[]{:S(2)}) collective-permute-start(bf16[4,128,512]{2,1,0:T(8,128)(2,1)} %get-tuple-element.82), channel_id=1, source_target_pairs={{0,8},{8,0},{16,24},{24,16},{1,9},{9,1},{17,25},{25,17},{2,10},{10... | collective-permute-start | bytes 1572872 | tf_op jit(solution)/shard_map/ppermute | solution.py:518
  283.6 11.8 %collective-permute-start.49 = (bf16[3,128,512]{2,1,0:T(8,128)(2,1)}, bf16[3,128,512]{2,1,0:T(8,128)(2,1)}, u32[]{:S(2)}, u32[]{:S(2)}) collective-permute-start(bf16[3,128,512]{2,1,0:T(8,128)(2,1)} %collective-permute-done.47.refs_1_.refs_11_), channel_id=1, source_target_pairs={{0,2},{2,4},{4,6},{6,7},{7,5},{5,3},{3,1},{1,0},{8,10},{10,12},{12... | collective-permute-start | bytes 1179656 | tf_op jit(solution)/shard_map/ppermute | solution.py:515
  284.4 11.8 %collective-permute-start.50 = (bf16[3,128,512]{2,1,0:T(8,128)(2,1)}, bf16[3,128,512]{2,1,0:T(8,128)(2,1)}, u32[]{:S(2)}, u32[]{:S(2)}) collective-permute-start(bf16[3,128,512]{2,1,0:T(8,128)(2,1)} %collective-permute-done.48.refs_2_.refs_12_), channel_id=1, source_target_pairs={{0,1},{2,0},{4,2},{6,4},{7,6},{5,7},{3,5},{1,3},{8,9},{10,8},{12,1... | collective-permute-start | bytes 1179656 | tf_op jit(solution)/shard_map/ppermute | solution.py:515
  295.4 11.0 %collective-permute-start.51 = (bf16[3,128,512]{2,1,0:T(8,128)(2,1)}, bf16[3,128,512]{2,1,0:T(8,128)(2,1)}, u32[]{:S(2)}, u32[]{:S(2)}) collective-permute-start(bf16[3,128,512]{2,1,0:T(8,128)(2,1)} %collective-permute-done.49.refs_3_.refs_13_), channel_id=1, source_target_pairs={{0,2},{2,4},{4,6},{6,7},{7,5},{5,3},{3,1},{1,0},{8,10},{10,12},{12... | collective-permute-start | bytes 1179656 | tf_op jit(solution)/shard_map/ppermute | solution.py:515
  296.2 11.1 %collective-permute-start.52 = (bf16[3,128,512]{2,1,0:T(8,128)(2,1)}, bf16[3,128,512]{2,1,0:T(8,128)(2,1)}, u32[]{:S(2)}, u32[]{:S(2)}) collective-permute-start(bf16[3,128,512]{2,1,0:T(8,128)(2,1)} %collective-permute-done.50.refs_4_.refs_14_), channel_id=1, source_target_pairs={{0,1},{2,0},{4,2},{6,4},{7,6},{5,7},{3,5},{1,3},{8,9},{10,8},{12,1... | collective-permute-start | bytes 1179656 | tf_op jit(solution)/shard_map/ppermute | solution.py:515
  298.3 2.7 collective-permute-start.45
  301.0 10.2 %collective-permute-start.46 = (f32[256,1]{0,1:T(1,128)S(1)}, f32[256,1]{0,1:T(1,128)S(1)}, u32[]{:S(2)}, u32[]{:S(2)}) collective-permute-start(f32[256,1]{0,1:T(1,128)S(1)} %add.119), channel_id=1, source_target_pairs={{0,16},{8,24},{16,0},{24,8},{1,17},{9,25},{17,1},{25,9},{2,18},{10... | collective-permute-start | bytes 3080 | tf_op jit(solution)/shard_map/ppermute | solution.py:518
  308.3 5.7 %collective-permute-start.53 = (bf16[3,64,512]{2,1,0:T(8,128)(2,1)S(1)}, bf16[3,64,512]{2,1,0:T(8,128)(2,1)S(1)}, u32[]{:S(2)}, u32[]{:S(2)}) collective-permute-start(bf16[3,64,512]{2,1,0:T(8,128)(2,1)S(1)} %slice.67), channel_id=1, source_target_pairs={{0,2},{2,4},{4,6},{6,7},{7,5},{5,3},{3,1},{1,0},{8,10},{10,12},{12... | collective-permute-start | bytes 589832 | tf_op jit(solution)/shard_map/ppermute | solution.py:515
  309.2 5.7 %collective-permute-start.54 = (bf16[3,64,512]{2,1,0:T(8,128)(2,1)S(1)}, bf16[3,64,512]{2,1,0:T(8,128)(2,1)S(1)}, u32[]{:S(2)}, u32[]{:S(2)}) collective-permute-start(bf16[3,64,512]{2,1,0:T(8,128)(2,1)S(1)} %slice.68), channel_id=1, source_target_pairs={{0,1},{2,0},{4,2},{6,4},{7,6},{5,7},{3,5},{1,3},{8,9},{10,8},{12,1... | collective-permute-start | bytes 589832 | tf_op jit(solution)/shard_map/ppermute | solution.py:515
  311.3 12.3 %collective-permute-start.42 = (bf16[1,2,128,512]{3,2,1,0:T(8,128)(2,1)S(1)}, bf16[1,2,128,512]{3,2,1,0:T(8,128)(2,1)S(1)}, u32[]{:S(2)}, u32[]{:S(2)}) collective-permute-start(bf16[1,2,128,512]{3,2,1,0:T(8,128)(2,1)S(1)} %fusion.10), channel_id=1, source_target_pairs={{0,16},{8,24},{16,0},{24,8},{1,17},{9,25},{17,1},{25,9},{2,18},{10... | collective-permute-start | bytes 786440 | tf_op jit(solution)/shard_map/ppermute | solution.py:518
  323.6 6.6 %collective-permute-start.55 = (bf16[4,128,512]{2,1,0:T(8,128)(2,1)}, bf16[4,128,512]{2,1,0:T(8,128)(2,1)S(1)}, u32[]{:S(2)}, u32[]{:S(2)}) collective-permute-start(bf16[4,128,512]{2,1,0:T(8,128)(2,1)} %get-tuple-element.92), channel_id=1, source_target_pairs={{0,8},{8,0},{16,24},{24,16},{1,9},{9,1},{17,25},{25,17},{2,10},{10... | collective-permute-start | bytes 1572872 | tf_op jit(solution)/shard_map/ppermute | solution.py:518
  323.7 15.9 %collective-permute-start.43 = (bf16[128,512]{1,0:T(8,128)(2,1)S(1)}, bf16[128,512]{1,0:T(8,128)(2,1)S(1)}, u32[]{:S(2)}, u32[]{:S(2)}) collective-permute-start(bf16[128,512]{1,0:T(8,128)(2,1)S(1)} %get-tuple-element.104), channel_id=1, source_target_pairs={{0,0},{1,1},{2,8},{3,9},{4,16},{5,17},{6,24},{7,25},{8,2},{9,3},{1... | collective-permute-start | bytes 393224 | tf_op jit(solution)/shard_map/ppermute | solution.py:592
  327.4 14.4 %collective-permute-start.44 = (bf16[128,512]{1,0:T(8,128)(2,1)S(1)}, bf16[128,512]{1,0:T(8,128)(2,1)S(1)}, u32[]{:S(2)}, u32[]{:S(2)}) collective-permute-start(bf16[128,512]{1,0:T(8,128)(2,1)S(1)} %get-tuple-element.103), channel_id=1, source_target_pairs={{0,1},{1,0},{2,9},{3,8},{4,17},{5,16},{6,25},{7,24},{8,3},{9,2},{1... | collective-permute-start | bytes 393224 | tf_op jit(solution)/shard_map/ppermute | solution.py:592
  331.6 13.1 %collective-permute-start.56 = (bf16[1,2,128,512]{3,2,1,0:T(8,128)(2,1)S(1)}, bf16[1,2,128,512]{3,2,1,0:T(8,128)(2,1)S(1)}, u32[]{:S(2)}, u32[]{:S(2)}) collective-permute-start(bf16[1,2,128,512]{3,2,1,0:T(8,128)(2,1)S(1)} %fusion.11), channel_id=1, source_target_pairs={{0,16},{8,24},{16,0},{24,8},{1,17},{9,25},{17,1},{25,9},{2,18},{10... | collective-permute-start | bytes 786440 | tf_op jit(solution)/shard_map/ppermute | solution.py:518
  344.8 16.7 %collective-permute-start.57 = (bf16[128,512]{1,0:T(8,128)(2,1)S(1)}, bf16[128,512]{1,0:T(8,128)(2,1)S(1)}, u32[]{:S(2)}, u32[]{:S(2)}) collective-permute-start(bf16[128,512]{1,0:T(8,128)(2,1)S(1)} %get-tuple-element.108), channel_id=1, source_target_pairs={{0,0},{1,1},{2,8},{3,9},{4,16},{5,17},{6,24},{7,25},{8,2},{9,3},{1... | collective-permute-start | bytes 393224 | tf_op jit(solution)/shard_map/ppermute | solution.py:592
  346.8 14.7 %collective-permute-start.58 = (bf16[128,512]{1,0:T(8,128)(2,1)S(1)}, bf16[128,512]{1,0:T(8,128)(2,1)S(1)}, u32[]{:S(2)}, u32[]{:S(2)}) collective-permute-start(bf16[128,512]{1,0:T(8,128)(2,1)S(1)} %get-tuple-element.107), channel_id=1, source_target_pairs={{0,1},{1,0},{2,9},{3,8},{4,17},{5,16},{6,25},{7,24},{8,3},{9,2},{1... | collective-permute-start | bytes 393224 | tf_op jit(solution)/shard_map/ppermute | solution.py:592
  (23 other events, 391.4 us)

commit v4 on v3

--- a/solution.py
+++ b/solution.py
@@ -360,100 +360,91 @@
     )(idx, mine, other, weights, weights, from_left, from_right, d_out, *tables)
 
 
-def grads_kernel(count, sets, turned, *refs):
-    pieces, out = refs[:-1], refs[-1]
-    length = turned.shape[1] // count
-    total, start = None, 0
-    for position in range(sets):
-        group = pieces[position * (count + 1) : (position + 1) * (count + 1)]
-        rows = group[0].shape[1]
-        for place in range(count):
-            if place < count - 1:
-                block = group[place][0]
-            else:
-                block = jnp.concatenate([group[place][0], group[place + 1][0]], axis=0)
-            low = place * length + start
-            product = mm(turned[:, low : low + rows], block)
-            total = product if total is None else total + product
-        start += rows
-    out[0] = total
-
-
-def grads_chunk(count, turned, gathered, before, chunk, wide, columns):
+def grads_chunk(count, turned, pieces, start, before, add, chunk, wide, columns):
     depth, span = turned.shape
     in_specs = [pl.BlockSpec((depth, span), lambda m: (0, 0))]
     operands = [turned]
-    for pieces in gathered:
-        for piece in pieces:
-            in_specs.append(pl.BlockSpec((1, *piece.shape[1:]), lambda m: (m, 0, 0)))
-            operands.append(piece)
+    for piece in pieces:
+        in_specs.append(pl.BlockSpec((1, *piece.shape[1:]), lambda m: (m, 0, 0)))
+        operands.append(piece)
+    result = pl.BlockSpec((1, depth, wide), lambda m: (m, 0, chunk))
     aliases = {}
-    kernel = functools.partial(grads_kernel, count, len(gathered))
     if before is not None:
         aliases = {len(operands): 0}
         operands.append(before)
-        in_specs.append(pl.BlockSpec(memory_space=pl.ANY))
-        inner = kernel
-
-        def kernel(*refs):
-            inner(*refs[:-2], refs[-1])
+        in_specs.append(result if add else pl.BlockSpec(memory_space=pl.ANY))
+    length = span // count
+    rows = pieces[0].shape[1]
+
+    def kernel(turned_ref, *refs):
+        blocks = jnp.concatenate([piece[0] for piece in refs[: count + 1]], axis=0)
+        left = [
+            turned_ref[:, place * length + start : place * length + start + rows]
+            for place in range(count)
+        ]
+        total = mm(jnp.concatenate(left, axis=1), blocks)
+        refs[-1][0] = total + refs[-2][0] if add else total
 
     return pl.pallas_call(
         kernel,
         grid=(3,),
         in_specs=in_specs,
-        out_specs=pl.BlockSpec((1, depth, wide), lambda m: (m, 0, chunk)),
+        out_specs=result,
         out_shape=jax.ShapeDtypeStruct((3, depth, columns), jnp.float32),
         input_output_aliases=aliases,
         compiler_params=params(LARGE),
-        cost_estimate=cost(6 * span * depth * wide, 6 * span * wide + 12 * depth * wide),
+        cost_estimate=cost(
+            6 * count * rows * depth * wide, 6 * count * rows * wide + 12 * depth * wide
+        ),
         name="grads",
     )(*operands)
 
 
-def back(pieces, turned, place, count):
-    def one(piece):
-        total = mm(piece[0], turned[0])
-        for m in range(1, 3):
-            total += mm(piece[m], turned[m])
-        return total
-
-    if place < count - 1:
-        return one(pieces[place])
-    return jnp.concatenate([one(pieces[place]), one(pieces[place + 1])], axis=0)
-
-
-def term_first_kernel(count, idx, turned, *refs):
+def back(pieces, turned):
+    wide, depth = turned.shape[1:]
+    rows = [jnp.concatenate([piece[m] for m in range(3)], axis=1) for piece in pieces]
+    return mm(jnp.concatenate(rows, axis=0), turned[...].reshape(3 * wide, depth))
+
+
+def term_step(turned, pieces, befores, part, chunk, wide):
+    depth = turned.shape[2]
+    count = len(pieces)
+    rows = pieces[0].shape[1]
+    results = [pl.BlockSpec((rows, depth), lambda i: (0, 0))] * count
+    takes = [
+        pl.BlockSpec((rows, depth), lambda i, row=(part if before.shape[0] > rows else 0): (row, 0))
+        for before in befores
+    ]
+
+    def kernel(turned_ref, *refs):
+        total = back(refs[:count], turned_ref)
+        for place in range(count):
+            block = total[place * rows : (place + 1) * rows]
+            if befores:
+                block += refs[count + place][...]
+            refs[len(refs) - count + place][...] = block
+
+    return pl.pallas_call(
+        kernel,
+        grid=(1,),
+        in_specs=[
+            pl.BlockSpec((3, wide, depth), lambda i: (0, chunk, 0)),
+            *[pl.BlockSpec(piece.shape, lambda i: (0, 0, 0)) for piece in pieces],
+            *takes,
+        ],
+        out_specs=results,
+        out_shape=[jax.ShapeDtypeStruct((rows, depth), jnp.float32)] * count,
+        compiler_params=params(SMALL),
+        cost_estimate=cost(6 * count * rows * depth * wide, 12 * count * rows * wide),
+        name="term_step",
+    )(turned, *pieces, *befores)
+
+
+def term_last_kernel(count, idx, turned, before, far_r, far_l, *refs):
+    nears, keep, send = refs[:-2], refs[-2], refs[-1]
+    last = back([far_r, far_l], turned) + before[...]
     for place in range(count):
-        refs[-1][idx[count + 1 + place]] = back(refs, turned, place, count)
-
-
-def term_first(idx, turned, pieces, chunk, wide):
-    count = len(pieces) - 1
-    length = pieces[0].shape[1]
-    depth = turned.shape[2]
-    return pl.pallas_call(
-        functools.partial(term_first_kernel, count),
-        grid_spec=pltpu.PrefetchScalarGridSpec(
-            num_scalar_prefetch=1,
-            grid=(1,),
-            in_specs=[
-                pl.BlockSpec((3, wide, depth), lambda i, idx: (0, chunk, 0)),
-                *[pl.BlockSpec(piece.shape, lambda i, idx: (0, 0, 0)) for piece in pieces],
-            ],
-            out_specs=pl.BlockSpec((count, length, depth), lambda i, idx: (0, 0, 0)),
-        ),
-        out_shape=jax.ShapeDtypeStruct((count, length, depth), jnp.float32),
-        compiler_params=params(LARGE),
-        cost_estimate=cost(6 * count * length * depth * wide, 6 * count * length * wide),
-        name="term_first",
-    )(idx, turned, *pieces)
-
-
-def term_last_kernel(count, idx, turned, before, *refs):
-    keep, send = refs[-2], refs[-1]
-    for place in range(count):
-        total = back(refs, turned, place, count) + before[idx[count + 1 + place]]
+        total = nears[place][...] if place < count - 1 else last
 
         @pl.when(idx[2 * count + 1 + place] == 0)
         def _():
@@ -464,10 +455,11 @@
             send[idx[3 * count + 1 + place]] = total.astype(jnp.bfloat16)
 
 
-def term_last(idx, turned, before, pieces, part, chunk, wide):
-    count, _, depth = before.shape
-    rows = pieces[0].shape[1]
+def term_last(idx, turned, before, pieces, nears, chunk, wide):
+    count = len(nears) + 1
+    rows, depth = before.shape
     result = pl.BlockSpec((count // 2, rows, depth), lambda i, idx: (0, 0, 0))
+    block = pl.BlockSpec((rows, depth), lambda i, idx: (0, 0))
     return pl.pallas_call(
         functools.partial(term_last_kernel, count),
         grid_spec=pltpu.PrefetchScalarGridSpec(
@@ -475,8 +467,9 @@
             grid=(1,),
             in_specs=[
                 pl.BlockSpec((3, wide, depth), lambda i, idx: (0, chunk, 0)),
-                pl.BlockSpec((count, rows, depth), lambda i, idx: (0, part, 0)),
+                block,
                 *[pl.BlockSpec(piece.shape, lambda i, idx: (0, 0, 0)) for piece in pieces],
+                *[block] * (count - 1),
             ],
             out_specs=[result, result],
         ),
@@ -484,10 +477,10 @@
             jax.ShapeDtypeStruct((count // 2, rows, depth), jnp.float32),
             jax.ShapeDtypeStruct((count // 2, rows, depth), jnp.bfloat16),
         ],
-        compiler_params=params(LARGE),
-        cost_estimate=cost(6 * count * rows * depth * wide, 6 * count * rows * wide),
+        compiler_params=params(SMALL),
+        cost_estimate=cost(6 * rows * depth * wide, 12 * count * rows * depth),
         name="term_last",
-    )(idx, turned, before, *pieces)
+    )(idx, turned, before, *pieces, *nears)
 
 
 def after(first, *arrays):
@@ -522,7 +515,9 @@
     other_far = swap(mine_far, 1)
     weights, turned = scaled_weights(w_quant, w_scale)
     firsts = sum_first(idx, size, mine_far, other_far, weights)
-    mine = jnp.stack([shift(blocks[-d % size], -d) if d else blocks[0] for d in distances[:-1]])
+    nears = after(mine_far, *blocks[:far], *blocks[far + 1 :])
+    nears = [*nears[:far], None, *nears[far:]]
+    mine = jnp.stack([shift(nears[-d % size], -d) if d else blocks[0] for d in distances[:-1]])
     other = swap(mine, 1)
 
     tables = rope_tables(length, HEAD_DIM)
@@ -557,20 +552,23 @@
     gathered = [[block] for block in sets]
     moving = [(block, block) for block in sets]
     schedule = [(0, 1)]
-    for step in range(2, far + 1):
+    for step in range(2, far):
         schedule += [(0, step), (1, step - 1)]
-    schedule += [(2, 1), (1, far)] + [(2, step) for step in range(2, far + 1)]
+    schedule += [(2, 1), (0, far), (1, far - 1), (1, far)]
+    schedule += [(2, step) for step in range(2, far + 1)]
 
     share = width // nodes
     values_part = lax.dynamic_slice_in_dim(tokens, node * share, share, 1).astype(jnp.float32)
     gains_part = lax.dynamic_slice_in_dim(norm_gain, node * share, share, 0).astype(jnp.float32)
     inverse_rms = inverse_rms[:, :1]
 
-    def start_term(before, part):
-        keep, send = term_last(idx, turned, before, gathered[1 + part], part, 1, wide)
+    def start_term(part):
+        keep, send = term_last(
+            idx, turned, lasts[0][part], gathered[1 + part][-2:], terms[1 + part], 1, wide
+        )
         return keep + swap(send, 1).astype(jnp.float32)
 
-    def end_term(summed, part):
+    def sum_nodes(summed):
         bit = 2
         while bit < nodes:
             pair = summed.reshape(-1, 2, group, *summed.shape[1:])
@@ -580,7 +578,9 @@
             summed = keep + swap(send.astype(jnp.bfloat16), bit).astype(jnp.float32)
             summed = summed.reshape(-1, *pair.shape[3:])
             bit *= 2
-        summed = summed.astype(jnp.bfloat16)
+        return summed.astype(jnp.bfloat16)
+
+    def end_term(summed, part):
         came = []
         for turn in range(group):
             block = lax.dynamic_index_in_dim(summed, (here + turn) % group, 0, keepdims=False)
@@ -605,7 +605,9 @@
         )
         return d_rows.astype(jnp.bfloat16)
 
-    term = early = None
+    terms = [[], [], []]
+    lasts = [None]
+    first_grads = half_grads = early = None
     for ring, step in schedule:
         right, left = moving[ring]
         if step == far:
@@ -615,22 +617,33 @@
             right, left = after(moving[0][0], right, left)
         if (ring, step) == (2, 1):
             right, left = after(moving[0][0], right, left)
-        if (ring, step) == (2, min(2, far)):
-            right, left = after(term, right, left)
+        if (ring, step) == (2, far - 1):
+            right, left = after((first_grads, early), right, left)
         if (ring, step) == (2, far):
-            right, left = after(early, right, left)
+            right, left = after((half_grads, summed), right, left)
         right, left = shift(right, 1), shift(left, -1)
         moving[ring] = right, left
         gathered[ring] += [right, left]
-        if (ring, step) == (0, far):
-            term = term_first(idx, turned, gathered[0], 0, wide)
-        if (ring, step) == (1, far):
-            early = start_term(term, 0)
-    late = start_term(term, 1)
-    d_tokens = jnp.concatenate([end_term(early, 0), end_term(late, 1)], axis=0)
-
-    grads = grads_chunk(size, rows_turned, gathered[:1], None, 0, wide, columns)
-    grads = grads_chunk(size, rows_turned, gathered[1:], grads, 1, wide, columns)
+        chunk, part = min(ring, 1), max(ring - 1, 0)
+        if step < far:
+            pieces = gathered[ring] if step == 1 else [right, left]
+            known = len(terms[ring])
+            befores = terms[0][known : known + len(pieces)] if ring else []
+            terms[ring] += term_step(turned, pieces, befores, part, chunk, wide)
+        elif ring == 0:
+            lasts[0] = term_step(turned, [right, left], [], 0, 0, wide)
+            first_grads = grads_chunk(
+                size, rows_turned, gathered[0], 0, None, False, 0, wide, columns
+            )
+        elif ring == 1:
+            early = start_term(0)
+            half_grads = grads_chunk(
+                size, rows_turned, gathered[1], 0, first_grads, False, 1, wide, columns
+            )
+            summed = sum_nodes(early)
+    late = start_term(1)
+    d_tokens = jnp.concatenate([end_term(summed, 0), end_term(sum_nodes(late), 1)], axis=0)
+    grads = grads_chunk(size, rows_turned, gathered[2], half, half_grads, True, 1, wide, columns)
     return (jnp.concatenate(outputs, axis=-1), d_tokens, grads)
 
 

time: 364 us -> 350 us (0.962)
  waiting for transfers between devices: 199 us -> 180 us
  Pallas kernels: 76.2 us -> 66.8 us
  starting transfers between devices: 67.5 us -> 75.1 us
    ppermute x47, waiting for transfers between devices: 193 us -> 162 us  [shift(): return lax.ppermute(array, 'local', moves)]
    pallas_call x2, Pallas kernels: 16.2 us -> 3.92 us  [term_last(): pl.pallas_call(functools.partial(term_last_kernel, count), grid_spec=pltp...]
    ppermute x4, waiting for transfers between devices: 2.19 us -> 13.1 us  [end_term(): came.append(lax.ppermute(block, ('node', 'local'), moves))]
    ppermute x47, starting transfers between devices: 53.5 us -> 60 us  [shift(): return lax.ppermute(array, 'local', moves)]
    unnamed x62 -> x142, local copies, waits for them, and re-layouts: 5.38 us -> 9.99 us
    pallas_call x3 -> x13, Pallas kernels: 27.6 us -> 30.6 us  [the longest x3 21.7 us: grads_chunk(): pl.pallas_call(kernel, grid=(3,), in_specs=in_specs, out_specs=result, ou...]
  transfers between devices with their start and end apart: 59 -> 59, of which waited for: 29 -> 36; matrix products, arithmetic and copies ran while one was open for 3% -> 4% of each run, Pallas kernels for 19% -> 18%
where the time goes in v4:
time: 350 us; the launch traced here: 349 us
  waiting for transfers between devices  180 us (51%)
  starting transfers between devices  75.1 us (21%)
  Pallas kernels  66.8 us (19%)
  local copies, waits for them, and re-layouts  13.5 us (4%)
  other arithmetic  12.3 us (4%)
    ppermute x47, waiting for transfers between devices, shift(): return lax.ppermute(array, 'local', moves)  162 us
    ppermute x47, starting transfers between devices, shift(): return lax.ppermute(array, 'local', moves)  60 us
    pallas_call x3, Pallas kernels, grads_chunk(): pl.pallas_call(kernel, grid=(3,), in_specs=in_specs, out_specs=result, ou...  21.7 us
    pallas_call x2, Pallas kernels, attention(): pl.pallas_call(attention_kernel, grid_spec=pltpu.PrefetchScalarGridSpec(n...  14.4 us
    ppermute x4, waiting for transfers between devices, end_term(): came.append(lax.ppermute(block, ('node', 'local'), moves))  13.1 us
    pallas_call x6, Pallas kernels, sum_step(): pl.pallas_call(sum_step_kernel, grid_spec=pltpu.PrefetchScalarGridSpec(nu...  12.3 us
    ppermute x4, starting transfers between devices, end_term(): came.append(lax.ppermute(block, ('node', 'local'), moves))  12 us
    unnamed x142, local copies, waits for them, and re-layouts  9.99 us
  transfers between devices with their start and end apart: 59, of which 36 were waited for; matrix products, arithmetic and copies ran while one was open for 4% of the time, Pallas kernels for 18%

profile of v4, /device:TPU:2, one launch (start us, length us, event | category | flops | bytes accessed | tf_op | source)
XLA Modules:
  0.0 349.0 jit_solution(9322054616985136510)
XLA Ops:
  5.1 4.6 %collective-permute-start = (bf16[256,256]{1,0:T(8,128)(2,1)S(1)}, bf16[256,256]{1,0:T(8,128)(2,1)S(1)}, u32[]{:S(2)}, u32[]{:S(2)}) collective-permute-start(bf16[256,256]{1,0:T(8,128)(2,1)S(1)} %get-tuple-element.78), channel_id=1, source_target_pairs={{0,7},{2,5},{4,3},{6,1},{7,0},{5,2},{3,4},{1,6},{8,15},{10,13},{12... | collective-permute-start | bytes 393224 | tf_op jit(solution)/shard_map/ppermute | solution.py:508
  9.7 3.6 %collective-permute-done.mine.mine_far = bf16[256,256]{1,0:T(8,128)(2,1)S(1)} collective-permute-done((bf16[256,256]{1,0:T(8,128)(2,1)S(1)}, bf16[256,256]{1,0:T(8,128)(2,1)S(1)}, u32[]{:S(2)}, u32[]{:S(2)}) %collective-permute-start) | collective-permute-done | bytes 131104 | tf_op jit(solution)/shard_map/ppermute | solution.py:508
  13.3 2.4 collective-permute-start.1
  15.8 3.0 collective-permute-start.3
  18.8 3.0 collective-permute-start.5
  21.8 2.1 collective-permute-start.6
  24.1 9.3 %collective-permute-done.4 = bf16[256,256]{1,0:T(8,128)(2,1)S(1)} collective-permute-done((bf16[256,256]{1,0:T(8,128)(2,1)S(1)}, bf16[256,256]{1,0:T(8,128)(2,1)S(1)}, u32[]{:S(2)}, u32[]{:S(2)}) %collective-permute-start.4) | collective-permute-done | bytes 131104 | tf_op jit(solution)/shard_map/ppermute | solution.py:508
  39.5 2.0 collective-permute-start.10
  41.5 9.1 %collective-permute-done.9.from_left = bf16[3,128,512]{2,1,0:T(8,128)(2,1)S(1)} collective-permute-done((bf16[3,128,512]{2,1,0:T(8,128)(2,1)S(1)}, bf16[3,128,512]{2,1,0:T(8,128)(2,1)S(1)}, u32[]{:S(2)}, u32[]{:S(2)}) %collective-permute-start.9) | collective-permute-done | bytes 393248 | tf_op jit(solution)/shard_map/ppermute | solution.py:508
  50.7 2.1 sum_step.6
  52.8 2.4 collective-permute-start.11
  55.2 2.0 collective-permute-start.17
  57.2 16.1 %collective-permute-done.11.from_left = bf16[3,256,512]{2,1,0:T(8,128)(2,1)S(1)} collective-permute-done((bf16[3,256,512]{2,1,0:T(8,128)(2,1)S(1)}, bf16[3,256,512]{2,1,0:T(8,128)(2,1)S(1)}, u32[]{:S(2)}, u32[]{:S(2)}) %collective-permute-start.11) | collective-permute-done | bytes 786464 | tf_op jit(solution)/shard_map/ppermute | solution.py:508
  73.3 2.4 collective-permute-done.12.from_right
  75.7 2.1 sum_step.7
  79.8 1.9 collective-permute-done.17.from_left
  81.8 2.4 collective-permute-done.18.from_right
  84.1 2.1 sum_step.9
  88.3 10.4 %collective-permute-done.13.from_left = bf16[3,256,512]{2,1,0:T(8,128)(2,1)S(1)} collective-permute-done((bf16[3,256,512]{2,1,0:T(8,128)(2,1)S(1)}, bf16[3,256,512]{2,1,0:T(8,128)(2,1)S(1)}, u32[]{:S(2)}, u32[]{:S(2)}) %collective-permute-start.13) | collective-permute-done | bytes 786464 | tf_op jit(solution)/shard_map/ppermute | solution.py:508
  98.6 2.4 collective-permute-done.14.from_right
  101.0 2.1 sum_step.8
  105.1 10.3 %collective-permute-done.19.from_left = bf16[3,256,512]{2,1,0:T(8,128)(2,1)S(1)} collective-permute-done((bf16[3,256,512]{2,1,0:T(8,128)(2,1)S(1)}, bf16[3,256,512]{2,1,0:T(8,128)(2,1)S(1)}, u32[]{:S(2)}, u32[]{:S(2)}) %collective-permute-start.19) | collective-permute-done | bytes 786464 | tf_op jit(solution)/shard_map/ppermute | solution.py:508
  115.5 2.4 collective-permute-done.20.from_right
  117.8 2.1 sum_step.10
  122.6 9.7 %collective-permute-done.15.from_left = bf16[3,256,512]{2,1,0:T(8,128)(2,1)S(1)} collective-permute-done((bf16[3,256,512]{2,1,0:T(8,128)(2,1)S(1)}, bf16[3,256,512]{2,1,0:T(8,128)(2,1)S(1)}, u32[]{:S(2)}, u32[]{:S(2)}) %collective-permute-start.15) | collective-permute-done | bytes 786464 | tf_op jit(solution)/shard_map/ppermute | solution.py:508
  132.3 2.4 collective-permute-done.16.from_right
  134.7 7.2 %attention.2 = (bf16[256,512]{1,0:T(8,128)(2,1)S(1)}, bf16[3,256,512]{2,1,0:T(8,128)(2,1)S(1)}, f32[256,128]{1,0:T(8,128)S(1)}) custom-call(s32[33]{0:T(128)S(1)} %fusion.21.idx, bf16[7,256,256]{2,1,0:T(8,128)(2,1)S(1)} %bitcast_dynamic-update-slice_fusion.mine_r.mine_l.mine, bf16[7,256,256]{2,1,0:T(8,128)(2,1)S(1)} %collective-permute-done.7.other_r.other_l.other, ...), custom_call_target="tpu_custom_call" | custom-call | flops 402653184 | bytes 3145728 | tf_op jit(solution)/shard_map/attention/pallas_call | solution.py:330
  144.5 4.6 %collective-permute-done.21.from_left = bf16[3,256,512]{2,1,0:T(8,128)(2,1)S(1)} collective-permute-done((bf16[3,256,512]{2,1,0:T(8,128)(2,1)S(1)}, bf16[3,256,512]{2,1,0:T(8,128)(2,1)S(1)}, u32[]{:S(2)}, u32[]{:S(2)}) %collective-permute-start.21) | collective-permute-done | bytes 786464 | tf_op jit(solution)/shard_map/ppermute | solution.py:508
  149.2 2.4 collective-permute-done.22.from_right
  151.5 2.1 sum_step.11
  155.7 10.3 %collective-permute-done.25.refs_1_ = bf16[3,256,512]{2,1,0:T(8,128)(2,1)S(1)} collective-permute-done((bf16[3,256,512]{2,1,0:T(8,128)(2,1)S(1)}, bf16[3,256,512]{2,1,0:T(8,128)(2,1)S(1)}, u32[]{:S(2)}, u32[]{:S(2)}) %collective-permute-start.25) | collective-permute-done | bytes 786464 | tf_op jit(solution)/shard_map/ppermute | solution.py:508
  166.0 2.4 collective-permute-start.26
  168.4 14.5 %collective-permute-done.23.from_left = bf16[3,256,512]{2,1,0:T(8,128)(2,1)S(1)} collective-permute-done((bf16[3,256,512]{2,1,0:T(8,128)(2,1)S(1)}, bf16[3,256,512]{2,1,0:T(8,128)(2,1)S(1)}, u32[]{:S(2)}, u32[]{:S(2)}) %collective-permute-start.23) | collective-permute-done | bytes 786464 | tf_op jit(solution)/shard_map/ppermute | solution.py:508
  182.9 2.4 collective-permute-done.24.from_right
  185.2 7.2 %attention.3 = (bf16[256,512]{1,0:T(8,128)(2,1)S(1)}, bf16[3,256,512]{2,1,0:T(8,128)(2,1)S(1)}, f32[256,128]{1,0:T(8,128)S(1)}) custom-call(s32[33]{0:T(128)S(1)} %fusion.21.idx, bf16[7,256,256]{2,1,0:T(8,128)(2,1)S(1)} %bitcast_dynamic-update-slice_fusion.mine_r.mine_l.mine, bf16[7,256,256]{2,1,0:T(8,128)(2,1)S(1)} %collective-permute-done.7.other_r.other_l.other, ...), custom_call_target="tpu_custom_call" | custom-call | flops 402653184 | bytes 3145728 | tf_op jit(solution)/shard_map/attention/pallas_call | solution.py:330
  192.6 5.4 %collective-permute-done.26.refs_0_.refs_3_ = bf16[3,256,512]{2,1,0:T(8,128)(2,1)S(1)} collective-permute-done((bf16[3,256,512]{2,1,0:T(8,128)(2,1)S(1)}, bf16[3,256,512]{2,1,0:T(8,128)(2,1)S(1)}, u32[]{:S(2)}, u32[]{:S(2)}) %collective-permute-start.26) | collective-permute-done | bytes 786464 | tf_op jit(solution)/shard_map/ppermute | solution.py:508
  198.0 2.4 collective-permute-start.33
  200.4 2.0 collective-permute-start.27
  202.4 7.7 %collective-permute-done.33.refs_1_ = bf16[3,128,512]{2,1,0:T(8,128)(2,1)S(1)} collective-permute-done((bf16[3,128,512]{2,1,0:T(8,128)(2,1)S(1)}, bf16[3,128,512]{2,1,0:T(8,128)(2,1)S(1)}, u32[]{:S(2)}, u32[]{:S(2)}) %collective-permute-start.33) | collective-permute-done | bytes 393248 | tf_op jit(solution)/shard_map/ppermute | solution.py:508
  210.1 2.4 collective-permute-start.34
  212.4 20.3 %collective-permute-done.34.refs_0_.refs_3_ = bf16[3,128,512]{2,1,0:T(8,128)(2,1)S(1)} collective-permute-done((bf16[3,128,512]{2,1,0:T(8,128)(2,1)S(1)}, bf16[3,128,512]{2,1,0:T(8,128)(2,1)S(1)}, u32[]{:S(2)}, u32[]{:S(2)}) %collective-permute-start.34) | collective-permute-done | bytes 393248 | tf_op jit(solution)/shard_map/ppermute | solution.py:508
  232.7 2.4 collective-permute-start.35
  235.1 2.0 collective-permute-start.28
  239.7 5.0 %collective-permute-done.35.refs_0_.refs_5_ = bf16[3,128,512]{2,1,0:T(8,128)(2,1)S(1)} collective-permute-done((bf16[3,128,512]{2,1,0:T(8,128)(2,1)S(1)}, bf16[3,128,512]{2,1,0:T(8,128)(2,1)S(1)}, u32[]{:S(2)}, u32[]{:S(2)}) %collective-permute-start.35) | collective-permute-done | bytes 393248 | tf_op jit(solution)/shard_map/ppermute | solution.py:508
  244.8 2.4 collective-permute-start.36
  248.3 2.0 collective-permute-start.47
  250.3 2.8 collective-permute-done.28.refs_0_.refs_7_
  257.4 2.3 collective-permute-done.40.far_l.refs_8_
  259.8 2.0 term_last.2
  271.4 7.9 %grads.3.refs_9_ = f32[3,512,1024]{2,1,0:T(8,128)} custom-call(bf16[512,2048]{1,0:T(8,128)(2,1)} %copy-done.4, bf16[3,256,512]{2,1,0:T(8,128)(2,1)} %copy-done.12, bf16[3,256,512]{2,1,0:T(8,128)(2,1)} %copy-done.13, bf16[3,256,512]{2,1,0:T(8,128)(2,1)} %copy-done.14, bf16[3,256,512]{2,1,0:T(8,128)(2,1)} %copy-done.10, bf16[3,256,512]{2,1,0:T(8,128)(2,1)} %copy-done.11, ...), custom_call_target="tpu_custom_call" | custom-call | flops 3221225472 | bytes 9437184 | tf_op jit(solution)/shard_map/grads/pallas_call | solution.py:388
  279.3 2.2 convert_add_fusion.1
  284.9 2.1 dynamic-slice_convert_fusion.1
  287.0 6.4 %grads.4.refs_9_ = f32[3,512,1024]{2,1,0:T(8,128)} custom-call(bf16[512,2048]{1,0:T(8,128)(2,1)} %copy-done.4, bf16[3,128,512]{2,1,0:T(8,128)(2,1)} %copy-done.8, bf16[3,128,512]{2,1,0:T(8,128)(2,1)} %copy-done.37, bf16[3,128,512]{2,1,0:T(8,128)(2,1)} %copy-done.38, bf16[3,128,512]{2,1,0:T(8,128)(2,1)} %copy-done.39, ...), custom_call_target="tpu_custom_call", output_to_operand_aliasing={{}: (10, {})} | custom-call | flops 1610612736 | bytes 6291456 | tf_op jit(solution)/shard_map/grads/pallas_call | solution.py:388
  295.7 2.0 term_step.17
  301.4 2.0 term_last.3
  312.4 3.9 %collective-permute-start.43 = (bf16[128,512]{1,0:T(8,128)(2,1)S(1)}, bf16[128,512]{1,0:T(8,128)(2,1)S(1)}, u32[]{:S(2)}, u32[]{:S(2)}) collective-permute-start(bf16[128,512]{1,0:T(8,128)(2,1)S(1)} %get-tuple-element.162), channel_id=1, source_target_pairs={{0,0},{1,1},{2,8},{3,9},{4,16},{5,17},{6,24},{7,25},{8,2},{9,3},{1... | collective-permute-start | bytes 393224 | tf_op jit(solution)/shard_map/ppermute | solution.py:592
  316.3 2.0 collective-permute-start.44
  318.6 8.6 %collective-permute-done.43 = bf16[128,512]{1,0:T(8,128)(2,1)S(1)} collective-permute-done((bf16[128,512]{1,0:T(8,128)(2,1)S(1)}, bf16[128,512]{1,0:T(8,128)(2,1)S(1)}, u32[]{:S(2)}, u32[]{:S(2)}) %collective-permute-start.43) | collective-permute-done | bytes 131104 | tf_op jit(solution)/shard_map/ppermute | solution.py:592
  327.2 2.5 collective-permute-done.44
  329.8 2.2 collective-permute-done.56
  332.2 1.9 collective-permute-start.57
  334.1 4.1 %collective-permute-start.58 = (bf16[128,512]{1,0:T(8,128)(2,1)S(1)}, bf16[128,512]{1,0:T(8,128)(2,1)S(1)}, u32[]{:S(2)}, u32[]{:S(2)}) collective-permute-start(bf16[128,512]{1,0:T(8,128)(2,1)S(1)} %get-tuple-element.165), channel_id=1, source_target_pairs={{0,1},{1,0},{2,9},{3,8},{4,17},{5,16},{6,25},{7,24},{8,3},{9,2},{1... | collective-permute-start | bytes 393224 | tf_op jit(solution)/shard_map/ppermute | solution.py:592
  338.2 7.4 %grads.5 = f32[3,512,1024]{2,1,0:T(8,128)} custom-call(bf16[512,2048]{1,0:T(8,128)(2,1)} %copy-done.4, bf16[3,128,512]{2,1,0:T(8,128)(2,1)} %copy-done.7, bf16[3,128,512]{2,1,0:T(8,128)(2,1)} %collective-permute-done.47.refs_1_, bf16[3,128,512]{2,1,0:T(8,128)(2,1)} %collective-permute-done.49.refs_2_, ...), custom_call_target="tpu_custom_call", output_to_operand_aliasing={{}: (10, {})} | custom-call | flops 1610612736 | bytes 6291456 | tf_op jit(solution)/shard_map/grads/pallas_call | solution.py:388
  345.6 2.0 collective-permute-done.58
  (259 shorter events, 61.9 us)
Async XLA Ops:
  5.1 8.2 %collective-permute-start = (bf16[256,256]{1,0:T(8,128)(2,1)S(1)}, bf16[256,256]{1,0:T(8,128)(2,1)S(1)}, u32[]{:S(2)}, u32[]{:S(2)}) collective-permute-start(bf16[256,256]{1,0:T(8,128)(2,1)S(1)} %get-tuple-element.78), channel_id=1, source_target_pairs={{0,7},{2,5},{4,3},{6,1},{7,0},{5,2},{3,4},{1,6},{8,15},{10,13},{12... | collective-permute-start | bytes 393224 | tf_op jit(solution)/shard_map/ppermute | solution.py:508
  13.3 8.5 %collective-permute-start.1 = (bf16[256,256]{1,0:T(8,128)(2,1)S(1)}, bf16[256,256]{1,0:T(8,128)(2,1)S(1)}, u32[]{:S(2)}, u32[]{:S(2)}) collective-permute-start(bf16[256,256]{1,0:T(8,128)(2,1)S(1)} %get-tuple-element.85), channel_id=1, source_target_pairs={{0,2},{2,4},{4,6},{6,7},{7,5},{5,3},{3,1},{1,0},{8,10},{10,12},{12... | collective-permute-start | bytes 393224 | tf_op jit(solution)/shard_map/ppermute | solution.py:508
  15.7 8.3 %collective-permute-start.2 = (bf16[256,256]{1,0:T(8,128)(2,1)S(1)}, bf16[256,256]{1,0:T(8,128)(2,1)S(1)}, u32[]{:S(2)}, u32[]{:S(2)}) collective-permute-start(bf16[256,256]{1,0:T(8,128)(2,1)S(1)} %get-tuple-element.86), channel_id=1, source_target_pairs={{0,1},{2,0},{4,2},{6,4},{7,6},{5,7},{3,5},{1,3},{8,9},{10,8},{12,1... | collective-permute-start | bytes 393224 | tf_op jit(solution)/shard_map/ppermute | solution.py:508
  15.8 8.4 %collective-permute-start.3 = (bf16[256,256]{1,0:T(8,128)(2,1)S(1)}, bf16[256,256]{1,0:T(8,128)(2,1)S(1)}, u32[]{:S(2)}, u32[]{:S(2)}) collective-permute-start(bf16[256,256]{1,0:T(8,128)(2,1)S(1)} %get-tuple-element.87), channel_id=1, source_target_pairs={{0,4},{2,6},{4,7},{6,5},{7,3},{5,1},{3,0},{1,2},{8,12},{10,14},{12... | collective-permute-start | bytes 393224 | tf_op jit(solution)/shard_map/ppermute | solution.py:508
  18.8 14.7 %collective-permute-start.4 = (bf16[256,256]{1,0:T(8,128)(2,1)S(1)}, bf16[256,256]{1,0:T(8,128)(2,1)S(1)}, u32[]{:S(2)}, u32[]{:S(2)}) collective-permute-start(bf16[256,256]{1,0:T(8,128)(2,1)S(1)} %get-tuple-element.88), channel_id=1, source_target_pairs={{0,3},{2,1},{4,0},{6,2},{7,4},{5,6},{3,7},{1,5},{8,11},{10,9},{12,... | collective-permute-start | bytes 393224 | tf_op jit(solution)/shard_map/ppermute | solution.py:508
  18.8 15.9 %collective-permute-start.5 = (bf16[256,256]{1,0:T(8,128)(2,1)S(1)}, bf16[256,256]{1,0:T(8,128)(2,1)S(1)}, u32[]{:S(2)}, u32[]{:S(2)}) collective-permute-start(bf16[256,256]{1,0:T(8,128)(2,1)S(1)} %get-tuple-element.89), channel_id=1, source_target_pairs={{0,6},{2,7},{4,5},{6,3},{7,1},{5,0},{3,2},{1,4},{8,14},{10,15},{12... | collective-permute-start | bytes 393224 | tf_op jit(solution)/shard_map/ppermute | solution.py:508
  21.8 12.9 %collective-permute-start.6 = (bf16[256,256]{1,0:T(8,128)(2,1)S(1)}, bf16[256,256]{1,0:T(8,128)(2,1)S(1)}, u32[]{:S(2)}, u32[]{:S(2)}) collective-permute-start(bf16[256,256]{1,0:T(8,128)(2,1)S(1)} %get-tuple-element.90), channel_id=1, source_target_pairs={{0,5},{2,3},{4,1},{6,0},{7,2},{5,4},{3,6},{1,7},{8,13},{10,11},{12... | collective-permute-start | bytes 393224 | tf_op jit(solution)/shard_map/ppermute | solution.py:508
  34.8 150.5 %copy-start = (bf16[7,256,256]{2,1,0:T(8,128)(2,1)}, bf16[7,256,256]{2,1,0:T(8,128)(2,1)S(1)}, u32[]{:S(2)}) copy-start(bf16[7,256,256]{2,1,0:T(8,128)(2,1)S(1)} %bitcast_dynamic-update-slice_fusion.mine_r.mine_l.mine) | copy-start | bytes 2752516
  34.8 15.9 %collective-permute-start.7 = (bf16[7,256,256]{2,1,0:T(8,128)(2,1)S(1)}, bf16[7,256,256]{2,1,0:T(8,128)(2,1)S(1)}, u32[]{:S(2)}, u32[]{:S(2)}) collective-permute-start(bf16[7,256,256]{2,1,0:T(8,128)(2,1)S(1)} %bitcast_dynamic-update-slice_fusion.mine_r.mine_l.mine), channel_id=1, source_target_pairs={{0,8},{8,0},{16,24},{24,16},{1,9},{9,1},{17,25},{25,17},{2,10},{10... | collective-permute-start | bytes 2752520 | tf_op jit(solution)/shard_map/ppermute | solution.py:511
  34.9 2.6 collective-permute-start.8
  39.5 11.2 %collective-permute-start.9 = (bf16[3,128,512]{2,1,0:T(8,128)(2,1)S(1)}, bf16[3,128,512]{2,1,0:T(8,128)(2,1)S(1)}, u32[]{:S(2)}, u32[]{:S(2)}) collective-permute-start(bf16[3,128,512]{2,1,0:T(8,128)(2,1)S(1)} %get-tuple-element.92), channel_id=1, source_target_pairs={{0,2},{2,4},{4,6},{6,7},{7,5},{5,3},{3,1},{1,0},{8,10},{10,12},{12... | collective-permute-start | bytes 1179656 | tf_op jit(solution)/shard_map/ppermute | solution.py:508
  39.5 11.2 %collective-permute-start.10 = (bf16[3,128,512]{2,1,0:T(8,128)(2,1)S(1)}, bf16[3,128,512]{2,1,0:T(8,128)(2,1)S(1)}, u32[]{:S(2)}, u32[]{:S(2)}) collective-permute-start(bf16[3,128,512]{2,1,0:T(8,128)(2,1)S(1)} %get-tuple-element.93), channel_id=1, source_target_pairs={{0,1},{2,0},{4,2},{6,4},{7,6},{5,7},{3,5},{1,3},{8,9},{10,8},{12,1... | collective-permute-start | bytes 1179656 | tf_op jit(solution)/shard_map/ppermute | solution.py:508
  50.7 134.5 %copy-start.2 = (bf16[7,256,256]{2,1,0:T(8,128)(2,1)}, bf16[7,256,256]{2,1,0:T(8,128)(2,1)S(1)}, u32[]{:S(2)}) copy-start(bf16[7,256,256]{2,1,0:T(8,128)(2,1)S(1)} %collective-permute-done.7.other_r.other_l.other) | copy-start | bytes 2752516
  52.8 20.5 %collective-permute-start.11 = (bf16[3,256,512]{2,1,0:T(8,128)(2,1)S(1)}, bf16[3,256,512]{2,1,0:T(8,128)(2,1)S(1)}, u32[]{:S(2)}, u32[]{:S(2)}) collective-permute-start(bf16[3,256,512]{2,1,0:T(8,128)(2,1)S(1)} %get-tuple-element.94), channel_id=1, source_target_pairs={{0,2},{2,4},{4,6},{6,7},{7,5},{5,3},{3,1},{1,0},{8,10},{10,12},{12... | collective-permute-start | bytes 2359304 | tf_op jit(solution)/shard_map/ppermute | solution.py:508
  55.2 20.5 %collective-permute-start.12 = (bf16[3,256,512]{2,1,0:T(8,128)(2,1)S(1)}, bf16[3,256,512]{2,1,0:T(8,128)(2,1)S(1)}, u32[]{:S(2)}, u32[]{:S(2)}) collective-permute-start(bf16[3,256,512]{2,1,0:T(8,128)(2,1)S(1)} %get-tuple-element.95), channel_id=1, source_target_pairs={{0,1},{2,0},{4,2},{6,4},{7,6},{5,7},{3,5},{1,3},{8,9},{10,8},{12,1... | collective-permute-start | bytes 2359304 | tf_op jit(solution)/shard_map/ppermute | solution.py:508
  55.2 26.5 %collective-permute-start.17 = (bf16[3,128,512]{2,1,0:T(8,128)(2,1)S(1)}, bf16[3,128,512]{2,1,0:T(8,128)(2,1)S(1)}, u32[]{:S(2)}, u32[]{:S(2)}) collective-permute-start(bf16[3,128,512]{2,1,0:T(8,128)(2,1)S(1)} %get-tuple-element.101), channel_id=1, source_target_pairs={{0,2},{2,4},{4,6},{6,7},{7,5},{5,3},{3,1},{1,0},{8,10},{10,12},{12... | collective-permute-start | bytes 1179656 | tf_op jit(solution)/shard_map/ppermute | solution.py:508
  57.2 26.9 %collective-permute-start.18 = (bf16[3,128,512]{2,1,0:T(8,128)(2,1)S(1)}, bf16[3,128,512]{2,1,0:T(8,128)(2,1)S(1)}, u32[]{:S(2)}, u32[]{:S(2)}) collective-permute-start(bf16[3,128,512]{2,1,0:T(8,128)(2,1)S(1)} %get-tuple-element.102), channel_id=1, source_target_pairs={{0,1},{2,0},{4,2},{6,4},{7,6},{5,7},{3,5},{1,3},{8,9},{10,8},{12,1... | collective-permute-start | bytes 1179656 | tf_op jit(solution)/shard_map/ppermute | solution.py:508
  77.7 20.9 %collective-permute-start.13 = (bf16[3,256,512]{2,1,0:T(8,128)(2,1)S(1)}, bf16[3,256,512]{2,1,0:T(8,128)(2,1)S(1)}, u32[]{:S(2)}, u32[]{:S(2)}) collective-permute-start(bf16[3,256,512]{2,1,0:T(8,128)(2,1)S(1)} %get-tuple-element.96), channel_id=1, source_target_pairs={{0,2},{2,4},{4,6},{6,7},{7,5},{5,3},{3,1},{1,0},{8,10},{10,12},{12... | collective-permute-start | bytes 2359304 | tf_op jit(solution)/shard_map/ppermute | solution.py:508
  79.5 21.4 %collective-permute-start.14 = (bf16[3,256,512]{2,1,0:T(8,128)(2,1)S(1)}, bf16[3,256,512]{2,1,0:T(8,128)(2,1)S(1)}, u32[]{:S(2)}, u32[]{:S(2)}) collective-permute-start(bf16[3,256,512]{2,1,0:T(8,128)(2,1)S(1)} %get-tuple-element.97), channel_id=1, source_target_pairs={{0,1},{2,0},{4,2},{6,4},{7,6},{5,7},{3,5},{1,3},{8,9},{10,8},{12,1... | collective-permute-start | bytes 2359304 | tf_op jit(solution)/shard_map/ppermute | solution.py:508
  86.2 29.3 %collective-permute-start.19 = (bf16[3,256,512]{2,1,0:T(8,128)(2,1)S(1)}, bf16[3,256,512]{2,1,0:T(8,128)(2,1)S(1)}, u32[]{:S(2)}, u32[]{:S(2)}) collective-permute-start(bf16[3,256,512]{2,1,0:T(8,128)(2,1)S(1)} %get-tuple-element.103), channel_id=1, source_target_pairs={{0,2},{2,4},{4,6},{6,7},{7,5},{5,3},{3,1},{1,0},{8,10},{10,12},{12... | collective-permute-start | bytes 2359304 | tf_op jit(solution)/shard_map/ppermute | solution.py:508
  88.0 29.8 %collective-permute-start.20 = (bf16[3,256,512]{2,1,0:T(8,128)(2,1)S(1)}, bf16[3,256,512]{2,1,0:T(8,128)(2,1)S(1)}, u32[]{:S(2)}, u32[]{:S(2)}) collective-permute-start(bf16[3,256,512]{2,1,0:T(8,128)(2,1)S(1)} %get-tuple-element.104), channel_id=1, source_target_pairs={{0,1},{2,0},{4,2},{6,4},{7,6},{5,7},{3,5},{1,3},{8,9},{10,8},{12,1... | collective-permute-start | bytes 2359304 | tf_op jit(solution)/shard_map/ppermute | solution.py:508
  103.0 29.3 %collective-permute-start.15 = (bf16[3,256,512]{2,1,0:T(8,128)(2,1)S(1)}, bf16[3,256,512]{2,1,0:T(8,128)(2,1)S(1)}, u32[]{:S(2)}, u32[]{:S(2)}) collective-permute-start(bf16[3,256,512]{2,1,0:T(8,128)(2,1)S(1)} %get-tuple-element.98), channel_id=1, source_target_pairs={{0,2},{2,4},{4,6},{6,7},{7,5},{5,3},{3,1},{1,0},{8,10},{10,12},{12... | collective-permute-start | bytes 2359304 | tf_op jit(solution)/shard_map/ppermute | solution.py:508
  104.8 29.8 %collective-permute-start.16 = (bf16[3,256,512]{2,1,0:T(8,128)(2,1)S(1)}, bf16[3,256,512]{2,1,0:T(8,128)(2,1)S(1)}, u32[]{:S(2)}, u32[]{:S(2)}) collective-permute-start(bf16[3,256,512]{2,1,0:T(8,128)(2,1)S(1)} %get-tuple-element.99), channel_id=1, source_target_pairs={{0,1},{2,0},{4,2},{6,4},{7,6},{5,7},{3,5},{1,3},{8,9},{10,8},{12,1... | collective-permute-start | bytes 2359304 | tf_op jit(solution)/shard_map/ppermute | solution.py:508
  119.9 29.3 %collective-permute-start.21 = (bf16[3,256,512]{2,1,0:T(8,128)(2,1)S(1)}, bf16[3,256,512]{2,1,0:T(8,128)(2,1)S(1)}, u32[]{:S(2)}, u32[]{:S(2)}) collective-permute-start(bf16[3,256,512]{2,1,0:T(8,128)(2,1)S(1)} %get-tuple-element.105), channel_id=1, source_target_pairs={{0,2},{2,4},{4,6},{6,7},{7,5},{5,3},{3,1},{1,0},{8,10},{10,12},{12... | collective-permute-start | bytes 2359304 | tf_op jit(solution)/shard_map/ppermute | solution.py:508
  121.7 29.8 %collective-permute-start.22 = (bf16[3,256,512]{2,1,0:T(8,128)(2,1)S(1)}, bf16[3,256,512]{2,1,0:T(8,128)(2,1)S(1)}, u32[]{:S(2)}, u32[]{:S(2)}) collective-permute-start(bf16[3,256,512]{2,1,0:T(8,128)(2,1)S(1)} %get-tuple-element.106), channel_id=1, source_target_pairs={{0,1},{2,0},{4,2},{6,4},{7,6},{5,7},{3,5},{1,3},{8,9},{10,8},{12,1... | collective-permute-start | bytes 2359304 | tf_op jit(solution)/shard_map/ppermute | solution.py:508
  142.5 94.8 %copy-start.12 = (bf16[3,256,512]{2,1,0:T(8,128)(2,1)}, bf16[3,256,512]{2,1,0:T(8,128)(2,1)S(1)}, u32[]{:S(2)}) copy-start(bf16[3,256,512]{2,1,0:T(8,128)(2,1)S(1)} %get-tuple-element.112.refs_0_) | copy-start | bytes 2359300
  142.5 23.5 %collective-permute-start.25 = (bf16[3,256,512]{2,1,0:T(8,128)(2,1)S(1)}, bf16[3,256,512]{2,1,0:T(8,128)(2,1)S(1)}, u32[]{:S(2)}, u32[]{:S(2)}) collective-permute-start(bf16[3,256,512]{2,1,0:T(8,128)(2,1)S(1)} %get-tuple-element.112.refs_0_), channel_id=1, source_target_pairs={{0,2},{2,4},{4,6},{6,7},{7,5},{5,3},{3,1},{1,0},{8,10},{10,12},{12... | collective-permute-start | bytes 2359304 | tf_op jit(solution)/shard_map/ppermute | solution.py:508
  144.2 24.1 %collective-permute-start.29 = (bf16[3,256,512]{2,1,0:T(8,128)(2,1)S(1)}, bf16[3,256,512]{2,1,0:T(8,128)(2,1)S(1)}, u32[]{:S(2)}, u32[]{:S(2)}) collective-permute-start(bf16[3,256,512]{2,1,0:T(8,128)(2,1)S(1)} %get-tuple-element.112.refs_0_), channel_id=1, source_target_pairs={{0,1},{2,0},{4,2},{6,4},{7,6},{5,7},{3,5},{1,3},{8,9},{10,8},{12,1... | collective-permute-start | bytes 2359304 | tf_op jit(solution)/shard_map/ppermute | solution.py:508
  153.6 29.3 %collective-permute-start.23 = (bf16[3,256,512]{2,1,0:T(8,128)(2,1)S(1)}, bf16[3,256,512]{2,1,0:T(8,128)(2,1)S(1)}, u32[]{:S(2)}, u32[]{:S(2)}) collective-permute-start(bf16[3,256,512]{2,1,0:T(8,128)(2,1)S(1)} %get-tuple-element.107), channel_id=1, source_target_pairs={{0,2},{2,4},{4,6},{6,7},{7,5},{5,3},{3,1},{1,0},{8,10},{10,12},{12... | collective-permute-start | bytes 2359304 | tf_op jit(solution)/shard_map/ppermute | solution.py:508
  155.4 29.8 %collective-permute-start.24 = (bf16[3,256,512]{2,1,0:T(8,128)(2,1)S(1)}, bf16[3,256,512]{2,1,0:T(8,128)(2,1)S(1)}, u32[]{:S(2)}, u32[]{:S(2)}) collective-permute-start(bf16[3,256,512]{2,1,0:T(8,128)(2,1)S(1)} %get-tuple-element.108), channel_id=1, source_target_pairs={{0,1},{2,0},{4,2},{6,4},{7,6},{5,7},{3,5},{1,3},{8,9},{10,8},{12,1... | collective-permute-start | bytes 2359304 | tf_op jit(solution)/shard_map/ppermute | solution.py:508
  166.0 71.3 %copy-start.13 = (bf16[3,256,512]{2,1,0:T(8,128)(2,1)}, bf16[3,256,512]{2,1,0:T(8,128)(2,1)S(1)}, u32[]{:S(2)}) copy-start(bf16[3,256,512]{2,1,0:T(8,128)(2,1)S(1)} %collective-permute-done.25.refs_1_) | copy-start | bytes 2359300
  166.0 32.0 %collective-permute-start.26 = (bf16[3,256,512]{2,1,0:T(8,128)(2,1)S(1)}, bf16[3,256,512]{2,1,0:T(8,128)(2,1)S(1)}, u32[]{:S(2)}, u32[]{:S(2)}) collective-permute-start(bf16[3,256,512]{2,1,0:T(8,128)(2,1)S(1)} %collective-permute-done.25.refs_1_), channel_id=1, source_target_pairs={{0,2},{2,4},{4,6},{6,7},{7,5},{5,3},{3,1},{1,0},{8,10},{10,12},{12... | collective-permute-start | bytes 2359304 | tf_op jit(solution)/shard_map/ppermute | solution.py:508
  168.4 34.0 %collective-permute-start.30 = (bf16[3,256,512]{2,1,0:T(8,128)(2,1)S(1)}, bf16[3,256,512]{2,1,0:T(8,128)(2,1)S(1)}, u32[]{:S(2)}, u32[]{:S(2)}) collective-permute-start(bf16[3,256,512]{2,1,0:T(8,128)(2,1)S(1)} %collective-permute-done.29.refs_2_), channel_id=1, source_target_pairs={{0,1},{2,0},{4,2},{6,4},{7,6},{5,7},{3,5},{1,3},{8,9},{10,8},{12,1... | collective-permute-start | bytes 2359304 | tf_op jit(solution)/shard_map/ppermute | solution.py:508
  192.6 103.1 %copy-start.7 = (bf16[3,128,512]{2,1,0:T(8,128)(2,1)}, bf16[3,128,512]{2,1,0:T(8,128)(2,1)S(1)}, u32[]{:S(2)}) copy-start(bf16[3,128,512]{2,1,0:T(8,128)(2,1)S(1)} %get-tuple-element.137.refs_0_) | copy-start | bytes 1179652
  198.0 12.1 %collective-permute-start.33 = (bf16[3,128,512]{2,1,0:T(8,128)(2,1)S(1)}, bf16[3,128,512]{2,1,0:T(8,128)(2,1)S(1)}, u32[]{:S(2)}, u32[]{:S(2)}) collective-permute-start(bf16[3,128,512]{2,1,0:T(8,128)(2,1)S(1)} %get-tuple-element.116.refs_0_), channel_id=1, source_target_pairs={{0,2},{2,4},{4,6},{6,7},{7,5},{5,3},{3,1},{1,0},{8,10},{10,12},{12... | collective-permute-start | bytes 1179656 | tf_op jit(solution)/shard_map/ppermute | solution.py:508
  200.4 12.1 %collective-permute-start.37 = (bf16[3,128,512]{2,1,0:T(8,128)(2,1)S(1)}, bf16[3,128,512]{2,1,0:T(8,128)(2,1)S(1)}, u32[]{:S(2)}, u32[]{:S(2)}) collective-permute-start(bf16[3,128,512]{2,1,0:T(8,128)(2,1)S(1)} %get-tuple-element.116.refs_0_), channel_id=1, source_target_pairs={{0,1},{2,0},{4,2},{6,4},{7,6},{5,7},{3,5},{1,3},{8,9},{10,8},{12,1... | collective-permute-start | bytes 1179656 | tf_op jit(solution)/shard_map/ppermute | solution.py:508
  200.4 34.7 %collective-permute-start.27 = (bf16[3,256,512]{2,1,0:T(8,128)(2,1)S(1)}, bf16[3,256,512]{2,1,0:T(8,128)(2,1)S(1)}, u32[]{:S(2)}, u32[]{:S(2)}) collective-permute-start(bf16[3,256,512]{2,1,0:T(8,128)(2,1)S(1)} %collective-permute-done.26.refs_0_.refs_3_), channel_id=1, source_target_pairs={{0,2},{2,4},{4,6},{6,7},{7,5},{5,3},{3,1},{1,0},{8,10},{10,12},{12... | collective-permute-start | bytes 2359304 | tf_op jit(solution)/shard_map/ppermute | solution.py:508
  202.4 34.8 %collective-permute-start.31 = (bf16[3,256,512]{2,1,0:T(8,128)(2,1)S(1)}, bf16[3,256,512]{2,1,0:T(8,128)(2,1)S(1)}, u32[]{:S(2)}, u32[]{:S(2)}) collective-permute-start(bf16[3,256,512]{2,1,0:T(8,128)(2,1)S(1)} %collective-permute-done.30.refs_1_.refs_4_), channel_id=1, source_target_pairs={{0,1},{2,0},{4,2},{6,4},{7,6},{5,7},{3,5},{1,3},{8,9},{10,8},{12,1... | collective-permute-start | bytes 2359304 | tf_op jit(solution)/shard_map/ppermute | solution.py:508
  210.1 22.6 %collective-permute-start.34 = (bf16[3,128,512]{2,1,0:T(8,128)(2,1)S(1)}, bf16[3,128,512]{2,1,0:T(8,128)(2,1)S(1)}, u32[]{:S(2)}, u32[]{:S(2)}) collective-permute-start(bf16[3,128,512]{2,1,0:T(8,128)(2,1)S(1)} %collective-permute-done.33.refs_1_), channel_id=1, source_target_pairs={{0,2},{2,4},{4,6},{6,7},{7,5},{5,3},{3,1},{1,0},{8,10},{10,12},{12... | collective-permute-start | bytes 1179656 | tf_op jit(solution)/shard_map/ppermute | solution.py:508
  212.4 22.6 %collective-permute-start.38 = (bf16[3,128,512]{2,1,0:T(8,128)(2,1)S(1)}, bf16[3,128,512]{2,1,0:T(8,128)(2,1)S(1)}, u32[]{:S(2)}, u32[]{:S(2)}) collective-permute-start(bf16[3,128,512]{2,1,0:T(8,128)(2,1)S(1)} %collective-permute-done.37.refs_2_), channel_id=1, source_target_pairs={{0,1},{2,0},{4,2},{6,4},{7,6},{5,7},{3,5},{1,3},{8,9},{10,8},{12,1... | collective-permute-start | bytes 1179656 | tf_op jit(solution)/shard_map/ppermute | solution.py:508
  232.7 12.1 %collective-permute-start.35 = (bf16[3,128,512]{2,1,0:T(8,128)(2,1)S(1)}, bf16[3,128,512]{2,1,0:T(8,128)(2,1)S(1)}, u32[]{:S(2)}, u32[]{:S(2)}) collective-permute-start(bf16[3,128,512]{2,1,0:T(8,128)(2,1)S(1)} %collective-permute-done.34.refs_0_.refs_3_), channel_id=1, source_target_pairs={{0,2},{2,4},{4,6},{6,7},{7,5},{5,3},{3,1},{1,0},{8,10},{10,12},{12... | collective-permute-start | bytes 1179656 | tf_op jit(solution)/shard_map/ppermute | solution.py:508
  235.1 12.1 %collective-permute-start.39 = (bf16[3,128,512]{2,1,0:T(8,128)(2,1)S(1)}, bf16[3,128,512]{2,1,0:T(8,128)(2,1)S(1)}, u32[]{:S(2)}, u32[]{:S(2)}) collective-permute-start(bf16[3,128,512]{2,1,0:T(8,128)(2,1)S(1)} %collective-permute-done.38.refs_1_.refs_4_), channel_id=1, source_target_pairs={{0,1},{2,0},{4,2},{6,4},{7,6},{5,7},{3,5},{1,3},{8,9},{10,8},{12,1... | collective-permute-start | bytes 1179656 | tf_op jit(solution)/shard_map/ppermute | solution.py:508
  235.1 18.0 %collective-permute-start.28 = (bf16[3,128,512]{2,1,0:T(8,128)(2,1)S(1)}, bf16[3,128,512]{2,1,0:T(8,128)(2,1)S(1)}, u32[]{:S(2)}, u32[]{:S(2)}) collective-permute-start(bf16[3,128,512]{2,1,0:T(8,128)(2,1)S(1)} %slice.61), channel_id=1, source_target_pairs={{0,2},{2,4},{4,6},{6,7},{7,5},{5,3},{3,1},{1,0},{8,10},{10,12},{12... | collective-permute-start | bytes 1179656 | tf_op jit(solution)/shard_map/ppermute | solution.py:508
  237.2 19.0 %collective-permute-start.32 = (bf16[3,128,512]{2,1,0:T(8,128)(2,1)S(1)}, bf16[3,128,512]{2,1,0:T(8,128)(2,1)S(1)}, u32[]{:S(2)}, u32[]{:S(2)}) collective-permute-start(bf16[3,128,512]{2,1,0:T(8,128)(2,1)S(1)} %slice.62), channel_id=1, source_target_pairs={{0,1},{2,0},{4,2},{6,4},{7,6},{5,7},{3,5},{1,3},{8,9},{10,8},{12,1... | collective-permute-start | bytes 1179656 | tf_op jit(solution)/shard_map/ppermute | solution.py:508
  244.8 12.7 %collective-permute-start.36 = (bf16[3,64,512]{2,1,0:T(8,128)(2,1)S(1)}, bf16[3,64,512]{2,1,0:T(8,128)(2,1)S(1)}, u32[]{:S(2)}, u32[]{:S(2)}) collective-permute-start(bf16[3,64,512]{2,1,0:T(8,128)(2,1)S(1)} %slice.63), channel_id=1, source_target_pairs={{0,2},{2,4},{4,6},{6,7},{7,5},{5,3},{3,1},{1,0},{8,10},{10,12},{12... | collective-permute-start | bytes 589832 | tf_op jit(solution)/shard_map/ppermute | solution.py:508
  247.2 12.6 %collective-permute-start.40 = (bf16[3,64,512]{2,1,0:T(8,128)(2,1)S(1)}, bf16[3,64,512]{2,1,0:T(8,128)(2,1)S(1)}, u32[]{:S(2)}, u32[]{:S(2)}) collective-permute-start(bf16[3,64,512]{2,1,0:T(8,128)(2,1)S(1)} %slice.64), channel_id=1, source_target_pairs={{0,1},{2,0},{4,2},{6,4},{7,6},{5,7},{3,5},{1,3},{8,9},{10,8},{12,1... | collective-permute-start | bytes 589832 | tf_op jit(solution)/shard_map/ppermute | solution.py:508
  248.3 21.1 %collective-permute-start.47 = (bf16[3,128,512]{2,1,0:T(8,128)(2,1)S(1)}, bf16[3,128,512]{2,1,0:T(8,128)(2,1)}, u32[]{:S(2)}, u32[]{:S(2)}) collective-permute-start(bf16[3,128,512]{2,1,0:T(8,128)(2,1)S(1)} %get-tuple-element.137.refs_0_), channel_id=1, source_target_pairs={{0,2},{2,4},{4,6},{6,7},{7,5},{5,3},{3,1},{1,0},{8,10},{10,12},{12... | collective-permute-start | bytes 1179656 | tf_op jit(solution)/shard_map/ppermute | solution.py:508
  253.2 17.5 %collective-permute-start.49 = (bf16[3,128,512]{2,1,0:T(8,128)(2,1)S(1)}, bf16[3,128,512]{2,1,0:T(8,128)(2,1)}, u32[]{:S(2)}, u32[]{:S(2)}) collective-permute-start(bf16[3,128,512]{2,1,0:T(8,128)(2,1)S(1)} %get-tuple-element.137.refs_0_), channel_id=1, source_target_pairs={{0,1},{2,0},{4,2},{6,4},{7,6},{5,7},{3,5},{1,3},{8,9},{10,8},{12,1... | collective-permute-start | bytes 1179656 | tf_op jit(solution)/shard_map/ppermute | solution.py:508
  262.7 16.6 %collective-permute-start.41 = (bf16[4,128,512]{2,1,0:T(8,128)(2,1)}, bf16[4,128,512]{2,1,0:T(8,128)(2,1)}, u32[]{:S(2)}, u32[]{:S(2)}) collective-permute-start(bf16[4,128,512]{2,1,0:T(8,128)(2,1)} %get-tuple-element.132), channel_id=1, source_target_pairs={{0,8},{8,0},{16,24},{24,16},{1,9},{9,1},{17,25},{25,17},{2,10},{10... | collective-permute-start | bytes 1572872 | tf_op jit(solution)/shard_map/ppermute | solution.py:511
  269.4 12.2 %collective-permute-start.48 = (bf16[3,128,512]{2,1,0:T(8,128)(2,1)}, bf16[3,128,512]{2,1,0:T(8,128)(2,1)S(1)}, u32[]{:S(2)}, u32[]{:S(2)}) collective-permute-start(bf16[3,128,512]{2,1,0:T(8,128)(2,1)} %collective-permute-done.47.refs_1_), channel_id=1, source_target_pairs={{0,2},{2,4},{4,6},{6,7},{7,5},{5,3},{3,1},{1,0},{8,10},{10,12},{12... | collective-permute-start | bytes 1179656 | tf_op jit(solution)/shard_map/ppermute | solution.py:508
  270.7 11.5 %collective-permute-start.50 = (bf16[3,128,512]{2,1,0:T(8,128)(2,1)}, bf16[3,128,512]{2,1,0:T(8,128)(2,1)S(1)}, u32[]{:S(2)}, u32[]{:S(2)}) collective-permute-start(bf16[3,128,512]{2,1,0:T(8,128)(2,1)} %collective-permute-done.49.refs_2_), channel_id=1, source_target_pairs={{0,1},{2,0},{4,2},{6,4},{7,6},{5,7},{3,5},{1,3},{8,9},{10,8},{12,1... | collective-permute-start | bytes 1179656 | tf_op jit(solution)/shard_map/ppermute | solution.py:508
  282.1 11.3 %collective-permute-start.51 = (bf16[3,128,512]{2,1,0:T(8,128)(2,1)S(1)}, bf16[3,128,512]{2,1,0:T(8,128)(2,1)S(1)}, u32[]{:S(2)}, u32[]{:S(2)}) collective-permute-start(bf16[3,128,512]{2,1,0:T(8,128)(2,1)S(1)} %collective-permute-done.48.refs_0_.refs_3_), channel_id=1, source_target_pairs={{0,2},{2,4},{4,6},{6,7},{7,5},{5,3},{3,1},{1,0},{8,10},{10,12},{12... | collective-permute-start | bytes 1179656 | tf_op jit(solution)/shard_map/ppermute | solution.py:508
  282.9 10.7 %collective-permute-start.52 = (bf16[3,128,512]{2,1,0:T(8,128)(2,1)S(1)}, bf16[3,128,512]{2,1,0:T(8,128)(2,1)S(1)}, u32[]{:S(2)}, u32[]{:S(2)}) collective-permute-start(bf16[3,128,512]{2,1,0:T(8,128)(2,1)S(1)} %collective-permute-done.50.refs_1_.refs_4_), channel_id=1, source_target_pairs={{0,1},{2,0},{4,2},{6,4},{7,6},{5,7},{3,5},{1,3},{8,9},{10,8},{12,1... | collective-permute-start | bytes 1179656 | tf_op jit(solution)/shard_map/ppermute | solution.py:508
  293.6 7.7 %collective-permute-start.53 = (bf16[3,64,512]{2,1,0:T(8,128)(2,1)S(1)}, bf16[3,64,512]{2,1,0:T(8,128)(2,1)S(1)}, u32[]{:S(2)}, u32[]{:S(2)}) collective-permute-start(bf16[3,64,512]{2,1,0:T(8,128)(2,1)S(1)} %slice.67), channel_id=1, source_target_pairs={{0,2},{2,4},{4,6},{6,7},{7,5},{5,3},{3,1},{1,0},{8,10},{10,12},{12... | collective-permute-start | bytes 589832 | tf_op jit(solution)/shard_map/ppermute | solution.py:508
  294.5 6.9 %collective-permute-start.54 = (bf16[3,64,512]{2,1,0:T(8,128)(2,1)S(1)}, bf16[3,64,512]{2,1,0:T(8,128)(2,1)S(1)}, u32[]{:S(2)}, u32[]{:S(2)}) collective-permute-start(bf16[3,64,512]{2,1,0:T(8,128)(2,1)S(1)} %slice.68), channel_id=1, source_target_pairs={{0,1},{2,0},{4,2},{6,4},{7,6},{5,7},{3,5},{1,3},{8,9},{10,8},{12,1... | collective-permute-start | bytes 589832 | tf_op jit(solution)/shard_map/ppermute | solution.py:508
  300.2 11.0 %collective-permute-start.42 = (bf16[1,2,128,512]{3,2,1,0:T(8,128)(2,1)}, bf16[1,2,128,512]{3,2,1,0:T(8,128)(2,1)}, u32[]{:S(2)}, u32[]{:S(2)}) collective-permute-start(bf16[1,2,128,512]{3,2,1,0:T(8,128)(2,1)} %fusion.10), channel_id=1, source_target_pairs={{0,16},{8,24},{16,0},{24,8},{1,17},{9,25},{17,1},{25,9},{2,18},{10... | collective-permute-start | bytes 786440 | tf_op jit(solution)/shard_map/ppermute | solution.py:511
  304.3 14.0 %collective-permute-start.55 = (bf16[4,128,512]{2,1,0:T(8,128)(2,1)}, bf16[4,128,512]{2,1,0:T(8,128)(2,1)S(1)}, u32[]{:S(2)}, u32[]{:S(2)}) collective-permute-start(bf16[4,128,512]{2,1,0:T(8,128)(2,1)} %get-tuple-element.150), channel_id=1, source_target_pairs={{0,8},{8,0},{16,24},{24,16},{1,9},{9,1},{17,25},{25,17},{2,10},{10... | collective-permute-start | bytes 1572872 | tf_op jit(solution)/shard_map/ppermute | solution.py:511
  306.3 1.3 collective-permute-start.45
  307.6 3.6 %collective-permute-start.46 = (f32[256,1]{0,1:T(1,128)S(1)}, f32[256,1]{0,1:T(1,128)S(1)}, u32[]{:S(2)}, u32[]{:S(2)}) collective-permute-start(f32[256,1]{0,1:T(1,128)S(1)} %add.119), channel_id=1, source_target_pairs={{0,16},{8,24},{16,0},{24,8},{1,17},{9,25},{17,1},{25,9},{2,18},{10... | collective-permute-start | bytes 3080 | tf_op jit(solution)/shard_map/ppermute | solution.py:511
  312.4 14.8 %collective-permute-start.43 = (bf16[128,512]{1,0:T(8,128)(2,1)S(1)}, bf16[128,512]{1,0:T(8,128)(2,1)S(1)}, u32[]{:S(2)}, u32[]{:S(2)}) collective-permute-start(bf16[128,512]{1,0:T(8,128)(2,1)S(1)} %get-tuple-element.162), channel_id=1, source_target_pairs={{0,0},{1,1},{2,8},{3,9},{4,16},{5,17},{6,24},{7,25},{8,2},{9,3},{1... | collective-permute-start | bytes 393224 | tf_op jit(solution)/shard_map/ppermute | solution.py:592
  316.3 13.4 %collective-permute-start.44 = (bf16[128,512]{1,0:T(8,128)(2,1)S(1)}, bf16[128,512]{1,0:T(8,128)(2,1)S(1)}, u32[]{:S(2)}, u32[]{:S(2)}) collective-permute-start(bf16[128,512]{1,0:T(8,128)(2,1)S(1)} %get-tuple-element.161), channel_id=1, source_target_pairs={{0,1},{1,0},{2,9},{3,8},{4,17},{5,16},{6,25},{7,24},{8,3},{9,2},{1... | collective-permute-start | bytes 393224 | tf_op jit(solution)/shard_map/ppermute | solution.py:592
  318.6 13.5 %collective-permute-start.56 = (bf16[1,2,128,512]{3,2,1,0:T(8,128)(2,1)S(1)}, bf16[1,2,128,512]{3,2,1,0:T(8,128)(2,1)S(1)}, u32[]{:S(2)}, u32[]{:S(2)}) collective-permute-start(bf16[1,2,128,512]{3,2,1,0:T(8,128)(2,1)S(1)} %fusion.11), channel_id=1, source_target_pairs={{0,16},{8,24},{16,0},{24,8},{1,17},{9,25},{17,1},{25,9},{2,18},{10... | collective-permute-start | bytes 786440 | tf_op jit(solution)/shard_map/ppermute | solution.py:511
  332.2 13.5 %collective-permute-start.57 = (bf16[128,512]{1,0:T(8,128)(2,1)S(1)}, bf16[128,512]{1,0:T(8,128)(2,1)S(1)}, u32[]{:S(2)}, u32[]{:S(2)}) collective-permute-start(bf16[128,512]{1,0:T(8,128)(2,1)S(1)} %get-tuple-element.166), channel_id=1, source_target_pairs={{0,0},{1,1},{2,8},{3,9},{4,16},{5,17},{6,24},{7,25},{8,2},{9,3},{1... | collective-permute-start | bytes 393224 | tf_op jit(solution)/shard_map/ppermute | solution.py:592
  334.1 13.5 %collective-permute-start.58 = (bf16[128,512]{1,0:T(8,128)(2,1)S(1)}, bf16[128,512]{1,0:T(8,128)(2,1)S(1)}, u32[]{:S(2)}, u32[]{:S(2)}) collective-permute-start(bf16[128,512]{1,0:T(8,128)(2,1)S(1)} %get-tuple-element.165), channel_id=1, source_target_pairs={{0,1},{1,0},{2,9},{3,8},{4,17},{5,16},{6,25},{7,24},{8,3},{9,2},{1... | collective-permute-start | bytes 393224 | tf_op jit(solution)/shard_map/ppermute | solution.py:592
  (63 other events, 888.1 us)

commit v5 on v4

--- a/solution.py
+++ b/solution.py
@@ -11,11 +11,22 @@
 
 HEAD_DIM = 128
 NORM_EPS = 1e-05
-SMALL, LARGE = 20 * 1024 * 1024, 56 * 1024 * 1024
-
-
-def params(limit):
-    return pltpu.CompilerParams(dimension_semantics=("arbitrary",), vmem_limit_bytes=limit)
+VMEM = 24 * 1024 * 1024
+
+
+def params():
+    return pltpu.CompilerParams(dimension_semantics=("arbitrary",), vmem_limit_bytes=VMEM)
+
+
+def tied(kernel, inputs, ties):
+    def inner(*refs):
+        kernel(*refs[:inputs], *refs[inputs + ties :])
+
+    return inner
+
+
+def tie_specs(ties):
+    return [pl.BlockSpec(memory_space=pl.ANY)] * len(ties)
 
 
 def cost(flops, moved):
@@ -106,7 +117,7 @@
             jax.ShapeDtypeStruct((3, depth, columns), jnp.bfloat16),
             jax.ShapeDtypeStruct((3, columns, depth), jnp.bfloat16),
         ],
-        compiler_params=params(SMALL),
+        compiler_params=params(),
         cost_estimate=cost(3 * depth * columns, 18 * depth * columns),
         name="scaled_weights",
     )(w_quant, w_scale)
@@ -145,11 +156,53 @@
         ),
         out_shape=[jax.ShapeDtypeStruct((length, part), jnp.bfloat16)] * size
         + [jax.ShapeDtypeStruct((length, 128), jnp.float32)],
-        compiler_params=params(SMALL),
+        compiler_params=params(),
         cost_estimate=cost(8 * length * width, 4 * length * width),
         name="normed_blocks",
     )(idx, tokens, gain)
     return blocks, inverse
+
+
+def stack_kernel(*refs):
+    for place, block in enumerate(refs[:-1]):
+        refs[-1][place] = block[...]
+
+
+def stack(blocks, ties):
+    count, shape = len(blocks), blocks[0].shape
+    block = pl.BlockSpec(shape, lambda i: (0, 0))
+    return pl.pallas_call(
+        tied(stack_kernel, count, len(ties)),
+        grid=(1,),
+        in_specs=[block] * count + tie_specs(ties),
+        out_specs=pl.BlockSpec((count, *shape), lambda i: (0, 0, 0)),
+        out_shape=jax.ShapeDtypeStruct((count, *shape), blocks[0].dtype),
+        compiler_params=params(),
+        cost_estimate=cost(0, 4 * count * shape[0] * shape[1]),
+        name="stack",
+    )(*blocks, *ties)
+
+
+def pass_kernel(right, left, right_out, left_out):
+    rows, sent = right.shape[1], right_out.shape[1]
+    right_out[...] = right[:, :sent]
+    left_out[...] = left[:, rows - sent :]
+
+
+def pass_on(right, left, halve, ties):
+    _, rows, wide = right.shape
+    sent = rows // 2 if halve else rows
+    result = jax.ShapeDtypeStruct((3, sent, wide), right.dtype)
+    return pl.pallas_call(
+        tied(pass_kernel, 2, len(ties)),
+        grid=(1,),
+        in_specs=[pl.BlockSpec(right.shape, lambda i: (0, 0, 0))] * 2 + tie_specs(ties),
+        out_specs=[pl.BlockSpec(result.shape, lambda i: (0, 0, 0))] * 2,
+        out_shape=[result, result],
+        compiler_params=params(),
+        cost_estimate=cost(0, 12 * sent * wide),
+        name="pass_on",
+    )(right, left, *ties)
 
 
 def turn_kernel(count, idx, mine, other, mine_far, other_far, out):
@@ -177,7 +230,7 @@
             out_specs=pl.BlockSpec(shape, lambda i, idx: (0, 0)),
         ),
         out_shape=jax.ShapeDtypeStruct(shape, jnp.bfloat16),
-        compiler_params=params(SMALL),
+        compiler_params=params(),
         cost_estimate=cost(2 * count * length * part, 8 * count * length * part),
         name="turn",
     )(idx, mine, other, mine_far, other_far)
@@ -229,20 +282,20 @@
             out_specs=[pl.BlockSpec((1, half, wide), lambda m, idx: (m, 0, 0))] * 4,
         ),
         out_shape=[result] * 4,
-        compiler_params=params(SMALL),
+        compiler_params=params(),
         cost_estimate=cost(12 * length * part * columns, 16 * part * columns),
         name="sum_first",
     )(idx, mine, other, weights, weights)
 
 
-def sum_step(idx, size, mine, other, places, weights, from_left, from_right, chunk, wide):
+def sum_step(idx, size, mine, other, places, weights, from_left, from_right, chunk, wide, ties):
     _, length, part = mine.shape
     block_r = pl.BlockSpec((1, length, part), lambda m, idx: (places[0], 0, 0))
     block_l = pl.BlockSpec((1, length, part), lambda m, idx: (places[1], 0, 0))
     came = pl.BlockSpec((1, from_left.shape[1], wide), lambda m, idx: (m, 0, 0))
     whole = jax.ShapeDtypeStruct((3, length, wide), jnp.bfloat16)
     return pl.pallas_call(
-        sum_step_kernel,
+        tied(sum_step_kernel, 9, len(ties)),
         grid_spec=pltpu.PrefetchScalarGridSpec(
             num_scalar_prefetch=1,
             grid=(3,),
@@ -254,19 +307,20 @@
                 *weight_halves(size, part, wide, chunk),
                 came,
                 came,
+                *tie_specs(ties),
             ],
             out_specs=[pl.BlockSpec((1, length, wide), lambda m, idx: (m, 0, 0))] * 2,
         ),
         out_shape=[whole, whole],
-        compiler_params=params(SMALL),
+        compiler_params=params(),
         cost_estimate=cost(24 * length * part * wide, 24 * part * wide),
         name="sum_step",
-    )(idx, mine, other, mine, other, weights, weights, from_left, from_right)
+    )(idx, mine, other, mine, other, weights, weights, from_left, from_right, *ties)
 
 
 def attention_kernel(
     idx, mine, other, weight, weight_other, from_left, from_right, d_out, cosine, sine,
-    output, pre, dots,
+    output, dots, *pres,
 ):
     length = mine.shape[1]
     proj = [
@@ -302,9 +356,12 @@
     d_key = mm_tn(d_scores, query).astype(jnp.bfloat16).astype(jnp.float32)
     pre_query = rotate(d_query, -sin).astype(jnp.bfloat16)
     pre_key = rotate(d_key, -sin).astype(jnp.bfloat16)
-    pre[0] = pre_query
-    pre[1] = pre_key
-    pre[2] = d_value
+    rows = length // len(pres)
+    for position, pre in enumerate(pres):
+        span = slice(position * rows, (position + 1) * rows)
+        pre[0] = pre_query[span]
+        pre[1] = pre_key[span]
+        pre[2] = d_value[span]
     product = (
         pre_query.astype(jnp.float32) * proj[0]
         + pre_key.astype(jnp.float32) * proj[1]
@@ -320,7 +377,7 @@
         dots[...] += product
 
 
-def attention(idx, size, mine, other, weights, from_left, from_right, d_out, tables, chunk, wide):
+def attention(idx, size, mine, other, weights, from_left, from_right, d_out, tables, chunk, wide, parts):
     _, length, part = mine.shape
     heads = wide // HEAD_DIM
     first = chunk * heads
@@ -345,16 +402,16 @@
             ],
             out_specs=[
                 pl.BlockSpec((length, HEAD_DIM), lambda h, idx: (0, h)),
-                stack,
                 table,
+                *[pl.BlockSpec((3, length // parts, HEAD_DIM), lambda h, idx: (0, 0, h))] * parts,
             ],
         ),
         out_shape=[
             jax.ShapeDtypeStruct((length, wide), jnp.bfloat16),
-            jax.ShapeDtypeStruct((3, length, wide), jnp.bfloat16),
             jax.ShapeDtypeStruct((length, HEAD_DIM), jnp.float32),
+            *[jax.ShapeDtypeStruct((3, length // parts, wide), jnp.bfloat16)] * parts,
         ],
-        compiler_params=params(SMALL),
+        compiler_params=params(),
         cost_estimate=cost(12 * length * part * wide, 24 * part * wide),
         name="attention",
     )(idx, mine, other, weights, weights, from_left, from_right, d_out, *tables)
@@ -392,7 +449,7 @@
         out_specs=result,
         out_shape=jax.ShapeDtypeStruct((3, depth, columns), jnp.float32),
         input_output_aliases=aliases,
-        compiler_params=params(LARGE),
+        compiler_params=params(),
         cost_estimate=cost(
             6 * count * rows * depth * wide, 6 * count * rows * wide + 12 * depth * wide
         ),
@@ -434,7 +491,7 @@
         ],
         out_specs=results,
         out_shape=[jax.ShapeDtypeStruct((rows, depth), jnp.float32)] * count,
-        compiler_params=params(SMALL),
+        compiler_params=params(),
         cost_estimate=cost(6 * count * rows * depth * wide, 12 * count * rows * wide),
         name="term_step",
     )(turned, *pieces, *befores)
@@ -455,13 +512,13 @@
             send[idx[3 * count + 1 + place]] = total.astype(jnp.bfloat16)
 
 
-def term_last(idx, turned, before, pieces, nears, chunk, wide):
+def term_last(idx, turned, before, pieces, nears, chunk, wide, ties):
     count = len(nears) + 1
     rows, depth = before.shape
     result = pl.BlockSpec((count // 2, rows, depth), lambda i, idx: (0, 0, 0))
     block = pl.BlockSpec((rows, depth), lambda i, idx: (0, 0))
     return pl.pallas_call(
-        functools.partial(term_last_kernel, count),
+        tied(functools.partial(term_last_kernel, count), count + 4, len(ties)),
         grid_spec=pltpu.PrefetchScalarGridSpec(
             num_scalar_prefetch=1,
             grid=(1,),
@@ -470,6 +527,7 @@
                 block,
                 *[pl.BlockSpec(piece.shape, lambda i, idx: (0, 0, 0)) for piece in pieces],
                 *[block] * (count - 1),
+                *tie_specs(ties),
             ],
             out_specs=[result, result],
         ),
@@ -477,15 +535,10 @@
             jax.ShapeDtypeStruct((count // 2, rows, depth), jnp.float32),
             jax.ShapeDtypeStruct((count // 2, rows, depth), jnp.bfloat16),
         ],
-        compiler_params=params(SMALL),
+        compiler_params=params(),
         cost_estimate=cost(6 * rows * depth * wide, 12 * count * rows * depth),
         name="term_last",
-    )(idx, turned, before, *pieces, *nears)
-
-
-def after(first, *arrays):
-    tied = lax.optimization_barrier((first, *arrays))
-    return tied[1:]
+    )(idx, turned, before, *pieces, *nears, *ties)
 
 
 def local(tokens, norm_gain, w_quant, w_scale, d_out):
@@ -515,10 +568,12 @@
     other_far = swap(mine_far, 1)
     weights, turned = scaled_weights(w_quant, w_scale)
     firsts = sum_first(idx, size, mine_far, other_far, weights)
-    nears = after(mine_far, *blocks[:far], *blocks[far + 1 :])
-    nears = [*nears[:far], None, *nears[far:]]
-    mine = jnp.stack([shift(nears[-d % size], -d) if d else blocks[0] for d in distances[:-1]])
+    mine = stack(
+        [shift(blocks[-d % size], -d) if d else blocks[0] for d in distances[:-1]], firsts[:1]
+    )
     other = swap(mine, 1)
+
+    rows_turned = turn(idx, mine, other, mine_far, other_far)
 
     tables = rope_tables(length, HEAD_DIM)
     arrived = []
@@ -528,27 +583,26 @@
             from_left, from_right = shift(right, 1), shift(left, -1)
             if distance:
                 places = distances.index(distance), distances.index(-distance)
+                ties = [rows_turned] if distance == 1 else []
                 right, left = sum_step(
-                    idx, size, mine, other, places, weights, from_left, from_right, chunk, wide
+                    idx, size, mine, other, places, weights, from_left, from_right, chunk, wide, ties
                 )
         arrived.append((from_left, from_right))
 
-    outputs, pres, dots = [], [], 0.0
+    outputs, sets, dots = [], [], 0.0
     for chunk in range(2):
-        output, pre, product = attention(
-            idx, size, mine, other, weights, *arrived[chunk], d_out, tables, chunk, wide
+        output, product, *parts = attention(
+            idx, size, mine, other, weights, *arrived[chunk], d_out, tables, chunk, wide, chunk + 1
         )
         outputs.append(output)
-        pres.append(pre)
+        sets += parts
         dots += jnp.sum(product, axis=-1, keepdims=True)
     bit = 1
     while bit < nodes:
         dots = dots + swap(dots, bit)
         bit *= 2
-    rows_turned = turn(idx, mine, other, mine_far, other_far)
 
     half = length // 2
-    sets = [pres[0], pres[1][:, :half], pres[1][:, half:]]
     gathered = [[block] for block in sets]
     moving = [(block, block) for block in sets]
     schedule = [(0, 1)]
@@ -562,9 +616,9 @@
     gains_part = lax.dynamic_slice_in_dim(norm_gain, node * share, share, 0).astype(jnp.float32)
     inverse_rms = inverse_rms[:, :1]
 
-    def start_term(part):
+    def start_term(part, ties):
         keep, send = term_last(
-            idx, turned, lasts[0][part], gathered[1 + part][-2:], terms[1 + part], 1, wide
+            idx, turned, lasts[part], gathered[1 + part][-2:], terms[1 + part], 1, wide, ties
         )
         return keep + swap(send, 1).astype(jnp.float32)
 
@@ -580,7 +634,7 @@
             bit *= 2
         return summed.astype(jnp.bfloat16)
 
-    def end_term(summed, part):
+    def relocate(summed):
         came = []
         for turn in range(group):
             block = lax.dynamic_index_in_dim(summed, (here + turn) % group, 0, keepdims=False)
@@ -590,6 +644,9 @@
                 for s in range(size)
             ]
             came.append(lax.ppermute(block, ("node", "local"), moves))
+        return came
+
+    def end_term(came, part):
         came = jnp.stack(came)
         upstream = jnp.concatenate(
             [
@@ -606,21 +663,14 @@
         return d_rows.astype(jnp.bfloat16)
 
     terms = [[], [], []]
-    lasts = [None]
-    first_grads = half_grads = early = None
+    early = summed = None
     for ring, step in schedule:
         right, left = moving[ring]
         if step == far:
-            middle = right.shape[1] // 2
-            right, left = right[:, :middle], left[:, middle:]
-        if (ring, step) == (1, 1):
-            right, left = after(moving[0][0], right, left)
-        if (ring, step) == (2, 1):
-            right, left = after(moving[0][0], right, left)
-        if (ring, step) == (2, far - 1):
-            right, left = after((first_grads, early), right, left)
-        if (ring, step) == (2, far):
-            right, left = after((half_grads, summed), right, left)
+            ties = [[], [dots, *moving[2]], [summed]][ring]
+            right, left = pass_on(right, left, True, ties)
+        elif (ring, step) == (2, far - 1):
+            right, left = pass_on(right, left, False, [early, first_grads])
         right, left = shift(right, 1), shift(left, -1)
         moving[ring] = right, left
         gathered[ring] += [right, left]
@@ -631,18 +681,19 @@
             befores = terms[0][known : known + len(pieces)] if ring else []
             terms[ring] += term_step(turned, pieces, befores, part, chunk, wide)
         elif ring == 0:
-            lasts[0] = term_step(turned, [right, left], [], 0, 0, wide)
+            lasts = term_step(turned, [right, left], [], 0, 0, wide)
             first_grads = grads_chunk(
                 size, rows_turned, gathered[0], 0, None, False, 0, wide, columns
             )
         elif ring == 1:
-            early = start_term(0)
+            early = start_term(0, [])
             half_grads = grads_chunk(
                 size, rows_turned, gathered[1], 0, first_grads, False, 1, wide, columns
             )
             summed = sum_nodes(early)
-    late = start_term(1)
-    d_tokens = jnp.concatenate([end_term(summed, 0), end_term(sum_nodes(late), 1)], axis=0)
+    came = relocate(summed)
+    late = start_term(1, came)
+    d_tokens = jnp.concatenate([end_term(came, 0), end_term(relocate(sum_nodes(late)), 1)], axis=0)
     grads = grads_chunk(size, rows_turned, gathered[2], half, half_grads, True, 1, wide, columns)
     return (jnp.concatenate(outputs, axis=-1), d_tokens, grads)
 

time: 350 us -> 366 us (1.046)
  local copies, waits for them, and re-layouts: 13.5 us -> 36.5 us
  waiting for transfers between devices: 180 us -> 171 us
  starting transfers between devices: 75.1 us -> 67.8 us
  Pallas kernels: 66.8 us -> 71.9 us
    unnamed x142 -> x154, local copies, waits for them, and re-layouts: 9.99 us -> 32.4 us
    ppermute x4, waiting for transfers between devices: 13.1 us -> 4.21 us  [relocate(): came.append(lax.ppermute(block, ('node', 'local'), moves))]
    pallas_call x10, Pallas kernels: 8.93 us -> 14.8 us  [term_step(): pl.pallas_call(kernel, grid=(1,), in_specs=[pl.BlockSpec((3, wide, depth)...]
    ppermute x47, starting transfers between devices: 60 us -> 55 us  [shift(): return lax.ppermute(array, 'local', moves)]
    pallas_call x3, Pallas kernels: 21.7 us -> 17 us  [grads_chunk(): pl.pallas_call(kernel, grid=(3,), in_specs=in_specs, out_specs=result, ou...]
    pallas_call x8 -> x13, Pallas kernels: 16.3 us -> 20 us  [the longest x6 12.3 us: sum_step(): pl.pallas_call(tied(sum_step_kernel, 9, len(ties)), grid_spec=pltpu.Prefe...]
  transfers between devices with their start and end apart: 59 -> 59, of which waited for: 36 -> 32; matrix products, arithmetic and copies ran while one was open for 4% -> 4% of each run, Pallas kernels for 18% -> 17%
where the time goes in v5:
time: 366 us; the launch traced here: 363 us
  waiting for transfers between devices  171 us (47%)
  Pallas kernels  71.9 us (20%)
  starting transfers between devices  67.8 us (19%)
  local copies, waits for them, and re-layouts  36.5 us (10%)
  other arithmetic  14.1 us (4%)
    ppermute x47, waiting for transfers between devices, shift(): return lax.ppermute(array, 'local', moves)  160 us
    ppermute x47, starting transfers between devices, shift(): return lax.ppermute(array, 'local', moves)  55 us
    unnamed x154, local copies, waits for them, and re-layouts  32.4 us
    pallas_call x3, Pallas kernels, grads_chunk(): pl.pallas_call(kernel, grid=(3,), in_specs=in_specs, out_specs=result, ou...  17 us
    pallas_call x10, Pallas kernels, term_step(): pl.pallas_call(kernel, grid=(1,), in_specs=[pl.BlockSpec((3, wide, depth)...  14.8 us
    pallas_call x2, Pallas kernels, attention(): pl.pallas_call(attention_kernel, grid_spec=pltpu.PrefetchScalarGridSpec(n...  14.5 us
    pallas_call x6, Pallas kernels, sum_step(): pl.pallas_call(tied(sum_step_kernel, 9, len(ties)), grid_spec=pltpu.Prefe...  12.3 us
    ppermute x4, starting transfers between devices, relocate(): came.append(lax.ppermute(block, ('node', 'local'), moves))  11.4 us
  transfers between devices with their start and end apart: 59, of which 32 were waited for; matrix products, arithmetic and copies ran while one was open for 4% of the time, Pallas kernels for 17%

profile of v5, /device:TPU:2, one launch (start us, length us, event | category | flops | bytes accessed | tf_op | source)
XLA Modules:
  0.0 363.0 jit_solution(17011850429734699065)
XLA Ops:
  2.1 1.6 copy-done.18
  3.6 1.4 normed_blocks.1
  5.7 4.6 %collective-permute-start.6 = (bf16[256,256]{1,0:T(8,128)(2,1)S(1)}, bf16[256,256]{1,0:T(8,128)(2,1)S(1)}, u32[]{:S(2)}, u32[]{:S(2)}) collective-permute-start(bf16[256,256]{1,0:T(8,128)(2,1)S(1)} %get-tuple-element.79), channel_id=1, source_target_pairs={{0,7},{2,5},{4,3},{6,1},{7,0},{5,2},{3,4},{1,6},{8,15},{10,13},{12... | collective-permute-start | bytes 393224 | tf_op jit(solution)/shard_map/ppermute | solution.py:561
  10.3 4.5 %collective-permute-done.6.mine.mine_far = bf16[256,256]{1,0:T(8,128)(2,1)S(1)} collective-permute-done((bf16[256,256]{1,0:T(8,128)(2,1)S(1)}, bf16[256,256]{1,0:T(8,128)(2,1)S(1)}, u32[]{:S(2)}, u32[]{:S(2)}) %collective-permute-start.6) | collective-permute-done | bytes 131104 | tf_op jit(solution)/shard_map/ppermute | solution.py:561
  15.3 3.4 collective-permute-start.2
  19.9 1.7 collective-permute-start.4
  21.7 2.1 collective-permute-start.5
  23.8 1.9 copy-done.28
  27.5 1.9 sum_first.1
  29.4 4.6 %collective-permute-done.3.refs_4_ = bf16[256,256]{1,0:T(8,128)(2,1)S(1)} collective-permute-done((bf16[256,256]{1,0:T(8,128)(2,1)S(1)}, bf16[256,256]{1,0:T(8,128)(2,1)S(1)}, u32[]{:S(2)}, u32[]{:S(2)}) %collective-permute-start.3) | collective-permute-done | bytes 131104 | tf_op jit(solution)/shard_map/ppermute | solution.py:561
  35.2 3.1 collective-permute-start.10
  38.4 9.0 %collective-permute-done.10.refs_8_ = bf16[3,128,512]{2,1,0:T(8,128)(2,1)S(1)} collective-permute-done((bf16[3,128,512]{2,1,0:T(8,128)(2,1)S(1)}, bf16[3,128,512]{2,1,0:T(8,128)(2,1)S(1)}, u32[]{:S(2)}, u32[]{:S(2)}) %collective-permute-start.10) | collective-permute-done | bytes 393248 | tf_op jit(solution)/shard_map/ppermute | solution.py:561
  47.3 2.2 collective-permute-done.9.refs_7_
  49.5 2.1 sum_step.6
  51.9 1.7 collective-permute-start.12
  53.7 16.8 %collective-permute-done.11.refs_7_ = bf16[3,256,512]{2,1,0:T(8,128)(2,1)S(1)} collective-permute-done((bf16[3,256,512]{2,1,0:T(8,128)(2,1)S(1)}, bf16[3,256,512]{2,1,0:T(8,128)(2,1)S(1)}, u32[]{:S(2)}, u32[]{:S(2)}) %collective-permute-start.11) | collective-permute-done | bytes 786464 | tf_op jit(solution)/shard_map/ppermute | solution.py:561
  70.8 2.1 sum_step.7
  72.8 1.7 collective-permute-start.13
  74.9 1.6 collective-permute-start.17
  76.9 22.3 %collective-permute-done.17.refs_7_ = bf16[3,128,512]{2,1,0:T(8,128)(2,1)S(1)} collective-permute-done((bf16[3,128,512]{2,1,0:T(8,128)(2,1)S(1)}, bf16[3,128,512]{2,1,0:T(8,128)(2,1)S(1)}, u32[]{:S(2)}, u32[]{:S(2)}) %collective-permute-start.17) | collective-permute-done | bytes 393248 | tf_op jit(solution)/shard_map/ppermute | solution.py:561
  99.2 1.6 collective-permute-done.18.refs_8_
  100.8 2.1 sum_step.9
  102.9 1.4 collective-permute-start.19
  106.2 2.1 sum_step.8
  108.2 1.4 collective-permute-start.15
  110.9 12.5 %collective-permute-done.19.refs_7_ = bf16[3,256,512]{2,1,0:T(8,128)(2,1)S(1)} collective-permute-done((bf16[3,256,512]{2,1,0:T(8,128)(2,1)S(1)}, bf16[3,256,512]{2,1,0:T(8,128)(2,1)S(1)}, u32[]{:S(2)}, u32[]{:S(2)}) %collective-permute-start.19) | collective-permute-done | bytes 786464 | tf_op jit(solution)/shard_map/ppermute | solution.py:561
  124.7 2.1 sum_step.10
  129.0 11.2 %collective-permute-done.15.from_left = bf16[3,256,512]{2,1,0:T(8,128)(2,1)S(1)} collective-permute-done((bf16[3,256,512]{2,1,0:T(8,128)(2,1)S(1)}, bf16[3,256,512]{2,1,0:T(8,128)(2,1)S(1)}, u32[]{:S(2)}, u32[]{:S(2)}) %collective-permute-start.15) | collective-permute-done | bytes 786464 | tf_op jit(solution)/shard_map/ppermute | solution.py:561
  141.6 7.2 %attention.2 = (bf16[256,512]{1,0:T(8,128)(2,1)S(1)}, f32[256,128]{1,0:T(8,128)S(1)}, bf16[3,256,512]{2,1,0:T(8,128)(2,1)S(1)}) custom-call(s32[33]{0:T(128)S(1)} %fusion.21.idx.refs_0_, bf16[7,256,256]{2,1,0:T(8,128)(2,1)S(1)} %stack.25.refs_1_.refs_3_.mine, bf16[7,256,256]{2,1,0:T(8,128)(2,1)S(1)} %collective-permute-done.8.refs_2_.refs_4_.other, ...), custom_call_target="tpu_custom_call" | custom-call | flops 402653184 | bytes 3145728 | tf_op jit(solution)/shard_map/attention/pallas_call | solution.py:387
  151.5 5.6 %collective-permute-done.21.refs_7_ = bf16[3,256,512]{2,1,0:T(8,128)(2,1)S(1)} collective-permute-done((bf16[3,256,512]{2,1,0:T(8,128)(2,1)S(1)}, bf16[3,256,512]{2,1,0:T(8,128)(2,1)S(1)}, u32[]{:S(2)}, u32[]{:S(2)}) %collective-permute-start.21) | collective-permute-done | bytes 786464 | tf_op jit(solution)/shard_map/ppermute | solution.py:561
  158.4 2.1 sum_step.11
  162.6 12.7 %collective-permute-done.28.refs_2_ = bf16[3,256,512]{2,1,0:T(8,128)(2,1)S(1)} collective-permute-done((bf16[3,256,512]{2,1,0:T(8,128)(2,1)S(1)}, bf16[3,256,512]{2,1,0:T(8,128)(2,1)S(1)}, u32[]{:S(2)}, u32[]{:S(2)}) %collective-permute-start.28) | collective-permute-done | bytes 786464 | tf_op jit(solution)/shard_map/ppermute | solution.py:561
  177.3 13.5 %collective-permute-done.23.from_left = bf16[3,256,512]{2,1,0:T(8,128)(2,1)S(1)} collective-permute-done((bf16[3,256,512]{2,1,0:T(8,128)(2,1)S(1)}, bf16[3,256,512]{2,1,0:T(8,128)(2,1)S(1)}, u32[]{:S(2)}, u32[]{:S(2)}) %collective-permute-start.23) | collective-permute-done | bytes 786464 | tf_op jit(solution)/shard_map/ppermute | solution.py:561
  192.1 7.3 %attention.3 = (bf16[256,512]{1,0:T(8,128)(2,1)S(1)}, f32[256,128]{1,0:T(8,128)S(1)}, bf16[3,128,512]{2,1,0:T(8,128)(2,1)S(1)}, bf16[3,128,512]{2,1,0:T(8,128)(2,1)S(1)}) custom-call(s32[33]{0:T(128)S(1)} %fusion.21.idx.refs_0_, bf16[7,256,256]{2,1,0:T(8,128)(2,1)S(1)} %stack.25.refs_1_.refs_3_.mine, ...), custom_call_target="tpu_custom_call" | custom-call | flops 402653184 | bytes 3145728 | tf_op jit(solution)/shard_map/attention/pallas_call | solution.py:387
  203.6 5.5 %collective-permute-done.29.refs_1_.refs_4_ = bf16[3,256,512]{2,1,0:T(8,128)(2,1)} collective-permute-done((bf16[3,256,512]{2,1,0:T(8,128)(2,1)S(1)}, bf16[3,256,512]{2,1,0:T(8,128)(2,1)}, u32[]{:S(2)}, u32[]{:S(2)}) %collective-permute-start.29) | collective-permute-done | bytes 786464 | tf_op jit(solution)/shard_map/ppermute | solution.py:561
  211.1 6.4 %collective-permute-done.36.refs_2_ = bf16[3,128,512]{2,1,0:T(8,128)(2,1)} collective-permute-done((bf16[3,128,512]{2,1,0:T(8,128)(2,1)S(1)}, bf16[3,128,512]{2,1,0:T(8,128)(2,1)}, u32[]{:S(2)}, u32[]{:S(2)}) %collective-permute-start.36) | collective-permute-done | bytes 393248 | tf_op jit(solution)/shard_map/ppermute | solution.py:561
  222.4 1.6 collective-permute-done.39
  225.5 5.0 %collective-permute-done.40 = f32[256,1]{1,0:T(8,128)S(1)} collective-permute-done((f32[256,1]{1,0:T(8,128)S(1)}, f32[256,1]{1,0:T(8,128)S(1)}, u32[]{:S(2)}, u32[]{:S(2)}) %collective-permute-start.40) | collective-permute-done | bytes 1056 | tf_op jit(solution)/shard_map/ppermute | solution.py:564
  231.2 11.6 %collective-permute-done.37.refs_1_.refs_4_ = bf16[3,128,512]{2,1,0:T(8,128)(2,1)} collective-permute-done((bf16[3,128,512]{2,1,0:T(8,128)(2,1)}, bf16[3,128,512]{2,1,0:T(8,128)(2,1)}, u32[]{:S(2)}, u32[]{:S(2)}) %collective-permute-start.37) | collective-permute-done | bytes 393248 | tf_op jit(solution)/shard_map/ppermute | solution.py:561
  246.0 1.5 pass_on.4
  248.4 2.7 collective-permute-done.42.refs_4_.refs_2_
  255.2 1.4 term_step.11
  256.6 2.4 term_step.12
  259.6 1.4 collective-permute-done.35.refs_0_.refs_5_
  263.1 2.4 term_step.13
  265.6 1.9 term_step.14
  268.3 2.4 term_step.15
  272.7 2.0 term_last.2
  277.9 1.5 convert_add_fusion.1.refs_2_
  285.1 6.2 %grads.3.refs_3_.refs_9_ = f32[3,512,1024]{2,1,0:T(8,128)} custom-call(bf16[512,2048]{1,0:T(8,128)(2,1)S(1)} %copy-done.2, bf16[3,256,512]{2,1,0:T(8,128)(2,1)S(1)} %copy-done.21, bf16[3,256,512]{2,1,0:T(8,128)(2,1)S(1)} %copy-done.27, bf16[3,256,512]{2,1,0:T(8,128)(2,1)S(1)} %copy-done.24, bf16[3,256,512]{2,1,0:T(8,128)(2,1)} %collective-permute-done.26.refs_0_.refs_3_, ...), custom_call_target="tpu_custom_call" | custom-call | flops 3221225472 | bytes 9437184 | tf_op jit(solution)/shard_map/grads/pallas_call | solution.py:445
  291.4 2.8 copy-done
  298.4 8.0 %collective-permute-done.51.refs_0_.refs_5_ = bf16[3,128,512]{2,1,0:T(8,128)(2,1)} collective-permute-done((bf16[3,128,512]{2,1,0:T(8,128)(2,1)}, bf16[3,128,512]{2,1,0:T(8,128)(2,1)}, u32[]{:S(2)}, u32[]{:S(2)}) %collective-permute-start.51) | collective-permute-done | bytes 393248 | tf_op jit(solution)/shard_map/ppermute | solution.py:561
  310.5 2.0 collective-permute-start.48
  312.5 4.1 %collective-permute-start.47 = (bf16[128,512]{1,0:T(8,128)(2,1)S(1)}, bf16[128,512]{1,0:T(8,128)(2,1)S(1)}, u32[]{:S(2)}, u32[]{:S(2)}) collective-permute-start(bf16[128,512]{1,0:T(8,128)(2,1)S(1)} %get-tuple-element.156), channel_id=1, source_target_pairs={{0,0},{1,1},{2,8},{3,9},{4,16},{5,17},{6,24},{7,25},{8,2},{9,3},{1... | collective-permute-start | bytes 393224 | tf_op jit(solution)/shard_map/ppermute | solution.py:646
  324.8 1.8 term_step.19
  327.7 2.0 term_last.3
  333.7 1.9 pad_maximum_fusion
  336.6 1.4 convert_add_fusion
  342.2 5.1 %grads.4.refs_9_ = f32[3,512,1024]{2,1,0:T(8,128)} custom-call(bf16[512,2048]{1,0:T(8,128)(2,1)S(1)} %copy-done.3, bf16[3,128,512]{2,1,0:T(8,128)(2,1)S(1)} %copy-done.49, bf16[3,128,512]{2,1,0:T(8,128)(2,1)} %collective-permute-done.33.refs_1_, bf16[3,128,512]{2,1,0:T(8,128)(2,1)} %collective-permute-done.36.refs_2_, ...), custom_call_target="tpu_custom_call", output_to_operand_aliasing={{}: (10, {})} | custom-call | flops 1610612736 | bytes 6291456 | tf_op jit(solution)/shard_map/grads/pallas_call | solution.py:445
  347.5 2.0 collective-permute-start.58
  349.5 3.3 collective-permute-start.57
  352.9 5.7 %grads.5 = f32[3,512,1024]{2,1,0:T(8,128)} custom-call(bf16[512,2048]{1,0:T(8,128)(2,1)S(1)} %copy-done.3, bf16[3,128,512]{2,1,0:T(8,128)(2,1)S(1)} %copy-done.46, bf16[3,128,512]{2,1,0:T(8,128)(2,1)S(1)} %copy-done.13, bf16[3,128,512]{2,1,0:T(8,128)(2,1)S(1)} %copy-done.10, bf16[3,128,512]{2,1,0:T(8,128)(2,1)S(1)} %copy-done.7, ...), custom_call_target="tpu_custom_call", output_to_operand_aliasing={{}: (10, {})} | custom-call | flops 1610612736 | bytes 6291456 | tf_op jit(solution)/shard_map/grads/pallas_call | solution.py:445
  358.6 1.5 collective-permute-done.58
  360.0 1.7 collective-permute-done.57
  (269 shorter events, 89.3 us)
Async XLA Ops:
  5.7 9.1 %collective-permute-start.6 = (bf16[256,256]{1,0:T(8,128)(2,1)S(1)}, bf16[256,256]{1,0:T(8,128)(2,1)S(1)}, u32[]{:S(2)}, u32[]{:S(2)}) collective-permute-start(bf16[256,256]{1,0:T(8,128)(2,1)S(1)} %get-tuple-element.79), channel_id=1, source_target_pairs={{0,7},{2,5},{4,3},{6,1},{7,0},{5,2},{3,4},{1,6},{8,15},{10,13},{12... | collective-permute-start | bytes 393224 | tf_op jit(solution)/shard_map/ppermute | solution.py:561
  10.3 9.7 %collective-permute-start = (bf16[256,256]{1,0:T(8,128)(2,1)S(1)}, bf16[256,256]{1,0:T(8,128)(2,1)S(1)}, u32[]{:S(2)}, u32[]{:S(2)}) collective-permute-start(bf16[256,256]{1,0:T(8,128)(2,1)S(1)} %get-tuple-element.73), channel_id=1, source_target_pairs={{0,2},{2,4},{4,6},{6,7},{7,5},{5,3},{3,1},{1,0},{8,10},{10,12},{12... | collective-permute-start | bytes 393224 | tf_op jit(solution)/shard_map/ppermute | solution.py:561
  14.8 6.9 %collective-permute-start.7 = (bf16[256,256]{1,0:T(8,128)(2,1)S(1)}, bf16[256,256]{1,0:T(8,128)(2,1)S(1)}, u32[]{:S(2)}, u32[]{:S(2)}) collective-permute-start(bf16[256,256]{1,0:T(8,128)(2,1)S(1)} %collective-permute-done.6.mine.mine_far), channel_id=1, source_target_pairs={{0,8},{8,0},{16,24},{24,16},{1,9},{9,1},{17,25},{25,17},{2,10},{10... | collective-permute-start | bytes 393224 | tf_op jit(solution)/shard_map/ppermute | solution.py:564
  14.8 14.6 %collective-permute-start.1 = (bf16[256,256]{1,0:T(8,128)(2,1)S(1)}, bf16[256,256]{1,0:T(8,128)(2,1)S(1)}, u32[]{:S(2)}, u32[]{:S(2)}) collective-permute-start(bf16[256,256]{1,0:T(8,128)(2,1)S(1)} %get-tuple-element.74), channel_id=1, source_target_pairs={{0,1},{2,0},{4,2},{6,4},{7,6},{5,7},{3,5},{1,3},{8,9},{10,8},{12,1... | collective-permute-start | bytes 393224 | tf_op jit(solution)/shard_map/ppermute | solution.py:561
  15.3 14.1 %collective-permute-start.2 = (bf16[256,256]{1,0:T(8,128)(2,1)S(1)}, bf16[256,256]{1,0:T(8,128)(2,1)S(1)}, u32[]{:S(2)}, u32[]{:S(2)}) collective-permute-start(bf16[256,256]{1,0:T(8,128)(2,1)S(1)} %get-tuple-element.75), channel_id=1, source_target_pairs={{0,4},{2,6},{4,7},{6,5},{7,3},{5,1},{3,0},{1,2},{8,12},{10,14},{12... | collective-permute-start | bytes 393224 | tf_op jit(solution)/shard_map/ppermute | solution.py:561
  18.7 15.3 %collective-permute-start.3 = (bf16[256,256]{1,0:T(8,128)(2,1)S(1)}, bf16[256,256]{1,0:T(8,128)(2,1)S(1)}, u32[]{:S(2)}, u32[]{:S(2)}) collective-permute-start(bf16[256,256]{1,0:T(8,128)(2,1)S(1)} %get-tuple-element.76), channel_id=1, source_target_pairs={{0,3},{2,1},{4,0},{6,2},{7,4},{5,6},{3,7},{1,5},{8,11},{10,9},{12,... | collective-permute-start | bytes 393224 | tf_op jit(solution)/shard_map/ppermute | solution.py:561
  19.9 15.2 %collective-permute-start.4 = (bf16[256,256]{1,0:T(8,128)(2,1)S(1)}, bf16[256,256]{1,0:T(8,128)(2,1)S(1)}, u32[]{:S(2)}, u32[]{:S(2)}) collective-permute-start(bf16[256,256]{1,0:T(8,128)(2,1)S(1)} %get-tuple-element.77), channel_id=1, source_target_pairs={{0,6},{2,7},{4,5},{6,3},{7,1},{5,0},{3,2},{1,4},{8,14},{10,15},{12... | collective-permute-start | bytes 393224 | tf_op jit(solution)/shard_map/ppermute | solution.py:561
  21.7 13.4 %collective-permute-start.5 = (bf16[256,256]{1,0:T(8,128)(2,1)S(1)}, bf16[256,256]{1,0:T(8,128)(2,1)S(1)}, u32[]{:S(2)}, u32[]{:S(2)}) collective-permute-start(bf16[256,256]{1,0:T(8,128)(2,1)S(1)} %get-tuple-element.78), channel_id=1, source_target_pairs={{0,5},{2,3},{4,1},{6,0},{7,2},{5,4},{3,6},{1,7},{8,13},{10,11},{12... | collective-permute-start | bytes 393224 | tf_op jit(solution)/shard_map/ppermute | solution.py:561
  35.2 14.4 %collective-permute-start.8 = (bf16[7,256,256]{2,1,0:T(8,128)(2,1)S(1)}, bf16[7,256,256]{2,1,0:T(8,128)(2,1)S(1)}, u32[]{:S(2)}, u32[]{:S(2)}) collective-permute-start(bf16[7,256,256]{2,1,0:T(8,128)(2,1)S(1)} %stack.25.refs_1_.refs_3_.mine), channel_id=1, source_target_pairs={{0,8},{8,0},{16,24},{24,16},{1,9},{9,1},{17,25},{25,17},{2,10},{10... | collective-permute-start | bytes 2752520 | tf_op jit(solution)/shard_map/ppermute | solution.py:564
  35.2 12.1 %collective-permute-start.10 = (bf16[3,128,512]{2,1,0:T(8,128)(2,1)S(1)}, bf16[3,128,512]{2,1,0:T(8,128)(2,1)S(1)}, u32[]{:S(2)}, u32[]{:S(2)}) collective-permute-start(bf16[3,128,512]{2,1,0:T(8,128)(2,1)S(1)} %get-tuple-element.82), channel_id=1, source_target_pairs={{0,1},{2,0},{4,2},{6,4},{7,6},{5,7},{3,5},{1,3},{8,9},{10,8},{12,1... | collective-permute-start | bytes 1179656 | tf_op jit(solution)/shard_map/ppermute | solution.py:561
  38.4 11.2 %collective-permute-start.9 = (bf16[3,128,512]{2,1,0:T(8,128)(2,1)S(1)}, bf16[3,128,512]{2,1,0:T(8,128)(2,1)S(1)}, u32[]{:S(2)}, u32[]{:S(2)}) collective-permute-start(bf16[3,128,512]{2,1,0:T(8,128)(2,1)S(1)} %get-tuple-element.81.refs_7_), channel_id=1, source_target_pairs={{0,2},{2,4},{4,6},{6,7},{7,5},{5,3},{3,1},{1,0},{8,10},{10,12},{12... | collective-permute-start | bytes 1179656 | tf_op jit(solution)/shard_map/ppermute | solution.py:561
  51.6 18.8 %collective-permute-start.11 = (bf16[3,256,512]{2,1,0:T(8,128)(2,1)S(1)}, bf16[3,256,512]{2,1,0:T(8,128)(2,1)S(1)}, u32[]{:S(2)}, u32[]{:S(2)}) collective-permute-start(bf16[3,256,512]{2,1,0:T(8,128)(2,1)S(1)} %get-tuple-element.83), channel_id=1, source_target_pairs={{0,2},{2,4},{4,6},{6,7},{7,5},{5,3},{3,1},{1,0},{8,10},{10,12},{12... | collective-permute-start | bytes 2359304 | tf_op jit(solution)/shard_map/ppermute | solution.py:561
  51.9 18.8 %collective-permute-start.12 = (bf16[3,256,512]{2,1,0:T(8,128)(2,1)S(1)}, bf16[3,256,512]{2,1,0:T(8,128)(2,1)S(1)}, u32[]{:S(2)}, u32[]{:S(2)}) collective-permute-start(bf16[3,256,512]{2,1,0:T(8,128)(2,1)S(1)} %get-tuple-element.84), channel_id=1, source_target_pairs={{0,1},{2,0},{4,2},{6,4},{7,6},{5,7},{3,5},{1,3},{8,9},{10,8},{12,1... | collective-permute-start | bytes 2359304 | tf_op jit(solution)/shard_map/ppermute | solution.py:561
  72.8 33.3 %collective-permute-start.13 = (bf16[3,256,512]{2,1,0:T(8,128)(2,1)S(1)}, bf16[3,256,512]{2,1,0:T(8,128)(2,1)S(1)}, u32[]{:S(2)}, u32[]{:S(2)}) collective-permute-start(bf16[3,256,512]{2,1,0:T(8,128)(2,1)S(1)} %get-tuple-element.85), channel_id=1, source_target_pairs={{0,2},{2,4},{4,6},{6,7},{7,5},{5,3},{3,1},{1,0},{8,10},{10,12},{12... | collective-permute-start | bytes 2359304 | tf_op jit(solution)/shard_map/ppermute | solution.py:561
  74.5 31.6 %collective-permute-start.14 = (bf16[3,256,512]{2,1,0:T(8,128)(2,1)S(1)}, bf16[3,256,512]{2,1,0:T(8,128)(2,1)S(1)}, u32[]{:S(2)}, u32[]{:S(2)}) collective-permute-start(bf16[3,256,512]{2,1,0:T(8,128)(2,1)S(1)} %get-tuple-element.86), channel_id=1, source_target_pairs={{0,1},{2,0},{4,2},{6,4},{7,6},{5,7},{3,5},{1,3},{8,9},{10,8},{12,1... | collective-permute-start | bytes 2359304 | tf_op jit(solution)/shard_map/ppermute | solution.py:561
  74.9 24.3 %collective-permute-start.17 = (bf16[3,128,512]{2,1,0:T(8,128)(2,1)S(1)}, bf16[3,128,512]{2,1,0:T(8,128)(2,1)S(1)}, u32[]{:S(2)}, u32[]{:S(2)}) collective-permute-start(bf16[3,128,512]{2,1,0:T(8,128)(2,1)S(1)} %get-tuple-element.90), channel_id=1, source_target_pairs={{0,2},{2,4},{4,6},{6,7},{7,5},{5,3},{3,1},{1,0},{8,10},{10,12},{12... | collective-permute-start | bytes 1179656 | tf_op jit(solution)/shard_map/ppermute | solution.py:561
  76.6 24.2 %collective-permute-start.18 = (bf16[3,128,512]{2,1,0:T(8,128)(2,1)S(1)}, bf16[3,128,512]{2,1,0:T(8,128)(2,1)S(1)}, u32[]{:S(2)}, u32[]{:S(2)}) collective-permute-start(bf16[3,128,512]{2,1,0:T(8,128)(2,1)S(1)} %get-tuple-element.91), channel_id=1, source_target_pairs={{0,1},{2,0},{4,2},{6,4},{7,6},{5,7},{3,5},{1,3},{8,9},{10,8},{12,1... | collective-permute-start | bytes 1179656 | tf_op jit(solution)/shard_map/ppermute | solution.py:561
  102.9 20.5 %collective-permute-start.19 = (bf16[3,256,512]{2,1,0:T(8,128)(2,1)S(1)}, bf16[3,256,512]{2,1,0:T(8,128)(2,1)S(1)}, u32[]{:S(2)}, u32[]{:S(2)}) collective-permute-start(bf16[3,256,512]{2,1,0:T(8,128)(2,1)S(1)} %get-tuple-element.92), channel_id=1, source_target_pairs={{0,2},{2,4},{4,6},{6,7},{7,5},{5,3},{3,1},{1,0},{8,10},{10,12},{12... | collective-permute-start | bytes 2359304 | tf_op jit(solution)/shard_map/ppermute | solution.py:561
  104.2 20.5 %collective-permute-start.20 = (bf16[3,256,512]{2,1,0:T(8,128)(2,1)S(1)}, bf16[3,256,512]{2,1,0:T(8,128)(2,1)S(1)}, u32[]{:S(2)}, u32[]{:S(2)}) collective-permute-start(bf16[3,256,512]{2,1,0:T(8,128)(2,1)S(1)} %get-tuple-element.93), channel_id=1, source_target_pairs={{0,1},{2,0},{4,2},{6,4},{7,6},{5,7},{3,5},{1,3},{8,9},{10,8},{12,1... | collective-permute-start | bytes 2359304 | tf_op jit(solution)/shard_map/ppermute | solution.py:561
  106.1 52.3 %copy-start.1 = (bf16[512,2048]{1,0:T(8,128)(2,1)}, bf16[512,2048]{1,0:T(8,128)(2,1)S(1)}, u32[]{:S(2)}) copy-start(bf16[512,2048]{1,0:T(8,128)(2,1)S(1)} %turn.1.refs_9_.turned_ref) | copy-start | bytes 6291460
  108.2 32.0 %collective-permute-start.15 = (bf16[3,256,512]{2,1,0:T(8,128)(2,1)S(1)}, bf16[3,256,512]{2,1,0:T(8,128)(2,1)S(1)}, u32[]{:S(2)}, u32[]{:S(2)}) collective-permute-start(bf16[3,256,512]{2,1,0:T(8,128)(2,1)S(1)} %get-tuple-element.87), channel_id=1, source_target_pairs={{0,2},{2,4},{4,6},{6,7},{7,5},{5,3},{3,1},{1,0},{8,10},{10,12},{12... | collective-permute-start | bytes 2359304 | tf_op jit(solution)/shard_map/ppermute | solution.py:561
  109.6 32.0 %collective-permute-start.16 = (bf16[3,256,512]{2,1,0:T(8,128)(2,1)S(1)}, bf16[3,256,512]{2,1,0:T(8,128)(2,1)S(1)}, u32[]{:S(2)}, u32[]{:S(2)}) collective-permute-start(bf16[3,256,512]{2,1,0:T(8,128)(2,1)S(1)} %get-tuple-element.88), channel_id=1, source_target_pairs={{0,1},{2,0},{4,2},{6,4},{7,6},{5,7},{3,5},{1,3},{8,9},{10,8},{12,1... | collective-permute-start | bytes 2359304 | tf_op jit(solution)/shard_map/ppermute | solution.py:561
  110.9 30.7 %copy-start.43 = (bf16[256,1024]{1,0:T(8,128)(2,1)S(1)}, bf16[256,1024]{1,0:T(8,128)(2,1)}, u32[]{:S(2)}) copy-start(bf16[256,1024]{1,0:T(8,128)(2,1)} %d_out.3) | copy-start | bytes 1572868
  126.8 30.3 %collective-permute-start.21 = (bf16[3,256,512]{2,1,0:T(8,128)(2,1)S(1)}, bf16[3,256,512]{2,1,0:T(8,128)(2,1)S(1)}, u32[]{:S(2)}, u32[]{:S(2)}) collective-permute-start(bf16[3,256,512]{2,1,0:T(8,128)(2,1)S(1)} %get-tuple-element.94), channel_id=1, source_target_pairs={{0,2},{2,4},{4,6},{6,7},{7,5},{5,3},{3,1},{1,0},{8,10},{10,12},{12... | collective-permute-start | bytes 2359304 | tf_op jit(solution)/shard_map/ppermute | solution.py:561
  127.9 30.5 %collective-permute-start.22 = (bf16[3,256,512]{2,1,0:T(8,128)(2,1)S(1)}, bf16[3,256,512]{2,1,0:T(8,128)(2,1)S(1)}, u32[]{:S(2)}, u32[]{:S(2)}) collective-permute-start(bf16[3,256,512]{2,1,0:T(8,128)(2,1)S(1)} %get-tuple-element.95), channel_id=1, source_target_pairs={{0,1},{2,0},{4,2},{6,4},{7,6},{5,7},{3,5},{1,3},{8,9},{10,8},{12,1... | collective-permute-start | bytes 2359304 | tf_op jit(solution)/shard_map/ppermute | solution.py:561
  149.5 25.8 %collective-permute-start.28 = (bf16[3,256,512]{2,1,0:T(8,128)(2,1)S(1)}, bf16[3,256,512]{2,1,0:T(8,128)(2,1)S(1)}, u32[]{:S(2)}, u32[]{:S(2)}) collective-permute-start(bf16[3,256,512]{2,1,0:T(8,128)(2,1)S(1)} %get-tuple-element.101.refs_0_), channel_id=1, source_target_pairs={{0,1},{2,0},{4,2},{6,4},{7,6},{5,7},{3,5},{1,3},{8,9},{10,8},{12,1... | collective-permute-start | bytes 2359304 | tf_op jit(solution)/shard_map/ppermute | solution.py:561
  150.2 25.8 %collective-permute-start.25 = (bf16[3,256,512]{2,1,0:T(8,128)(2,1)S(1)}, bf16[3,256,512]{2,1,0:T(8,128)(2,1)S(1)}, u32[]{:S(2)}, u32[]{:S(2)}) collective-permute-start(bf16[3,256,512]{2,1,0:T(8,128)(2,1)S(1)} %get-tuple-element.101.refs_0_), channel_id=1, source_target_pairs={{0,2},{2,4},{4,6},{6,7},{7,5},{5,3},{3,1},{1,0},{8,10},{10,12},{12... | collective-permute-start | bytes 2359304 | tf_op jit(solution)/shard_map/ppermute | solution.py:561
  160.5 30.3 %collective-permute-start.23 = (bf16[3,256,512]{2,1,0:T(8,128)(2,1)S(1)}, bf16[3,256,512]{2,1,0:T(8,128)(2,1)S(1)}, u32[]{:S(2)}, u32[]{:S(2)}) collective-permute-start(bf16[3,256,512]{2,1,0:T(8,128)(2,1)S(1)} %get-tuple-element.96), channel_id=1, source_target_pairs={{0,2},{2,4},{4,6},{6,7},{7,5},{5,3},{3,1},{1,0},{8,10},{10,12},{12... | collective-permute-start | bytes 2359304 | tf_op jit(solution)/shard_map/ppermute | solution.py:561
  161.7 30.5 %collective-permute-start.24 = (bf16[3,256,512]{2,1,0:T(8,128)(2,1)S(1)}, bf16[3,256,512]{2,1,0:T(8,128)(2,1)S(1)}, u32[]{:S(2)}, u32[]{:S(2)}) collective-permute-start(bf16[3,256,512]{2,1,0:T(8,128)(2,1)S(1)} %get-tuple-element.97), channel_id=1, source_target_pairs={{0,1},{2,0},{4,2},{6,4},{7,6},{5,7},{3,5},{1,3},{8,9},{10,8},{12,1... | collective-permute-start | bytes 2359304 | tf_op jit(solution)/shard_map/ppermute | solution.py:561
  175.3 24.1 %copy-start.22 = (bf16[3,256,512]{2,1,0:T(8,128)(2,1)}, bf16[3,256,512]{2,1,0:T(8,128)(2,1)S(1)}, u32[]{:S(2)}) copy-start(bf16[3,256,512]{2,1,0:T(8,128)(2,1)S(1)} %collective-permute-done.28.refs_2_) | copy-start | bytes 2359300
  175.3 33.8 %collective-permute-start.29 = (bf16[3,256,512]{2,1,0:T(8,128)(2,1)S(1)}, bf16[3,256,512]{2,1,0:T(8,128)(2,1)}, u32[]{:S(2)}, u32[]{:S(2)}) collective-permute-start(bf16[3,256,512]{2,1,0:T(8,128)(2,1)S(1)} %collective-permute-done.28.refs_2_), channel_id=1, source_target_pairs={{0,1},{2,0},{4,2},{6,4},{7,6},{5,7},{3,5},{1,3},{8,9},{10,8},{12,1... | collective-permute-start | bytes 2359304 | tf_op jit(solution)/shard_map/ppermute | solution.py:561
  176.0 23.4 %copy-start.25 = (bf16[3,256,512]{2,1,0:T(8,128)(2,1)}, bf16[3,256,512]{2,1,0:T(8,128)(2,1)S(1)}, u32[]{:S(2)}) copy-start(bf16[3,256,512]{2,1,0:T(8,128)(2,1)S(1)} %collective-permute-done.25.refs_1_) | copy-start | bytes 2359300
  176.0 33.8 %collective-permute-start.26 = (bf16[3,256,512]{2,1,0:T(8,128)(2,1)S(1)}, bf16[3,256,512]{2,1,0:T(8,128)(2,1)}, u32[]{:S(2)}, u32[]{:S(2)}) collective-permute-start(bf16[3,256,512]{2,1,0:T(8,128)(2,1)S(1)} %collective-permute-done.25.refs_1_), channel_id=1, source_target_pairs={{0,2},{2,4},{4,6},{6,7},{7,5},{5,3},{3,1},{1,0},{8,10},{10,12},{12... | collective-permute-start | bytes 2359304 | tf_op jit(solution)/shard_map/ppermute | solution.py:561
  201.5 42.4 %copy-start.47 = (bf16[3,128,512]{2,1,0:T(8,128)(2,1)}, bf16[3,128,512]{2,1,0:T(8,128)(2,1)S(1)}, u32[]{:S(2)}) copy-start(bf16[3,128,512]{2,1,0:T(8,128)(2,1)S(1)} %get-tuple-element.105.refs_0_) | copy-start | bytes 1179652
  201.5 16.0 %collective-permute-start.36 = (bf16[3,128,512]{2,1,0:T(8,128)(2,1)S(1)}, bf16[3,128,512]{2,1,0:T(8,128)(2,1)}, u32[]{:S(2)}, u32[]{:S(2)}) collective-permute-start(bf16[3,128,512]{2,1,0:T(8,128)(2,1)S(1)} %get-tuple-element.105.refs_0_), channel_id=1, source_target_pairs={{0,1},{2,0},{4,2},{6,4},{7,6},{5,7},{3,5},{1,3},{8,9},{10,8},{12,1... | collective-permute-start | bytes 1179656 | tf_op jit(solution)/shard_map/ppermute | solution.py:561
  202.2 16.0 %collective-permute-start.33 = (bf16[3,128,512]{2,1,0:T(8,128)(2,1)S(1)}, bf16[3,128,512]{2,1,0:T(8,128)(2,1)}, u32[]{:S(2)}, u32[]{:S(2)}) collective-permute-start(bf16[3,128,512]{2,1,0:T(8,128)(2,1)S(1)} %get-tuple-element.105.refs_0_), channel_id=1, source_target_pairs={{0,2},{2,4},{4,6},{6,7},{7,5},{5,3},{3,1},{1,0},{8,10},{10,12},{12... | collective-permute-start | bytes 1179656 | tf_op jit(solution)/shard_map/ppermute | solution.py:561
  209.1 35.7 %collective-permute-start.30 = (bf16[3,256,512]{2,1,0:T(8,128)(2,1)}, bf16[3,256,512]{2,1,0:T(8,128)(2,1)}, u32[]{:S(2)}, u32[]{:S(2)}) collective-permute-start(bf16[3,256,512]{2,1,0:T(8,128)(2,1)} %collective-permute-done.29.refs_1_.refs_4_), channel_id=1, source_target_pairs={{0,1},{2,0},{4,2},{6,4},{7,6},{5,7},{3,5},{1,3},{8,9},{10,8},{12,1... | collective-permute-start | bytes 2359304 | tf_op jit(solution)/shard_map/ppermute | solution.py:561
  209.8 36.2 %collective-permute-start.27 = (bf16[3,256,512]{2,1,0:T(8,128)(2,1)}, bf16[3,256,512]{2,1,0:T(8,128)(2,1)}, u32[]{:S(2)}, u32[]{:S(2)}) collective-permute-start(bf16[3,256,512]{2,1,0:T(8,128)(2,1)} %collective-permute-done.26.refs_0_.refs_3_), channel_id=1, source_target_pairs={{0,2},{2,4},{4,6},{6,7},{7,5},{5,3},{3,1},{1,0},{8,10},{10,12},{12... | collective-permute-start | bytes 2359304 | tf_op jit(solution)/shard_map/ppermute | solution.py:561
  217.5 25.3 %collective-permute-start.37 = (bf16[3,128,512]{2,1,0:T(8,128)(2,1)}, bf16[3,128,512]{2,1,0:T(8,128)(2,1)}, u32[]{:S(2)}, u32[]{:S(2)}) collective-permute-start(bf16[3,128,512]{2,1,0:T(8,128)(2,1)} %collective-permute-done.36.refs_2_), channel_id=1, source_target_pairs={{0,1},{2,0},{4,2},{6,4},{7,6},{5,7},{3,5},{1,3},{8,9},{10,8},{12,1... | collective-permute-start | bytes 1179656 | tf_op jit(solution)/shard_map/ppermute | solution.py:561
  218.2 25.7 %collective-permute-start.34 = (bf16[3,128,512]{2,1,0:T(8,128)(2,1)}, bf16[3,128,512]{2,1,0:T(8,128)(2,1)}, u32[]{:S(2)}, u32[]{:S(2)}) collective-permute-start(bf16[3,128,512]{2,1,0:T(8,128)(2,1)} %collective-permute-done.33.refs_1_), channel_id=1, source_target_pairs={{0,2},{2,4},{4,6},{6,7},{7,5},{5,3},{3,1},{1,0},{8,10},{10,12},{12... | collective-permute-start | bytes 1179656 | tf_op jit(solution)/shard_map/ppermute | solution.py:561
  222.4 1.6 collective-permute-start.39
  224.9 5.6 %collective-permute-start.40 = (f32[256,1]{1,0:T(8,128)S(1)}, f32[256,1]{1,0:T(8,128)S(1)}, u32[]{:S(2)}, u32[]{:S(2)}) collective-permute-start(f32[256,1]{1,0:T(8,128)S(1)} %add.106), channel_id=1, source_target_pairs={{0,16},{8,24},{16,0},{24,8},{1,17},{9,25},{17,1},{25,9},{2,18},{10... | collective-permute-start | bytes 3080 | tf_op jit(solution)/shard_map/ppermute | solution.py:564
  230.5 20.6 %collective-permute-start.42 = (bf16[3,128,512]{2,1,0:T(8,128)(2,1)}, bf16[3,128,512]{2,1,0:T(8,128)(2,1)S(1)}, u32[]{:S(2)}, u32[]{:S(2)}) collective-permute-start(bf16[3,128,512]{2,1,0:T(8,128)(2,1)} %copy-done.44), channel_id=1, source_target_pairs={{0,1},{2,0},{4,2},{6,4},{7,6},{5,7},{3,5},{1,3},{8,9},{10,8},{12,1... | collective-permute-start | bytes 1179656 | tf_op jit(solution)/shard_map/ppermute | solution.py:561
  242.8 16.3 %collective-permute-start.41 = (bf16[3,128,512]{2,1,0:T(8,128)(2,1)}, bf16[3,128,512]{2,1,0:T(8,128)(2,1)S(1)}, u32[]{:S(2)}, u32[]{:S(2)}) collective-permute-start(bf16[3,128,512]{2,1,0:T(8,128)(2,1)} %copy-done.44), channel_id=1, source_target_pairs={{0,2},{2,4},{4,6},{6,7},{7,5},{5,3},{3,1},{1,0},{8,10},{10,12},{12... | collective-permute-start | bytes 1179656 | tf_op jit(solution)/shard_map/ppermute | solution.py:561
  243.9 15.6 %collective-permute-start.38 = (bf16[3,128,512]{2,1,0:T(8,128)(2,1)}, bf16[3,128,512]{2,1,0:T(8,128)(2,1)S(1)}, u32[]{:S(2)}, u32[]{:S(2)}) collective-permute-start(bf16[3,128,512]{2,1,0:T(8,128)(2,1)} %collective-permute-done.37.refs_1_.refs_4_), channel_id=1, source_target_pairs={{0,1},{2,0},{4,2},{6,4},{7,6},{5,7},{3,5},{1,3},{8,9},{10,8},{12,1... | collective-permute-start | bytes 1179656 | tf_op jit(solution)/shard_map/ppermute | solution.py:561
  244.8 16.2 %collective-permute-start.35 = (bf16[3,128,512]{2,1,0:T(8,128)(2,1)}, bf16[3,128,512]{2,1,0:T(8,128)(2,1)S(1)}, u32[]{:S(2)}, u32[]{:S(2)}) collective-permute-start(bf16[3,128,512]{2,1,0:T(8,128)(2,1)} %collective-permute-done.34.refs_0_.refs_3_), channel_id=1, source_target_pairs={{0,2},{2,4},{4,6},{6,7},{7,5},{5,3},{3,1},{1,0},{8,10},{10,12},{12... | collective-permute-start | bytes 1179656 | tf_op jit(solution)/shard_map/ppermute | solution.py:561
  247.5 23.9 %collective-permute-start.31 = (bf16[3,128,512]{2,1,0:T(8,128)(2,1)S(1)}, bf16[3,128,512]{2,1,0:T(8,128)(2,1)S(1)}, u32[]{:S(2)}, u32[]{:S(2)}) collective-permute-start(bf16[3,128,512]{2,1,0:T(8,128)(2,1)S(1)} %get-tuple-element.102), channel_id=1, source_target_pairs={{0,2},{2,4},{4,6},{6,7},{7,5},{5,3},{3,1},{1,0},{8,10},{10,12},{12... | collective-permute-start | bytes 1179656 | tf_op jit(solution)/shard_map/ppermute | solution.py:561
  251.1 20.3 %collective-permute-start.32 = (bf16[3,128,512]{2,1,0:T(8,128)(2,1)S(1)}, bf16[3,128,512]{2,1,0:T(8,128)(2,1)S(1)}, u32[]{:S(2)}, u32[]{:S(2)}) collective-permute-start(bf16[3,128,512]{2,1,0:T(8,128)(2,1)S(1)} %get-tuple-element.103), channel_id=1, source_target_pairs={{0,1},{2,0},{4,2},{6,4},{7,6},{5,7},{3,5},{1,3},{8,9},{10,8},{12,1... | collective-permute-start | bytes 1179656 | tf_op jit(solution)/shard_map/ppermute | solution.py:561
  261.1 11.6 %collective-permute-start.43 = (bf16[3,64,512]{2,1,0:T(8,128)(2,1)S(1)}, bf16[3,64,512]{2,1,0:T(8,128)(2,1)S(1)}, u32[]{:S(2)}, u32[]{:S(2)}) collective-permute-start(bf16[3,64,512]{2,1,0:T(8,128)(2,1)S(1)} %get-tuple-element.109), channel_id=1, source_target_pairs={{0,2},{2,4},{4,6},{6,7},{7,5},{5,3},{3,1},{1,0},{8,10},{10,12},{12... | collective-permute-start | bytes 589832 | tf_op jit(solution)/shard_map/ppermute | solution.py:561
  262.2 10.5 %collective-permute-start.44 = (bf16[3,64,512]{2,1,0:T(8,128)(2,1)S(1)}, bf16[3,64,512]{2,1,0:T(8,128)(2,1)S(1)}, u32[]{:S(2)}, u32[]{:S(2)}) collective-permute-start(bf16[3,64,512]{2,1,0:T(8,128)(2,1)S(1)} %get-tuple-element.110), channel_id=1, source_target_pairs={{0,1},{2,0},{4,2},{6,4},{7,6},{5,7},{3,5},{1,3},{8,9},{10,8},{12,1... | collective-permute-start | bytes 589832 | tf_op jit(solution)/shard_map/ppermute | solution.py:561
  275.7 2.3 collective-permute-start.45
  275.7 15.6 %collective-permute-start.50 = (bf16[3,128,512]{2,1,0:T(8,128)(2,1)}, bf16[3,128,512]{2,1,0:T(8,128)(2,1)S(1)}, u32[]{:S(2)}, u32[]{:S(2)}) collective-permute-start(bf16[3,128,512]{2,1,0:T(8,128)(2,1)} %copy-done.8), channel_id=1, source_target_pairs={{0,1},{2,0},{4,2},{6,4},{7,6},{5,7},{3,5},{1,3},{8,9},{10,8},{12,1... | collective-permute-start | bytes 1179656 | tf_op jit(solution)/shard_map/ppermute | solution.py:561
  276.7 14.6 %collective-permute-start.49 = (bf16[3,128,512]{2,1,0:T(8,128)(2,1)}, bf16[3,128,512]{2,1,0:T(8,128)(2,1)S(1)}, u32[]{:S(2)}, u32[]{:S(2)}) collective-permute-start(bf16[3,128,512]{2,1,0:T(8,128)(2,1)} %copy-done.11), channel_id=1, source_target_pairs={{0,2},{2,4},{4,6},{6,7},{7,5},{5,3},{3,1},{1,0},{8,10},{10,12},{12... | collective-permute-start | bytes 1179656 | tf_op jit(solution)/shard_map/ppermute | solution.py:561
  280.3 16.9 %collective-permute-start.46 = (bf16[1,2,128,512]{3,2,1,0:T(8,128)(2,1)}, bf16[1,2,128,512]{3,2,1,0:T(8,128)(2,1)}, u32[]{:S(2)}, u32[]{:S(2)}) collective-permute-start(bf16[1,2,128,512]{3,2,1,0:T(8,128)(2,1)} %fusion.10), channel_id=1, source_target_pairs={{0,16},{8,24},{16,0},{24,8},{1,17},{9,25},{17,1},{25,9},{2,18},{10... | collective-permute-start | bytes 786440 | tf_op jit(solution)/shard_map/ppermute | solution.py:564
  295.2 11.2 %collective-permute-start.51 = (bf16[3,128,512]{2,1,0:T(8,128)(2,1)}, bf16[3,128,512]{2,1,0:T(8,128)(2,1)}, u32[]{:S(2)}, u32[]{:S(2)}) collective-permute-start(bf16[3,128,512]{2,1,0:T(8,128)(2,1)} %get-tuple-element.128), channel_id=1, source_target_pairs={{0,2},{2,4},{4,6},{6,7},{7,5},{5,3},{3,1},{1,0},{8,10},{10,12},{12... | collective-permute-start | bytes 1179656 | tf_op jit(solution)/shard_map/ppermute | solution.py:561
  296.3 10.9 %collective-permute-start.52 = (bf16[3,128,512]{2,1,0:T(8,128)(2,1)}, bf16[3,128,512]{2,1,0:T(8,128)(2,1)}, u32[]{:S(2)}, u32[]{:S(2)}) collective-permute-start(bf16[3,128,512]{2,1,0:T(8,128)(2,1)} %get-tuple-element.129), channel_id=1, source_target_pairs={{0,1},{2,0},{4,2},{6,4},{7,6},{5,7},{3,5},{1,3},{8,9},{10,8},{12,1... | collective-permute-start | bytes 1179656 | tf_op jit(solution)/shard_map/ppermute | solution.py:561
  308.4 19.3 %collective-permute-start.53 = (bf16[3,64,512]{2,1,0:T(8,128)(2,1)S(1)}, bf16[3,64,512]{2,1,0:T(8,128)(2,1)S(1)}, u32[]{:S(2)}, u32[]{:S(2)}) collective-permute-start(bf16[3,64,512]{2,1,0:T(8,128)(2,1)S(1)} %get-tuple-element.130), channel_id=1, source_target_pairs={{0,2},{2,4},{4,6},{6,7},{7,5},{5,3},{3,1},{1,0},{8,10},{10,12},{12... | collective-permute-start | bytes 589832 | tf_op jit(solution)/shard_map/ppermute | solution.py:561
  309.2 18.4 %collective-permute-start.54 = (bf16[3,64,512]{2,1,0:T(8,128)(2,1)S(1)}, bf16[3,64,512]{2,1,0:T(8,128)(2,1)S(1)}, u32[]{:S(2)}, u32[]{:S(2)}) collective-permute-start(bf16[3,64,512]{2,1,0:T(8,128)(2,1)S(1)} %get-tuple-element.131), channel_id=1, source_target_pairs={{0,1},{2,0},{4,2},{6,4},{7,6},{5,7},{3,5},{1,3},{8,9},{10,8},{12,1... | collective-permute-start | bytes 589832 | tf_op jit(solution)/shard_map/ppermute | solution.py:561
  310.5 16.1 %collective-permute-start.48 = (bf16[128,512]{1,0:T(8,128)(2,1)S(1)}, bf16[128,512]{1,0:T(8,128)(2,1)S(1)}, u32[]{:S(2)}, u32[]{:S(2)}) collective-permute-start(bf16[128,512]{1,0:T(8,128)(2,1)S(1)} %get-tuple-element.155), channel_id=1, source_target_pairs={{0,1},{1,0},{2,9},{3,8},{4,17},{5,16},{6,25},{7,24},{8,3},{9,2},{1... | collective-permute-start | bytes 393224 | tf_op jit(solution)/shard_map/ppermute | solution.py:646
  312.5 15.2 %collective-permute-start.47 = (bf16[128,512]{1,0:T(8,128)(2,1)S(1)}, bf16[128,512]{1,0:T(8,128)(2,1)S(1)}, u32[]{:S(2)}, u32[]{:S(2)}) collective-permute-start(bf16[128,512]{1,0:T(8,128)(2,1)S(1)} %get-tuple-element.156), channel_id=1, source_target_pairs={{0,0},{1,1},{2,8},{3,9},{4,16},{5,17},{6,24},{7,25},{8,2},{9,3},{1... | collective-permute-start | bytes 393224 | tf_op jit(solution)/shard_map/ppermute | solution.py:646
  330.7 5.9 %collective-permute-start.55 = (bf16[4,128,512]{2,1,0:T(8,128)(2,1)}, bf16[4,128,512]{2,1,0:T(8,128)(2,1)S(1)}, u32[]{:S(2)}, u32[]{:S(2)}) collective-permute-start(bf16[4,128,512]{2,1,0:T(8,128)(2,1)} %get-tuple-element.140), channel_id=1, source_target_pairs={{0,8},{8,0},{16,24},{24,16},{1,9},{9,1},{17,25},{25,17},{2,10},{10... | collective-permute-start | bytes 1572872 | tf_op jit(solution)/shard_map/ppermute | solution.py:564
  338.1 9.3 %collective-permute-start.56 = (bf16[1,2,128,512]{3,2,1,0:T(8,128)(2,1)S(1)}, bf16[1,2,128,512]{3,2,1,0:T(8,128)(2,1)S(1)}, u32[]{:S(2)}, u32[]{:S(2)}) collective-permute-start(bf16[1,2,128,512]{3,2,1,0:T(8,128)(2,1)S(1)} %fusion.11), channel_id=1, source_target_pairs={{0,16},{8,24},{16,0},{24,8},{1,17},{9,25},{17,1},{25,9},{2,18},{10... | collective-permute-start | bytes 786440 | tf_op jit(solution)/shard_map/ppermute | solution.py:564
  347.5 12.5 %collective-permute-start.58 = (bf16[128,512]{1,0:T(8,128)(2,1)S(1)}, bf16[128,512]{1,0:T(8,128)(2,1)S(1)}, u32[]{:S(2)}, u32[]{:S(2)}) collective-permute-start(bf16[128,512]{1,0:T(8,128)(2,1)S(1)} %get-tuple-element.153), channel_id=1, source_target_pairs={{0,1},{1,0},{2,9},{3,8},{4,17},{5,16},{6,25},{7,24},{8,3},{9,2},{1... | collective-permute-start | bytes 393224 | tf_op jit(solution)/shard_map/ppermute | solution.py:646
  349.5 12.3 %collective-permute-start.57 = (bf16[128,512]{1,0:T(8,128)(2,1)S(1)}, bf16[128,512]{1,0:T(8,128)(2,1)S(1)}, u32[]{:S(2)}, u32[]{:S(2)}) collective-permute-start(bf16[128,512]{1,0:T(8,128)(2,1)S(1)} %get-tuple-element.154), channel_id=1, source_target_pairs={{0,0},{1,1},{2,8},{3,9},{4,16},{5,17},{6,24},{7,25},{8,2},{9,3},{1... | collective-permute-start | bytes 393224 | tf_op jit(solution)/shard_map/ppermute | solution.py:646
  (72 other events, 339.3 us)

commit v6 on v5

--- a/solution.py
+++ b/solution.py
@@ -11,11 +11,13 @@
 
 HEAD_DIM = 128
 NORM_EPS = 1e-05
-VMEM = 24 * 1024 * 1024
-
-
-def params():
-    return pltpu.CompilerParams(dimension_semantics=("arbitrary",), vmem_limit_bytes=VMEM)
+MIB = 1024 * 1024
+
+
+def params(limit):
+    return pltpu.CompilerParams(
+        dimension_semantics=("arbitrary",), vmem_limit_bytes=limit * MIB
+    )
 
 
 def tied(kernel, inputs, ties):
@@ -84,6 +86,8 @@
                 + seqs
                 + [owner_ % 2 ^ node % 2 for owner_ in owner]
                 + [(o // 2) * group + seq % group for o, seq in zip(owner, seqs)]
+                + [node >> level & 1 for level in range(1, nodes.bit_length() - 1)]
+                + [(here + turn) % group for turn in range(group)]
             )
     return np.array(rows, np.int32)
 
@@ -117,7 +121,7 @@
             jax.ShapeDtypeStruct((3, depth, columns), jnp.bfloat16),
             jax.ShapeDtypeStruct((3, columns, depth), jnp.bfloat16),
         ],
-        compiler_params=params(),
+        compiler_params=params(20),
         cost_estimate=cost(3 * depth * columns, 18 * depth * columns),
         name="scaled_weights",
     )(w_quant, w_scale)
@@ -156,7 +160,7 @@
         ),
         out_shape=[jax.ShapeDtypeStruct((length, part), jnp.bfloat16)] * size
         + [jax.ShapeDtypeStruct((length, 128), jnp.float32)],
-        compiler_params=params(),
+        compiler_params=params(12),
         cost_estimate=cost(8 * length * width, 4 * length * width),
         name="normed_blocks",
     )(idx, tokens, gain)
@@ -177,31 +181,30 @@
         in_specs=[block] * count + tie_specs(ties),
         out_specs=pl.BlockSpec((count, *shape), lambda i: (0, 0, 0)),
         out_shape=jax.ShapeDtypeStruct((count, *shape), blocks[0].dtype),
-        compiler_params=params(),
+        compiler_params=params(10),
         cost_estimate=cost(0, 4 * count * shape[0] * shape[1]),
         name="stack",
     )(*blocks, *ties)
 
 
-def pass_kernel(right, left, right_out, left_out):
-    rows, sent = right.shape[1], right_out.shape[1]
-    right_out[...] = right[:, :sent]
-    left_out[...] = left[:, rows - sent :]
-
-
-def pass_on(right, left, halve, ties):
+def halve_kernel(right, left, right_out, left_out):
+    half = right_out.shape[1]
+    right_out[...] = right[:, :half]
+    left_out[...] = left[:, half:]
+
+
+def halve(right, left, ties):
     _, rows, wide = right.shape
-    sent = rows // 2 if halve else rows
-    result = jax.ShapeDtypeStruct((3, sent, wide), right.dtype)
-    return pl.pallas_call(
-        tied(pass_kernel, 2, len(ties)),
-        grid=(1,),
-        in_specs=[pl.BlockSpec(right.shape, lambda i: (0, 0, 0))] * 2 + tie_specs(ties),
-        out_specs=[pl.BlockSpec(result.shape, lambda i: (0, 0, 0))] * 2,
+    result = jax.ShapeDtypeStruct((3, rows // 2, wide), right.dtype)
+    whole = pl.BlockSpec(memory_space=pltpu.VMEM)
+    return pl.pallas_call(
+        tied(halve_kernel, 2, len(ties)),
+        in_specs=[whole, whole] + tie_specs(ties),
+        out_specs=[whole, whole],
         out_shape=[result, result],
-        compiler_params=params(),
-        cost_estimate=cost(0, 12 * sent * wide),
-        name="pass_on",
+        compiler_params=pltpu.CompilerParams(vmem_limit_bytes=4 * MIB),
+        cost_estimate=cost(0, 6 * rows * wide),
+        name="halve",
     )(right, left, *ties)
 
 
@@ -230,7 +233,7 @@
             out_specs=pl.BlockSpec(shape, lambda i, idx: (0, 0)),
         ),
         out_shape=jax.ShapeDtypeStruct(shape, jnp.bfloat16),
-        compiler_params=params(),
+        compiler_params=params(12),
         cost_estimate=cost(2 * count * length * part, 8 * count * length * part),
         name="turn",
     )(idx, mine, other, mine_far, other_far)
@@ -282,7 +285,7 @@
             out_specs=[pl.BlockSpec((1, half, wide), lambda m, idx: (m, 0, 0))] * 4,
         ),
         out_shape=[result] * 4,
-        compiler_params=params(),
+        compiler_params=params(12),
         cost_estimate=cost(12 * length * part * columns, 16 * part * columns),
         name="sum_first",
     )(idx, mine, other, weights, weights)
@@ -312,7 +315,7 @@
             out_specs=[pl.BlockSpec((1, length, wide), lambda m, idx: (m, 0, 0))] * 2,
         ),
         out_shape=[whole, whole],
-        compiler_params=params(),
+        compiler_params=params(12),
         cost_estimate=cost(24 * length * part * wide, 24 * part * wide),
         name="sum_step",
     )(idx, mine, other, mine, other, weights, weights, from_left, from_right, *ties)
@@ -320,7 +323,7 @@
 
 def attention_kernel(
     idx, mine, other, weight, weight_other, from_left, from_right, d_out, cosine, sine,
-    output, dots, *pres,
+    output, dots, pre,
 ):
     length = mine.shape[1]
     proj = [
@@ -356,12 +359,9 @@
     d_key = mm_tn(d_scores, query).astype(jnp.bfloat16).astype(jnp.float32)
     pre_query = rotate(d_query, -sin).astype(jnp.bfloat16)
     pre_key = rotate(d_key, -sin).astype(jnp.bfloat16)
-    rows = length // len(pres)
-    for position, pre in enumerate(pres):
-        span = slice(position * rows, (position + 1) * rows)
-        pre[0] = pre_query[span]
-        pre[1] = pre_key[span]
-        pre[2] = d_value[span]
+    pre[0] = pre_query
+    pre[1] = pre_key
+    pre[2] = d_value
     product = (
         pre_query.astype(jnp.float32) * proj[0]
         + pre_key.astype(jnp.float32) * proj[1]
@@ -377,7 +377,7 @@
         dots[...] += product
 
 
-def attention(idx, size, mine, other, weights, from_left, from_right, d_out, tables, chunk, wide, parts):
+def attention(idx, size, mine, other, weights, from_left, from_right, d_out, tables, chunk, wide):
     _, length, part = mine.shape
     heads = wide // HEAD_DIM
     first = chunk * heads
@@ -403,78 +403,59 @@
             out_specs=[
                 pl.BlockSpec((length, HEAD_DIM), lambda h, idx: (0, h)),
                 table,
-                *[pl.BlockSpec((3, length // parts, HEAD_DIM), lambda h, idx: (0, 0, h))] * parts,
+                stack,
             ],
         ),
         out_shape=[
             jax.ShapeDtypeStruct((length, wide), jnp.bfloat16),
             jax.ShapeDtypeStruct((length, HEAD_DIM), jnp.float32),
-            *[jax.ShapeDtypeStruct((3, length // parts, wide), jnp.bfloat16)] * parts,
+            jax.ShapeDtypeStruct((3, length, wide), jnp.bfloat16),
         ],
-        compiler_params=params(),
+        compiler_params=params(16),
         cost_estimate=cost(12 * length * part * wide, 24 * part * wide),
         name="attention",
     )(idx, mine, other, weights, weights, from_left, from_right, d_out, *tables)
 
 
-def grads_chunk(count, turned, pieces, start, before, add, chunk, wide, columns):
+def grads_kernel(turned, *refs):
+    blocks = jnp.concatenate([piece[0] for piece in refs[:-1]], axis=0)
+    refs[-1][0] = mm(turned[...], blocks)
+
+
+def grads_chunk(turned, pieces, before, chunk, wide, columns):
     depth, span = turned.shape
-    in_specs = [pl.BlockSpec((depth, span), lambda m: (0, 0))]
-    operands = [turned]
-    for piece in pieces:
-        in_specs.append(pl.BlockSpec((1, *piece.shape[1:]), lambda m: (m, 0, 0)))
-        operands.append(piece)
-    result = pl.BlockSpec((1, depth, wide), lambda m: (m, 0, chunk))
-    aliases = {}
-    if before is not None:
-        aliases = {len(operands): 0}
-        operands.append(before)
-        in_specs.append(result if add else pl.BlockSpec(memory_space=pl.ANY))
-    length = span // count
-    rows = pieces[0].shape[1]
+    ties = [] if before is None else [before]
+    return pl.pallas_call(
+        tied(grads_kernel, 1 + len(pieces), len(ties)),
+        grid=(3,),
+        in_specs=[
+            pl.BlockSpec((depth, span), lambda m: (0, 0)),
+            *[pl.BlockSpec((1, *piece.shape[1:]), lambda m: (m, 0, 0)) for piece in pieces],
+            *tie_specs(ties),
+        ],
+        out_specs=pl.BlockSpec((1, depth, wide), lambda m: (m, 0, chunk)),
+        out_shape=jax.ShapeDtypeStruct((3, depth, columns), jnp.float32),
+        input_output_aliases={1 + len(pieces): 0} if ties else {},
+        compiler_params=params(24),
+        cost_estimate=cost(6 * span * depth * wide, 6 * span * wide + 12 * depth * wide),
+        name="grads",
+    )(turned, *pieces, *ties)
+
+
+def back(pieces, turned, chunk):
+    wide = pieces[0].shape[2]
+    rows = [jnp.concatenate([piece[m] for m in range(3)], axis=1) for piece in pieces]
+    weight = [turned[m, chunk * wide : (chunk + 1) * wide] for m in range(3)]
+    return mm(jnp.concatenate(rows, axis=0), jnp.concatenate(weight, axis=0))
+
+
+def term_step(turned, pieces, befores, chunk):
+    depth, wide = turned.shape[2], pieces[0].shape[2]
+    count, rows = len(pieces), pieces[0].shape[1]
+    whole = pl.BlockSpec(memory_space=pltpu.VMEM)
 
     def kernel(turned_ref, *refs):
-        blocks = jnp.concatenate([piece[0] for piece in refs[: count + 1]], axis=0)
-        left = [
-            turned_ref[:, place * length + start : place * length + start + rows]
-            for place in range(count)
-        ]
-        total = mm(jnp.concatenate(left, axis=1), blocks)
-        refs[-1][0] = total + refs[-2][0] if add else total
-
-    return pl.pallas_call(
-        kernel,
-        grid=(3,),
-        in_specs=in_specs,
-        out_specs=result,
-        out_shape=jax.ShapeDtypeStruct((3, depth, columns), jnp.float32),
-        input_output_aliases=aliases,
-        compiler_params=params(),
-        cost_estimate=cost(
-            6 * count * rows * depth * wide, 6 * count * rows * wide + 12 * depth * wide
-        ),
-        name="grads",
-    )(*operands)
-
-
-def back(pieces, turned):
-    wide, depth = turned.shape[1:]
-    rows = [jnp.concatenate([piece[m] for m in range(3)], axis=1) for piece in pieces]
-    return mm(jnp.concatenate(rows, axis=0), turned[...].reshape(3 * wide, depth))
-
-
-def term_step(turned, pieces, befores, part, chunk, wide):
-    depth = turned.shape[2]
-    count = len(pieces)
-    rows = pieces[0].shape[1]
-    results = [pl.BlockSpec((rows, depth), lambda i: (0, 0))] * count
-    takes = [
-        pl.BlockSpec((rows, depth), lambda i, row=(part if before.shape[0] > rows else 0): (row, 0))
-        for before in befores
-    ]
-
-    def kernel(turned_ref, *refs):
-        total = back(refs[:count], turned_ref)
+        total = back(refs[:count], turned_ref, chunk)
         for place in range(count):
             block = total[place * rows : (place + 1) * rows]
             if befores:
@@ -483,62 +464,96 @@
 
     return pl.pallas_call(
         kernel,
-        grid=(1,),
-        in_specs=[
-            pl.BlockSpec((3, wide, depth), lambda i: (0, chunk, 0)),
-            *[pl.BlockSpec(piece.shape, lambda i: (0, 0, 0)) for piece in pieces],
-            *takes,
-        ],
-        out_specs=results,
+        in_specs=[whole] * (1 + count + len(befores)),
+        out_specs=[whole] * count,
         out_shape=[jax.ShapeDtypeStruct((rows, depth), jnp.float32)] * count,
-        compiler_params=params(),
+        compiler_params=pltpu.CompilerParams(vmem_limit_bytes=16 * MIB),
         cost_estimate=cost(6 * count * rows * depth * wide, 12 * count * rows * wide),
         name="term_step",
     )(turned, *pieces, *befores)
 
 
-def term_last_kernel(count, idx, turned, before, far_r, far_l, *refs):
-    nears, keep, send = refs[:-2], refs[-2], refs[-1]
-    last = back([far_r, far_l], turned) + before[...]
+def term_last_kernel(count, idx, turned, *refs):
+    befores, fars, nears = refs[:2], refs[2:4], refs[4 : 3 + count]
+    keeps, sends = refs[-4:-2], refs[-2:]
+    half = keeps[0].shape[1]
+    last = back(fars, turned, 1)
     for place in range(count):
-        total = nears[place][...] if place < count - 1 else last
-
-        @pl.when(idx[2 * count + 1 + place] == 0)
-        def _():
-            keep[idx[3 * count + 1 + place]] = total
-
-        @pl.when(idx[2 * count + 1 + place] == 1)
-        def _():
-            send[idx[3 * count + 1 + place]] = total.astype(jnp.bfloat16)
-
-
-def term_last(idx, turned, before, pieces, nears, chunk, wide, ties):
+        for part in range(2):
+            span = slice(part * half, (part + 1) * half)
+            total = nears[place][span] if place < count - 1 else last[span] + befores[part][...]
+
+            @pl.when(idx[2 * count + 1 + place] == 0)
+            def _():
+                keeps[part][idx[3 * count + 1 + place]] = total
+
+            @pl.when(idx[2 * count + 1 + place] == 1)
+            def _():
+                sends[part][idx[3 * count + 1 + place]] = total.astype(jnp.bfloat16)
+
+
+def term_last(idx, turned, befores, pieces, nears):
     count = len(nears) + 1
-    rows, depth = before.shape
-    result = pl.BlockSpec((count // 2, rows, depth), lambda i, idx: (0, 0, 0))
-    block = pl.BlockSpec((rows, depth), lambda i, idx: (0, 0))
-    return pl.pallas_call(
-        tied(functools.partial(term_last_kernel, count), count + 4, len(ties)),
-        grid_spec=pltpu.PrefetchScalarGridSpec(
-            num_scalar_prefetch=1,
-            grid=(1,),
-            in_specs=[
-                pl.BlockSpec((3, wide, depth), lambda i, idx: (0, chunk, 0)),
-                block,
-                *[pl.BlockSpec(piece.shape, lambda i, idx: (0, 0, 0)) for piece in pieces],
-                *[block] * (count - 1),
-                *tie_specs(ties),
-            ],
-            out_specs=[result, result],
-        ),
+    rows, depth = nears[0].shape
+    whole = pl.BlockSpec(memory_space=pltpu.VMEM)
+    shape = (count // 2, rows // 2, depth)
+    return pl.pallas_call(
+        functools.partial(term_last_kernel, count),
+        in_specs=[pl.BlockSpec(memory_space=pltpu.SMEM)] + [whole] * (count + 4),
+        out_specs=[whole] * 4,
+        out_shape=[jax.ShapeDtypeStruct(shape, jnp.float32)] * 2
+        + [jax.ShapeDtypeStruct(shape, jnp.bfloat16)] * 2,
+        compiler_params=pltpu.CompilerParams(vmem_limit_bytes=12 * MIB),
+        cost_estimate=cost(rows * depth * depth, 12 * count * rows * depth),
+        name="term_last",
+    )(idx, turned, *befores, *pieces, *nears)
+
+
+def split_kernel(column, group, idx, keep, came, keep_out, send_out):
+    own = idx[column]
+    for block in range(keep_out.shape[0]):
+        high, low = block // group, block % group
+        mine = (2 * high + own) * group + low
+        other = (2 * high + 1 - own) * group + low
+        keep_out[block] = keep[mine] + came[mine].astype(jnp.float32)
+        send_out[block] = (keep[other] + came[other].astype(jnp.float32)).astype(jnp.bfloat16)
+
+
+def split_sum(idx, column, group, keep, came):
+    whole = pl.BlockSpec(memory_space=pltpu.VMEM)
+    shape = (keep.shape[0] // 2, *keep.shape[1:])
+    return pl.pallas_call(
+        functools.partial(split_kernel, column, group),
+        in_specs=[pl.BlockSpec(memory_space=pltpu.SMEM), whole, whole],
+        out_specs=[whole, whole],
         out_shape=[
-            jax.ShapeDtypeStruct((count // 2, rows, depth), jnp.float32),
-            jax.ShapeDtypeStruct((count // 2, rows, depth), jnp.bfloat16),
+            jax.ShapeDtypeStruct(shape, jnp.float32),
+            jax.ShapeDtypeStruct(shape, jnp.bfloat16),
         ],
-        compiler_params=params(),
-        cost_estimate=cost(6 * rows * depth * wide, 12 * count * rows * depth),
-        name="term_last",
-    )(idx, turned, before, *pieces, *nears, *ties)
+        compiler_params=pltpu.CompilerParams(vmem_limit_bytes=4 * MIB),
+        cost_estimate=cost(0, 8 * keep.shape[0] * keep.shape[1] * keep.shape[2]),
+        name="split_sum",
+    )(idx, keep, came)
+
+
+def order_kernel(column, idx, keep, came, *outs):
+    for turn, out in enumerate(outs):
+        block = idx[column + turn]
+        out[...] = (keep[block] + came[block].astype(jnp.float32)).astype(jnp.bfloat16)
+
+
+def order_sum(idx, column, keep, came):
+    whole = pl.BlockSpec(memory_space=pltpu.VMEM)
+    count = keep.shape[0]
+    return pl.pallas_call(
+        functools.partial(order_kernel, column),
+        in_specs=[pl.BlockSpec(memory_space=pltpu.SMEM), whole, whole],
+        out_specs=[whole] * count,
+        out_shape=[jax.ShapeDtypeStruct(keep.shape[1:], jnp.bfloat16)] * count,
+        compiler_params=pltpu.CompilerParams(vmem_limit_bytes=4 * MIB),
+        cost_estimate=cost(0, 8 * count * keep.shape[1] * keep.shape[2]),
+        name="order_sum",
+    )(idx, keep, came)
 
 
 def local(tokens, norm_gain, w_quant, w_scale, d_out):
@@ -591,11 +606,11 @@
 
     outputs, sets, dots = [], [], 0.0
     for chunk in range(2):
-        output, product, *parts = attention(
-            idx, size, mine, other, weights, *arrived[chunk], d_out, tables, chunk, wide, chunk + 1
+        output, product, pre = attention(
+            idx, size, mine, other, weights, *arrived[chunk], d_out, tables, chunk, wide
         )
         outputs.append(output)
-        sets += parts
+        sets.append(pre)
         dots += jnp.sum(product, axis=-1, keepdims=True)
     bit = 1
     while bit < nodes:
@@ -603,41 +618,20 @@
         bit *= 2
 
     half = length // 2
-    gathered = [[block] for block in sets]
-    moving = [(block, block) for block in sets]
-    schedule = [(0, 1)]
-    for step in range(2, far):
-        schedule += [(0, step), (1, step - 1)]
-    schedule += [(2, 1), (0, far), (1, far - 1), (1, far)]
-    schedule += [(2, step) for step in range(2, far + 1)]
-
     share = width // nodes
     values_part = lax.dynamic_slice_in_dim(tokens, node * share, share, 1).astype(jnp.float32)
     gains_part = lax.dynamic_slice_in_dim(norm_gain, node * share, share, 0).astype(jnp.float32)
     inverse_rms = inverse_rms[:, :1]
 
-    def start_term(part, ties):
-        keep, send = term_last(
-            idx, turned, lasts[part], gathered[1 + part][-2:], terms[1 + part], 1, wide, ties
-        )
-        return keep + swap(send, 1).astype(jnp.float32)
-
-    def sum_nodes(summed):
-        bit = 2
-        while bit < nodes:
-            pair = summed.reshape(-1, 2, group, *summed.shape[1:])
-            own = (node // bit) % 2
-            keep = lax.dynamic_index_in_dim(pair, own, 1, keepdims=False)
-            send = lax.dynamic_index_in_dim(pair, 1 - own, 1, keepdims=False)
-            summed = keep + swap(send.astype(jnp.bfloat16), bit).astype(jnp.float32)
-            summed = summed.reshape(-1, *pair.shape[3:])
+    def to_place(keep, send):
+        column = 4 * size + 1
+        bit = 1
+        while 2 * bit < nodes:
+            keep, send = split_sum(idx, column, group, keep, swap(send, bit))
+            column += 1
             bit *= 2
-        return summed.astype(jnp.bfloat16)
-
-    def relocate(summed):
         came = []
-        for turn in range(group):
-            block = lax.dynamic_index_in_dim(summed, (here + turn) % group, 0, keepdims=False)
+        for turn, block in enumerate(order_sum(idx, column, keep, swap(send, bit))):
             moves = [
                 (n * size + s, (s // group) * size + n * group + (s + turn) % group)
                 for n in range(nodes)
@@ -662,39 +656,30 @@
         )
         return d_rows.astype(jnp.bfloat16)
 
-    terms = [[], [], []]
-    early = summed = None
-    for ring, step in schedule:
-        right, left = moving[ring]
-        if step == far:
-            ties = [[], [dots, *moving[2]], [summed]][ring]
-            right, left = pass_on(right, left, True, ties)
-        elif (ring, step) == (2, far - 1):
-            right, left = pass_on(right, left, False, [early, first_grads])
-        right, left = shift(right, 1), shift(left, -1)
-        moving[ring] = right, left
-        gathered[ring] += [right, left]
-        chunk, part = min(ring, 1), max(ring - 1, 0)
-        if step < far:
-            pieces = gathered[ring] if step == 1 else [right, left]
-            known = len(terms[ring])
-            befores = terms[0][known : known + len(pieces)] if ring else []
-            terms[ring] += term_step(turned, pieces, befores, part, chunk, wide)
-        elif ring == 0:
-            lasts = term_step(turned, [right, left], [], 0, 0, wide)
-            first_grads = grads_chunk(
-                size, rows_turned, gathered[0], 0, None, False, 0, wide, columns
-            )
-        elif ring == 1:
-            early = start_term(0, [])
-            half_grads = grads_chunk(
-                size, rows_turned, gathered[1], 0, first_grads, False, 1, wide, columns
-            )
-            summed = sum_nodes(early)
-    came = relocate(summed)
-    late = start_term(1, came)
-    d_tokens = jnp.concatenate([end_term(came, 0), end_term(relocate(sum_nodes(late)), 1)], axis=0)
-    grads = grads_chunk(size, rows_turned, gathered[2], half, half_grads, True, 1, wide, columns)
+    gathered = [[block] for block in sets]
+    moving = [(block, block) for block in sets]
+    terms = [[], []]
+    for step in range(1, far + 1):
+        for chunk in range(2):
+            right, left = moving[chunk]
+            if step == far:
+                early = [dots] if chunk == 0 else terms[1][: size - 3]
+                right, left = halve(right, left, early)
+            right, left = shift(right, 1), shift(left, -1)
+            moving[chunk] = right, left
+            gathered[chunk] += [right, left]
+            if step < far:
+                pieces = gathered[chunk] if step == 1 else [right, left]
+                known = len(terms[chunk])
+                befores = terms[0][known : known + len(pieces)] if chunk else []
+                terms[chunk] += term_step(turned, pieces, befores, chunk)
+            elif chunk == 0:
+                lasts = term_step(turned, [right, left], [], 0)
+    keep_0, keep_1, send_0, send_1 = term_last(idx, turned, lasts, gathered[1][-2:], terms[1])
+    first, second = to_place(keep_0, send_0), to_place(keep_1, send_1)
+    d_tokens = jnp.concatenate([end_term(first, 0), end_term(second, 1)], axis=0)
+    grads = grads_chunk(rows_turned, gathered[0], None, 0, wide, columns)
+    grads = grads_chunk(rows_turned, gathered[1], grads, 1, wide, columns)
     return (jnp.concatenate(outputs, axis=-1), d_tokens, grads)
 
 

time: 366 us -> 334 us (0.913)
  local copies, waits for them, and re-layouts: 36.5 us -> 21.2 us
  waiting for transfers between devices: 171 us -> 162 us
  other arithmetic: 14.1 us -> 7.39 us
    ppermute x47 -> x39, waiting for transfers between devices: 160 us -> 145 us  [shift(): return lax.ppermute(array, 'local', moves)]
    unnamed x154 -> x84, local copies, waits for them, and re-layouts: 32.4 us -> 18.7 us
    ppermute x4, waiting for transfers between devices: 4.21 us -> 10.5 us  [to_place(): came.append(lax.ppermute(block, ('node', 'local'), moves))]
    ppermute x47 -> x39, starting transfers between devices: 55 us -> 53.8 us  [shift(): return lax.ppermute(array, 'local', moves)]
    pallas_call x19 -> x16, Pallas kernels: 39.5 us -> 38.4 us  [the longest x7 14.5 us: term_step(): pl.pallas_call(kernel, in_specs=[whole] * (1 + count + len(befores)), out...]
  transfers between devices with their start and end apart: 59 -> 51, of which waited for: 32 -> 30; matrix products, arithmetic and copies ran while one was open for 4% -> 2% of each run, Pallas kernels for 17% -> 20%
where the time goes in v6:
time: 334 us; the launch traced here: 333 us
  waiting for transfers between devices  162 us (49%)
  Pallas kernels  70.7 us (21%)
  starting transfers between devices  70.1 us (21%)
  local copies, waits for them, and re-layouts  21.2 us (6%)
  other arithmetic  7.39 us (2%)
    ppermute x39, waiting for transfers between devices, shift(): return lax.ppermute(array, 'local', moves)  145 us
    ppermute x39, starting transfers between devices, shift(): return lax.ppermute(array, 'local', moves)  53.8 us
    unnamed x84, local copies, waits for them, and re-layouts  18.7 us
    pallas_call x7, Pallas kernels, term_step(): pl.pallas_call(kernel, in_specs=[whole] * (1 + count + len(befores)), out...  14.5 us
    pallas_call x2, Pallas kernels, attention(): pl.pallas_call(attention_kernel, grid_spec=pltpu.PrefetchScalarGridSpec(n...  14.4 us
    ppermute x4, starting transfers between devices, to_place(): came.append(lax.ppermute(block, ('node', 'local'), moves))  12.9 us
    pallas_call x2, Pallas kernels, grads_chunk(): pl.pallas_call(tied(grads_kernel, 1 + len(pieces), len(ties)), grid=(3,),...  12.7 us
    pallas_call x6, Pallas kernels, sum_step(): pl.pallas_call(tied(sum_step_kernel, 9, len(ties)), grid_spec=pltpu.Prefe...  12.3 us
  transfers between devices with their start and end apart: 51, of which 30 were waited for; matrix products, arithmetic and copies ran while one was open for 2% of the time, Pallas kernels for 20%

profile of v6, /device:TPU:2, one launch (start us, length us, event | category | flops | bytes accessed | tf_op | source)
XLA Modules:
  0.0 332.9 jit_solution(9222413432021834904)
XLA Ops:
  2.1 1.6 copy-done.2
  5.7 4.6 %collective-permute-start.6 = (bf16[256,256]{1,0:T(8,128)(2,1)S(1)}, bf16[256,256]{1,0:T(8,128)(2,1)S(1)}, u32[]{:S(2)}, u32[]{:S(2)}) collective-permute-start(bf16[256,256]{1,0:T(8,128)(2,1)S(1)} %get-tuple-element.75), channel_id=1, source_target_pairs={{0,7},{2,5},{4,3},{6,1},{7,0},{5,2},{3,4},{1,6},{8,15},{10,13},{12... | collective-permute-start | bytes 393224 | tf_op jit(solution)/shard_map/ppermute | solution.py:576
  10.3 4.5 %collective-permute-done.6.mine.mine_far = bf16[256,256]{1,0:T(8,128)(2,1)S(1)} collective-permute-done((bf16[256,256]{1,0:T(8,128)(2,1)S(1)}, bf16[256,256]{1,0:T(8,128)(2,1)S(1)}, u32[]{:S(2)}, u32[]{:S(2)}) %collective-permute-start.6) | collective-permute-done | bytes 131104 | tf_op jit(solution)/shard_map/ppermute | solution.py:576
  15.3 3.4 %collective-permute-start.2 = (bf16[256,256]{1,0:T(8,128)(2,1)S(1)}, bf16[256,256]{1,0:T(8,128)(2,1)S(1)}, u32[]{:S(2)}, u32[]{:S(2)}) collective-permute-start(bf16[256,256]{1,0:T(8,128)(2,1)S(1)} %get-tuple-element.71), channel_id=1, source_target_pairs={{0,4},{2,6},{4,7},{6,5},{7,3},{5,1},{3,0},{1,2},{8,12},{10,14},{12... | collective-permute-start | bytes 393224 | tf_op jit(solution)/shard_map/ppermute | solution.py:576
  19.9 1.7 collective-permute-start.4
  21.6 2.1 collective-permute-start.5
  23.8 1.9 copy-done.21
  27.5 1.9 sum_first.1
  29.4 4.6 %collective-permute-done.3.refs_4_ = bf16[256,256]{1,0:T(8,128)(2,1)S(1)} collective-permute-done((bf16[256,256]{1,0:T(8,128)(2,1)S(1)}, bf16[256,256]{1,0:T(8,128)(2,1)S(1)}, u32[]{:S(2)}, u32[]{:S(2)}) %collective-permute-start.3) | collective-permute-done | bytes 131104 | tf_op jit(solution)/shard_map/ppermute | solution.py:576
  35.3 3.1 collective-permute-start.10
  38.4 2.0 collective-permute-start.18
  40.5 7.9 %collective-permute-done.9.refs_7_ = bf16[3,128,512]{2,1,0:T(8,128)(2,1)S(1)} collective-permute-done((bf16[3,128,512]{2,1,0:T(8,128)(2,1)S(1)}, bf16[3,128,512]{2,1,0:T(8,128)(2,1)S(1)}, u32[]{:S(2)}, u32[]{:S(2)}) %collective-permute-start.9) | collective-permute-done | bytes 393248 | tf_op jit(solution)/shard_map/ppermute | solution.py:576
  48.3 2.1 sum_step.6
  50.4 3.2 collective-permute-start.11
  53.5 3.2 collective-permute-done.17.refs_7_
  56.7 2.1 sum_step.9
  58.8 3.2 collective-permute-start.19
  62.0 11.6 %collective-permute-done.11.refs_7_ = bf16[3,256,512]{2,1,0:T(8,128)(2,1)S(1)} collective-permute-done((bf16[3,256,512]{2,1,0:T(8,128)(2,1)S(1)}, bf16[3,256,512]{2,1,0:T(8,128)(2,1)S(1)}, u32[]{:S(2)}, u32[]{:S(2)}) %collective-permute-start.11) | collective-permute-done | bytes 786464 | tf_op jit(solution)/shard_map/ppermute | solution.py:576
  74.1 2.1 sum_step.7
  76.1 2.7 collective-permute-start.13
  78.8 11.6 %collective-permute-done.19.refs_7_ = bf16[3,256,512]{2,1,0:T(8,128)(2,1)S(1)} collective-permute-done((bf16[3,256,512]{2,1,0:T(8,128)(2,1)S(1)}, bf16[3,256,512]{2,1,0:T(8,128)(2,1)S(1)}, u32[]{:S(2)}, u32[]{:S(2)}) %collective-permute-start.19) | collective-permute-done | bytes 786464 | tf_op jit(solution)/shard_map/ppermute | solution.py:576
  90.9 2.1 sum_step.10
  93.0 2.7 collective-permute-start.21
  96.9 10.4 %collective-permute-done.13.refs_7_ = bf16[3,256,512]{2,1,0:T(8,128)(2,1)S(1)} collective-permute-done((bf16[3,256,512]{2,1,0:T(8,128)(2,1)S(1)}, bf16[3,256,512]{2,1,0:T(8,128)(2,1)S(1)}, u32[]{:S(2)}, u32[]{:S(2)}) %collective-permute-start.13) | collective-permute-done | bytes 786464 | tf_op jit(solution)/shard_map/ppermute | solution.py:576
  107.8 2.1 sum_step.8
  109.8 2.7 collective-permute-start.15
  112.5 11.6 %collective-permute-done.21.refs_7_ = bf16[3,256,512]{2,1,0:T(8,128)(2,1)S(1)} collective-permute-done((bf16[3,256,512]{2,1,0:T(8,128)(2,1)S(1)}, bf16[3,256,512]{2,1,0:T(8,128)(2,1)S(1)}, u32[]{:S(2)}, u32[]{:S(2)}) %collective-permute-start.21) | collective-permute-done | bytes 786464 | tf_op jit(solution)/shard_map/ppermute | solution.py:576
  124.6 2.1 sum_step.11
  126.7 2.7 collective-permute-start.23
  130.1 10.9 %collective-permute-done.15.from_left = bf16[3,256,512]{2,1,0:T(8,128)(2,1)S(1)} collective-permute-done((bf16[3,256,512]{2,1,0:T(8,128)(2,1)S(1)}, bf16[3,256,512]{2,1,0:T(8,128)(2,1)S(1)}, u32[]{:S(2)}, u32[]{:S(2)}) %collective-permute-start.15) | collective-permute-done | bytes 786464 | tf_op jit(solution)/shard_map/ppermute | solution.py:576
  141.5 7.2 %attention.2 = (bf16[256,512]{1,0:T(8,128)(2,1)S(1)}, f32[256,128]{1,0:T(8,128)S(1)}, bf16[3,256,512]{2,1,0:T(8,128)(2,1)S(1)}) custom-call(s32[36]{0:T(128)S(1)} %fusion.17.idx.refs_0_, bf16[7,256,256]{2,1,0:T(8,128)(2,1)S(1)} %stack.25.refs_1_.refs_3_.mine, bf16[7,256,256]{2,1,0:T(8,128)(2,1)S(1)} %collective-permute-done.8.refs_2_.refs_4_.other, ...), custom_call_target="tpu_custom_call" | custom-call | flops 402653184 | bytes 3145728 | tf_op jit(solution)/shard_map/attention/pallas_call | solution.py:387
  149.4 2.6 collective-permute-start.25
  152.0 5.9 %collective-permute-done.23.from_left = bf16[3,256,512]{2,1,0:T(8,128)(2,1)S(1)} collective-permute-done((bf16[3,256,512]{2,1,0:T(8,128)(2,1)S(1)}, bf16[3,256,512]{2,1,0:T(8,128)(2,1)S(1)}, u32[]{:S(2)}, u32[]{:S(2)}) %collective-permute-start.23) | collective-permute-done | bytes 786464 | tf_op jit(solution)/shard_map/ppermute | solution.py:576
  158.3 7.2 %attention.3 = (bf16[256,512]{1,0:T(8,128)(2,1)S(1)}, f32[256,128]{1,0:T(8,128)S(1)}, bf16[3,256,512]{2,1,0:T(8,128)(2,1)S(1)}) custom-call(s32[36]{0:T(128)S(1)} %fusion.17.idx.refs_0_, bf16[7,256,256]{2,1,0:T(8,128)(2,1)S(1)} %stack.25.refs_1_.refs_3_.mine, bf16[7,256,256]{2,1,0:T(8,128)(2,1)S(1)} %collective-permute-done.8.refs_2_.refs_4_.other, ...), custom_call_target="tpu_custom_call" | custom-call | flops 402653184 | bytes 3145728 | tf_op jit(solution)/shard_map/attention/pallas_call | solution.py:387
  166.3 2.6 collective-permute-start.35
  169.8 4.9 %collective-permute-done.25.refs_1_.refs_2_ = bf16[3,256,512]{2,1,0:T(8,128)(2,1)S(1)} collective-permute-done((bf16[3,256,512]{2,1,0:T(8,128)(2,1)S(1)}, bf16[3,256,512]{2,1,0:T(8,128)(2,1)S(1)}, u32[]{:S(2)}, u32[]{:S(2)}) %collective-permute-start.25) | collective-permute-done | bytes 786464 | tf_op jit(solution)/shard_map/ppermute | solution.py:576
  176.0 1.6 collective-permute-start.29
  178.5 13.0 %collective-permute-done.35.refs_1_.refs_2_ = bf16[3,256,512]{2,1,0:T(8,128)(2,1)S(1)} collective-permute-done((bf16[3,256,512]{2,1,0:T(8,128)(2,1)S(1)}, bf16[3,256,512]{2,1,0:T(8,128)(2,1)S(1)}, u32[]{:S(2)}, u32[]{:S(2)}) %collective-permute-start.35) | collective-permute-done | bytes 786464 | tf_op jit(solution)/shard_map/ppermute | solution.py:576
  192.9 1.6 collective-permute-start.39
  195.4 13.1 %collective-permute-done.26.refs_0_.refs_4_ = bf16[3,256,512]{2,1,0:T(8,128)(2,1)} collective-permute-done((bf16[3,256,512]{2,1,0:T(8,128)(2,1)S(1)}, bf16[3,256,512]{2,1,0:T(8,128)(2,1)}, u32[]{:S(2)}, u32[]{:S(2)}) %collective-permute-start.26) | collective-permute-done | bytes 786464 | tf_op jit(solution)/shard_map/ppermute | solution.py:576
  210.6 14.8 %collective-permute-done.36.refs_0_.refs_4_ = bf16[3,256,512]{2,1,0:T(8,128)(2,1)} collective-permute-done((bf16[3,256,512]{2,1,0:T(8,128)(2,1)S(1)}, bf16[3,256,512]{2,1,0:T(8,128)(2,1)}, u32[]{:S(2)}, u32[]{:S(2)}) %collective-permute-start.36) | collective-permute-done | bytes 786464 | tf_op jit(solution)/shard_map/ppermute | solution.py:576
  225.8 1.6 collective-permute-start.40
  229.9 5.0 %collective-permute-done.32 = f32[256,1]{1,0:T(8,128)S(1)} collective-permute-done((f32[256,1]{1,0:T(8,128)S(1)}, f32[256,1]{1,0:T(8,128)S(1)}, u32[]{:S(2)}, u32[]{:S(2)}) %collective-permute-start.32) | collective-permute-done | bytes 1056 | tf_op jit(solution)/shard_map/ppermute | solution.py:579
  241.2 2.9 term_step.10
  244.1 2.3 halve.2
  248.4 2.3 term_step.11
  250.8 8.3 %collective-permute-done.37.refs_0_.refs_6_ = bf16[3,256,512]{2,1,0:T(8,128)(2,1)} collective-permute-done((bf16[3,256,512]{2,1,0:T(8,128)(2,1)}, bf16[3,256,512]{2,1,0:T(8,128)(2,1)}, u32[]{:S(2)}, u32[]{:S(2)}) %collective-permute-start.37) | collective-permute-done | bytes 786464 | tf_op jit(solution)/shard_map/ppermute | solution.py:576
  259.6 2.3 halve.3
  261.9 2.6 collective-permute-start.41
  264.5 2.3 term_step.12
  266.9 2.3 term_step.13
  269.3 1.8 term_step.7
  271.1 4.5 %collective-permute-done.41.refs_2_.refs_8_ = bf16[3,128,512]{2,1,0:T(8,128)(2,1)S(1)} collective-permute-done((bf16[3,128,512]{2,1,0:T(8,128)(2,1)}, bf16[3,128,512]{2,1,0:T(8,128)(2,1)S(1)}, u32[]{:S(2)}, u32[]{:S(2)}) %collective-permute-start.41) | collective-permute-done | bytes 393248 | tf_op jit(solution)/shard_map/ppermute | solution.py:576
  275.6 3.1 term_last.1
  284.4 1.9 pad_maximum_fusion
  294.2 6.4 %grads.2.refs_10_ = f32[3,512,1024]{2,1,0:T(8,128)} custom-call(bf16[512,2048]{1,0:T(8,128)(2,1)S(1)} %copy-done.1, bf16[3,256,512]{2,1,0:T(8,128)(2,1)S(1)} %copy-done.14, bf16[3,256,512]{2,1,0:T(8,128)(2,1)S(1)} %copy-done.17, bf16[3,256,512]{2,1,0:T(8,128)(2,1)S(1)} %copy-done.20, bf16[3,256,512]{2,1,0:T(8,128)(2,1)} %collective-permute-done.26.refs_0_.refs_4_, ...), custom_call_target="tpu_custom_call" | custom-call | flops 3221225472 | bytes 9437184 | tf_op jit(solution)/shard_map/grads/pallas_call | solution.py:428
  301.2 6.1 %collective-permute-start.45 = (bf16[128,512]{1,0:T(8,128)(2,1)S(1)}, bf16[128,512]{1,0:T(8,128)(2,1)S(1)}, u32[]{:S(2)}, u32[]{:S(2)}) collective-permute-start(bf16[128,512]{1,0:T(8,128)(2,1)S(1)} %get-tuple-element.125), channel_id=1, source_target_pairs={{0,0},{1,1},{2,8},{3,9},{4,16},{5,17},{6,24},{7,25},{8,2},{9,3},{1... | collective-permute-start | bytes 393224 | tf_op jit(solution)/shard_map/ppermute | solution.py:640
  308.9 3.4 %collective-permute-start.49 = (bf16[128,512]{1,0:T(8,128)(2,1)S(1)}, bf16[128,512]{1,0:T(8,128)(2,1)S(1)}, u32[]{:S(2)}, u32[]{:S(2)}) collective-permute-start(bf16[128,512]{1,0:T(8,128)(2,1)S(1)} %get-tuple-element.131), channel_id=1, source_target_pairs={{0,0},{1,1},{2,8},{3,9},{4,16},{5,17},{6,24},{7,25},{8,2},{9,3},{1... | collective-permute-start | bytes 393224 | tf_op jit(solution)/shard_map/ppermute | solution.py:640
  312.3 2.4 collective-permute-start.50
  314.7 6.3 %grads.3 = f32[3,512,1024]{2,1,0:T(8,128)} custom-call(bf16[512,2048]{1,0:T(8,128)(2,1)S(1)} %copy-done.1, bf16[3,256,512]{2,1,0:T(8,128)(2,1)S(1)} %copy-done.5, bf16[3,256,512]{2,1,0:T(8,128)(2,1)S(1)} %copy-done.8, bf16[3,256,512]{2,1,0:T(8,128)(2,1)S(1)} %copy-done.11, ...), custom_call_target="tpu_custom_call", output_to_operand_aliasing={{}: (10, {})} | custom-call | flops 3221225472 | bytes 9437184 | tf_op jit(solution)/shard_map/grads/pallas_call | solution.py:428
  321.1 1.6 collective-permute-done.45
  322.6 3.4 %collective-permute-done.46 = bf16[128,512]{1,0:T(8,128)(2,1)S(1)} collective-permute-done((bf16[128,512]{1,0:T(8,128)(2,1)S(1)}, bf16[128,512]{1,0:T(8,128)(2,1)S(1)}, u32[]{:S(2)}, u32[]{:S(2)}) %collective-permute-start.46) | collective-permute-done | bytes 131104 | tf_op jit(solution)/shard_map/ppermute | solution.py:640
  326.2 2.1 collective-permute-done.49
  328.3 3.4 %collective-permute-done.50 = bf16[128,512]{1,0:T(8,128)(2,1)S(1)} collective-permute-done((bf16[128,512]{1,0:T(8,128)(2,1)S(1)}, bf16[128,512]{1,0:T(8,128)(2,1)S(1)}, u32[]{:S(2)}, u32[]{:S(2)}) %collective-permute-start.50) | collective-permute-done | bytes 131104 | tf_op jit(solution)/shard_map/ppermute | solution.py:640
  (172 shorter events, 50.4 us)
Async XLA Ops:
  5.7 9.1 %collective-permute-start.6 = (bf16[256,256]{1,0:T(8,128)(2,1)S(1)}, bf16[256,256]{1,0:T(8,128)(2,1)S(1)}, u32[]{:S(2)}, u32[]{:S(2)}) collective-permute-start(bf16[256,256]{1,0:T(8,128)(2,1)S(1)} %get-tuple-element.75), channel_id=1, source_target_pairs={{0,7},{2,5},{4,3},{6,1},{7,0},{5,2},{3,4},{1,6},{8,15},{10,13},{12... | collective-permute-start | bytes 393224 | tf_op jit(solution)/shard_map/ppermute | solution.py:576
  10.3 9.7 %collective-permute-start = (bf16[256,256]{1,0:T(8,128)(2,1)S(1)}, bf16[256,256]{1,0:T(8,128)(2,1)S(1)}, u32[]{:S(2)}, u32[]{:S(2)}) collective-permute-start(bf16[256,256]{1,0:T(8,128)(2,1)S(1)} %get-tuple-element.69), channel_id=1, source_target_pairs={{0,2},{2,4},{4,6},{6,7},{7,5},{5,3},{3,1},{1,0},{8,10},{10,12},{12... | collective-permute-start | bytes 393224 | tf_op jit(solution)/shard_map/ppermute | solution.py:576
  14.8 6.9 %collective-permute-start.7 = (bf16[256,256]{1,0:T(8,128)(2,1)S(1)}, bf16[256,256]{1,0:T(8,128)(2,1)S(1)}, u32[]{:S(2)}, u32[]{:S(2)}) collective-permute-start(bf16[256,256]{1,0:T(8,128)(2,1)S(1)} %collective-permute-done.6.mine.mine_far), channel_id=1, source_target_pairs={{0,8},{8,0},{16,24},{24,16},{1,9},{9,1},{17,25},{25,17},{2,10},{10... | collective-permute-start | bytes 393224 | tf_op jit(solution)/shard_map/ppermute | solution.py:579
  14.8 14.6 %collective-permute-start.1 = (bf16[256,256]{1,0:T(8,128)(2,1)S(1)}, bf16[256,256]{1,0:T(8,128)(2,1)S(1)}, u32[]{:S(2)}, u32[]{:S(2)}) collective-permute-start(bf16[256,256]{1,0:T(8,128)(2,1)S(1)} %get-tuple-element.70), channel_id=1, source_target_pairs={{0,1},{2,0},{4,2},{6,4},{7,6},{5,7},{3,5},{1,3},{8,9},{10,8},{12,1... | collective-permute-start | bytes 393224 | tf_op jit(solution)/shard_map/ppermute | solution.py:576
  15.3 14.1 %collective-permute-start.2 = (bf16[256,256]{1,0:T(8,128)(2,1)S(1)}, bf16[256,256]{1,0:T(8,128)(2,1)S(1)}, u32[]{:S(2)}, u32[]{:S(2)}) collective-permute-start(bf16[256,256]{1,0:T(8,128)(2,1)S(1)} %get-tuple-element.71), channel_id=1, source_target_pairs={{0,4},{2,6},{4,7},{6,5},{7,3},{5,1},{3,0},{1,2},{8,12},{10,14},{12... | collective-permute-start | bytes 393224 | tf_op jit(solution)/shard_map/ppermute | solution.py:576
  18.7 15.3 %collective-permute-start.3 = (bf16[256,256]{1,0:T(8,128)(2,1)S(1)}, bf16[256,256]{1,0:T(8,128)(2,1)S(1)}, u32[]{:S(2)}, u32[]{:S(2)}) collective-permute-start(bf16[256,256]{1,0:T(8,128)(2,1)S(1)} %get-tuple-element.72), channel_id=1, source_target_pairs={{0,3},{2,1},{4,0},{6,2},{7,4},{5,6},{3,7},{1,5},{8,11},{10,9},{12,... | collective-permute-start | bytes 393224 | tf_op jit(solution)/shard_map/ppermute | solution.py:576
  19.9 15.2 %collective-permute-start.4 = (bf16[256,256]{1,0:T(8,128)(2,1)S(1)}, bf16[256,256]{1,0:T(8,128)(2,1)S(1)}, u32[]{:S(2)}, u32[]{:S(2)}) collective-permute-start(bf16[256,256]{1,0:T(8,128)(2,1)S(1)} %get-tuple-element.73), channel_id=1, source_target_pairs={{0,6},{2,7},{4,5},{6,3},{7,1},{5,0},{3,2},{1,4},{8,14},{10,15},{12... | collective-permute-start | bytes 393224 | tf_op jit(solution)/shard_map/ppermute | solution.py:576
  21.6 13.4 %collective-permute-start.5 = (bf16[256,256]{1,0:T(8,128)(2,1)S(1)}, bf16[256,256]{1,0:T(8,128)(2,1)S(1)}, u32[]{:S(2)}, u32[]{:S(2)}) collective-permute-start(bf16[256,256]{1,0:T(8,128)(2,1)S(1)} %get-tuple-element.74), channel_id=1, source_target_pairs={{0,5},{2,3},{4,1},{6,0},{7,2},{5,4},{3,6},{1,7},{8,13},{10,11},{12... | collective-permute-start | bytes 393224 | tf_op jit(solution)/shard_map/ppermute | solution.py:576
  35.2 13.2 %collective-permute-start.8 = (bf16[7,256,256]{2,1,0:T(8,128)(2,1)S(1)}, bf16[7,256,256]{2,1,0:T(8,128)(2,1)S(1)}, u32[]{:S(2)}, u32[]{:S(2)}) collective-permute-start(bf16[7,256,256]{2,1,0:T(8,128)(2,1)S(1)} %stack.25.refs_1_.refs_3_.mine), channel_id=1, source_target_pairs={{0,8},{8,0},{16,24},{24,16},{1,9},{9,1},{17,25},{25,17},{2,10},{10... | collective-permute-start | bytes 2752520 | tf_op jit(solution)/shard_map/ppermute | solution.py:579
  35.2 13.1 %collective-permute-start.9 = (bf16[3,128,512]{2,1,0:T(8,128)(2,1)S(1)}, bf16[3,128,512]{2,1,0:T(8,128)(2,1)S(1)}, u32[]{:S(2)}, u32[]{:S(2)}) collective-permute-start(bf16[3,128,512]{2,1,0:T(8,128)(2,1)S(1)} %get-tuple-element.77.refs_7_), channel_id=1, source_target_pairs={{0,2},{2,4},{4,6},{6,7},{7,5},{5,3},{3,1},{1,0},{8,10},{10,12},{12... | collective-permute-start | bytes 1179656 | tf_op jit(solution)/shard_map/ppermute | solution.py:576
  35.3 13.0 %collective-permute-start.10 = (bf16[3,128,512]{2,1,0:T(8,128)(2,1)S(1)}, bf16[3,128,512]{2,1,0:T(8,128)(2,1)S(1)}, u32[]{:S(2)}, u32[]{:S(2)}) collective-permute-start(bf16[3,128,512]{2,1,0:T(8,128)(2,1)S(1)} %get-tuple-element.78), channel_id=1, source_target_pairs={{0,1},{2,0},{4,2},{6,4},{7,6},{5,7},{3,5},{1,3},{8,9},{10,8},{12,1... | collective-permute-start | bytes 1179656 | tf_op jit(solution)/shard_map/ppermute | solution.py:576
  38.4 18.3 %collective-permute-start.17 = (bf16[3,128,512]{2,1,0:T(8,128)(2,1)S(1)}, bf16[3,128,512]{2,1,0:T(8,128)(2,1)S(1)}, u32[]{:S(2)}, u32[]{:S(2)}) collective-permute-start(bf16[3,128,512]{2,1,0:T(8,128)(2,1)S(1)} %get-tuple-element.86), channel_id=1, source_target_pairs={{0,2},{2,4},{4,6},{6,7},{7,5},{5,3},{3,1},{1,0},{8,10},{10,12},{12... | collective-permute-start | bytes 1179656 | tf_op jit(solution)/shard_map/ppermute | solution.py:576
  38.4 18.3 %collective-permute-start.18 = (bf16[3,128,512]{2,1,0:T(8,128)(2,1)S(1)}, bf16[3,128,512]{2,1,0:T(8,128)(2,1)S(1)}, u32[]{:S(2)}, u32[]{:S(2)}) collective-permute-start(bf16[3,128,512]{2,1,0:T(8,128)(2,1)S(1)} %get-tuple-element.87), channel_id=1, source_target_pairs={{0,1},{2,0},{4,2},{6,4},{7,6},{5,7},{3,5},{1,3},{8,9},{10,8},{12,1... | collective-permute-start | bytes 1179656 | tf_op jit(solution)/shard_map/ppermute | solution.py:576
  50.4 23.2 %collective-permute-start.11 = (bf16[3,256,512]{2,1,0:T(8,128)(2,1)S(1)}, bf16[3,256,512]{2,1,0:T(8,128)(2,1)S(1)}, u32[]{:S(2)}, u32[]{:S(2)}) collective-permute-start(bf16[3,256,512]{2,1,0:T(8,128)(2,1)S(1)} %get-tuple-element.79), channel_id=1, source_target_pairs={{0,2},{2,4},{4,6},{6,7},{7,5},{5,3},{3,1},{1,0},{8,10},{10,12},{12... | collective-permute-start | bytes 2359304 | tf_op jit(solution)/shard_map/ppermute | solution.py:576
  53.5 20.5 %collective-permute-start.12 = (bf16[3,256,512]{2,1,0:T(8,128)(2,1)S(1)}, bf16[3,256,512]{2,1,0:T(8,128)(2,1)S(1)}, u32[]{:S(2)}, u32[]{:S(2)}) collective-permute-start(bf16[3,256,512]{2,1,0:T(8,128)(2,1)S(1)} %get-tuple-element.80), channel_id=1, source_target_pairs={{0,1},{2,0},{4,2},{6,4},{7,6},{5,7},{3,5},{1,3},{8,9},{10,8},{12,1... | collective-permute-start | bytes 2359304 | tf_op jit(solution)/shard_map/ppermute | solution.py:576
  58.8 31.6 %collective-permute-start.19 = (bf16[3,256,512]{2,1,0:T(8,128)(2,1)S(1)}, bf16[3,256,512]{2,1,0:T(8,128)(2,1)S(1)}, u32[]{:S(2)}, u32[]{:S(2)}) collective-permute-start(bf16[3,256,512]{2,1,0:T(8,128)(2,1)S(1)} %get-tuple-element.88), channel_id=1, source_target_pairs={{0,2},{2,4},{4,6},{6,7},{7,5},{5,3},{3,1},{1,0},{8,10},{10,12},{12... | collective-permute-start | bytes 2359304 | tf_op jit(solution)/shard_map/ppermute | solution.py:576
  62.0 29.0 %collective-permute-start.20 = (bf16[3,256,512]{2,1,0:T(8,128)(2,1)S(1)}, bf16[3,256,512]{2,1,0:T(8,128)(2,1)S(1)}, u32[]{:S(2)}, u32[]{:S(2)}) collective-permute-start(bf16[3,256,512]{2,1,0:T(8,128)(2,1)S(1)} %get-tuple-element.89), channel_id=1, source_target_pairs={{0,1},{2,0},{4,2},{6,4},{7,6},{5,7},{3,5},{1,3},{8,9},{10,8},{12,1... | collective-permute-start | bytes 2359304 | tf_op jit(solution)/shard_map/ppermute | solution.py:576
  76.1 31.2 %collective-permute-start.13 = (bf16[3,256,512]{2,1,0:T(8,128)(2,1)S(1)}, bf16[3,256,512]{2,1,0:T(8,128)(2,1)S(1)}, u32[]{:S(2)}, u32[]{:S(2)}) collective-permute-start(bf16[3,256,512]{2,1,0:T(8,128)(2,1)S(1)} %get-tuple-element.81), channel_id=1, source_target_pairs={{0,2},{2,4},{4,6},{6,7},{7,5},{5,3},{3,1},{1,0},{8,10},{10,12},{12... | collective-permute-start | bytes 2359304 | tf_op jit(solution)/shard_map/ppermute | solution.py:576
  78.8 29.0 %collective-permute-start.14 = (bf16[3,256,512]{2,1,0:T(8,128)(2,1)S(1)}, bf16[3,256,512]{2,1,0:T(8,128)(2,1)S(1)}, u32[]{:S(2)}, u32[]{:S(2)}) collective-permute-start(bf16[3,256,512]{2,1,0:T(8,128)(2,1)S(1)} %get-tuple-element.82), channel_id=1, source_target_pairs={{0,1},{2,0},{4,2},{6,4},{7,6},{5,7},{3,5},{1,3},{8,9},{10,8},{12,1... | collective-permute-start | bytes 2359304 | tf_op jit(solution)/shard_map/ppermute | solution.py:576
  93.0 31.2 %collective-permute-start.21 = (bf16[3,256,512]{2,1,0:T(8,128)(2,1)S(1)}, bf16[3,256,512]{2,1,0:T(8,128)(2,1)S(1)}, u32[]{:S(2)}, u32[]{:S(2)}) collective-permute-start(bf16[3,256,512]{2,1,0:T(8,128)(2,1)S(1)} %get-tuple-element.90), channel_id=1, source_target_pairs={{0,2},{2,4},{4,6},{6,7},{7,5},{5,3},{3,1},{1,0},{8,10},{10,12},{12... | collective-permute-start | bytes 2359304 | tf_op jit(solution)/shard_map/ppermute | solution.py:576
  95.7 29.0 %collective-permute-start.22 = (bf16[3,256,512]{2,1,0:T(8,128)(2,1)S(1)}, bf16[3,256,512]{2,1,0:T(8,128)(2,1)S(1)}, u32[]{:S(2)}, u32[]{:S(2)}) collective-permute-start(bf16[3,256,512]{2,1,0:T(8,128)(2,1)S(1)} %get-tuple-element.91), channel_id=1, source_target_pairs={{0,1},{2,0},{4,2},{6,4},{7,6},{5,7},{3,5},{1,3},{8,9},{10,8},{12,1... | collective-permute-start | bytes 2359304 | tf_op jit(solution)/shard_map/ppermute | solution.py:576
  96.8 27.8 %copy-start = (bf16[512,2048]{1,0:T(8,128)(2,1)}, bf16[512,2048]{1,0:T(8,128)(2,1)S(1)}, u32[]{:S(2)}) copy-start(bf16[512,2048]{1,0:T(8,128)(2,1)S(1)} %turn.1.refs_9_.refs_0_) | copy-start | bytes 6291460
  109.8 31.2 %collective-permute-start.15 = (bf16[3,256,512]{2,1,0:T(8,128)(2,1)S(1)}, bf16[3,256,512]{2,1,0:T(8,128)(2,1)S(1)}, u32[]{:S(2)}, u32[]{:S(2)}) collective-permute-start(bf16[3,256,512]{2,1,0:T(8,128)(2,1)S(1)} %get-tuple-element.83), channel_id=1, source_target_pairs={{0,2},{2,4},{4,6},{6,7},{7,5},{5,3},{3,1},{1,0},{8,10},{10,12},{12... | collective-permute-start | bytes 2359304 | tf_op jit(solution)/shard_map/ppermute | solution.py:576
  112.5 29.0 %copy-start.32 = (bf16[256,1024]{1,0:T(8,128)(2,1)S(1)}, bf16[256,1024]{1,0:T(8,128)(2,1)}, u32[]{:S(2)}) copy-start(bf16[256,1024]{1,0:T(8,128)(2,1)} %d_out.3) | copy-start | bytes 1572868
  112.5 29.0 %collective-permute-start.16 = (bf16[3,256,512]{2,1,0:T(8,128)(2,1)S(1)}, bf16[3,256,512]{2,1,0:T(8,128)(2,1)S(1)}, u32[]{:S(2)}, u32[]{:S(2)}) collective-permute-start(bf16[3,256,512]{2,1,0:T(8,128)(2,1)S(1)} %get-tuple-element.84), channel_id=1, source_target_pairs={{0,1},{2,0},{4,2},{6,4},{7,6},{5,7},{3,5},{1,3},{8,9},{10,8},{12,1... | collective-permute-start | bytes 2359304 | tf_op jit(solution)/shard_map/ppermute | solution.py:576
  126.7 31.2 %collective-permute-start.23 = (bf16[3,256,512]{2,1,0:T(8,128)(2,1)S(1)}, bf16[3,256,512]{2,1,0:T(8,128)(2,1)S(1)}, u32[]{:S(2)}, u32[]{:S(2)}) collective-permute-start(bf16[3,256,512]{2,1,0:T(8,128)(2,1)S(1)} %get-tuple-element.92), channel_id=1, source_target_pairs={{0,2},{2,4},{4,6},{6,7},{7,5},{5,3},{3,1},{1,0},{8,10},{10,12},{12... | collective-permute-start | bytes 2359304 | tf_op jit(solution)/shard_map/ppermute | solution.py:576
  129.4 29.0 %collective-permute-start.24 = (bf16[3,256,512]{2,1,0:T(8,128)(2,1)S(1)}, bf16[3,256,512]{2,1,0:T(8,128)(2,1)S(1)}, u32[]{:S(2)}, u32[]{:S(2)}) collective-permute-start(bf16[3,256,512]{2,1,0:T(8,128)(2,1)S(1)} %get-tuple-element.93), channel_id=1, source_target_pairs={{0,1},{2,0},{4,2},{6,4},{7,6},{5,7},{3,5},{1,3},{8,9},{10,8},{12,1... | collective-permute-start | bytes 2359304 | tf_op jit(solution)/shard_map/ppermute | solution.py:576
  149.3 16.2 %copy-start.12 = (bf16[3,256,512]{2,1,0:T(8,128)(2,1)}, bf16[3,256,512]{2,1,0:T(8,128)(2,1)S(1)}, u32[]{:S(2)}) copy-start(bf16[3,256,512]{2,1,0:T(8,128)(2,1)S(1)} %get-tuple-element.97.refs_0_.refs_1_) | copy-start | bytes 2359300
  149.4 25.4 %collective-permute-start.25 = (bf16[3,256,512]{2,1,0:T(8,128)(2,1)S(1)}, bf16[3,256,512]{2,1,0:T(8,128)(2,1)S(1)}, u32[]{:S(2)}, u32[]{:S(2)}) collective-permute-start(bf16[3,256,512]{2,1,0:T(8,128)(2,1)S(1)} %get-tuple-element.97.refs_0_.refs_1_), channel_id=1, source_target_pairs={{0,2},{2,4},{4,6},{6,7},{7,5},{5,3},{3,1},{1,0},{8,10},{10,12},{12... | collective-permute-start | bytes 2359304 | tf_op jit(solution)/shard_map/ppermute | solution.py:576
  152.0 24.0 %collective-permute-start.28 = (bf16[3,256,512]{2,1,0:T(8,128)(2,1)S(1)}, bf16[3,256,512]{2,1,0:T(8,128)(2,1)S(1)}, u32[]{:S(2)}, u32[]{:S(2)}) collective-permute-start(bf16[3,256,512]{2,1,0:T(8,128)(2,1)S(1)} %get-tuple-element.97.refs_0_.refs_1_), channel_id=1, source_target_pairs={{0,1},{2,0},{4,2},{6,4},{7,6},{5,7},{3,5},{1,3},{8,9},{10,8},{12,1... | collective-permute-start | bytes 2359304 | tf_op jit(solution)/shard_map/ppermute | solution.py:576
  166.3 25.3 %collective-permute-start.35 = (bf16[3,256,512]{2,1,0:T(8,128)(2,1)S(1)}, bf16[3,256,512]{2,1,0:T(8,128)(2,1)S(1)}, u32[]{:S(2)}, u32[]{:S(2)}) collective-permute-start(bf16[3,256,512]{2,1,0:T(8,128)(2,1)S(1)} %get-tuple-element.104.refs_0_.refs_1_), channel_id=1, source_target_pairs={{0,2},{2,4},{4,6},{6,7},{7,5},{5,3},{3,1},{1,0},{8,10},{10,12},{12... | collective-permute-start | bytes 2359304 | tf_op jit(solution)/shard_map/ppermute | solution.py:576
  168.9 24.0 %collective-permute-start.38 = (bf16[3,256,512]{2,1,0:T(8,128)(2,1)S(1)}, bf16[3,256,512]{2,1,0:T(8,128)(2,1)S(1)}, u32[]{:S(2)}, u32[]{:S(2)}) collective-permute-start(bf16[3,256,512]{2,1,0:T(8,128)(2,1)S(1)} %get-tuple-element.104.refs_0_.refs_1_), channel_id=1, source_target_pairs={{0,1},{2,0},{4,2},{6,4},{7,6},{5,7},{3,5},{1,3},{8,9},{10,8},{12,1... | collective-permute-start | bytes 2359304 | tf_op jit(solution)/shard_map/ppermute | solution.py:576
  174.7 33.8 %collective-permute-start.26 = (bf16[3,256,512]{2,1,0:T(8,128)(2,1)S(1)}, bf16[3,256,512]{2,1,0:T(8,128)(2,1)}, u32[]{:S(2)}, u32[]{:S(2)}) collective-permute-start(bf16[3,256,512]{2,1,0:T(8,128)(2,1)S(1)} %collective-permute-done.25.refs_1_.refs_2_), channel_id=1, source_target_pairs={{0,2},{2,4},{4,6},{6,7},{7,5},{5,3},{3,1},{1,0},{8,10},{10,12},{12... | collective-permute-start | bytes 2359304 | tf_op jit(solution)/shard_map/ppermute | solution.py:576
  176.0 33.0 %collective-permute-start.29 = (bf16[3,256,512]{2,1,0:T(8,128)(2,1)S(1)}, bf16[3,256,512]{2,1,0:T(8,128)(2,1)}, u32[]{:S(2)}, u32[]{:S(2)}) collective-permute-start(bf16[3,256,512]{2,1,0:T(8,128)(2,1)S(1)} %collective-permute-done.28.refs_2_.refs_3_), channel_id=1, source_target_pairs={{0,1},{2,0},{4,2},{6,4},{7,6},{5,7},{3,5},{1,3},{8,9},{10,8},{12,1... | collective-permute-start | bytes 2359304 | tf_op jit(solution)/shard_map/ppermute | solution.py:576
  191.6 33.8 %collective-permute-start.36 = (bf16[3,256,512]{2,1,0:T(8,128)(2,1)S(1)}, bf16[3,256,512]{2,1,0:T(8,128)(2,1)}, u32[]{:S(2)}, u32[]{:S(2)}) collective-permute-start(bf16[3,256,512]{2,1,0:T(8,128)(2,1)S(1)} %collective-permute-done.35.refs_1_.refs_2_), channel_id=1, source_target_pairs={{0,2},{2,4},{4,6},{6,7},{7,5},{5,3},{3,1},{1,0},{8,10},{10,12},{12... | collective-permute-start | bytes 2359304 | tf_op jit(solution)/shard_map/ppermute | solution.py:576
  192.9 33.0 %collective-permute-start.39 = (bf16[3,256,512]{2,1,0:T(8,128)(2,1)S(1)}, bf16[3,256,512]{2,1,0:T(8,128)(2,1)}, u32[]{:S(2)}, u32[]{:S(2)}) collective-permute-start(bf16[3,256,512]{2,1,0:T(8,128)(2,1)S(1)} %collective-permute-done.38.refs_2_.refs_3_), channel_id=1, source_target_pairs={{0,1},{2,0},{4,2},{6,4},{7,6},{5,7},{3,5},{1,3},{8,9},{10,8},{12,1... | collective-permute-start | bytes 2359304 | tf_op jit(solution)/shard_map/ppermute | solution.py:576
  208.5 35.6 %collective-permute-start.27 = (bf16[3,256,512]{2,1,0:T(8,128)(2,1)}, bf16[3,256,512]{2,1,0:T(8,128)(2,1)}, u32[]{:S(2)}, u32[]{:S(2)}) collective-permute-start(bf16[3,256,512]{2,1,0:T(8,128)(2,1)} %collective-permute-done.26.refs_0_.refs_4_), channel_id=1, source_target_pairs={{0,2},{2,4},{4,6},{6,7},{7,5},{5,3},{3,1},{1,0},{8,10},{10,12},{12... | collective-permute-start | bytes 2359304 | tf_op jit(solution)/shard_map/ppermute | solution.py:576
  209.0 35.1 %collective-permute-start.30 = (bf16[3,256,512]{2,1,0:T(8,128)(2,1)}, bf16[3,256,512]{2,1,0:T(8,128)(2,1)}, u32[]{:S(2)}, u32[]{:S(2)}) collective-permute-start(bf16[3,256,512]{2,1,0:T(8,128)(2,1)} %collective-permute-done.29.refs_1_.refs_5_), channel_id=1, source_target_pairs={{0,1},{2,0},{4,2},{6,4},{7,6},{5,7},{3,5},{1,3},{8,9},{10,8},{12,1... | collective-permute-start | bytes 2359304 | tf_op jit(solution)/shard_map/ppermute | solution.py:576
  225.4 33.7 %collective-permute-start.37 = (bf16[3,256,512]{2,1,0:T(8,128)(2,1)}, bf16[3,256,512]{2,1,0:T(8,128)(2,1)}, u32[]{:S(2)}, u32[]{:S(2)}) collective-permute-start(bf16[3,256,512]{2,1,0:T(8,128)(2,1)} %collective-permute-done.36.refs_0_.refs_4_), channel_id=1, source_target_pairs={{0,2},{2,4},{4,6},{6,7},{7,5},{5,3},{3,1},{1,0},{8,10},{10,12},{12... | collective-permute-start | bytes 2359304 | tf_op jit(solution)/shard_map/ppermute | solution.py:576
  225.8 33.7 %collective-permute-start.40 = (bf16[3,256,512]{2,1,0:T(8,128)(2,1)}, bf16[3,256,512]{2,1,0:T(8,128)(2,1)}, u32[]{:S(2)}, u32[]{:S(2)}) collective-permute-start(bf16[3,256,512]{2,1,0:T(8,128)(2,1)} %collective-permute-done.39.refs_1_.refs_5_), channel_id=1, source_target_pairs={{0,1},{2,0},{4,2},{6,4},{7,6},{5,7},{3,5},{1,3},{8,9},{10,8},{12,1... | collective-permute-start | bytes 2359304 | tf_op jit(solution)/shard_map/ppermute | solution.py:576
  227.8 1.4 collective-permute-start.31
  229.3 5.6 %collective-permute-start.32 = (f32[256,1]{1,0:T(8,128)S(1)}, f32[256,1]{1,0:T(8,128)S(1)}, u32[]{:S(2)}, u32[]{:S(2)}) collective-permute-start(f32[256,1]{1,0:T(8,128)S(1)} %add.63), channel_id=1, source_target_pairs={{0,16},{8,24},{16,0},{24,8},{1,17},{9,25},{17,1},{25,9},{2,18},{10... | collective-permute-start | bytes 3080 | tf_op jit(solution)/shard_map/ppermute | solution.py:579
  241.2 18.4 %copy-start.22 = (f32[256,512]{1,0:T(8,128)}, f32[256,512]{1,0:T(8,128)S(1)}, u32[]{:S(2)}) copy-start(f32[256,512]{1,0:T(8,128)S(1)} %get-tuple-element.108.refs_2_.refs_4_) | copy-start | bytes 1572868
  241.2 18.4 %copy-start.24 = (f32[256,512]{1,0:T(8,128)}, f32[256,512]{1,0:T(8,128)S(1)}, u32[]{:S(2)}) copy-start(f32[256,512]{1,0:T(8,128)S(1)} %get-tuple-element.109.refs_3_.refs_5_) | copy-start | bytes 1572868
  241.2 18.4 %copy-start.26 = (f32[256,512]{1,0:T(8,128)}, f32[256,512]{1,0:T(8,128)S(1)}, u32[]{:S(2)}) copy-start(f32[256,512]{1,0:T(8,128)S(1)} %get-tuple-element.110.refs_4_.refs_6_) | copy-start | bytes 1572868
  246.4 22.8 %collective-permute-start.33 = (bf16[3,128,512]{2,1,0:T(8,128)(2,1)}, bf16[3,128,512]{2,1,0:T(8,128)(2,1)}, u32[]{:S(2)}, u32[]{:S(2)}) collective-permute-start(bf16[3,128,512]{2,1,0:T(8,128)(2,1)} %get-tuple-element.100), channel_id=1, source_target_pairs={{0,2},{2,4},{4,6},{6,7},{7,5},{5,3},{3,1},{1,0},{8,10},{10,12},{12... | collective-permute-start | bytes 1179656 | tf_op jit(solution)/shard_map/ppermute | solution.py:576
  247.6 21.6 %collective-permute-start.34 = (bf16[3,128,512]{2,1,0:T(8,128)(2,1)}, bf16[3,128,512]{2,1,0:T(8,128)(2,1)}, u32[]{:S(2)}, u32[]{:S(2)}) collective-permute-start(bf16[3,128,512]{2,1,0:T(8,128)(2,1)} %get-tuple-element.101), channel_id=1, source_target_pairs={{0,1},{2,0},{4,2},{6,4},{7,6},{5,7},{3,5},{1,3},{8,9},{10,8},{12,1... | collective-permute-start | bytes 1179656 | tf_op jit(solution)/shard_map/ppermute | solution.py:576
  261.9 13.7 %collective-permute-start.41 = (bf16[3,128,512]{2,1,0:T(8,128)(2,1)}, bf16[3,128,512]{2,1,0:T(8,128)(2,1)S(1)}, u32[]{:S(2)}, u32[]{:S(2)}) collective-permute-start(bf16[3,128,512]{2,1,0:T(8,128)(2,1)} %get-tuple-element.115), channel_id=1, source_target_pairs={{0,2},{2,4},{4,6},{6,7},{7,5},{5,3},{3,1},{1,0},{8,10},{10,12},{12... | collective-permute-start | bytes 1179656 | tf_op jit(solution)/shard_map/ppermute | solution.py:576
  264.5 11.1 %collective-permute-start.42 = (bf16[3,128,512]{2,1,0:T(8,128)(2,1)}, bf16[3,128,512]{2,1,0:T(8,128)(2,1)}, u32[]{:S(2)}, u32[]{:S(2)}) collective-permute-start(bf16[3,128,512]{2,1,0:T(8,128)(2,1)} %get-tuple-element.116), channel_id=1, source_target_pairs={{0,1},{2,0},{4,2},{6,4},{7,6},{5,7},{3,5},{1,3},{8,9},{10,8},{12,1... | collective-permute-start | bytes 1179656 | tf_op jit(solution)/shard_map/ppermute | solution.py:576
  280.7 13.6 %copy-start.1 = (bf16[512,2048]{1,0:T(8,128)(2,1)S(1)}, bf16[512,2048]{1,0:T(8,128)(2,1)}, u32[]{:S(2)}) copy-start(bf16[512,2048]{1,0:T(8,128)(2,1)} %copy-done) | copy-start | bytes 6291460
  280.7 13.6 %copy-start.14 = (bf16[3,256,512]{2,1,0:T(8,128)(2,1)S(1)}, bf16[3,256,512]{2,1,0:T(8,128)(2,1)}, u32[]{:S(2)}) copy-start(bf16[3,256,512]{2,1,0:T(8,128)(2,1)} %copy-done.12) | copy-start | bytes 2359300
  280.7 6.6 %collective-permute-start.43 = (bf16[4,128,512]{2,1,0:T(8,128)(2,1)}, bf16[4,128,512]{2,1,0:T(8,128)(2,1)}, u32[]{:S(2)}, u32[]{:S(2)}) collective-permute-start(bf16[4,128,512]{2,1,0:T(8,128)(2,1)} %get-tuple-element.122), channel_id=1, source_target_pairs={{0,8},{8,0},{16,24},{24,16},{1,9},{9,1},{17,25},{25,17},{2,10},{10... | collective-permute-start | bytes 1572872 | tf_op jit(solution)/shard_map/ppermute | solution.py:579
  280.7 9.6 %collective-permute-start.47 = (bf16[4,128,512]{2,1,0:T(8,128)(2,1)}, bf16[4,128,512]{2,1,0:T(8,128)(2,1)}, u32[]{:S(2)}, u32[]{:S(2)}) collective-permute-start(bf16[4,128,512]{2,1,0:T(8,128)(2,1)} %get-tuple-element.128), channel_id=1, source_target_pairs={{0,8},{8,0},{16,24},{24,16},{1,9},{9,1},{17,25},{25,17},{2,10},{10... | collective-permute-start | bytes 1572872 | tf_op jit(solution)/shard_map/ppermute | solution.py:579
  282.1 12.1 %copy-start.17 = (bf16[3,256,512]{2,1,0:T(8,128)(2,1)S(1)}, bf16[3,256,512]{2,1,0:T(8,128)(2,1)}, u32[]{:S(2)}) copy-start(bf16[3,256,512]{2,1,0:T(8,128)(2,1)} %copy-done.15) | copy-start | bytes 2359300
  282.1 12.1 %copy-start.20 = (bf16[3,256,512]{2,1,0:T(8,128)(2,1)S(1)}, bf16[3,256,512]{2,1,0:T(8,128)(2,1)}, u32[]{:S(2)}) copy-start(bf16[3,256,512]{2,1,0:T(8,128)(2,1)} %copy-done.18) | copy-start | bytes 2359300
  289.7 11.0 %collective-permute-start.44 = (bf16[2,128,512]{2,1,0:T(8,128)(2,1)S(1)}, bf16[2,128,512]{2,1,0:T(8,128)(2,1)S(1)}, u32[]{:S(2)}, u32[]{:S(2)}) collective-permute-start(bf16[2,128,512]{2,1,0:T(8,128)(2,1)S(1)} %get-tuple-element.124), channel_id=1, source_target_pairs={{0,16},{8,24},{16,0},{24,8},{1,17},{9,25},{17,1},{25,9},{2,18},{10... | collective-permute-start | bytes 786440 | tf_op jit(solution)/shard_map/ppermute | solution.py:579
  292.6 22.1 %copy-start.5 = (bf16[3,256,512]{2,1,0:T(8,128)(2,1)S(1)}, bf16[3,256,512]{2,1,0:T(8,128)(2,1)}, u32[]{:S(2)}) copy-start(bf16[3,256,512]{2,1,0:T(8,128)(2,1)} %copy-done.3) | copy-start | bytes 2359300
  292.7 22.1 %copy-start.8 = (bf16[3,256,512]{2,1,0:T(8,128)(2,1)S(1)}, bf16[3,256,512]{2,1,0:T(8,128)(2,1)}, u32[]{:S(2)}) copy-start(bf16[3,256,512]{2,1,0:T(8,128)(2,1)} %copy-done.6) | copy-start | bytes 2359300
  292.7 22.1 %copy-start.11 = (bf16[3,256,512]{2,1,0:T(8,128)(2,1)S(1)}, bf16[3,256,512]{2,1,0:T(8,128)(2,1)}, u32[]{:S(2)}) copy-start(bf16[3,256,512]{2,1,0:T(8,128)(2,1)} %copy-done.9) | copy-start | bytes 2359300
  292.7 15.7 %collective-permute-start.48 = (bf16[2,128,512]{2,1,0:T(8,128)(2,1)S(1)}, bf16[2,128,512]{2,1,0:T(8,128)(2,1)S(1)}, u32[]{:S(2)}, u32[]{:S(2)}) collective-permute-start(bf16[2,128,512]{2,1,0:T(8,128)(2,1)S(1)} %get-tuple-element.130), channel_id=1, source_target_pairs={{0,16},{8,24},{16,0},{24,8},{1,17},{9,25},{17,1},{25,9},{2,18},{10... | collective-permute-start | bytes 786440 | tf_op jit(solution)/shard_map/ppermute | solution.py:579
  301.2 21.4 %collective-permute-start.45 = (bf16[128,512]{1,0:T(8,128)(2,1)S(1)}, bf16[128,512]{1,0:T(8,128)(2,1)S(1)}, u32[]{:S(2)}, u32[]{:S(2)}) collective-permute-start(bf16[128,512]{1,0:T(8,128)(2,1)S(1)} %get-tuple-element.125), channel_id=1, source_target_pairs={{0,0},{1,1},{2,8},{3,9},{4,16},{5,17},{6,24},{7,25},{8,2},{9,3},{1... | collective-permute-start | bytes 393224 | tf_op jit(solution)/shard_map/ppermute | solution.py:640
  307.4 18.7 %collective-permute-start.46 = (bf16[128,512]{1,0:T(8,128)(2,1)S(1)}, bf16[128,512]{1,0:T(8,128)(2,1)S(1)}, u32[]{:S(2)}, u32[]{:S(2)}) collective-permute-start(bf16[128,512]{1,0:T(8,128)(2,1)S(1)} %get-tuple-element.126), channel_id=1, source_target_pairs={{0,1},{1,0},{2,9},{3,8},{4,17},{5,16},{6,25},{7,24},{8,3},{9,2},{1... | collective-permute-start | bytes 393224 | tf_op jit(solution)/shard_map/ppermute | solution.py:640
  308.9 19.3 %collective-permute-start.49 = (bf16[128,512]{1,0:T(8,128)(2,1)S(1)}, bf16[128,512]{1,0:T(8,128)(2,1)S(1)}, u32[]{:S(2)}, u32[]{:S(2)}) collective-permute-start(bf16[128,512]{1,0:T(8,128)(2,1)S(1)} %get-tuple-element.131), channel_id=1, source_target_pairs={{0,0},{1,1},{2,8},{3,9},{4,16},{5,17},{6,24},{7,25},{8,2},{9,3},{1... | collective-permute-start | bytes 393224 | tf_op jit(solution)/shard_map/ppermute | solution.py:640
  312.3 19.3 %collective-permute-start.50 = (bf16[128,512]{1,0:T(8,128)(2,1)S(1)}, bf16[128,512]{1,0:T(8,128)(2,1)S(1)}, u32[]{:S(2)}, u32[]{:S(2)}) collective-permute-start(bf16[128,512]{1,0:T(8,128)(2,1)S(1)} %get-tuple-element.132), channel_id=1, source_target_pairs={{0,1},{1,0},{2,9},{3,8},{4,17},{5,16},{6,25},{7,24},{8,3},{9,2},{1... | collective-permute-start | bytes 393224 | tf_op jit(solution)/shard_map/ppermute | solution.py:640
  (29 other events, 117.6 us)

commit v7 on v6

--- a/solution.py
+++ b/solution.py
@@ -88,6 +88,8 @@
                 + [(o // 2) * group + seq % group for o, seq in zip(owner, seqs)]
                 + [node >> level & 1 for level in range(1, nodes.bit_length() - 1)]
                 + [(here + turn) % group for turn in range(group)]
+                + [(here - turn) % group for turn in range(group)]
+                + [node]
             )
     return np.array(rows, np.int32)
 
@@ -422,9 +424,10 @@
     refs[-1][0] = mm(turned[...], blocks)
 
 
-def grads_chunk(turned, pieces, before, chunk, wide, columns):
+def grads_chunk(turned, pieces, before, ties, chunk, wide, columns):
     depth, span = turned.shape
-    ties = [] if before is None else [before]
+    aliases = {} if before is None else {1 + len(pieces): 0}
+    ties = ties if before is None else [before, *ties]
     return pl.pallas_call(
         tied(grads_kernel, 1 + len(pieces), len(ties)),
         grid=(3,),
@@ -435,7 +438,7 @@
         ],
         out_specs=pl.BlockSpec((1, depth, wide), lambda m: (m, 0, chunk)),
         out_shape=jax.ShapeDtypeStruct((3, depth, columns), jnp.float32),
-        input_output_aliases={1 + len(pieces): 0} if ties else {},
+        input_output_aliases=aliases,
         compiler_params=params(24),
         cost_estimate=cost(6 * span * depth * wide, 6 * span * wide + 12 * depth * wide),
         name="grads",
@@ -554,6 +557,48 @@
         cost_estimate=cost(0, 8 * count * keep.shape[1] * keep.shape[2]),
         name="order_sum",
     )(idx, keep, came)
+
+
+def finish_kernel(column, width, idx, tokens, gain, inverse, dots, *refs):
+    came, out, gains = refs[:-2], refs[-2], refs[-1]
+    rows, depth = came[0].shape
+    group = out.shape[1] // depth
+    gains[...] = gain[...].astype(jnp.float32)
+    for turn in range(group):
+        features = pl.ds(pl.multiple_of(idx[column + turn] * depth, depth), depth)
+        for part in range(len(came) // group):
+            span = slice(part * rows, (part + 1) * rows)
+            scale = inverse[span, :1]
+            upstream = came[part * group + turn][...].astype(jnp.float32)
+            values = tokens[span, features].astype(jnp.float32)
+            common = scale * scale * dots[span] / width
+            out[span, features] = (
+                scale * gains[:, features] * upstream - values * common
+            ).astype(jnp.bfloat16)
+
+
+def finish(idx, column, tokens, gain, inverse, dots, came, share):
+    length, width = tokens.shape
+    node = column + share // came[0].shape[1]
+    whole = pl.BlockSpec(memory_space=pltpu.VMEM)
+    return pl.pallas_call(
+        functools.partial(finish_kernel, column, width),
+        grid_spec=pltpu.PrefetchScalarGridSpec(
+            num_scalar_prefetch=1,
+            grid=(1,),
+            in_specs=[
+                pl.BlockSpec((length, share), lambda i, idx: (0, idx[node])),
+                pl.BlockSpec((1, share), lambda i, idx: (0, idx[node])),
+                *[whole] * (2 + len(came)),
+            ],
+            out_specs=pl.BlockSpec((length, share), lambda i, idx: (0, 0)),
+            scratch_shapes=[pltpu.VMEM((1, share), jnp.float32)],
+        ),
+        out_shape=jax.ShapeDtypeStruct((length, share), jnp.bfloat16),
+        compiler_params=params(12),
+        cost_estimate=cost(8 * length * share, 6 * length * share),
+        name="finish",
+    )(idx, tokens, gain, inverse, dots, *came)
 
 
 def local(tokens, norm_gain, w_quant, w_scale, d_out):
@@ -617,21 +662,18 @@
         dots = dots + swap(dots, bit)
         bit *= 2
 
-    half = length // 2
-    share = width // nodes
-    values_part = lax.dynamic_slice_in_dim(tokens, node * share, share, 1).astype(jnp.float32)
-    gains_part = lax.dynamic_slice_in_dim(norm_gain, node * share, share, 0).astype(jnp.float32)
-    inverse_rms = inverse_rms[:, :1]
-
-    def to_place(keep, send):
+    def sum_nodes(keep, send):
         column = 4 * size + 1
         bit = 1
         while 2 * bit < nodes:
             keep, send = split_sum(idx, column, group, keep, swap(send, bit))
             column += 1
             bit *= 2
+        return order_sum(idx, column, keep, swap(send, bit))
+
+    def relocate(blocks):
         came = []
-        for turn, block in enumerate(order_sum(idx, column, keep, swap(send, bit))):
+        for turn, block in enumerate(blocks):
             moves = [
                 (n * size + s, (s // group) * size + n * group + (s + turn) % group)
                 for n in range(nodes)
@@ -639,22 +681,6 @@
             ]
             came.append(lax.ppermute(block, ("node", "local"), moves))
         return came
-
-    def end_term(came, part):
-        came = jnp.stack(came)
-        upstream = jnp.concatenate(
-            [
-                lax.dynamic_index_in_dim(came, (here + group - i) % group, 0, keepdims=False)
-                for i in range(group)
-            ],
-            axis=-1,
-        ).astype(jnp.float32)
-        rows = slice(part * half, (part + 1) * half)
-        d_rows = (
-            inverse_rms[rows] * gains_part * upstream
-            - values_part[rows] * inverse_rms[rows] ** 2 * dots[rows] / width
-        )
-        return d_rows.astype(jnp.bfloat16)
 
     gathered = [[block] for block in sets]
     moving = [(block, block) for block in sets]
@@ -676,10 +702,15 @@
             elif chunk == 0:
                 lasts = term_step(turned, [right, left], [], 0)
     keep_0, keep_1, send_0, send_1 = term_last(idx, turned, lasts, gathered[1][-2:], terms[1])
-    first, second = to_place(keep_0, send_0), to_place(keep_1, send_1)
-    d_tokens = jnp.concatenate([end_term(first, 0), end_term(second, 1)], axis=0)
-    grads = grads_chunk(rows_turned, gathered[0], None, 0, wide, columns)
-    grads = grads_chunk(rows_turned, gathered[1], grads, 1, wide, columns)
+    first, second = sum_nodes(keep_0, send_0), sum_nodes(keep_1, send_1)
+    came = [*relocate(first), *relocate(second)]
+    column = idx.shape[0] - 1 - group
+    d_tokens = finish(
+        idx, column, tokens, norm_gain[None], inverse_rms, dots, came, width // nodes
+    )
+    sums = [first[0], second[0]]
+    grads = grads_chunk(rows_turned, gathered[0], None, sums, 0, wide, columns)
+    grads = grads_chunk(rows_turned, gathered[1], grads, [], 1, wide, columns)
     return (jnp.concatenate(outputs, axis=-1), d_tokens, grads)
 
 

time: 334 us -> 320 us (0.958)
  starting transfers between devices: 70.1 us -> 65.3 us
  Pallas kernels: 70.7 us -> 66.4 us
  local copies, waits for them, and re-layouts: 21.2 us -> 17.1 us
    ppermute x4, waiting for transfers between devices: 10.5 us -> 0.01 us  [relocate(): came.append(lax.ppermute(block, ('node', 'local'), moves))]
    ppermute x8, waiting for transfers between devices: 6.37 us -> 13.5 us  [swap(): return lax.ppermute(array, 'node', [(n, n ^ bit) for n in range(nodes)])]
    ppermute x39, waiting for transfers between devices: 145 us -> 151 us  [shift(): return lax.ppermute(array, 'local', moves)]
    ppermute x39, starting transfers between devices: 53.8 us -> 49.5 us  [shift(): return lax.ppermute(array, 'local', moves)]
    unnamed x84 -> x56, local copies, waits for them, and re-layouts: 18.7 us -> 14.9 us
  transfers between devices with their start and end apart: 51 -> 51, of which waited for: 30 -> 24; matrix products, arithmetic and copies ran while one was open for 2% -> 2% of each run, Pallas kernels for 20% -> 19%
where the time goes in v7:
time: 320 us; the launch traced here: 319 us
  waiting for transfers between devices  164 us (51%)
  Pallas kernels  66.4 us (21%)
  starting transfers between devices  65.3 us (20%)
  local copies, waits for them, and re-layouts  17.1 us (5%)
  other arithmetic  4.53 us (1%)
    ppermute x39, waiting for transfers between devices, shift(): return lax.ppermute(array, 'local', moves)  151 us
    ppermute x39, starting transfers between devices, shift(): return lax.ppermute(array, 'local', moves)  49.5 us
    unnamed x56, local copies, waits for them, and re-layouts  14.9 us
    pallas_call x2, Pallas kernels, attention(): pl.pallas_call(attention_kernel, grid_spec=pltpu.PrefetchScalarGridSpec(n...  14.5 us
    ppermute x8, waiting for transfers between devices, swap(): return lax.ppermute(array, 'node', [(n, n ^ bit) for n in range(nodes)])  13.5 us
    pallas_call x7, Pallas kernels, term_step(): pl.pallas_call(kernel, in_specs=[whole] * (1 + count + len(befores)), out...  12.7 us
    pallas_call x2, Pallas kernels, grads_chunk(): pl.pallas_call(tied(grads_kernel, 1 + len(pieces), len(ties)), grid=(3,),...  12.7 us
    ppermute x4, starting transfers between devices, relocate(): came.append(lax.ppermute(block, ('node', 'local'), moves))  12.5 us
  transfers between devices with their start and end apart: 51, of which 24 were waited for; matrix products, arithmetic and copies ran while one was open for 2% of the time, Pallas kernels for 19%

profile of v7, /device:TPU:2, one launch (start us, length us, event | category | flops | bytes accessed | tf_op | source)
XLA Modules:
  0.0 318.7 jit_solution(5949864835685014529)
XLA Ops:
  2.0 1.6 copy-done.2
  5.7 4.6 %collective-permute-start.6 = (bf16[256,256]{1,0:T(8,128)(2,1)S(1)}, bf16[256,256]{1,0:T(8,128)(2,1)S(1)}, u32[]{:S(2)}, u32[]{:S(2)}) collective-permute-start(bf16[256,256]{1,0:T(8,128)(2,1)S(1)} %get-tuple-element.75), channel_id=1, source_target_pairs={{0,7},{2,5},{4,3},{6,1},{7,0},{5,2},{3,4},{1,6},{8,15},{10,13},{12... | collective-permute-start | bytes 393224 | tf_op jit(solution)/shard_map/ppermute | solution.py:621
  10.3 4.5 %collective-permute-done.6.mine.mine_far = bf16[256,256]{1,0:T(8,128)(2,1)S(1)} collective-permute-done((bf16[256,256]{1,0:T(8,128)(2,1)S(1)}, bf16[256,256]{1,0:T(8,128)(2,1)S(1)}, u32[]{:S(2)}, u32[]{:S(2)}) %collective-permute-start.6) | collective-permute-done | bytes 131104 | tf_op jit(solution)/shard_map/ppermute | solution.py:621
  15.3 3.4 %collective-permute-start.2 = (bf16[256,256]{1,0:T(8,128)(2,1)S(1)}, bf16[256,256]{1,0:T(8,128)(2,1)S(1)}, u32[]{:S(2)}, u32[]{:S(2)}) collective-permute-start(bf16[256,256]{1,0:T(8,128)(2,1)S(1)} %get-tuple-element.71), channel_id=1, source_target_pairs={{0,4},{2,6},{4,7},{6,5},{7,3},{5,1},{3,0},{1,2},{8,12},{10,14},{12... | collective-permute-start | bytes 393224 | tf_op jit(solution)/shard_map/ppermute | solution.py:621
  19.9 1.7 collective-permute-start.4
  21.7 2.1 collective-permute-start.5
  23.8 1.9 copy-done.19
  27.5 1.9 sum_first.1
  29.4 4.6 %collective-permute-done.3.refs_4_ = bf16[256,256]{1,0:T(8,128)(2,1)S(1)} collective-permute-done((bf16[256,256]{1,0:T(8,128)(2,1)S(1)}, bf16[256,256]{1,0:T(8,128)(2,1)S(1)}, u32[]{:S(2)}, u32[]{:S(2)}) %collective-permute-start.3) | collective-permute-done | bytes 131104 | tf_op jit(solution)/shard_map/ppermute | solution.py:621
  35.2 3.1 collective-permute-start.10
  38.4 2.1 collective-permute-start.18
  40.4 7.4 %collective-permute-done.10.refs_8_ = bf16[3,128,512]{2,1,0:T(8,128)(2,1)S(1)} collective-permute-done((bf16[3,128,512]{2,1,0:T(8,128)(2,1)S(1)}, bf16[3,128,512]{2,1,0:T(8,128)(2,1)S(1)}, u32[]{:S(2)}, u32[]{:S(2)}) %collective-permute-start.10) | collective-permute-done | bytes 393248 | tf_op jit(solution)/shard_map/ppermute | solution.py:621
  47.8 2.5 collective-permute-done.9.refs_7_
  50.3 2.1 sum_step.6
  52.4 2.0 collective-permute-start.12
  54.5 4.3 %collective-permute-done.17.refs_7_ = bf16[3,128,512]{2,1,0:T(8,128)(2,1)S(1)} collective-permute-done((bf16[3,128,512]{2,1,0:T(8,128)(2,1)S(1)}, bf16[3,128,512]{2,1,0:T(8,128)(2,1)S(1)}, u32[]{:S(2)}, u32[]{:S(2)}) %collective-permute-start.17) | collective-permute-done | bytes 393248 | tf_op jit(solution)/shard_map/ppermute | solution.py:621
  58.7 2.1 sum_step.9
  60.9 2.0 collective-permute-start.20
  62.9 12.7 %collective-permute-done.11.refs_7_ = bf16[3,256,512]{2,1,0:T(8,128)(2,1)S(1)} collective-permute-done((bf16[3,256,512]{2,1,0:T(8,128)(2,1)S(1)}, bf16[3,256,512]{2,1,0:T(8,128)(2,1)S(1)}, u32[]{:S(2)}, u32[]{:S(2)}) %collective-permute-start.11) | collective-permute-done | bytes 786464 | tf_op jit(solution)/shard_map/ppermute | solution.py:621
  75.6 2.1 sum_step.7
  77.7 2.0 collective-permute-start.14
  79.7 12.7 %collective-permute-done.19.refs_7_ = bf16[3,256,512]{2,1,0:T(8,128)(2,1)S(1)} collective-permute-done((bf16[3,256,512]{2,1,0:T(8,128)(2,1)S(1)}, bf16[3,256,512]{2,1,0:T(8,128)(2,1)S(1)}, u32[]{:S(2)}, u32[]{:S(2)}) %collective-permute-start.19) | collective-permute-done | bytes 786464 | tf_op jit(solution)/shard_map/ppermute | solution.py:621
  92.4 2.1 sum_step.10
  94.6 2.0 collective-permute-start.22
  97.8 11.5 %collective-permute-done.13.refs_7_ = bf16[3,256,512]{2,1,0:T(8,128)(2,1)S(1)} collective-permute-done((bf16[3,256,512]{2,1,0:T(8,128)(2,1)S(1)}, bf16[3,256,512]{2,1,0:T(8,128)(2,1)S(1)}, u32[]{:S(2)}, u32[]{:S(2)}) %collective-permute-start.13) | collective-permute-done | bytes 786464 | tf_op jit(solution)/shard_map/ppermute | solution.py:621
  109.3 2.1 sum_step.8
  111.4 2.0 collective-permute-start.16
  113.4 12.7 %collective-permute-done.21.refs_7_ = bf16[3,256,512]{2,1,0:T(8,128)(2,1)S(1)} collective-permute-done((bf16[3,256,512]{2,1,0:T(8,128)(2,1)S(1)}, bf16[3,256,512]{2,1,0:T(8,128)(2,1)S(1)}, u32[]{:S(2)}, u32[]{:S(2)}) %collective-permute-start.21) | collective-permute-done | bytes 786464 | tf_op jit(solution)/shard_map/ppermute | solution.py:621
  126.2 2.1 sum_step.11
  128.3 2.0 collective-permute-start.24
  131.0 12.0 %collective-permute-done.15.from_left = bf16[3,256,512]{2,1,0:T(8,128)(2,1)S(1)} collective-permute-done((bf16[3,256,512]{2,1,0:T(8,128)(2,1)S(1)}, bf16[3,256,512]{2,1,0:T(8,128)(2,1)S(1)}, u32[]{:S(2)}, u32[]{:S(2)}) %collective-permute-start.15) | collective-permute-done | bytes 786464 | tf_op jit(solution)/shard_map/ppermute | solution.py:621
  143.0 7.2 %attention.2 = (bf16[256,512]{1,0:T(8,128)(2,1)S(1)}, f32[256,128]{1,0:T(8,128)S(1)}, bf16[3,256,512]{2,1,0:T(8,128)(2,1)S(1)}) custom-call(s32[39]{0:T(128)S(1)} %dynamic-slice_bitcast_fusion.idx.refs_0_, bf16[7,256,256]{2,1,0:T(8,128)(2,1)S(1)} %stack.1.refs_1_.refs_3_.mine, bf16[7,256,256]{2,1,0:T(8,128)(2,1)S(1)} %collective-permute-done.8.refs_2_.refs_4_.other, ...), custom_call_target="tpu_custom_call" | custom-call | flops 402653184 | bytes 3145728 | tf_op jit(solution)/shard_map/attention/pallas_call | solution.py:389
  151.0 2.0 collective-permute-start.27
  152.9 6.9 %collective-permute-done.23.from_left = bf16[3,256,512]{2,1,0:T(8,128)(2,1)S(1)} collective-permute-done((bf16[3,256,512]{2,1,0:T(8,128)(2,1)S(1)}, bf16[3,256,512]{2,1,0:T(8,128)(2,1)S(1)}, u32[]{:S(2)}, u32[]{:S(2)}) %collective-permute-start.23) | collective-permute-done | bytes 786464 | tf_op jit(solution)/shard_map/ppermute | solution.py:621
  159.9 7.3 %attention.3 = (bf16[256,512]{1,0:T(8,128)(2,1)S(1)}, f32[256,128]{1,0:T(8,128)S(1)}, bf16[3,256,512]{2,1,0:T(8,128)(2,1)S(1)}) custom-call(s32[39]{0:T(128)S(1)} %dynamic-slice_bitcast_fusion.idx.refs_0_, bf16[7,256,256]{2,1,0:T(8,128)(2,1)S(1)} %stack.1.refs_1_.refs_3_.mine, bf16[7,256,256]{2,1,0:T(8,128)(2,1)S(1)} %collective-permute-done.8.refs_2_.refs_4_.other, ...), custom_call_target="tpu_custom_call" | custom-call | flops 402653184 | bytes 3145728 | tf_op jit(solution)/shard_map/attention/pallas_call | solution.py:389
  168.6 2.0 collective-permute-start.35
  171.5 2.7 collective-permute-done.30.refs_2_.refs_3_
  174.2 2.5 collective-permute-start.31
  178.5 12.5 %collective-permute-done.38.refs_2_.refs_3_ = bf16[3,256,512]{2,1,0:T(8,128)(2,1)S(1)} collective-permute-done((bf16[3,256,512]{2,1,0:T(8,128)(2,1)S(1)}, bf16[3,256,512]{2,1,0:T(8,128)(2,1)S(1)}, u32[]{:S(2)}, u32[]{:S(2)}) %collective-permute-start.38) | collective-permute-done | bytes 786464 | tf_op jit(solution)/shard_map/ppermute | solution.py:621
  191.0 2.5 collective-permute-start.39
  195.3 12.6 %collective-permute-done.31.refs_1_.refs_5_ = bf16[3,256,512]{2,1,0:T(8,128)(2,1)} collective-permute-done((bf16[3,256,512]{2,1,0:T(8,128)(2,1)S(1)}, bf16[3,256,512]{2,1,0:T(8,128)(2,1)}, u32[]{:S(2)}, u32[]{:S(2)}) %collective-permute-start.31) | collective-permute-done | bytes 786464 | tf_op jit(solution)/shard_map/ppermute | solution.py:621
  207.9 2.6 collective-permute-start.32
  210.5 14.2 %collective-permute-done.39.refs_1_.refs_5_ = bf16[3,256,512]{2,1,0:T(8,128)(2,1)} collective-permute-done((bf16[3,256,512]{2,1,0:T(8,128)(2,1)S(1)}, bf16[3,256,512]{2,1,0:T(8,128)(2,1)}, u32[]{:S(2)}, u32[]{:S(2)}) %collective-permute-start.39) | collective-permute-done | bytes 786464 | tf_op jit(solution)/shard_map/ppermute | solution.py:621
  224.8 2.6 collective-permute-start.40
  230.2 1.6 collective-permute-done.25
  233.3 5.0 %collective-permute-done.26 = f32[256,1]{1,0:T(8,128)S(1)} collective-permute-done((f32[256,1]{1,0:T(8,128)S(1)}, f32[256,1]{1,0:T(8,128)S(1)}, u32[]{:S(2)}, u32[]{:S(2)}) %collective-permute-start.26) | collective-permute-done | bytes 1056 | tf_op jit(solution)/shard_map/ppermute | solution.py:624
  244.5 2.3 term_step.10
  250.5 2.3 term_step.11
  252.8 5.7 %collective-permute-done.40.refs_1_.refs_7_ = bf16[3,256,512]{2,1,0:T(8,128)(2,1)} collective-permute-done((bf16[3,256,512]{2,1,0:T(8,128)(2,1)}, bf16[3,256,512]{2,1,0:T(8,128)(2,1)}, u32[]{:S(2)}, u32[]{:S(2)}) %collective-permute-start.40) | collective-permute-done | bytes 786464 | tf_op jit(solution)/shard_map/ppermute | solution.py:621
  258.6 2.5 collective-permute-done.37.refs_0_.refs_6_
  262.6 2.0 collective-permute-start.42
  264.6 2.3 term_step.12
  266.9 2.3 term_step.13
  270.0 7.1 %collective-permute-done.41.refs_2_.refs_8_ = bf16[3,128,512]{2,1,0:T(8,128)(2,1)S(1)} collective-permute-done((bf16[3,128,512]{2,1,0:T(8,128)(2,1)S(1)}, bf16[3,128,512]{2,1,0:T(8,128)(2,1)S(1)}, u32[]{:S(2)}, u32[]{:S(2)}) %collective-permute-start.41) | collective-permute-done | bytes 393248 | tf_op jit(solution)/shard_map/ppermute | solution.py:621
  277.1 1.6 term_last.1
  282.6 1.6 collective-permute-start.48
  285.0 5.5 %collective-permute-done.44.came = bf16[2,128,512]{2,1,0:T(8,128)(2,1)S(1)} collective-permute-done((bf16[2,128,512]{2,1,0:T(8,128)(2,1)S(1)}, bf16[2,128,512]{2,1,0:T(8,128)(2,1)S(1)}, u32[]{:S(2)}, u32[]{:S(2)}) %collective-permute-start.44) | collective-permute-done | bytes 262176 | tf_op jit(solution)/shard_map/ppermute | solution.py:624
  291.2 2.4 collective-permute-start.46
  293.5 3.1 collective-permute-start.45
  297.3 3.4 %collective-permute-start.50 = (bf16[128,512]{1,0:T(8,128)(2,1)S(1)}, bf16[128,512]{1,0:T(8,128)(2,1)S(1)}, u32[]{:S(2)}, u32[]{:S(2)}) collective-permute-start(bf16[128,512]{1,0:T(8,128)(2,1)S(1)} %get-tuple-element.132), channel_id=1, source_target_pairs={{0,1},{1,0},{2,9},{3,8},{4,17},{5,16},{6,25},{7,24},{8,3},{9,2},{1... | collective-permute-start | bytes 393224 | tf_op jit(solution)/shard_map/ppermute | solution.py:682
  300.7 3.5 %collective-permute-start.49 = (bf16[128,512]{1,0:T(8,128)(2,1)S(1)}, bf16[128,512]{1,0:T(8,128)(2,1)S(1)}, u32[]{:S(2)}, u32[]{:S(2)}) collective-permute-start(bf16[128,512]{1,0:T(8,128)(2,1)S(1)} %get-tuple-element.131.refs_11_), channel_id=1, source_target_pairs={{0,0},{1,1},{2,8},{3,9},{4,16},{5,17},{6,24},{7,25},{8,2},{9,3},{1... | collective-permute-start | bytes 393224 | tf_op jit(solution)/shard_map/ppermute | solution.py:682
  304.3 6.3 %grads.2.refs_10_ = f32[3,512,1024]{2,1,0:T(8,128)} custom-call(bf16[512,2048]{1,0:T(8,128)(2,1)S(1)} %copy-done.1, bf16[3,256,512]{2,1,0:T(8,128)(2,1)S(1)} %copy-done.12, bf16[3,256,512]{2,1,0:T(8,128)(2,1)S(1)} %copy-done.18, bf16[3,256,512]{2,1,0:T(8,128)(2,1)S(1)} %copy-done.15, bf16[3,256,512]{2,1,0:T(8,128)(2,1)} %collective-permute-done.28.refs_0_.refs_4_, ...), custom_call_target="tpu_custom_call" | custom-call | flops 3221225472 | bytes 9437184 | tf_op jit(solution)/shard_map/grads/pallas_call | solution.py:431
  310.6 6.4 %grads.3 = f32[3,512,1024]{2,1,0:T(8,128)} custom-call(bf16[512,2048]{1,0:T(8,128)(2,1)S(1)} %copy-done.1, bf16[3,256,512]{2,1,0:T(8,128)(2,1)S(1)} %copy-done.5, bf16[3,256,512]{2,1,0:T(8,128)(2,1)S(1)} %copy-done.9, bf16[3,256,512]{2,1,0:T(8,128)(2,1)S(1)} %copy-done.7, ...), custom_call_target="tpu_custom_call", output_to_operand_aliasing={{}: (10, {})} | custom-call | flops 3221225472 | bytes 9437184 | tf_op jit(solution)/shard_map/grads/pallas_call | solution.py:431
  317.0 1.6 finish.1
  (137 shorter events, 39.4 us)
Async XLA Ops:
  5.7 9.1 %collective-permute-start.6 = (bf16[256,256]{1,0:T(8,128)(2,1)S(1)}, bf16[256,256]{1,0:T(8,128)(2,1)S(1)}, u32[]{:S(2)}, u32[]{:S(2)}) collective-permute-start(bf16[256,256]{1,0:T(8,128)(2,1)S(1)} %get-tuple-element.75), channel_id=1, source_target_pairs={{0,7},{2,5},{4,3},{6,1},{7,0},{5,2},{3,4},{1,6},{8,15},{10,13},{12... | collective-permute-start | bytes 393224 | tf_op jit(solution)/shard_map/ppermute | solution.py:621
  10.3 9.7 %collective-permute-start = (bf16[256,256]{1,0:T(8,128)(2,1)S(1)}, bf16[256,256]{1,0:T(8,128)(2,1)S(1)}, u32[]{:S(2)}, u32[]{:S(2)}) collective-permute-start(bf16[256,256]{1,0:T(8,128)(2,1)S(1)} %get-tuple-element.69), channel_id=1, source_target_pairs={{0,2},{2,4},{4,6},{6,7},{7,5},{5,3},{3,1},{1,0},{8,10},{10,12},{12... | collective-permute-start | bytes 393224 | tf_op jit(solution)/shard_map/ppermute | solution.py:621
  14.8 6.9 %collective-permute-start.7 = (bf16[256,256]{1,0:T(8,128)(2,1)S(1)}, bf16[256,256]{1,0:T(8,128)(2,1)S(1)}, u32[]{:S(2)}, u32[]{:S(2)}) collective-permute-start(bf16[256,256]{1,0:T(8,128)(2,1)S(1)} %collective-permute-done.6.mine.mine_far), channel_id=1, source_target_pairs={{0,8},{8,0},{16,24},{24,16},{1,9},{9,1},{17,25},{25,17},{2,10},{10... | collective-permute-start | bytes 393224 | tf_op jit(solution)/shard_map/ppermute | solution.py:624
  14.8 14.6 %collective-permute-start.1 = (bf16[256,256]{1,0:T(8,128)(2,1)S(1)}, bf16[256,256]{1,0:T(8,128)(2,1)S(1)}, u32[]{:S(2)}, u32[]{:S(2)}) collective-permute-start(bf16[256,256]{1,0:T(8,128)(2,1)S(1)} %get-tuple-element.70), channel_id=1, source_target_pairs={{0,1},{2,0},{4,2},{6,4},{7,6},{5,7},{3,5},{1,3},{8,9},{10,8},{12,1... | collective-permute-start | bytes 393224 | tf_op jit(solution)/shard_map/ppermute | solution.py:621
  15.3 14.1 %collective-permute-start.2 = (bf16[256,256]{1,0:T(8,128)(2,1)S(1)}, bf16[256,256]{1,0:T(8,128)(2,1)S(1)}, u32[]{:S(2)}, u32[]{:S(2)}) collective-permute-start(bf16[256,256]{1,0:T(8,128)(2,1)S(1)} %get-tuple-element.71), channel_id=1, source_target_pairs={{0,4},{2,6},{4,7},{6,5},{7,3},{5,1},{3,0},{1,2},{8,12},{10,14},{12... | collective-permute-start | bytes 393224 | tf_op jit(solution)/shard_map/ppermute | solution.py:621
  18.7 15.3 %collective-permute-start.3 = (bf16[256,256]{1,0:T(8,128)(2,1)S(1)}, bf16[256,256]{1,0:T(8,128)(2,1)S(1)}, u32[]{:S(2)}, u32[]{:S(2)}) collective-permute-start(bf16[256,256]{1,0:T(8,128)(2,1)S(1)} %get-tuple-element.72), channel_id=1, source_target_pairs={{0,3},{2,1},{4,0},{6,2},{7,4},{5,6},{3,7},{1,5},{8,11},{10,9},{12,... | collective-permute-start | bytes 393224 | tf_op jit(solution)/shard_map/ppermute | solution.py:621
  19.9 15.2 %collective-permute-start.4 = (bf16[256,256]{1,0:T(8,128)(2,1)S(1)}, bf16[256,256]{1,0:T(8,128)(2,1)S(1)}, u32[]{:S(2)}, u32[]{:S(2)}) collective-permute-start(bf16[256,256]{1,0:T(8,128)(2,1)S(1)} %get-tuple-element.73), channel_id=1, source_target_pairs={{0,6},{2,7},{4,5},{6,3},{7,1},{5,0},{3,2},{1,4},{8,14},{10,15},{12... | collective-permute-start | bytes 393224 | tf_op jit(solution)/shard_map/ppermute | solution.py:621
  21.7 13.4 %collective-permute-start.5 = (bf16[256,256]{1,0:T(8,128)(2,1)S(1)}, bf16[256,256]{1,0:T(8,128)(2,1)S(1)}, u32[]{:S(2)}, u32[]{:S(2)}) collective-permute-start(bf16[256,256]{1,0:T(8,128)(2,1)S(1)} %get-tuple-element.74), channel_id=1, source_target_pairs={{0,5},{2,3},{4,1},{6,0},{7,2},{5,4},{3,6},{1,7},{8,13},{10,11},{12... | collective-permute-start | bytes 393224 | tf_op jit(solution)/shard_map/ppermute | solution.py:621
  35.2 15.1 %collective-permute-start.8 = (bf16[7,256,256]{2,1,0:T(8,128)(2,1)S(1)}, bf16[7,256,256]{2,1,0:T(8,128)(2,1)S(1)}, u32[]{:S(2)}, u32[]{:S(2)}) collective-permute-start(bf16[7,256,256]{2,1,0:T(8,128)(2,1)S(1)} %stack.1.refs_1_.refs_3_.mine), channel_id=1, source_target_pairs={{0,8},{8,0},{16,24},{24,16},{1,9},{9,1},{17,25},{25,17},{2,10},{10... | collective-permute-start | bytes 2752520 | tf_op jit(solution)/shard_map/ppermute | solution.py:624
  35.2 12.5 %collective-permute-start.10 = (bf16[3,128,512]{2,1,0:T(8,128)(2,1)S(1)}, bf16[3,128,512]{2,1,0:T(8,128)(2,1)S(1)}, u32[]{:S(2)}, u32[]{:S(2)}) collective-permute-start(bf16[3,128,512]{2,1,0:T(8,128)(2,1)S(1)} %get-tuple-element.78), channel_id=1, source_target_pairs={{0,1},{2,0},{4,2},{6,4},{7,6},{5,7},{3,5},{1,3},{8,9},{10,8},{12,1... | collective-permute-start | bytes 1179656 | tf_op jit(solution)/shard_map/ppermute | solution.py:621
  38.4 12.0 %collective-permute-start.9 = (bf16[3,128,512]{2,1,0:T(8,128)(2,1)S(1)}, bf16[3,128,512]{2,1,0:T(8,128)(2,1)S(1)}, u32[]{:S(2)}, u32[]{:S(2)}) collective-permute-start(bf16[3,128,512]{2,1,0:T(8,128)(2,1)S(1)} %get-tuple-element.77.refs_7_), channel_id=1, source_target_pairs={{0,2},{2,4},{4,6},{6,7},{7,5},{5,3},{3,1},{1,0},{8,10},{10,12},{12... | collective-permute-start | bytes 1179656 | tf_op jit(solution)/shard_map/ppermute | solution.py:621
  38.4 20.4 %collective-permute-start.17 = (bf16[3,128,512]{2,1,0:T(8,128)(2,1)S(1)}, bf16[3,128,512]{2,1,0:T(8,128)(2,1)S(1)}, u32[]{:S(2)}, u32[]{:S(2)}) collective-permute-start(bf16[3,128,512]{2,1,0:T(8,128)(2,1)S(1)} %get-tuple-element.86), channel_id=1, source_target_pairs={{0,2},{2,4},{4,6},{6,7},{7,5},{5,3},{3,1},{1,0},{8,10},{10,12},{12... | collective-permute-start | bytes 1179656 | tf_op jit(solution)/shard_map/ppermute | solution.py:621
  38.4 20.4 %collective-permute-start.18 = (bf16[3,128,512]{2,1,0:T(8,128)(2,1)S(1)}, bf16[3,128,512]{2,1,0:T(8,128)(2,1)S(1)}, u32[]{:S(2)}, u32[]{:S(2)}) collective-permute-start(bf16[3,128,512]{2,1,0:T(8,128)(2,1)S(1)} %get-tuple-element.87), channel_id=1, source_target_pairs={{0,1},{2,0},{4,2},{6,4},{7,6},{5,7},{3,5},{1,3},{8,9},{10,8},{12,1... | collective-permute-start | bytes 1179656 | tf_op jit(solution)/shard_map/ppermute | solution.py:621
  52.4 23.2 %collective-permute-start.11 = (bf16[3,256,512]{2,1,0:T(8,128)(2,1)S(1)}, bf16[3,256,512]{2,1,0:T(8,128)(2,1)S(1)}, u32[]{:S(2)}, u32[]{:S(2)}) collective-permute-start(bf16[3,256,512]{2,1,0:T(8,128)(2,1)S(1)} %get-tuple-element.79), channel_id=1, source_target_pairs={{0,2},{2,4},{4,6},{6,7},{7,5},{5,3},{3,1},{1,0},{8,10},{10,12},{12... | collective-permute-start | bytes 2359304 | tf_op jit(solution)/shard_map/ppermute | solution.py:621
  52.4 23.1 %collective-permute-start.12 = (bf16[3,256,512]{2,1,0:T(8,128)(2,1)S(1)}, bf16[3,256,512]{2,1,0:T(8,128)(2,1)S(1)}, u32[]{:S(2)}, u32[]{:S(2)}) collective-permute-start(bf16[3,256,512]{2,1,0:T(8,128)(2,1)S(1)} %get-tuple-element.80), channel_id=1, source_target_pairs={{0,1},{2,0},{4,2},{6,4},{7,6},{5,7},{3,5},{1,3},{8,9},{10,8},{12,1... | collective-permute-start | bytes 2359304 | tf_op jit(solution)/shard_map/ppermute | solution.py:621
  60.8 31.6 %collective-permute-start.19 = (bf16[3,256,512]{2,1,0:T(8,128)(2,1)S(1)}, bf16[3,256,512]{2,1,0:T(8,128)(2,1)S(1)}, u32[]{:S(2)}, u32[]{:S(2)}) collective-permute-start(bf16[3,256,512]{2,1,0:T(8,128)(2,1)S(1)} %get-tuple-element.88), channel_id=1, source_target_pairs={{0,2},{2,4},{4,6},{6,7},{7,5},{5,3},{3,1},{1,0},{8,10},{10,12},{12... | collective-permute-start | bytes 2359304 | tf_op jit(solution)/shard_map/ppermute | solution.py:621
  60.9 31.6 %collective-permute-start.20 = (bf16[3,256,512]{2,1,0:T(8,128)(2,1)S(1)}, bf16[3,256,512]{2,1,0:T(8,128)(2,1)S(1)}, u32[]{:S(2)}, u32[]{:S(2)}) collective-permute-start(bf16[3,256,512]{2,1,0:T(8,128)(2,1)S(1)} %get-tuple-element.89), channel_id=1, source_target_pairs={{0,1},{2,0},{4,2},{6,4},{7,6},{5,7},{3,5},{1,3},{8,9},{10,8},{12,1... | collective-permute-start | bytes 2359304 | tf_op jit(solution)/shard_map/ppermute | solution.py:621
  77.7 31.6 %collective-permute-start.13 = (bf16[3,256,512]{2,1,0:T(8,128)(2,1)S(1)}, bf16[3,256,512]{2,1,0:T(8,128)(2,1)S(1)}, u32[]{:S(2)}, u32[]{:S(2)}) collective-permute-start(bf16[3,256,512]{2,1,0:T(8,128)(2,1)S(1)} %get-tuple-element.81), channel_id=1, source_target_pairs={{0,2},{2,4},{4,6},{6,7},{7,5},{5,3},{3,1},{1,0},{8,10},{10,12},{12... | collective-permute-start | bytes 2359304 | tf_op jit(solution)/shard_map/ppermute | solution.py:621
  77.7 31.6 %collective-permute-start.14 = (bf16[3,256,512]{2,1,0:T(8,128)(2,1)S(1)}, bf16[3,256,512]{2,1,0:T(8,128)(2,1)S(1)}, u32[]{:S(2)}, u32[]{:S(2)}) collective-permute-start(bf16[3,256,512]{2,1,0:T(8,128)(2,1)S(1)} %get-tuple-element.82), channel_id=1, source_target_pairs={{0,1},{2,0},{4,2},{6,4},{7,6},{5,7},{3,5},{1,3},{8,9},{10,8},{12,1... | collective-permute-start | bytes 2359304 | tf_op jit(solution)/shard_map/ppermute | solution.py:621
  94.5 31.6 %collective-permute-start.21 = (bf16[3,256,512]{2,1,0:T(8,128)(2,1)S(1)}, bf16[3,256,512]{2,1,0:T(8,128)(2,1)S(1)}, u32[]{:S(2)}, u32[]{:S(2)}) collective-permute-start(bf16[3,256,512]{2,1,0:T(8,128)(2,1)S(1)} %get-tuple-element.90), channel_id=1, source_target_pairs={{0,2},{2,4},{4,6},{6,7},{7,5},{5,3},{3,1},{1,0},{8,10},{10,12},{12... | collective-permute-start | bytes 2359304 | tf_op jit(solution)/shard_map/ppermute | solution.py:621
  94.6 31.6 %collective-permute-start.22 = (bf16[3,256,512]{2,1,0:T(8,128)(2,1)S(1)}, bf16[3,256,512]{2,1,0:T(8,128)(2,1)S(1)}, u32[]{:S(2)}, u32[]{:S(2)}) collective-permute-start(bf16[3,256,512]{2,1,0:T(8,128)(2,1)S(1)} %get-tuple-element.91), channel_id=1, source_target_pairs={{0,1},{2,0},{4,2},{6,4},{7,6},{5,7},{3,5},{1,3},{8,9},{10,8},{12,1... | collective-permute-start | bytes 2359304 | tf_op jit(solution)/shard_map/ppermute | solution.py:621
  97.8 28.4 %copy-start = (bf16[512,2048]{1,0:T(8,128)(2,1)}, bf16[512,2048]{1,0:T(8,128)(2,1)S(1)}, u32[]{:S(2)}) copy-start(bf16[512,2048]{1,0:T(8,128)(2,1)S(1)} %turn.1.refs_9_.refs_0_) | copy-start | bytes 6291460
  111.4 31.6 %collective-permute-start.15 = (bf16[3,256,512]{2,1,0:T(8,128)(2,1)S(1)}, bf16[3,256,512]{2,1,0:T(8,128)(2,1)S(1)}, u32[]{:S(2)}, u32[]{:S(2)}) collective-permute-start(bf16[3,256,512]{2,1,0:T(8,128)(2,1)S(1)} %get-tuple-element.83), channel_id=1, source_target_pairs={{0,2},{2,4},{4,6},{6,7},{7,5},{5,3},{3,1},{1,0},{8,10},{10,12},{12... | collective-permute-start | bytes 2359304 | tf_op jit(solution)/shard_map/ppermute | solution.py:621
  111.4 31.6 %copy-start.20 = (bf16[256,1024]{1,0:T(8,128)(2,1)S(1)}, bf16[256,1024]{1,0:T(8,128)(2,1)}, u32[]{:S(2)}) copy-start(bf16[256,1024]{1,0:T(8,128)(2,1)} %d_out.3) | copy-start | bytes 1572868
  111.4 31.6 %collective-permute-start.16 = (bf16[3,256,512]{2,1,0:T(8,128)(2,1)S(1)}, bf16[3,256,512]{2,1,0:T(8,128)(2,1)S(1)}, u32[]{:S(2)}, u32[]{:S(2)}) collective-permute-start(bf16[3,256,512]{2,1,0:T(8,128)(2,1)S(1)} %get-tuple-element.84), channel_id=1, source_target_pairs={{0,1},{2,0},{4,2},{6,4},{7,6},{5,7},{3,5},{1,3},{8,9},{10,8},{12,1... | collective-permute-start | bytes 2359304 | tf_op jit(solution)/shard_map/ppermute | solution.py:621
  128.2 31.6 %collective-permute-start.23 = (bf16[3,256,512]{2,1,0:T(8,128)(2,1)S(1)}, bf16[3,256,512]{2,1,0:T(8,128)(2,1)S(1)}, u32[]{:S(2)}, u32[]{:S(2)}) collective-permute-start(bf16[3,256,512]{2,1,0:T(8,128)(2,1)S(1)} %get-tuple-element.92), channel_id=1, source_target_pairs={{0,2},{2,4},{4,6},{6,7},{7,5},{5,3},{3,1},{1,0},{8,10},{10,12},{12... | collective-permute-start | bytes 2359304 | tf_op jit(solution)/shard_map/ppermute | solution.py:621
  128.3 31.6 %collective-permute-start.24 = (bf16[3,256,512]{2,1,0:T(8,128)(2,1)S(1)}, bf16[3,256,512]{2,1,0:T(8,128)(2,1)S(1)}, u32[]{:S(2)}, u32[]{:S(2)}) collective-permute-start(bf16[3,256,512]{2,1,0:T(8,128)(2,1)S(1)} %get-tuple-element.93), channel_id=1, source_target_pairs={{0,1},{2,0},{4,2},{6,4},{7,6},{5,7},{3,5},{1,3},{8,9},{10,8},{12,1... | collective-permute-start | bytes 2359304 | tf_op jit(solution)/shard_map/ppermute | solution.py:621
  150.9 16.2 %copy-start.10 = (bf16[3,256,512]{2,1,0:T(8,128)(2,1)}, bf16[3,256,512]{2,1,0:T(8,128)(2,1)S(1)}, u32[]{:S(2)}) copy-start(bf16[3,256,512]{2,1,0:T(8,128)(2,1)S(1)} %get-tuple-element.99.refs_0_.refs_1_) | copy-start | bytes 2359300
  150.9 23.3 %collective-permute-start.30 = (bf16[3,256,512]{2,1,0:T(8,128)(2,1)S(1)}, bf16[3,256,512]{2,1,0:T(8,128)(2,1)S(1)}, u32[]{:S(2)}, u32[]{:S(2)}) collective-permute-start(bf16[3,256,512]{2,1,0:T(8,128)(2,1)S(1)} %get-tuple-element.99.refs_0_.refs_1_), channel_id=1, source_target_pairs={{0,1},{2,0},{4,2},{6,4},{7,6},{5,7},{3,5},{1,3},{8,9},{10,8},{12,1... | collective-permute-start | bytes 2359304 | tf_op jit(solution)/shard_map/ppermute | solution.py:621
  151.0 26.6 %collective-permute-start.27 = (bf16[3,256,512]{2,1,0:T(8,128)(2,1)S(1)}, bf16[3,256,512]{2,1,0:T(8,128)(2,1)S(1)}, u32[]{:S(2)}, u32[]{:S(2)}) collective-permute-start(bf16[3,256,512]{2,1,0:T(8,128)(2,1)S(1)} %get-tuple-element.99.refs_0_.refs_1_), channel_id=1, source_target_pairs={{0,2},{2,4},{4,6},{6,7},{7,5},{5,3},{3,1},{1,0},{8,10},{10,12},{12... | collective-permute-start | bytes 2359304 | tf_op jit(solution)/shard_map/ppermute | solution.py:621
  168.5 22.5 %collective-permute-start.38 = (bf16[3,256,512]{2,1,0:T(8,128)(2,1)S(1)}, bf16[3,256,512]{2,1,0:T(8,128)(2,1)S(1)}, u32[]{:S(2)}, u32[]{:S(2)}) collective-permute-start(bf16[3,256,512]{2,1,0:T(8,128)(2,1)S(1)} %get-tuple-element.104.refs_0_.refs_1_), channel_id=1, source_target_pairs={{0,1},{2,0},{4,2},{6,4},{7,6},{5,7},{3,5},{1,3},{8,9},{10,8},{12,1... | collective-permute-start | bytes 2359304 | tf_op jit(solution)/shard_map/ppermute | solution.py:621
  168.6 25.9 %collective-permute-start.35 = (bf16[3,256,512]{2,1,0:T(8,128)(2,1)S(1)}, bf16[3,256,512]{2,1,0:T(8,128)(2,1)S(1)}, u32[]{:S(2)}, u32[]{:S(2)}) collective-permute-start(bf16[3,256,512]{2,1,0:T(8,128)(2,1)S(1)} %get-tuple-element.104.refs_0_.refs_1_), channel_id=1, source_target_pairs={{0,2},{2,4},{4,6},{6,7},{7,5},{5,3},{3,1},{1,0},{8,10},{10,12},{12... | collective-permute-start | bytes 2359304 | tf_op jit(solution)/shard_map/ppermute | solution.py:621
  174.2 33.7 %collective-permute-start.31 = (bf16[3,256,512]{2,1,0:T(8,128)(2,1)S(1)}, bf16[3,256,512]{2,1,0:T(8,128)(2,1)}, u32[]{:S(2)}, u32[]{:S(2)}) collective-permute-start(bf16[3,256,512]{2,1,0:T(8,128)(2,1)S(1)} %collective-permute-done.30.refs_2_.refs_3_), channel_id=1, source_target_pairs={{0,1},{2,0},{4,2},{6,4},{7,6},{5,7},{3,5},{1,3},{8,9},{10,8},{12,1... | collective-permute-start | bytes 2359304 | tf_op jit(solution)/shard_map/ppermute | solution.py:621
  177.6 32.9 %collective-permute-start.28 = (bf16[3,256,512]{2,1,0:T(8,128)(2,1)S(1)}, bf16[3,256,512]{2,1,0:T(8,128)(2,1)}, u32[]{:S(2)}, u32[]{:S(2)}) collective-permute-start(bf16[3,256,512]{2,1,0:T(8,128)(2,1)S(1)} %collective-permute-done.27.refs_1_.refs_2_), channel_id=1, source_target_pairs={{0,2},{2,4},{4,6},{6,7},{7,5},{5,3},{3,1},{1,0},{8,10},{10,12},{12... | collective-permute-start | bytes 2359304 | tf_op jit(solution)/shard_map/ppermute | solution.py:621
  191.0 33.7 %collective-permute-start.39 = (bf16[3,256,512]{2,1,0:T(8,128)(2,1)S(1)}, bf16[3,256,512]{2,1,0:T(8,128)(2,1)}, u32[]{:S(2)}, u32[]{:S(2)}) collective-permute-start(bf16[3,256,512]{2,1,0:T(8,128)(2,1)S(1)} %collective-permute-done.38.refs_2_.refs_3_), channel_id=1, source_target_pairs={{0,1},{2,0},{4,2},{6,4},{7,6},{5,7},{3,5},{1,3},{8,9},{10,8},{12,1... | collective-permute-start | bytes 2359304 | tf_op jit(solution)/shard_map/ppermute | solution.py:621
  194.4 33.0 %collective-permute-start.36 = (bf16[3,256,512]{2,1,0:T(8,128)(2,1)S(1)}, bf16[3,256,512]{2,1,0:T(8,128)(2,1)}, u32[]{:S(2)}, u32[]{:S(2)}) collective-permute-start(bf16[3,256,512]{2,1,0:T(8,128)(2,1)S(1)} %collective-permute-done.35.refs_1_.refs_2_), channel_id=1, source_target_pairs={{0,2},{2,4},{4,6},{6,7},{7,5},{5,3},{3,1},{1,0},{8,10},{10,12},{12... | collective-permute-start | bytes 2359304 | tf_op jit(solution)/shard_map/ppermute | solution.py:621
  207.9 39.0 %collective-permute-start.32 = (bf16[3,256,512]{2,1,0:T(8,128)(2,1)}, bf16[3,256,512]{2,1,0:T(8,128)(2,1)}, u32[]{:S(2)}, u32[]{:S(2)}) collective-permute-start(bf16[3,256,512]{2,1,0:T(8,128)(2,1)} %collective-permute-done.31.refs_1_.refs_5_), channel_id=1, source_target_pairs={{0,1},{2,0},{4,2},{6,4},{7,6},{5,7},{3,5},{1,3},{8,9},{10,8},{12,1... | collective-permute-start | bytes 2359304 | tf_op jit(solution)/shard_map/ppermute | solution.py:621
  210.5 36.4 %collective-permute-start.29 = (bf16[3,256,512]{2,1,0:T(8,128)(2,1)}, bf16[3,256,512]{2,1,0:T(8,128)(2,1)}, u32[]{:S(2)}, u32[]{:S(2)}) collective-permute-start(bf16[3,256,512]{2,1,0:T(8,128)(2,1)} %collective-permute-done.28.refs_0_.refs_4_), channel_id=1, source_target_pairs={{0,2},{2,4},{4,6},{6,7},{7,5},{5,3},{3,1},{1,0},{8,10},{10,12},{12... | collective-permute-start | bytes 2359304 | tf_op jit(solution)/shard_map/ppermute | solution.py:621
  224.8 33.8 %collective-permute-start.40 = (bf16[3,256,512]{2,1,0:T(8,128)(2,1)}, bf16[3,256,512]{2,1,0:T(8,128)(2,1)}, u32[]{:S(2)}, u32[]{:S(2)}) collective-permute-start(bf16[3,256,512]{2,1,0:T(8,128)(2,1)} %collective-permute-done.39.refs_1_.refs_5_), channel_id=1, source_target_pairs={{0,1},{2,0},{4,2},{6,4},{7,6},{5,7},{3,5},{1,3},{8,9},{10,8},{12,1... | collective-permute-start | bytes 2359304 | tf_op jit(solution)/shard_map/ppermute | solution.py:621
  227.4 33.7 %collective-permute-start.37 = (bf16[3,256,512]{2,1,0:T(8,128)(2,1)}, bf16[3,256,512]{2,1,0:T(8,128)(2,1)}, u32[]{:S(2)}, u32[]{:S(2)}) collective-permute-start(bf16[3,256,512]{2,1,0:T(8,128)(2,1)} %collective-permute-done.36.refs_0_.refs_4_), channel_id=1, source_target_pairs={{0,2},{2,4},{4,6},{6,7},{7,5},{5,3},{3,1},{1,0},{8,10},{10,12},{12... | collective-permute-start | bytes 2359304 | tf_op jit(solution)/shard_map/ppermute | solution.py:621
  230.2 12.9 %copy-start.5 = (bf16[3,256,512]{2,1,0:T(8,128)(2,1)S(1)}, bf16[3,256,512]{2,1,0:T(8,128)(2,1)}, u32[]{:S(2)}) copy-start(bf16[3,256,512]{2,1,0:T(8,128)(2,1)} %copy-done.4) | copy-start | bytes 2359300
  230.2 12.9 %copy-start.7 = (bf16[3,256,512]{2,1,0:T(8,128)(2,1)S(1)}, bf16[3,256,512]{2,1,0:T(8,128)(2,1)}, u32[]{:S(2)}) copy-start(bf16[3,256,512]{2,1,0:T(8,128)(2,1)} %copy-done.6) | copy-start | bytes 2359300
  230.2 12.9 %copy-start.9 = (bf16[3,256,512]{2,1,0:T(8,128)(2,1)S(1)}, bf16[3,256,512]{2,1,0:T(8,128)(2,1)}, u32[]{:S(2)}) copy-start(bf16[3,256,512]{2,1,0:T(8,128)(2,1)} %copy-done.8) | copy-start | bytes 2359300
  230.2 1.6 collective-permute-start.25
  232.7 5.6 %collective-permute-start.26 = (f32[256,1]{1,0:T(8,128)S(1)}, f32[256,1]{1,0:T(8,128)S(1)}, u32[]{:S(2)}, u32[]{:S(2)}) collective-permute-start(f32[256,1]{1,0:T(8,128)S(1)} %add.31), channel_id=1, source_target_pairs={{0,16},{8,24},{16,0},{24,8},{1,17},{9,25},{17,1},{25,9},{2,18},{10... | collective-permute-start | bytes 3080 | tf_op jit(solution)/shard_map/ppermute | solution.py:624
  248.3 21.1 %collective-permute-start.33 = (bf16[3,128,512]{2,1,0:T(8,128)(2,1)S(1)}, bf16[3,128,512]{2,1,0:T(8,128)(2,1)S(1)}, u32[]{:S(2)}, u32[]{:S(2)}) collective-permute-start(bf16[3,128,512]{2,1,0:T(8,128)(2,1)S(1)} %get-tuple-element.100), channel_id=1, source_target_pairs={{0,2},{2,4},{4,6},{6,7},{7,5},{5,3},{3,1},{1,0},{8,10},{10,12},{12... | collective-permute-start | bytes 1179656 | tf_op jit(solution)/shard_map/ppermute | solution.py:621
  249.6 19.8 %collective-permute-start.34 = (bf16[3,128,512]{2,1,0:T(8,128)(2,1)S(1)}, bf16[3,128,512]{2,1,0:T(8,128)(2,1)S(1)}, u32[]{:S(2)}, u32[]{:S(2)}) collective-permute-start(bf16[3,128,512]{2,1,0:T(8,128)(2,1)S(1)} %get-tuple-element.101), channel_id=1, source_target_pairs={{0,1},{2,0},{4,2},{6,4},{7,6},{5,7},{3,5},{1,3},{8,9},{10,8},{12,1... | collective-permute-start | bytes 1179656 | tf_op jit(solution)/shard_map/ppermute | solution.py:621
  262.5 14.5 %collective-permute-start.41 = (bf16[3,128,512]{2,1,0:T(8,128)(2,1)S(1)}, bf16[3,128,512]{2,1,0:T(8,128)(2,1)S(1)}, u32[]{:S(2)}, u32[]{:S(2)}) collective-permute-start(bf16[3,128,512]{2,1,0:T(8,128)(2,1)S(1)} %get-tuple-element.115), channel_id=1, source_target_pairs={{0,2},{2,4},{4,6},{6,7},{7,5},{5,3},{3,1},{1,0},{8,10},{10,12},{12... | collective-permute-start | bytes 1179656 | tf_op jit(solution)/shard_map/ppermute | solution.py:621
  262.6 14.5 %collective-permute-start.42 = (bf16[3,128,512]{2,1,0:T(8,128)(2,1)S(1)}, bf16[3,128,512]{2,1,0:T(8,128)(2,1)S(1)}, u32[]{:S(2)}, u32[]{:S(2)}) collective-permute-start(bf16[3,128,512]{2,1,0:T(8,128)(2,1)S(1)} %get-tuple-element.116), channel_id=1, source_target_pairs={{0,1},{2,0},{4,2},{6,4},{7,6},{5,7},{3,5},{1,3},{8,9},{10,8},{12,1... | collective-permute-start | bytes 1179656 | tf_op jit(solution)/shard_map/ppermute | solution.py:621
  277.1 7.1 %copy-start.22 = (bf16[256,512]{1,0:T(8,128)(2,1)S(1)}, bf16[256,512]{1,0:T(8,128)(2,1)}, u32[]{:S(2)}) copy-start(bf16[256,512]{1,0:T(8,128)(2,1)} %copy-done.21) | copy-start | bytes 786436
  278.7 25.6 %copy-start.1 = (bf16[512,2048]{1,0:T(8,128)(2,1)S(1)}, bf16[512,2048]{1,0:T(8,128)(2,1)}, u32[]{:S(2)}) copy-start(bf16[512,2048]{1,0:T(8,128)(2,1)} %copy-done) | copy-start | bytes 6291460
  278.7 25.6 %copy-start.12 = (bf16[3,256,512]{2,1,0:T(8,128)(2,1)S(1)}, bf16[3,256,512]{2,1,0:T(8,128)(2,1)}, u32[]{:S(2)}) copy-start(bf16[3,256,512]{2,1,0:T(8,128)(2,1)} %copy-done.10) | copy-start | bytes 2359300
  278.7 25.6 %copy-start.15 = (bf16[3,256,512]{2,1,0:T(8,128)(2,1)S(1)}, bf16[3,256,512]{2,1,0:T(8,128)(2,1)}, u32[]{:S(2)}) copy-start(bf16[3,256,512]{2,1,0:T(8,128)(2,1)} %copy-done.13) | copy-start | bytes 2359300
  278.7 25.6 %copy-start.18 = (bf16[3,256,512]{2,1,0:T(8,128)(2,1)S(1)}, bf16[3,256,512]{2,1,0:T(8,128)(2,1)}, u32[]{:S(2)}) copy-start(bf16[3,256,512]{2,1,0:T(8,128)(2,1)} %copy-done.16) | copy-start | bytes 2359300
  278.7 2.0 collective-permute-start.43
  278.8 3.1 collective-permute-start.47
  281.4 9.2 %collective-permute-start.44 = (bf16[2,128,512]{2,1,0:T(8,128)(2,1)S(1)}, bf16[2,128,512]{2,1,0:T(8,128)(2,1)S(1)}, u32[]{:S(2)}, u32[]{:S(2)}) collective-permute-start(bf16[2,128,512]{2,1,0:T(8,128)(2,1)S(1)} %get-tuple-element.124), channel_id=1, source_target_pairs={{0,16},{8,24},{16,0},{24,8},{1,17},{9,25},{17,1},{25,9},{2,18},{10... | collective-permute-start | bytes 786440 | tf_op jit(solution)/shard_map/ppermute | solution.py:624
  282.6 14.1 %collective-permute-start.48 = (bf16[2,128,512]{2,1,0:T(8,128)(2,1)S(1)}, bf16[2,128,512]{2,1,0:T(8,128)(2,1)S(1)}, u32[]{:S(2)}, u32[]{:S(2)}) collective-permute-start(bf16[2,128,512]{2,1,0:T(8,128)(2,1)S(1)} %get-tuple-element.130), channel_id=1, source_target_pairs={{0,16},{8,24},{16,0},{24,8},{1,17},{9,25},{17,1},{25,9},{2,18},{10... | collective-permute-start | bytes 786440 | tf_op jit(solution)/shard_map/ppermute | solution.py:624
  291.2 25.8 %collective-permute-start.46 = (bf16[128,512]{1,0:T(8,128)(2,1)S(1)}, bf16[128,512]{1,0:T(8,128)(2,1)S(1)}, u32[]{:S(2)}, u32[]{:S(2)}) collective-permute-start(bf16[128,512]{1,0:T(8,128)(2,1)S(1)} %get-tuple-element.126), channel_id=1, source_target_pairs={{0,1},{1,0},{2,9},{3,8},{4,17},{5,16},{6,25},{7,24},{8,3},{9,2},{1... | collective-permute-start | bytes 393224 | tf_op jit(solution)/shard_map/ppermute | solution.py:682
  293.5 23.4 %collective-permute-start.45 = (bf16[128,512]{1,0:T(8,128)(2,1)S(1)}, bf16[128,512]{1,0:T(8,128)(2,1)S(1)}, u32[]{:S(2)}, u32[]{:S(2)}) collective-permute-start(bf16[128,512]{1,0:T(8,128)(2,1)S(1)} %get-tuple-element.125.refs_10_), channel_id=1, source_target_pairs={{0,0},{1,1},{2,8},{3,9},{4,16},{5,17},{6,24},{7,25},{8,2},{9,3},{1... | collective-permute-start | bytes 393224 | tf_op jit(solution)/shard_map/ppermute | solution.py:682
  297.3 19.7 %collective-permute-start.50 = (bf16[128,512]{1,0:T(8,128)(2,1)S(1)}, bf16[128,512]{1,0:T(8,128)(2,1)S(1)}, u32[]{:S(2)}, u32[]{:S(2)}) collective-permute-start(bf16[128,512]{1,0:T(8,128)(2,1)S(1)} %get-tuple-element.132), channel_id=1, source_target_pairs={{0,1},{1,0},{2,9},{3,8},{4,17},{5,16},{6,25},{7,24},{8,3},{9,2},{1... | collective-permute-start | bytes 393224 | tf_op jit(solution)/shard_map/ppermute | solution.py:682
  300.7 16.3 %collective-permute-start.49 = (bf16[128,512]{1,0:T(8,128)(2,1)S(1)}, bf16[128,512]{1,0:T(8,128)(2,1)S(1)}, u32[]{:S(2)}, u32[]{:S(2)}) collective-permute-start(bf16[128,512]{1,0:T(8,128)(2,1)S(1)} %get-tuple-element.131.refs_11_), channel_id=1, source_target_pairs={{0,0},{1,1},{2,8},{3,9},{4,16},{5,17},{6,24},{7,25},{8,2},{9,3},{1... | collective-permute-start | bytes 393224 | tf_op jit(solution)/shard_map/ppermute | solution.py:682
  310.6 6.4 %copy-start.3 = (bf16[256,4096]{1,0:T(8,128)(2,1)S(1)}, bf16[256,4096]{1,0:T(8,128)(2,1)}, u32[]{:S(2)}) copy-start(bf16[256,4096]{1,0:T(8,128)(2,1)} %tokens.3) | copy-start | bytes 6291460
  310.6 6.5 %copy-start.24 = (f32[256,128]{1,0:T(8,128)S(1)}, f32[256,128]{1,0:T(8,128)}, u32[]{:S(2)}) copy-start(f32[256,128]{1,0:T(8,128)} %copy-done.23) | copy-start | bytes 393220
  (15 other events, 14.9 us)

commit v8 on v7

--- a/solution.py
+++ b/solution.py
@@ -129,27 +129,29 @@
     )(w_quant, w_scale)
 
 
-def normed_kernel(idx, tokens, gain, *refs):
+def normed_kernel(split, idx, tokens, gain, *refs):
     outs, gains = refs[:-1], refs[-1]
     width, part = tokens.shape[1], outs[0].shape[1]
     gains[...] = gain[...].astype(jnp.float32)
     values = tokens[...].astype(jnp.float32)
     inverse = lax.rsqrt(jnp.mean(values * values, axis=-1, keepdims=True) + NORM_EPS)
     size = len(outs) - 1
+    share = idx[size] if split == 2 else 2 * idx[size] + idx[4 * size + 1]
     for distance in range(size):
-        start = pl.multiple_of(idx[distance] * (width // size) + idx[size] * part, part)
+        start = pl.multiple_of(idx[distance] * (width // size) + share * part, part)
         block = tokens[:, pl.ds(start, part)].astype(jnp.float32)
         scale = gains[:, pl.ds(start, part)]
         outs[distance][...] = (block * inverse * scale).astype(jnp.bfloat16)
     outs[size][...] = jnp.broadcast_to(inverse, outs[size].shape)
 
 
-def normed_blocks(idx, tokens, gain, size, part):
+def normed_blocks(idx, tokens, gain, size, split):
     length, width = tokens.shape
+    part = width // (size * split)
     tile = length // 4
     block = pl.BlockSpec((tile, part), lambda i, idx: (i, 0))
     *blocks, inverse = pl.pallas_call(
-        normed_kernel,
+        functools.partial(normed_kernel, split),
         grid_spec=pltpu.PrefetchScalarGridSpec(
             num_scalar_prefetch=1,
             grid=(4,),
@@ -187,6 +189,26 @@
         cost_estimate=cost(0, 4 * count * shape[0] * shape[1]),
         name="stack",
     )(*blocks, *ties)
+
+
+def join_kernel(column, idx, own, came, out):
+    part = own.shape[-1]
+    out[..., pl.ds(pl.multiple_of(idx[column] * part, part), part)] = own[...]
+    out[..., pl.ds(pl.multiple_of((1 - idx[column]) * part, part), part)] = came[...]
+
+
+def join(idx, column, own, came):
+    whole = pl.BlockSpec(memory_space=pltpu.VMEM)
+    shape = (*own.shape[:-1], 2 * own.shape[-1])
+    return pl.pallas_call(
+        functools.partial(join_kernel, column),
+        in_specs=[pl.BlockSpec(memory_space=pltpu.SMEM), whole, whole],
+        out_specs=whole,
+        out_shape=jax.ShapeDtypeStruct(shape, own.dtype),
+        compiler_params=pltpu.CompilerParams(vmem_limit_bytes=4 * MIB),
+        cost_estimate=cost(0, 4 * math.prod(shape)),
+        name="join",
+    )(idx, own, came)
 
 
 def halve_kernel(right, left, right_out, left_out):
@@ -495,21 +517,23 @@
                 sends[part][idx[3 * count + 1 + place]] = total.astype(jnp.bfloat16)
 
 
-def term_last(idx, turned, befores, pieces, nears):
+def term_last(idx, turned, befores, pieces, nears, ties):
     count = len(nears) + 1
     rows, depth = nears[0].shape
     whole = pl.BlockSpec(memory_space=pltpu.VMEM)
     shape = (count // 2, rows // 2, depth)
     return pl.pallas_call(
-        functools.partial(term_last_kernel, count),
-        in_specs=[pl.BlockSpec(memory_space=pltpu.SMEM)] + [whole] * (count + 4),
+        tied(functools.partial(term_last_kernel, count), count + 5, len(ties)),
+        in_specs=[pl.BlockSpec(memory_space=pltpu.SMEM)]
+        + [whole] * (count + 4)
+        + tie_specs(ties),
         out_specs=[whole] * 4,
         out_shape=[jax.ShapeDtypeStruct(shape, jnp.float32)] * 2
         + [jax.ShapeDtypeStruct(shape, jnp.bfloat16)] * 2,
         compiler_params=pltpu.CompilerParams(vmem_limit_bytes=12 * MIB),
         cost_estimate=cost(rows * depth * depth, 12 * count * rows * depth),
         name="term_last",
-    )(idx, turned, *befores, *pieces, *nears)
+    )(idx, turned, *befores, *pieces, *nears, *ties)
 
 
 def split_kernel(column, group, idx, keep, came, keep_out, send_out):
@@ -623,14 +647,18 @@
     def swap(array, bit):
         return lax.ppermute(array, "node", [(n, n ^ bit) for n in range(nodes)])
 
-    blocks, inverse_rms = normed_blocks(idx, tokens, norm_gain[None], size, depth // 2)
-    mine_far = shift(blocks[far], far)
+    split = 4 if nodes >= 4 and depth % 512 == 0 else 2
+
+    def whole_half(block):
+        return join(idx, 4 * size + 1, block, swap(block, 2)) if split == 4 else block
+
+    blocks, inverse_rms = normed_blocks(idx, tokens, norm_gain[None], size, split)
+    mine_far = whole_half(shift(blocks[far], far))
     other_far = swap(mine_far, 1)
     weights, turned = scaled_weights(w_quant, w_scale)
     firsts = sum_first(idx, size, mine_far, other_far, weights)
-    mine = stack(
-        [shift(blocks[-d % size], -d) if d else blocks[0] for d in distances[:-1]], firsts[:1]
-    )
+    nears = [shift(blocks[-d % size], -d) if d else blocks[0] for d in distances[:-1]]
+    mine = whole_half(stack(nears, firsts[:1]))
     other = swap(mine, 1)
 
     rows_turned = turn(idx, mine, other, mine_far, other_far)
@@ -701,7 +729,10 @@
                 terms[chunk] += term_step(turned, pieces, befores, chunk)
             elif chunk == 0:
                 lasts = term_step(turned, [right, left], [], 0)
-    keep_0, keep_1, send_0, send_1 = term_last(idx, turned, lasts, gathered[1][-2:], terms[1])
+    grads = grads_chunk(rows_turned, gathered[0], None, [], 0, wide, columns)
+    keep_0, keep_1, send_0, send_1 = term_last(
+        idx, turned, lasts, gathered[1][-2:], terms[1], [grads]
+    )
     first, second = sum_nodes(keep_0, send_0), sum_nodes(keep_1, send_1)
     came = [*relocate(first), *relocate(second)]
     column = idx.shape[0] - 1 - group
@@ -709,8 +740,7 @@
         idx, column, tokens, norm_gain[None], inverse_rms, dots, came, width // nodes
     )
     sums = [first[0], second[0]]
-    grads = grads_chunk(rows_turned, gathered[0], None, sums, 0, wide, columns)
-    grads = grads_chunk(rows_turned, gathered[1], grads, [], 1, wide, columns)
+    grads = grads_chunk(rows_turned, gathered[1], grads, sums, 1, wide, columns)
     return (jnp.concatenate(outputs, axis=-1), d_tokens, grads)
 
 

time: 320 us -> 336 us (1.050)
  waiting for transfers between devices: 164 us -> 178 us
  local copies, waits for them, and re-layouts: 17.1 us -> 20.6 us
    ppermute x8 -> x10, waiting for transfers between devices: 13.5 us -> 27.2 us  [swap(): return lax.ppermute(array, 'node', [(n, n ^ bit) for n in range(nodes)])]
    ppermute x39, waiting for transfers between devices: 151 us -> 141 us  [shift(): return lax.ppermute(array, 'local', moves)]
    ppermute x4, waiting for transfers between devices: 0.01 us -> 9.53 us  [relocate(): came.append(lax.ppermute(block, ('node', 'local'), moves))]
    unnamed x56 -> x58, local copies, waits for them, and re-layouts: 14.9 us -> 18.4 us
  transfers between devices with their start and end apart: 51 -> 53, of which waited for: 24 -> 35; matrix products, arithmetic and copies ran while one was open for 2% -> 2% of each run, Pallas kernels for 19% -> 18%
where the time goes in v8:
time: 336 us; the launch traced here: 335 us
  waiting for transfers between devices  178 us (53%)
  Pallas kernels  67.4 us (20%)
  starting transfers between devices  63.6 us (19%)
  local copies, waits for them, and re-layouts  20.6 us (6%)
  other arithmetic  4.52 us (1%)
    ppermute x39, waiting for transfers between devices, shift(): return lax.ppermute(array, 'local', moves)  141 us
    ppermute x39, starting transfers between devices, shift(): return lax.ppermute(array, 'local', moves)  46.7 us
    ppermute x10, waiting for transfers between devices, swap(): return lax.ppermute(array, 'node', [(n, n ^ bit) for n in range(nodes)])  27.2 us
    unnamed x58, local copies, waits for them, and re-layouts  18.4 us
    pallas_call x2, Pallas kernels, attention(): pl.pallas_call(attention_kernel, grid_spec=pltpu.PrefetchScalarGridSpec(n...  14.5 us
    pallas_call x7, Pallas kernels, term_step(): pl.pallas_call(kernel, in_specs=[whole] * (1 + count + len(befores)), out...  12.8 us
    ppermute x4, starting transfers between devices, relocate(): came.append(lax.ppermute(block, ('node', 'local'), moves))  12.5 us
    pallas_call x2, Pallas kernels, grads_chunk(): pl.pallas_call(tied(grads_kernel, 1 + len(pieces), len(ties)), grid=(3,),...  12.5 us
  transfers between devices with their start and end apart: 53, of which 35 were waited for; matrix products, arithmetic and copies ran while one was open for 2% of the time, Pallas kernels for 18%

profile of v8, /device:TPU:2, one launch (start us, length us, event | category | flops | bytes accessed | tf_op | source)
XLA Modules:
  0.0 334.9 jit_solution(4868637949132874941)
XLA Ops:
  2.0 1.6 copy-done.3
  5.0 4.6 %collective-permute-start.6 = (bf16[256,128]{1,0:T(8,128)(2,1)S(1)}, bf16[256,128]{1,0:T(8,128)(2,1)S(1)}, u32[]{:S(2)}, u32[]{:S(2)}) collective-permute-start(bf16[256,128]{1,0:T(8,128)(2,1)S(1)} %get-tuple-element.75), channel_id=1, source_target_pairs={{0,7},{2,5},{4,3},{6,1},{7,0},{5,2},{3,4},{1,6},{8,15},{10,13},{12... | collective-permute-start | bytes 196616 | tf_op jit(solution)/shard_map/ppermute | solution.py:645
  9.7 2.4 collective-permute-done.6.own
  12.4 3.9 %collective-permute-done.7.came = bf16[256,128]{1,0:T(8,128)(2,1)S(1)} collective-permute-done((bf16[256,128]{1,0:T(8,128)(2,1)S(1)}, bf16[256,128]{1,0:T(8,128)(2,1)S(1)}, u32[]{:S(2)}, u32[]{:S(2)}) %collective-permute-start.7) | collective-permute-done | bytes 65568 | tf_op jit(solution)/shard_map/ppermute | solution.py:648
  19.1 2.1 collective-permute-start.2
  22.0 1.9 copy-done.14
  25.7 3.7 %collective-permute-start.4 = (bf16[256,128]{1,0:T(8,128)(2,1)S(1)}, bf16[256,128]{1,0:T(8,128)(2,1)S(1)}, u32[]{:S(2)}, u32[]{:S(2)}) collective-permute-start(bf16[256,128]{1,0:T(8,128)(2,1)S(1)} %get-tuple-element.73), channel_id=1, source_target_pairs={{0,6},{2,7},{4,5},{6,3},{7,1},{5,0},{3,2},{1,4},{8,14},{10,15},{12... | collective-permute-start | bytes 196616 | tf_op jit(solution)/shard_map/ppermute | solution.py:645
  29.6 1.9 sum_first.1
  31.9 3.5 %collective-permute-done.5.refs_6_ = bf16[256,128]{1,0:T(8,128)(2,1)S(1)} collective-permute-done((bf16[256,128]{1,0:T(8,128)(2,1)S(1)}, bf16[256,128]{1,0:T(8,128)(2,1)S(1)}, u32[]{:S(2)}, u32[]{:S(2)}) %collective-permute-start.5) | collective-permute-done | bytes 65568 | tf_op jit(solution)/shard_map/ppermute | solution.py:645
  36.1 9.8 %collective-permute-done.9.came = bf16[7,256,128]{2,1,0:T(8,128)(2,1)S(1)} collective-permute-done((bf16[7,256,128]{2,1,0:T(8,128)(2,1)S(1)}, bf16[7,256,128]{2,1,0:T(8,128)(2,1)S(1)}, u32[]{:S(2)}, u32[]{:S(2)}) %collective-permute-start.9) | collective-permute-done | bytes 458784 | tf_op jit(solution)/shard_map/ppermute | solution.py:648
  46.6 1.6 collective-permute-start.11
  51.0 7.9 %collective-permute-done.11.refs_7_ = bf16[3,128,512]{2,1,0:T(8,128)(2,1)S(1)} collective-permute-done((bf16[3,128,512]{2,1,0:T(8,128)(2,1)S(1)}, bf16[3,128,512]{2,1,0:T(8,128)(2,1)S(1)}, u32[]{:S(2)}, u32[]{:S(2)}) %collective-permute-start.11) | collective-permute-done | bytes 393248 | tf_op jit(solution)/shard_map/ppermute | solution.py:645
  60.2 2.1 sum_step.6
  62.2 1.7 collective-permute-start.13
  64.3 3.0 collective-permute-done.19.refs_7_
  68.6 2.1 sum_step.9
  70.6 1.7 collective-permute-start.21
  72.7 11.5 %collective-permute-done.13.refs_7_ = bf16[3,256,512]{2,1,0:T(8,128)(2,1)S(1)} collective-permute-done((bf16[3,256,512]{2,1,0:T(8,128)(2,1)S(1)}, bf16[3,256,512]{2,1,0:T(8,128)(2,1)S(1)}, u32[]{:S(2)}, u32[]{:S(2)}) %collective-permute-start.13) | collective-permute-done | bytes 786464 | tf_op jit(solution)/shard_map/ppermute | solution.py:645
  85.4 2.1 sum_step.7
  87.5 1.7 collective-permute-start.15
  89.6 11.5 %collective-permute-done.21.refs_7_ = bf16[3,256,512]{2,1,0:T(8,128)(2,1)S(1)} collective-permute-done((bf16[3,256,512]{2,1,0:T(8,128)(2,1)S(1)}, bf16[3,256,512]{2,1,0:T(8,128)(2,1)S(1)}, u32[]{:S(2)}, u32[]{:S(2)}) %collective-permute-start.21) | collective-permute-done | bytes 786464 | tf_op jit(solution)/shard_map/ppermute | solution.py:645
  102.3 2.1 sum_step.10
  104.4 1.7 collective-permute-start.23
  107.6 10.3 %collective-permute-done.15.refs_7_ = bf16[3,256,512]{2,1,0:T(8,128)(2,1)S(1)} collective-permute-done((bf16[3,256,512]{2,1,0:T(8,128)(2,1)S(1)}, bf16[3,256,512]{2,1,0:T(8,128)(2,1)S(1)}, u32[]{:S(2)}, u32[]{:S(2)}) %collective-permute-start.15) | collective-permute-done | bytes 786464 | tf_op jit(solution)/shard_map/ppermute | solution.py:645
  119.1 2.1 sum_step.8
  121.2 1.7 collective-permute-start.17
  123.3 11.5 %collective-permute-done.23.refs_7_ = bf16[3,256,512]{2,1,0:T(8,128)(2,1)S(1)} collective-permute-done((bf16[3,256,512]{2,1,0:T(8,128)(2,1)S(1)}, bf16[3,256,512]{2,1,0:T(8,128)(2,1)S(1)}, u32[]{:S(2)}, u32[]{:S(2)}) %collective-permute-start.23) | collective-permute-done | bytes 786464 | tf_op jit(solution)/shard_map/ppermute | solution.py:645
  136.0 2.1 sum_step.11
  138.1 1.7 collective-permute-start.25
  140.8 10.8 %collective-permute-done.17.from_left = bf16[3,256,512]{2,1,0:T(8,128)(2,1)S(1)} collective-permute-done((bf16[3,256,512]{2,1,0:T(8,128)(2,1)S(1)}, bf16[3,256,512]{2,1,0:T(8,128)(2,1)S(1)}, u32[]{:S(2)}, u32[]{:S(2)}) %collective-permute-start.17) | collective-permute-done | bytes 786464 | tf_op jit(solution)/shard_map/ppermute | solution.py:645
  152.8 7.2 %attention.2 = (bf16[256,512]{1,0:T(8,128)(2,1)S(1)}, f32[256,128]{1,0:T(8,128)S(1)}, bf16[3,256,512]{2,1,0:T(8,128)(2,1)S(1)}) custom-call(s32[39]{0:T(128)S(1)} %dynamic-slice_bitcast_fusion.idx.refs_0_, bf16[7,256,256]{2,1,0:T(8,128)(2,1)S(1)} %join.3.refs_1_.refs_3_.mine, bf16[7,256,256]{2,1,0:T(8,128)(2,1)S(1)} %collective-permute-done.10.refs_2_.refs_4_.other, ...), custom_call_target="tpu_custom_call" | custom-call | flops 402653184 | bytes 3145728 | tf_op jit(solution)/shard_map/attention/pallas_call | solution.py:411
  160.7 1.6 collective-permute-start.29
  162.8 5.7 %collective-permute-done.25.from_left = bf16[3,256,512]{2,1,0:T(8,128)(2,1)S(1)} collective-permute-done((bf16[3,256,512]{2,1,0:T(8,128)(2,1)S(1)}, bf16[3,256,512]{2,1,0:T(8,128)(2,1)S(1)}, u32[]{:S(2)}, u32[]{:S(2)}) %collective-permute-start.25) | collective-permute-done | bytes 786464 | tf_op jit(solution)/shard_map/ppermute | solution.py:645
  169.7 7.3 %attention.3 = (bf16[256,512]{1,0:T(8,128)(2,1)S(1)}, f32[256,128]{1,0:T(8,128)S(1)}, bf16[3,256,512]{2,1,0:T(8,128)(2,1)S(1)}) custom-call(s32[39]{0:T(128)S(1)} %dynamic-slice_bitcast_fusion.idx.refs_0_, bf16[7,256,256]{2,1,0:T(8,128)(2,1)S(1)} %join.3.refs_1_.refs_3_.mine, bf16[7,256,256]{2,1,0:T(8,128)(2,1)S(1)} %collective-permute-done.10.refs_2_.refs_4_.other, ...), custom_call_target="tpu_custom_call" | custom-call | flops 402653184 | bytes 3145728 | tf_op jit(solution)/shard_map/attention/pallas_call | solution.py:411
  178.3 1.6 collective-permute-start.37
  181.3 4.0 %collective-permute-done.29.refs_1_.refs_2_ = bf16[3,256,512]{2,1,0:T(8,128)(2,1)S(1)} collective-permute-done((bf16[3,256,512]{2,1,0:T(8,128)(2,1)S(1)}, bf16[3,256,512]{2,1,0:T(8,128)(2,1)S(1)}, u32[]{:S(2)}, u32[]{:S(2)}) %collective-permute-start.29) | collective-permute-done | bytes 786464 | tf_op jit(solution)/shard_map/ppermute | solution.py:645
  189.1 13.0 %collective-permute-done.37.refs_1_.refs_2_ = bf16[3,256,512]{2,1,0:T(8,128)(2,1)S(1)} collective-permute-done((bf16[3,256,512]{2,1,0:T(8,128)(2,1)S(1)}, bf16[3,256,512]{2,1,0:T(8,128)(2,1)S(1)}, u32[]{:S(2)}, u32[]{:S(2)}) %collective-permute-start.37) | collective-permute-done | bytes 786464 | tf_op jit(solution)/shard_map/ppermute | solution.py:645
  206.0 13.1 %collective-permute-done.30.refs_0_.refs_4_ = bf16[3,256,512]{2,1,0:T(8,128)(2,1)} collective-permute-done((bf16[3,256,512]{2,1,0:T(8,128)(2,1)S(1)}, bf16[3,256,512]{2,1,0:T(8,128)(2,1)}, u32[]{:S(2)}, u32[]{:S(2)}) %collective-permute-start.30) | collective-permute-done | bytes 786464 | tf_op jit(solution)/shard_map/ppermute | solution.py:645
  221.2 14.8 %collective-permute-done.38.refs_0_.refs_4_ = bf16[3,256,512]{2,1,0:T(8,128)(2,1)} collective-permute-done((bf16[3,256,512]{2,1,0:T(8,128)(2,1)S(1)}, bf16[3,256,512]{2,1,0:T(8,128)(2,1)}, u32[]{:S(2)}, u32[]{:S(2)}) %collective-permute-start.38) | collective-permute-done | bytes 786464 | tf_op jit(solution)/shard_map/ppermute | solution.py:645
  240.9 1.6 collective-permute-done.27
  243.9 5.0 %collective-permute-done.28 = f32[256,1]{1,0:T(8,128)S(1)} collective-permute-done((f32[256,1]{1,0:T(8,128)S(1)}, f32[256,1]{1,0:T(8,128)S(1)}, u32[]{:S(2)}, u32[]{:S(2)}) %collective-permute-start.28) | collective-permute-done | bytes 1056 | tf_op jit(solution)/shard_map/ppermute | solution.py:648
  254.1 1.4 halve.2
  255.5 1.7 collective-permute-start.35
  259.0 2.3 term_step.10
  261.3 2.3 term_step.11
  263.7 6.0 %collective-permute-done.39.refs_0_.refs_6_ = bf16[3,256,512]{2,1,0:T(8,128)(2,1)} collective-permute-done((bf16[3,256,512]{2,1,0:T(8,128)(2,1)}, bf16[3,256,512]{2,1,0:T(8,128)(2,1)}, u32[]{:S(2)}, u32[]{:S(2)}) %collective-permute-start.39) | collective-permute-done | bytes 786464 | tf_op jit(solution)/shard_map/ppermute | solution.py:645
  270.9 1.4 halve.3
  272.3 1.7 collective-permute-start.43
  274.4 2.3 term_step.12
  276.8 2.4 term_step.13
  281.2 6.2 %grads.2.refs_13_.refs_10_ = f32[3,512,1024]{2,1,0:T(8,128)} custom-call(bf16[512,2048]{1,0:T(8,128)(2,1)S(1)} %copy-done.2, bf16[3,256,512]{2,1,0:T(8,128)(2,1)S(1)} %copy-done.7, bf16[3,256,512]{2,1,0:T(8,128)(2,1)S(1)} %copy-done.10, bf16[3,256,512]{2,1,0:T(8,128)(2,1)S(1)} %copy-done.13, bf16[3,256,512]{2,1,0:T(8,128)(2,1)} %collective-permute-done.30.refs_0_.refs_4_, ...), custom_call_target="tpu_custom_call" | custom-call | flops 3221225472 | bytes 9437184 | tf_op jit(solution)/shard_map/grads/pallas_call | solution.py:453
  287.5 2.8 copy-done
  290.3 1.6 term_last.1
  292.5 1.4 collective-permute-done.49.came
  295.8 1.6 collective-permute-start.46
  298.2 5.5 %collective-permute-done.50.came = bf16[2,128,512]{2,1,0:T(8,128)(2,1)S(1)} collective-permute-done((bf16[2,128,512]{2,1,0:T(8,128)(2,1)S(1)}, bf16[2,128,512]{2,1,0:T(8,128)(2,1)S(1)}, u32[]{:S(2)}, u32[]{:S(2)}) %collective-permute-start.50) | collective-permute-done | bytes 262176 | tf_op jit(solution)/shard_map/ppermute | solution.py:648
  304.3 5.0 %collective-permute-start.51 = (bf16[128,512]{1,0:T(8,128)(2,1)S(1)}, bf16[128,512]{1,0:T(8,128)(2,1)S(1)}, u32[]{:S(2)}, u32[]{:S(2)}) collective-permute-start(bf16[128,512]{1,0:T(8,128)(2,1)S(1)} %get-tuple-element.131.refs_12_), channel_id=1, source_target_pairs={{0,0},{1,1},{2,8},{3,9},{4,16},{5,17},{6,24},{7,25},{8,2},{9,3},{1... | collective-permute-start | bytes 393224 | tf_op jit(solution)/shard_map/ppermute | solution.py:710
  311.0 3.5 %collective-permute-start.47 = (bf16[128,512]{1,0:T(8,128)(2,1)S(1)}, bf16[128,512]{1,0:T(8,128)(2,1)S(1)}, u32[]{:S(2)}, u32[]{:S(2)}) collective-permute-start(bf16[128,512]{1,0:T(8,128)(2,1)S(1)} %get-tuple-element.125.refs_11_), channel_id=1, source_target_pairs={{0,0},{1,1},{2,8},{3,9},{4,16},{5,17},{6,24},{7,25},{8,2},{9,3},{1... | collective-permute-start | bytes 393224 | tf_op jit(solution)/shard_map/ppermute | solution.py:710
  314.5 2.9 collective-permute-start.48
  317.5 6.2 %grads.3 = f32[3,512,1024]{2,1,0:T(8,128)} custom-call(bf16[512,2048]{1,0:T(8,128)(2,1)S(1)} %copy-done.2, bf16[3,256,512]{2,1,0:T(8,128)(2,1)S(1)} %copy-done.16, bf16[3,256,512]{2,1,0:T(8,128)(2,1)S(1)} %copy-done.18, bf16[3,256,512]{2,1,0:T(8,128)(2,1)S(1)} %copy-done.20, ...), custom_call_target="tpu_custom_call", output_to_operand_aliasing={{}: (10, {})} | custom-call | flops 3221225472 | bytes 9437184 | tf_op jit(solution)/shard_map/grads/pallas_call | solution.py:453
  323.7 3.9 %collective-permute-done.52.refs_3_ = bf16[128,512]{1,0:T(8,128)(2,1)S(1)} collective-permute-done((bf16[128,512]{1,0:T(8,128)(2,1)S(1)}, bf16[128,512]{1,0:T(8,128)(2,1)S(1)}, u32[]{:S(2)}, u32[]{:S(2)}) %collective-permute-start.52) | collective-permute-done | bytes 131104 | tf_op jit(solution)/shard_map/ppermute | solution.py:710
  327.6 2.3 collective-permute-done.47.refs_0_
  330.0 3.3 collective-permute-done.48.refs_1_
  333.3 1.6 finish.1
  (145 shorter events, 63.3 us)
Async XLA Ops:
  5.0 16.2 %copy-start.24 = (f32[256,128]{1,0:T(8,128)}, f32[256,128]{1,0:T(8,128)S(1)}, u32[]{:S(2)}) copy-start(f32[256,128]{1,0:T(8,128)S(1)} %get-tuple-element.95.inverse) | copy-start | bytes 393220
  5.0 7.0 %collective-permute-start.6 = (bf16[256,128]{1,0:T(8,128)(2,1)S(1)}, bf16[256,128]{1,0:T(8,128)(2,1)S(1)}, u32[]{:S(2)}, u32[]{:S(2)}) collective-permute-start(bf16[256,128]{1,0:T(8,128)(2,1)S(1)} %get-tuple-element.75), channel_id=1, source_target_pairs={{0,7},{2,5},{4,3},{6,1},{7,0},{5,2},{3,4},{1,6},{8,15},{10,13},{12... | collective-permute-start | bytes 196616 | tf_op jit(solution)/shard_map/ppermute | solution.py:645
  12.1 4.3 %collective-permute-start.7 = (bf16[256,128]{1,0:T(8,128)(2,1)S(1)}, bf16[256,128]{1,0:T(8,128)(2,1)S(1)}, u32[]{:S(2)}, u32[]{:S(2)}) collective-permute-start(bf16[256,128]{1,0:T(8,128)(2,1)S(1)} %collective-permute-done.6.own), channel_id=1, source_target_pairs={{0,16},{8,24},{16,0},{24,8},{1,17},{9,25},{17,1},{25,9},{2,18},{10... | collective-permute-start | bytes 196616 | tf_op jit(solution)/shard_map/ppermute | solution.py:648
  16.9 12.4 %collective-permute-start.8 = (bf16[256,256]{1,0:T(8,128)(2,1)S(1)}, bf16[256,256]{1,0:T(8,128)(2,1)S(1)}, u32[]{:S(2)}, u32[]{:S(2)}) collective-permute-start(bf16[256,256]{1,0:T(8,128)(2,1)S(1)} %join.2.mine.mine_far), channel_id=1, source_target_pairs={{0,8},{8,0},{16,24},{24,16},{1,9},{9,1},{17,25},{25,17},{2,10},{10... | collective-permute-start | bytes 393224 | tf_op jit(solution)/shard_map/ppermute | solution.py:648
  17.0 8.7 %collective-permute-start = (bf16[256,128]{1,0:T(8,128)(2,1)S(1)}, bf16[256,128]{1,0:T(8,128)(2,1)S(1)}, u32[]{:S(2)}, u32[]{:S(2)}) collective-permute-start(bf16[256,128]{1,0:T(8,128)(2,1)S(1)} %get-tuple-element.69), channel_id=1, source_target_pairs={{0,2},{2,4},{4,6},{6,7},{7,5},{5,3},{3,1},{1,0},{8,10},{10,12},{12... | collective-permute-start | bytes 196616 | tf_op jit(solution)/shard_map/ppermute | solution.py:645
  18.0 13.5 %collective-permute-start.1 = (bf16[256,128]{1,0:T(8,128)(2,1)S(1)}, bf16[256,128]{1,0:T(8,128)(2,1)S(1)}, u32[]{:S(2)}, u32[]{:S(2)}) collective-permute-start(bf16[256,128]{1,0:T(8,128)(2,1)S(1)} %get-tuple-element.70), channel_id=1, source_target_pairs={{0,1},{2,0},{4,2},{6,4},{7,6},{5,7},{3,5},{1,3},{8,9},{10,8},{12,1... | collective-permute-start | bytes 196616 | tf_op jit(solution)/shard_map/ppermute | solution.py:645
  19.1 12.4 %collective-permute-start.2 = (bf16[256,128]{1,0:T(8,128)(2,1)S(1)}, bf16[256,128]{1,0:T(8,128)(2,1)S(1)}, u32[]{:S(2)}, u32[]{:S(2)}) collective-permute-start(bf16[256,128]{1,0:T(8,128)(2,1)S(1)} %get-tuple-element.71), channel_id=1, source_target_pairs={{0,4},{2,6},{4,7},{6,5},{7,3},{5,1},{3,0},{1,2},{8,12},{10,14},{12... | collective-permute-start | bytes 196616 | tf_op jit(solution)/shard_map/ppermute | solution.py:645
  21.2 10.3 %collective-permute-start.3 = (bf16[256,128]{1,0:T(8,128)(2,1)S(1)}, bf16[256,128]{1,0:T(8,128)(2,1)S(1)}, u32[]{:S(2)}, u32[]{:S(2)}) collective-permute-start(bf16[256,128]{1,0:T(8,128)(2,1)S(1)} %get-tuple-element.72), channel_id=1, source_target_pairs={{0,3},{2,1},{4,0},{6,2},{7,4},{5,6},{3,7},{1,5},{8,11},{10,9},{12,... | collective-permute-start | bytes 196616 | tf_op jit(solution)/shard_map/ppermute | solution.py:645
  25.7 6.2 %collective-permute-start.4 = (bf16[256,128]{1,0:T(8,128)(2,1)S(1)}, bf16[256,128]{1,0:T(8,128)(2,1)S(1)}, u32[]{:S(2)}, u32[]{:S(2)}) collective-permute-start(bf16[256,128]{1,0:T(8,128)(2,1)S(1)} %get-tuple-element.73), channel_id=1, source_target_pairs={{0,6},{2,7},{4,5},{6,3},{7,1},{5,0},{3,2},{1,4},{8,14},{10,15},{12... | collective-permute-start | bytes 196616 | tf_op jit(solution)/shard_map/ppermute | solution.py:645
  29.4 6.1 %collective-permute-start.5 = (bf16[256,128]{1,0:T(8,128)(2,1)S(1)}, bf16[256,128]{1,0:T(8,128)(2,1)S(1)}, u32[]{:S(2)}, u32[]{:S(2)}) collective-permute-start(bf16[256,128]{1,0:T(8,128)(2,1)S(1)} %get-tuple-element.74), channel_id=1, source_target_pairs={{0,5},{2,3},{4,1},{6,0},{7,2},{5,4},{3,6},{1,7},{8,13},{10,11},{12... | collective-permute-start | bytes 196616 | tf_op jit(solution)/shard_map/ppermute | solution.py:645
  35.5 10.4 %collective-permute-start.9 = (bf16[7,256,128]{2,1,0:T(8,128)(2,1)S(1)}, bf16[7,256,128]{2,1,0:T(8,128)(2,1)S(1)}, u32[]{:S(2)}, u32[]{:S(2)}) collective-permute-start(bf16[7,256,128]{2,1,0:T(8,128)(2,1)S(1)} %stack.1.own), channel_id=1, source_target_pairs={{0,16},{8,24},{16,0},{24,8},{1,17},{9,25},{17,1},{25,9},{2,18},{10... | collective-permute-start | bytes 1376264 | tf_op jit(solution)/shard_map/ppermute | solution.py:648
  46.5 13.6 %collective-permute-start.10 = (bf16[7,256,256]{2,1,0:T(8,128)(2,1)S(1)}, bf16[7,256,256]{2,1,0:T(8,128)(2,1)S(1)}, u32[]{:S(2)}, u32[]{:S(2)}) collective-permute-start(bf16[7,256,256]{2,1,0:T(8,128)(2,1)S(1)} %join.3.refs_1_.refs_3_.mine), channel_id=1, source_target_pairs={{0,8},{8,0},{16,24},{24,16},{1,9},{9,1},{17,25},{25,17},{2,10},{10... | collective-permute-start | bytes 2752520 | tf_op jit(solution)/shard_map/ppermute | solution.py:648
  46.6 12.3 %collective-permute-start.11 = (bf16[3,128,512]{2,1,0:T(8,128)(2,1)S(1)}, bf16[3,128,512]{2,1,0:T(8,128)(2,1)S(1)}, u32[]{:S(2)}, u32[]{:S(2)}) collective-permute-start(bf16[3,128,512]{2,1,0:T(8,128)(2,1)S(1)} %get-tuple-element.77.refs_7_), channel_id=1, source_target_pairs={{0,2},{2,4},{4,6},{6,7},{7,5},{5,3},{3,1},{1,0},{8,10},{10,12},{12... | collective-permute-start | bytes 1179656 | tf_op jit(solution)/shard_map/ppermute | solution.py:645
  48.2 12.0 %collective-permute-start.12 = (bf16[3,128,512]{2,1,0:T(8,128)(2,1)S(1)}, bf16[3,128,512]{2,1,0:T(8,128)(2,1)S(1)}, u32[]{:S(2)}, u32[]{:S(2)}) collective-permute-start(bf16[3,128,512]{2,1,0:T(8,128)(2,1)S(1)} %get-tuple-element.78), channel_id=1, source_target_pairs={{0,1},{2,0},{4,2},{6,4},{7,6},{5,7},{3,5},{1,3},{8,9},{10,8},{12,1... | collective-permute-start | bytes 1179656 | tf_op jit(solution)/shard_map/ppermute | solution.py:645
  49.0 18.3 %collective-permute-start.19 = (bf16[3,128,512]{2,1,0:T(8,128)(2,1)S(1)}, bf16[3,128,512]{2,1,0:T(8,128)(2,1)S(1)}, u32[]{:S(2)}, u32[]{:S(2)}) collective-permute-start(bf16[3,128,512]{2,1,0:T(8,128)(2,1)S(1)} %get-tuple-element.86), channel_id=1, source_target_pairs={{0,2},{2,4},{4,6},{6,7},{7,5},{5,3},{3,1},{1,0},{8,10},{10,12},{12... | collective-permute-start | bytes 1179656 | tf_op jit(solution)/shard_map/ppermute | solution.py:645
  50.2 18.4 %collective-permute-start.20 = (bf16[3,128,512]{2,1,0:T(8,128)(2,1)S(1)}, bf16[3,128,512]{2,1,0:T(8,128)(2,1)S(1)}, u32[]{:S(2)}, u32[]{:S(2)}) collective-permute-start(bf16[3,128,512]{2,1,0:T(8,128)(2,1)S(1)} %get-tuple-element.87), channel_id=1, source_target_pairs={{0,1},{2,0},{4,2},{6,4},{7,6},{5,7},{3,5},{1,3},{8,9},{10,8},{12,1... | collective-permute-start | bytes 1179656 | tf_op jit(solution)/shard_map/ppermute | solution.py:645
  62.2 22.0 %collective-permute-start.13 = (bf16[3,256,512]{2,1,0:T(8,128)(2,1)S(1)}, bf16[3,256,512]{2,1,0:T(8,128)(2,1)S(1)}, u32[]{:S(2)}, u32[]{:S(2)}) collective-permute-start(bf16[3,256,512]{2,1,0:T(8,128)(2,1)S(1)} %get-tuple-element.79), channel_id=1, source_target_pairs={{0,2},{2,4},{4,6},{6,7},{7,5},{5,3},{3,1},{1,0},{8,10},{10,12},{12... | collective-permute-start | bytes 2359304 | tf_op jit(solution)/shard_map/ppermute | solution.py:645
  63.9 21.5 %collective-permute-start.14 = (bf16[3,256,512]{2,1,0:T(8,128)(2,1)S(1)}, bf16[3,256,512]{2,1,0:T(8,128)(2,1)S(1)}, u32[]{:S(2)}, u32[]{:S(2)}) collective-permute-start(bf16[3,256,512]{2,1,0:T(8,128)(2,1)S(1)} %get-tuple-element.80), channel_id=1, source_target_pairs={{0,1},{2,0},{4,2},{6,4},{7,6},{5,7},{3,5},{1,3},{8,9},{10,8},{12,1... | collective-permute-start | bytes 2359304 | tf_op jit(solution)/shard_map/ppermute | solution.py:645
  70.6 30.4 %collective-permute-start.21 = (bf16[3,256,512]{2,1,0:T(8,128)(2,1)S(1)}, bf16[3,256,512]{2,1,0:T(8,128)(2,1)S(1)}, u32[]{:S(2)}, u32[]{:S(2)}) collective-permute-start(bf16[3,256,512]{2,1,0:T(8,128)(2,1)S(1)} %get-tuple-element.88), channel_id=1, source_target_pairs={{0,2},{2,4},{4,6},{6,7},{7,5},{5,3},{3,1},{1,0},{8,10},{10,12},{12... | collective-permute-start | bytes 2359304 | tf_op jit(solution)/shard_map/ppermute | solution.py:645
  72.3 29.9 %collective-permute-start.22 = (bf16[3,256,512]{2,1,0:T(8,128)(2,1)S(1)}, bf16[3,256,512]{2,1,0:T(8,128)(2,1)S(1)}, u32[]{:S(2)}, u32[]{:S(2)}) collective-permute-start(bf16[3,256,512]{2,1,0:T(8,128)(2,1)S(1)} %get-tuple-element.89), channel_id=1, source_target_pairs={{0,1},{2,0},{4,2},{6,4},{7,6},{5,7},{3,5},{1,3},{8,9},{10,8},{12,1... | collective-permute-start | bytes 2359304 | tf_op jit(solution)/shard_map/ppermute | solution.py:645
  87.5 30.4 %collective-permute-start.15 = (bf16[3,256,512]{2,1,0:T(8,128)(2,1)S(1)}, bf16[3,256,512]{2,1,0:T(8,128)(2,1)S(1)}, u32[]{:S(2)}, u32[]{:S(2)}) collective-permute-start(bf16[3,256,512]{2,1,0:T(8,128)(2,1)S(1)} %get-tuple-element.81), channel_id=1, source_target_pairs={{0,2},{2,4},{4,6},{6,7},{7,5},{5,3},{3,1},{1,0},{8,10},{10,12},{12... | collective-permute-start | bytes 2359304 | tf_op jit(solution)/shard_map/ppermute | solution.py:645
  89.2 29.9 %collective-permute-start.16 = (bf16[3,256,512]{2,1,0:T(8,128)(2,1)S(1)}, bf16[3,256,512]{2,1,0:T(8,128)(2,1)S(1)}, u32[]{:S(2)}, u32[]{:S(2)}) collective-permute-start(bf16[3,256,512]{2,1,0:T(8,128)(2,1)S(1)} %get-tuple-element.82), channel_id=1, source_target_pairs={{0,1},{2,0},{4,2},{6,4},{7,6},{5,7},{3,5},{1,3},{8,9},{10,8},{12,1... | collective-permute-start | bytes 2359304 | tf_op jit(solution)/shard_map/ppermute | solution.py:645
  104.4 30.4 %collective-permute-start.23 = (bf16[3,256,512]{2,1,0:T(8,128)(2,1)S(1)}, bf16[3,256,512]{2,1,0:T(8,128)(2,1)S(1)}, u32[]{:S(2)}, u32[]{:S(2)}) collective-permute-start(bf16[3,256,512]{2,1,0:T(8,128)(2,1)S(1)} %get-tuple-element.90), channel_id=1, source_target_pairs={{0,2},{2,4},{4,6},{6,7},{7,5},{5,3},{3,1},{1,0},{8,10},{10,12},{12... | collective-permute-start | bytes 2359304 | tf_op jit(solution)/shard_map/ppermute | solution.py:645
  106.0 29.9 %collective-permute-start.24 = (bf16[3,256,512]{2,1,0:T(8,128)(2,1)S(1)}, bf16[3,256,512]{2,1,0:T(8,128)(2,1)S(1)}, u32[]{:S(2)}, u32[]{:S(2)}) collective-permute-start(bf16[3,256,512]{2,1,0:T(8,128)(2,1)S(1)} %get-tuple-element.91), channel_id=1, source_target_pairs={{0,1},{2,0},{4,2},{6,4},{7,6},{5,7},{3,5},{1,3},{8,9},{10,8},{12,1... | collective-permute-start | bytes 2359304 | tf_op jit(solution)/shard_map/ppermute | solution.py:645
  107.6 28.4 %copy-start.1 = (bf16[512,2048]{1,0:T(8,128)(2,1)}, bf16[512,2048]{1,0:T(8,128)(2,1)S(1)}, u32[]{:S(2)}) copy-start(bf16[512,2048]{1,0:T(8,128)(2,1)S(1)} %turn.1.refs_9_.refs_0_) | copy-start | bytes 6291460
  121.2 30.4 %collective-permute-start.17 = (bf16[3,256,512]{2,1,0:T(8,128)(2,1)S(1)}, bf16[3,256,512]{2,1,0:T(8,128)(2,1)S(1)}, u32[]{:S(2)}, u32[]{:S(2)}) collective-permute-start(bf16[3,256,512]{2,1,0:T(8,128)(2,1)S(1)} %get-tuple-element.83), channel_id=1, source_target_pairs={{0,2},{2,4},{4,6},{6,7},{7,5},{5,3},{3,1},{1,0},{8,10},{10,12},{12... | collective-permute-start | bytes 2359304 | tf_op jit(solution)/shard_map/ppermute | solution.py:645
  122.9 29.9 %copy-start.21 = (bf16[256,1024]{1,0:T(8,128)(2,1)S(1)}, bf16[256,1024]{1,0:T(8,128)(2,1)}, u32[]{:S(2)}) copy-start(bf16[256,1024]{1,0:T(8,128)(2,1)} %d_out.3) | copy-start | bytes 1572868
  122.9 29.9 %collective-permute-start.18 = (bf16[3,256,512]{2,1,0:T(8,128)(2,1)S(1)}, bf16[3,256,512]{2,1,0:T(8,128)(2,1)S(1)}, u32[]{:S(2)}, u32[]{:S(2)}) collective-permute-start(bf16[3,256,512]{2,1,0:T(8,128)(2,1)S(1)} %get-tuple-element.84), channel_id=1, source_target_pairs={{0,1},{2,0},{4,2},{6,4},{7,6},{5,7},{3,5},{1,3},{8,9},{10,8},{12,1... | collective-permute-start | bytes 2359304 | tf_op jit(solution)/shard_map/ppermute | solution.py:645
  138.1 30.4 %collective-permute-start.25 = (bf16[3,256,512]{2,1,0:T(8,128)(2,1)S(1)}, bf16[3,256,512]{2,1,0:T(8,128)(2,1)S(1)}, u32[]{:S(2)}, u32[]{:S(2)}) collective-permute-start(bf16[3,256,512]{2,1,0:T(8,128)(2,1)S(1)} %get-tuple-element.92), channel_id=1, source_target_pairs={{0,2},{2,4},{4,6},{6,7},{7,5},{5,3},{3,1},{1,0},{8,10},{10,12},{12... | collective-permute-start | bytes 2359304 | tf_op jit(solution)/shard_map/ppermute | solution.py:645
  139.8 29.9 %collective-permute-start.26 = (bf16[3,256,512]{2,1,0:T(8,128)(2,1)S(1)}, bf16[3,256,512]{2,1,0:T(8,128)(2,1)S(1)}, u32[]{:S(2)}, u32[]{:S(2)}) collective-permute-start(bf16[3,256,512]{2,1,0:T(8,128)(2,1)S(1)} %get-tuple-element.93), channel_id=1, source_target_pairs={{0,1},{2,0},{4,2},{6,4},{7,6},{5,7},{3,5},{1,3},{8,9},{10,8},{12,1... | collective-permute-start | bytes 2359304 | tf_op jit(solution)/shard_map/ppermute | solution.py:645
  160.7 16.2 %copy-start.5 = (bf16[3,256,512]{2,1,0:T(8,128)(2,1)}, bf16[3,256,512]{2,1,0:T(8,128)(2,1)S(1)}, u32[]{:S(2)}) copy-start(bf16[3,256,512]{2,1,0:T(8,128)(2,1)S(1)} %get-tuple-element.99.refs_0_.refs_1_) | copy-start | bytes 2359300
  160.7 24.6 %collective-permute-start.29 = (bf16[3,256,512]{2,1,0:T(8,128)(2,1)S(1)}, bf16[3,256,512]{2,1,0:T(8,128)(2,1)S(1)}, u32[]{:S(2)}, u32[]{:S(2)}) collective-permute-start(bf16[3,256,512]{2,1,0:T(8,128)(2,1)S(1)} %get-tuple-element.99.refs_0_.refs_1_), channel_id=1, source_target_pairs={{0,2},{2,4},{4,6},{6,7},{7,5},{5,3},{3,1},{1,0},{8,10},{10,12},{12... | collective-permute-start | bytes 2359304 | tf_op jit(solution)/shard_map/ppermute | solution.py:645
  162.4 25.0 %collective-permute-start.32 = (bf16[3,256,512]{2,1,0:T(8,128)(2,1)S(1)}, bf16[3,256,512]{2,1,0:T(8,128)(2,1)S(1)}, u32[]{:S(2)}, u32[]{:S(2)}) collective-permute-start(bf16[3,256,512]{2,1,0:T(8,128)(2,1)S(1)} %get-tuple-element.99.refs_0_.refs_1_), channel_id=1, source_target_pairs={{0,1},{2,0},{4,2},{6,4},{7,6},{5,7},{3,5},{1,3},{8,9},{10,8},{12,1... | collective-permute-start | bytes 2359304 | tf_op jit(solution)/shard_map/ppermute | solution.py:645
  178.3 23.8 %collective-permute-start.37 = (bf16[3,256,512]{2,1,0:T(8,128)(2,1)S(1)}, bf16[3,256,512]{2,1,0:T(8,128)(2,1)S(1)}, u32[]{:S(2)}, u32[]{:S(2)}) collective-permute-start(bf16[3,256,512]{2,1,0:T(8,128)(2,1)S(1)} %get-tuple-element.104.refs_0_.refs_1_), channel_id=1, source_target_pairs={{0,2},{2,4},{4,6},{6,7},{7,5},{5,3},{3,1},{1,0},{8,10},{10,12},{12... | collective-permute-start | bytes 2359304 | tf_op jit(solution)/shard_map/ppermute | solution.py:645
  180.0 24.3 %collective-permute-start.40 = (bf16[3,256,512]{2,1,0:T(8,128)(2,1)S(1)}, bf16[3,256,512]{2,1,0:T(8,128)(2,1)S(1)}, u32[]{:S(2)}, u32[]{:S(2)}) collective-permute-start(bf16[3,256,512]{2,1,0:T(8,128)(2,1)S(1)} %get-tuple-element.104.refs_0_.refs_1_), channel_id=1, source_target_pairs={{0,1},{2,0},{4,2},{6,4},{7,6},{5,7},{3,5},{1,3},{8,9},{10,8},{12,1... | collective-permute-start | bytes 2359304 | tf_op jit(solution)/shard_map/ppermute | solution.py:645
  185.3 33.8 %collective-permute-start.30 = (bf16[3,256,512]{2,1,0:T(8,128)(2,1)S(1)}, bf16[3,256,512]{2,1,0:T(8,128)(2,1)}, u32[]{:S(2)}, u32[]{:S(2)}) collective-permute-start(bf16[3,256,512]{2,1,0:T(8,128)(2,1)S(1)} %collective-permute-done.29.refs_1_.refs_2_), channel_id=1, source_target_pairs={{0,2},{2,4},{4,6},{6,7},{7,5},{5,3},{3,1},{1,0},{8,10},{10,12},{12... | collective-permute-start | bytes 2359304 | tf_op jit(solution)/shard_map/ppermute | solution.py:645
  187.4 33.0 %collective-permute-start.33 = (bf16[3,256,512]{2,1,0:T(8,128)(2,1)S(1)}, bf16[3,256,512]{2,1,0:T(8,128)(2,1)}, u32[]{:S(2)}, u32[]{:S(2)}) collective-permute-start(bf16[3,256,512]{2,1,0:T(8,128)(2,1)S(1)} %collective-permute-done.32.refs_2_.refs_3_), channel_id=1, source_target_pairs={{0,1},{2,0},{4,2},{6,4},{7,6},{5,7},{3,5},{1,3},{8,9},{10,8},{12,1... | collective-permute-start | bytes 2359304 | tf_op jit(solution)/shard_map/ppermute | solution.py:645
  202.2 33.8 %collective-permute-start.38 = (bf16[3,256,512]{2,1,0:T(8,128)(2,1)S(1)}, bf16[3,256,512]{2,1,0:T(8,128)(2,1)}, u32[]{:S(2)}, u32[]{:S(2)}) collective-permute-start(bf16[3,256,512]{2,1,0:T(8,128)(2,1)S(1)} %collective-permute-done.37.refs_1_.refs_2_), channel_id=1, source_target_pairs={{0,2},{2,4},{4,6},{6,7},{7,5},{5,3},{3,1},{1,0},{8,10},{10,12},{12... | collective-permute-start | bytes 2359304 | tf_op jit(solution)/shard_map/ppermute | solution.py:645
  204.3 33.0 %collective-permute-start.41 = (bf16[3,256,512]{2,1,0:T(8,128)(2,1)S(1)}, bf16[3,256,512]{2,1,0:T(8,128)(2,1)}, u32[]{:S(2)}, u32[]{:S(2)}) collective-permute-start(bf16[3,256,512]{2,1,0:T(8,128)(2,1)S(1)} %collective-permute-done.40.refs_2_.refs_3_), channel_id=1, source_target_pairs={{0,1},{2,0},{4,2},{6,4},{7,6},{5,7},{3,5},{1,3},{8,9},{10,8},{12,1... | collective-permute-start | bytes 2359304 | tf_op jit(solution)/shard_map/ppermute | solution.py:645
  219.1 34.7 %collective-permute-start.31 = (bf16[3,256,512]{2,1,0:T(8,128)(2,1)}, bf16[3,256,512]{2,1,0:T(8,128)(2,1)}, u32[]{:S(2)}, u32[]{:S(2)}) collective-permute-start(bf16[3,256,512]{2,1,0:T(8,128)(2,1)} %collective-permute-done.30.refs_0_.refs_4_), channel_id=1, source_target_pairs={{0,2},{2,4},{4,6},{6,7},{7,5},{5,3},{3,1},{1,0},{8,10},{10,12},{12... | collective-permute-start | bytes 2359304 | tf_op jit(solution)/shard_map/ppermute | solution.py:645
  220.4 33.7 %collective-permute-start.34 = (bf16[3,256,512]{2,1,0:T(8,128)(2,1)}, bf16[3,256,512]{2,1,0:T(8,128)(2,1)}, u32[]{:S(2)}, u32[]{:S(2)}) collective-permute-start(bf16[3,256,512]{2,1,0:T(8,128)(2,1)} %collective-permute-done.33.refs_1_.refs_5_), channel_id=1, source_target_pairs={{0,1},{2,0},{4,2},{6,4},{7,6},{5,7},{3,5},{1,3},{8,9},{10,8},{12,1... | collective-permute-start | bytes 2359304 | tf_op jit(solution)/shard_map/ppermute | solution.py:645
  236.0 33.7 %collective-permute-start.39 = (bf16[3,256,512]{2,1,0:T(8,128)(2,1)}, bf16[3,256,512]{2,1,0:T(8,128)(2,1)}, u32[]{:S(2)}, u32[]{:S(2)}) collective-permute-start(bf16[3,256,512]{2,1,0:T(8,128)(2,1)} %collective-permute-done.38.refs_0_.refs_4_), channel_id=1, source_target_pairs={{0,2},{2,4},{4,6},{6,7},{7,5},{5,3},{3,1},{1,0},{8,10},{10,12},{12... | collective-permute-start | bytes 2359304 | tf_op jit(solution)/shard_map/ppermute | solution.py:645
  237.2 33.7 %collective-permute-start.42 = (bf16[3,256,512]{2,1,0:T(8,128)(2,1)}, bf16[3,256,512]{2,1,0:T(8,128)(2,1)}, u32[]{:S(2)}, u32[]{:S(2)}) collective-permute-start(bf16[3,256,512]{2,1,0:T(8,128)(2,1)} %collective-permute-done.41.refs_1_.refs_5_), channel_id=1, source_target_pairs={{0,1},{2,0},{4,2},{6,4},{7,6},{5,7},{3,5},{1,3},{8,9},{10,8},{12,1... | collective-permute-start | bytes 2359304 | tf_op jit(solution)/shard_map/ppermute | solution.py:645
  240.9 1.6 collective-permute-start.27
  243.3 5.6 %collective-permute-start.28 = (f32[256,1]{1,0:T(8,128)S(1)}, f32[256,1]{1,0:T(8,128)S(1)}, u32[]{:S(2)}, u32[]{:S(2)}) collective-permute-start(f32[256,1]{1,0:T(8,128)S(1)} %add.31), channel_id=1, source_target_pairs={{0,16},{8,24},{16,0},{24,8},{1,17},{9,25},{17,1},{25,9},{2,18},{10... | collective-permute-start | bytes 3080 | tf_op jit(solution)/shard_map/ppermute | solution.py:648
  252.4 5.2 %copy-start.16 = (bf16[3,256,512]{2,1,0:T(8,128)(2,1)S(1)}, bf16[3,256,512]{2,1,0:T(8,128)(2,1)}, u32[]{:S(2)}) copy-start(bf16[3,256,512]{2,1,0:T(8,128)(2,1)} %copy-done.15) | copy-start | bytes 2359300
  252.4 5.2 %copy-start.18 = (bf16[3,256,512]{2,1,0:T(8,128)(2,1)S(1)}, bf16[3,256,512]{2,1,0:T(8,128)(2,1)}, u32[]{:S(2)}) copy-start(bf16[3,256,512]{2,1,0:T(8,128)(2,1)} %copy-done.17) | copy-start | bytes 2359300
  252.4 5.2 %copy-start.20 = (bf16[3,256,512]{2,1,0:T(8,128)(2,1)S(1)}, bf16[3,256,512]{2,1,0:T(8,128)(2,1)}, u32[]{:S(2)}) copy-start(bf16[3,256,512]{2,1,0:T(8,128)(2,1)} %copy-done.19) | copy-start | bytes 2359300
  255.5 23.8 %collective-permute-start.35 = (bf16[3,128,512]{2,1,0:T(8,128)(2,1)S(1)}, bf16[3,128,512]{2,1,0:T(8,128)(2,1)S(1)}, u32[]{:S(2)}, u32[]{:S(2)}) collective-permute-start(bf16[3,128,512]{2,1,0:T(8,128)(2,1)S(1)} %get-tuple-element.100), channel_id=1, source_target_pairs={{0,2},{2,4},{4,6},{6,7},{7,5},{5,3},{3,1},{1,0},{8,10},{10,12},{12... | collective-permute-start | bytes 1179656 | tf_op jit(solution)/shard_map/ppermute | solution.py:645
  257.2 22.1 %collective-permute-start.36 = (bf16[3,128,512]{2,1,0:T(8,128)(2,1)S(1)}, bf16[3,128,512]{2,1,0:T(8,128)(2,1)S(1)}, u32[]{:S(2)}, u32[]{:S(2)}) collective-permute-start(bf16[3,128,512]{2,1,0:T(8,128)(2,1)S(1)} %get-tuple-element.101), channel_id=1, source_target_pairs={{0,1},{2,0},{4,2},{6,4},{7,6},{5,7},{3,5},{1,3},{8,9},{10,8},{12,1... | collective-permute-start | bytes 1179656 | tf_op jit(solution)/shard_map/ppermute | solution.py:645
  272.3 15.1 %collective-permute-start.43 = (bf16[3,128,512]{2,1,0:T(8,128)(2,1)S(1)}, bf16[3,128,512]{2,1,0:T(8,128)(2,1)S(1)}, u32[]{:S(2)}, u32[]{:S(2)}) collective-permute-start(bf16[3,128,512]{2,1,0:T(8,128)(2,1)S(1)} %get-tuple-element.115), channel_id=1, source_target_pairs={{0,2},{2,4},{4,6},{6,7},{7,5},{5,3},{3,1},{1,0},{8,10},{10,12},{12... | collective-permute-start | bytes 1179656 | tf_op jit(solution)/shard_map/ppermute | solution.py:645
  274.0 13.4 %collective-permute-start.44 = (bf16[3,128,512]{2,1,0:T(8,128)(2,1)S(1)}, bf16[3,128,512]{2,1,0:T(8,128)(2,1)S(1)}, u32[]{:S(2)}, u32[]{:S(2)}) collective-permute-start(bf16[3,128,512]{2,1,0:T(8,128)(2,1)S(1)} %get-tuple-element.116), channel_id=1, source_target_pairs={{0,1},{2,0},{4,2},{6,4},{7,6},{5,7},{3,5},{1,3},{8,9},{10,8},{12,1... | collective-permute-start | bytes 1179656 | tf_op jit(solution)/shard_map/ppermute | solution.py:645
  276.8 3.1 copy-start.13
  291.9 5.4 %copy-start.23 = (bf16[256,512]{1,0:T(8,128)(2,1)S(1)}, bf16[256,512]{1,0:T(8,128)(2,1)}, u32[]{:S(2)}) copy-start(bf16[256,512]{1,0:T(8,128)(2,1)} %copy-done.22) | copy-start | bytes 786436
  291.9 2.0 collective-permute-start.49
  292.0 3.1 collective-permute-start.45
  294.5 9.2 %collective-permute-start.50 = (bf16[2,128,512]{2,1,0:T(8,128)(2,1)S(1)}, bf16[2,128,512]{2,1,0:T(8,128)(2,1)S(1)}, u32[]{:S(2)}, u32[]{:S(2)}) collective-permute-start(bf16[2,128,512]{2,1,0:T(8,128)(2,1)S(1)} %get-tuple-element.130), channel_id=1, source_target_pairs={{0,16},{8,24},{16,0},{24,8},{1,17},{9,25},{17,1},{25,9},{2,18},{10... | collective-permute-start | bytes 786440 | tf_op jit(solution)/shard_map/ppermute | solution.py:648
  295.8 14.6 %collective-permute-start.46 = (bf16[2,128,512]{2,1,0:T(8,128)(2,1)S(1)}, bf16[2,128,512]{2,1,0:T(8,128)(2,1)S(1)}, u32[]{:S(2)}, u32[]{:S(2)}) collective-permute-start(bf16[2,128,512]{2,1,0:T(8,128)(2,1)S(1)} %get-tuple-element.124), channel_id=1, source_target_pairs={{0,16},{8,24},{16,0},{24,8},{1,17},{9,25},{17,1},{25,9},{2,18},{10... | collective-permute-start | bytes 786440 | tf_op jit(solution)/shard_map/ppermute | solution.py:648
  304.3 19.4 %collective-permute-start.51 = (bf16[128,512]{1,0:T(8,128)(2,1)S(1)}, bf16[128,512]{1,0:T(8,128)(2,1)S(1)}, u32[]{:S(2)}, u32[]{:S(2)}) collective-permute-start(bf16[128,512]{1,0:T(8,128)(2,1)S(1)} %get-tuple-element.131.refs_12_), channel_id=1, source_target_pairs={{0,0},{1,1},{2,8},{3,9},{4,16},{5,17},{6,24},{7,25},{8,2},{9,3},{1... | collective-permute-start | bytes 393224 | tf_op jit(solution)/shard_map/ppermute | solution.py:710
  309.4 18.3 %collective-permute-start.52 = (bf16[128,512]{1,0:T(8,128)(2,1)S(1)}, bf16[128,512]{1,0:T(8,128)(2,1)S(1)}, u32[]{:S(2)}, u32[]{:S(2)}) collective-permute-start(bf16[128,512]{1,0:T(8,128)(2,1)S(1)} %get-tuple-element.132), channel_id=1, source_target_pairs={{0,1},{1,0},{2,9},{3,8},{4,17},{5,16},{6,25},{7,24},{8,3},{9,2},{1... | collective-permute-start | bytes 393224 | tf_op jit(solution)/shard_map/ppermute | solution.py:710
  311.0 19.0 %collective-permute-start.47 = (bf16[128,512]{1,0:T(8,128)(2,1)S(1)}, bf16[128,512]{1,0:T(8,128)(2,1)S(1)}, u32[]{:S(2)}, u32[]{:S(2)}) collective-permute-start(bf16[128,512]{1,0:T(8,128)(2,1)S(1)} %get-tuple-element.125.refs_11_), channel_id=1, source_target_pairs={{0,0},{1,1},{2,8},{3,9},{4,16},{5,17},{6,24},{7,25},{8,2},{9,3},{1... | collective-permute-start | bytes 393224 | tf_op jit(solution)/shard_map/ppermute | solution.py:710
  314.5 18.7 %copy-start.4 = (bf16[256,4096]{1,0:T(8,128)(2,1)S(1)}, bf16[256,4096]{1,0:T(8,128)(2,1)}, u32[]{:S(2)}) copy-start(bf16[256,4096]{1,0:T(8,128)(2,1)} %tokens.3) | copy-start | bytes 6291460
  314.5 18.7 %copy-start.25 = (f32[256,128]{1,0:T(8,128)S(1)}, f32[256,128]{1,0:T(8,128)}, u32[]{:S(2)}) copy-start(f32[256,128]{1,0:T(8,128)} %copy-done.24) | copy-start | bytes 393220
  314.5 18.7 %collective-permute-start.48 = (bf16[128,512]{1,0:T(8,128)(2,1)S(1)}, bf16[128,512]{1,0:T(8,128)(2,1)S(1)}, u32[]{:S(2)}, u32[]{:S(2)}) collective-permute-start(bf16[128,512]{1,0:T(8,128)(2,1)S(1)} %get-tuple-element.126), channel_id=1, source_target_pairs={{0,1},{1,0},{2,9},{3,8},{4,17},{5,16},{6,25},{7,24},{8,3},{9,2},{1... | collective-permute-start | bytes 393224 | tf_op jit(solution)/shard_map/ppermute | solution.py:710
  (18 other events, 22.3 us)

commit v9 on v7

--- a/solution.py
+++ b/solution.py
@@ -195,19 +195,19 @@
     left_out[...] = left[:, half:]
 
 
-def halve(right, left, ties):
+def halve(right, left):
     _, rows, wide = right.shape
     result = jax.ShapeDtypeStruct((3, rows // 2, wide), right.dtype)
     whole = pl.BlockSpec(memory_space=pltpu.VMEM)
     return pl.pallas_call(
-        tied(halve_kernel, 2, len(ties)),
-        in_specs=[whole, whole] + tie_specs(ties),
+        halve_kernel,
+        in_specs=[whole, whole],
         out_specs=[whole, whole],
         out_shape=[result, result],
         compiler_params=pltpu.CompilerParams(vmem_limit_bytes=4 * MIB),
         cost_estimate=cost(0, 6 * rows * wide),
         name="halve",
-    )(right, left, *ties)
+    )(right, left)
 
 
 def turn_kernel(count, idx, mine, other, mine_far, other_far, out):
@@ -689,8 +689,7 @@
         for chunk in range(2):
             right, left = moving[chunk]
             if step == far:
-                early = [dots] if chunk == 0 else terms[1][: size - 3]
-                right, left = halve(right, left, early)
+                right, left = halve(right, left)
             right, left = shift(right, 1), shift(left, -1)
             moving[chunk] = right, left
             gathered[chunk] += [right, left]

time: 320 us -> 333 us (1.041)
  waiting for transfers between devices: 164 us -> 188 us
  Pallas kernels: 66.4 us -> 57.3 us
    ppermute x39, waiting for transfers between devices: 151 us -> 180 us  [shift(): return lax.ppermute(array, 'local', moves)]
    ppermute x8, waiting for transfers between devices: 13.5 us -> 8.02 us  [swap(): return lax.ppermute(array, 'node', [(n, n ^ bit) for n in range(nodes)])]
    pallas_call x7, Pallas kernels: 12.7 us -> 7.22 us  [term_step(): pl.pallas_call(kernel, in_specs=[whole] * (1 + count + len(befores)), out...]
    unnamed x56 -> x96, local copies, waits for them, and re-layouts: 14.9 us -> 12.3 us
  transfers between devices with their start and end apart: 51 -> 51, of which waited for: 24 -> 25; matrix products, arithmetic and copies ran while one was open for 2% -> 2% of each run, Pallas kernels for 19% -> 16%
where the time goes in v9:
time: 333 us; the launch traced here: 332 us
  waiting for transfers between devices  188 us (56%)
  starting transfers between devices  65.5 us (20%)
  Pallas kernels  57.3 us (17%)
  local copies, waits for them, and re-layouts  14.5 us (4%)
  other arithmetic  5.45 us (2%)
    ppermute x39, waiting for transfers between devices, shift(): return lax.ppermute(array, 'local', moves)  180 us
    ppermute x39, starting transfers between devices, shift(): return lax.ppermute(array, 'local', moves)  49.4 us
    pallas_call x2, Pallas kernels, attention(): pl.pallas_call(attention_kernel, grid_spec=pltpu.PrefetchScalarGridSpec(n...  14.5 us
    ppermute x4, starting transfers between devices, relocate(): came.append(lax.ppermute(block, ('node', 'local'), moves))  12.7 us
    pallas_call x6, Pallas kernels, sum_step(): pl.pallas_call(tied(sum_step_kernel, 9, len(ties)), grid_spec=pltpu.Prefe...  12.3 us
    unnamed x96, local copies, waits for them, and re-layouts  12.3 us
    pallas_call x2, Pallas kernels, grads_chunk(): pl.pallas_call(tied(grads_kernel, 1 + len(pieces), len(ties)), grid=(3,),...  9.49 us
    ppermute x8, waiting for transfers between devices, swap(): return lax.ppermute(array, 'node', [(n, n ^ bit) for n in range(nodes)])  8.02 us
  transfers between devices with their start and end apart: 51, of which 25 were waited for; matrix products, arithmetic and copies ran while one was open for 2% of the time, Pallas kernels for 16%

profile of v9, /device:TPU:2, one launch (start us, length us, event | category | flops | bytes accessed | tf_op | source)
XLA Modules:
  0.0 331.8 jit_solution(4641405715541065576)
XLA Ops:
  2.1 1.6 copy-done
  3.6 1.4 normed_blocks.1
  5.1 4.6 %collective-permute-start.6 = (bf16[256,256]{1,0:T(8,128)(2,1)S(1)}, bf16[256,256]{1,0:T(8,128)(2,1)S(1)}, u32[]{:S(2)}, u32[]{:S(2)}) collective-permute-start(bf16[256,256]{1,0:T(8,128)(2,1)S(1)} %get-tuple-element.75), channel_id=1, source_target_pairs={{0,7},{2,5},{4,3},{6,1},{7,0},{5,2},{3,4},{1,6},{8,15},{10,13},{12... | collective-permute-start | bytes 393224 | tf_op jit(solution)/shard_map/ppermute | solution.py:621
  9.7 4.5 %collective-permute-done.6.mine.mine_far = bf16[256,256]{1,0:T(8,128)(2,1)S(1)} collective-permute-done((bf16[256,256]{1,0:T(8,128)(2,1)S(1)}, bf16[256,256]{1,0:T(8,128)(2,1)S(1)}, u32[]{:S(2)}, u32[]{:S(2)}) %collective-permute-start.6) | collective-permute-done | bytes 131104 | tf_op jit(solution)/shard_map/ppermute | solution.py:621
  14.7 3.4 %collective-permute-start.2 = (bf16[256,256]{1,0:T(8,128)(2,1)S(1)}, bf16[256,256]{1,0:T(8,128)(2,1)S(1)}, u32[]{:S(2)}, u32[]{:S(2)}) collective-permute-start(bf16[256,256]{1,0:T(8,128)(2,1)S(1)} %get-tuple-element.71), channel_id=1, source_target_pairs={{0,4},{2,6},{4,7},{6,5},{7,3},{5,1},{3,0},{1,2},{8,12},{10,14},{12... | collective-permute-start | bytes 393224 | tf_op jit(solution)/shard_map/ppermute | solution.py:621
  19.4 1.7 collective-permute-start.4
  21.1 2.1 collective-permute-start.5
  23.2 1.9 copy-done.28
  26.9 1.9 sum_first.1
  28.9 4.6 %collective-permute-done.3.refs_4_ = bf16[256,256]{1,0:T(8,128)(2,1)S(1)} collective-permute-done((bf16[256,256]{1,0:T(8,128)(2,1)S(1)}, bf16[256,256]{1,0:T(8,128)(2,1)S(1)}, u32[]{:S(2)}, u32[]{:S(2)}) %collective-permute-start.3) | collective-permute-done | bytes 131104 | tf_op jit(solution)/shard_map/ppermute | solution.py:621
  34.7 3.1 collective-permute-start.10
  37.8 2.1 collective-permute-start.18
  39.9 7.4 %collective-permute-done.10.refs_8_ = bf16[3,128,512]{2,1,0:T(8,128)(2,1)S(1)} collective-permute-done((bf16[3,128,512]{2,1,0:T(8,128)(2,1)S(1)}, bf16[3,128,512]{2,1,0:T(8,128)(2,1)S(1)}, u32[]{:S(2)}, u32[]{:S(2)}) %collective-permute-start.10) | collective-permute-done | bytes 393248 | tf_op jit(solution)/shard_map/ppermute | solution.py:621
  47.2 2.5 collective-permute-done.9.refs_7_
  49.8 2.1 sum_step.6
  51.9 2.0 collective-permute-start.12
  53.9 4.3 %collective-permute-done.17.refs_7_ = bf16[3,128,512]{2,1,0:T(8,128)(2,1)S(1)} collective-permute-done((bf16[3,128,512]{2,1,0:T(8,128)(2,1)S(1)}, bf16[3,128,512]{2,1,0:T(8,128)(2,1)S(1)}, u32[]{:S(2)}, u32[]{:S(2)}) %collective-permute-start.17) | collective-permute-done | bytes 393248 | tf_op jit(solution)/shard_map/ppermute | solution.py:621
  58.2 2.1 sum_step.9
  60.3 2.0 collective-permute-start.20
  62.3 12.7 %collective-permute-done.11.refs_7_ = bf16[3,256,512]{2,1,0:T(8,128)(2,1)S(1)} collective-permute-done((bf16[3,256,512]{2,1,0:T(8,128)(2,1)S(1)}, bf16[3,256,512]{2,1,0:T(8,128)(2,1)S(1)}, u32[]{:S(2)}, u32[]{:S(2)}) %collective-permute-start.11) | collective-permute-done | bytes 786464 | tf_op jit(solution)/shard_map/ppermute | solution.py:621
  75.0 2.1 sum_step.7
  77.2 2.0 collective-permute-start.14
  79.2 12.7 %collective-permute-done.19.refs_7_ = bf16[3,256,512]{2,1,0:T(8,128)(2,1)S(1)} collective-permute-done((bf16[3,256,512]{2,1,0:T(8,128)(2,1)S(1)}, bf16[3,256,512]{2,1,0:T(8,128)(2,1)S(1)}, u32[]{:S(2)}, u32[]{:S(2)}) %collective-permute-start.19) | collective-permute-done | bytes 786464 | tf_op jit(solution)/shard_map/ppermute | solution.py:621
  91.9 2.1 sum_step.10
  94.0 2.0 collective-permute-start.22
  97.2 11.5 %collective-permute-done.13.refs_7_ = bf16[3,256,512]{2,1,0:T(8,128)(2,1)S(1)} collective-permute-done((bf16[3,256,512]{2,1,0:T(8,128)(2,1)S(1)}, bf16[3,256,512]{2,1,0:T(8,128)(2,1)S(1)}, u32[]{:S(2)}, u32[]{:S(2)}) %collective-permute-start.13) | collective-permute-done | bytes 786464 | tf_op jit(solution)/shard_map/ppermute | solution.py:621
  108.7 2.1 sum_step.8
  110.9 2.0 collective-permute-start.16
  112.9 12.7 %collective-permute-done.21.refs_7_ = bf16[3,256,512]{2,1,0:T(8,128)(2,1)S(1)} collective-permute-done((bf16[3,256,512]{2,1,0:T(8,128)(2,1)S(1)}, bf16[3,256,512]{2,1,0:T(8,128)(2,1)S(1)}, u32[]{:S(2)}, u32[]{:S(2)}) %collective-permute-start.21) | collective-permute-done | bytes 786464 | tf_op jit(solution)/shard_map/ppermute | solution.py:621
  125.6 2.1 sum_step.11
  127.7 2.0 collective-permute-start.24
  130.4 12.0 %collective-permute-done.15.from_left = bf16[3,256,512]{2,1,0:T(8,128)(2,1)S(1)} collective-permute-done((bf16[3,256,512]{2,1,0:T(8,128)(2,1)S(1)}, bf16[3,256,512]{2,1,0:T(8,128)(2,1)S(1)}, u32[]{:S(2)}, u32[]{:S(2)}) %collective-permute-start.15) | collective-permute-done | bytes 786464 | tf_op jit(solution)/shard_map/ppermute | solution.py:621
  142.4 7.2 %attention.2 = (bf16[256,512]{1,0:T(8,128)(2,1)S(1)}, f32[256,128]{1,0:T(8,128)S(1)}, bf16[3,256,512]{2,1,0:T(8,128)(2,1)S(1)}) custom-call(s32[39]{0:T(128)S(1)} %dynamic-slice_bitcast_fusion.idx.refs_0_, bf16[7,256,256]{2,1,0:T(8,128)(2,1)S(1)} %stack.1.refs_1_.refs_3_.mine, bf16[7,256,256]{2,1,0:T(8,128)(2,1)S(1)} %collective-permute-done.8.refs_2_.refs_4_.other, ...), custom_call_target="tpu_custom_call" | custom-call | flops 402653184 | bytes 3145728 | tf_op jit(solution)/shard_map/attention/pallas_call | solution.py:389
  149.8 2.0 collective-permute-start.27
  151.8 7.5 %collective-permute-done.23.from_left = bf16[3,256,512]{2,1,0:T(8,128)(2,1)S(1)} collective-permute-done((bf16[3,256,512]{2,1,0:T(8,128)(2,1)S(1)}, bf16[3,256,512]{2,1,0:T(8,128)(2,1)S(1)}, u32[]{:S(2)}, u32[]{:S(2)}) %collective-permute-start.23) | collective-permute-done | bytes 786464 | tf_op jit(solution)/shard_map/ppermute | solution.py:621
  159.3 7.3 %attention.3 = (bf16[256,512]{1,0:T(8,128)(2,1)S(1)}, f32[256,128]{1,0:T(8,128)S(1)}, bf16[3,256,512]{2,1,0:T(8,128)(2,1)S(1)}) custom-call(s32[39]{0:T(128)S(1)} %dynamic-slice_bitcast_fusion.idx.refs_0_, bf16[7,256,256]{2,1,0:T(8,128)(2,1)S(1)} %stack.1.refs_1_.refs_3_.mine, bf16[7,256,256]{2,1,0:T(8,128)(2,1)S(1)} %collective-permute-done.8.refs_2_.refs_4_.other, ...), custom_call_target="tpu_custom_call" | custom-call | flops 402653184 | bytes 3145728 | tf_op jit(solution)/shard_map/attention/pallas_call | solution.py:389
  166.7 2.0 collective-permute-start.35
  168.7 4.9 %collective-permute-done.30.refs_2_.refs_3_ = bf16[3,256,512]{2,1,0:T(8,128)(2,1)S(1)} collective-permute-done((bf16[3,256,512]{2,1,0:T(8,128)(2,1)S(1)}, bf16[3,256,512]{2,1,0:T(8,128)(2,1)S(1)}, u32[]{:S(2)}, u32[]{:S(2)}) %collective-permute-start.30) | collective-permute-done | bytes 786464 | tf_op jit(solution)/shard_map/ppermute | solution.py:621
  173.6 2.5 collective-permute-start.31
  176.2 14.3 %collective-permute-done.38.refs_2_.refs_3_ = bf16[3,256,512]{2,1,0:T(8,128)(2,1)S(1)} collective-permute-done((bf16[3,256,512]{2,1,0:T(8,128)(2,1)S(1)}, bf16[3,256,512]{2,1,0:T(8,128)(2,1)S(1)}, u32[]{:S(2)}, u32[]{:S(2)}) %collective-permute-start.38) | collective-permute-done | bytes 786464 | tf_op jit(solution)/shard_map/ppermute | solution.py:621
  190.5 2.5 collective-permute-start.39
  193.0 14.3 %collective-permute-done.31.refs_1_.refs_5_ = bf16[3,256,512]{2,1,0:T(8,128)(2,1)S(1)} collective-permute-done((bf16[3,256,512]{2,1,0:T(8,128)(2,1)S(1)}, bf16[3,256,512]{2,1,0:T(8,128)(2,1)S(1)}, u32[]{:S(2)}, u32[]{:S(2)}) %collective-permute-start.31) | collective-permute-done | bytes 786464 | tf_op jit(solution)/shard_map/ppermute | solution.py:621
  207.3 2.5 collective-permute-start.32
  209.9 14.3 %collective-permute-done.39.refs_1_.refs_5_ = bf16[3,256,512]{2,1,0:T(8,128)(2,1)S(1)} collective-permute-done((bf16[3,256,512]{2,1,0:T(8,128)(2,1)S(1)}, bf16[3,256,512]{2,1,0:T(8,128)(2,1)S(1)}, u32[]{:S(2)}, u32[]{:S(2)}) %collective-permute-start.39) | collective-permute-done | bytes 786464 | tf_op jit(solution)/shard_map/ppermute | solution.py:621
  224.2 2.5 collective-permute-start.40
  228.1 12.9 %collective-permute-done.32.left.refs_1_.refs_7_ = bf16[3,256,512]{2,1,0:T(8,128)(2,1)S(1)} collective-permute-done((bf16[3,256,512]{2,1,0:T(8,128)(2,1)S(1)}, bf16[3,256,512]{2,1,0:T(8,128)(2,1)S(1)}, u32[]{:S(2)}, u32[]{:S(2)}) %collective-permute-start.32) | collective-permute-done | bytes 786464 | tf_op jit(solution)/shard_map/ppermute | solution.py:621
  241.0 2.5 collective-permute-done.29.right.refs_0_.refs_6_
  243.7 2.0 collective-permute-start.34
  245.7 12.2 %collective-permute-done.40.left.refs_1_.refs_7_ = bf16[3,256,512]{2,1,0:T(8,128)(2,1)S(1)} collective-permute-done((bf16[3,256,512]{2,1,0:T(8,128)(2,1)S(1)}, bf16[3,256,512]{2,1,0:T(8,128)(2,1)S(1)}, u32[]{:S(2)}, u32[]{:S(2)}) %collective-permute-start.40) | collective-permute-done | bytes 786464 | tf_op jit(solution)/shard_map/ppermute | solution.py:621
  257.9 2.5 collective-permute-done.37.right.refs_0_.refs_6_
  260.5 2.0 collective-permute-start.42
  269.4 7.1 %collective-permute-done.41.refs_2_.refs_8_ = bf16[3,128,512]{2,1,0:T(8,128)(2,1)S(1)} collective-permute-done((bf16[3,128,512]{2,1,0:T(8,128)(2,1)S(1)}, bf16[3,128,512]{2,1,0:T(8,128)(2,1)S(1)}, u32[]{:S(2)}, u32[]{:S(2)}) %collective-permute-start.41) | collective-permute-done | bytes 393248 | tf_op jit(solution)/shard_map/ppermute | solution.py:621
  276.5 1.6 term_last.1
  284.9 1.5 collective-permute-start.48
  289.3 1.5 collective-permute-done.25
  292.4 1.8 pad_maximum_fusion
  294.2 5.1 %collective-permute-done.26 = f32[256,1]{1,0:T(8,128)S(1)} collective-permute-done((f32[256,1]{1,0:T(8,128)S(1)}, f32[256,1]{1,0:T(8,128)S(1)}, u32[]{:S(2)}, u32[]{:S(2)}) %collective-permute-start.26) | collective-permute-done | bytes 1056 | tf_op jit(solution)/shard_map/ppermute | solution.py:624
  301.4 2.4 collective-permute-start.46
  303.7 3.1 collective-permute-start.45
  308.9 2.4 collective-permute-start.50
  311.3 4.9 %collective-permute-start.49 = (bf16[128,512]{1,0:T(8,128)(2,1)S(1)}, bf16[128,512]{1,0:T(8,128)(2,1)S(1)}, u32[]{:S(2)}, u32[]{:S(2)}) collective-permute-start(bf16[128,512]{1,0:T(8,128)(2,1)S(1)} %get-tuple-element.131.refs_11_), channel_id=1, source_target_pairs={{0,0},{1,1},{2,8},{3,9},{4,16},{5,17},{6,24},{7,25},{8,2},{9,3},{1... | collective-permute-start | bytes 393224 | tf_op jit(solution)/shard_map/ppermute | solution.py:682
  320.5 4.7 %grads.2.refs_10_ = f32[3,512,1024]{2,1,0:T(8,128)} custom-call(bf16[512,2048]{1,0:T(8,128)(2,1)S(1)} %turn.1.refs_9_.refs_0_, bf16[3,256,512]{2,1,0:T(8,128)(2,1)S(1)} %copy-done.19, bf16[3,256,512]{2,1,0:T(8,128)(2,1)S(1)} %copy-done.23, bf16[3,256,512]{2,1,0:T(8,128)(2,1)S(1)} %copy-done.21, bf16[3,256,512]{2,1,0:T(8,128)(2,1)S(1)} %copy-done.17, ...), custom_call_target="tpu_custom_call" | custom-call | flops 3221225472 | bytes 9437184 | tf_op jit(solution)/shard_map/grads/pallas_call | solution.py:431
  325.3 4.8 %grads.3 = f32[3,512,1024]{2,1,0:T(8,128)} custom-call(bf16[512,2048]{1,0:T(8,128)(2,1)S(1)} %turn.1.refs_9_.refs_0_, bf16[3,256,512]{2,1,0:T(8,128)(2,1)S(1)} %copy-done.9, bf16[3,256,512]{2,1,0:T(8,128)(2,1)S(1)} %copy-done.13, bf16[3,256,512]{2,1,0:T(8,128)(2,1)S(1)} %copy-done.11, ...), custom_call_target="tpu_custom_call", output_to_operand_aliasing={{}: (10, {})} | custom-call | flops 3221225472 | bytes 9437184 | tf_op jit(solution)/shard_map/grads/pallas_call | solution.py:431
  330.2 1.6 finish.1
  (177 shorter events, 36.7 us)
Async XLA Ops:
  1.3 27.5 %copy-start.41 = (bf16[1,4096]{1,0:T(2,128)(2,1)}, bf16[1,4096]{1,0:T(2,128)(2,1)S(1)}, u32[]{:S(2)}) copy-start(bf16[1,4096]{1,0:T(2,128)(2,1)S(1)} %broadcast_in_dim.2.gain) | copy-start | bytes 24580
  5.1 9.1 %collective-permute-start.6 = (bf16[256,256]{1,0:T(8,128)(2,1)S(1)}, bf16[256,256]{1,0:T(8,128)(2,1)S(1)}, u32[]{:S(2)}, u32[]{:S(2)}) collective-permute-start(bf16[256,256]{1,0:T(8,128)(2,1)S(1)} %get-tuple-element.75), channel_id=1, source_target_pairs={{0,7},{2,5},{4,3},{6,1},{7,0},{5,2},{3,4},{1,6},{8,15},{10,13},{12... | collective-permute-start | bytes 393224 | tf_op jit(solution)/shard_map/ppermute | solution.py:621
  9.7 9.7 %collective-permute-start = (bf16[256,256]{1,0:T(8,128)(2,1)S(1)}, bf16[256,256]{1,0:T(8,128)(2,1)S(1)}, u32[]{:S(2)}, u32[]{:S(2)}) collective-permute-start(bf16[256,256]{1,0:T(8,128)(2,1)S(1)} %get-tuple-element.69), channel_id=1, source_target_pairs={{0,2},{2,4},{4,6},{6,7},{7,5},{5,3},{3,1},{1,0},{8,10},{10,12},{12... | collective-permute-start | bytes 393224 | tf_op jit(solution)/shard_map/ppermute | solution.py:621
  14.2 6.9 %collective-permute-start.7 = (bf16[256,256]{1,0:T(8,128)(2,1)S(1)}, bf16[256,256]{1,0:T(8,128)(2,1)S(1)}, u32[]{:S(2)}, u32[]{:S(2)}) collective-permute-start(bf16[256,256]{1,0:T(8,128)(2,1)S(1)} %collective-permute-done.6.mine.mine_far), channel_id=1, source_target_pairs={{0,8},{8,0},{16,24},{24,16},{1,9},{9,1},{17,25},{25,17},{2,10},{10... | collective-permute-start | bytes 393224 | tf_op jit(solution)/shard_map/ppermute | solution.py:624
  14.2 14.6 %collective-permute-start.1 = (bf16[256,256]{1,0:T(8,128)(2,1)S(1)}, bf16[256,256]{1,0:T(8,128)(2,1)S(1)}, u32[]{:S(2)}, u32[]{:S(2)}) collective-permute-start(bf16[256,256]{1,0:T(8,128)(2,1)S(1)} %get-tuple-element.70), channel_id=1, source_target_pairs={{0,1},{2,0},{4,2},{6,4},{7,6},{5,7},{3,5},{1,3},{8,9},{10,8},{12,1... | collective-permute-start | bytes 393224 | tf_op jit(solution)/shard_map/ppermute | solution.py:621
  14.7 14.2 %collective-permute-start.2 = (bf16[256,256]{1,0:T(8,128)(2,1)S(1)}, bf16[256,256]{1,0:T(8,128)(2,1)S(1)}, u32[]{:S(2)}, u32[]{:S(2)}) collective-permute-start(bf16[256,256]{1,0:T(8,128)(2,1)S(1)} %get-tuple-element.71), channel_id=1, source_target_pairs={{0,4},{2,6},{4,7},{6,5},{7,3},{5,1},{3,0},{1,2},{8,12},{10,14},{12... | collective-permute-start | bytes 393224 | tf_op jit(solution)/shard_map/ppermute | solution.py:621
  18.2 15.3 %collective-permute-start.3 = (bf16[256,256]{1,0:T(8,128)(2,1)S(1)}, bf16[256,256]{1,0:T(8,128)(2,1)S(1)}, u32[]{:S(2)}, u32[]{:S(2)}) collective-permute-start(bf16[256,256]{1,0:T(8,128)(2,1)S(1)} %get-tuple-element.72), channel_id=1, source_target_pairs={{0,3},{2,1},{4,0},{6,2},{7,4},{5,6},{3,7},{1,5},{8,11},{10,9},{12,... | collective-permute-start | bytes 393224 | tf_op jit(solution)/shard_map/ppermute | solution.py:621
  19.4 15.2 %collective-permute-start.4 = (bf16[256,256]{1,0:T(8,128)(2,1)S(1)}, bf16[256,256]{1,0:T(8,128)(2,1)S(1)}, u32[]{:S(2)}, u32[]{:S(2)}) collective-permute-start(bf16[256,256]{1,0:T(8,128)(2,1)S(1)} %get-tuple-element.73), channel_id=1, source_target_pairs={{0,6},{2,7},{4,5},{6,3},{7,1},{5,0},{3,2},{1,4},{8,14},{10,15},{12... | collective-permute-start | bytes 393224 | tf_op jit(solution)/shard_map/ppermute | solution.py:621
  21.1 13.4 %collective-permute-start.5 = (bf16[256,256]{1,0:T(8,128)(2,1)S(1)}, bf16[256,256]{1,0:T(8,128)(2,1)S(1)}, u32[]{:S(2)}, u32[]{:S(2)}) collective-permute-start(bf16[256,256]{1,0:T(8,128)(2,1)S(1)} %get-tuple-element.74), channel_id=1, source_target_pairs={{0,5},{2,3},{4,1},{6,0},{7,2},{5,4},{3,6},{1,7},{8,13},{10,11},{12... | collective-permute-start | bytes 393224 | tf_op jit(solution)/shard_map/ppermute | solution.py:621
  34.6 15.1 %collective-permute-start.8 = (bf16[7,256,256]{2,1,0:T(8,128)(2,1)S(1)}, bf16[7,256,256]{2,1,0:T(8,128)(2,1)S(1)}, u32[]{:S(2)}, u32[]{:S(2)}) collective-permute-start(bf16[7,256,256]{2,1,0:T(8,128)(2,1)S(1)} %stack.1.refs_1_.refs_3_.mine), channel_id=1, source_target_pairs={{0,8},{8,0},{16,24},{24,16},{1,9},{9,1},{17,25},{25,17},{2,10},{10... | collective-permute-start | bytes 2752520 | tf_op jit(solution)/shard_map/ppermute | solution.py:624
  34.7 12.5 %collective-permute-start.10 = (bf16[3,128,512]{2,1,0:T(8,128)(2,1)S(1)}, bf16[3,128,512]{2,1,0:T(8,128)(2,1)S(1)}, u32[]{:S(2)}, u32[]{:S(2)}) collective-permute-start(bf16[3,128,512]{2,1,0:T(8,128)(2,1)S(1)} %get-tuple-element.78), channel_id=1, source_target_pairs={{0,1},{2,0},{4,2},{6,4},{7,6},{5,7},{3,5},{1,3},{8,9},{10,8},{12,1... | collective-permute-start | bytes 1179656 | tf_op jit(solution)/shard_map/ppermute | solution.py:621
  37.8 12.0 %collective-permute-start.9 = (bf16[3,128,512]{2,1,0:T(8,128)(2,1)S(1)}, bf16[3,128,512]{2,1,0:T(8,128)(2,1)S(1)}, u32[]{:S(2)}, u32[]{:S(2)}) collective-permute-start(bf16[3,128,512]{2,1,0:T(8,128)(2,1)S(1)} %get-tuple-element.77.refs_7_), channel_id=1, source_target_pairs={{0,2},{2,4},{4,6},{6,7},{7,5},{5,3},{3,1},{1,0},{8,10},{10,12},{12... | collective-permute-start | bytes 1179656 | tf_op jit(solution)/shard_map/ppermute | solution.py:621
  37.8 20.4 %collective-permute-start.17 = (bf16[3,128,512]{2,1,0:T(8,128)(2,1)S(1)}, bf16[3,128,512]{2,1,0:T(8,128)(2,1)S(1)}, u32[]{:S(2)}, u32[]{:S(2)}) collective-permute-start(bf16[3,128,512]{2,1,0:T(8,128)(2,1)S(1)} %get-tuple-element.86), channel_id=1, source_target_pairs={{0,2},{2,4},{4,6},{6,7},{7,5},{5,3},{3,1},{1,0},{8,10},{10,12},{12... | collective-permute-start | bytes 1179656 | tf_op jit(solution)/shard_map/ppermute | solution.py:621
  37.8 20.4 %collective-permute-start.18 = (bf16[3,128,512]{2,1,0:T(8,128)(2,1)S(1)}, bf16[3,128,512]{2,1,0:T(8,128)(2,1)S(1)}, u32[]{:S(2)}, u32[]{:S(2)}) collective-permute-start(bf16[3,128,512]{2,1,0:T(8,128)(2,1)S(1)} %get-tuple-element.87), channel_id=1, source_target_pairs={{0,1},{2,0},{4,2},{6,4},{7,6},{5,7},{3,5},{1,3},{8,9},{10,8},{12,1... | collective-permute-start | bytes 1179656 | tf_op jit(solution)/shard_map/ppermute | solution.py:621
  51.8 23.2 %collective-permute-start.11 = (bf16[3,256,512]{2,1,0:T(8,128)(2,1)S(1)}, bf16[3,256,512]{2,1,0:T(8,128)(2,1)S(1)}, u32[]{:S(2)}, u32[]{:S(2)}) collective-permute-start(bf16[3,256,512]{2,1,0:T(8,128)(2,1)S(1)} %get-tuple-element.79), channel_id=1, source_target_pairs={{0,2},{2,4},{4,6},{6,7},{7,5},{5,3},{3,1},{1,0},{8,10},{10,12},{12... | collective-permute-start | bytes 2359304 | tf_op jit(solution)/shard_map/ppermute | solution.py:621
  51.9 23.1 %collective-permute-start.12 = (bf16[3,256,512]{2,1,0:T(8,128)(2,1)S(1)}, bf16[3,256,512]{2,1,0:T(8,128)(2,1)S(1)}, u32[]{:S(2)}, u32[]{:S(2)}) collective-permute-start(bf16[3,256,512]{2,1,0:T(8,128)(2,1)S(1)} %get-tuple-element.80), channel_id=1, source_target_pairs={{0,1},{2,0},{4,2},{6,4},{7,6},{5,7},{3,5},{1,3},{8,9},{10,8},{12,1... | collective-permute-start | bytes 2359304 | tf_op jit(solution)/shard_map/ppermute | solution.py:621
  60.2 31.6 %collective-permute-start.19 = (bf16[3,256,512]{2,1,0:T(8,128)(2,1)S(1)}, bf16[3,256,512]{2,1,0:T(8,128)(2,1)S(1)}, u32[]{:S(2)}, u32[]{:S(2)}) collective-permute-start(bf16[3,256,512]{2,1,0:T(8,128)(2,1)S(1)} %get-tuple-element.88), channel_id=1, source_target_pairs={{0,2},{2,4},{4,6},{6,7},{7,5},{5,3},{3,1},{1,0},{8,10},{10,12},{12... | collective-permute-start | bytes 2359304 | tf_op jit(solution)/shard_map/ppermute | solution.py:621
  60.3 31.6 %collective-permute-start.20 = (bf16[3,256,512]{2,1,0:T(8,128)(2,1)S(1)}, bf16[3,256,512]{2,1,0:T(8,128)(2,1)S(1)}, u32[]{:S(2)}, u32[]{:S(2)}) collective-permute-start(bf16[3,256,512]{2,1,0:T(8,128)(2,1)S(1)} %get-tuple-element.89), channel_id=1, source_target_pairs={{0,1},{2,0},{4,2},{6,4},{7,6},{5,7},{3,5},{1,3},{8,9},{10,8},{12,1... | collective-permute-start | bytes 2359304 | tf_op jit(solution)/shard_map/ppermute | solution.py:621
  77.1 31.6 %collective-permute-start.13 = (bf16[3,256,512]{2,1,0:T(8,128)(2,1)S(1)}, bf16[3,256,512]{2,1,0:T(8,128)(2,1)S(1)}, u32[]{:S(2)}, u32[]{:S(2)}) collective-permute-start(bf16[3,256,512]{2,1,0:T(8,128)(2,1)S(1)} %get-tuple-element.81), channel_id=1, source_target_pairs={{0,2},{2,4},{4,6},{6,7},{7,5},{5,3},{3,1},{1,0},{8,10},{10,12},{12... | collective-permute-start | bytes 2359304 | tf_op jit(solution)/shard_map/ppermute | solution.py:621
  77.2 31.6 %collective-permute-start.14 = (bf16[3,256,512]{2,1,0:T(8,128)(2,1)S(1)}, bf16[3,256,512]{2,1,0:T(8,128)(2,1)S(1)}, u32[]{:S(2)}, u32[]{:S(2)}) collective-permute-start(bf16[3,256,512]{2,1,0:T(8,128)(2,1)S(1)} %get-tuple-element.82), channel_id=1, source_target_pairs={{0,1},{2,0},{4,2},{6,4},{7,6},{5,7},{3,5},{1,3},{8,9},{10,8},{12,1... | collective-permute-start | bytes 2359304 | tf_op jit(solution)/shard_map/ppermute | solution.py:621
  93.9 31.6 %collective-permute-start.21 = (bf16[3,256,512]{2,1,0:T(8,128)(2,1)S(1)}, bf16[3,256,512]{2,1,0:T(8,128)(2,1)S(1)}, u32[]{:S(2)}, u32[]{:S(2)}) collective-permute-start(bf16[3,256,512]{2,1,0:T(8,128)(2,1)S(1)} %get-tuple-element.90), channel_id=1, source_target_pairs={{0,2},{2,4},{4,6},{6,7},{7,5},{5,3},{3,1},{1,0},{8,10},{10,12},{12... | collective-permute-start | bytes 2359304 | tf_op jit(solution)/shard_map/ppermute | solution.py:621
  94.0 31.6 %collective-permute-start.22 = (bf16[3,256,512]{2,1,0:T(8,128)(2,1)S(1)}, bf16[3,256,512]{2,1,0:T(8,128)(2,1)S(1)}, u32[]{:S(2)}, u32[]{:S(2)}) collective-permute-start(bf16[3,256,512]{2,1,0:T(8,128)(2,1)S(1)} %get-tuple-element.91), channel_id=1, source_target_pairs={{0,1},{2,0},{4,2},{6,4},{7,6},{5,7},{3,5},{1,3},{8,9},{10,8},{12,1... | collective-permute-start | bytes 2359304 | tf_op jit(solution)/shard_map/ppermute | solution.py:621
  110.8 31.6 %collective-permute-start.15 = (bf16[3,256,512]{2,1,0:T(8,128)(2,1)S(1)}, bf16[3,256,512]{2,1,0:T(8,128)(2,1)S(1)}, u32[]{:S(2)}, u32[]{:S(2)}) collective-permute-start(bf16[3,256,512]{2,1,0:T(8,128)(2,1)S(1)} %get-tuple-element.83), channel_id=1, source_target_pairs={{0,2},{2,4},{4,6},{6,7},{7,5},{5,3},{3,1},{1,0},{8,10},{10,12},{12... | collective-permute-start | bytes 2359304 | tf_op jit(solution)/shard_map/ppermute | solution.py:621
  110.9 31.6 %copy-start.29 = (bf16[256,1024]{1,0:T(8,128)(2,1)S(1)}, bf16[256,1024]{1,0:T(8,128)(2,1)}, u32[]{:S(2)}) copy-start(bf16[256,1024]{1,0:T(8,128)(2,1)} %d_out.3) | copy-start | bytes 1572868
  110.9 31.6 %collective-permute-start.16 = (bf16[3,256,512]{2,1,0:T(8,128)(2,1)S(1)}, bf16[3,256,512]{2,1,0:T(8,128)(2,1)S(1)}, u32[]{:S(2)}, u32[]{:S(2)}) collective-permute-start(bf16[3,256,512]{2,1,0:T(8,128)(2,1)S(1)} %get-tuple-element.84), channel_id=1, source_target_pairs={{0,1},{2,0},{4,2},{6,4},{7,6},{5,7},{3,5},{1,3},{8,9},{10,8},{12,1... | collective-permute-start | bytes 2359304 | tf_op jit(solution)/shard_map/ppermute | solution.py:621
  127.7 31.6 %collective-permute-start.23 = (bf16[3,256,512]{2,1,0:T(8,128)(2,1)S(1)}, bf16[3,256,512]{2,1,0:T(8,128)(2,1)S(1)}, u32[]{:S(2)}, u32[]{:S(2)}) collective-permute-start(bf16[3,256,512]{2,1,0:T(8,128)(2,1)S(1)} %get-tuple-element.92), channel_id=1, source_target_pairs={{0,2},{2,4},{4,6},{6,7},{7,5},{5,3},{3,1},{1,0},{8,10},{10,12},{12... | collective-permute-start | bytes 2359304 | tf_op jit(solution)/shard_map/ppermute | solution.py:621
  127.7 31.6 %collective-permute-start.24 = (bf16[3,256,512]{2,1,0:T(8,128)(2,1)S(1)}, bf16[3,256,512]{2,1,0:T(8,128)(2,1)S(1)}, u32[]{:S(2)}, u32[]{:S(2)}) collective-permute-start(bf16[3,256,512]{2,1,0:T(8,128)(2,1)S(1)} %get-tuple-element.93), channel_id=1, source_target_pairs={{0,1},{2,0},{4,2},{6,4},{7,6},{5,7},{3,5},{1,3},{8,9},{10,8},{12,1... | collective-permute-start | bytes 2359304 | tf_op jit(solution)/shard_map/ppermute | solution.py:621
  149.7 77.0 %copy-start.18 = (bf16[3,256,512]{2,1,0:T(8,128)(2,1)}, bf16[3,256,512]{2,1,0:T(8,128)(2,1)S(1)}, u32[]{:S(2)}) copy-start(bf16[3,256,512]{2,1,0:T(8,128)(2,1)S(1)} %get-tuple-element.99.refs_0_.refs_1_) | copy-start | bytes 2359300
  149.7 23.9 %collective-permute-start.30 = (bf16[3,256,512]{2,1,0:T(8,128)(2,1)S(1)}, bf16[3,256,512]{2,1,0:T(8,128)(2,1)S(1)}, u32[]{:S(2)}, u32[]{:S(2)}) collective-permute-start(bf16[3,256,512]{2,1,0:T(8,128)(2,1)S(1)} %get-tuple-element.99.refs_0_.refs_1_), channel_id=1, source_target_pairs={{0,1},{2,0},{4,2},{6,4},{7,6},{5,7},{3,5},{1,3},{8,9},{10,8},{12,1... | collective-permute-start | bytes 2359304 | tf_op jit(solution)/shard_map/ppermute | solution.py:621
  149.8 26.3 %collective-permute-start.27 = (bf16[3,256,512]{2,1,0:T(8,128)(2,1)S(1)}, bf16[3,256,512]{2,1,0:T(8,128)(2,1)S(1)}, u32[]{:S(2)}, u32[]{:S(2)}) collective-permute-start(bf16[3,256,512]{2,1,0:T(8,128)(2,1)S(1)} %get-tuple-element.99.refs_0_.refs_1_), channel_id=1, source_target_pairs={{0,2},{2,4},{4,6},{6,7},{7,5},{5,3},{3,1},{1,0},{8,10},{10,12},{12... | collective-permute-start | bytes 2359304 | tf_op jit(solution)/shard_map/ppermute | solution.py:621
  166.6 95.9 %copy-start.8 = (bf16[3,256,512]{2,1,0:T(8,128)(2,1)}, bf16[3,256,512]{2,1,0:T(8,128)(2,1)S(1)}, u32[]{:S(2)}) copy-start(bf16[3,256,512]{2,1,0:T(8,128)(2,1)S(1)} %get-tuple-element.104.refs_0_.refs_1_) | copy-start | bytes 2359300
  166.6 23.8 %collective-permute-start.38 = (bf16[3,256,512]{2,1,0:T(8,128)(2,1)S(1)}, bf16[3,256,512]{2,1,0:T(8,128)(2,1)S(1)}, u32[]{:S(2)}, u32[]{:S(2)}) collective-permute-start(bf16[3,256,512]{2,1,0:T(8,128)(2,1)S(1)} %get-tuple-element.104.refs_0_.refs_1_), channel_id=1, source_target_pairs={{0,1},{2,0},{4,2},{6,4},{7,6},{5,7},{3,5},{1,3},{8,9},{10,8},{12,1... | collective-permute-start | bytes 2359304 | tf_op jit(solution)/shard_map/ppermute | solution.py:621
  166.7 26.3 %collective-permute-start.35 = (bf16[3,256,512]{2,1,0:T(8,128)(2,1)S(1)}, bf16[3,256,512]{2,1,0:T(8,128)(2,1)S(1)}, u32[]{:S(2)}, u32[]{:S(2)}) collective-permute-start(bf16[3,256,512]{2,1,0:T(8,128)(2,1)S(1)} %get-tuple-element.104.refs_0_.refs_1_), channel_id=1, source_target_pairs={{0,2},{2,4},{4,6},{6,7},{7,5},{5,3},{3,1},{1,0},{8,10},{10,12},{12... | collective-permute-start | bytes 2359304 | tf_op jit(solution)/shard_map/ppermute | solution.py:621
  173.6 70.0 %copy-start.20 = (bf16[3,256,512]{2,1,0:T(8,128)(2,1)}, bf16[3,256,512]{2,1,0:T(8,128)(2,1)S(1)}, u32[]{:S(2)}) copy-start(bf16[3,256,512]{2,1,0:T(8,128)(2,1)S(1)} %collective-permute-done.30.refs_2_.refs_3_) | copy-start | bytes 2359300
  173.6 33.7 %collective-permute-start.31 = (bf16[3,256,512]{2,1,0:T(8,128)(2,1)S(1)}, bf16[3,256,512]{2,1,0:T(8,128)(2,1)S(1)}, u32[]{:S(2)}, u32[]{:S(2)}) collective-permute-start(bf16[3,256,512]{2,1,0:T(8,128)(2,1)S(1)} %collective-permute-done.30.refs_2_.refs_3_), channel_id=1, source_target_pairs={{0,1},{2,0},{4,2},{6,4},{7,6},{5,7},{3,5},{1,3},{8,9},{10,8},{12,1... | collective-permute-start | bytes 2359304 | tf_op jit(solution)/shard_map/ppermute | solution.py:621
  176.1 67.5 %copy-start.22 = (bf16[3,256,512]{2,1,0:T(8,128)(2,1)}, bf16[3,256,512]{2,1,0:T(8,128)(2,1)S(1)}, u32[]{:S(2)}) copy-start(bf16[3,256,512]{2,1,0:T(8,128)(2,1)S(1)} %collective-permute-done.27.refs_1_.refs_2_) | copy-start | bytes 2359300
  176.1 33.7 %collective-permute-start.28 = (bf16[3,256,512]{2,1,0:T(8,128)(2,1)S(1)}, bf16[3,256,512]{2,1,0:T(8,128)(2,1)S(1)}, u32[]{:S(2)}, u32[]{:S(2)}) collective-permute-start(bf16[3,256,512]{2,1,0:T(8,128)(2,1)S(1)} %collective-permute-done.27.refs_1_.refs_2_), channel_id=1, source_target_pairs={{0,2},{2,4},{4,6},{6,7},{7,5},{5,3},{3,1},{1,0},{8,10},{10,12},{12... | collective-permute-start | bytes 2359304 | tf_op jit(solution)/shard_map/ppermute | solution.py:621
  190.5 72.1 %copy-start.10 = (bf16[3,256,512]{2,1,0:T(8,128)(2,1)}, bf16[3,256,512]{2,1,0:T(8,128)(2,1)S(1)}, u32[]{:S(2)}) copy-start(bf16[3,256,512]{2,1,0:T(8,128)(2,1)S(1)} %collective-permute-done.38.refs_2_.refs_3_) | copy-start | bytes 2359300
  190.5 33.7 %collective-permute-start.39 = (bf16[3,256,512]{2,1,0:T(8,128)(2,1)S(1)}, bf16[3,256,512]{2,1,0:T(8,128)(2,1)S(1)}, u32[]{:S(2)}, u32[]{:S(2)}) collective-permute-start(bf16[3,256,512]{2,1,0:T(8,128)(2,1)S(1)} %collective-permute-done.38.refs_2_.refs_3_), channel_id=1, source_target_pairs={{0,1},{2,0},{4,2},{6,4},{7,6},{5,7},{3,5},{1,3},{8,9},{10,8},{12,1... | collective-permute-start | bytes 2359304 | tf_op jit(solution)/shard_map/ppermute | solution.py:621
  193.0 69.6 %copy-start.12 = (bf16[3,256,512]{2,1,0:T(8,128)(2,1)}, bf16[3,256,512]{2,1,0:T(8,128)(2,1)S(1)}, u32[]{:S(2)}) copy-start(bf16[3,256,512]{2,1,0:T(8,128)(2,1)S(1)} %collective-permute-done.35.refs_1_.refs_2_) | copy-start | bytes 2359300
  193.0 33.7 %collective-permute-start.36 = (bf16[3,256,512]{2,1,0:T(8,128)(2,1)S(1)}, bf16[3,256,512]{2,1,0:T(8,128)(2,1)S(1)}, u32[]{:S(2)}, u32[]{:S(2)}) collective-permute-start(bf16[3,256,512]{2,1,0:T(8,128)(2,1)S(1)} %collective-permute-done.35.refs_1_.refs_2_), channel_id=1, source_target_pairs={{0,2},{2,4},{4,6},{6,7},{7,5},{5,3},{3,1},{1,0},{8,10},{10,12},{12... | collective-permute-start | bytes 2359304 | tf_op jit(solution)/shard_map/ppermute | solution.py:621
  207.3 56.6 %copy-start.14 = (bf16[3,256,512]{2,1,0:T(8,128)(2,1)}, bf16[3,256,512]{2,1,0:T(8,128)(2,1)S(1)}, u32[]{:S(2)}) copy-start(bf16[3,256,512]{2,1,0:T(8,128)(2,1)S(1)} %collective-permute-done.31.refs_1_.refs_5_) | copy-start | bytes 2359300
  207.3 33.7 %collective-permute-start.32 = (bf16[3,256,512]{2,1,0:T(8,128)(2,1)S(1)}, bf16[3,256,512]{2,1,0:T(8,128)(2,1)S(1)}, u32[]{:S(2)}, u32[]{:S(2)}) collective-permute-start(bf16[3,256,512]{2,1,0:T(8,128)(2,1)S(1)} %collective-permute-done.31.refs_1_.refs_5_), channel_id=1, source_target_pairs={{0,1},{2,0},{4,2},{6,4},{7,6},{5,7},{3,5},{1,3},{8,9},{10,8},{12,1... | collective-permute-start | bytes 2359304 | tf_op jit(solution)/shard_map/ppermute | solution.py:621
  209.9 54.1 %copy-start.16 = (bf16[3,256,512]{2,1,0:T(8,128)(2,1)}, bf16[3,256,512]{2,1,0:T(8,128)(2,1)S(1)}, u32[]{:S(2)}) copy-start(bf16[3,256,512]{2,1,0:T(8,128)(2,1)S(1)} %collective-permute-done.28.refs_0_.refs_4_) | copy-start | bytes 2359300
  209.9 33.7 %collective-permute-start.29 = (bf16[3,256,512]{2,1,0:T(8,128)(2,1)S(1)}, bf16[3,256,512]{2,1,0:T(8,128)(2,1)S(1)}, u32[]{:S(2)}, u32[]{:S(2)}) collective-permute-start(bf16[3,256,512]{2,1,0:T(8,128)(2,1)S(1)} %collective-permute-done.28.refs_0_.refs_4_), channel_id=1, source_target_pairs={{0,2},{2,4},{4,6},{6,7},{7,5},{5,3},{3,1},{1,0},{8,10},{10,12},{12... | collective-permute-start | bytes 2359304 | tf_op jit(solution)/shard_map/ppermute | solution.py:621
  224.2 40.8 %copy-start.24 = (bf16[3,256,512]{2,1,0:T(8,128)(2,1)}, bf16[3,256,512]{2,1,0:T(8,128)(2,1)S(1)}, u32[]{:S(2)}) copy-start(bf16[3,256,512]{2,1,0:T(8,128)(2,1)S(1)} %collective-permute-done.39.refs_1_.refs_5_) | copy-start | bytes 2359300
  224.2 33.7 %collective-permute-start.40 = (bf16[3,256,512]{2,1,0:T(8,128)(2,1)S(1)}, bf16[3,256,512]{2,1,0:T(8,128)(2,1)S(1)}, u32[]{:S(2)}, u32[]{:S(2)}) collective-permute-start(bf16[3,256,512]{2,1,0:T(8,128)(2,1)S(1)} %collective-permute-done.39.refs_1_.refs_5_), channel_id=1, source_target_pairs={{0,1},{2,0},{4,2},{6,4},{7,6},{5,7},{3,5},{1,3},{8,9},{10,8},{12,1... | collective-permute-start | bytes 2359304 | tf_op jit(solution)/shard_map/ppermute | solution.py:621
  226.7 38.2 %copy-start.26 = (bf16[3,256,512]{2,1,0:T(8,128)(2,1)}, bf16[3,256,512]{2,1,0:T(8,128)(2,1)S(1)}, u32[]{:S(2)}) copy-start(bf16[3,256,512]{2,1,0:T(8,128)(2,1)S(1)} %collective-permute-done.36.refs_0_.refs_4_) | copy-start | bytes 2359300
  226.7 33.7 %collective-permute-start.37 = (bf16[3,256,512]{2,1,0:T(8,128)(2,1)S(1)}, bf16[3,256,512]{2,1,0:T(8,128)(2,1)S(1)}, u32[]{:S(2)}, u32[]{:S(2)}) collective-permute-start(bf16[3,256,512]{2,1,0:T(8,128)(2,1)S(1)} %collective-permute-done.36.refs_0_.refs_4_), channel_id=1, source_target_pairs={{0,2},{2,4},{4,6},{6,7},{7,5},{5,3},{3,1},{1,0},{8,10},{10,12},{12... | collective-permute-start | bytes 2359304 | tf_op jit(solution)/shard_map/ppermute | solution.py:621
  243.6 25.2 %collective-permute-start.33 = (bf16[3,128,512]{2,1,0:T(8,128)(2,1)S(1)}, bf16[3,128,512]{2,1,0:T(8,128)(2,1)S(1)}, u32[]{:S(2)}, u32[]{:S(2)}) collective-permute-start(bf16[3,128,512]{2,1,0:T(8,128)(2,1)S(1)} %get-tuple-element.100), channel_id=1, source_target_pairs={{0,2},{2,4},{4,6},{6,7},{7,5},{5,3},{3,1},{1,0},{8,10},{10,12},{12... | collective-permute-start | bytes 1179656 | tf_op jit(solution)/shard_map/ppermute | solution.py:621
  243.7 25.1 %collective-permute-start.34 = (bf16[3,128,512]{2,1,0:T(8,128)(2,1)S(1)}, bf16[3,128,512]{2,1,0:T(8,128)(2,1)S(1)}, u32[]{:S(2)}, u32[]{:S(2)}) collective-permute-start(bf16[3,128,512]{2,1,0:T(8,128)(2,1)S(1)} %get-tuple-element.101), channel_id=1, source_target_pairs={{0,1},{2,0},{4,2},{6,4},{7,6},{5,7},{3,5},{1,3},{8,9},{10,8},{12,1... | collective-permute-start | bytes 1179656 | tf_op jit(solution)/shard_map/ppermute | solution.py:621
  260.5 16.0 %collective-permute-start.41 = (bf16[3,128,512]{2,1,0:T(8,128)(2,1)S(1)}, bf16[3,128,512]{2,1,0:T(8,128)(2,1)S(1)}, u32[]{:S(2)}, u32[]{:S(2)}) collective-permute-start(bf16[3,128,512]{2,1,0:T(8,128)(2,1)S(1)} %get-tuple-element.105), channel_id=1, source_target_pairs={{0,2},{2,4},{4,6},{6,7},{7,5},{5,3},{3,1},{1,0},{8,10},{10,12},{12... | collective-permute-start | bytes 1179656 | tf_op jit(solution)/shard_map/ppermute | solution.py:621
  260.5 16.0 %collective-permute-start.42 = (bf16[3,128,512]{2,1,0:T(8,128)(2,1)S(1)}, bf16[3,128,512]{2,1,0:T(8,128)(2,1)S(1)}, u32[]{:S(2)}, u32[]{:S(2)}) collective-permute-start(bf16[3,128,512]{2,1,0:T(8,128)(2,1)S(1)} %get-tuple-element.106), channel_id=1, source_target_pairs={{0,1},{2,0},{4,2},{6,4},{7,6},{5,7},{3,5},{1,3},{8,9},{10,8},{12,1... | collective-permute-start | bytes 1179656 | tf_op jit(solution)/shard_map/ppermute | solution.py:621
  278.2 2.0 collective-permute-start.43
  278.2 4.6 %collective-permute-start.47 = (bf16[4,128,512]{2,1,0:T(8,128)(2,1)S(1)}, bf16[4,128,512]{2,1,0:T(8,128)(2,1)S(1)}, u32[]{:S(2)}, u32[]{:S(2)}) collective-permute-start(bf16[4,128,512]{2,1,0:T(8,128)(2,1)S(1)} %get-tuple-element.128), channel_id=1, source_target_pairs={{0,8},{8,0},{16,24},{24,16},{1,9},{9,1},{17,25},{25,17},{2,10},{10... | collective-permute-start | bytes 1572872 | tf_op jit(solution)/shard_map/ppermute | solution.py:624
  282.3 17.0 %collective-permute-start.44 = (bf16[2,128,512]{2,1,0:T(8,128)(2,1)}, bf16[2,128,512]{2,1,0:T(8,128)(2,1)}, u32[]{:S(2)}, u32[]{:S(2)}) collective-permute-start(bf16[2,128,512]{2,1,0:T(8,128)(2,1)} %get-tuple-element.124), channel_id=1, source_target_pairs={{0,16},{8,24},{16,0},{24,8},{1,17},{9,25},{17,1},{25,9},{2,18},{10... | collective-permute-start | bytes 786440 | tf_op jit(solution)/shard_map/ppermute | solution.py:624
  284.9 22.0 %collective-permute-start.48 = (bf16[2,128,512]{2,1,0:T(8,128)(2,1)}, bf16[2,128,512]{2,1,0:T(8,128)(2,1)}, u32[]{:S(2)}, u32[]{:S(2)}) collective-permute-start(bf16[2,128,512]{2,1,0:T(8,128)(2,1)} %get-tuple-element.130), channel_id=1, source_target_pairs={{0,16},{8,24},{16,0},{24,8},{1,17},{9,25},{17,1},{25,9},{2,18},{10... | collective-permute-start | bytes 786440 | tf_op jit(solution)/shard_map/ppermute | solution.py:624
  289.2 27.0 %copy-start.19 = (bf16[3,256,512]{2,1,0:T(8,128)(2,1)S(1)}, bf16[3,256,512]{2,1,0:T(8,128)(2,1)}, u32[]{:S(2)}) copy-start(bf16[3,256,512]{2,1,0:T(8,128)(2,1)} %copy-done.18) | copy-start | bytes 2359300
  289.3 1.6 collective-permute-start.25
  291.8 7.5 %collective-permute-start.26 = (f32[256,1]{1,0:T(8,128)S(1)}, f32[256,1]{1,0:T(8,128)S(1)}, u32[]{:S(2)}, u32[]{:S(2)}) collective-permute-start(f32[256,1]{1,0:T(8,128)S(1)} %add.31), channel_id=1, source_target_pairs={{0,16},{8,24},{16,0},{24,8},{1,17},{9,25},{17,1},{25,9},{2,18},{10... | collective-permute-start | bytes 3080 | tf_op jit(solution)/shard_map/ppermute | solution.py:624
  301.4 28.8 %collective-permute-start.46 = (bf16[128,512]{1,0:T(8,128)(2,1)S(1)}, bf16[128,512]{1,0:T(8,128)(2,1)S(1)}, u32[]{:S(2)}, u32[]{:S(2)}) collective-permute-start(bf16[128,512]{1,0:T(8,128)(2,1)S(1)} %get-tuple-element.126), channel_id=1, source_target_pairs={{0,1},{1,0},{2,9},{3,8},{4,17},{5,16},{6,25},{7,24},{8,3},{9,2},{1... | collective-permute-start | bytes 393224 | tf_op jit(solution)/shard_map/ppermute | solution.py:682
  303.7 26.4 %collective-permute-start.45 = (bf16[128,512]{1,0:T(8,128)(2,1)S(1)}, bf16[128,512]{1,0:T(8,128)(2,1)S(1)}, u32[]{:S(2)}, u32[]{:S(2)}) collective-permute-start(bf16[128,512]{1,0:T(8,128)(2,1)S(1)} %get-tuple-element.125.refs_10_), channel_id=1, source_target_pairs={{0,0},{1,1},{2,8},{3,9},{4,16},{5,17},{6,24},{7,25},{8,2},{9,3},{1... | collective-permute-start | bytes 393224 | tf_op jit(solution)/shard_map/ppermute | solution.py:682
  308.9 21.2 %collective-permute-start.50 = (bf16[128,512]{1,0:T(8,128)(2,1)S(1)}, bf16[128,512]{1,0:T(8,128)(2,1)S(1)}, u32[]{:S(2)}, u32[]{:S(2)}) collective-permute-start(bf16[128,512]{1,0:T(8,128)(2,1)S(1)} %get-tuple-element.132), channel_id=1, source_target_pairs={{0,1},{1,0},{2,9},{3,8},{4,17},{5,16},{6,25},{7,24},{8,3},{9,2},{1... | collective-permute-start | bytes 393224 | tf_op jit(solution)/shard_map/ppermute | solution.py:682
  311.3 18.8 %collective-permute-start.49 = (bf16[128,512]{1,0:T(8,128)(2,1)S(1)}, bf16[128,512]{1,0:T(8,128)(2,1)S(1)}, u32[]{:S(2)}, u32[]{:S(2)}) collective-permute-start(bf16[128,512]{1,0:T(8,128)(2,1)S(1)} %get-tuple-element.131.refs_11_), channel_id=1, source_target_pairs={{0,0},{1,1},{2,8},{3,9},{4,16},{5,17},{6,24},{7,25},{8,2},{9,3},{1... | collective-permute-start | bytes 393224 | tf_op jit(solution)/shard_map/ppermute | solution.py:682
  (35 other events, 336.0 us)

commit v10 on v7

--- a/solution.py
+++ b/solution.py
@@ -72,6 +72,11 @@
     return [*distances, far]
 
 
+def group_of(nodes):
+    bits = nodes.bit_length() - 1
+    return [sum((node >> bit & 1) << (bits - 1 - bit) for bit in range(bits)) for node in range(nodes)]
+
+
 def index_table(size, nodes):
     order, group = ring_order(size), size // nodes
     rows = []
@@ -79,7 +84,7 @@
         for here in range(size):
             place = order.index(here)
             seqs = [order[(place + distance) % size] for distance in ring_distances(size)]
-            owner = [seq // group for seq in seqs]
+            owner = [group_of(nodes).index(seq // group) for seq in seqs]
             rows.append(
                 [order[(place + distance) % size] for distance in range(size)]
                 + [node % 2]
@@ -608,8 +613,7 @@
     here, node = lax.axis_index("local"), lax.axis_index("node")
     wide = columns // 2
     far = size // 2
-    group = size // nodes
-    core = node % 2
+    group, groups = size // nodes, group_of(nodes)
 
     order = ring_order(size)
     distances = ring_distances(size)
@@ -675,7 +679,7 @@
         came = []
         for turn, block in enumerate(blocks):
             moves = [
-                (n * size + s, (s // group) * size + n * group + (s + turn) % group)
+                (n * size + s, (s // group) * size + groups[n] * group + (s + turn) % group)
                 for n in range(nodes)
                 for s in range(size)
             ]
@@ -689,8 +693,7 @@
         for chunk in range(2):
             right, left = moving[chunk]
             if step == far:
-                early = [dots] if chunk == 0 else terms[1][: size - 3]
-                right, left = halve(right, left, early)
+                right, left = halve(right, left, [] if chunk else [dots])
             right, left = shift(right, 1), shift(left, -1)
             moving[chunk] = right, left
             gathered[chunk] += [right, left]

time: 320 us -> 323 us (level)
  the two profiles are of different devices: /device:TPU:2 before, /device:TPU:24 now
where the time goes in v10:
time: 323 us; the launch traced here: 322 us
  waiting for transfers between devices  169 us (52%)
  Pallas kernels  66.4 us (21%)
  starting transfers between devices  64.3 us (20%)
  local copies, waits for them, and re-layouts  17.1 us (5%)
  other arithmetic  4.52 us (1%)
    ppermute x39, waiting for transfers between devices, shift(): return lax.ppermute(array, 'local', moves)  156 us
    ppermute x39, starting transfers between devices, shift(): return lax.ppermute(array, 'local', moves)  42.6 us
    ppermute x4, starting transfers between devices, relocate(): came.append(lax.ppermute(block, ('node', 'local'), moves))  17.4 us
    unnamed x56, local copies, waits for them, and re-layouts  14.9 us
    pallas_call x2, Pallas kernels, attention(): pl.pallas_call(attention_kernel, grid_spec=pltpu.PrefetchScalarGridSpec(n...  14.5 us
    pallas_call x7, Pallas kernels, term_step(): pl.pallas_call(kernel, in_specs=[whole] * (1 + count + len(befores)), out...  12.7 us
    pallas_call x2, Pallas kernels, grads_chunk(): pl.pallas_call(tied(grads_kernel, 1 + len(pieces), len(ties)), grid=(3,),...  12.7 us
    ppermute x8, waiting for transfers between devices, swap(): return lax.ppermute(array, 'node', [(n, n ^ bit) for n in range(nodes)])  12.6 us
  transfers between devices with their start and end apart: 51, of which 23 were waited for; matrix products, arithmetic and copies ran while one was open for 2% of the time, Pallas kernels for 19%

profile of v10, /device:TPU:24, one launch (start us, length us, event | category | flops | bytes accessed | tf_op | source)
XLA Modules:
  0.0 322.4 jit_solution(4157434134496549485)
XLA Ops:
  2.0 1.6 copy-done.2
  3.6 1.4 normed_blocks.1
  7.2 6.5 %collective-permute-done.6.mine.mine_far = bf16[256,256]{1,0:T(8,128)(2,1)S(1)} collective-permute-done((bf16[256,256]{1,0:T(8,128)(2,1)S(1)}, bf16[256,256]{1,0:T(8,128)(2,1)S(1)}, u32[]{:S(2)}, u32[]{:S(2)}) %collective-permute-start.6) | collective-permute-done | bytes 131104 | tf_op jit(solution)/shard_map/ppermute | solution.py:625
  15.1 2.7 collective-permute-start.2
  18.0 3.6 %collective-permute-start.4 = (bf16[256,256]{1,0:T(8,128)(2,1)S(1)}, bf16[256,256]{1,0:T(8,128)(2,1)S(1)}, u32[]{:S(2)}, u32[]{:S(2)}) collective-permute-start(bf16[256,256]{1,0:T(8,128)(2,1)S(1)} %get-tuple-element.73), channel_id=1, source_target_pairs={{0,6},{2,7},{4,5},{6,3},{7,1},{5,0},{3,2},{1,4},{8,14},{10,15},{12... | collective-permute-start | bytes 393224 | tf_op jit(solution)/shard_map/ppermute | solution.py:625
  21.9 1.9 copy-done.19
  25.6 1.9 sum_first.1
  27.5 1.5 collective-permute-done.4.refs_5_
  29.1 7.6 %collective-permute-done.5.refs_6_ = bf16[256,256]{1,0:T(8,128)(2,1)S(1)} collective-permute-done((bf16[256,256]{1,0:T(8,128)(2,1)S(1)}, bf16[256,256]{1,0:T(8,128)(2,1)S(1)}, u32[]{:S(2)}, u32[]{:S(2)}) %collective-permute-start.5) | collective-permute-done | bytes 131104 | tf_op jit(solution)/shard_map/ppermute | solution.py:625
  36.8 2.0 collective-permute-start.9
  38.9 2.0 collective-permute-start.18
  40.9 7.9 %collective-permute-done.10.refs_8_ = bf16[3,128,512]{2,1,0:T(8,128)(2,1)S(1)} collective-permute-done((bf16[3,128,512]{2,1,0:T(8,128)(2,1)S(1)}, bf16[3,128,512]{2,1,0:T(8,128)(2,1)S(1)}, u32[]{:S(2)}, u32[]{:S(2)}) %collective-permute-start.10) | collective-permute-done | bytes 393248 | tf_op jit(solution)/shard_map/ppermute | solution.py:625
  48.8 2.1 sum_step.6
  50.9 2.0 collective-permute-start.11
  53.0 4.3 %collective-permute-done.17.refs_7_ = bf16[3,128,512]{2,1,0:T(8,128)(2,1)S(1)} collective-permute-done((bf16[3,128,512]{2,1,0:T(8,128)(2,1)S(1)}, bf16[3,128,512]{2,1,0:T(8,128)(2,1)S(1)}, u32[]{:S(2)}, u32[]{:S(2)}) %collective-permute-start.17) | collective-permute-done | bytes 393248 | tf_op jit(solution)/shard_map/ppermute | solution.py:625
  57.3 2.1 sum_step.9
  59.3 2.0 collective-permute-start.19
  61.4 12.7 %collective-permute-done.11.refs_7_ = bf16[3,256,512]{2,1,0:T(8,128)(2,1)S(1)} collective-permute-done((bf16[3,256,512]{2,1,0:T(8,128)(2,1)S(1)}, bf16[3,256,512]{2,1,0:T(8,128)(2,1)S(1)}, u32[]{:S(2)}, u32[]{:S(2)}) %collective-permute-start.11) | collective-permute-done | bytes 786464 | tf_op jit(solution)/shard_map/ppermute | solution.py:625
  74.1 2.1 sum_step.7
  76.2 2.0 collective-permute-start.13
  78.3 12.7 %collective-permute-done.19.refs_7_ = bf16[3,256,512]{2,1,0:T(8,128)(2,1)S(1)} collective-permute-done((bf16[3,256,512]{2,1,0:T(8,128)(2,1)S(1)}, bf16[3,256,512]{2,1,0:T(8,128)(2,1)S(1)}, u32[]{:S(2)}, u32[]{:S(2)}) %collective-permute-start.19) | collective-permute-done | bytes 786464 | tf_op jit(solution)/shard_map/ppermute | solution.py:625
  91.0 2.1 sum_step.10
  93.0 2.0 collective-permute-start.21
  96.3 11.5 %collective-permute-done.13.refs_7_ = bf16[3,256,512]{2,1,0:T(8,128)(2,1)S(1)} collective-permute-done((bf16[3,256,512]{2,1,0:T(8,128)(2,1)S(1)}, bf16[3,256,512]{2,1,0:T(8,128)(2,1)S(1)}, u32[]{:S(2)}, u32[]{:S(2)}) %collective-permute-start.13) | collective-permute-done | bytes 786464 | tf_op jit(solution)/shard_map/ppermute | solution.py:625
  107.8 2.1 sum_step.8
  109.9 2.0 collective-permute-start.15
  112.0 12.7 %collective-permute-done.21.refs_7_ = bf16[3,256,512]{2,1,0:T(8,128)(2,1)S(1)} collective-permute-done((bf16[3,256,512]{2,1,0:T(8,128)(2,1)S(1)}, bf16[3,256,512]{2,1,0:T(8,128)(2,1)S(1)}, u32[]{:S(2)}, u32[]{:S(2)}) %collective-permute-start.21) | collective-permute-done | bytes 786464 | tf_op jit(solution)/shard_map/ppermute | solution.py:625
  124.7 2.1 sum_step.11
  126.7 2.0 collective-permute-start.23
  129.5 12.0 %collective-permute-done.15.from_left = bf16[3,256,512]{2,1,0:T(8,128)(2,1)S(1)} collective-permute-done((bf16[3,256,512]{2,1,0:T(8,128)(2,1)S(1)}, bf16[3,256,512]{2,1,0:T(8,128)(2,1)S(1)}, u32[]{:S(2)}, u32[]{:S(2)}) %collective-permute-start.15) | collective-permute-done | bytes 786464 | tf_op jit(solution)/shard_map/ppermute | solution.py:625
  141.5 7.2 %attention.2 = (bf16[256,512]{1,0:T(8,128)(2,1)S(1)}, f32[256,128]{1,0:T(8,128)S(1)}, bf16[3,256,512]{2,1,0:T(8,128)(2,1)S(1)}) custom-call(s32[39]{0:T(128)S(1)} %dynamic-slice_bitcast_fusion.idx.refs_0_, bf16[7,256,256]{2,1,0:T(8,128)(2,1)S(1)} %stack.1.refs_1_.refs_3_.mine, bf16[7,256,256]{2,1,0:T(8,128)(2,1)S(1)} %collective-permute-done.8.refs_2_.refs_4_.other, ...), custom_call_target="tpu_custom_call" | custom-call | flops 402653184 | bytes 3145728 | tf_op jit(solution)/shard_map/attention/pallas_call | solution.py:394
  149.4 2.0 collective-permute-start.27
  151.4 6.9 %collective-permute-done.23.from_left = bf16[3,256,512]{2,1,0:T(8,128)(2,1)S(1)} collective-permute-done((bf16[3,256,512]{2,1,0:T(8,128)(2,1)S(1)}, bf16[3,256,512]{2,1,0:T(8,128)(2,1)S(1)}, u32[]{:S(2)}, u32[]{:S(2)}) %collective-permute-start.23) | collective-permute-done | bytes 786464 | tf_op jit(solution)/shard_map/ppermute | solution.py:625
  158.4 7.3 %attention.3 = (bf16[256,512]{1,0:T(8,128)(2,1)S(1)}, f32[256,128]{1,0:T(8,128)S(1)}, bf16[3,256,512]{2,1,0:T(8,128)(2,1)S(1)}) custom-call(s32[39]{0:T(128)S(1)} %dynamic-slice_bitcast_fusion.idx.refs_0_, bf16[7,256,256]{2,1,0:T(8,128)(2,1)S(1)} %stack.1.refs_1_.refs_3_.mine, bf16[7,256,256]{2,1,0:T(8,128)(2,1)S(1)} %collective-permute-done.8.refs_2_.refs_4_.other, ...), custom_call_target="tpu_custom_call" | custom-call | flops 402653184 | bytes 3145728 | tf_op jit(solution)/shard_map/attention/pallas_call | solution.py:394
  167.0 2.0 collective-permute-start.35
  170.0 5.1 %collective-permute-done.30.refs_2_.refs_3_ = bf16[3,256,512]{2,1,0:T(8,128)(2,1)S(1)} collective-permute-done((bf16[3,256,512]{2,1,0:T(8,128)(2,1)S(1)}, bf16[3,256,512]{2,1,0:T(8,128)(2,1)S(1)}, u32[]{:S(2)}, u32[]{:S(2)}) %collective-permute-start.30) | collective-permute-done | bytes 786464 | tf_op jit(solution)/shard_map/ppermute | solution.py:625
  176.1 1.9 collective-permute-start.28
  179.0 13.0 %collective-permute-done.38.refs_2_.refs_3_ = bf16[3,256,512]{2,1,0:T(8,128)(2,1)S(1)} collective-permute-done((bf16[3,256,512]{2,1,0:T(8,128)(2,1)S(1)}, bf16[3,256,512]{2,1,0:T(8,128)(2,1)S(1)}, u32[]{:S(2)}, u32[]{:S(2)}) %collective-permute-start.38) | collective-permute-done | bytes 786464 | tf_op jit(solution)/shard_map/ppermute | solution.py:625
  192.9 1.9 collective-permute-start.36
  195.8 13.1 %collective-permute-done.31.refs_1_.refs_5_ = bf16[3,256,512]{2,1,0:T(8,128)(2,1)} collective-permute-done((bf16[3,256,512]{2,1,0:T(8,128)(2,1)S(1)}, bf16[3,256,512]{2,1,0:T(8,128)(2,1)}, u32[]{:S(2)}, u32[]{:S(2)}) %collective-permute-start.31) | collective-permute-done | bytes 786464 | tf_op jit(solution)/shard_map/ppermute | solution.py:625
  209.0 2.0 collective-permute-start.29
  211.0 14.8 %collective-permute-done.39.refs_1_.refs_5_ = bf16[3,256,512]{2,1,0:T(8,128)(2,1)} collective-permute-done((bf16[3,256,512]{2,1,0:T(8,128)(2,1)S(1)}, bf16[3,256,512]{2,1,0:T(8,128)(2,1)}, u32[]{:S(2)}, u32[]{:S(2)}) %collective-permute-start.39) | collective-permute-done | bytes 786464 | tf_op jit(solution)/shard_map/ppermute | solution.py:625
  225.9 2.0 collective-permute-start.37
  230.7 1.6 collective-permute-done.25
  233.2 1.6 collective-permute-start.26
  234.8 4.1 %collective-permute-done.26 = f32[256,1]{1,0:T(8,128)S(1)} collective-permute-done((f32[256,1]{1,0:T(8,128)S(1)}, f32[256,1]{1,0:T(8,128)S(1)}, u32[]{:S(2)}, u32[]{:S(2)}) %collective-permute-start.26) | collective-permute-done | bytes 1056 | tf_op jit(solution)/shard_map/ppermute | solution.py:628
  243.6 1.4 halve.2
  247.1 12.4 %collective-permute-done.40.refs_1_.refs_7_ = bf16[3,256,512]{2,1,0:T(8,128)(2,1)} collective-permute-done((bf16[3,256,512]{2,1,0:T(8,128)(2,1)}, bf16[3,256,512]{2,1,0:T(8,128)(2,1)}, u32[]{:S(2)}, u32[]{:S(2)}) %collective-permute-start.40) | collective-permute-done | bytes 786464 | tf_op jit(solution)/shard_map/ppermute | solution.py:625
  259.6 1.4 halve.3
  261.0 2.0 collective-permute-start.41
  263.1 1.4 term_step.9
  264.5 2.3 term_step.10
  266.8 2.3 term_step.11
  269.2 2.3 term_step.12
  271.5 2.3 term_step.13
  275.8 1.6 term_last.1
  278.1 1.4 collective-permute-done.43.came
  280.1 1.6 collective-permute-start.44
  283.8 5.5 %collective-permute-done.44.came = bf16[2,128,512]{2,1,0:T(8,128)(2,1)S(1)} collective-permute-done((bf16[2,128,512]{2,1,0:T(8,128)(2,1)S(1)}, bf16[2,128,512]{2,1,0:T(8,128)(2,1)S(1)}, u32[]{:S(2)}, u32[]{:S(2)}) %collective-permute-start.44) | collective-permute-done | bytes 262176 | tf_op jit(solution)/shard_map/ppermute | solution.py:628
  290.2 7.3 %collective-permute-start.45 = (bf16[128,512]{1,0:T(8,128)(2,1)S(1)}, bf16[128,512]{1,0:T(8,128)(2,1)S(1)}, u32[]{:S(2)}, u32[]{:S(2)}) collective-permute-start(bf16[128,512]{1,0:T(8,128)(2,1)S(1)} %get-tuple-element.125.refs_10_), channel_id=1, source_target_pairs={{0,0},{1,1},{2,8},{3,9},{4,16},{5,17},{6,24},{7,25},{8,4},{9,5},{1... | collective-permute-start | bytes 393224 | tf_op jit(solution)/shard_map/ppermute | solution.py:686
  298.4 9.5 %collective-permute-start.49 = (bf16[128,512]{1,0:T(8,128)(2,1)S(1)}, bf16[128,512]{1,0:T(8,128)(2,1)S(1)}, u32[]{:S(2)}, u32[]{:S(2)}) collective-permute-start(bf16[128,512]{1,0:T(8,128)(2,1)S(1)} %get-tuple-element.131.refs_11_), channel_id=1, source_target_pairs={{0,0},{1,1},{2,8},{3,9},{4,16},{5,17},{6,24},{7,25},{8,4},{9,5},{1... | collective-permute-start | bytes 393224 | tf_op jit(solution)/shard_map/ppermute | solution.py:686
  308.0 6.3 %grads.2.refs_10_ = f32[3,512,1024]{2,1,0:T(8,128)} custom-call(bf16[512,2048]{1,0:T(8,128)(2,1)S(1)} %copy-done.1, bf16[3,256,512]{2,1,0:T(8,128)(2,1)S(1)} %copy-done.12, bf16[3,256,512]{2,1,0:T(8,128)(2,1)S(1)} %copy-done.18, bf16[3,256,512]{2,1,0:T(8,128)(2,1)S(1)} %copy-done.15, bf16[3,256,512]{2,1,0:T(8,128)(2,1)} %collective-permute-done.28.refs_0_.refs_4_, ...), custom_call_target="tpu_custom_call" | custom-call | flops 3221225472 | bytes 9437184 | tf_op jit(solution)/shard_map/grads/pallas_call | solution.py:436
  314.3 6.4 %grads.3 = f32[3,512,1024]{2,1,0:T(8,128)} custom-call(bf16[512,2048]{1,0:T(8,128)(2,1)S(1)} %copy-done.1, bf16[3,256,512]{2,1,0:T(8,128)(2,1)S(1)} %copy-done.5, bf16[3,256,512]{2,1,0:T(8,128)(2,1)S(1)} %copy-done.9, bf16[3,256,512]{2,1,0:T(8,128)(2,1)S(1)} %copy-done.7, ...), custom_call_target="tpu_custom_call", output_to_operand_aliasing={{}: (10, {})} | custom-call | flops 3221225472 | bytes 9437184 | tf_op jit(solution)/shard_map/grads/pallas_call | solution.py:436
  320.7 1.6 finish.1
  (137 shorter events, 34.5 us)
Async XLA Ops:
  5.7 8.0 %collective-permute-start.6 = (bf16[256,256]{1,0:T(8,128)(2,1)S(1)}, bf16[256,256]{1,0:T(8,128)(2,1)S(1)}, u32[]{:S(2)}, u32[]{:S(2)}) collective-permute-start(bf16[256,256]{1,0:T(8,128)(2,1)S(1)} %get-tuple-element.75), channel_id=1, source_target_pairs={{0,7},{2,5},{4,3},{6,1},{7,0},{5,2},{3,4},{1,6},{8,15},{10,13},{12... | collective-permute-start | bytes 393224 | tf_op jit(solution)/shard_map/ppermute | solution.py:625
  6.9 11.1 %collective-permute-start = (bf16[256,256]{1,0:T(8,128)(2,1)S(1)}, bf16[256,256]{1,0:T(8,128)(2,1)S(1)}, u32[]{:S(2)}, u32[]{:S(2)}) collective-permute-start(bf16[256,256]{1,0:T(8,128)(2,1)S(1)} %get-tuple-element.69), channel_id=1, source_target_pairs={{0,2},{2,4},{4,6},{6,7},{7,5},{5,3},{3,1},{1,0},{8,10},{10,12},{12... | collective-permute-start | bytes 393224 | tf_op jit(solution)/shard_map/ppermute | solution.py:625
  13.8 7.9 %collective-permute-start.7 = (bf16[256,256]{1,0:T(8,128)(2,1)S(1)}, bf16[256,256]{1,0:T(8,128)(2,1)S(1)}, u32[]{:S(2)}, u32[]{:S(2)}) collective-permute-start(bf16[256,256]{1,0:T(8,128)(2,1)S(1)} %collective-permute-done.6.mine.mine_far), channel_id=1, source_target_pairs={{0,8},{8,0},{16,24},{24,16},{1,9},{9,1},{17,25},{25,17},{2,10},{10... | collective-permute-start | bytes 393224 | tf_op jit(solution)/shard_map/ppermute | solution.py:628
  13.8 13.7 %collective-permute-start.1 = (bf16[256,256]{1,0:T(8,128)(2,1)S(1)}, bf16[256,256]{1,0:T(8,128)(2,1)S(1)}, u32[]{:S(2)}, u32[]{:S(2)}) collective-permute-start(bf16[256,256]{1,0:T(8,128)(2,1)S(1)} %get-tuple-element.70), channel_id=1, source_target_pairs={{0,1},{2,0},{4,2},{6,4},{7,6},{5,7},{3,5},{1,3},{8,9},{10,8},{12,1... | collective-permute-start | bytes 393224 | tf_op jit(solution)/shard_map/ppermute | solution.py:625
  15.1 12.4 %collective-permute-start.2 = (bf16[256,256]{1,0:T(8,128)(2,1)S(1)}, bf16[256,256]{1,0:T(8,128)(2,1)S(1)}, u32[]{:S(2)}, u32[]{:S(2)}) collective-permute-start(bf16[256,256]{1,0:T(8,128)(2,1)S(1)} %get-tuple-element.71), channel_id=1, source_target_pairs={{0,4},{2,6},{4,7},{6,5},{7,3},{5,1},{3,0},{1,2},{8,12},{10,14},{12... | collective-permute-start | bytes 393224 | tf_op jit(solution)/shard_map/ppermute | solution.py:625
  17.8 9.7 %collective-permute-start.3 = (bf16[256,256]{1,0:T(8,128)(2,1)S(1)}, bf16[256,256]{1,0:T(8,128)(2,1)S(1)}, u32[]{:S(2)}, u32[]{:S(2)}) collective-permute-start(bf16[256,256]{1,0:T(8,128)(2,1)S(1)} %get-tuple-element.72), channel_id=1, source_target_pairs={{0,3},{2,1},{4,0},{6,2},{7,4},{5,6},{3,7},{1,5},{8,11},{10,9},{12,... | collective-permute-start | bytes 393224 | tf_op jit(solution)/shard_map/ppermute | solution.py:625
  18.0 11.0 %collective-permute-start.4 = (bf16[256,256]{1,0:T(8,128)(2,1)S(1)}, bf16[256,256]{1,0:T(8,128)(2,1)S(1)}, u32[]{:S(2)}, u32[]{:S(2)}) collective-permute-start(bf16[256,256]{1,0:T(8,128)(2,1)S(1)} %get-tuple-element.73), channel_id=1, source_target_pairs={{0,6},{2,7},{4,5},{6,3},{7,1},{5,0},{3,2},{1,4},{8,14},{10,15},{12... | collective-permute-start | bytes 393224 | tf_op jit(solution)/shard_map/ppermute | solution.py:625
  21.6 15.0 %collective-permute-start.5 = (bf16[256,256]{1,0:T(8,128)(2,1)S(1)}, bf16[256,256]{1,0:T(8,128)(2,1)S(1)}, u32[]{:S(2)}, u32[]{:S(2)}) collective-permute-start(bf16[256,256]{1,0:T(8,128)(2,1)S(1)} %get-tuple-element.74), channel_id=1, source_target_pairs={{0,5},{2,3},{4,1},{6,0},{7,2},{5,4},{3,6},{1,7},{8,13},{10,11},{12... | collective-permute-start | bytes 393224 | tf_op jit(solution)/shard_map/ppermute | solution.py:625
  36.7 12.2 %collective-permute-start.8 = (bf16[7,256,256]{2,1,0:T(8,128)(2,1)S(1)}, bf16[7,256,256]{2,1,0:T(8,128)(2,1)S(1)}, u32[]{:S(2)}, u32[]{:S(2)}) collective-permute-start(bf16[7,256,256]{2,1,0:T(8,128)(2,1)S(1)} %stack.1.refs_1_.refs_3_.mine), channel_id=1, source_target_pairs={{0,8},{8,0},{16,24},{24,16},{1,9},{9,1},{17,25},{25,17},{2,10},{10... | collective-permute-start | bytes 2752520 | tf_op jit(solution)/shard_map/ppermute | solution.py:628
  36.8 12.0 %collective-permute-start.10 = (bf16[3,128,512]{2,1,0:T(8,128)(2,1)S(1)}, bf16[3,128,512]{2,1,0:T(8,128)(2,1)S(1)}, u32[]{:S(2)}, u32[]{:S(2)}) collective-permute-start(bf16[3,128,512]{2,1,0:T(8,128)(2,1)S(1)} %get-tuple-element.78), channel_id=1, source_target_pairs={{0,1},{2,0},{4,2},{6,4},{7,6},{5,7},{3,5},{1,3},{8,9},{10,8},{12,1... | collective-permute-start | bytes 1179656 | tf_op jit(solution)/shard_map/ppermute | solution.py:625
  36.8 12.0 %collective-permute-start.9 = (bf16[3,128,512]{2,1,0:T(8,128)(2,1)S(1)}, bf16[3,128,512]{2,1,0:T(8,128)(2,1)S(1)}, u32[]{:S(2)}, u32[]{:S(2)}) collective-permute-start(bf16[3,128,512]{2,1,0:T(8,128)(2,1)S(1)} %get-tuple-element.77.refs_7_), channel_id=1, source_target_pairs={{0,2},{2,4},{4,6},{6,7},{7,5},{5,3},{3,1},{1,0},{8,10},{10,12},{12... | collective-permute-start | bytes 1179656 | tf_op jit(solution)/shard_map/ppermute | solution.py:625
  38.8 18.4 %collective-permute-start.17 = (bf16[3,128,512]{2,1,0:T(8,128)(2,1)S(1)}, bf16[3,128,512]{2,1,0:T(8,128)(2,1)S(1)}, u32[]{:S(2)}, u32[]{:S(2)}) collective-permute-start(bf16[3,128,512]{2,1,0:T(8,128)(2,1)S(1)} %get-tuple-element.86), channel_id=1, source_target_pairs={{0,2},{2,4},{4,6},{6,7},{7,5},{5,3},{3,1},{1,0},{8,10},{10,12},{12... | collective-permute-start | bytes 1179656 | tf_op jit(solution)/shard_map/ppermute | solution.py:625
  38.9 18.4 %collective-permute-start.18 = (bf16[3,128,512]{2,1,0:T(8,128)(2,1)S(1)}, bf16[3,128,512]{2,1,0:T(8,128)(2,1)S(1)}, u32[]{:S(2)}, u32[]{:S(2)}) collective-permute-start(bf16[3,128,512]{2,1,0:T(8,128)(2,1)S(1)} %get-tuple-element.87), channel_id=1, source_target_pairs={{0,1},{2,0},{4,2},{6,4},{7,6},{5,7},{3,5},{1,3},{8,9},{10,8},{12,1... | collective-permute-start | bytes 1179656 | tf_op jit(solution)/shard_map/ppermute | solution.py:625
  50.9 23.2 %collective-permute-start.11 = (bf16[3,256,512]{2,1,0:T(8,128)(2,1)S(1)}, bf16[3,256,512]{2,1,0:T(8,128)(2,1)S(1)}, u32[]{:S(2)}, u32[]{:S(2)}) collective-permute-start(bf16[3,256,512]{2,1,0:T(8,128)(2,1)S(1)} %get-tuple-element.79), channel_id=1, source_target_pairs={{0,2},{2,4},{4,6},{6,7},{7,5},{5,3},{3,1},{1,0},{8,10},{10,12},{12... | collective-permute-start | bytes 2359304 | tf_op jit(solution)/shard_map/ppermute | solution.py:625
  52.9 21.2 %collective-permute-start.12 = (bf16[3,256,512]{2,1,0:T(8,128)(2,1)S(1)}, bf16[3,256,512]{2,1,0:T(8,128)(2,1)S(1)}, u32[]{:S(2)}, u32[]{:S(2)}) collective-permute-start(bf16[3,256,512]{2,1,0:T(8,128)(2,1)S(1)} %get-tuple-element.80), channel_id=1, source_target_pairs={{0,1},{2,0},{4,2},{6,4},{7,6},{5,7},{3,5},{1,3},{8,9},{10,8},{12,1... | collective-permute-start | bytes 2359304 | tf_op jit(solution)/shard_map/ppermute | solution.py:625
  59.3 31.6 %collective-permute-start.19 = (bf16[3,256,512]{2,1,0:T(8,128)(2,1)S(1)}, bf16[3,256,512]{2,1,0:T(8,128)(2,1)S(1)}, u32[]{:S(2)}, u32[]{:S(2)}) collective-permute-start(bf16[3,256,512]{2,1,0:T(8,128)(2,1)S(1)} %get-tuple-element.88), channel_id=1, source_target_pairs={{0,2},{2,4},{4,6},{6,7},{7,5},{5,3},{3,1},{1,0},{8,10},{10,12},{12... | collective-permute-start | bytes 2359304 | tf_op jit(solution)/shard_map/ppermute | solution.py:625
  61.3 29.6 %collective-permute-start.20 = (bf16[3,256,512]{2,1,0:T(8,128)(2,1)S(1)}, bf16[3,256,512]{2,1,0:T(8,128)(2,1)S(1)}, u32[]{:S(2)}, u32[]{:S(2)}) collective-permute-start(bf16[3,256,512]{2,1,0:T(8,128)(2,1)S(1)} %get-tuple-element.89), channel_id=1, source_target_pairs={{0,1},{2,0},{4,2},{6,4},{7,6},{5,7},{3,5},{1,3},{8,9},{10,8},{12,1... | collective-permute-start | bytes 2359304 | tf_op jit(solution)/shard_map/ppermute | solution.py:625
  76.2 31.6 %collective-permute-start.13 = (bf16[3,256,512]{2,1,0:T(8,128)(2,1)S(1)}, bf16[3,256,512]{2,1,0:T(8,128)(2,1)S(1)}, u32[]{:S(2)}, u32[]{:S(2)}) collective-permute-start(bf16[3,256,512]{2,1,0:T(8,128)(2,1)S(1)} %get-tuple-element.81), channel_id=1, source_target_pairs={{0,2},{2,4},{4,6},{6,7},{7,5},{5,3},{3,1},{1,0},{8,10},{10,12},{12... | collective-permute-start | bytes 2359304 | tf_op jit(solution)/shard_map/ppermute | solution.py:625
  78.2 29.6 %collective-permute-start.14 = (bf16[3,256,512]{2,1,0:T(8,128)(2,1)S(1)}, bf16[3,256,512]{2,1,0:T(8,128)(2,1)S(1)}, u32[]{:S(2)}, u32[]{:S(2)}) collective-permute-start(bf16[3,256,512]{2,1,0:T(8,128)(2,1)S(1)} %get-tuple-element.82), channel_id=1, source_target_pairs={{0,1},{2,0},{4,2},{6,4},{7,6},{5,7},{3,5},{1,3},{8,9},{10,8},{12,1... | collective-permute-start | bytes 2359304 | tf_op jit(solution)/shard_map/ppermute | solution.py:625
  93.0 31.6 %collective-permute-start.21 = (bf16[3,256,512]{2,1,0:T(8,128)(2,1)S(1)}, bf16[3,256,512]{2,1,0:T(8,128)(2,1)S(1)}, u32[]{:S(2)}, u32[]{:S(2)}) collective-permute-start(bf16[3,256,512]{2,1,0:T(8,128)(2,1)S(1)} %get-tuple-element.90), channel_id=1, source_target_pairs={{0,2},{2,4},{4,6},{6,7},{7,5},{5,3},{3,1},{1,0},{8,10},{10,12},{12... | collective-permute-start | bytes 2359304 | tf_op jit(solution)/shard_map/ppermute | solution.py:625
  95.0 29.6 %collective-permute-start.22 = (bf16[3,256,512]{2,1,0:T(8,128)(2,1)S(1)}, bf16[3,256,512]{2,1,0:T(8,128)(2,1)S(1)}, u32[]{:S(2)}, u32[]{:S(2)}) collective-permute-start(bf16[3,256,512]{2,1,0:T(8,128)(2,1)S(1)} %get-tuple-element.91), channel_id=1, source_target_pairs={{0,1},{2,0},{4,2},{6,4},{7,6},{5,7},{3,5},{1,3},{8,9},{10,8},{12,1... | collective-permute-start | bytes 2359304 | tf_op jit(solution)/shard_map/ppermute | solution.py:625
  96.3 28.4 %copy-start = (bf16[512,2048]{1,0:T(8,128)(2,1)}, bf16[512,2048]{1,0:T(8,128)(2,1)S(1)}, u32[]{:S(2)}) copy-start(bf16[512,2048]{1,0:T(8,128)(2,1)S(1)} %turn.1.refs_9_.refs_0_) | copy-start | bytes 6291460
  109.9 31.6 %collective-permute-start.15 = (bf16[3,256,512]{2,1,0:T(8,128)(2,1)S(1)}, bf16[3,256,512]{2,1,0:T(8,128)(2,1)S(1)}, u32[]{:S(2)}, u32[]{:S(2)}) collective-permute-start(bf16[3,256,512]{2,1,0:T(8,128)(2,1)S(1)} %get-tuple-element.83), channel_id=1, source_target_pairs={{0,2},{2,4},{4,6},{6,7},{7,5},{5,3},{3,1},{1,0},{8,10},{10,12},{12... | collective-permute-start | bytes 2359304 | tf_op jit(solution)/shard_map/ppermute | solution.py:625
  111.9 29.6 %copy-start.20 = (bf16[256,1024]{1,0:T(8,128)(2,1)S(1)}, bf16[256,1024]{1,0:T(8,128)(2,1)}, u32[]{:S(2)}) copy-start(bf16[256,1024]{1,0:T(8,128)(2,1)} %d_out.3) | copy-start | bytes 1572868
  111.9 29.6 %collective-permute-start.16 = (bf16[3,256,512]{2,1,0:T(8,128)(2,1)S(1)}, bf16[3,256,512]{2,1,0:T(8,128)(2,1)S(1)}, u32[]{:S(2)}, u32[]{:S(2)}) collective-permute-start(bf16[3,256,512]{2,1,0:T(8,128)(2,1)S(1)} %get-tuple-element.84), channel_id=1, source_target_pairs={{0,1},{2,0},{4,2},{6,4},{7,6},{5,7},{3,5},{1,3},{8,9},{10,8},{12,1... | collective-permute-start | bytes 2359304 | tf_op jit(solution)/shard_map/ppermute | solution.py:625
  126.7 31.6 %collective-permute-start.23 = (bf16[3,256,512]{2,1,0:T(8,128)(2,1)S(1)}, bf16[3,256,512]{2,1,0:T(8,128)(2,1)S(1)}, u32[]{:S(2)}, u32[]{:S(2)}) collective-permute-start(bf16[3,256,512]{2,1,0:T(8,128)(2,1)S(1)} %get-tuple-element.92), channel_id=1, source_target_pairs={{0,2},{2,4},{4,6},{6,7},{7,5},{5,3},{3,1},{1,0},{8,10},{10,12},{12... | collective-permute-start | bytes 2359304 | tf_op jit(solution)/shard_map/ppermute | solution.py:625
  128.8 29.6 %collective-permute-start.24 = (bf16[3,256,512]{2,1,0:T(8,128)(2,1)S(1)}, bf16[3,256,512]{2,1,0:T(8,128)(2,1)S(1)}, u32[]{:S(2)}, u32[]{:S(2)}) collective-permute-start(bf16[3,256,512]{2,1,0:T(8,128)(2,1)S(1)} %get-tuple-element.93), channel_id=1, source_target_pairs={{0,1},{2,0},{4,2},{6,4},{7,6},{5,7},{3,5},{1,3},{8,9},{10,8},{12,1... | collective-permute-start | bytes 2359304 | tf_op jit(solution)/shard_map/ppermute | solution.py:625
  149.4 16.2 %copy-start.10 = (bf16[3,256,512]{2,1,0:T(8,128)(2,1)}, bf16[3,256,512]{2,1,0:T(8,128)(2,1)S(1)}, u32[]{:S(2)}) copy-start(bf16[3,256,512]{2,1,0:T(8,128)(2,1)S(1)} %get-tuple-element.99.refs_0_.refs_1_) | copy-start | bytes 2359300
  149.4 25.7 %collective-permute-start.30 = (bf16[3,256,512]{2,1,0:T(8,128)(2,1)S(1)}, bf16[3,256,512]{2,1,0:T(8,128)(2,1)S(1)}, u32[]{:S(2)}, u32[]{:S(2)}) collective-permute-start(bf16[3,256,512]{2,1,0:T(8,128)(2,1)S(1)} %get-tuple-element.99.refs_0_.refs_1_), channel_id=1, source_target_pairs={{0,1},{2,0},{4,2},{6,4},{7,6},{5,7},{3,5},{1,3},{8,9},{10,8},{12,1... | collective-permute-start | bytes 2359304 | tf_op jit(solution)/shard_map/ppermute | solution.py:625
  149.4 26.7 %collective-permute-start.27 = (bf16[3,256,512]{2,1,0:T(8,128)(2,1)S(1)}, bf16[3,256,512]{2,1,0:T(8,128)(2,1)S(1)}, u32[]{:S(2)}, u32[]{:S(2)}) collective-permute-start(bf16[3,256,512]{2,1,0:T(8,128)(2,1)S(1)} %get-tuple-element.99.refs_0_.refs_1_), channel_id=1, source_target_pairs={{0,2},{2,4},{4,6},{6,7},{7,5},{5,3},{3,1},{1,0},{8,10},{10,12},{12... | collective-permute-start | bytes 2359304 | tf_op jit(solution)/shard_map/ppermute | solution.py:625
  167.0 25.0 %collective-permute-start.38 = (bf16[3,256,512]{2,1,0:T(8,128)(2,1)S(1)}, bf16[3,256,512]{2,1,0:T(8,128)(2,1)S(1)}, u32[]{:S(2)}, u32[]{:S(2)}) collective-permute-start(bf16[3,256,512]{2,1,0:T(8,128)(2,1)S(1)} %get-tuple-element.104.refs_0_.refs_1_), channel_id=1, source_target_pairs={{0,1},{2,0},{4,2},{6,4},{7,6},{5,7},{3,5},{1,3},{8,9},{10,8},{12,1... | collective-permute-start | bytes 2359304 | tf_op jit(solution)/shard_map/ppermute | solution.py:625
  167.0 25.9 %collective-permute-start.35 = (bf16[3,256,512]{2,1,0:T(8,128)(2,1)S(1)}, bf16[3,256,512]{2,1,0:T(8,128)(2,1)S(1)}, u32[]{:S(2)}, u32[]{:S(2)}) collective-permute-start(bf16[3,256,512]{2,1,0:T(8,128)(2,1)S(1)} %get-tuple-element.104.refs_0_.refs_1_), channel_id=1, source_target_pairs={{0,2},{2,4},{4,6},{6,7},{7,5},{5,3},{3,1},{1,0},{8,10},{10,12},{12... | collective-permute-start | bytes 2359304 | tf_op jit(solution)/shard_map/ppermute | solution.py:625
  175.1 33.8 %collective-permute-start.31 = (bf16[3,256,512]{2,1,0:T(8,128)(2,1)S(1)}, bf16[3,256,512]{2,1,0:T(8,128)(2,1)}, u32[]{:S(2)}, u32[]{:S(2)}) collective-permute-start(bf16[3,256,512]{2,1,0:T(8,128)(2,1)S(1)} %collective-permute-done.30.refs_2_.refs_3_), channel_id=1, source_target_pairs={{0,1},{2,0},{4,2},{6,4},{7,6},{5,7},{3,5},{1,3},{8,9},{10,8},{12,1... | collective-permute-start | bytes 2359304 | tf_op jit(solution)/shard_map/ppermute | solution.py:625
  176.1 32.9 %collective-permute-start.28 = (bf16[3,256,512]{2,1,0:T(8,128)(2,1)S(1)}, bf16[3,256,512]{2,1,0:T(8,128)(2,1)}, u32[]{:S(2)}, u32[]{:S(2)}) collective-permute-start(bf16[3,256,512]{2,1,0:T(8,128)(2,1)S(1)} %collective-permute-done.27.refs_1_.refs_2_), channel_id=1, source_target_pairs={{0,2},{2,4},{4,6},{6,7},{7,5},{5,3},{3,1},{1,0},{8,10},{10,12},{12... | collective-permute-start | bytes 2359304 | tf_op jit(solution)/shard_map/ppermute | solution.py:625
  192.0 33.8 %collective-permute-start.39 = (bf16[3,256,512]{2,1,0:T(8,128)(2,1)S(1)}, bf16[3,256,512]{2,1,0:T(8,128)(2,1)}, u32[]{:S(2)}, u32[]{:S(2)}) collective-permute-start(bf16[3,256,512]{2,1,0:T(8,128)(2,1)S(1)} %collective-permute-done.38.refs_2_.refs_3_), channel_id=1, source_target_pairs={{0,1},{2,0},{4,2},{6,4},{7,6},{5,7},{3,5},{1,3},{8,9},{10,8},{12,1... | collective-permute-start | bytes 2359304 | tf_op jit(solution)/shard_map/ppermute | solution.py:625
  192.9 32.9 %collective-permute-start.36 = (bf16[3,256,512]{2,1,0:T(8,128)(2,1)S(1)}, bf16[3,256,512]{2,1,0:T(8,128)(2,1)}, u32[]{:S(2)}, u32[]{:S(2)}) collective-permute-start(bf16[3,256,512]{2,1,0:T(8,128)(2,1)S(1)} %collective-permute-done.35.refs_1_.refs_2_), channel_id=1, source_target_pairs={{0,2},{2,4},{4,6},{6,7},{7,5},{5,3},{3,1},{1,0},{8,10},{10,12},{12... | collective-permute-start | bytes 2359304 | tf_op jit(solution)/shard_map/ppermute | solution.py:625
  208.9 34.7 %collective-permute-start.32 = (bf16[3,256,512]{2,1,0:T(8,128)(2,1)}, bf16[3,256,512]{2,1,0:T(8,128)(2,1)}, u32[]{:S(2)}, u32[]{:S(2)}) collective-permute-start(bf16[3,256,512]{2,1,0:T(8,128)(2,1)} %collective-permute-done.31.refs_1_.refs_5_), channel_id=1, source_target_pairs={{0,1},{2,0},{4,2},{6,4},{7,6},{5,7},{3,5},{1,3},{8,9},{10,8},{12,1... | collective-permute-start | bytes 2359304 | tf_op jit(solution)/shard_map/ppermute | solution.py:625
  209.0 34.6 %collective-permute-start.29 = (bf16[3,256,512]{2,1,0:T(8,128)(2,1)}, bf16[3,256,512]{2,1,0:T(8,128)(2,1)}, u32[]{:S(2)}, u32[]{:S(2)}) collective-permute-start(bf16[3,256,512]{2,1,0:T(8,128)(2,1)} %collective-permute-done.28.refs_0_.refs_4_), channel_id=1, source_target_pairs={{0,2},{2,4},{4,6},{6,7},{7,5},{5,3},{3,1},{1,0},{8,10},{10,12},{12... | collective-permute-start | bytes 2359304 | tf_op jit(solution)/shard_map/ppermute | solution.py:625
  225.8 33.7 %collective-permute-start.40 = (bf16[3,256,512]{2,1,0:T(8,128)(2,1)}, bf16[3,256,512]{2,1,0:T(8,128)(2,1)}, u32[]{:S(2)}, u32[]{:S(2)}) collective-permute-start(bf16[3,256,512]{2,1,0:T(8,128)(2,1)} %collective-permute-done.39.refs_1_.refs_5_), channel_id=1, source_target_pairs={{0,1},{2,0},{4,2},{6,4},{7,6},{5,7},{3,5},{1,3},{8,9},{10,8},{12,1... | collective-permute-start | bytes 2359304 | tf_op jit(solution)/shard_map/ppermute | solution.py:625
  225.9 33.7 %collective-permute-start.37 = (bf16[3,256,512]{2,1,0:T(8,128)(2,1)}, bf16[3,256,512]{2,1,0:T(8,128)(2,1)}, u32[]{:S(2)}, u32[]{:S(2)}) collective-permute-start(bf16[3,256,512]{2,1,0:T(8,128)(2,1)} %collective-permute-done.36.refs_0_.refs_4_), channel_id=1, source_target_pairs={{0,2},{2,4},{4,6},{6,7},{7,5},{5,3},{3,1},{1,0},{8,10},{10,12},{12... | collective-permute-start | bytes 2359304 | tf_op jit(solution)/shard_map/ppermute | solution.py:625
  230.7 1.6 collective-permute-start.25
  233.2 5.6 %collective-permute-start.26 = (f32[256,1]{1,0:T(8,128)S(1)}, f32[256,1]{1,0:T(8,128)S(1)}, u32[]{:S(2)}, u32[]{:S(2)}) collective-permute-start(f32[256,1]{1,0:T(8,128)S(1)} %add.31), channel_id=1, source_target_pairs={{0,16},{8,24},{16,0},{24,8},{1,17},{9,25},{17,1},{25,9},{2,18},{10... | collective-permute-start | bytes 3080 | tf_op jit(solution)/shard_map/ppermute | solution.py:628
  242.2 20.9 %copy-start.5 = (bf16[3,256,512]{2,1,0:T(8,128)(2,1)S(1)}, bf16[3,256,512]{2,1,0:T(8,128)(2,1)}, u32[]{:S(2)}) copy-start(bf16[3,256,512]{2,1,0:T(8,128)(2,1)} %copy-done.4) | copy-start | bytes 2359300
  242.2 20.9 %copy-start.7 = (bf16[3,256,512]{2,1,0:T(8,128)(2,1)S(1)}, bf16[3,256,512]{2,1,0:T(8,128)(2,1)}, u32[]{:S(2)}) copy-start(bf16[3,256,512]{2,1,0:T(8,128)(2,1)} %copy-done.6) | copy-start | bytes 2359300
  242.2 20.9 %copy-start.9 = (bf16[3,256,512]{2,1,0:T(8,128)(2,1)S(1)}, bf16[3,256,512]{2,1,0:T(8,128)(2,1)}, u32[]{:S(2)}) copy-start(bf16[3,256,512]{2,1,0:T(8,128)(2,1)} %copy-done.8) | copy-start | bytes 2359300
  245.1 28.8 %collective-permute-start.33 = (bf16[3,128,512]{2,1,0:T(8,128)(2,1)S(1)}, bf16[3,128,512]{2,1,0:T(8,128)(2,1)S(1)}, u32[]{:S(2)}, u32[]{:S(2)}) collective-permute-start(bf16[3,128,512]{2,1,0:T(8,128)(2,1)S(1)} %get-tuple-element.100), channel_id=1, source_target_pairs={{0,2},{2,4},{4,6},{6,7},{7,5},{5,3},{3,1},{1,0},{8,10},{10,12},{12... | collective-permute-start | bytes 1179656 | tf_op jit(solution)/shard_map/ppermute | solution.py:625
  246.2 27.7 %collective-permute-start.34 = (bf16[3,128,512]{2,1,0:T(8,128)(2,1)S(1)}, bf16[3,128,512]{2,1,0:T(8,128)(2,1)S(1)}, u32[]{:S(2)}, u32[]{:S(2)}) collective-permute-start(bf16[3,128,512]{2,1,0:T(8,128)(2,1)S(1)} %get-tuple-element.101), channel_id=1, source_target_pairs={{0,1},{2,0},{4,2},{6,4},{7,6},{5,7},{3,5},{1,3},{8,9},{10,8},{12,1... | collective-permute-start | bytes 1179656 | tf_op jit(solution)/shard_map/ppermute | solution.py:625
  261.0 14.8 %collective-permute-start.41 = (bf16[3,128,512]{2,1,0:T(8,128)(2,1)S(1)}, bf16[3,128,512]{2,1,0:T(8,128)(2,1)S(1)}, u32[]{:S(2)}, u32[]{:S(2)}) collective-permute-start(bf16[3,128,512]{2,1,0:T(8,128)(2,1)S(1)} %get-tuple-element.105), channel_id=1, source_target_pairs={{0,2},{2,4},{4,6},{6,7},{7,5},{5,3},{3,1},{1,0},{8,10},{10,12},{12... | collective-permute-start | bytes 1179656 | tf_op jit(solution)/shard_map/ppermute | solution.py:625
  263.0 12.8 %collective-permute-start.42 = (bf16[3,128,512]{2,1,0:T(8,128)(2,1)S(1)}, bf16[3,128,512]{2,1,0:T(8,128)(2,1)S(1)}, u32[]{:S(2)}, u32[]{:S(2)}) collective-permute-start(bf16[3,128,512]{2,1,0:T(8,128)(2,1)S(1)} %get-tuple-element.106), channel_id=1, source_target_pairs={{0,1},{2,0},{4,2},{6,4},{7,6},{5,7},{3,5},{1,3},{8,9},{10,8},{12,1... | collective-permute-start | bytes 1179656 | tf_op jit(solution)/shard_map/ppermute | solution.py:625
  275.8 7.1 %copy-start.22 = (bf16[256,512]{1,0:T(8,128)(2,1)S(1)}, bf16[256,512]{1,0:T(8,128)(2,1)}, u32[]{:S(2)}) copy-start(bf16[256,512]{1,0:T(8,128)(2,1)} %copy-done.21) | copy-start | bytes 786436
  277.5 30.5 %copy-start.1 = (bf16[512,2048]{1,0:T(8,128)(2,1)S(1)}, bf16[512,2048]{1,0:T(8,128)(2,1)}, u32[]{:S(2)}) copy-start(bf16[512,2048]{1,0:T(8,128)(2,1)} %copy-done) | copy-start | bytes 6291460
  277.5 30.5 %copy-start.12 = (bf16[3,256,512]{2,1,0:T(8,128)(2,1)S(1)}, bf16[3,256,512]{2,1,0:T(8,128)(2,1)}, u32[]{:S(2)}) copy-start(bf16[3,256,512]{2,1,0:T(8,128)(2,1)} %copy-done.10) | copy-start | bytes 2359300
  277.5 30.5 %copy-start.15 = (bf16[3,256,512]{2,1,0:T(8,128)(2,1)S(1)}, bf16[3,256,512]{2,1,0:T(8,128)(2,1)}, u32[]{:S(2)}) copy-start(bf16[3,256,512]{2,1,0:T(8,128)(2,1)} %copy-done.13) | copy-start | bytes 2359300
  277.5 30.5 %copy-start.18 = (bf16[3,256,512]{2,1,0:T(8,128)(2,1)S(1)}, bf16[3,256,512]{2,1,0:T(8,128)(2,1)}, u32[]{:S(2)}) copy-start(bf16[3,256,512]{2,1,0:T(8,128)(2,1)} %copy-done.16) | copy-start | bytes 2359300
  277.5 2.0 collective-permute-start.43
  277.6 4.1 %collective-permute-start.47 = (bf16[4,128,512]{2,1,0:T(8,128)(2,1)S(1)}, bf16[4,128,512]{2,1,0:T(8,128)(2,1)S(1)}, u32[]{:S(2)}, u32[]{:S(2)}) collective-permute-start(bf16[4,128,512]{2,1,0:T(8,128)(2,1)S(1)} %get-tuple-element.128), channel_id=1, source_target_pairs={{0,8},{8,0},{16,24},{24,16},{1,9},{9,1},{17,25},{25,17},{2,10},{10... | collective-permute-start | bytes 1572872 | tf_op jit(solution)/shard_map/ppermute | solution.py:628
  280.1 9.2 %collective-permute-start.44 = (bf16[2,128,512]{2,1,0:T(8,128)(2,1)S(1)}, bf16[2,128,512]{2,1,0:T(8,128)(2,1)S(1)}, u32[]{:S(2)}, u32[]{:S(2)}) collective-permute-start(bf16[2,128,512]{2,1,0:T(8,128)(2,1)S(1)} %get-tuple-element.124), channel_id=1, source_target_pairs={{0,16},{8,24},{16,0},{24,8},{1,17},{9,25},{17,1},{25,9},{2,18},{10... | collective-permute-start | bytes 786440 | tf_op jit(solution)/shard_map/ppermute | solution.py:628
  282.3 15.2 %collective-permute-start.48 = (bf16[2,128,512]{2,1,0:T(8,128)(2,1)S(1)}, bf16[2,128,512]{2,1,0:T(8,128)(2,1)S(1)}, u32[]{:S(2)}, u32[]{:S(2)}) collective-permute-start(bf16[2,128,512]{2,1,0:T(8,128)(2,1)S(1)} %get-tuple-element.130), channel_id=1, source_target_pairs={{0,16},{8,24},{16,0},{24,8},{1,17},{9,25},{17,1},{25,9},{2,18},{10... | collective-permute-start | bytes 786440 | tf_op jit(solution)/shard_map/ppermute | solution.py:628
  289.9 30.7 %collective-permute-start.46 = (bf16[128,512]{1,0:T(8,128)(2,1)S(1)}, bf16[128,512]{1,0:T(8,128)(2,1)S(1)}, u32[]{:S(2)}, u32[]{:S(2)}) collective-permute-start(bf16[128,512]{1,0:T(8,128)(2,1)S(1)} %get-tuple-element.126), channel_id=1, source_target_pairs={{0,1},{1,0},{2,9},{3,8},{4,17},{5,16},{6,25},{7,24},{8,5},{9,4},{1... | collective-permute-start | bytes 393224 | tf_op jit(solution)/shard_map/ppermute | solution.py:686
  290.2 30.5 %collective-permute-start.45 = (bf16[128,512]{1,0:T(8,128)(2,1)S(1)}, bf16[128,512]{1,0:T(8,128)(2,1)S(1)}, u32[]{:S(2)}, u32[]{:S(2)}) collective-permute-start(bf16[128,512]{1,0:T(8,128)(2,1)S(1)} %get-tuple-element.125.refs_10_), channel_id=1, source_target_pairs={{0,0},{1,1},{2,8},{3,9},{4,16},{5,17},{6,24},{7,25},{8,4},{9,5},{1... | collective-permute-start | bytes 393224 | tf_op jit(solution)/shard_map/ppermute | solution.py:686
  298.1 22.6 %collective-permute-start.50 = (bf16[128,512]{1,0:T(8,128)(2,1)S(1)}, bf16[128,512]{1,0:T(8,128)(2,1)S(1)}, u32[]{:S(2)}, u32[]{:S(2)}) collective-permute-start(bf16[128,512]{1,0:T(8,128)(2,1)S(1)} %get-tuple-element.132), channel_id=1, source_target_pairs={{0,1},{1,0},{2,9},{3,8},{4,17},{5,16},{6,25},{7,24},{8,5},{9,4},{1... | collective-permute-start | bytes 393224 | tf_op jit(solution)/shard_map/ppermute | solution.py:686
  298.4 22.3 %collective-permute-start.49 = (bf16[128,512]{1,0:T(8,128)(2,1)S(1)}, bf16[128,512]{1,0:T(8,128)(2,1)S(1)}, u32[]{:S(2)}, u32[]{:S(2)}) collective-permute-start(bf16[128,512]{1,0:T(8,128)(2,1)S(1)} %get-tuple-element.131.refs_11_), channel_id=1, source_target_pairs={{0,0},{1,1},{2,8},{3,9},{4,16},{5,17},{6,24},{7,25},{8,4},{9,5},{1... | collective-permute-start | bytes 393224 | tf_op jit(solution)/shard_map/ppermute | solution.py:686
  314.2 6.4 %copy-start.3 = (bf16[256,4096]{1,0:T(8,128)(2,1)S(1)}, bf16[256,4096]{1,0:T(8,128)(2,1)}, u32[]{:S(2)}) copy-start(bf16[256,4096]{1,0:T(8,128)(2,1)} %tokens.3) | copy-start | bytes 6291460
  314.3 6.5 %copy-start.24 = (f32[256,128]{1,0:T(8,128)S(1)}, f32[256,128]{1,0:T(8,128)}, u32[]{:S(2)}) copy-start(f32[256,128]{1,0:T(8,128)} %copy-done.23) | copy-start | bytes 393220
  (15 other events, 14.9 us)

commit v11 on v7

--- a/solution.py
+++ b/solution.py
@@ -708,9 +708,9 @@
     d_tokens = finish(
         idx, column, tokens, norm_gain[None], inverse_rms, dots, came, width // nodes
     )
+    grads = grads_chunk(rows_turned, gathered[0], None, [keep_1], 0, wide, columns)
     sums = [first[0], second[0]]
-    grads = grads_chunk(rows_turned, gathered[0], None, sums, 0, wide, columns)
-    grads = grads_chunk(rows_turned, gathered[1], grads, [], 1, wide, columns)
+    grads = grads_chunk(rows_turned, gathered[1], grads, sums, 1, wide, columns)
     return (jnp.concatenate(outputs, axis=-1), d_tokens, grads)
 
 

time: 320 us -> 320 us (level)
    ppermute x4, waiting for transfers between devices: 0.01 us -> 6.4 us  [relocate(): came.append(lax.ppermute(block, ('node', 'local'), moves))]
    ppermute x8, waiting for transfers between devices: 13.5 us -> 7.25 us  [swap(): return lax.ppermute(array, 'node', [(n, n ^ bit) for n in range(nodes)])]
  transfers between devices with their start and end apart: 51 -> 51, of which waited for: 24 -> 27; matrix products, arithmetic and copies ran while one was open for 2% -> 2% of each run, Pallas kernels for 19% -> 19%
where the time goes in v11:
time: 320 us; the launch traced here: 319 us
  waiting for transfers between devices  164 us (51%)
  Pallas kernels  66.2 us (21%)
  starting transfers between devices  65.5 us (20%)
  local copies, waits for them, and re-layouts  17.1 us (5%)
  other arithmetic  4.53 us (1%)
    ppermute x39, waiting for transfers between devices, shift(): return lax.ppermute(array, 'local', moves)  151 us
    ppermute x39, starting transfers between devices, shift(): return lax.ppermute(array, 'local', moves)  49.5 us
    unnamed x56, local copies, waits for them, and re-layouts  14.9 us
    pallas_call x2, Pallas kernels, attention(): pl.pallas_call(attention_kernel, grid_spec=pltpu.PrefetchScalarGridSpec(n...  14.5 us
    pallas_call x7, Pallas kernels, term_step(): pl.pallas_call(kernel, in_specs=[whole] * (1 + count + len(befores)), out...  12.7 us
    ppermute x4, starting transfers between devices, relocate(): came.append(lax.ppermute(block, ('node', 'local'), moves))  12.6 us
    pallas_call x2, Pallas kernels, grads_chunk(): pl.pallas_call(tied(grads_kernel, 1 + len(pieces), len(ties)), grid=(3,),...  12.5 us
    pallas_call x6, Pallas kernels, sum_step(): pl.pallas_call(tied(sum_step_kernel, 9, len(ties)), grid_spec=pltpu.Prefe...  12.3 us
  transfers between devices with their start and end apart: 51, of which 27 were waited for; matrix products, arithmetic and copies ran while one was open for 2% of the time, Pallas kernels for 19%

profile of v11, /device:TPU:2, one launch (start us, length us, event | category | flops | bytes accessed | tf_op | source)
XLA Modules:
  0.0 318.7 jit_solution(8654955414577554374)
XLA Ops:
  2.0 1.6 copy-done.2
  5.7 4.6 %collective-permute-start.6 = (bf16[256,256]{1,0:T(8,128)(2,1)S(1)}, bf16[256,256]{1,0:T(8,128)(2,1)S(1)}, u32[]{:S(2)}, u32[]{:S(2)}) collective-permute-start(bf16[256,256]{1,0:T(8,128)(2,1)S(1)} %get-tuple-element.75), channel_id=1, source_target_pairs={{0,7},{2,5},{4,3},{6,1},{7,0},{5,2},{3,4},{1,6},{8,15},{10,13},{12... | collective-permute-start | bytes 393224 | tf_op jit(solution)/shard_map/ppermute | solution.py:621
  10.3 4.5 %collective-permute-done.6.mine.mine_far = bf16[256,256]{1,0:T(8,128)(2,1)S(1)} collective-permute-done((bf16[256,256]{1,0:T(8,128)(2,1)S(1)}, bf16[256,256]{1,0:T(8,128)(2,1)S(1)}, u32[]{:S(2)}, u32[]{:S(2)}) %collective-permute-start.6) | collective-permute-done | bytes 131104 | tf_op jit(solution)/shard_map/ppermute | solution.py:621
  15.3 3.4 %collective-permute-start.2 = (bf16[256,256]{1,0:T(8,128)(2,1)S(1)}, bf16[256,256]{1,0:T(8,128)(2,1)S(1)}, u32[]{:S(2)}, u32[]{:S(2)}) collective-permute-start(bf16[256,256]{1,0:T(8,128)(2,1)S(1)} %get-tuple-element.71), channel_id=1, source_target_pairs={{0,4},{2,6},{4,7},{6,5},{7,3},{5,1},{3,0},{1,2},{8,12},{10,14},{12... | collective-permute-start | bytes 393224 | tf_op jit(solution)/shard_map/ppermute | solution.py:621
  19.9 1.7 collective-permute-start.4
  21.7 2.1 collective-permute-start.5
  23.8 1.9 copy-done.4
  27.5 1.9 sum_first.1
  29.4 4.6 %collective-permute-done.3.refs_4_ = bf16[256,256]{1,0:T(8,128)(2,1)S(1)} collective-permute-done((bf16[256,256]{1,0:T(8,128)(2,1)S(1)}, bf16[256,256]{1,0:T(8,128)(2,1)S(1)}, u32[]{:S(2)}, u32[]{:S(2)}) %collective-permute-start.3) | collective-permute-done | bytes 131104 | tf_op jit(solution)/shard_map/ppermute | solution.py:621
  35.2 3.1 collective-permute-start.10
  38.4 2.1 collective-permute-start.18
  40.4 7.4 %collective-permute-done.10.refs_8_ = bf16[3,128,512]{2,1,0:T(8,128)(2,1)S(1)} collective-permute-done((bf16[3,128,512]{2,1,0:T(8,128)(2,1)S(1)}, bf16[3,128,512]{2,1,0:T(8,128)(2,1)S(1)}, u32[]{:S(2)}, u32[]{:S(2)}) %collective-permute-start.10) | collective-permute-done | bytes 393248 | tf_op jit(solution)/shard_map/ppermute | solution.py:621
  47.8 2.5 collective-permute-done.9.refs_7_
  50.3 2.1 sum_step.6
  52.4 2.0 collective-permute-start.12
  54.5 4.3 %collective-permute-done.17.refs_7_ = bf16[3,128,512]{2,1,0:T(8,128)(2,1)S(1)} collective-permute-done((bf16[3,128,512]{2,1,0:T(8,128)(2,1)S(1)}, bf16[3,128,512]{2,1,0:T(8,128)(2,1)S(1)}, u32[]{:S(2)}, u32[]{:S(2)}) %collective-permute-start.17) | collective-permute-done | bytes 393248 | tf_op jit(solution)/shard_map/ppermute | solution.py:621
  58.7 2.1 sum_step.9
  60.9 2.0 collective-permute-start.20
  62.9 12.7 %collective-permute-done.11.refs_7_ = bf16[3,256,512]{2,1,0:T(8,128)(2,1)S(1)} collective-permute-done((bf16[3,256,512]{2,1,0:T(8,128)(2,1)S(1)}, bf16[3,256,512]{2,1,0:T(8,128)(2,1)S(1)}, u32[]{:S(2)}, u32[]{:S(2)}) %collective-permute-start.11) | collective-permute-done | bytes 786464 | tf_op jit(solution)/shard_map/ppermute | solution.py:621
  75.6 2.1 sum_step.7
  77.7 2.0 collective-permute-start.14
  79.7 12.7 %collective-permute-done.19.refs_7_ = bf16[3,256,512]{2,1,0:T(8,128)(2,1)S(1)} collective-permute-done((bf16[3,256,512]{2,1,0:T(8,128)(2,1)S(1)}, bf16[3,256,512]{2,1,0:T(8,128)(2,1)S(1)}, u32[]{:S(2)}, u32[]{:S(2)}) %collective-permute-start.19) | collective-permute-done | bytes 786464 | tf_op jit(solution)/shard_map/ppermute | solution.py:621
  92.4 2.1 sum_step.10
  94.6 2.0 collective-permute-start.22
  97.8 11.5 %collective-permute-done.13.refs_7_ = bf16[3,256,512]{2,1,0:T(8,128)(2,1)S(1)} collective-permute-done((bf16[3,256,512]{2,1,0:T(8,128)(2,1)S(1)}, bf16[3,256,512]{2,1,0:T(8,128)(2,1)S(1)}, u32[]{:S(2)}, u32[]{:S(2)}) %collective-permute-start.13) | collective-permute-done | bytes 786464 | tf_op jit(solution)/shard_map/ppermute | solution.py:621
  109.3 2.1 sum_step.8
  111.4 2.0 collective-permute-start.16
  113.4 12.7 %collective-permute-done.21.refs_7_ = bf16[3,256,512]{2,1,0:T(8,128)(2,1)S(1)} collective-permute-done((bf16[3,256,512]{2,1,0:T(8,128)(2,1)S(1)}, bf16[3,256,512]{2,1,0:T(8,128)(2,1)S(1)}, u32[]{:S(2)}, u32[]{:S(2)}) %collective-permute-start.21) | collective-permute-done | bytes 786464 | tf_op jit(solution)/shard_map/ppermute | solution.py:621
  126.2 2.1 sum_step.11
  128.3 2.0 collective-permute-start.24
  131.0 12.0 %collective-permute-done.15.from_left = bf16[3,256,512]{2,1,0:T(8,128)(2,1)S(1)} collective-permute-done((bf16[3,256,512]{2,1,0:T(8,128)(2,1)S(1)}, bf16[3,256,512]{2,1,0:T(8,128)(2,1)S(1)}, u32[]{:S(2)}, u32[]{:S(2)}) %collective-permute-start.15) | collective-permute-done | bytes 786464 | tf_op jit(solution)/shard_map/ppermute | solution.py:621
  143.0 7.2 %attention.2 = (bf16[256,512]{1,0:T(8,128)(2,1)S(1)}, f32[256,128]{1,0:T(8,128)S(1)}, bf16[3,256,512]{2,1,0:T(8,128)(2,1)S(1)}) custom-call(s32[39]{0:T(128)S(1)} %dynamic-slice_bitcast_fusion.idx.refs_0_, bf16[7,256,256]{2,1,0:T(8,128)(2,1)S(1)} %stack.1.refs_1_.refs_3_.mine, bf16[7,256,256]{2,1,0:T(8,128)(2,1)S(1)} %collective-permute-done.8.refs_2_.refs_4_.other, ...), custom_call_target="tpu_custom_call" | custom-call | flops 402653184 | bytes 3145728 | tf_op jit(solution)/shard_map/attention/pallas_call | solution.py:389
  151.0 2.0 collective-permute-start.27
  152.9 6.9 %collective-permute-done.23.from_left = bf16[3,256,512]{2,1,0:T(8,128)(2,1)S(1)} collective-permute-done((bf16[3,256,512]{2,1,0:T(8,128)(2,1)S(1)}, bf16[3,256,512]{2,1,0:T(8,128)(2,1)S(1)}, u32[]{:S(2)}, u32[]{:S(2)}) %collective-permute-start.23) | collective-permute-done | bytes 786464 | tf_op jit(solution)/shard_map/ppermute | solution.py:621
  159.9 7.3 %attention.3 = (bf16[256,512]{1,0:T(8,128)(2,1)S(1)}, f32[256,128]{1,0:T(8,128)S(1)}, bf16[3,256,512]{2,1,0:T(8,128)(2,1)S(1)}) custom-call(s32[39]{0:T(128)S(1)} %dynamic-slice_bitcast_fusion.idx.refs_0_, bf16[7,256,256]{2,1,0:T(8,128)(2,1)S(1)} %stack.1.refs_1_.refs_3_.mine, bf16[7,256,256]{2,1,0:T(8,128)(2,1)S(1)} %collective-permute-done.8.refs_2_.refs_4_.other, ...), custom_call_target="tpu_custom_call" | custom-call | flops 402653184 | bytes 3145728 | tf_op jit(solution)/shard_map/attention/pallas_call | solution.py:389
  168.6 2.0 collective-permute-start.35
  171.5 2.7 collective-permute-done.30.refs_2_.refs_3_
  174.2 2.5 collective-permute-start.31
  178.5 12.6 %collective-permute-done.38.refs_2_.refs_3_ = bf16[3,256,512]{2,1,0:T(8,128)(2,1)S(1)} collective-permute-done((bf16[3,256,512]{2,1,0:T(8,128)(2,1)S(1)}, bf16[3,256,512]{2,1,0:T(8,128)(2,1)S(1)}, u32[]{:S(2)}, u32[]{:S(2)}) %collective-permute-start.38) | collective-permute-done | bytes 786464 | tf_op jit(solution)/shard_map/ppermute | solution.py:621
  191.0 2.5 collective-permute-start.39
  195.3 12.6 %collective-permute-done.31.refs_1_.refs_5_ = bf16[3,256,512]{2,1,0:T(8,128)(2,1)} collective-permute-done((bf16[3,256,512]{2,1,0:T(8,128)(2,1)S(1)}, bf16[3,256,512]{2,1,0:T(8,128)(2,1)}, u32[]{:S(2)}, u32[]{:S(2)}) %collective-permute-start.31) | collective-permute-done | bytes 786464 | tf_op jit(solution)/shard_map/ppermute | solution.py:621
  207.9 2.6 collective-permute-start.32
  210.5 14.2 %collective-permute-done.39.refs_1_.refs_5_ = bf16[3,256,512]{2,1,0:T(8,128)(2,1)} collective-permute-done((bf16[3,256,512]{2,1,0:T(8,128)(2,1)S(1)}, bf16[3,256,512]{2,1,0:T(8,128)(2,1)}, u32[]{:S(2)}, u32[]{:S(2)}) %collective-permute-start.39) | collective-permute-done | bytes 786464 | tf_op jit(solution)/shard_map/ppermute | solution.py:621
  224.8 2.6 collective-permute-start.40
  230.2 1.6 collective-permute-done.25
  233.3 5.0 %collective-permute-done.26 = f32[256,1]{1,0:T(8,128)S(1)} collective-permute-done((f32[256,1]{1,0:T(8,128)S(1)}, f32[256,1]{1,0:T(8,128)S(1)}, u32[]{:S(2)}, u32[]{:S(2)}) %collective-permute-start.26) | collective-permute-done | bytes 1056 | tf_op jit(solution)/shard_map/ppermute | solution.py:624
  244.5 2.3 term_step.10
  250.5 2.3 term_step.11
  252.8 5.7 %collective-permute-done.40.refs_1_.refs_7_ = bf16[3,256,512]{2,1,0:T(8,128)(2,1)} collective-permute-done((bf16[3,256,512]{2,1,0:T(8,128)(2,1)}, bf16[3,256,512]{2,1,0:T(8,128)(2,1)}, u32[]{:S(2)}, u32[]{:S(2)}) %collective-permute-start.40) | collective-permute-done | bytes 786464 | tf_op jit(solution)/shard_map/ppermute | solution.py:621
  258.6 2.5 collective-permute-done.37.refs_0_.refs_6_
  262.6 2.0 collective-permute-start.42
  264.6 2.3 term_step.12
  266.9 2.3 term_step.13
  270.0 7.1 %collective-permute-done.41.refs_2_.refs_8_ = bf16[3,128,512]{2,1,0:T(8,128)(2,1)S(1)} collective-permute-done((bf16[3,128,512]{2,1,0:T(8,128)(2,1)S(1)}, bf16[3,128,512]{2,1,0:T(8,128)(2,1)S(1)}, u32[]{:S(2)}, u32[]{:S(2)}) %collective-permute-start.41) | collective-permute-done | bytes 393248 | tf_op jit(solution)/shard_map/ppermute | solution.py:621
  277.1 1.6 term_last.1
  282.6 1.6 collective-permute-start.48
  284.2 6.3 %grads.2.refs_10_ = f32[3,512,1024]{2,1,0:T(8,128)} custom-call(bf16[512,2048]{1,0:T(8,128)(2,1)S(1)} %copy-done.1, bf16[3,256,512]{2,1,0:T(8,128)(2,1)S(1)} %copy-done.13, bf16[3,256,512]{2,1,0:T(8,128)(2,1)S(1)} %copy-done.19, bf16[3,256,512]{2,1,0:T(8,128)(2,1)S(1)} %copy-done.16, bf16[3,256,512]{2,1,0:T(8,128)(2,1)} %collective-permute-done.28.refs_0_.refs_4_, ...), custom_call_target="tpu_custom_call" | custom-call | flops 3221225472 | bytes 9437184 | tf_op jit(solution)/shard_map/grads/pallas_call | solution.py:431
  291.2 2.4 collective-permute-start.46
  293.5 3.1 collective-permute-start.45
  297.3 3.1 collective-permute-start.50
  300.4 4.0 %collective-permute-start.49 = (bf16[128,512]{1,0:T(8,128)(2,1)S(1)}, bf16[128,512]{1,0:T(8,128)(2,1)S(1)}, u32[]{:S(2)}, u32[]{:S(2)}) collective-permute-start(bf16[128,512]{1,0:T(8,128)(2,1)S(1)} %get-tuple-element.131.refs_12_), channel_id=1, source_target_pairs={{0,0},{1,1},{2,8},{3,9},{4,16},{5,17},{6,24},{7,25},{8,2},{9,3},{1... | collective-permute-start | bytes 393224 | tf_op jit(solution)/shard_map/ppermute | solution.py:682
  304.4 6.3 %grads.3 = f32[3,512,1024]{2,1,0:T(8,128)} custom-call(bf16[512,2048]{1,0:T(8,128)(2,1)S(1)} %copy-done.1, bf16[3,256,512]{2,1,0:T(8,128)(2,1)S(1)} %copy-done.6, bf16[3,256,512]{2,1,0:T(8,128)(2,1)S(1)} %copy-done.10, bf16[3,256,512]{2,1,0:T(8,128)(2,1)S(1)} %copy-done.8, ...), custom_call_target="tpu_custom_call", output_to_operand_aliasing={{}: (10, {})} | custom-call | flops 3221225472 | bytes 9437184 | tf_op jit(solution)/shard_map/grads/pallas_call | solution.py:431
  311.7 3.9 %collective-permute-done.50.refs_3_ = bf16[128,512]{1,0:T(8,128)(2,1)S(1)} collective-permute-done((bf16[128,512]{1,0:T(8,128)(2,1)S(1)}, bf16[128,512]{1,0:T(8,128)(2,1)S(1)}, u32[]{:S(2)}, u32[]{:S(2)}) %collective-permute-start.50) | collective-permute-done | bytes 131104 | tf_op jit(solution)/shard_map/ppermute | solution.py:682
  317.1 1.6 finish.1
  (137 shorter events, 41.1 us)
Async XLA Ops:
  5.7 9.1 %collective-permute-start.6 = (bf16[256,256]{1,0:T(8,128)(2,1)S(1)}, bf16[256,256]{1,0:T(8,128)(2,1)S(1)}, u32[]{:S(2)}, u32[]{:S(2)}) collective-permute-start(bf16[256,256]{1,0:T(8,128)(2,1)S(1)} %get-tuple-element.75), channel_id=1, source_target_pairs={{0,7},{2,5},{4,3},{6,1},{7,0},{5,2},{3,4},{1,6},{8,15},{10,13},{12... | collective-permute-start | bytes 393224 | tf_op jit(solution)/shard_map/ppermute | solution.py:621
  10.3 9.7 %collective-permute-start = (bf16[256,256]{1,0:T(8,128)(2,1)S(1)}, bf16[256,256]{1,0:T(8,128)(2,1)S(1)}, u32[]{:S(2)}, u32[]{:S(2)}) collective-permute-start(bf16[256,256]{1,0:T(8,128)(2,1)S(1)} %get-tuple-element.69), channel_id=1, source_target_pairs={{0,2},{2,4},{4,6},{6,7},{7,5},{5,3},{3,1},{1,0},{8,10},{10,12},{12... | collective-permute-start | bytes 393224 | tf_op jit(solution)/shard_map/ppermute | solution.py:621
  14.8 6.9 %collective-permute-start.7 = (bf16[256,256]{1,0:T(8,128)(2,1)S(1)}, bf16[256,256]{1,0:T(8,128)(2,1)S(1)}, u32[]{:S(2)}, u32[]{:S(2)}) collective-permute-start(bf16[256,256]{1,0:T(8,128)(2,1)S(1)} %collective-permute-done.6.mine.mine_far), channel_id=1, source_target_pairs={{0,8},{8,0},{16,24},{24,16},{1,9},{9,1},{17,25},{25,17},{2,10},{10... | collective-permute-start | bytes 393224 | tf_op jit(solution)/shard_map/ppermute | solution.py:624
  14.8 14.6 %collective-permute-start.1 = (bf16[256,256]{1,0:T(8,128)(2,1)S(1)}, bf16[256,256]{1,0:T(8,128)(2,1)S(1)}, u32[]{:S(2)}, u32[]{:S(2)}) collective-permute-start(bf16[256,256]{1,0:T(8,128)(2,1)S(1)} %get-tuple-element.70), channel_id=1, source_target_pairs={{0,1},{2,0},{4,2},{6,4},{7,6},{5,7},{3,5},{1,3},{8,9},{10,8},{12,1... | collective-permute-start | bytes 393224 | tf_op jit(solution)/shard_map/ppermute | solution.py:621
  15.3 14.1 %collective-permute-start.2 = (bf16[256,256]{1,0:T(8,128)(2,1)S(1)}, bf16[256,256]{1,0:T(8,128)(2,1)S(1)}, u32[]{:S(2)}, u32[]{:S(2)}) collective-permute-start(bf16[256,256]{1,0:T(8,128)(2,1)S(1)} %get-tuple-element.71), channel_id=1, source_target_pairs={{0,4},{2,6},{4,7},{6,5},{7,3},{5,1},{3,0},{1,2},{8,12},{10,14},{12... | collective-permute-start | bytes 393224 | tf_op jit(solution)/shard_map/ppermute | solution.py:621
  18.7 15.3 %collective-permute-start.3 = (bf16[256,256]{1,0:T(8,128)(2,1)S(1)}, bf16[256,256]{1,0:T(8,128)(2,1)S(1)}, u32[]{:S(2)}, u32[]{:S(2)}) collective-permute-start(bf16[256,256]{1,0:T(8,128)(2,1)S(1)} %get-tuple-element.72), channel_id=1, source_target_pairs={{0,3},{2,1},{4,0},{6,2},{7,4},{5,6},{3,7},{1,5},{8,11},{10,9},{12,... | collective-permute-start | bytes 393224 | tf_op jit(solution)/shard_map/ppermute | solution.py:621
  19.9 15.2 %collective-permute-start.4 = (bf16[256,256]{1,0:T(8,128)(2,1)S(1)}, bf16[256,256]{1,0:T(8,128)(2,1)S(1)}, u32[]{:S(2)}, u32[]{:S(2)}) collective-permute-start(bf16[256,256]{1,0:T(8,128)(2,1)S(1)} %get-tuple-element.73), channel_id=1, source_target_pairs={{0,6},{2,7},{4,5},{6,3},{7,1},{5,0},{3,2},{1,4},{8,14},{10,15},{12... | collective-permute-start | bytes 393224 | tf_op jit(solution)/shard_map/ppermute | solution.py:621
  21.7 13.4 %collective-permute-start.5 = (bf16[256,256]{1,0:T(8,128)(2,1)S(1)}, bf16[256,256]{1,0:T(8,128)(2,1)S(1)}, u32[]{:S(2)}, u32[]{:S(2)}) collective-permute-start(bf16[256,256]{1,0:T(8,128)(2,1)S(1)} %get-tuple-element.74), channel_id=1, source_target_pairs={{0,5},{2,3},{4,1},{6,0},{7,2},{5,4},{3,6},{1,7},{8,13},{10,11},{12... | collective-permute-start | bytes 393224 | tf_op jit(solution)/shard_map/ppermute | solution.py:621
  35.2 15.1 %collective-permute-start.8 = (bf16[7,256,256]{2,1,0:T(8,128)(2,1)S(1)}, bf16[7,256,256]{2,1,0:T(8,128)(2,1)S(1)}, u32[]{:S(2)}, u32[]{:S(2)}) collective-permute-start(bf16[7,256,256]{2,1,0:T(8,128)(2,1)S(1)} %stack.1.refs_1_.refs_3_.mine), channel_id=1, source_target_pairs={{0,8},{8,0},{16,24},{24,16},{1,9},{9,1},{17,25},{25,17},{2,10},{10... | collective-permute-start | bytes 2752520 | tf_op jit(solution)/shard_map/ppermute | solution.py:624
  35.2 12.5 %collective-permute-start.10 = (bf16[3,128,512]{2,1,0:T(8,128)(2,1)S(1)}, bf16[3,128,512]{2,1,0:T(8,128)(2,1)S(1)}, u32[]{:S(2)}, u32[]{:S(2)}) collective-permute-start(bf16[3,128,512]{2,1,0:T(8,128)(2,1)S(1)} %get-tuple-element.78), channel_id=1, source_target_pairs={{0,1},{2,0},{4,2},{6,4},{7,6},{5,7},{3,5},{1,3},{8,9},{10,8},{12,1... | collective-permute-start | bytes 1179656 | tf_op jit(solution)/shard_map/ppermute | solution.py:621
  38.4 12.0 %collective-permute-start.9 = (bf16[3,128,512]{2,1,0:T(8,128)(2,1)S(1)}, bf16[3,128,512]{2,1,0:T(8,128)(2,1)S(1)}, u32[]{:S(2)}, u32[]{:S(2)}) collective-permute-start(bf16[3,128,512]{2,1,0:T(8,128)(2,1)S(1)} %get-tuple-element.77.refs_7_), channel_id=1, source_target_pairs={{0,2},{2,4},{4,6},{6,7},{7,5},{5,3},{3,1},{1,0},{8,10},{10,12},{12... | collective-permute-start | bytes 1179656 | tf_op jit(solution)/shard_map/ppermute | solution.py:621
  38.4 20.4 %collective-permute-start.17 = (bf16[3,128,512]{2,1,0:T(8,128)(2,1)S(1)}, bf16[3,128,512]{2,1,0:T(8,128)(2,1)S(1)}, u32[]{:S(2)}, u32[]{:S(2)}) collective-permute-start(bf16[3,128,512]{2,1,0:T(8,128)(2,1)S(1)} %get-tuple-element.86), channel_id=1, source_target_pairs={{0,2},{2,4},{4,6},{6,7},{7,5},{5,3},{3,1},{1,0},{8,10},{10,12},{12... | collective-permute-start | bytes 1179656 | tf_op jit(solution)/shard_map/ppermute | solution.py:621
  38.4 20.4 %collective-permute-start.18 = (bf16[3,128,512]{2,1,0:T(8,128)(2,1)S(1)}, bf16[3,128,512]{2,1,0:T(8,128)(2,1)S(1)}, u32[]{:S(2)}, u32[]{:S(2)}) collective-permute-start(bf16[3,128,512]{2,1,0:T(8,128)(2,1)S(1)} %get-tuple-element.87), channel_id=1, source_target_pairs={{0,1},{2,0},{4,2},{6,4},{7,6},{5,7},{3,5},{1,3},{8,9},{10,8},{12,1... | collective-permute-start | bytes 1179656 | tf_op jit(solution)/shard_map/ppermute | solution.py:621
  52.4 23.2 %collective-permute-start.11 = (bf16[3,256,512]{2,1,0:T(8,128)(2,1)S(1)}, bf16[3,256,512]{2,1,0:T(8,128)(2,1)S(1)}, u32[]{:S(2)}, u32[]{:S(2)}) collective-permute-start(bf16[3,256,512]{2,1,0:T(8,128)(2,1)S(1)} %get-tuple-element.79), channel_id=1, source_target_pairs={{0,2},{2,4},{4,6},{6,7},{7,5},{5,3},{3,1},{1,0},{8,10},{10,12},{12... | collective-permute-start | bytes 2359304 | tf_op jit(solution)/shard_map/ppermute | solution.py:621
  52.4 23.1 %collective-permute-start.12 = (bf16[3,256,512]{2,1,0:T(8,128)(2,1)S(1)}, bf16[3,256,512]{2,1,0:T(8,128)(2,1)S(1)}, u32[]{:S(2)}, u32[]{:S(2)}) collective-permute-start(bf16[3,256,512]{2,1,0:T(8,128)(2,1)S(1)} %get-tuple-element.80), channel_id=1, source_target_pairs={{0,1},{2,0},{4,2},{6,4},{7,6},{5,7},{3,5},{1,3},{8,9},{10,8},{12,1... | collective-permute-start | bytes 2359304 | tf_op jit(solution)/shard_map/ppermute | solution.py:621
  60.8 31.6 %collective-permute-start.19 = (bf16[3,256,512]{2,1,0:T(8,128)(2,1)S(1)}, bf16[3,256,512]{2,1,0:T(8,128)(2,1)S(1)}, u32[]{:S(2)}, u32[]{:S(2)}) collective-permute-start(bf16[3,256,512]{2,1,0:T(8,128)(2,1)S(1)} %get-tuple-element.88), channel_id=1, source_target_pairs={{0,2},{2,4},{4,6},{6,7},{7,5},{5,3},{3,1},{1,0},{8,10},{10,12},{12... | collective-permute-start | bytes 2359304 | tf_op jit(solution)/shard_map/ppermute | solution.py:621
  60.9 31.6 %collective-permute-start.20 = (bf16[3,256,512]{2,1,0:T(8,128)(2,1)S(1)}, bf16[3,256,512]{2,1,0:T(8,128)(2,1)S(1)}, u32[]{:S(2)}, u32[]{:S(2)}) collective-permute-start(bf16[3,256,512]{2,1,0:T(8,128)(2,1)S(1)} %get-tuple-element.89), channel_id=1, source_target_pairs={{0,1},{2,0},{4,2},{6,4},{7,6},{5,7},{3,5},{1,3},{8,9},{10,8},{12,1... | collective-permute-start | bytes 2359304 | tf_op jit(solution)/shard_map/ppermute | solution.py:621
  77.7 31.6 %collective-permute-start.13 = (bf16[3,256,512]{2,1,0:T(8,128)(2,1)S(1)}, bf16[3,256,512]{2,1,0:T(8,128)(2,1)S(1)}, u32[]{:S(2)}, u32[]{:S(2)}) collective-permute-start(bf16[3,256,512]{2,1,0:T(8,128)(2,1)S(1)} %get-tuple-element.81), channel_id=1, source_target_pairs={{0,2},{2,4},{4,6},{6,7},{7,5},{5,3},{3,1},{1,0},{8,10},{10,12},{12... | collective-permute-start | bytes 2359304 | tf_op jit(solution)/shard_map/ppermute | solution.py:621
  77.7 31.6 %collective-permute-start.14 = (bf16[3,256,512]{2,1,0:T(8,128)(2,1)S(1)}, bf16[3,256,512]{2,1,0:T(8,128)(2,1)S(1)}, u32[]{:S(2)}, u32[]{:S(2)}) collective-permute-start(bf16[3,256,512]{2,1,0:T(8,128)(2,1)S(1)} %get-tuple-element.82), channel_id=1, source_target_pairs={{0,1},{2,0},{4,2},{6,4},{7,6},{5,7},{3,5},{1,3},{8,9},{10,8},{12,1... | collective-permute-start | bytes 2359304 | tf_op jit(solution)/shard_map/ppermute | solution.py:621
  94.5 31.6 %collective-permute-start.21 = (bf16[3,256,512]{2,1,0:T(8,128)(2,1)S(1)}, bf16[3,256,512]{2,1,0:T(8,128)(2,1)S(1)}, u32[]{:S(2)}, u32[]{:S(2)}) collective-permute-start(bf16[3,256,512]{2,1,0:T(8,128)(2,1)S(1)} %get-tuple-element.90), channel_id=1, source_target_pairs={{0,2},{2,4},{4,6},{6,7},{7,5},{5,3},{3,1},{1,0},{8,10},{10,12},{12... | collective-permute-start | bytes 2359304 | tf_op jit(solution)/shard_map/ppermute | solution.py:621
  94.6 31.6 %collective-permute-start.22 = (bf16[3,256,512]{2,1,0:T(8,128)(2,1)S(1)}, bf16[3,256,512]{2,1,0:T(8,128)(2,1)S(1)}, u32[]{:S(2)}, u32[]{:S(2)}) collective-permute-start(bf16[3,256,512]{2,1,0:T(8,128)(2,1)S(1)} %get-tuple-element.91), channel_id=1, source_target_pairs={{0,1},{2,0},{4,2},{6,4},{7,6},{5,7},{3,5},{1,3},{8,9},{10,8},{12,1... | collective-permute-start | bytes 2359304 | tf_op jit(solution)/shard_map/ppermute | solution.py:621
  97.8 28.4 %copy-start = (bf16[512,2048]{1,0:T(8,128)(2,1)}, bf16[512,2048]{1,0:T(8,128)(2,1)S(1)}, u32[]{:S(2)}) copy-start(bf16[512,2048]{1,0:T(8,128)(2,1)S(1)} %turn.1.refs_9_.refs_0_) | copy-start | bytes 6291460
  111.4 31.6 %collective-permute-start.15 = (bf16[3,256,512]{2,1,0:T(8,128)(2,1)S(1)}, bf16[3,256,512]{2,1,0:T(8,128)(2,1)S(1)}, u32[]{:S(2)}, u32[]{:S(2)}) collective-permute-start(bf16[3,256,512]{2,1,0:T(8,128)(2,1)S(1)} %get-tuple-element.83), channel_id=1, source_target_pairs={{0,2},{2,4},{4,6},{6,7},{7,5},{5,3},{3,1},{1,0},{8,10},{10,12},{12... | collective-permute-start | bytes 2359304 | tf_op jit(solution)/shard_map/ppermute | solution.py:621
  111.4 31.6 %copy-start.20 = (bf16[256,1024]{1,0:T(8,128)(2,1)S(1)}, bf16[256,1024]{1,0:T(8,128)(2,1)}, u32[]{:S(2)}) copy-start(bf16[256,1024]{1,0:T(8,128)(2,1)} %d_out.3) | copy-start | bytes 1572868
  111.4 31.6 %collective-permute-start.16 = (bf16[3,256,512]{2,1,0:T(8,128)(2,1)S(1)}, bf16[3,256,512]{2,1,0:T(8,128)(2,1)S(1)}, u32[]{:S(2)}, u32[]{:S(2)}) collective-permute-start(bf16[3,256,512]{2,1,0:T(8,128)(2,1)S(1)} %get-tuple-element.84), channel_id=1, source_target_pairs={{0,1},{2,0},{4,2},{6,4},{7,6},{5,7},{3,5},{1,3},{8,9},{10,8},{12,1... | collective-permute-start | bytes 2359304 | tf_op jit(solution)/shard_map/ppermute | solution.py:621
  128.2 31.6 %collective-permute-start.23 = (bf16[3,256,512]{2,1,0:T(8,128)(2,1)S(1)}, bf16[3,256,512]{2,1,0:T(8,128)(2,1)S(1)}, u32[]{:S(2)}, u32[]{:S(2)}) collective-permute-start(bf16[3,256,512]{2,1,0:T(8,128)(2,1)S(1)} %get-tuple-element.92), channel_id=1, source_target_pairs={{0,2},{2,4},{4,6},{6,7},{7,5},{5,3},{3,1},{1,0},{8,10},{10,12},{12... | collective-permute-start | bytes 2359304 | tf_op jit(solution)/shard_map/ppermute | solution.py:621
  128.3 31.6 %collective-permute-start.24 = (bf16[3,256,512]{2,1,0:T(8,128)(2,1)S(1)}, bf16[3,256,512]{2,1,0:T(8,128)(2,1)S(1)}, u32[]{:S(2)}, u32[]{:S(2)}) collective-permute-start(bf16[3,256,512]{2,1,0:T(8,128)(2,1)S(1)} %get-tuple-element.93), channel_id=1, source_target_pairs={{0,1},{2,0},{4,2},{6,4},{7,6},{5,7},{3,5},{1,3},{8,9},{10,8},{12,1... | collective-permute-start | bytes 2359304 | tf_op jit(solution)/shard_map/ppermute | solution.py:621
  150.9 16.2 %copy-start.11 = (bf16[3,256,512]{2,1,0:T(8,128)(2,1)}, bf16[3,256,512]{2,1,0:T(8,128)(2,1)S(1)}, u32[]{:S(2)}) copy-start(bf16[3,256,512]{2,1,0:T(8,128)(2,1)S(1)} %get-tuple-element.99.refs_0_.refs_1_) | copy-start | bytes 2359300
  150.9 23.3 %collective-permute-start.30 = (bf16[3,256,512]{2,1,0:T(8,128)(2,1)S(1)}, bf16[3,256,512]{2,1,0:T(8,128)(2,1)S(1)}, u32[]{:S(2)}, u32[]{:S(2)}) collective-permute-start(bf16[3,256,512]{2,1,0:T(8,128)(2,1)S(1)} %get-tuple-element.99.refs_0_.refs_1_), channel_id=1, source_target_pairs={{0,1},{2,0},{4,2},{6,4},{7,6},{5,7},{3,5},{1,3},{8,9},{10,8},{12,1... | collective-permute-start | bytes 2359304 | tf_op jit(solution)/shard_map/ppermute | solution.py:621
  151.0 26.6 %collective-permute-start.27 = (bf16[3,256,512]{2,1,0:T(8,128)(2,1)S(1)}, bf16[3,256,512]{2,1,0:T(8,128)(2,1)S(1)}, u32[]{:S(2)}, u32[]{:S(2)}) collective-permute-start(bf16[3,256,512]{2,1,0:T(8,128)(2,1)S(1)} %get-tuple-element.99.refs_0_.refs_1_), channel_id=1, source_target_pairs={{0,2},{2,4},{4,6},{6,7},{7,5},{5,3},{3,1},{1,0},{8,10},{10,12},{12... | collective-permute-start | bytes 2359304 | tf_op jit(solution)/shard_map/ppermute | solution.py:621
  168.5 22.5 %collective-permute-start.38 = (bf16[3,256,512]{2,1,0:T(8,128)(2,1)S(1)}, bf16[3,256,512]{2,1,0:T(8,128)(2,1)S(1)}, u32[]{:S(2)}, u32[]{:S(2)}) collective-permute-start(bf16[3,256,512]{2,1,0:T(8,128)(2,1)S(1)} %get-tuple-element.104.refs_0_.refs_1_), channel_id=1, source_target_pairs={{0,1},{2,0},{4,2},{6,4},{7,6},{5,7},{3,5},{1,3},{8,9},{10,8},{12,1... | collective-permute-start | bytes 2359304 | tf_op jit(solution)/shard_map/ppermute | solution.py:621
  168.6 25.9 %collective-permute-start.35 = (bf16[3,256,512]{2,1,0:T(8,128)(2,1)S(1)}, bf16[3,256,512]{2,1,0:T(8,128)(2,1)S(1)}, u32[]{:S(2)}, u32[]{:S(2)}) collective-permute-start(bf16[3,256,512]{2,1,0:T(8,128)(2,1)S(1)} %get-tuple-element.104.refs_0_.refs_1_), channel_id=1, source_target_pairs={{0,2},{2,4},{4,6},{6,7},{7,5},{5,3},{3,1},{1,0},{8,10},{10,12},{12... | collective-permute-start | bytes 2359304 | tf_op jit(solution)/shard_map/ppermute | solution.py:621
  174.2 33.7 %collective-permute-start.31 = (bf16[3,256,512]{2,1,0:T(8,128)(2,1)S(1)}, bf16[3,256,512]{2,1,0:T(8,128)(2,1)}, u32[]{:S(2)}, u32[]{:S(2)}) collective-permute-start(bf16[3,256,512]{2,1,0:T(8,128)(2,1)S(1)} %collective-permute-done.30.refs_2_.refs_3_), channel_id=1, source_target_pairs={{0,1},{2,0},{4,2},{6,4},{7,6},{5,7},{3,5},{1,3},{8,9},{10,8},{12,1... | collective-permute-start | bytes 2359304 | tf_op jit(solution)/shard_map/ppermute | solution.py:621
  177.6 32.9 %collective-permute-start.28 = (bf16[3,256,512]{2,1,0:T(8,128)(2,1)S(1)}, bf16[3,256,512]{2,1,0:T(8,128)(2,1)}, u32[]{:S(2)}, u32[]{:S(2)}) collective-permute-start(bf16[3,256,512]{2,1,0:T(8,128)(2,1)S(1)} %collective-permute-done.27.refs_1_.refs_2_), channel_id=1, source_target_pairs={{0,2},{2,4},{4,6},{6,7},{7,5},{5,3},{3,1},{1,0},{8,10},{10,12},{12... | collective-permute-start | bytes 2359304 | tf_op jit(solution)/shard_map/ppermute | solution.py:621
  191.0 33.7 %collective-permute-start.39 = (bf16[3,256,512]{2,1,0:T(8,128)(2,1)S(1)}, bf16[3,256,512]{2,1,0:T(8,128)(2,1)}, u32[]{:S(2)}, u32[]{:S(2)}) collective-permute-start(bf16[3,256,512]{2,1,0:T(8,128)(2,1)S(1)} %collective-permute-done.38.refs_2_.refs_3_), channel_id=1, source_target_pairs={{0,1},{2,0},{4,2},{6,4},{7,6},{5,7},{3,5},{1,3},{8,9},{10,8},{12,1... | collective-permute-start | bytes 2359304 | tf_op jit(solution)/shard_map/ppermute | solution.py:621
  194.4 33.0 %collective-permute-start.36 = (bf16[3,256,512]{2,1,0:T(8,128)(2,1)S(1)}, bf16[3,256,512]{2,1,0:T(8,128)(2,1)}, u32[]{:S(2)}, u32[]{:S(2)}) collective-permute-start(bf16[3,256,512]{2,1,0:T(8,128)(2,1)S(1)} %collective-permute-done.35.refs_1_.refs_2_), channel_id=1, source_target_pairs={{0,2},{2,4},{4,6},{6,7},{7,5},{5,3},{3,1},{1,0},{8,10},{10,12},{12... | collective-permute-start | bytes 2359304 | tf_op jit(solution)/shard_map/ppermute | solution.py:621
  207.9 39.0 %collective-permute-start.32 = (bf16[3,256,512]{2,1,0:T(8,128)(2,1)}, bf16[3,256,512]{2,1,0:T(8,128)(2,1)}, u32[]{:S(2)}, u32[]{:S(2)}) collective-permute-start(bf16[3,256,512]{2,1,0:T(8,128)(2,1)} %collective-permute-done.31.refs_1_.refs_5_), channel_id=1, source_target_pairs={{0,1},{2,0},{4,2},{6,4},{7,6},{5,7},{3,5},{1,3},{8,9},{10,8},{12,1... | collective-permute-start | bytes 2359304 | tf_op jit(solution)/shard_map/ppermute | solution.py:621
  210.5 36.4 %collective-permute-start.29 = (bf16[3,256,512]{2,1,0:T(8,128)(2,1)}, bf16[3,256,512]{2,1,0:T(8,128)(2,1)}, u32[]{:S(2)}, u32[]{:S(2)}) collective-permute-start(bf16[3,256,512]{2,1,0:T(8,128)(2,1)} %collective-permute-done.28.refs_0_.refs_4_), channel_id=1, source_target_pairs={{0,2},{2,4},{4,6},{6,7},{7,5},{5,3},{3,1},{1,0},{8,10},{10,12},{12... | collective-permute-start | bytes 2359304 | tf_op jit(solution)/shard_map/ppermute | solution.py:621
  224.8 33.8 %collective-permute-start.40 = (bf16[3,256,512]{2,1,0:T(8,128)(2,1)}, bf16[3,256,512]{2,1,0:T(8,128)(2,1)}, u32[]{:S(2)}, u32[]{:S(2)}) collective-permute-start(bf16[3,256,512]{2,1,0:T(8,128)(2,1)} %collective-permute-done.39.refs_1_.refs_5_), channel_id=1, source_target_pairs={{0,1},{2,0},{4,2},{6,4},{7,6},{5,7},{3,5},{1,3},{8,9},{10,8},{12,1... | collective-permute-start | bytes 2359304 | tf_op jit(solution)/shard_map/ppermute | solution.py:621
  227.4 33.7 %collective-permute-start.37 = (bf16[3,256,512]{2,1,0:T(8,128)(2,1)}, bf16[3,256,512]{2,1,0:T(8,128)(2,1)}, u32[]{:S(2)}, u32[]{:S(2)}) collective-permute-start(bf16[3,256,512]{2,1,0:T(8,128)(2,1)} %collective-permute-done.36.refs_0_.refs_4_), channel_id=1, source_target_pairs={{0,2},{2,4},{4,6},{6,7},{7,5},{5,3},{3,1},{1,0},{8,10},{10,12},{12... | collective-permute-start | bytes 2359304 | tf_op jit(solution)/shard_map/ppermute | solution.py:621
  230.2 12.9 %copy-start.6 = (bf16[3,256,512]{2,1,0:T(8,128)(2,1)S(1)}, bf16[3,256,512]{2,1,0:T(8,128)(2,1)}, u32[]{:S(2)}) copy-start(bf16[3,256,512]{2,1,0:T(8,128)(2,1)} %copy-done.5) | copy-start | bytes 2359300
  230.2 12.9 %copy-start.8 = (bf16[3,256,512]{2,1,0:T(8,128)(2,1)S(1)}, bf16[3,256,512]{2,1,0:T(8,128)(2,1)}, u32[]{:S(2)}) copy-start(bf16[3,256,512]{2,1,0:T(8,128)(2,1)} %copy-done.7) | copy-start | bytes 2359300
  230.2 12.9 %copy-start.10 = (bf16[3,256,512]{2,1,0:T(8,128)(2,1)S(1)}, bf16[3,256,512]{2,1,0:T(8,128)(2,1)}, u32[]{:S(2)}) copy-start(bf16[3,256,512]{2,1,0:T(8,128)(2,1)} %copy-done.9) | copy-start | bytes 2359300
  230.2 1.6 collective-permute-start.25
  232.7 5.6 %collective-permute-start.26 = (f32[256,1]{1,0:T(8,128)S(1)}, f32[256,1]{1,0:T(8,128)S(1)}, u32[]{:S(2)}, u32[]{:S(2)}) collective-permute-start(f32[256,1]{1,0:T(8,128)S(1)} %add.31), channel_id=1, source_target_pairs={{0,16},{8,24},{16,0},{24,8},{1,17},{9,25},{17,1},{25,9},{2,18},{10... | collective-permute-start | bytes 3080 | tf_op jit(solution)/shard_map/ppermute | solution.py:624
  248.3 21.1 %collective-permute-start.33 = (bf16[3,128,512]{2,1,0:T(8,128)(2,1)S(1)}, bf16[3,128,512]{2,1,0:T(8,128)(2,1)S(1)}, u32[]{:S(2)}, u32[]{:S(2)}) collective-permute-start(bf16[3,128,512]{2,1,0:T(8,128)(2,1)S(1)} %get-tuple-element.100), channel_id=1, source_target_pairs={{0,2},{2,4},{4,6},{6,7},{7,5},{5,3},{3,1},{1,0},{8,10},{10,12},{12... | collective-permute-start | bytes 1179656 | tf_op jit(solution)/shard_map/ppermute | solution.py:621
  249.6 19.8 %collective-permute-start.34 = (bf16[3,128,512]{2,1,0:T(8,128)(2,1)S(1)}, bf16[3,128,512]{2,1,0:T(8,128)(2,1)S(1)}, u32[]{:S(2)}, u32[]{:S(2)}) collective-permute-start(bf16[3,128,512]{2,1,0:T(8,128)(2,1)S(1)} %get-tuple-element.101), channel_id=1, source_target_pairs={{0,1},{2,0},{4,2},{6,4},{7,6},{5,7},{3,5},{1,3},{8,9},{10,8},{12,1... | collective-permute-start | bytes 1179656 | tf_op jit(solution)/shard_map/ppermute | solution.py:621
  262.5 14.5 %collective-permute-start.41 = (bf16[3,128,512]{2,1,0:T(8,128)(2,1)S(1)}, bf16[3,128,512]{2,1,0:T(8,128)(2,1)S(1)}, u32[]{:S(2)}, u32[]{:S(2)}) collective-permute-start(bf16[3,128,512]{2,1,0:T(8,128)(2,1)S(1)} %get-tuple-element.115), channel_id=1, source_target_pairs={{0,2},{2,4},{4,6},{6,7},{7,5},{5,3},{3,1},{1,0},{8,10},{10,12},{12... | collective-permute-start | bytes 1179656 | tf_op jit(solution)/shard_map/ppermute | solution.py:621
  262.6 14.5 %collective-permute-start.42 = (bf16[3,128,512]{2,1,0:T(8,128)(2,1)S(1)}, bf16[3,128,512]{2,1,0:T(8,128)(2,1)S(1)}, u32[]{:S(2)}, u32[]{:S(2)}) collective-permute-start(bf16[3,128,512]{2,1,0:T(8,128)(2,1)S(1)} %get-tuple-element.116), channel_id=1, source_target_pairs={{0,1},{2,0},{4,2},{6,4},{7,6},{5,7},{3,5},{1,3},{8,9},{10,8},{12,1... | collective-permute-start | bytes 1179656 | tf_op jit(solution)/shard_map/ppermute | solution.py:621
  277.1 2.3 copy-start.22
  277.1 7.1 %copy-start.19 = (bf16[3,256,512]{2,1,0:T(8,128)(2,1)S(1)}, bf16[3,256,512]{2,1,0:T(8,128)(2,1)}, u32[]{:S(2)}) copy-start(bf16[3,256,512]{2,1,0:T(8,128)(2,1)} %copy-done.17) | copy-start | bytes 2359300
  278.7 5.4 %copy-start.1 = (bf16[512,2048]{1,0:T(8,128)(2,1)S(1)}, bf16[512,2048]{1,0:T(8,128)(2,1)}, u32[]{:S(2)}) copy-start(bf16[512,2048]{1,0:T(8,128)(2,1)} %copy-done) | copy-start | bytes 6291460
  278.7 5.4 %copy-start.13 = (bf16[3,256,512]{2,1,0:T(8,128)(2,1)S(1)}, bf16[3,256,512]{2,1,0:T(8,128)(2,1)}, u32[]{:S(2)}) copy-start(bf16[3,256,512]{2,1,0:T(8,128)(2,1)} %copy-done.11) | copy-start | bytes 2359300
  278.7 5.4 %copy-start.16 = (bf16[3,256,512]{2,1,0:T(8,128)(2,1)S(1)}, bf16[3,256,512]{2,1,0:T(8,128)(2,1)}, u32[]{:S(2)}) copy-start(bf16[3,256,512]{2,1,0:T(8,128)(2,1)} %copy-done.14) | copy-start | bytes 2359300
  278.7 2.0 collective-permute-start.43
  278.8 3.1 collective-permute-start.47
  281.4 9.2 %collective-permute-start.44 = (bf16[2,128,512]{2,1,0:T(8,128)(2,1)S(1)}, bf16[2,128,512]{2,1,0:T(8,128)(2,1)S(1)}, u32[]{:S(2)}, u32[]{:S(2)}) collective-permute-start(bf16[2,128,512]{2,1,0:T(8,128)(2,1)S(1)} %get-tuple-element.124), channel_id=1, source_target_pairs={{0,16},{8,24},{16,0},{24,8},{1,17},{9,25},{17,1},{25,9},{2,18},{10... | collective-permute-start | bytes 786440 | tf_op jit(solution)/shard_map/ppermute | solution.py:624
  282.6 14.1 %collective-permute-start.48 = (bf16[2,128,512]{2,1,0:T(8,128)(2,1)S(1)}, bf16[2,128,512]{2,1,0:T(8,128)(2,1)S(1)}, u32[]{:S(2)}, u32[]{:S(2)}) collective-permute-start(bf16[2,128,512]{2,1,0:T(8,128)(2,1)S(1)} %get-tuple-element.130), channel_id=1, source_target_pairs={{0,16},{8,24},{16,0},{24,8},{1,17},{9,25},{17,1},{25,9},{2,18},{10... | collective-permute-start | bytes 786440 | tf_op jit(solution)/shard_map/ppermute | solution.py:624
  291.2 19.5 %collective-permute-start.46 = (bf16[128,512]{1,0:T(8,128)(2,1)S(1)}, bf16[128,512]{1,0:T(8,128)(2,1)S(1)}, u32[]{:S(2)}, u32[]{:S(2)}) collective-permute-start(bf16[128,512]{1,0:T(8,128)(2,1)S(1)} %get-tuple-element.126), channel_id=1, source_target_pairs={{0,1},{1,0},{2,9},{3,8},{4,17},{5,16},{6,25},{7,24},{8,3},{9,2},{1... | collective-permute-start | bytes 393224 | tf_op jit(solution)/shard_map/ppermute | solution.py:682
  293.5 18.2 %collective-permute-start.45 = (bf16[128,512]{1,0:T(8,128)(2,1)S(1)}, bf16[128,512]{1,0:T(8,128)(2,1)S(1)}, u32[]{:S(2)}, u32[]{:S(2)}) collective-permute-start(bf16[128,512]{1,0:T(8,128)(2,1)S(1)} %get-tuple-element.125.refs_11_), channel_id=1, source_target_pairs={{0,0},{1,1},{2,8},{3,9},{4,16},{5,17},{6,24},{7,25},{8,2},{9,3},{1... | collective-permute-start | bytes 393224 | tf_op jit(solution)/shard_map/ppermute | solution.py:682
  297.3 18.4 %collective-permute-start.50 = (bf16[128,512]{1,0:T(8,128)(2,1)S(1)}, bf16[128,512]{1,0:T(8,128)(2,1)S(1)}, u32[]{:S(2)}, u32[]{:S(2)}) collective-permute-start(bf16[128,512]{1,0:T(8,128)(2,1)S(1)} %get-tuple-element.132), channel_id=1, source_target_pairs={{0,1},{1,0},{2,9},{3,8},{4,17},{5,16},{6,25},{7,24},{8,3},{9,2},{1... | collective-permute-start | bytes 393224 | tf_op jit(solution)/shard_map/ppermute | solution.py:682
  300.4 16.6 %copy-start.3 = (bf16[256,4096]{1,0:T(8,128)(2,1)S(1)}, bf16[256,4096]{1,0:T(8,128)(2,1)}, u32[]{:S(2)}) copy-start(bf16[256,4096]{1,0:T(8,128)(2,1)} %tokens.3) | copy-start | bytes 6291460
  300.4 16.6 %copy-start.24 = (f32[256,128]{1,0:T(8,128)S(1)}, f32[256,128]{1,0:T(8,128)}, u32[]{:S(2)}) copy-start(f32[256,128]{1,0:T(8,128)} %copy-done.23) | copy-start | bytes 393220
  300.4 16.6 %collective-permute-start.49 = (bf16[128,512]{1,0:T(8,128)(2,1)S(1)}, bf16[128,512]{1,0:T(8,128)(2,1)S(1)}, u32[]{:S(2)}, u32[]{:S(2)}) collective-permute-start(bf16[128,512]{1,0:T(8,128)(2,1)S(1)} %get-tuple-element.131.refs_12_), channel_id=1, source_target_pairs={{0,0},{1,1},{2,8},{3,9},{4,16},{5,17},{6,24},{7,25},{8,2},{9,3},{1... | collective-permute-start | bytes 393224 | tf_op jit(solution)/shard_map/ppermute | solution.py:682
  (15 other events, 14.8 us)

commit v12 on v10

--- a/solution.py
+++ b/solution.py
@@ -693,7 +693,8 @@
         for chunk in range(2):
             right, left = moving[chunk]
             if step == far:
-                right, left = halve(right, left, [] if chunk else [dots])
+                early = [dots] if chunk == 0 else terms[1][: size - 3]
+                right, left = halve(right, left, early)
             right, left = shift(right, 1), shift(left, -1)
             moving[chunk] = right, left
             gathered[chunk] += [right, left]
@@ -711,9 +712,9 @@
     d_tokens = finish(
         idx, column, tokens, norm_gain[None], inverse_rms, dots, came, width // nodes
     )
+    grads = grads_chunk(rows_turned, gathered[0], None, [keep_1], 0, wide, columns)
     sums = [first[0], second[0]]
-    grads = grads_chunk(rows_turned, gathered[0], None, sums, 0, wide, columns)
-    grads = grads_chunk(rows_turned, gathered[1], grads, [], 1, wide, columns)
+    grads = grads_chunk(rows_turned, gathered[1], grads, sums, 1, wide, columns)
     return (jnp.concatenate(outputs, axis=-1), d_tokens, grads)
 
 

time: 323 us -> 316 us (0.978)
  the two profiles are of different devices: /device:TPU:24 before, /device:TPU:2 now
where the time goes in v12:
time: 316 us; the launch traced here: 310 us
  waiting for transfers between devices  159 us (50%)
  Pallas kernels  66.2 us (21%)
  starting transfers between devices  61.9 us (20%)
  local copies, waits for them, and re-layouts  17.1 us (5%)
  other arithmetic  4.53 us (1%)
    ppermute x39, waiting for transfers between devices, shift(): return lax.ppermute(array, 'local', moves)  151 us
    ppermute x39, starting transfers between devices, shift(): return lax.ppermute(array, 'local', moves)  49.5 us
    unnamed x56, local copies, waits for them, and re-layouts  14.9 us
    pallas_call x2, Pallas kernels, attention(): pl.pallas_call(attention_kernel, grid_spec=pltpu.PrefetchScalarGridSpec(n...  14.5 us
    pallas_call x7, Pallas kernels, term_step(): pl.pallas_call(kernel, in_specs=[whole] * (1 + count + len(befores)), out...  12.7 us
    pallas_call x2, Pallas kernels, grads_chunk(): pl.pallas_call(tied(grads_kernel, 1 + len(pieces), len(ties)), grid=(3,),...  12.5 us
    pallas_call x6, Pallas kernels, sum_step(): pl.pallas_call(tied(sum_step_kernel, 9, len(ties)), grid_spec=pltpu.Prefe...  12.3 us
    ppermute x4, starting transfers between devices, relocate(): came.append(lax.ppermute(block, ('node', 'local'), moves))  9.02 us
  transfers between devices with their start and end apart: 51, of which 25 were waited for; matrix products, arithmetic and copies ran while one was open for 2% of the time, Pallas kernels for 20%

profile of v12, /device:TPU:2, one launch (start us, length us, event | category | flops | bytes accessed | tf_op | source)
XLA Modules:
  0.0 310.3 jit_solution(17944014021815950223)
XLA Ops:
  2.0 1.6 copy-done.2
  5.7 4.6 %collective-permute-start.6 = (bf16[256,256]{1,0:T(8,128)(2,1)S(1)}, bf16[256,256]{1,0:T(8,128)(2,1)S(1)}, u32[]{:S(2)}, u32[]{:S(2)}) collective-permute-start(bf16[256,256]{1,0:T(8,128)(2,1)S(1)} %get-tuple-element.75), channel_id=1, source_target_pairs={{0,7},{2,5},{4,3},{6,1},{7,0},{5,2},{3,4},{1,6},{8,15},{10,13},{12... | collective-permute-start | bytes 393224 | tf_op jit(solution)/shard_map/ppermute | solution.py:625
  10.3 4.5 %collective-permute-done.6.mine.mine_far = bf16[256,256]{1,0:T(8,128)(2,1)S(1)} collective-permute-done((bf16[256,256]{1,0:T(8,128)(2,1)S(1)}, bf16[256,256]{1,0:T(8,128)(2,1)S(1)}, u32[]{:S(2)}, u32[]{:S(2)}) %collective-permute-start.6) | collective-permute-done | bytes 131104 | tf_op jit(solution)/shard_map/ppermute | solution.py:625
  15.3 3.4 %collective-permute-start.2 = (bf16[256,256]{1,0:T(8,128)(2,1)S(1)}, bf16[256,256]{1,0:T(8,128)(2,1)S(1)}, u32[]{:S(2)}, u32[]{:S(2)}) collective-permute-start(bf16[256,256]{1,0:T(8,128)(2,1)S(1)} %get-tuple-element.71), channel_id=1, source_target_pairs={{0,4},{2,6},{4,7},{6,5},{7,3},{5,1},{3,0},{1,2},{8,12},{10,14},{12... | collective-permute-start | bytes 393224 | tf_op jit(solution)/shard_map/ppermute | solution.py:625
  19.9 1.7 collective-permute-start.4
  21.7 2.1 collective-permute-start.5
  23.8 1.9 copy-done.4
  27.5 1.9 sum_first.1
  29.4 4.6 %collective-permute-done.3.refs_4_ = bf16[256,256]{1,0:T(8,128)(2,1)S(1)} collective-permute-done((bf16[256,256]{1,0:T(8,128)(2,1)S(1)}, bf16[256,256]{1,0:T(8,128)(2,1)S(1)}, u32[]{:S(2)}, u32[]{:S(2)}) %collective-permute-start.3) | collective-permute-done | bytes 131104 | tf_op jit(solution)/shard_map/ppermute | solution.py:625
  35.2 3.1 %collective-permute-start.10 = (bf16[3,128,512]{2,1,0:T(8,128)(2,1)S(1)}, bf16[3,128,512]{2,1,0:T(8,128)(2,1)S(1)}, u32[]{:S(2)}, u32[]{:S(2)}) collective-permute-start(bf16[3,128,512]{2,1,0:T(8,128)(2,1)S(1)} %get-tuple-element.78), channel_id=1, source_target_pairs={{0,1},{2,0},{4,2},{6,4},{7,6},{5,7},{3,5},{1,3},{8,9},{10,8},{12,1... | collective-permute-start | bytes 1179656 | tf_op jit(solution)/shard_map/ppermute | solution.py:625
  38.4 2.1 collective-permute-start.18
  40.4 7.4 %collective-permute-done.10.refs_8_ = bf16[3,128,512]{2,1,0:T(8,128)(2,1)S(1)} collective-permute-done((bf16[3,128,512]{2,1,0:T(8,128)(2,1)S(1)}, bf16[3,128,512]{2,1,0:T(8,128)(2,1)S(1)}, u32[]{:S(2)}, u32[]{:S(2)}) %collective-permute-start.10) | collective-permute-done | bytes 393248 | tf_op jit(solution)/shard_map/ppermute | solution.py:625
  47.8 2.5 collective-permute-done.9.refs_7_
  50.3 2.1 sum_step.6
  52.4 2.0 collective-permute-start.12
  54.5 4.3 %collective-permute-done.17.refs_7_ = bf16[3,128,512]{2,1,0:T(8,128)(2,1)S(1)} collective-permute-done((bf16[3,128,512]{2,1,0:T(8,128)(2,1)S(1)}, bf16[3,128,512]{2,1,0:T(8,128)(2,1)S(1)}, u32[]{:S(2)}, u32[]{:S(2)}) %collective-permute-start.17) | collective-permute-done | bytes 393248 | tf_op jit(solution)/shard_map/ppermute | solution.py:625
  58.7 2.1 sum_step.9
  60.9 2.0 collective-permute-start.20
  62.9 12.7 %collective-permute-done.11.refs_7_ = bf16[3,256,512]{2,1,0:T(8,128)(2,1)S(1)} collective-permute-done((bf16[3,256,512]{2,1,0:T(8,128)(2,1)S(1)}, bf16[3,256,512]{2,1,0:T(8,128)(2,1)S(1)}, u32[]{:S(2)}, u32[]{:S(2)}) %collective-permute-start.11) | collective-permute-done | bytes 786464 | tf_op jit(solution)/shard_map/ppermute | solution.py:625
  75.6 2.1 sum_step.7
  77.7 2.0 collective-permute-start.14
  79.7 12.7 %collective-permute-done.19.refs_7_ = bf16[3,256,512]{2,1,0:T(8,128)(2,1)S(1)} collective-permute-done((bf16[3,256,512]{2,1,0:T(8,128)(2,1)S(1)}, bf16[3,256,512]{2,1,0:T(8,128)(2,1)S(1)}, u32[]{:S(2)}, u32[]{:S(2)}) %collective-permute-start.19) | collective-permute-done | bytes 786464 | tf_op jit(solution)/shard_map/ppermute | solution.py:625
  92.4 2.1 sum_step.10
  94.6 2.0 collective-permute-start.22
  97.8 11.5 %collective-permute-done.13.refs_7_ = bf16[3,256,512]{2,1,0:T(8,128)(2,1)S(1)} collective-permute-done((bf16[3,256,512]{2,1,0:T(8,128)(2,1)S(1)}, bf16[3,256,512]{2,1,0:T(8,128)(2,1)S(1)}, u32[]{:S(2)}, u32[]{:S(2)}) %collective-permute-start.13) | collective-permute-done | bytes 786464 | tf_op jit(solution)/shard_map/ppermute | solution.py:625
  109.3 2.1 sum_step.8
  111.4 2.0 collective-permute-start.16
  113.4 12.7 %collective-permute-done.21.refs_7_ = bf16[3,256,512]{2,1,0:T(8,128)(2,1)S(1)} collective-permute-done((bf16[3,256,512]{2,1,0:T(8,128)(2,1)S(1)}, bf16[3,256,512]{2,1,0:T(8,128)(2,1)S(1)}, u32[]{:S(2)}, u32[]{:S(2)}) %collective-permute-start.21) | collective-permute-done | bytes 786464 | tf_op jit(solution)/shard_map/ppermute | solution.py:625
  126.2 2.1 sum_step.11
  128.3 2.0 collective-permute-start.24
  131.0 12.0 %collective-permute-done.15.from_left = bf16[3,256,512]{2,1,0:T(8,128)(2,1)S(1)} collective-permute-done((bf16[3,256,512]{2,1,0:T(8,128)(2,1)S(1)}, bf16[3,256,512]{2,1,0:T(8,128)(2,1)S(1)}, u32[]{:S(2)}, u32[]{:S(2)}) %collective-permute-start.15) | collective-permute-done | bytes 786464 | tf_op jit(solution)/shard_map/ppermute | solution.py:625
  143.0 7.2 %attention.2 = (bf16[256,512]{1,0:T(8,128)(2,1)S(1)}, f32[256,128]{1,0:T(8,128)S(1)}, bf16[3,256,512]{2,1,0:T(8,128)(2,1)S(1)}) custom-call(s32[39]{0:T(128)S(1)} %dynamic-slice_bitcast_fusion.idx.refs_0_, bf16[7,256,256]{2,1,0:T(8,128)(2,1)S(1)} %stack.1.refs_1_.refs_3_.mine, bf16[7,256,256]{2,1,0:T(8,128)(2,1)S(1)} %collective-permute-done.8.refs_2_.refs_4_.other, ...), custom_call_target="tpu_custom_call" | custom-call | flops 402653184 | bytes 3145728 | tf_op jit(solution)/shard_map/attention/pallas_call | solution.py:394
  151.0 2.0 collective-permute-start.27
  152.9 6.9 %collective-permute-done.23.from_left = bf16[3,256,512]{2,1,0:T(8,128)(2,1)S(1)} collective-permute-done((bf16[3,256,512]{2,1,0:T(8,128)(2,1)S(1)}, bf16[3,256,512]{2,1,0:T(8,128)(2,1)S(1)}, u32[]{:S(2)}, u32[]{:S(2)}) %collective-permute-start.23) | collective-permute-done | bytes 786464 | tf_op jit(solution)/shard_map/ppermute | solution.py:625
  159.9 7.3 %attention.3 = (bf16[256,512]{1,0:T(8,128)(2,1)S(1)}, f32[256,128]{1,0:T(8,128)S(1)}, bf16[3,256,512]{2,1,0:T(8,128)(2,1)S(1)}) custom-call(s32[39]{0:T(128)S(1)} %dynamic-slice_bitcast_fusion.idx.refs_0_, bf16[7,256,256]{2,1,0:T(8,128)(2,1)S(1)} %stack.1.refs_1_.refs_3_.mine, bf16[7,256,256]{2,1,0:T(8,128)(2,1)S(1)} %collective-permute-done.8.refs_2_.refs_4_.other, ...), custom_call_target="tpu_custom_call" | custom-call | flops 402653184 | bytes 3145728 | tf_op jit(solution)/shard_map/attention/pallas_call | solution.py:394
  168.6 2.0 collective-permute-start.35
  171.5 2.7 collective-permute-done.30.refs_2_.refs_3_
  174.2 2.5 collective-permute-start.31
  178.5 12.6 %collective-permute-done.38.refs_2_.refs_3_ = bf16[3,256,512]{2,1,0:T(8,128)(2,1)S(1)} collective-permute-done((bf16[3,256,512]{2,1,0:T(8,128)(2,1)S(1)}, bf16[3,256,512]{2,1,0:T(8,128)(2,1)S(1)}, u32[]{:S(2)}, u32[]{:S(2)}) %collective-permute-start.38) | collective-permute-done | bytes 786464 | tf_op jit(solution)/shard_map/ppermute | solution.py:625
  191.0 2.5 collective-permute-start.39
  195.3 12.6 %collective-permute-done.31.refs_1_.refs_5_ = bf16[3,256,512]{2,1,0:T(8,128)(2,1)} collective-permute-done((bf16[3,256,512]{2,1,0:T(8,128)(2,1)S(1)}, bf16[3,256,512]{2,1,0:T(8,128)(2,1)}, u32[]{:S(2)}, u32[]{:S(2)}) %collective-permute-start.31) | collective-permute-done | bytes 786464 | tf_op jit(solution)/shard_map/ppermute | solution.py:625
  207.9 2.6 collective-permute-start.32
  210.5 14.2 %collective-permute-done.39.refs_1_.refs_5_ = bf16[3,256,512]{2,1,0:T(8,128)(2,1)} collective-permute-done((bf16[3,256,512]{2,1,0:T(8,128)(2,1)S(1)}, bf16[3,256,512]{2,1,0:T(8,128)(2,1)}, u32[]{:S(2)}, u32[]{:S(2)}) %collective-permute-start.39) | collective-permute-done | bytes 786464 | tf_op jit(solution)/shard_map/ppermute | solution.py:625
  224.8 2.6 collective-permute-start.40
  230.2 1.6 collective-permute-done.25
  233.3 5.0 %collective-permute-done.26 = f32[256,1]{1,0:T(8,128)S(1)} collective-permute-done((f32[256,1]{1,0:T(8,128)S(1)}, f32[256,1]{1,0:T(8,128)S(1)}, u32[]{:S(2)}, u32[]{:S(2)}) %collective-permute-start.26) | collective-permute-done | bytes 1056 | tf_op jit(solution)/shard_map/ppermute | solution.py:628
  244.5 2.3 term_step.10
  246.9 1.4 halve.2
  250.5 2.3 term_step.11
  252.8 5.7 %collective-permute-done.40.refs_1_.refs_7_ = bf16[3,256,512]{2,1,0:T(8,128)(2,1)} collective-permute-done((bf16[3,256,512]{2,1,0:T(8,128)(2,1)}, bf16[3,256,512]{2,1,0:T(8,128)(2,1)}, u32[]{:S(2)}, u32[]{:S(2)}) %collective-permute-start.40) | collective-permute-done | bytes 786464 | tf_op jit(solution)/shard_map/ppermute | solution.py:625
  258.6 2.5 collective-permute-done.37.refs_0_.refs_6_
  262.6 2.0 collective-permute-start.42
  264.6 2.3 term_step.12
  266.9 2.3 term_step.13
  270.0 7.1 %collective-permute-done.41.refs_2_.refs_8_ = bf16[3,128,512]{2,1,0:T(8,128)(2,1)S(1)} collective-permute-done((bf16[3,128,512]{2,1,0:T(8,128)(2,1)S(1)}, bf16[3,128,512]{2,1,0:T(8,128)(2,1)S(1)}, u32[]{:S(2)}, u32[]{:S(2)}) %collective-permute-start.41) | collective-permute-done | bytes 393248 | tf_op jit(solution)/shard_map/ppermute | solution.py:625
  277.1 1.6 term_last.1
  282.6 1.6 collective-permute-start.48
  284.2 6.3 %grads.2.refs_10_ = f32[3,512,1024]{2,1,0:T(8,128)} custom-call(bf16[512,2048]{1,0:T(8,128)(2,1)S(1)} %copy-done.1, bf16[3,256,512]{2,1,0:T(8,128)(2,1)S(1)} %copy-done.13, bf16[3,256,512]{2,1,0:T(8,128)(2,1)S(1)} %copy-done.19, bf16[3,256,512]{2,1,0:T(8,128)(2,1)S(1)} %copy-done.16, bf16[3,256,512]{2,1,0:T(8,128)(2,1)} %collective-permute-done.28.refs_0_.refs_4_, ...), custom_call_target="tpu_custom_call" | custom-call | flops 3221225472 | bytes 9437184 | tf_op jit(solution)/shard_map/grads/pallas_call | solution.py:436
  291.2 2.6 collective-permute-start.45
  293.9 1.5 collective-permute-done.48.came
  296.0 1.6 collective-permute-start.50
  297.6 4.7 %collective-permute-start.49 = (bf16[128,512]{1,0:T(8,128)(2,1)S(1)}, bf16[128,512]{1,0:T(8,128)(2,1)S(1)}, u32[]{:S(2)}, u32[]{:S(2)}) collective-permute-start(bf16[128,512]{1,0:T(8,128)(2,1)S(1)} %get-tuple-element.131.refs_12_), channel_id=1, source_target_pairs={{0,0},{1,1},{2,8},{3,9},{4,16},{5,17},{6,24},{7,25},{8,4},{9,5},{1... | collective-permute-start | bytes 393224 | tf_op jit(solution)/shard_map/ppermute | solution.py:686
  302.3 6.3 %grads.3 = f32[3,512,1024]{2,1,0:T(8,128)} custom-call(bf16[512,2048]{1,0:T(8,128)(2,1)S(1)} %copy-done.1, bf16[3,256,512]{2,1,0:T(8,128)(2,1)S(1)} %copy-done.6, bf16[3,256,512]{2,1,0:T(8,128)(2,1)S(1)} %copy-done.10, bf16[3,256,512]{2,1,0:T(8,128)(2,1)S(1)} %copy-done.8, ...), custom_call_target="tpu_custom_call", output_to_operand_aliasing={{}: (10, {})} | custom-call | flops 3221225472 | bytes 9437184 | tf_op jit(solution)/shard_map/grads/pallas_call | solution.py:436
  308.6 1.6 finish.1
  (137 shorter events, 37.3 us)
Async XLA Ops:
  5.7 9.1 %collective-permute-start.6 = (bf16[256,256]{1,0:T(8,128)(2,1)S(1)}, bf16[256,256]{1,0:T(8,128)(2,1)S(1)}, u32[]{:S(2)}, u32[]{:S(2)}) collective-permute-start(bf16[256,256]{1,0:T(8,128)(2,1)S(1)} %get-tuple-element.75), channel_id=1, source_target_pairs={{0,7},{2,5},{4,3},{6,1},{7,0},{5,2},{3,4},{1,6},{8,15},{10,13},{12... | collective-permute-start | bytes 393224 | tf_op jit(solution)/shard_map/ppermute | solution.py:625
  10.3 9.7 %collective-permute-start = (bf16[256,256]{1,0:T(8,128)(2,1)S(1)}, bf16[256,256]{1,0:T(8,128)(2,1)S(1)}, u32[]{:S(2)}, u32[]{:S(2)}) collective-permute-start(bf16[256,256]{1,0:T(8,128)(2,1)S(1)} %get-tuple-element.69), channel_id=1, source_target_pairs={{0,2},{2,4},{4,6},{6,7},{7,5},{5,3},{3,1},{1,0},{8,10},{10,12},{12... | collective-permute-start | bytes 393224 | tf_op jit(solution)/shard_map/ppermute | solution.py:625
  14.8 6.9 %collective-permute-start.7 = (bf16[256,256]{1,0:T(8,128)(2,1)S(1)}, bf16[256,256]{1,0:T(8,128)(2,1)S(1)}, u32[]{:S(2)}, u32[]{:S(2)}) collective-permute-start(bf16[256,256]{1,0:T(8,128)(2,1)S(1)} %collective-permute-done.6.mine.mine_far), channel_id=1, source_target_pairs={{0,8},{8,0},{16,24},{24,16},{1,9},{9,1},{17,25},{25,17},{2,10},{10... | collective-permute-start | bytes 393224 | tf_op jit(solution)/shard_map/ppermute | solution.py:628
  14.8 14.6 %collective-permute-start.1 = (bf16[256,256]{1,0:T(8,128)(2,1)S(1)}, bf16[256,256]{1,0:T(8,128)(2,1)S(1)}, u32[]{:S(2)}, u32[]{:S(2)}) collective-permute-start(bf16[256,256]{1,0:T(8,128)(2,1)S(1)} %get-tuple-element.70), channel_id=1, source_target_pairs={{0,1},{2,0},{4,2},{6,4},{7,6},{5,7},{3,5},{1,3},{8,9},{10,8},{12,1... | collective-permute-start | bytes 393224 | tf_op jit(solution)/shard_map/ppermute | solution.py:625
  15.3 14.1 %collective-permute-start.2 = (bf16[256,256]{1,0:T(8,128)(2,1)S(1)}, bf16[256,256]{1,0:T(8,128)(2,1)S(1)}, u32[]{:S(2)}, u32[]{:S(2)}) collective-permute-start(bf16[256,256]{1,0:T(8,128)(2,1)S(1)} %get-tuple-element.71), channel_id=1, source_target_pairs={{0,4},{2,6},{4,7},{6,5},{7,3},{5,1},{3,0},{1,2},{8,12},{10,14},{12... | collective-permute-start | bytes 393224 | tf_op jit(solution)/shard_map/ppermute | solution.py:625
  18.7 15.3 %collective-permute-start.3 = (bf16[256,256]{1,0:T(8,128)(2,1)S(1)}, bf16[256,256]{1,0:T(8,128)(2,1)S(1)}, u32[]{:S(2)}, u32[]{:S(2)}) collective-permute-start(bf16[256,256]{1,0:T(8,128)(2,1)S(1)} %get-tuple-element.72), channel_id=1, source_target_pairs={{0,3},{2,1},{4,0},{6,2},{7,4},{5,6},{3,7},{1,5},{8,11},{10,9},{12,... | collective-permute-start | bytes 393224 | tf_op jit(solution)/shard_map/ppermute | solution.py:625
  19.9 15.2 %collective-permute-start.4 = (bf16[256,256]{1,0:T(8,128)(2,1)S(1)}, bf16[256,256]{1,0:T(8,128)(2,1)S(1)}, u32[]{:S(2)}, u32[]{:S(2)}) collective-permute-start(bf16[256,256]{1,0:T(8,128)(2,1)S(1)} %get-tuple-element.73), channel_id=1, source_target_pairs={{0,6},{2,7},{4,5},{6,3},{7,1},{5,0},{3,2},{1,4},{8,14},{10,15},{12... | collective-permute-start | bytes 393224 | tf_op jit(solution)/shard_map/ppermute | solution.py:625
  21.7 13.4 %collective-permute-start.5 = (bf16[256,256]{1,0:T(8,128)(2,1)S(1)}, bf16[256,256]{1,0:T(8,128)(2,1)S(1)}, u32[]{:S(2)}, u32[]{:S(2)}) collective-permute-start(bf16[256,256]{1,0:T(8,128)(2,1)S(1)} %get-tuple-element.74), channel_id=1, source_target_pairs={{0,5},{2,3},{4,1},{6,0},{7,2},{5,4},{3,6},{1,7},{8,13},{10,11},{12... | collective-permute-start | bytes 393224 | tf_op jit(solution)/shard_map/ppermute | solution.py:625
  35.2 15.1 %collective-permute-start.8 = (bf16[7,256,256]{2,1,0:T(8,128)(2,1)S(1)}, bf16[7,256,256]{2,1,0:T(8,128)(2,1)S(1)}, u32[]{:S(2)}, u32[]{:S(2)}) collective-permute-start(bf16[7,256,256]{2,1,0:T(8,128)(2,1)S(1)} %stack.1.refs_1_.refs_3_.mine), channel_id=1, source_target_pairs={{0,8},{8,0},{16,24},{24,16},{1,9},{9,1},{17,25},{25,17},{2,10},{10... | collective-permute-start | bytes 2752520 | tf_op jit(solution)/shard_map/ppermute | solution.py:628
  35.2 12.5 %collective-permute-start.10 = (bf16[3,128,512]{2,1,0:T(8,128)(2,1)S(1)}, bf16[3,128,512]{2,1,0:T(8,128)(2,1)S(1)}, u32[]{:S(2)}, u32[]{:S(2)}) collective-permute-start(bf16[3,128,512]{2,1,0:T(8,128)(2,1)S(1)} %get-tuple-element.78), channel_id=1, source_target_pairs={{0,1},{2,0},{4,2},{6,4},{7,6},{5,7},{3,5},{1,3},{8,9},{10,8},{12,1... | collective-permute-start | bytes 1179656 | tf_op jit(solution)/shard_map/ppermute | solution.py:625
  38.4 12.0 %collective-permute-start.9 = (bf16[3,128,512]{2,1,0:T(8,128)(2,1)S(1)}, bf16[3,128,512]{2,1,0:T(8,128)(2,1)S(1)}, u32[]{:S(2)}, u32[]{:S(2)}) collective-permute-start(bf16[3,128,512]{2,1,0:T(8,128)(2,1)S(1)} %get-tuple-element.77.refs_7_), channel_id=1, source_target_pairs={{0,2},{2,4},{4,6},{6,7},{7,5},{5,3},{3,1},{1,0},{8,10},{10,12},{12... | collective-permute-start | bytes 1179656 | tf_op jit(solution)/shard_map/ppermute | solution.py:625
  38.4 20.4 %collective-permute-start.17 = (bf16[3,128,512]{2,1,0:T(8,128)(2,1)S(1)}, bf16[3,128,512]{2,1,0:T(8,128)(2,1)S(1)}, u32[]{:S(2)}, u32[]{:S(2)}) collective-permute-start(bf16[3,128,512]{2,1,0:T(8,128)(2,1)S(1)} %get-tuple-element.86), channel_id=1, source_target_pairs={{0,2},{2,4},{4,6},{6,7},{7,5},{5,3},{3,1},{1,0},{8,10},{10,12},{12... | collective-permute-start | bytes 1179656 | tf_op jit(solution)/shard_map/ppermute | solution.py:625
  38.4 20.4 %collective-permute-start.18 = (bf16[3,128,512]{2,1,0:T(8,128)(2,1)S(1)}, bf16[3,128,512]{2,1,0:T(8,128)(2,1)S(1)}, u32[]{:S(2)}, u32[]{:S(2)}) collective-permute-start(bf16[3,128,512]{2,1,0:T(8,128)(2,1)S(1)} %get-tuple-element.87), channel_id=1, source_target_pairs={{0,1},{2,0},{4,2},{6,4},{7,6},{5,7},{3,5},{1,3},{8,9},{10,8},{12,1... | collective-permute-start | bytes 1179656 | tf_op jit(solution)/shard_map/ppermute | solution.py:625
  52.4 23.2 %collective-permute-start.11 = (bf16[3,256,512]{2,1,0:T(8,128)(2,1)S(1)}, bf16[3,256,512]{2,1,0:T(8,128)(2,1)S(1)}, u32[]{:S(2)}, u32[]{:S(2)}) collective-permute-start(bf16[3,256,512]{2,1,0:T(8,128)(2,1)S(1)} %get-tuple-element.79), channel_id=1, source_target_pairs={{0,2},{2,4},{4,6},{6,7},{7,5},{5,3},{3,1},{1,0},{8,10},{10,12},{12... | collective-permute-start | bytes 2359304 | tf_op jit(solution)/shard_map/ppermute | solution.py:625
  52.4 23.1 %collective-permute-start.12 = (bf16[3,256,512]{2,1,0:T(8,128)(2,1)S(1)}, bf16[3,256,512]{2,1,0:T(8,128)(2,1)S(1)}, u32[]{:S(2)}, u32[]{:S(2)}) collective-permute-start(bf16[3,256,512]{2,1,0:T(8,128)(2,1)S(1)} %get-tuple-element.80), channel_id=1, source_target_pairs={{0,1},{2,0},{4,2},{6,4},{7,6},{5,7},{3,5},{1,3},{8,9},{10,8},{12,1... | collective-permute-start | bytes 2359304 | tf_op jit(solution)/shard_map/ppermute | solution.py:625
  60.8 31.6 %collective-permute-start.19 = (bf16[3,256,512]{2,1,0:T(8,128)(2,1)S(1)}, bf16[3,256,512]{2,1,0:T(8,128)(2,1)S(1)}, u32[]{:S(2)}, u32[]{:S(2)}) collective-permute-start(bf16[3,256,512]{2,1,0:T(8,128)(2,1)S(1)} %get-tuple-element.88), channel_id=1, source_target_pairs={{0,2},{2,4},{4,6},{6,7},{7,5},{5,3},{3,1},{1,0},{8,10},{10,12},{12... | collective-permute-start | bytes 2359304 | tf_op jit(solution)/shard_map/ppermute | solution.py:625
  60.9 31.6 %collective-permute-start.20 = (bf16[3,256,512]{2,1,0:T(8,128)(2,1)S(1)}, bf16[3,256,512]{2,1,0:T(8,128)(2,1)S(1)}, u32[]{:S(2)}, u32[]{:S(2)}) collective-permute-start(bf16[3,256,512]{2,1,0:T(8,128)(2,1)S(1)} %get-tuple-element.89), channel_id=1, source_target_pairs={{0,1},{2,0},{4,2},{6,4},{7,6},{5,7},{3,5},{1,3},{8,9},{10,8},{12,1... | collective-permute-start | bytes 2359304 | tf_op jit(solution)/shard_map/ppermute | solution.py:625
  77.7 31.6 %collective-permute-start.13 = (bf16[3,256,512]{2,1,0:T(8,128)(2,1)S(1)}, bf16[3,256,512]{2,1,0:T(8,128)(2,1)S(1)}, u32[]{:S(2)}, u32[]{:S(2)}) collective-permute-start(bf16[3,256,512]{2,1,0:T(8,128)(2,1)S(1)} %get-tuple-element.81), channel_id=1, source_target_pairs={{0,2},{2,4},{4,6},{6,7},{7,5},{5,3},{3,1},{1,0},{8,10},{10,12},{12... | collective-permute-start | bytes 2359304 | tf_op jit(solution)/shard_map/ppermute | solution.py:625
  77.7 31.6 %collective-permute-start.14 = (bf16[3,256,512]{2,1,0:T(8,128)(2,1)S(1)}, bf16[3,256,512]{2,1,0:T(8,128)(2,1)S(1)}, u32[]{:S(2)}, u32[]{:S(2)}) collective-permute-start(bf16[3,256,512]{2,1,0:T(8,128)(2,1)S(1)} %get-tuple-element.82), channel_id=1, source_target_pairs={{0,1},{2,0},{4,2},{6,4},{7,6},{5,7},{3,5},{1,3},{8,9},{10,8},{12,1... | collective-permute-start | bytes 2359304 | tf_op jit(solution)/shard_map/ppermute | solution.py:625
  94.5 31.6 %collective-permute-start.21 = (bf16[3,256,512]{2,1,0:T(8,128)(2,1)S(1)}, bf16[3,256,512]{2,1,0:T(8,128)(2,1)S(1)}, u32[]{:S(2)}, u32[]{:S(2)}) collective-permute-start(bf16[3,256,512]{2,1,0:T(8,128)(2,1)S(1)} %get-tuple-element.90), channel_id=1, source_target_pairs={{0,2},{2,4},{4,6},{6,7},{7,5},{5,3},{3,1},{1,0},{8,10},{10,12},{12... | collective-permute-start | bytes 2359304 | tf_op jit(solution)/shard_map/ppermute | solution.py:625
  94.6 31.6 %collective-permute-start.22 = (bf16[3,256,512]{2,1,0:T(8,128)(2,1)S(1)}, bf16[3,256,512]{2,1,0:T(8,128)(2,1)S(1)}, u32[]{:S(2)}, u32[]{:S(2)}) collective-permute-start(bf16[3,256,512]{2,1,0:T(8,128)(2,1)S(1)} %get-tuple-element.91), channel_id=1, source_target_pairs={{0,1},{2,0},{4,2},{6,4},{7,6},{5,7},{3,5},{1,3},{8,9},{10,8},{12,1... | collective-permute-start | bytes 2359304 | tf_op jit(solution)/shard_map/ppermute | solution.py:625
  97.8 28.4 %copy-start = (bf16[512,2048]{1,0:T(8,128)(2,1)}, bf16[512,2048]{1,0:T(8,128)(2,1)S(1)}, u32[]{:S(2)}) copy-start(bf16[512,2048]{1,0:T(8,128)(2,1)S(1)} %turn.1.refs_9_.refs_0_) | copy-start | bytes 6291460
  111.4 31.6 %collective-permute-start.15 = (bf16[3,256,512]{2,1,0:T(8,128)(2,1)S(1)}, bf16[3,256,512]{2,1,0:T(8,128)(2,1)S(1)}, u32[]{:S(2)}, u32[]{:S(2)}) collective-permute-start(bf16[3,256,512]{2,1,0:T(8,128)(2,1)S(1)} %get-tuple-element.83), channel_id=1, source_target_pairs={{0,2},{2,4},{4,6},{6,7},{7,5},{5,3},{3,1},{1,0},{8,10},{10,12},{12... | collective-permute-start | bytes 2359304 | tf_op jit(solution)/shard_map/ppermute | solution.py:625
  111.4 31.6 %copy-start.20 = (bf16[256,1024]{1,0:T(8,128)(2,1)S(1)}, bf16[256,1024]{1,0:T(8,128)(2,1)}, u32[]{:S(2)}) copy-start(bf16[256,1024]{1,0:T(8,128)(2,1)} %d_out.3) | copy-start | bytes 1572868
  111.4 31.6 %collective-permute-start.16 = (bf16[3,256,512]{2,1,0:T(8,128)(2,1)S(1)}, bf16[3,256,512]{2,1,0:T(8,128)(2,1)S(1)}, u32[]{:S(2)}, u32[]{:S(2)}) collective-permute-start(bf16[3,256,512]{2,1,0:T(8,128)(2,1)S(1)} %get-tuple-element.84), channel_id=1, source_target_pairs={{0,1},{2,0},{4,2},{6,4},{7,6},{5,7},{3,5},{1,3},{8,9},{10,8},{12,1... | collective-permute-start | bytes 2359304 | tf_op jit(solution)/shard_map/ppermute | solution.py:625
  128.2 31.6 %collective-permute-start.23 = (bf16[3,256,512]{2,1,0:T(8,128)(2,1)S(1)}, bf16[3,256,512]{2,1,0:T(8,128)(2,1)S(1)}, u32[]{:S(2)}, u32[]{:S(2)}) collective-permute-start(bf16[3,256,512]{2,1,0:T(8,128)(2,1)S(1)} %get-tuple-element.92), channel_id=1, source_target_pairs={{0,2},{2,4},{4,6},{6,7},{7,5},{5,3},{3,1},{1,0},{8,10},{10,12},{12... | collective-permute-start | bytes 2359304 | tf_op jit(solution)/shard_map/ppermute | solution.py:625
  128.3 31.6 %collective-permute-start.24 = (bf16[3,256,512]{2,1,0:T(8,128)(2,1)S(1)}, bf16[3,256,512]{2,1,0:T(8,128)(2,1)S(1)}, u32[]{:S(2)}, u32[]{:S(2)}) collective-permute-start(bf16[3,256,512]{2,1,0:T(8,128)(2,1)S(1)} %get-tuple-element.93), channel_id=1, source_target_pairs={{0,1},{2,0},{4,2},{6,4},{7,6},{5,7},{3,5},{1,3},{8,9},{10,8},{12,1... | collective-permute-start | bytes 2359304 | tf_op jit(solution)/shard_map/ppermute | solution.py:625
  150.9 16.2 %copy-start.11 = (bf16[3,256,512]{2,1,0:T(8,128)(2,1)}, bf16[3,256,512]{2,1,0:T(8,128)(2,1)S(1)}, u32[]{:S(2)}) copy-start(bf16[3,256,512]{2,1,0:T(8,128)(2,1)S(1)} %get-tuple-element.99.refs_0_.refs_1_) | copy-start | bytes 2359300
  150.9 23.3 %collective-permute-start.30 = (bf16[3,256,512]{2,1,0:T(8,128)(2,1)S(1)}, bf16[3,256,512]{2,1,0:T(8,128)(2,1)S(1)}, u32[]{:S(2)}, u32[]{:S(2)}) collective-permute-start(bf16[3,256,512]{2,1,0:T(8,128)(2,1)S(1)} %get-tuple-element.99.refs_0_.refs_1_), channel_id=1, source_target_pairs={{0,1},{2,0},{4,2},{6,4},{7,6},{5,7},{3,5},{1,3},{8,9},{10,8},{12,1... | collective-permute-start | bytes 2359304 | tf_op jit(solution)/shard_map/ppermute | solution.py:625
  151.0 26.6 %collective-permute-start.27 = (bf16[3,256,512]{2,1,0:T(8,128)(2,1)S(1)}, bf16[3,256,512]{2,1,0:T(8,128)(2,1)S(1)}, u32[]{:S(2)}, u32[]{:S(2)}) collective-permute-start(bf16[3,256,512]{2,1,0:T(8,128)(2,1)S(1)} %get-tuple-element.99.refs_0_.refs_1_), channel_id=1, source_target_pairs={{0,2},{2,4},{4,6},{6,7},{7,5},{5,3},{3,1},{1,0},{8,10},{10,12},{12... | collective-permute-start | bytes 2359304 | tf_op jit(solution)/shard_map/ppermute | solution.py:625
  168.5 22.5 %collective-permute-start.38 = (bf16[3,256,512]{2,1,0:T(8,128)(2,1)S(1)}, bf16[3,256,512]{2,1,0:T(8,128)(2,1)S(1)}, u32[]{:S(2)}, u32[]{:S(2)}) collective-permute-start(bf16[3,256,512]{2,1,0:T(8,128)(2,1)S(1)} %get-tuple-element.104.refs_0_.refs_1_), channel_id=1, source_target_pairs={{0,1},{2,0},{4,2},{6,4},{7,6},{5,7},{3,5},{1,3},{8,9},{10,8},{12,1... | collective-permute-start | bytes 2359304 | tf_op jit(solution)/shard_map/ppermute | solution.py:625
  168.6 25.9 %collective-permute-start.35 = (bf16[3,256,512]{2,1,0:T(8,128)(2,1)S(1)}, bf16[3,256,512]{2,1,0:T(8,128)(2,1)S(1)}, u32[]{:S(2)}, u32[]{:S(2)}) collective-permute-start(bf16[3,256,512]{2,1,0:T(8,128)(2,1)S(1)} %get-tuple-element.104.refs_0_.refs_1_), channel_id=1, source_target_pairs={{0,2},{2,4},{4,6},{6,7},{7,5},{5,3},{3,1},{1,0},{8,10},{10,12},{12... | collective-permute-start | bytes 2359304 | tf_op jit(solution)/shard_map/ppermute | solution.py:625
  174.2 33.7 %collective-permute-start.31 = (bf16[3,256,512]{2,1,0:T(8,128)(2,1)S(1)}, bf16[3,256,512]{2,1,0:T(8,128)(2,1)}, u32[]{:S(2)}, u32[]{:S(2)}) collective-permute-start(bf16[3,256,512]{2,1,0:T(8,128)(2,1)S(1)} %collective-permute-done.30.refs_2_.refs_3_), channel_id=1, source_target_pairs={{0,1},{2,0},{4,2},{6,4},{7,6},{5,7},{3,5},{1,3},{8,9},{10,8},{12,1... | collective-permute-start | bytes 2359304 | tf_op jit(solution)/shard_map/ppermute | solution.py:625
  177.6 32.9 %collective-permute-start.28 = (bf16[3,256,512]{2,1,0:T(8,128)(2,1)S(1)}, bf16[3,256,512]{2,1,0:T(8,128)(2,1)}, u32[]{:S(2)}, u32[]{:S(2)}) collective-permute-start(bf16[3,256,512]{2,1,0:T(8,128)(2,1)S(1)} %collective-permute-done.27.refs_1_.refs_2_), channel_id=1, source_target_pairs={{0,2},{2,4},{4,6},{6,7},{7,5},{5,3},{3,1},{1,0},{8,10},{10,12},{12... | collective-permute-start | bytes 2359304 | tf_op jit(solution)/shard_map/ppermute | solution.py:625
  191.0 33.7 %collective-permute-start.39 = (bf16[3,256,512]{2,1,0:T(8,128)(2,1)S(1)}, bf16[3,256,512]{2,1,0:T(8,128)(2,1)}, u32[]{:S(2)}, u32[]{:S(2)}) collective-permute-start(bf16[3,256,512]{2,1,0:T(8,128)(2,1)S(1)} %collective-permute-done.38.refs_2_.refs_3_), channel_id=1, source_target_pairs={{0,1},{2,0},{4,2},{6,4},{7,6},{5,7},{3,5},{1,3},{8,9},{10,8},{12,1... | collective-permute-start | bytes 2359304 | tf_op jit(solution)/shard_map/ppermute | solution.py:625
  194.4 33.0 %collective-permute-start.36 = (bf16[3,256,512]{2,1,0:T(8,128)(2,1)S(1)}, bf16[3,256,512]{2,1,0:T(8,128)(2,1)}, u32[]{:S(2)}, u32[]{:S(2)}) collective-permute-start(bf16[3,256,512]{2,1,0:T(8,128)(2,1)S(1)} %collective-permute-done.35.refs_1_.refs_2_), channel_id=1, source_target_pairs={{0,2},{2,4},{4,6},{6,7},{7,5},{5,3},{3,1},{1,0},{8,10},{10,12},{12... | collective-permute-start | bytes 2359304 | tf_op jit(solution)/shard_map/ppermute | solution.py:625
  207.9 39.0 %collective-permute-start.32 = (bf16[3,256,512]{2,1,0:T(8,128)(2,1)}, bf16[3,256,512]{2,1,0:T(8,128)(2,1)}, u32[]{:S(2)}, u32[]{:S(2)}) collective-permute-start(bf16[3,256,512]{2,1,0:T(8,128)(2,1)} %collective-permute-done.31.refs_1_.refs_5_), channel_id=1, source_target_pairs={{0,1},{2,0},{4,2},{6,4},{7,6},{5,7},{3,5},{1,3},{8,9},{10,8},{12,1... | collective-permute-start | bytes 2359304 | tf_op jit(solution)/shard_map/ppermute | solution.py:625
  210.5 36.4 %collective-permute-start.29 = (bf16[3,256,512]{2,1,0:T(8,128)(2,1)}, bf16[3,256,512]{2,1,0:T(8,128)(2,1)}, u32[]{:S(2)}, u32[]{:S(2)}) collective-permute-start(bf16[3,256,512]{2,1,0:T(8,128)(2,1)} %collective-permute-done.28.refs_0_.refs_4_), channel_id=1, source_target_pairs={{0,2},{2,4},{4,6},{6,7},{7,5},{5,3},{3,1},{1,0},{8,10},{10,12},{12... | collective-permute-start | bytes 2359304 | tf_op jit(solution)/shard_map/ppermute | solution.py:625
  224.8 33.8 %collective-permute-start.40 = (bf16[3,256,512]{2,1,0:T(8,128)(2,1)}, bf16[3,256,512]{2,1,0:T(8,128)(2,1)}, u32[]{:S(2)}, u32[]{:S(2)}) collective-permute-start(bf16[3,256,512]{2,1,0:T(8,128)(2,1)} %collective-permute-done.39.refs_1_.refs_5_), channel_id=1, source_target_pairs={{0,1},{2,0},{4,2},{6,4},{7,6},{5,7},{3,5},{1,3},{8,9},{10,8},{12,1... | collective-permute-start | bytes 2359304 | tf_op jit(solution)/shard_map/ppermute | solution.py:625
  227.4 33.7 %collective-permute-start.37 = (bf16[3,256,512]{2,1,0:T(8,128)(2,1)}, bf16[3,256,512]{2,1,0:T(8,128)(2,1)}, u32[]{:S(2)}, u32[]{:S(2)}) collective-permute-start(bf16[3,256,512]{2,1,0:T(8,128)(2,1)} %collective-permute-done.36.refs_0_.refs_4_), channel_id=1, source_target_pairs={{0,2},{2,4},{4,6},{6,7},{7,5},{5,3},{3,1},{1,0},{8,10},{10,12},{12... | collective-permute-start | bytes 2359304 | tf_op jit(solution)/shard_map/ppermute | solution.py:625
  230.2 12.9 %copy-start.6 = (bf16[3,256,512]{2,1,0:T(8,128)(2,1)S(1)}, bf16[3,256,512]{2,1,0:T(8,128)(2,1)}, u32[]{:S(2)}) copy-start(bf16[3,256,512]{2,1,0:T(8,128)(2,1)} %copy-done.5) | copy-start | bytes 2359300
  230.2 12.9 %copy-start.8 = (bf16[3,256,512]{2,1,0:T(8,128)(2,1)S(1)}, bf16[3,256,512]{2,1,0:T(8,128)(2,1)}, u32[]{:S(2)}) copy-start(bf16[3,256,512]{2,1,0:T(8,128)(2,1)} %copy-done.7) | copy-start | bytes 2359300
  230.2 12.9 %copy-start.10 = (bf16[3,256,512]{2,1,0:T(8,128)(2,1)S(1)}, bf16[3,256,512]{2,1,0:T(8,128)(2,1)}, u32[]{:S(2)}) copy-start(bf16[3,256,512]{2,1,0:T(8,128)(2,1)} %copy-done.9) | copy-start | bytes 2359300
  230.2 1.6 collective-permute-start.25
  232.7 5.6 %collective-permute-start.26 = (f32[256,1]{1,0:T(8,128)S(1)}, f32[256,1]{1,0:T(8,128)S(1)}, u32[]{:S(2)}, u32[]{:S(2)}) collective-permute-start(f32[256,1]{1,0:T(8,128)S(1)} %add.31), channel_id=1, source_target_pairs={{0,16},{8,24},{16,0},{24,8},{1,17},{9,25},{17,1},{25,9},{2,18},{10... | collective-permute-start | bytes 3080 | tf_op jit(solution)/shard_map/ppermute | solution.py:628
  248.3 21.1 %collective-permute-start.33 = (bf16[3,128,512]{2,1,0:T(8,128)(2,1)S(1)}, bf16[3,128,512]{2,1,0:T(8,128)(2,1)S(1)}, u32[]{:S(2)}, u32[]{:S(2)}) collective-permute-start(bf16[3,128,512]{2,1,0:T(8,128)(2,1)S(1)} %get-tuple-element.100), channel_id=1, source_target_pairs={{0,2},{2,4},{4,6},{6,7},{7,5},{5,3},{3,1},{1,0},{8,10},{10,12},{12... | collective-permute-start | bytes 1179656 | tf_op jit(solution)/shard_map/ppermute | solution.py:625
  249.6 19.8 %collective-permute-start.34 = (bf16[3,128,512]{2,1,0:T(8,128)(2,1)S(1)}, bf16[3,128,512]{2,1,0:T(8,128)(2,1)S(1)}, u32[]{:S(2)}, u32[]{:S(2)}) collective-permute-start(bf16[3,128,512]{2,1,0:T(8,128)(2,1)S(1)} %get-tuple-element.101), channel_id=1, source_target_pairs={{0,1},{2,0},{4,2},{6,4},{7,6},{5,7},{3,5},{1,3},{8,9},{10,8},{12,1... | collective-permute-start | bytes 1179656 | tf_op jit(solution)/shard_map/ppermute | solution.py:625
  262.5 14.5 %collective-permute-start.41 = (bf16[3,128,512]{2,1,0:T(8,128)(2,1)S(1)}, bf16[3,128,512]{2,1,0:T(8,128)(2,1)S(1)}, u32[]{:S(2)}, u32[]{:S(2)}) collective-permute-start(bf16[3,128,512]{2,1,0:T(8,128)(2,1)S(1)} %get-tuple-element.115), channel_id=1, source_target_pairs={{0,2},{2,4},{4,6},{6,7},{7,5},{5,3},{3,1},{1,0},{8,10},{10,12},{12... | collective-permute-start | bytes 1179656 | tf_op jit(solution)/shard_map/ppermute | solution.py:625
  262.6 14.5 %collective-permute-start.42 = (bf16[3,128,512]{2,1,0:T(8,128)(2,1)S(1)}, bf16[3,128,512]{2,1,0:T(8,128)(2,1)S(1)}, u32[]{:S(2)}, u32[]{:S(2)}) collective-permute-start(bf16[3,128,512]{2,1,0:T(8,128)(2,1)S(1)} %get-tuple-element.116), channel_id=1, source_target_pairs={{0,1},{2,0},{4,2},{6,4},{7,6},{5,7},{3,5},{1,3},{8,9},{10,8},{12,1... | collective-permute-start | bytes 1179656 | tf_op jit(solution)/shard_map/ppermute | solution.py:625
  277.1 2.3 copy-start.22
  277.1 7.1 %copy-start.19 = (bf16[3,256,512]{2,1,0:T(8,128)(2,1)S(1)}, bf16[3,256,512]{2,1,0:T(8,128)(2,1)}, u32[]{:S(2)}) copy-start(bf16[3,256,512]{2,1,0:T(8,128)(2,1)} %copy-done.17) | copy-start | bytes 2359300
  278.7 5.4 %copy-start.1 = (bf16[512,2048]{1,0:T(8,128)(2,1)S(1)}, bf16[512,2048]{1,0:T(8,128)(2,1)}, u32[]{:S(2)}) copy-start(bf16[512,2048]{1,0:T(8,128)(2,1)} %copy-done) | copy-start | bytes 6291460
  278.7 5.4 %copy-start.13 = (bf16[3,256,512]{2,1,0:T(8,128)(2,1)S(1)}, bf16[3,256,512]{2,1,0:T(8,128)(2,1)}, u32[]{:S(2)}) copy-start(bf16[3,256,512]{2,1,0:T(8,128)(2,1)} %copy-done.11) | copy-start | bytes 2359300
  278.7 5.4 %copy-start.16 = (bf16[3,256,512]{2,1,0:T(8,128)(2,1)S(1)}, bf16[3,256,512]{2,1,0:T(8,128)(2,1)}, u32[]{:S(2)}) copy-start(bf16[3,256,512]{2,1,0:T(8,128)(2,1)} %copy-done.14) | copy-start | bytes 2359300
  278.7 2.0 collective-permute-start.43
  278.8 3.1 %collective-permute-start.47 = (bf16[4,128,512]{2,1,0:T(8,128)(2,1)S(1)}, bf16[4,128,512]{2,1,0:T(8,128)(2,1)S(1)}, u32[]{:S(2)}, u32[]{:S(2)}) collective-permute-start(bf16[4,128,512]{2,1,0:T(8,128)(2,1)S(1)} %get-tuple-element.128), channel_id=1, source_target_pairs={{0,8},{8,0},{16,24},{24,16},{1,9},{9,1},{17,25},{25,17},{2,10},{10... | collective-permute-start | bytes 1572872 | tf_op jit(solution)/shard_map/ppermute | solution.py:628
  281.4 9.2 %collective-permute-start.44 = (bf16[2,128,512]{2,1,0:T(8,128)(2,1)S(1)}, bf16[2,128,512]{2,1,0:T(8,128)(2,1)S(1)}, u32[]{:S(2)}, u32[]{:S(2)}) collective-permute-start(bf16[2,128,512]{2,1,0:T(8,128)(2,1)S(1)} %get-tuple-element.124), channel_id=1, source_target_pairs={{0,16},{8,24},{16,0},{24,8},{1,17},{9,25},{17,1},{25,9},{2,18},{10... | collective-permute-start | bytes 786440 | tf_op jit(solution)/shard_map/ppermute | solution.py:628
  282.6 12.8 %collective-permute-start.48 = (bf16[2,128,512]{2,1,0:T(8,128)(2,1)S(1)}, bf16[2,128,512]{2,1,0:T(8,128)(2,1)S(1)}, u32[]{:S(2)}, u32[]{:S(2)}) collective-permute-start(bf16[2,128,512]{2,1,0:T(8,128)(2,1)S(1)} %get-tuple-element.130), channel_id=1, source_target_pairs={{0,16},{8,24},{16,0},{24,8},{1,17},{9,25},{17,1},{25,9},{2,18},{10... | collective-permute-start | bytes 786440 | tf_op jit(solution)/shard_map/ppermute | solution.py:628
  291.2 17.4 %collective-permute-start.46 = (bf16[128,512]{1,0:T(8,128)(2,1)S(1)}, bf16[128,512]{1,0:T(8,128)(2,1)S(1)}, u32[]{:S(2)}, u32[]{:S(2)}) collective-permute-start(bf16[128,512]{1,0:T(8,128)(2,1)S(1)} %get-tuple-element.126), channel_id=1, source_target_pairs={{0,1},{1,0},{2,9},{3,8},{4,17},{5,16},{6,25},{7,24},{8,5},{9,4},{1... | collective-permute-start | bytes 393224 | tf_op jit(solution)/shard_map/ppermute | solution.py:686
  291.2 17.3 %collective-permute-start.45 = (bf16[128,512]{1,0:T(8,128)(2,1)S(1)}, bf16[128,512]{1,0:T(8,128)(2,1)S(1)}, u32[]{:S(2)}, u32[]{:S(2)}) collective-permute-start(bf16[128,512]{1,0:T(8,128)(2,1)S(1)} %get-tuple-element.125.refs_11_), channel_id=1, source_target_pairs={{0,0},{1,1},{2,8},{3,9},{4,16},{5,17},{6,24},{7,25},{8,4},{9,5},{1... | collective-permute-start | bytes 393224 | tf_op jit(solution)/shard_map/ppermute | solution.py:686
  296.0 12.6 %collective-permute-start.50 = (bf16[128,512]{1,0:T(8,128)(2,1)S(1)}, bf16[128,512]{1,0:T(8,128)(2,1)S(1)}, u32[]{:S(2)}, u32[]{:S(2)}) collective-permute-start(bf16[128,512]{1,0:T(8,128)(2,1)S(1)} %get-tuple-element.132), channel_id=1, source_target_pairs={{0,1},{1,0},{2,9},{3,8},{4,17},{5,16},{6,25},{7,24},{8,5},{9,4},{1... | collective-permute-start | bytes 393224 | tf_op jit(solution)/shard_map/ppermute | solution.py:686
  297.6 11.0 %copy-start.3 = (bf16[256,4096]{1,0:T(8,128)(2,1)S(1)}, bf16[256,4096]{1,0:T(8,128)(2,1)}, u32[]{:S(2)}) copy-start(bf16[256,4096]{1,0:T(8,128)(2,1)} %tokens.3) | copy-start | bytes 6291460
  297.6 11.0 %copy-start.24 = (f32[256,128]{1,0:T(8,128)S(1)}, f32[256,128]{1,0:T(8,128)}, u32[]{:S(2)}) copy-start(f32[256,128]{1,0:T(8,128)} %copy-done.23) | copy-start | bytes 393220
  297.6 11.0 %collective-permute-start.49 = (bf16[128,512]{1,0:T(8,128)(2,1)S(1)}, bf16[128,512]{1,0:T(8,128)(2,1)S(1)}, u32[]{:S(2)}, u32[]{:S(2)}) collective-permute-start(bf16[128,512]{1,0:T(8,128)(2,1)S(1)} %get-tuple-element.131.refs_12_), channel_id=1, source_target_pairs={{0,0},{1,1},{2,8},{3,9},{4,16},{5,17},{6,24},{7,25},{8,4},{9,5},{1... | collective-permute-start | bytes 393224 | tf_op jit(solution)/shard_map/ppermute | solution.py:686
  (15 other events, 14.8 us)

commit v13 on v12

--- a/solution.py
+++ b/solution.py
@@ -425,8 +425,10 @@
 
 
 def grads_kernel(turned, *refs):
-    blocks = jnp.concatenate([piece[0] for piece in refs[:-1]], axis=0)
-    refs[-1][0] = mm(turned[...], blocks)
+    pieces, out, token = refs[:-2], refs[-2], refs[-1]
+    blocks = jnp.concatenate([piece[0] for piece in pieces], axis=0)
+    out[0] = mm(turned[...], blocks)
+    token[...] = jnp.zeros_like(token)
 
 
 def grads_chunk(turned, pieces, before, ties, chunk, wide, columns):
@@ -441,8 +443,14 @@
             *[pl.BlockSpec((1, *piece.shape[1:]), lambda m: (m, 0, 0)) for piece in pieces],
             *tie_specs(ties),
         ],
-        out_specs=pl.BlockSpec((1, depth, wide), lambda m: (m, 0, chunk)),
-        out_shape=jax.ShapeDtypeStruct((3, depth, columns), jnp.float32),
+        out_specs=[
+            pl.BlockSpec((1, depth, wide), lambda m: (m, 0, chunk)),
+            pl.BlockSpec((8, 128), lambda m: (0, 0)),
+        ],
+        out_shape=[
+            jax.ShapeDtypeStruct((3, depth, columns), jnp.float32),
+            jax.ShapeDtypeStruct((8, 128), jnp.float32),
+        ],
         input_output_aliases=aliases,
         compiler_params=params(24),
         cost_estimate=cost(6 * span * depth * wide, 6 * span * wide + 12 * depth * wide),
@@ -500,21 +508,23 @@
                 sends[part][idx[3 * count + 1 + place]] = total.astype(jnp.bfloat16)
 
 
-def term_last(idx, turned, befores, pieces, nears):
+def term_last(idx, turned, befores, pieces, nears, ties):
     count = len(nears) + 1
     rows, depth = nears[0].shape
     whole = pl.BlockSpec(memory_space=pltpu.VMEM)
     shape = (count // 2, rows // 2, depth)
     return pl.pallas_call(
-        functools.partial(term_last_kernel, count),
-        in_specs=[pl.BlockSpec(memory_space=pltpu.SMEM)] + [whole] * (count + 4),
+        tied(functools.partial(term_last_kernel, count), count + 5, len(ties)),
+        in_specs=[pl.BlockSpec(memory_space=pltpu.SMEM)]
+        + [whole] * (count + 4)
+        + tie_specs(ties),
         out_specs=[whole] * 4,
         out_shape=[jax.ShapeDtypeStruct(shape, jnp.float32)] * 2
         + [jax.ShapeDtypeStruct(shape, jnp.bfloat16)] * 2,
         compiler_params=pltpu.CompilerParams(vmem_limit_bytes=12 * MIB),
         cost_estimate=cost(rows * depth * depth, 12 * count * rows * depth),
         name="term_last",
-    )(idx, turned, *befores, *pieces, *nears)
+    )(idx, turned, *befores, *pieces, *nears, *ties)
 
 
 def split_kernel(column, group, idx, keep, came, keep_out, send_out):
@@ -705,16 +715,17 @@
                 terms[chunk] += term_step(turned, pieces, befores, chunk)
             elif chunk == 0:
                 lasts = term_step(turned, [right, left], [], 0)
-    keep_0, keep_1, send_0, send_1 = term_last(idx, turned, lasts, gathered[1][-2:], terms[1])
+    grads, done = grads_chunk(rows_turned, gathered[0], None, [], 0, wide, columns)
+    keep_0, keep_1, send_0, send_1 = term_last(
+        idx, turned, lasts, gathered[1][-2:], terms[1], [done]
+    )
     first, second = sum_nodes(keep_0, send_0), sum_nodes(keep_1, send_1)
     came = [*relocate(first), *relocate(second)]
     column = idx.shape[0] - 1 - group
     d_tokens = finish(
         idx, column, tokens, norm_gain[None], inverse_rms, dots, came, width // nodes
     )
-    grads = grads_chunk(rows_turned, gathered[0], None, [keep_1], 0, wide, columns)
-    sums = [first[0], second[0]]
-    grads = grads_chunk(rows_turned, gathered[1], grads, sums, 1, wide, columns)
+    grads, _ = grads_chunk(rows_turned, gathered[1], grads, [keep_1], 1, wide, columns)
     return (jnp.concatenate(outputs, axis=-1), d_tokens, grads)
 
 

time: 316 us -> 317 us (level)
  the two profiles are of different devices: /device:TPU:2 before, /device:TPU:1 now
where the time goes in v13:
time: 317 us; the launch traced here: 316 us
  waiting for transfers between devices  156 us (49%)
  starting transfers between devices  69.8 us (22%)
  Pallas kernels  66.4 us (21%)
  local copies, waits for them, and re-layouts  18.4 us (6%)
  other arithmetic  4.52 us (1%)
    ppermute x39, waiting for transfers between devices, shift(): return lax.ppermute(array, 'local', moves)  140 us
    ppermute x39, starting transfers between devices, shift(): return lax.ppermute(array, 'local', moves)  47.4 us
    unnamed x56, local copies, waits for them, and re-layouts  16.2 us
    pallas_call x2, Pallas kernels, attention(): pl.pallas_call(attention_kernel, grid_spec=pltpu.PrefetchScalarGridSpec(n...  14.5 us
    pallas_call x7, Pallas kernels, term_step(): pl.pallas_call(kernel, in_specs=[whole] * (1 + count + len(befores)), out...  12.8 us
    pallas_call x2, Pallas kernels, grads_chunk(): pl.pallas_call(tied(grads_kernel, 1 + len(pieces), len(ties)), grid=(3,),...  12.7 us
    pallas_call x6, Pallas kernels, sum_step(): pl.pallas_call(tied(sum_step_kernel, 9, len(ties)), grid_spec=pltpu.Prefe...  12.3 us
    ppermute x4, starting transfers between devices, relocate(): came.append(lax.ppermute(block, ('node', 'local'), moves))  12.3 us
  transfers between devices with their start and end apart: 51, of which 23 were waited for; matrix products, arithmetic and copies ran while one was open for 2% of the time, Pallas kernels for 20%

profile of v13, /device:TPU:1, one launch (start us, length us, event | category | flops | bytes accessed | tf_op | source)
XLA Modules:
  0.0 316.0 jit_solution(13318911497978928650)
XLA Ops:
  2.0 1.6 copy-done.2
  5.7 5.1 %collective-permute-start.6 = (bf16[256,256]{1,0:T(8,128)(2,1)S(1)}, bf16[256,256]{1,0:T(8,128)(2,1)S(1)}, u32[]{:S(2)}, u32[]{:S(2)}) collective-permute-start(bf16[256,256]{1,0:T(8,128)(2,1)S(1)} %get-tuple-element.78), channel_id=1, source_target_pairs={{0,7},{2,5},{4,3},{6,1},{7,0},{5,2},{3,4},{1,6},{8,15},{10,13},{12... | collective-permute-start | bytes 393224 | tf_op jit(solution)/shard_map/ppermute | solution.py:635
  10.8 3.3 %collective-permute-done.6.mine.mine_far = bf16[256,256]{1,0:T(8,128)(2,1)S(1)} collective-permute-done((bf16[256,256]{1,0:T(8,128)(2,1)S(1)}, bf16[256,256]{1,0:T(8,128)(2,1)S(1)}, u32[]{:S(2)}, u32[]{:S(2)}) %collective-permute-start.6) | collective-permute-done | bytes 131104 | tf_op jit(solution)/shard_map/ppermute | solution.py:635
  14.1 2.1 collective-permute-start.7
  16.5 3.2 %collective-permute-start.2 = (bf16[256,256]{1,0:T(8,128)(2,1)S(1)}, bf16[256,256]{1,0:T(8,128)(2,1)S(1)}, u32[]{:S(2)}, u32[]{:S(2)}) collective-permute-start(bf16[256,256]{1,0:T(8,128)(2,1)S(1)} %get-tuple-element.74), channel_id=1, source_target_pairs={{0,4},{2,6},{4,7},{6,5},{7,3},{5,1},{3,0},{1,2},{8,12},{10,14},{12... | collective-permute-start | bytes 393224 | tf_op jit(solution)/shard_map/ppermute | solution.py:635
  22.1 2.1 collective-permute-start.5
  24.1 1.9 copy-done.4
  27.8 1.9 sum_first.1
  30.7 4.0 %collective-permute-done.5.refs_6_ = bf16[256,256]{1,0:T(8,128)(2,1)S(1)} collective-permute-done((bf16[256,256]{1,0:T(8,128)(2,1)S(1)}, bf16[256,256]{1,0:T(8,128)(2,1)S(1)}, u32[]{:S(2)}, u32[]{:S(2)}) %collective-permute-start.5) | collective-permute-done | bytes 131104 | tf_op jit(solution)/shard_map/ppermute | solution.py:635
  34.7 2.0 collective-permute-start.8
  36.7 2.8 collective-permute-start.10
  39.5 1.5 collective-permute-start.18
  41.0 7.9 %collective-permute-done.9.refs_7_ = bf16[3,128,512]{2,1,0:T(8,128)(2,1)S(1)} collective-permute-done((bf16[3,128,512]{2,1,0:T(8,128)(2,1)S(1)}, bf16[3,128,512]{2,1,0:T(8,128)(2,1)S(1)}, u32[]{:S(2)}, u32[]{:S(2)}) %collective-permute-start.9) | collective-permute-done | bytes 393248 | tf_op jit(solution)/shard_map/ppermute | solution.py:635
  48.9 2.1 sum_step.6
  51.0 2.5 collective-permute-start.11
  53.5 3.9 %collective-permute-done.17.refs_7_ = bf16[3,128,512]{2,1,0:T(8,128)(2,1)S(1)} collective-permute-done((bf16[3,128,512]{2,1,0:T(8,128)(2,1)S(1)}, bf16[3,128,512]{2,1,0:T(8,128)(2,1)S(1)}, u32[]{:S(2)}, u32[]{:S(2)}) %collective-permute-start.17) | collective-permute-done | bytes 393248 | tf_op jit(solution)/shard_map/ppermute | solution.py:635
  57.4 2.1 sum_step.9
  59.4 2.5 collective-permute-start.19
  61.9 12.3 %collective-permute-done.11.refs_7_ = bf16[3,256,512]{2,1,0:T(8,128)(2,1)S(1)} collective-permute-done((bf16[3,256,512]{2,1,0:T(8,128)(2,1)S(1)}, bf16[3,256,512]{2,1,0:T(8,128)(2,1)S(1)}, u32[]{:S(2)}, u32[]{:S(2)}) %collective-permute-start.11) | collective-permute-done | bytes 786464 | tf_op jit(solution)/shard_map/ppermute | solution.py:635
  74.2 2.1 sum_step.7
  76.3 2.5 collective-permute-start.13
  78.8 12.3 %collective-permute-done.19.refs_7_ = bf16[3,256,512]{2,1,0:T(8,128)(2,1)S(1)} collective-permute-done((bf16[3,256,512]{2,1,0:T(8,128)(2,1)S(1)}, bf16[3,256,512]{2,1,0:T(8,128)(2,1)S(1)}, u32[]{:S(2)}, u32[]{:S(2)}) %collective-permute-start.19) | collective-permute-done | bytes 786464 | tf_op jit(solution)/shard_map/ppermute | solution.py:635
  91.1 2.1 sum_step.10
  93.1 2.5 collective-permute-start.21
  96.8 11.1 %collective-permute-done.13.refs_7_ = bf16[3,256,512]{2,1,0:T(8,128)(2,1)S(1)} collective-permute-done((bf16[3,256,512]{2,1,0:T(8,128)(2,1)S(1)}, bf16[3,256,512]{2,1,0:T(8,128)(2,1)S(1)}, u32[]{:S(2)}, u32[]{:S(2)}) %collective-permute-start.13) | collective-permute-done | bytes 786464 | tf_op jit(solution)/shard_map/ppermute | solution.py:635
  107.9 2.1 sum_step.8
  110.0 2.5 collective-permute-start.15
  112.5 12.3 %collective-permute-done.21.refs_7_ = bf16[3,256,512]{2,1,0:T(8,128)(2,1)S(1)} collective-permute-done((bf16[3,256,512]{2,1,0:T(8,128)(2,1)S(1)}, bf16[3,256,512]{2,1,0:T(8,128)(2,1)S(1)}, u32[]{:S(2)}, u32[]{:S(2)}) %collective-permute-start.21) | collective-permute-done | bytes 786464 | tf_op jit(solution)/shard_map/ppermute | solution.py:635
  124.8 2.1 sum_step.11
  126.8 2.5 collective-permute-start.23
  130.0 11.6 %collective-permute-done.15.from_left = bf16[3,256,512]{2,1,0:T(8,128)(2,1)S(1)} collective-permute-done((bf16[3,256,512]{2,1,0:T(8,128)(2,1)S(1)}, bf16[3,256,512]{2,1,0:T(8,128)(2,1)S(1)}, u32[]{:S(2)}, u32[]{:S(2)}) %collective-permute-start.15) | collective-permute-done | bytes 786464 | tf_op jit(solution)/shard_map/ppermute | solution.py:635
  141.6 7.2 %attention.2 = (bf16[256,512]{1,0:T(8,128)(2,1)S(1)}, f32[256,128]{1,0:T(8,128)S(1)}, bf16[3,256,512]{2,1,0:T(8,128)(2,1)S(1)}) custom-call(s32[39]{0:T(128)S(1)} %dynamic-slice_bitcast_fusion.idx.refs_0_, bf16[7,256,256]{2,1,0:T(8,128)(2,1)S(1)} %stack.1.refs_1_.refs_3_.mine, bf16[7,256,256]{2,1,0:T(8,128)(2,1)S(1)} %collective-permute-done.8.refs_2_.refs_4_.other, ...), custom_call_target="tpu_custom_call" | custom-call | flops 402653184 | bytes 3145728 | tf_op jit(solution)/shard_map/attention/pallas_call | solution.py:394
  149.5 2.4 collective-permute-start.27
  151.9 6.5 %collective-permute-done.23.from_left = bf16[3,256,512]{2,1,0:T(8,128)(2,1)S(1)} collective-permute-done((bf16[3,256,512]{2,1,0:T(8,128)(2,1)S(1)}, bf16[3,256,512]{2,1,0:T(8,128)(2,1)S(1)}, u32[]{:S(2)}, u32[]{:S(2)}) %collective-permute-start.23) | collective-permute-done | bytes 786464 | tf_op jit(solution)/shard_map/ppermute | solution.py:635
  158.5 7.3 %attention.3 = (bf16[256,512]{1,0:T(8,128)(2,1)S(1)}, f32[256,128]{1,0:T(8,128)S(1)}, bf16[3,256,512]{2,1,0:T(8,128)(2,1)S(1)}) custom-call(s32[39]{0:T(128)S(1)} %dynamic-slice_bitcast_fusion.idx.refs_0_, bf16[7,256,256]{2,1,0:T(8,128)(2,1)S(1)} %stack.1.refs_1_.refs_3_.mine, bf16[7,256,256]{2,1,0:T(8,128)(2,1)S(1)} %collective-permute-done.8.refs_2_.refs_4_.other, ...), custom_call_target="tpu_custom_call" | custom-call | flops 402653184 | bytes 3145728 | tf_op jit(solution)/shard_map/attention/pallas_call | solution.py:394
  167.1 2.4 collective-permute-start.35
  170.5 4.8 %collective-permute-done.27.refs_1_.refs_2_ = bf16[3,256,512]{2,1,0:T(8,128)(2,1)S(1)} collective-permute-done((bf16[3,256,512]{2,1,0:T(8,128)(2,1)S(1)}, bf16[3,256,512]{2,1,0:T(8,128)(2,1)S(1)}, u32[]{:S(2)}, u32[]{:S(2)}) %collective-permute-start.27) | collective-permute-done | bytes 786464 | tf_op jit(solution)/shard_map/ppermute | solution.py:635
  176.2 1.5 collective-permute-start.31
  178.6 13.6 %collective-permute-done.35.refs_1_.refs_2_ = bf16[3,256,512]{2,1,0:T(8,128)(2,1)S(1)} collective-permute-done((bf16[3,256,512]{2,1,0:T(8,128)(2,1)S(1)}, bf16[3,256,512]{2,1,0:T(8,128)(2,1)S(1)}, u32[]{:S(2)}, u32[]{:S(2)}) %collective-permute-start.35) | collective-permute-done | bytes 786464 | tf_op jit(solution)/shard_map/ppermute | solution.py:635
  193.1 1.5 collective-permute-start.39
  195.5 13.7 %collective-permute-done.28.refs_0_.refs_4_ = bf16[3,256,512]{2,1,0:T(8,128)(2,1)} collective-permute-done((bf16[3,256,512]{2,1,0:T(8,128)(2,1)S(1)}, bf16[3,256,512]{2,1,0:T(8,128)(2,1)}, u32[]{:S(2)}, u32[]{:S(2)}) %collective-permute-start.28) | collective-permute-done | bytes 786464 | tf_op jit(solution)/shard_map/ppermute | solution.py:635
  209.2 1.5 collective-permute-start.32
  210.6 15.4 %collective-permute-done.36.refs_0_.refs_4_ = bf16[3,256,512]{2,1,0:T(8,128)(2,1)} collective-permute-done((bf16[3,256,512]{2,1,0:T(8,128)(2,1)S(1)}, bf16[3,256,512]{2,1,0:T(8,128)(2,1)}, u32[]{:S(2)}, u32[]{:S(2)}) %collective-permute-start.36) | collective-permute-done | bytes 786464 | tf_op jit(solution)/shard_map/ppermute | solution.py:635
  226.0 1.5 collective-permute-start.40
  230.3 1.5 collective-permute-start.25
  235.2 3.6 %collective-permute-done.26 = f32[256,1]{1,0:T(8,128)S(1)} collective-permute-done((f32[256,1]{1,0:T(8,128)S(1)}, f32[256,1]{1,0:T(8,128)S(1)}, u32[]{:S(2)}, u32[]{:S(2)}) %collective-permute-start.26) | collective-permute-done | bytes 1056 | tf_op jit(solution)/shard_map/ppermute | solution.py:638
  245.1 1.7 collective-permute-start.33
  248.4 2.3 term_step.10
  250.8 2.3 term_step.11
  253.1 6.6 %collective-permute-done.37.refs_0_.refs_6_ = bf16[3,256,512]{2,1,0:T(8,128)(2,1)} collective-permute-done((bf16[3,256,512]{2,1,0:T(8,128)(2,1)}, bf16[3,256,512]{2,1,0:T(8,128)(2,1)}, u32[]{:S(2)}, u32[]{:S(2)}) %collective-permute-start.37) | collective-permute-done | bytes 786464 | tf_op jit(solution)/shard_map/ppermute | solution.py:635
  261.1 2.5 collective-permute-start.41
  263.6 2.3 term_step.12
  266.0 2.4 term_step.13
  270.4 6.3 %grads.2 = (f32[3,512,1024]{2,1,0:T(8,128)}, f32[8,128]{1,0:T(8,128)S(1)}) custom-call(bf16[512,2048]{1,0:T(8,128)(2,1)S(1)} %copy-done.1, bf16[3,256,512]{2,1,0:T(8,128)(2,1)S(1)} %copy-done.14, bf16[3,256,512]{2,1,0:T(8,128)(2,1)S(1)} %copy-done.17, bf16[3,256,512]{2,1,0:T(8,128)(2,1)S(1)} %copy-done.20, ...), custom_call_target="tpu_custom_call" | custom-call | flops 3221225472 | bytes 9437184 | tf_op jit(solution)/shard_map/grads/pallas_call | solution.py:438
  276.7 1.7 term_last.1
  278.3 1.6 collective-permute-start.47
  280.0 1.5 collective-permute-done.47.came
  285.2 4.5 %collective-permute-done.48.came = bf16[2,128,512]{2,1,0:T(8,128)(2,1)S(1)} collective-permute-done((bf16[2,128,512]{2,1,0:T(8,128)(2,1)S(1)}, bf16[2,128,512]{2,1,0:T(8,128)(2,1)S(1)}, u32[]{:S(2)}, u32[]{:S(2)}) %collective-permute-start.48) | collective-permute-done | bytes 262176 | tf_op jit(solution)/shard_map/ppermute | solution.py:638
  290.3 7.1 %collective-permute-start.49 = (bf16[128,512]{1,0:T(8,128)(2,1)S(1)}, bf16[128,512]{1,0:T(8,128)(2,1)S(1)}, u32[]{:S(2)}, u32[]{:S(2)}) collective-permute-start(bf16[128,512]{1,0:T(8,128)(2,1)S(1)} %get-tuple-element.135), channel_id=1, source_target_pairs={{0,0},{1,1},{2,8},{3,9},{4,16},{5,17},{6,24},{7,25},{8,4},{9,5},{1... | collective-permute-start | bytes 393224 | tf_op jit(solution)/shard_map/ppermute | solution.py:696
  298.8 3.8 %collective-permute-start.45 = (bf16[128,512]{1,0:T(8,128)(2,1)S(1)}, bf16[128,512]{1,0:T(8,128)(2,1)S(1)}, u32[]{:S(2)}, u32[]{:S(2)}) collective-permute-start(bf16[128,512]{1,0:T(8,128)(2,1)S(1)} %get-tuple-element.129), channel_id=1, source_target_pairs={{0,0},{1,1},{2,8},{3,9},{4,16},{5,17},{6,24},{7,25},{8,4},{9,5},{1... | collective-permute-start | bytes 393224 | tf_op jit(solution)/shard_map/ppermute | solution.py:696
  303.3 6.4 %grads.3 = (f32[3,512,1024]{2,1,0:T(8,128)}, f32[8,128]{1,0:T(8,128)}) custom-call(bf16[512,2048]{1,0:T(8,128)(2,1)S(1)} %copy-done.1, bf16[3,256,512]{2,1,0:T(8,128)(2,1)S(1)} %copy-done.6, bf16[3,256,512]{2,1,0:T(8,128)(2,1)S(1)} %copy-done.8, bf16[3,256,512]{2,1,0:T(8,128)(2,1)S(1)} %copy-done.10, ...), custom_call_target="tpu_custom_call", output_to_operand_aliasing={{0}: (10, {})} | custom-call | flops 3221225472 | bytes 9437184 | tf_op jit(solution)/shard_map/grads/pallas_call | solution.py:438
  310.1 2.5 collective-permute-done.45.refs_0_
  312.6 1.7 collective-permute-done.46.refs_1_
  314.3 1.6 finish.1
  (137 shorter events, 41.8 us)
Async XLA Ops:
  5.7 8.4 %collective-permute-start.6 = (bf16[256,256]{1,0:T(8,128)(2,1)S(1)}, bf16[256,256]{1,0:T(8,128)(2,1)S(1)}, u32[]{:S(2)}, u32[]{:S(2)}) collective-permute-start(bf16[256,256]{1,0:T(8,128)(2,1)S(1)} %get-tuple-element.78), channel_id=1, source_target_pairs={{0,7},{2,5},{4,3},{6,1},{7,0},{5,2},{3,4},{1,6},{8,15},{10,13},{12... | collective-permute-start | bytes 393224 | tf_op jit(solution)/shard_map/ppermute | solution.py:635
  10.8 10.0 %collective-permute-start = (bf16[256,256]{1,0:T(8,128)(2,1)S(1)}, bf16[256,256]{1,0:T(8,128)(2,1)S(1)}, u32[]{:S(2)}, u32[]{:S(2)}) collective-permute-start(bf16[256,256]{1,0:T(8,128)(2,1)S(1)} %get-tuple-element.72), channel_id=1, source_target_pairs={{0,2},{2,4},{4,6},{6,7},{7,5},{5,3},{3,1},{1,0},{8,10},{10,12},{12... | collective-permute-start | bytes 393224 | tf_op jit(solution)/shard_map/ppermute | solution.py:635
  14.1 8.0 %collective-permute-start.7 = (bf16[256,256]{1,0:T(8,128)(2,1)S(1)}, bf16[256,256]{1,0:T(8,128)(2,1)S(1)}, u32[]{:S(2)}, u32[]{:S(2)}) collective-permute-start(bf16[256,256]{1,0:T(8,128)(2,1)S(1)} %collective-permute-done.6.mine.mine_far), channel_id=1, source_target_pairs={{0,8},{8,0},{16,24},{24,16},{1,9},{9,1},{17,25},{25,17},{2,10},{10... | collective-permute-start | bytes 393224 | tf_op jit(solution)/shard_map/ppermute | solution.py:638
  16.2 13.6 %collective-permute-start.1 = (bf16[256,256]{1,0:T(8,128)(2,1)S(1)}, bf16[256,256]{1,0:T(8,128)(2,1)S(1)}, u32[]{:S(2)}, u32[]{:S(2)}) collective-permute-start(bf16[256,256]{1,0:T(8,128)(2,1)S(1)} %get-tuple-element.73), channel_id=1, source_target_pairs={{0,1},{2,0},{4,2},{6,4},{7,6},{5,7},{3,5},{1,3},{8,9},{10,8},{12,1... | collective-permute-start | bytes 393224 | tf_op jit(solution)/shard_map/ppermute | solution.py:635
  16.5 13.3 %collective-permute-start.2 = (bf16[256,256]{1,0:T(8,128)(2,1)S(1)}, bf16[256,256]{1,0:T(8,128)(2,1)S(1)}, u32[]{:S(2)}, u32[]{:S(2)}) collective-permute-start(bf16[256,256]{1,0:T(8,128)(2,1)S(1)} %get-tuple-element.74), channel_id=1, source_target_pairs={{0,4},{2,6},{4,7},{6,5},{7,3},{5,1},{3,0},{1,2},{8,12},{10,14},{12... | collective-permute-start | bytes 393224 | tf_op jit(solution)/shard_map/ppermute | solution.py:635
  19.7 10.1 %collective-permute-start.3 = (bf16[256,256]{1,0:T(8,128)(2,1)S(1)}, bf16[256,256]{1,0:T(8,128)(2,1)S(1)}, u32[]{:S(2)}, u32[]{:S(2)}) collective-permute-start(bf16[256,256]{1,0:T(8,128)(2,1)S(1)} %get-tuple-element.75), channel_id=1, source_target_pairs={{0,3},{2,1},{4,0},{6,2},{7,4},{5,6},{3,7},{1,5},{8,11},{10,9},{12,... | collective-permute-start | bytes 393224 | tf_op jit(solution)/shard_map/ppermute | solution.py:635
  20.9 9.8 %collective-permute-start.4 = (bf16[256,256]{1,0:T(8,128)(2,1)S(1)}, bf16[256,256]{1,0:T(8,128)(2,1)S(1)}, u32[]{:S(2)}, u32[]{:S(2)}) collective-permute-start(bf16[256,256]{1,0:T(8,128)(2,1)S(1)} %get-tuple-element.76), channel_id=1, source_target_pairs={{0,6},{2,7},{4,5},{6,3},{7,1},{5,0},{3,2},{1,4},{8,14},{10,15},{12... | collective-permute-start | bytes 393224 | tf_op jit(solution)/shard_map/ppermute | solution.py:635
  22.1 12.6 %collective-permute-start.5 = (bf16[256,256]{1,0:T(8,128)(2,1)S(1)}, bf16[256,256]{1,0:T(8,128)(2,1)S(1)}, u32[]{:S(2)}, u32[]{:S(2)}) collective-permute-start(bf16[256,256]{1,0:T(8,128)(2,1)S(1)} %get-tuple-element.77), channel_id=1, source_target_pairs={{0,5},{2,3},{4,1},{6,0},{7,2},{5,4},{3,6},{1,7},{8,13},{10,11},{12... | collective-permute-start | bytes 393224 | tf_op jit(solution)/shard_map/ppermute | solution.py:635
  24.1 1.9 copy-start.4
  34.7 14.2 %collective-permute-start.8 = (bf16[7,256,256]{2,1,0:T(8,128)(2,1)S(1)}, bf16[7,256,256]{2,1,0:T(8,128)(2,1)S(1)}, u32[]{:S(2)}, u32[]{:S(2)}) collective-permute-start(bf16[7,256,256]{2,1,0:T(8,128)(2,1)S(1)} %stack.1.refs_1_.refs_3_.mine), channel_id=1, source_target_pairs={{0,8},{8,0},{16,24},{24,16},{1,9},{9,1},{17,25},{25,17},{2,10},{10... | collective-permute-start | bytes 2752520 | tf_op jit(solution)/shard_map/ppermute | solution.py:638
  36.7 12.2 %collective-permute-start.9 = (bf16[3,128,512]{2,1,0:T(8,128)(2,1)S(1)}, bf16[3,128,512]{2,1,0:T(8,128)(2,1)S(1)}, u32[]{:S(2)}, u32[]{:S(2)}) collective-permute-start(bf16[3,128,512]{2,1,0:T(8,128)(2,1)S(1)} %get-tuple-element.80.refs_7_), channel_id=1, source_target_pairs={{0,2},{2,4},{4,6},{6,7},{7,5},{5,3},{3,1},{1,0},{8,10},{10,12},{12... | collective-permute-start | bytes 1179656 | tf_op jit(solution)/shard_map/ppermute | solution.py:635
  36.7 12.2 %collective-permute-start.10 = (bf16[3,128,512]{2,1,0:T(8,128)(2,1)S(1)}, bf16[3,128,512]{2,1,0:T(8,128)(2,1)S(1)}, u32[]{:S(2)}, u32[]{:S(2)}) collective-permute-start(bf16[3,128,512]{2,1,0:T(8,128)(2,1)S(1)} %get-tuple-element.81), channel_id=1, source_target_pairs={{0,1},{2,0},{4,2},{6,4},{7,6},{5,7},{3,5},{1,3},{8,9},{10,8},{12,1... | collective-permute-start | bytes 1179656 | tf_op jit(solution)/shard_map/ppermute | solution.py:635
  39.5 17.8 %collective-permute-start.17 = (bf16[3,128,512]{2,1,0:T(8,128)(2,1)S(1)}, bf16[3,128,512]{2,1,0:T(8,128)(2,1)S(1)}, u32[]{:S(2)}, u32[]{:S(2)}) collective-permute-start(bf16[3,128,512]{2,1,0:T(8,128)(2,1)S(1)} %get-tuple-element.89), channel_id=1, source_target_pairs={{0,2},{2,4},{4,6},{6,7},{7,5},{5,3},{3,1},{1,0},{8,10},{10,12},{12... | collective-permute-start | bytes 1179656 | tf_op jit(solution)/shard_map/ppermute | solution.py:635
  39.5 17.8 %collective-permute-start.18 = (bf16[3,128,512]{2,1,0:T(8,128)(2,1)S(1)}, bf16[3,128,512]{2,1,0:T(8,128)(2,1)S(1)}, u32[]{:S(2)}, u32[]{:S(2)}) collective-permute-start(bf16[3,128,512]{2,1,0:T(8,128)(2,1)S(1)} %get-tuple-element.90), channel_id=1, source_target_pairs={{0,1},{2,0},{4,2},{6,4},{7,6},{5,7},{3,5},{1,3},{8,9},{10,8},{12,1... | collective-permute-start | bytes 1179656 | tf_op jit(solution)/shard_map/ppermute | solution.py:635
  51.0 23.2 %collective-permute-start.11 = (bf16[3,256,512]{2,1,0:T(8,128)(2,1)S(1)}, bf16[3,256,512]{2,1,0:T(8,128)(2,1)S(1)}, u32[]{:S(2)}, u32[]{:S(2)}) collective-permute-start(bf16[3,256,512]{2,1,0:T(8,128)(2,1)S(1)} %get-tuple-element.82), channel_id=1, source_target_pairs={{0,2},{2,4},{4,6},{6,7},{7,5},{5,3},{3,1},{1,0},{8,10},{10,12},{12... | collective-permute-start | bytes 2359304 | tf_op jit(solution)/shard_map/ppermute | solution.py:635
  53.5 20.7 %collective-permute-start.12 = (bf16[3,256,512]{2,1,0:T(8,128)(2,1)S(1)}, bf16[3,256,512]{2,1,0:T(8,128)(2,1)S(1)}, u32[]{:S(2)}, u32[]{:S(2)}) collective-permute-start(bf16[3,256,512]{2,1,0:T(8,128)(2,1)S(1)} %get-tuple-element.83), channel_id=1, source_target_pairs={{0,1},{2,0},{4,2},{6,4},{7,6},{5,7},{3,5},{1,3},{8,9},{10,8},{12,1... | collective-permute-start | bytes 2359304 | tf_op jit(solution)/shard_map/ppermute | solution.py:635
  59.4 31.6 %collective-permute-start.19 = (bf16[3,256,512]{2,1,0:T(8,128)(2,1)S(1)}, bf16[3,256,512]{2,1,0:T(8,128)(2,1)S(1)}, u32[]{:S(2)}, u32[]{:S(2)}) collective-permute-start(bf16[3,256,512]{2,1,0:T(8,128)(2,1)S(1)} %get-tuple-element.91), channel_id=1, source_target_pairs={{0,2},{2,4},{4,6},{6,7},{7,5},{5,3},{3,1},{1,0},{8,10},{10,12},{12... | collective-permute-start | bytes 2359304 | tf_op jit(solution)/shard_map/ppermute | solution.py:635
  61.9 29.2 %collective-permute-start.20 = (bf16[3,256,512]{2,1,0:T(8,128)(2,1)S(1)}, bf16[3,256,512]{2,1,0:T(8,128)(2,1)S(1)}, u32[]{:S(2)}, u32[]{:S(2)}) collective-permute-start(bf16[3,256,512]{2,1,0:T(8,128)(2,1)S(1)} %get-tuple-element.92), channel_id=1, source_target_pairs={{0,1},{2,0},{4,2},{6,4},{7,6},{5,7},{3,5},{1,3},{8,9},{10,8},{12,1... | collective-permute-start | bytes 2359304 | tf_op jit(solution)/shard_map/ppermute | solution.py:635
  76.3 31.6 %collective-permute-start.13 = (bf16[3,256,512]{2,1,0:T(8,128)(2,1)S(1)}, bf16[3,256,512]{2,1,0:T(8,128)(2,1)S(1)}, u32[]{:S(2)}, u32[]{:S(2)}) collective-permute-start(bf16[3,256,512]{2,1,0:T(8,128)(2,1)S(1)} %get-tuple-element.84), channel_id=1, source_target_pairs={{0,2},{2,4},{4,6},{6,7},{7,5},{5,3},{3,1},{1,0},{8,10},{10,12},{12... | collective-permute-start | bytes 2359304 | tf_op jit(solution)/shard_map/ppermute | solution.py:635
  78.8 29.2 %collective-permute-start.14 = (bf16[3,256,512]{2,1,0:T(8,128)(2,1)S(1)}, bf16[3,256,512]{2,1,0:T(8,128)(2,1)S(1)}, u32[]{:S(2)}, u32[]{:S(2)}) collective-permute-start(bf16[3,256,512]{2,1,0:T(8,128)(2,1)S(1)} %get-tuple-element.85), channel_id=1, source_target_pairs={{0,1},{2,0},{4,2},{6,4},{7,6},{5,7},{3,5},{1,3},{8,9},{10,8},{12,1... | collective-permute-start | bytes 2359304 | tf_op jit(solution)/shard_map/ppermute | solution.py:635
  93.1 31.6 %collective-permute-start.21 = (bf16[3,256,512]{2,1,0:T(8,128)(2,1)S(1)}, bf16[3,256,512]{2,1,0:T(8,128)(2,1)S(1)}, u32[]{:S(2)}, u32[]{:S(2)}) collective-permute-start(bf16[3,256,512]{2,1,0:T(8,128)(2,1)S(1)} %get-tuple-element.93), channel_id=1, source_target_pairs={{0,2},{2,4},{4,6},{6,7},{7,5},{5,3},{3,1},{1,0},{8,10},{10,12},{12... | collective-permute-start | bytes 2359304 | tf_op jit(solution)/shard_map/ppermute | solution.py:635
  95.6 29.2 %collective-permute-start.22 = (bf16[3,256,512]{2,1,0:T(8,128)(2,1)S(1)}, bf16[3,256,512]{2,1,0:T(8,128)(2,1)S(1)}, u32[]{:S(2)}, u32[]{:S(2)}) collective-permute-start(bf16[3,256,512]{2,1,0:T(8,128)(2,1)S(1)} %get-tuple-element.94), channel_id=1, source_target_pairs={{0,1},{2,0},{4,2},{6,4},{7,6},{5,7},{3,5},{1,3},{8,9},{10,8},{12,1... | collective-permute-start | bytes 2359304 | tf_op jit(solution)/shard_map/ppermute | solution.py:635
  96.8 28.0 %copy-start = (bf16[512,2048]{1,0:T(8,128)(2,1)}, bf16[512,2048]{1,0:T(8,128)(2,1)S(1)}, u32[]{:S(2)}) copy-start(bf16[512,2048]{1,0:T(8,128)(2,1)S(1)} %turn.1.refs_9_.refs_0_) | copy-start | bytes 6291460
  110.0 31.6 %collective-permute-start.15 = (bf16[3,256,512]{2,1,0:T(8,128)(2,1)S(1)}, bf16[3,256,512]{2,1,0:T(8,128)(2,1)S(1)}, u32[]{:S(2)}, u32[]{:S(2)}) collective-permute-start(bf16[3,256,512]{2,1,0:T(8,128)(2,1)S(1)} %get-tuple-element.86), channel_id=1, source_target_pairs={{0,2},{2,4},{4,6},{6,7},{7,5},{5,3},{3,1},{1,0},{8,10},{10,12},{12... | collective-permute-start | bytes 2359304 | tf_op jit(solution)/shard_map/ppermute | solution.py:635
  112.5 29.2 %copy-start.11 = (bf16[256,1024]{1,0:T(8,128)(2,1)S(1)}, bf16[256,1024]{1,0:T(8,128)(2,1)}, u32[]{:S(2)}) copy-start(bf16[256,1024]{1,0:T(8,128)(2,1)} %d_out.3) | copy-start | bytes 1572868
  112.5 29.2 %collective-permute-start.16 = (bf16[3,256,512]{2,1,0:T(8,128)(2,1)S(1)}, bf16[3,256,512]{2,1,0:T(8,128)(2,1)S(1)}, u32[]{:S(2)}, u32[]{:S(2)}) collective-permute-start(bf16[3,256,512]{2,1,0:T(8,128)(2,1)S(1)} %get-tuple-element.87), channel_id=1, source_target_pairs={{0,1},{2,0},{4,2},{6,4},{7,6},{5,7},{3,5},{1,3},{8,9},{10,8},{12,1... | collective-permute-start | bytes 2359304 | tf_op jit(solution)/shard_map/ppermute | solution.py:635
  126.8 31.6 %collective-permute-start.23 = (bf16[3,256,512]{2,1,0:T(8,128)(2,1)S(1)}, bf16[3,256,512]{2,1,0:T(8,128)(2,1)S(1)}, u32[]{:S(2)}, u32[]{:S(2)}) collective-permute-start(bf16[3,256,512]{2,1,0:T(8,128)(2,1)S(1)} %get-tuple-element.95), channel_id=1, source_target_pairs={{0,2},{2,4},{4,6},{6,7},{7,5},{5,3},{3,1},{1,0},{8,10},{10,12},{12... | collective-permute-start | bytes 2359304 | tf_op jit(solution)/shard_map/ppermute | solution.py:635
  129.3 29.2 %collective-permute-start.24 = (bf16[3,256,512]{2,1,0:T(8,128)(2,1)S(1)}, bf16[3,256,512]{2,1,0:T(8,128)(2,1)S(1)}, u32[]{:S(2)}, u32[]{:S(2)}) collective-permute-start(bf16[3,256,512]{2,1,0:T(8,128)(2,1)S(1)} %get-tuple-element.96), channel_id=1, source_target_pairs={{0,1},{2,0},{4,2},{6,4},{7,6},{5,7},{3,5},{1,3},{8,9},{10,8},{12,1... | collective-permute-start | bytes 2359304 | tf_op jit(solution)/shard_map/ppermute | solution.py:635
  149.5 16.2 %copy-start.12 = (bf16[3,256,512]{2,1,0:T(8,128)(2,1)}, bf16[3,256,512]{2,1,0:T(8,128)(2,1)S(1)}, u32[]{:S(2)}) copy-start(bf16[3,256,512]{2,1,0:T(8,128)(2,1)S(1)} %get-tuple-element.102.refs_0_.refs_1_) | copy-start | bytes 2359300
  149.5 25.8 %collective-permute-start.27 = (bf16[3,256,512]{2,1,0:T(8,128)(2,1)S(1)}, bf16[3,256,512]{2,1,0:T(8,128)(2,1)S(1)}, u32[]{:S(2)}, u32[]{:S(2)}) collective-permute-start(bf16[3,256,512]{2,1,0:T(8,128)(2,1)S(1)} %get-tuple-element.102.refs_0_.refs_1_), channel_id=1, source_target_pairs={{0,2},{2,4},{4,6},{6,7},{7,5},{5,3},{3,1},{1,0},{8,10},{10,12},{12... | collective-permute-start | bytes 2359304 | tf_op jit(solution)/shard_map/ppermute | solution.py:635
  151.9 24.3 %collective-permute-start.30 = (bf16[3,256,512]{2,1,0:T(8,128)(2,1)S(1)}, bf16[3,256,512]{2,1,0:T(8,128)(2,1)S(1)}, u32[]{:S(2)}, u32[]{:S(2)}) collective-permute-start(bf16[3,256,512]{2,1,0:T(8,128)(2,1)S(1)} %get-tuple-element.102.refs_0_.refs_1_), channel_id=1, source_target_pairs={{0,1},{2,0},{4,2},{6,4},{7,6},{5,7},{3,5},{1,3},{8,9},{10,8},{12,1... | collective-permute-start | bytes 2359304 | tf_op jit(solution)/shard_map/ppermute | solution.py:635
  167.1 25.1 %collective-permute-start.35 = (bf16[3,256,512]{2,1,0:T(8,128)(2,1)S(1)}, bf16[3,256,512]{2,1,0:T(8,128)(2,1)S(1)}, u32[]{:S(2)}, u32[]{:S(2)}) collective-permute-start(bf16[3,256,512]{2,1,0:T(8,128)(2,1)S(1)} %get-tuple-element.107.refs_0_.refs_1_), channel_id=1, source_target_pairs={{0,2},{2,4},{4,6},{6,7},{7,5},{5,3},{3,1},{1,0},{8,10},{10,12},{12... | collective-permute-start | bytes 2359304 | tf_op jit(solution)/shard_map/ppermute | solution.py:635
  169.5 23.5 %collective-permute-start.38 = (bf16[3,256,512]{2,1,0:T(8,128)(2,1)S(1)}, bf16[3,256,512]{2,1,0:T(8,128)(2,1)S(1)}, u32[]{:S(2)}, u32[]{:S(2)}) collective-permute-start(bf16[3,256,512]{2,1,0:T(8,128)(2,1)S(1)} %get-tuple-element.107.refs_0_.refs_1_), channel_id=1, source_target_pairs={{0,1},{2,0},{4,2},{6,4},{7,6},{5,7},{3,5},{1,3},{8,9},{10,8},{12,1... | collective-permute-start | bytes 2359304 | tf_op jit(solution)/shard_map/ppermute | solution.py:635
  175.3 33.8 %collective-permute-start.28 = (bf16[3,256,512]{2,1,0:T(8,128)(2,1)S(1)}, bf16[3,256,512]{2,1,0:T(8,128)(2,1)}, u32[]{:S(2)}, u32[]{:S(2)}) collective-permute-start(bf16[3,256,512]{2,1,0:T(8,128)(2,1)S(1)} %collective-permute-done.27.refs_1_.refs_2_), channel_id=1, source_target_pairs={{0,2},{2,4},{4,6},{6,7},{7,5},{5,3},{3,1},{1,0},{8,10},{10,12},{12... | collective-permute-start | bytes 2359304 | tf_op jit(solution)/shard_map/ppermute | solution.py:635
  176.2 32.9 %collective-permute-start.31 = (bf16[3,256,512]{2,1,0:T(8,128)(2,1)S(1)}, bf16[3,256,512]{2,1,0:T(8,128)(2,1)}, u32[]{:S(2)}, u32[]{:S(2)}) collective-permute-start(bf16[3,256,512]{2,1,0:T(8,128)(2,1)S(1)} %collective-permute-done.30.refs_2_.refs_3_), channel_id=1, source_target_pairs={{0,1},{2,0},{4,2},{6,4},{7,6},{5,7},{3,5},{1,3},{8,9},{10,8},{12,1... | collective-permute-start | bytes 2359304 | tf_op jit(solution)/shard_map/ppermute | solution.py:635
  192.2 33.8 %collective-permute-start.36 = (bf16[3,256,512]{2,1,0:T(8,128)(2,1)S(1)}, bf16[3,256,512]{2,1,0:T(8,128)(2,1)}, u32[]{:S(2)}, u32[]{:S(2)}) collective-permute-start(bf16[3,256,512]{2,1,0:T(8,128)(2,1)S(1)} %collective-permute-done.35.refs_1_.refs_2_), channel_id=1, source_target_pairs={{0,2},{2,4},{4,6},{6,7},{7,5},{5,3},{3,1},{1,0},{8,10},{10,12},{12... | collective-permute-start | bytes 2359304 | tf_op jit(solution)/shard_map/ppermute | solution.py:635
  193.1 32.9 %collective-permute-start.39 = (bf16[3,256,512]{2,1,0:T(8,128)(2,1)S(1)}, bf16[3,256,512]{2,1,0:T(8,128)(2,1)}, u32[]{:S(2)}, u32[]{:S(2)}) collective-permute-start(bf16[3,256,512]{2,1,0:T(8,128)(2,1)S(1)} %collective-permute-done.38.refs_2_.refs_3_), channel_id=1, source_target_pairs={{0,1},{2,0},{4,2},{6,4},{7,6},{5,7},{3,5},{1,3},{8,9},{10,8},{12,1... | collective-permute-start | bytes 2359304 | tf_op jit(solution)/shard_map/ppermute | solution.py:635
  209.1 34.5 %collective-permute-start.29 = (bf16[3,256,512]{2,1,0:T(8,128)(2,1)}, bf16[3,256,512]{2,1,0:T(8,128)(2,1)}, u32[]{:S(2)}, u32[]{:S(2)}) collective-permute-start(bf16[3,256,512]{2,1,0:T(8,128)(2,1)} %collective-permute-done.28.refs_0_.refs_4_), channel_id=1, source_target_pairs={{0,2},{2,4},{4,6},{6,7},{7,5},{5,3},{3,1},{1,0},{8,10},{10,12},{12... | collective-permute-start | bytes 2359304 | tf_op jit(solution)/shard_map/ppermute | solution.py:635
  209.2 34.5 %collective-permute-start.32 = (bf16[3,256,512]{2,1,0:T(8,128)(2,1)}, bf16[3,256,512]{2,1,0:T(8,128)(2,1)}, u32[]{:S(2)}, u32[]{:S(2)}) collective-permute-start(bf16[3,256,512]{2,1,0:T(8,128)(2,1)} %collective-permute-done.31.refs_1_.refs_5_), channel_id=1, source_target_pairs={{0,1},{2,0},{4,2},{6,4},{7,6},{5,7},{3,5},{1,3},{8,9},{10,8},{12,1... | collective-permute-start | bytes 2359304 | tf_op jit(solution)/shard_map/ppermute | solution.py:635
  226.0 33.7 %collective-permute-start.37 = (bf16[3,256,512]{2,1,0:T(8,128)(2,1)}, bf16[3,256,512]{2,1,0:T(8,128)(2,1)}, u32[]{:S(2)}, u32[]{:S(2)}) collective-permute-start(bf16[3,256,512]{2,1,0:T(8,128)(2,1)} %collective-permute-done.36.refs_0_.refs_4_), channel_id=1, source_target_pairs={{0,2},{2,4},{4,6},{6,7},{7,5},{5,3},{3,1},{1,0},{8,10},{10,12},{12... | collective-permute-start | bytes 2359304 | tf_op jit(solution)/shard_map/ppermute | solution.py:635
  226.0 33.7 %collective-permute-start.40 = (bf16[3,256,512]{2,1,0:T(8,128)(2,1)}, bf16[3,256,512]{2,1,0:T(8,128)(2,1)}, u32[]{:S(2)}, u32[]{:S(2)}) collective-permute-start(bf16[3,256,512]{2,1,0:T(8,128)(2,1)} %collective-permute-done.39.refs_1_.refs_5_), channel_id=1, source_target_pairs={{0,1},{2,0},{4,2},{6,4},{7,6},{5,7},{3,5},{1,3},{8,9},{10,8},{12,1... | collective-permute-start | bytes 2359304 | tf_op jit(solution)/shard_map/ppermute | solution.py:635
  230.3 2.7 collective-permute-start.25
  233.9 4.9 %collective-permute-start.26 = (f32[256,1]{1,0:T(8,128)S(1)}, f32[256,1]{1,0:T(8,128)S(1)}, u32[]{:S(2)}, u32[]{:S(2)}) collective-permute-start(f32[256,1]{1,0:T(8,128)S(1)} %add.31), channel_id=1, source_target_pairs={{0,16},{8,24},{16,0},{24,8},{1,17},{9,25},{17,1},{25,9},{2,18},{10... | collective-permute-start | bytes 3080 | tf_op jit(solution)/shard_map/ppermute | solution.py:638
  242.2 4.8 %copy-start.6 = (bf16[3,256,512]{2,1,0:T(8,128)(2,1)S(1)}, bf16[3,256,512]{2,1,0:T(8,128)(2,1)}, u32[]{:S(2)}) copy-start(bf16[3,256,512]{2,1,0:T(8,128)(2,1)} %copy-done.5) | copy-start | bytes 2359300
  242.2 4.8 %copy-start.8 = (bf16[3,256,512]{2,1,0:T(8,128)(2,1)S(1)}, bf16[3,256,512]{2,1,0:T(8,128)(2,1)}, u32[]{:S(2)}) copy-start(bf16[3,256,512]{2,1,0:T(8,128)(2,1)} %copy-done.7) | copy-start | bytes 2359300
  242.2 4.8 %copy-start.10 = (bf16[3,256,512]{2,1,0:T(8,128)(2,1)S(1)}, bf16[3,256,512]{2,1,0:T(8,128)(2,1)}, u32[]{:S(2)}) copy-start(bf16[3,256,512]{2,1,0:T(8,128)(2,1)} %copy-done.9) | copy-start | bytes 2359300
  245.1 23.4 %collective-permute-start.33 = (bf16[3,128,512]{2,1,0:T(8,128)(2,1)S(1)}, bf16[3,128,512]{2,1,0:T(8,128)(2,1)S(1)}, u32[]{:S(2)}, u32[]{:S(2)}) collective-permute-start(bf16[3,128,512]{2,1,0:T(8,128)(2,1)S(1)} %get-tuple-element.103), channel_id=1, source_target_pairs={{0,2},{2,4},{4,6},{6,7},{7,5},{5,3},{3,1},{1,0},{8,10},{10,12},{12... | collective-permute-start | bytes 1179656 | tf_op jit(solution)/shard_map/ppermute | solution.py:635
  246.8 21.7 %collective-permute-start.34 = (bf16[3,128,512]{2,1,0:T(8,128)(2,1)S(1)}, bf16[3,128,512]{2,1,0:T(8,128)(2,1)S(1)}, u32[]{:S(2)}, u32[]{:S(2)}) collective-permute-start(bf16[3,128,512]{2,1,0:T(8,128)(2,1)S(1)} %get-tuple-element.104), channel_id=1, source_target_pairs={{0,1},{2,0},{4,2},{6,4},{7,6},{5,7},{3,5},{1,3},{8,9},{10,8},{12,1... | collective-permute-start | bytes 1179656 | tf_op jit(solution)/shard_map/ppermute | solution.py:635
  261.1 15.5 %collective-permute-start.41 = (bf16[3,128,512]{2,1,0:T(8,128)(2,1)S(1)}, bf16[3,128,512]{2,1,0:T(8,128)(2,1)S(1)}, u32[]{:S(2)}, u32[]{:S(2)}) collective-permute-start(bf16[3,128,512]{2,1,0:T(8,128)(2,1)S(1)} %get-tuple-element.118), channel_id=1, source_target_pairs={{0,2},{2,4},{4,6},{6,7},{7,5},{5,3},{3,1},{1,0},{8,10},{10,12},{12... | collective-permute-start | bytes 1179656 | tf_op jit(solution)/shard_map/ppermute | solution.py:635
  263.6 13.0 %collective-permute-start.42 = (bf16[3,128,512]{2,1,0:T(8,128)(2,1)S(1)}, bf16[3,128,512]{2,1,0:T(8,128)(2,1)S(1)}, u32[]{:S(2)}, u32[]{:S(2)}) collective-permute-start(bf16[3,128,512]{2,1,0:T(8,128)(2,1)S(1)} %get-tuple-element.119), channel_id=1, source_target_pairs={{0,1},{2,0},{4,2},{6,4},{7,6},{5,7},{3,5},{1,3},{8,9},{10,8},{12,1... | collective-permute-start | bytes 1179656 | tf_op jit(solution)/shard_map/ppermute | solution.py:635
  266.0 3.1 copy-start.20
  268.4 1.8 copy-start.14
  268.4 2.0 copy-start.17
  278.3 6.1 %copy-start.22 = (bf16[256,512]{1,0:T(8,128)(2,1)S(1)}, bf16[256,512]{1,0:T(8,128)(2,1)}, u32[]{:S(2)}) copy-start(bf16[256,512]{1,0:T(8,128)(2,1)} %copy-done.21) | copy-start | bytes 786436
  278.3 3.2 %collective-permute-start.47 = (bf16[4,128,512]{2,1,0:T(8,128)(2,1)S(1)}, bf16[4,128,512]{2,1,0:T(8,128)(2,1)S(1)}, u32[]{:S(2)}, u32[]{:S(2)}) collective-permute-start(bf16[4,128,512]{2,1,0:T(8,128)(2,1)S(1)} %get-tuple-element.132), channel_id=1, source_target_pairs={{0,8},{8,0},{16,24},{24,16},{1,9},{9,1},{17,25},{25,17},{2,10},{10... | collective-permute-start | bytes 1572872 | tf_op jit(solution)/shard_map/ppermute | solution.py:638
  280.0 3.5 %collective-permute-start.43 = (bf16[4,128,512]{2,1,0:T(8,128)(2,1)S(1)}, bf16[4,128,512]{2,1,0:T(8,128)(2,1)S(1)}, u32[]{:S(2)}, u32[]{:S(2)}) collective-permute-start(bf16[4,128,512]{2,1,0:T(8,128)(2,1)S(1)} %get-tuple-element.126), channel_id=1, source_target_pairs={{0,8},{8,0},{16,24},{24,16},{1,9},{9,1},{17,25},{25,17},{2,10},{10... | collective-permute-start | bytes 1572872 | tf_op jit(solution)/shard_map/ppermute | solution.py:638
  282.1 7.6 %collective-permute-start.48 = (bf16[2,128,512]{2,1,0:T(8,128)(2,1)S(1)}, bf16[2,128,512]{2,1,0:T(8,128)(2,1)S(1)}, u32[]{:S(2)}, u32[]{:S(2)}) collective-permute-start(bf16[2,128,512]{2,1,0:T(8,128)(2,1)S(1)} %get-tuple-element.134), channel_id=1, source_target_pairs={{0,16},{8,24},{16,0},{24,8},{1,17},{9,25},{17,1},{25,9},{2,18},{10... | collective-permute-start | bytes 786440 | tf_op jit(solution)/shard_map/ppermute | solution.py:638
  284.1 14.1 %collective-permute-start.44 = (bf16[2,128,512]{2,1,0:T(8,128)(2,1)S(1)}, bf16[2,128,512]{2,1,0:T(8,128)(2,1)S(1)}, u32[]{:S(2)}, u32[]{:S(2)}) collective-permute-start(bf16[2,128,512]{2,1,0:T(8,128)(2,1)S(1)} %get-tuple-element.128), channel_id=1, source_target_pairs={{0,16},{8,24},{16,0},{24,8},{1,17},{9,25},{17,1},{25,9},{2,18},{10... | collective-permute-start | bytes 786440 | tf_op jit(solution)/shard_map/ppermute | solution.py:638
  290.3 19.4 %collective-permute-start.49 = (bf16[128,512]{1,0:T(8,128)(2,1)S(1)}, bf16[128,512]{1,0:T(8,128)(2,1)S(1)}, u32[]{:S(2)}, u32[]{:S(2)}) collective-permute-start(bf16[128,512]{1,0:T(8,128)(2,1)S(1)} %get-tuple-element.135), channel_id=1, source_target_pairs={{0,0},{1,1},{2,8},{3,9},{4,16},{5,17},{6,24},{7,25},{8,4},{9,5},{1... | collective-permute-start | bytes 393224 | tf_op jit(solution)/shard_map/ppermute | solution.py:696
  297.4 12.7 %collective-permute-start.50 = (bf16[128,512]{1,0:T(8,128)(2,1)S(1)}, bf16[128,512]{1,0:T(8,128)(2,1)S(1)}, u32[]{:S(2)}, u32[]{:S(2)}) collective-permute-start(bf16[128,512]{1,0:T(8,128)(2,1)S(1)} %get-tuple-element.136), channel_id=1, source_target_pairs={{0,1},{1,0},{2,9},{3,8},{4,17},{5,16},{6,25},{7,24},{8,5},{9,4},{1... | collective-permute-start | bytes 393224 | tf_op jit(solution)/shard_map/ppermute | solution.py:696
  298.8 13.8 %collective-permute-start.45 = (bf16[128,512]{1,0:T(8,128)(2,1)S(1)}, bf16[128,512]{1,0:T(8,128)(2,1)S(1)}, u32[]{:S(2)}, u32[]{:S(2)}) collective-permute-start(bf16[128,512]{1,0:T(8,128)(2,1)S(1)} %get-tuple-element.129), channel_id=1, source_target_pairs={{0,0},{1,1},{2,8},{3,9},{4,16},{5,17},{6,24},{7,25},{8,4},{9,5},{1... | collective-permute-start | bytes 393224 | tf_op jit(solution)/shard_map/ppermute | solution.py:696
  302.6 11.7 %collective-permute-start.46 = (bf16[128,512]{1,0:T(8,128)(2,1)S(1)}, bf16[128,512]{1,0:T(8,128)(2,1)S(1)}, u32[]{:S(2)}, u32[]{:S(2)}) collective-permute-start(bf16[128,512]{1,0:T(8,128)(2,1)S(1)} %get-tuple-element.130), channel_id=1, source_target_pairs={{0,1},{1,0},{2,9},{3,8},{4,17},{5,16},{6,25},{7,24},{8,5},{9,4},{1... | collective-permute-start | bytes 393224 | tf_op jit(solution)/shard_map/ppermute | solution.py:696
  303.3 11.0 %copy-start.3 = (bf16[256,4096]{1,0:T(8,128)(2,1)S(1)}, bf16[256,4096]{1,0:T(8,128)(2,1)}, u32[]{:S(2)}) copy-start(bf16[256,4096]{1,0:T(8,128)(2,1)} %tokens.3) | copy-start | bytes 6291460
  303.3 11.0 %copy-start.24 = (f32[256,128]{1,0:T(8,128)S(1)}, f32[256,128]{1,0:T(8,128)}, u32[]{:S(2)}) copy-start(f32[256,128]{1,0:T(8,128)} %copy-done.23) | copy-start | bytes 393220
  (15 other events, 14.6 us)

commit v14 on v13

--- a/solution.py
+++ b/solution.py
@@ -560,18 +560,18 @@
         out[...] = (keep[block] + came[block].astype(jnp.float32)).astype(jnp.bfloat16)
 
 
-def order_sum(idx, column, keep, came):
+def order_sum(idx, column, keep, came, ties):
     whole = pl.BlockSpec(memory_space=pltpu.VMEM)
     count = keep.shape[0]
     return pl.pallas_call(
-        functools.partial(order_kernel, column),
-        in_specs=[pl.BlockSpec(memory_space=pltpu.SMEM), whole, whole],
+        tied(functools.partial(order_kernel, column), 3, len(ties)),
+        in_specs=[pl.BlockSpec(memory_space=pltpu.SMEM), whole, whole, *tie_specs(ties)],
         out_specs=[whole] * count,
         out_shape=[jax.ShapeDtypeStruct(keep.shape[1:], jnp.bfloat16)] * count,
         compiler_params=pltpu.CompilerParams(vmem_limit_bytes=4 * MIB),
         cost_estimate=cost(0, 8 * count * keep.shape[1] * keep.shape[2]),
         name="order_sum",
-    )(idx, keep, came)
+    )(idx, keep, came, *ties)
 
 
 def finish_kernel(column, width, idx, tokens, gain, inverse, dots, *refs):
@@ -676,14 +676,14 @@
         dots = dots + swap(dots, bit)
         bit *= 2
 
-    def sum_nodes(keep, send):
+    def sum_nodes(keep, send, ties):
         column = 4 * size + 1
         bit = 1
         while 2 * bit < nodes:
             keep, send = split_sum(idx, column, group, keep, swap(send, bit))
             column += 1
             bit *= 2
-        return order_sum(idx, column, keep, swap(send, bit))
+        return order_sum(idx, column, keep, swap(send, bit), ties)
 
     def relocate(blocks):
         came = []
@@ -719,13 +719,13 @@
     keep_0, keep_1, send_0, send_1 = term_last(
         idx, turned, lasts, gathered[1][-2:], terms[1], [done]
     )
-    first, second = sum_nodes(keep_0, send_0), sum_nodes(keep_1, send_1)
+    grads, done = grads_chunk(rows_turned, gathered[1], grads, [keep_1], 1, wide, columns)
+    first, second = sum_nodes(keep_0, send_0, [done]), sum_nodes(keep_1, send_1, [done])
     came = [*relocate(first), *relocate(second)]
     column = idx.shape[0] - 1 - group
     d_tokens = finish(
         idx, column, tokens, norm_gain[None], inverse_rms, dots, came, width // nodes
     )
-    grads, _ = grads_chunk(rows_turned, gathered[1], grads, [keep_1], 1, wide, columns)
     return (jnp.concatenate(outputs, axis=-1), d_tokens, grads)
 
 

time: 317 us -> 317 us (level)
    ppermute x4, waiting for transfers between devices: 4.6 us -> 10.6 us  [relocate(): came.append(lax.ppermute(block, ('node', 'local'), moves))]
    ppermute x8, waiting for transfers between devices: 10.8 us -> 6.28 us  [swap(): return lax.ppermute(array, 'node', [(n, n ^ bit) for n in range(nodes)])]
  transfers between devices with their start and end apart: 51 -> 51, of which waited for: 23 -> 22; matrix products, arithmetic and copies ran while one was open for 2% -> 2% of each run, Pallas kernels for 20% -> 19%
where the time goes in v14:
time: 317 us; the launch traced here: 316 us
  waiting for transfers between devices  157 us (50%)
  starting transfers between devices  68.9 us (22%)
  Pallas kernels  66.3 us (21%)
  local copies, waits for them, and re-layouts  18.4 us (6%)
  other arithmetic  4.52 us (1%)
    ppermute x39, waiting for transfers between devices, shift(): return lax.ppermute(array, 'local', moves)  140 us
    ppermute x39, starting transfers between devices, shift(): return lax.ppermute(array, 'local', moves)  47.4 us
    unnamed x56, local copies, waits for them, and re-layouts  16.2 us
    pallas_call x2, Pallas kernels, attention(): pl.pallas_call(attention_kernel, grid_spec=pltpu.PrefetchScalarGridSpec(n...  14.5 us
    pallas_call x7, Pallas kernels, term_step(): pl.pallas_call(kernel, in_specs=[whole] * (1 + count + len(befores)), out...  12.8 us
    pallas_call x2, Pallas kernels, grads_chunk(): pl.pallas_call(tied(grads_kernel, 1 + len(pieces), len(ties)), grid=(3,),...  12.6 us
    pallas_call x6, Pallas kernels, sum_step(): pl.pallas_call(tied(sum_step_kernel, 9, len(ties)), grid_spec=pltpu.Prefe...  12.3 us
    ppermute x4, starting transfers between devices, relocate(): came.append(lax.ppermute(block, ('node', 'local'), moves))  11.4 us
  transfers between devices with their start and end apart: 51, of which 22 were waited for; matrix products, arithmetic and copies ran while one was open for 2% of the time, Pallas kernels for 19%

profile of v14, /device:TPU:1, one launch (start us, length us, event | category | flops | bytes accessed | tf_op | source)
XLA Modules:
  0.0 316.4 jit_solution(1876987277435360488)
XLA Ops:
  2.0 1.6 copy-done.2
  5.7 5.1 %collective-permute-start.6 = (bf16[256,256]{1,0:T(8,128)(2,1)S(1)}, bf16[256,256]{1,0:T(8,128)(2,1)S(1)}, u32[]{:S(2)}, u32[]{:S(2)}) collective-permute-start(bf16[256,256]{1,0:T(8,128)(2,1)S(1)} %get-tuple-element.79), channel_id=1, source_target_pairs={{0,7},{2,5},{4,3},{6,1},{7,0},{5,2},{3,4},{1,6},{8,15},{10,13},{12... | collective-permute-start | bytes 393224 | tf_op jit(solution)/shard_map/ppermute | solution.py:635
  10.8 3.3 %collective-permute-done.6.mine.mine_far = bf16[256,256]{1,0:T(8,128)(2,1)S(1)} collective-permute-done((bf16[256,256]{1,0:T(8,128)(2,1)S(1)}, bf16[256,256]{1,0:T(8,128)(2,1)S(1)}, u32[]{:S(2)}, u32[]{:S(2)}) %collective-permute-start.6) | collective-permute-done | bytes 131104 | tf_op jit(solution)/shard_map/ppermute | solution.py:635
  14.1 2.1 collective-permute-start.7
  16.5 3.2 %collective-permute-start.2 = (bf16[256,256]{1,0:T(8,128)(2,1)S(1)}, bf16[256,256]{1,0:T(8,128)(2,1)S(1)}, u32[]{:S(2)}, u32[]{:S(2)}) collective-permute-start(bf16[256,256]{1,0:T(8,128)(2,1)S(1)} %get-tuple-element.75), channel_id=1, source_target_pairs={{0,4},{2,6},{4,7},{6,5},{7,3},{5,1},{3,0},{1,2},{8,12},{10,14},{12... | collective-permute-start | bytes 393224 | tf_op jit(solution)/shard_map/ppermute | solution.py:635
  22.1 2.1 collective-permute-start.5
  24.1 1.9 copy-done.4
  27.8 1.9 sum_first.1
  30.7 4.0 %collective-permute-done.5.refs_6_ = bf16[256,256]{1,0:T(8,128)(2,1)S(1)} collective-permute-done((bf16[256,256]{1,0:T(8,128)(2,1)S(1)}, bf16[256,256]{1,0:T(8,128)(2,1)S(1)}, u32[]{:S(2)}, u32[]{:S(2)}) %collective-permute-start.5) | collective-permute-done | bytes 131104 | tf_op jit(solution)/shard_map/ppermute | solution.py:635
  34.7 2.0 collective-permute-start.8
  36.7 2.8 collective-permute-start.10
  39.5 1.5 collective-permute-start.18
  41.0 7.9 %collective-permute-done.9.refs_7_ = bf16[3,128,512]{2,1,0:T(8,128)(2,1)S(1)} collective-permute-done((bf16[3,128,512]{2,1,0:T(8,128)(2,1)S(1)}, bf16[3,128,512]{2,1,0:T(8,128)(2,1)S(1)}, u32[]{:S(2)}, u32[]{:S(2)}) %collective-permute-start.9) | collective-permute-done | bytes 393248 | tf_op jit(solution)/shard_map/ppermute | solution.py:635
  48.9 2.1 sum_step.6
  51.0 2.5 collective-permute-start.11
  53.5 3.9 %collective-permute-done.17.refs_7_ = bf16[3,128,512]{2,1,0:T(8,128)(2,1)S(1)} collective-permute-done((bf16[3,128,512]{2,1,0:T(8,128)(2,1)S(1)}, bf16[3,128,512]{2,1,0:T(8,128)(2,1)S(1)}, u32[]{:S(2)}, u32[]{:S(2)}) %collective-permute-start.17) | collective-permute-done | bytes 393248 | tf_op jit(solution)/shard_map/ppermute | solution.py:635
  57.4 2.1 sum_step.9
  59.4 2.5 collective-permute-start.19
  61.9 12.3 %collective-permute-done.11.refs_7_ = bf16[3,256,512]{2,1,0:T(8,128)(2,1)S(1)} collective-permute-done((bf16[3,256,512]{2,1,0:T(8,128)(2,1)S(1)}, bf16[3,256,512]{2,1,0:T(8,128)(2,1)S(1)}, u32[]{:S(2)}, u32[]{:S(2)}) %collective-permute-start.11) | collective-permute-done | bytes 786464 | tf_op jit(solution)/shard_map/ppermute | solution.py:635
  74.2 2.1 sum_step.7
  76.3 2.5 collective-permute-start.13
  78.8 12.3 %collective-permute-done.19.refs_7_ = bf16[3,256,512]{2,1,0:T(8,128)(2,1)S(1)} collective-permute-done((bf16[3,256,512]{2,1,0:T(8,128)(2,1)S(1)}, bf16[3,256,512]{2,1,0:T(8,128)(2,1)S(1)}, u32[]{:S(2)}, u32[]{:S(2)}) %collective-permute-start.19) | collective-permute-done | bytes 786464 | tf_op jit(solution)/shard_map/ppermute | solution.py:635
  91.1 2.1 sum_step.10
  93.1 2.5 collective-permute-start.21
  96.8 11.1 %collective-permute-done.13.refs_7_ = bf16[3,256,512]{2,1,0:T(8,128)(2,1)S(1)} collective-permute-done((bf16[3,256,512]{2,1,0:T(8,128)(2,1)S(1)}, bf16[3,256,512]{2,1,0:T(8,128)(2,1)S(1)}, u32[]{:S(2)}, u32[]{:S(2)}) %collective-permute-start.13) | collective-permute-done | bytes 786464 | tf_op jit(solution)/shard_map/ppermute | solution.py:635
  107.9 2.1 sum_step.8
  110.0 2.5 collective-permute-start.15
  112.5 12.3 %collective-permute-done.21.refs_7_ = bf16[3,256,512]{2,1,0:T(8,128)(2,1)S(1)} collective-permute-done((bf16[3,256,512]{2,1,0:T(8,128)(2,1)S(1)}, bf16[3,256,512]{2,1,0:T(8,128)(2,1)S(1)}, u32[]{:S(2)}, u32[]{:S(2)}) %collective-permute-start.21) | collective-permute-done | bytes 786464 | tf_op jit(solution)/shard_map/ppermute | solution.py:635
  124.8 2.1 sum_step.11
  126.8 2.5 collective-permute-start.23
  130.0 11.6 %collective-permute-done.15.from_left = bf16[3,256,512]{2,1,0:T(8,128)(2,1)S(1)} collective-permute-done((bf16[3,256,512]{2,1,0:T(8,128)(2,1)S(1)}, bf16[3,256,512]{2,1,0:T(8,128)(2,1)S(1)}, u32[]{:S(2)}, u32[]{:S(2)}) %collective-permute-start.15) | collective-permute-done | bytes 786464 | tf_op jit(solution)/shard_map/ppermute | solution.py:635
  141.6 7.2 %attention.2 = (bf16[256,512]{1,0:T(8,128)(2,1)S(1)}, f32[256,128]{1,0:T(8,128)S(1)}, bf16[3,256,512]{2,1,0:T(8,128)(2,1)S(1)}) custom-call(s32[39]{0:T(128)S(1)} %dynamic-slice_bitcast_fusion.idx.refs_0_, bf16[7,256,256]{2,1,0:T(8,128)(2,1)S(1)} %stack.1.refs_1_.refs_3_.mine, bf16[7,256,256]{2,1,0:T(8,128)(2,1)S(1)} %collective-permute-done.8.refs_2_.refs_4_.other, ...), custom_call_target="tpu_custom_call" | custom-call | flops 402653184 | bytes 3145728 | tf_op jit(solution)/shard_map/attention/pallas_call | solution.py:394
  149.5 2.4 collective-permute-start.27
  151.9 6.5 %collective-permute-done.23.from_left = bf16[3,256,512]{2,1,0:T(8,128)(2,1)S(1)} collective-permute-done((bf16[3,256,512]{2,1,0:T(8,128)(2,1)S(1)}, bf16[3,256,512]{2,1,0:T(8,128)(2,1)S(1)}, u32[]{:S(2)}, u32[]{:S(2)}) %collective-permute-start.23) | collective-permute-done | bytes 786464 | tf_op jit(solution)/shard_map/ppermute | solution.py:635
  158.5 7.3 %attention.3 = (bf16[256,512]{1,0:T(8,128)(2,1)S(1)}, f32[256,128]{1,0:T(8,128)S(1)}, bf16[3,256,512]{2,1,0:T(8,128)(2,1)S(1)}) custom-call(s32[39]{0:T(128)S(1)} %dynamic-slice_bitcast_fusion.idx.refs_0_, bf16[7,256,256]{2,1,0:T(8,128)(2,1)S(1)} %stack.1.refs_1_.refs_3_.mine, bf16[7,256,256]{2,1,0:T(8,128)(2,1)S(1)} %collective-permute-done.8.refs_2_.refs_4_.other, ...), custom_call_target="tpu_custom_call" | custom-call | flops 402653184 | bytes 3145728 | tf_op jit(solution)/shard_map/attention/pallas_call | solution.py:394
  167.1 2.4 collective-permute-start.35
  170.5 4.8 %collective-permute-done.27.refs_1_.refs_2_ = bf16[3,256,512]{2,1,0:T(8,128)(2,1)S(1)} collective-permute-done((bf16[3,256,512]{2,1,0:T(8,128)(2,1)S(1)}, bf16[3,256,512]{2,1,0:T(8,128)(2,1)S(1)}, u32[]{:S(2)}, u32[]{:S(2)}) %collective-permute-start.27) | collective-permute-done | bytes 786464 | tf_op jit(solution)/shard_map/ppermute | solution.py:635
  176.2 1.5 collective-permute-start.31
  178.6 13.6 %collective-permute-done.35.refs_1_.refs_2_ = bf16[3,256,512]{2,1,0:T(8,128)(2,1)S(1)} collective-permute-done((bf16[3,256,512]{2,1,0:T(8,128)(2,1)S(1)}, bf16[3,256,512]{2,1,0:T(8,128)(2,1)S(1)}, u32[]{:S(2)}, u32[]{:S(2)}) %collective-permute-start.35) | collective-permute-done | bytes 786464 | tf_op jit(solution)/shard_map/ppermute | solution.py:635
  193.1 1.5 collective-permute-start.39
  195.5 13.7 %collective-permute-done.28.refs_0_.refs_4_ = bf16[3,256,512]{2,1,0:T(8,128)(2,1)} collective-permute-done((bf16[3,256,512]{2,1,0:T(8,128)(2,1)S(1)}, bf16[3,256,512]{2,1,0:T(8,128)(2,1)}, u32[]{:S(2)}, u32[]{:S(2)}) %collective-permute-start.28) | collective-permute-done | bytes 786464 | tf_op jit(solution)/shard_map/ppermute | solution.py:635
  209.2 1.5 collective-permute-start.32
  210.6 15.4 %collective-permute-done.36.refs_0_.refs_4_ = bf16[3,256,512]{2,1,0:T(8,128)(2,1)} collective-permute-done((bf16[3,256,512]{2,1,0:T(8,128)(2,1)S(1)}, bf16[3,256,512]{2,1,0:T(8,128)(2,1)}, u32[]{:S(2)}, u32[]{:S(2)}) %collective-permute-start.36) | collective-permute-done | bytes 786464 | tf_op jit(solution)/shard_map/ppermute | solution.py:635
  226.0 1.5 collective-permute-start.40
  230.3 1.5 collective-permute-start.25
  235.2 3.6 %collective-permute-done.26 = f32[256,1]{1,0:T(8,128)S(1)} collective-permute-done((f32[256,1]{1,0:T(8,128)S(1)}, f32[256,1]{1,0:T(8,128)S(1)}, u32[]{:S(2)}, u32[]{:S(2)}) %collective-permute-start.26) | collective-permute-done | bytes 1056 | tf_op jit(solution)/shard_map/ppermute | solution.py:638
  243.6 1.4 halve.2
  245.1 1.7 collective-permute-start.33
  248.4 2.3 term_step.10
  250.8 2.3 term_step.11
  253.1 6.6 %collective-permute-done.37.refs_0_.refs_6_ = bf16[3,256,512]{2,1,0:T(8,128)(2,1)} collective-permute-done((bf16[3,256,512]{2,1,0:T(8,128)(2,1)}, bf16[3,256,512]{2,1,0:T(8,128)(2,1)}, u32[]{:S(2)}, u32[]{:S(2)}) %collective-permute-start.37) | collective-permute-done | bytes 786464 | tf_op jit(solution)/shard_map/ppermute | solution.py:635
  261.1 2.5 collective-permute-start.41
  263.6 2.3 term_step.12
  266.0 2.4 term_step.13
  270.4 6.3 %grads.2 = (f32[3,512,1024]{2,1,0:T(8,128)}, f32[8,128]{1,0:T(8,128)S(1)}) custom-call(bf16[512,2048]{1,0:T(8,128)(2,1)S(1)} %copy-done.1, bf16[3,256,512]{2,1,0:T(8,128)(2,1)S(1)} %copy-done.14, bf16[3,256,512]{2,1,0:T(8,128)(2,1)S(1)} %copy-done.17, bf16[3,256,512]{2,1,0:T(8,128)(2,1)S(1)} %copy-done.20, ...), custom_call_target="tpu_custom_call" | custom-call | flops 3221225472 | bytes 9437184 | tf_op jit(solution)/shard_map/grads/pallas_call | solution.py:438
  276.7 1.7 term_last.1
  278.3 1.6 collective-permute-start.47
  280.0 1.5 collective-permute-done.47.came
  284.4 6.3 %grads.3 = (f32[3,512,1024]{2,1,0:T(8,128)}, f32[8,128]{1,0:T(8,128)S(1)}) custom-call(bf16[512,2048]{1,0:T(8,128)(2,1)S(1)} %copy-done.1, bf16[3,256,512]{2,1,0:T(8,128)(2,1)S(1)} %copy-done.6, bf16[3,256,512]{2,1,0:T(8,128)(2,1)S(1)} %copy-done.8, bf16[3,256,512]{2,1,0:T(8,128)(2,1)S(1)} %copy-done.10, ...), custom_call_target="tpu_custom_call", output_to_operand_aliasing={{0}: (10, {})} | custom-call | flops 3221225472 | bytes 9437184 | tf_op jit(solution)/shard_map/grads/pallas_call | solution.py:438
  291.3 6.1 %collective-permute-start.49 = (bf16[128,512]{1,0:T(8,128)(2,1)S(1)}, bf16[128,512]{1,0:T(8,128)(2,1)S(1)}, u32[]{:S(2)}, u32[]{:S(2)}) collective-permute-start(bf16[128,512]{1,0:T(8,128)(2,1)S(1)} %get-tuple-element.138), channel_id=1, source_target_pairs={{0,0},{1,1},{2,8},{3,9},{4,16},{5,17},{6,24},{7,25},{8,4},{9,5},{1... | collective-permute-start | bytes 393224 | tf_op jit(solution)/shard_map/ppermute | solution.py:696
  298.8 3.8 %collective-permute-start.45 = (bf16[128,512]{1,0:T(8,128)(2,1)S(1)}, bf16[128,512]{1,0:T(8,128)(2,1)S(1)}, u32[]{:S(2)}, u32[]{:S(2)}) collective-permute-start(bf16[128,512]{1,0:T(8,128)(2,1)S(1)} %get-tuple-element.133), channel_id=1, source_target_pairs={{0,0},{1,1},{2,8},{3,9},{4,16},{5,17},{6,24},{7,25},{8,4},{9,5},{1... | collective-permute-start | bytes 393224 | tf_op jit(solution)/shard_map/ppermute | solution.py:696
  304.1 7.8 %collective-permute-done.50.refs_3_ = bf16[128,512]{1,0:T(8,128)(2,1)S(1)} collective-permute-done((bf16[128,512]{1,0:T(8,128)(2,1)S(1)}, bf16[128,512]{1,0:T(8,128)(2,1)S(1)}, u32[]{:S(2)}, u32[]{:S(2)}) %collective-permute-start.50) | collective-permute-done | bytes 131104 | tf_op jit(solution)/shard_map/ppermute | solution.py:696
  312.7 2.0 collective-permute-done.46.refs_1_
  314.8 1.6 finish.1
  (137 shorter events, 40.8 us)
Async XLA Ops:
  5.7 8.4 %collective-permute-start.6 = (bf16[256,256]{1,0:T(8,128)(2,1)S(1)}, bf16[256,256]{1,0:T(8,128)(2,1)S(1)}, u32[]{:S(2)}, u32[]{:S(2)}) collective-permute-start(bf16[256,256]{1,0:T(8,128)(2,1)S(1)} %get-tuple-element.79), channel_id=1, source_target_pairs={{0,7},{2,5},{4,3},{6,1},{7,0},{5,2},{3,4},{1,6},{8,15},{10,13},{12... | collective-permute-start | bytes 393224 | tf_op jit(solution)/shard_map/ppermute | solution.py:635
  10.8 10.0 %collective-permute-start = (bf16[256,256]{1,0:T(8,128)(2,1)S(1)}, bf16[256,256]{1,0:T(8,128)(2,1)S(1)}, u32[]{:S(2)}, u32[]{:S(2)}) collective-permute-start(bf16[256,256]{1,0:T(8,128)(2,1)S(1)} %get-tuple-element.73), channel_id=1, source_target_pairs={{0,2},{2,4},{4,6},{6,7},{7,5},{5,3},{3,1},{1,0},{8,10},{10,12},{12... | collective-permute-start | bytes 393224 | tf_op jit(solution)/shard_map/ppermute | solution.py:635
  14.1 8.0 %collective-permute-start.7 = (bf16[256,256]{1,0:T(8,128)(2,1)S(1)}, bf16[256,256]{1,0:T(8,128)(2,1)S(1)}, u32[]{:S(2)}, u32[]{:S(2)}) collective-permute-start(bf16[256,256]{1,0:T(8,128)(2,1)S(1)} %collective-permute-done.6.mine.mine_far), channel_id=1, source_target_pairs={{0,8},{8,0},{16,24},{24,16},{1,9},{9,1},{17,25},{25,17},{2,10},{10... | collective-permute-start | bytes 393224 | tf_op jit(solution)/shard_map/ppermute | solution.py:638
  16.2 13.6 %collective-permute-start.1 = (bf16[256,256]{1,0:T(8,128)(2,1)S(1)}, bf16[256,256]{1,0:T(8,128)(2,1)S(1)}, u32[]{:S(2)}, u32[]{:S(2)}) collective-permute-start(bf16[256,256]{1,0:T(8,128)(2,1)S(1)} %get-tuple-element.74), channel_id=1, source_target_pairs={{0,1},{2,0},{4,2},{6,4},{7,6},{5,7},{3,5},{1,3},{8,9},{10,8},{12,1... | collective-permute-start | bytes 393224 | tf_op jit(solution)/shard_map/ppermute | solution.py:635
  16.5 13.3 %collective-permute-start.2 = (bf16[256,256]{1,0:T(8,128)(2,1)S(1)}, bf16[256,256]{1,0:T(8,128)(2,1)S(1)}, u32[]{:S(2)}, u32[]{:S(2)}) collective-permute-start(bf16[256,256]{1,0:T(8,128)(2,1)S(1)} %get-tuple-element.75), channel_id=1, source_target_pairs={{0,4},{2,6},{4,7},{6,5},{7,3},{5,1},{3,0},{1,2},{8,12},{10,14},{12... | collective-permute-start | bytes 393224 | tf_op jit(solution)/shard_map/ppermute | solution.py:635
  19.7 10.1 %collective-permute-start.3 = (bf16[256,256]{1,0:T(8,128)(2,1)S(1)}, bf16[256,256]{1,0:T(8,128)(2,1)S(1)}, u32[]{:S(2)}, u32[]{:S(2)}) collective-permute-start(bf16[256,256]{1,0:T(8,128)(2,1)S(1)} %get-tuple-element.76), channel_id=1, source_target_pairs={{0,3},{2,1},{4,0},{6,2},{7,4},{5,6},{3,7},{1,5},{8,11},{10,9},{12,... | collective-permute-start | bytes 393224 | tf_op jit(solution)/shard_map/ppermute | solution.py:635
  20.9 9.8 %collective-permute-start.4 = (bf16[256,256]{1,0:T(8,128)(2,1)S(1)}, bf16[256,256]{1,0:T(8,128)(2,1)S(1)}, u32[]{:S(2)}, u32[]{:S(2)}) collective-permute-start(bf16[256,256]{1,0:T(8,128)(2,1)S(1)} %get-tuple-element.77), channel_id=1, source_target_pairs={{0,6},{2,7},{4,5},{6,3},{7,1},{5,0},{3,2},{1,4},{8,14},{10,15},{12... | collective-permute-start | bytes 393224 | tf_op jit(solution)/shard_map/ppermute | solution.py:635
  22.1 12.6 %collective-permute-start.5 = (bf16[256,256]{1,0:T(8,128)(2,1)S(1)}, bf16[256,256]{1,0:T(8,128)(2,1)S(1)}, u32[]{:S(2)}, u32[]{:S(2)}) collective-permute-start(bf16[256,256]{1,0:T(8,128)(2,1)S(1)} %get-tuple-element.78), channel_id=1, source_target_pairs={{0,5},{2,3},{4,1},{6,0},{7,2},{5,4},{3,6},{1,7},{8,13},{10,11},{12... | collective-permute-start | bytes 393224 | tf_op jit(solution)/shard_map/ppermute | solution.py:635
  24.1 1.9 copy-start.4
  34.7 14.2 %collective-permute-start.8 = (bf16[7,256,256]{2,1,0:T(8,128)(2,1)S(1)}, bf16[7,256,256]{2,1,0:T(8,128)(2,1)S(1)}, u32[]{:S(2)}, u32[]{:S(2)}) collective-permute-start(bf16[7,256,256]{2,1,0:T(8,128)(2,1)S(1)} %stack.1.refs_1_.refs_3_.mine), channel_id=1, source_target_pairs={{0,8},{8,0},{16,24},{24,16},{1,9},{9,1},{17,25},{25,17},{2,10},{10... | collective-permute-start | bytes 2752520 | tf_op jit(solution)/shard_map/ppermute | solution.py:638
  36.7 12.2 %collective-permute-start.9 = (bf16[3,128,512]{2,1,0:T(8,128)(2,1)S(1)}, bf16[3,128,512]{2,1,0:T(8,128)(2,1)S(1)}, u32[]{:S(2)}, u32[]{:S(2)}) collective-permute-start(bf16[3,128,512]{2,1,0:T(8,128)(2,1)S(1)} %get-tuple-element.81.refs_7_), channel_id=1, source_target_pairs={{0,2},{2,4},{4,6},{6,7},{7,5},{5,3},{3,1},{1,0},{8,10},{10,12},{12... | collective-permute-start | bytes 1179656 | tf_op jit(solution)/shard_map/ppermute | solution.py:635
  36.7 12.2 %collective-permute-start.10 = (bf16[3,128,512]{2,1,0:T(8,128)(2,1)S(1)}, bf16[3,128,512]{2,1,0:T(8,128)(2,1)S(1)}, u32[]{:S(2)}, u32[]{:S(2)}) collective-permute-start(bf16[3,128,512]{2,1,0:T(8,128)(2,1)S(1)} %get-tuple-element.82), channel_id=1, source_target_pairs={{0,1},{2,0},{4,2},{6,4},{7,6},{5,7},{3,5},{1,3},{8,9},{10,8},{12,1... | collective-permute-start | bytes 1179656 | tf_op jit(solution)/shard_map/ppermute | solution.py:635
  39.5 17.8 %collective-permute-start.17 = (bf16[3,128,512]{2,1,0:T(8,128)(2,1)S(1)}, bf16[3,128,512]{2,1,0:T(8,128)(2,1)S(1)}, u32[]{:S(2)}, u32[]{:S(2)}) collective-permute-start(bf16[3,128,512]{2,1,0:T(8,128)(2,1)S(1)} %get-tuple-element.90), channel_id=1, source_target_pairs={{0,2},{2,4},{4,6},{6,7},{7,5},{5,3},{3,1},{1,0},{8,10},{10,12},{12... | collective-permute-start | bytes 1179656 | tf_op jit(solution)/shard_map/ppermute | solution.py:635
  39.5 17.8 %collective-permute-start.18 = (bf16[3,128,512]{2,1,0:T(8,128)(2,1)S(1)}, bf16[3,128,512]{2,1,0:T(8,128)(2,1)S(1)}, u32[]{:S(2)}, u32[]{:S(2)}) collective-permute-start(bf16[3,128,512]{2,1,0:T(8,128)(2,1)S(1)} %get-tuple-element.91), channel_id=1, source_target_pairs={{0,1},{2,0},{4,2},{6,4},{7,6},{5,7},{3,5},{1,3},{8,9},{10,8},{12,1... | collective-permute-start | bytes 1179656 | tf_op jit(solution)/shard_map/ppermute | solution.py:635
  51.0 23.2 %collective-permute-start.11 = (bf16[3,256,512]{2,1,0:T(8,128)(2,1)S(1)}, bf16[3,256,512]{2,1,0:T(8,128)(2,1)S(1)}, u32[]{:S(2)}, u32[]{:S(2)}) collective-permute-start(bf16[3,256,512]{2,1,0:T(8,128)(2,1)S(1)} %get-tuple-element.83), channel_id=1, source_target_pairs={{0,2},{2,4},{4,6},{6,7},{7,5},{5,3},{3,1},{1,0},{8,10},{10,12},{12... | collective-permute-start | bytes 2359304 | tf_op jit(solution)/shard_map/ppermute | solution.py:635
  53.5 20.7 %collective-permute-start.12 = (bf16[3,256,512]{2,1,0:T(8,128)(2,1)S(1)}, bf16[3,256,512]{2,1,0:T(8,128)(2,1)S(1)}, u32[]{:S(2)}, u32[]{:S(2)}) collective-permute-start(bf16[3,256,512]{2,1,0:T(8,128)(2,1)S(1)} %get-tuple-element.84), channel_id=1, source_target_pairs={{0,1},{2,0},{4,2},{6,4},{7,6},{5,7},{3,5},{1,3},{8,9},{10,8},{12,1... | collective-permute-start | bytes 2359304 | tf_op jit(solution)/shard_map/ppermute | solution.py:635
  59.4 31.6 %collective-permute-start.19 = (bf16[3,256,512]{2,1,0:T(8,128)(2,1)S(1)}, bf16[3,256,512]{2,1,0:T(8,128)(2,1)S(1)}, u32[]{:S(2)}, u32[]{:S(2)}) collective-permute-start(bf16[3,256,512]{2,1,0:T(8,128)(2,1)S(1)} %get-tuple-element.92), channel_id=1, source_target_pairs={{0,2},{2,4},{4,6},{6,7},{7,5},{5,3},{3,1},{1,0},{8,10},{10,12},{12... | collective-permute-start | bytes 2359304 | tf_op jit(solution)/shard_map/ppermute | solution.py:635
  61.9 29.2 %collective-permute-start.20 = (bf16[3,256,512]{2,1,0:T(8,128)(2,1)S(1)}, bf16[3,256,512]{2,1,0:T(8,128)(2,1)S(1)}, u32[]{:S(2)}, u32[]{:S(2)}) collective-permute-start(bf16[3,256,512]{2,1,0:T(8,128)(2,1)S(1)} %get-tuple-element.93), channel_id=1, source_target_pairs={{0,1},{2,0},{4,2},{6,4},{7,6},{5,7},{3,5},{1,3},{8,9},{10,8},{12,1... | collective-permute-start | bytes 2359304 | tf_op jit(solution)/shard_map/ppermute | solution.py:635
  76.3 31.6 %collective-permute-start.13 = (bf16[3,256,512]{2,1,0:T(8,128)(2,1)S(1)}, bf16[3,256,512]{2,1,0:T(8,128)(2,1)S(1)}, u32[]{:S(2)}, u32[]{:S(2)}) collective-permute-start(bf16[3,256,512]{2,1,0:T(8,128)(2,1)S(1)} %get-tuple-element.85), channel_id=1, source_target_pairs={{0,2},{2,4},{4,6},{6,7},{7,5},{5,3},{3,1},{1,0},{8,10},{10,12},{12... | collective-permute-start | bytes 2359304 | tf_op jit(solution)/shard_map/ppermute | solution.py:635
  78.8 29.2 %collective-permute-start.14 = (bf16[3,256,512]{2,1,0:T(8,128)(2,1)S(1)}, bf16[3,256,512]{2,1,0:T(8,128)(2,1)S(1)}, u32[]{:S(2)}, u32[]{:S(2)}) collective-permute-start(bf16[3,256,512]{2,1,0:T(8,128)(2,1)S(1)} %get-tuple-element.86), channel_id=1, source_target_pairs={{0,1},{2,0},{4,2},{6,4},{7,6},{5,7},{3,5},{1,3},{8,9},{10,8},{12,1... | collective-permute-start | bytes 2359304 | tf_op jit(solution)/shard_map/ppermute | solution.py:635
  93.1 31.6 %collective-permute-start.21 = (bf16[3,256,512]{2,1,0:T(8,128)(2,1)S(1)}, bf16[3,256,512]{2,1,0:T(8,128)(2,1)S(1)}, u32[]{:S(2)}, u32[]{:S(2)}) collective-permute-start(bf16[3,256,512]{2,1,0:T(8,128)(2,1)S(1)} %get-tuple-element.94), channel_id=1, source_target_pairs={{0,2},{2,4},{4,6},{6,7},{7,5},{5,3},{3,1},{1,0},{8,10},{10,12},{12... | collective-permute-start | bytes 2359304 | tf_op jit(solution)/shard_map/ppermute | solution.py:635
  95.6 29.2 %collective-permute-start.22 = (bf16[3,256,512]{2,1,0:T(8,128)(2,1)S(1)}, bf16[3,256,512]{2,1,0:T(8,128)(2,1)S(1)}, u32[]{:S(2)}, u32[]{:S(2)}) collective-permute-start(bf16[3,256,512]{2,1,0:T(8,128)(2,1)S(1)} %get-tuple-element.95), channel_id=1, source_target_pairs={{0,1},{2,0},{4,2},{6,4},{7,6},{5,7},{3,5},{1,3},{8,9},{10,8},{12,1... | collective-permute-start | bytes 2359304 | tf_op jit(solution)/shard_map/ppermute | solution.py:635
  96.8 28.0 %copy-start = (bf16[512,2048]{1,0:T(8,128)(2,1)}, bf16[512,2048]{1,0:T(8,128)(2,1)S(1)}, u32[]{:S(2)}) copy-start(bf16[512,2048]{1,0:T(8,128)(2,1)S(1)} %turn.1.refs_9_.refs_0_) | copy-start | bytes 6291460
  110.0 31.6 %collective-permute-start.15 = (bf16[3,256,512]{2,1,0:T(8,128)(2,1)S(1)}, bf16[3,256,512]{2,1,0:T(8,128)(2,1)S(1)}, u32[]{:S(2)}, u32[]{:S(2)}) collective-permute-start(bf16[3,256,512]{2,1,0:T(8,128)(2,1)S(1)} %get-tuple-element.87), channel_id=1, source_target_pairs={{0,2},{2,4},{4,6},{6,7},{7,5},{5,3},{3,1},{1,0},{8,10},{10,12},{12... | collective-permute-start | bytes 2359304 | tf_op jit(solution)/shard_map/ppermute | solution.py:635
  112.5 29.2 %copy-start.11 = (bf16[256,1024]{1,0:T(8,128)(2,1)S(1)}, bf16[256,1024]{1,0:T(8,128)(2,1)}, u32[]{:S(2)}) copy-start(bf16[256,1024]{1,0:T(8,128)(2,1)} %d_out.3) | copy-start | bytes 1572868
  112.5 29.2 %collective-permute-start.16 = (bf16[3,256,512]{2,1,0:T(8,128)(2,1)S(1)}, bf16[3,256,512]{2,1,0:T(8,128)(2,1)S(1)}, u32[]{:S(2)}, u32[]{:S(2)}) collective-permute-start(bf16[3,256,512]{2,1,0:T(8,128)(2,1)S(1)} %get-tuple-element.88), channel_id=1, source_target_pairs={{0,1},{2,0},{4,2},{6,4},{7,6},{5,7},{3,5},{1,3},{8,9},{10,8},{12,1... | collective-permute-start | bytes 2359304 | tf_op jit(solution)/shard_map/ppermute | solution.py:635
  126.8 31.6 %collective-permute-start.23 = (bf16[3,256,512]{2,1,0:T(8,128)(2,1)S(1)}, bf16[3,256,512]{2,1,0:T(8,128)(2,1)S(1)}, u32[]{:S(2)}, u32[]{:S(2)}) collective-permute-start(bf16[3,256,512]{2,1,0:T(8,128)(2,1)S(1)} %get-tuple-element.96), channel_id=1, source_target_pairs={{0,2},{2,4},{4,6},{6,7},{7,5},{5,3},{3,1},{1,0},{8,10},{10,12},{12... | collective-permute-start | bytes 2359304 | tf_op jit(solution)/shard_map/ppermute | solution.py:635
  129.3 29.2 %collective-permute-start.24 = (bf16[3,256,512]{2,1,0:T(8,128)(2,1)S(1)}, bf16[3,256,512]{2,1,0:T(8,128)(2,1)S(1)}, u32[]{:S(2)}, u32[]{:S(2)}) collective-permute-start(bf16[3,256,512]{2,1,0:T(8,128)(2,1)S(1)} %get-tuple-element.97), channel_id=1, source_target_pairs={{0,1},{2,0},{4,2},{6,4},{7,6},{5,7},{3,5},{1,3},{8,9},{10,8},{12,1... | collective-permute-start | bytes 2359304 | tf_op jit(solution)/shard_map/ppermute | solution.py:635
  149.5 16.2 %copy-start.12 = (bf16[3,256,512]{2,1,0:T(8,128)(2,1)}, bf16[3,256,512]{2,1,0:T(8,128)(2,1)S(1)}, u32[]{:S(2)}) copy-start(bf16[3,256,512]{2,1,0:T(8,128)(2,1)S(1)} %get-tuple-element.103.refs_0_.refs_1_) | copy-start | bytes 2359300
  149.5 25.8 %collective-permute-start.27 = (bf16[3,256,512]{2,1,0:T(8,128)(2,1)S(1)}, bf16[3,256,512]{2,1,0:T(8,128)(2,1)S(1)}, u32[]{:S(2)}, u32[]{:S(2)}) collective-permute-start(bf16[3,256,512]{2,1,0:T(8,128)(2,1)S(1)} %get-tuple-element.103.refs_0_.refs_1_), channel_id=1, source_target_pairs={{0,2},{2,4},{4,6},{6,7},{7,5},{5,3},{3,1},{1,0},{8,10},{10,12},{12... | collective-permute-start | bytes 2359304 | tf_op jit(solution)/shard_map/ppermute | solution.py:635
  151.9 24.3 %collective-permute-start.30 = (bf16[3,256,512]{2,1,0:T(8,128)(2,1)S(1)}, bf16[3,256,512]{2,1,0:T(8,128)(2,1)S(1)}, u32[]{:S(2)}, u32[]{:S(2)}) collective-permute-start(bf16[3,256,512]{2,1,0:T(8,128)(2,1)S(1)} %get-tuple-element.103.refs_0_.refs_1_), channel_id=1, source_target_pairs={{0,1},{2,0},{4,2},{6,4},{7,6},{5,7},{3,5},{1,3},{8,9},{10,8},{12,1... | collective-permute-start | bytes 2359304 | tf_op jit(solution)/shard_map/ppermute | solution.py:635
  167.1 25.1 %collective-permute-start.35 = (bf16[3,256,512]{2,1,0:T(8,128)(2,1)S(1)}, bf16[3,256,512]{2,1,0:T(8,128)(2,1)S(1)}, u32[]{:S(2)}, u32[]{:S(2)}) collective-permute-start(bf16[3,256,512]{2,1,0:T(8,128)(2,1)S(1)} %get-tuple-element.108.refs_0_.refs_1_), channel_id=1, source_target_pairs={{0,2},{2,4},{4,6},{6,7},{7,5},{5,3},{3,1},{1,0},{8,10},{10,12},{12... | collective-permute-start | bytes 2359304 | tf_op jit(solution)/shard_map/ppermute | solution.py:635
  169.5 23.5 %collective-permute-start.38 = (bf16[3,256,512]{2,1,0:T(8,128)(2,1)S(1)}, bf16[3,256,512]{2,1,0:T(8,128)(2,1)S(1)}, u32[]{:S(2)}, u32[]{:S(2)}) collective-permute-start(bf16[3,256,512]{2,1,0:T(8,128)(2,1)S(1)} %get-tuple-element.108.refs_0_.refs_1_), channel_id=1, source_target_pairs={{0,1},{2,0},{4,2},{6,4},{7,6},{5,7},{3,5},{1,3},{8,9},{10,8},{12,1... | collective-permute-start | bytes 2359304 | tf_op jit(solution)/shard_map/ppermute | solution.py:635
  175.3 33.8 %collective-permute-start.28 = (bf16[3,256,512]{2,1,0:T(8,128)(2,1)S(1)}, bf16[3,256,512]{2,1,0:T(8,128)(2,1)}, u32[]{:S(2)}, u32[]{:S(2)}) collective-permute-start(bf16[3,256,512]{2,1,0:T(8,128)(2,1)S(1)} %collective-permute-done.27.refs_1_.refs_2_), channel_id=1, source_target_pairs={{0,2},{2,4},{4,6},{6,7},{7,5},{5,3},{3,1},{1,0},{8,10},{10,12},{12... | collective-permute-start | bytes 2359304 | tf_op jit(solution)/shard_map/ppermute | solution.py:635
  176.2 32.9 %collective-permute-start.31 = (bf16[3,256,512]{2,1,0:T(8,128)(2,1)S(1)}, bf16[3,256,512]{2,1,0:T(8,128)(2,1)}, u32[]{:S(2)}, u32[]{:S(2)}) collective-permute-start(bf16[3,256,512]{2,1,0:T(8,128)(2,1)S(1)} %collective-permute-done.30.refs_2_.refs_3_), channel_id=1, source_target_pairs={{0,1},{2,0},{4,2},{6,4},{7,6},{5,7},{3,5},{1,3},{8,9},{10,8},{12,1... | collective-permute-start | bytes 2359304 | tf_op jit(solution)/shard_map/ppermute | solution.py:635
  192.2 33.8 %collective-permute-start.36 = (bf16[3,256,512]{2,1,0:T(8,128)(2,1)S(1)}, bf16[3,256,512]{2,1,0:T(8,128)(2,1)}, u32[]{:S(2)}, u32[]{:S(2)}) collective-permute-start(bf16[3,256,512]{2,1,0:T(8,128)(2,1)S(1)} %collective-permute-done.35.refs_1_.refs_2_), channel_id=1, source_target_pairs={{0,2},{2,4},{4,6},{6,7},{7,5},{5,3},{3,1},{1,0},{8,10},{10,12},{12... | collective-permute-start | bytes 2359304 | tf_op jit(solution)/shard_map/ppermute | solution.py:635
  193.1 32.9 %collective-permute-start.39 = (bf16[3,256,512]{2,1,0:T(8,128)(2,1)S(1)}, bf16[3,256,512]{2,1,0:T(8,128)(2,1)}, u32[]{:S(2)}, u32[]{:S(2)}) collective-permute-start(bf16[3,256,512]{2,1,0:T(8,128)(2,1)S(1)} %collective-permute-done.38.refs_2_.refs_3_), channel_id=1, source_target_pairs={{0,1},{2,0},{4,2},{6,4},{7,6},{5,7},{3,5},{1,3},{8,9},{10,8},{12,1... | collective-permute-start | bytes 2359304 | tf_op jit(solution)/shard_map/ppermute | solution.py:635
  209.1 34.5 %collective-permute-start.29 = (bf16[3,256,512]{2,1,0:T(8,128)(2,1)}, bf16[3,256,512]{2,1,0:T(8,128)(2,1)}, u32[]{:S(2)}, u32[]{:S(2)}) collective-permute-start(bf16[3,256,512]{2,1,0:T(8,128)(2,1)} %collective-permute-done.28.refs_0_.refs_4_), channel_id=1, source_target_pairs={{0,2},{2,4},{4,6},{6,7},{7,5},{5,3},{3,1},{1,0},{8,10},{10,12},{12... | collective-permute-start | bytes 2359304 | tf_op jit(solution)/shard_map/ppermute | solution.py:635
  209.2 34.5 %collective-permute-start.32 = (bf16[3,256,512]{2,1,0:T(8,128)(2,1)}, bf16[3,256,512]{2,1,0:T(8,128)(2,1)}, u32[]{:S(2)}, u32[]{:S(2)}) collective-permute-start(bf16[3,256,512]{2,1,0:T(8,128)(2,1)} %collective-permute-done.31.refs_1_.refs_5_), channel_id=1, source_target_pairs={{0,1},{2,0},{4,2},{6,4},{7,6},{5,7},{3,5},{1,3},{8,9},{10,8},{12,1... | collective-permute-start | bytes 2359304 | tf_op jit(solution)/shard_map/ppermute | solution.py:635
  226.0 33.7 %collective-permute-start.37 = (bf16[3,256,512]{2,1,0:T(8,128)(2,1)}, bf16[3,256,512]{2,1,0:T(8,128)(2,1)}, u32[]{:S(2)}, u32[]{:S(2)}) collective-permute-start(bf16[3,256,512]{2,1,0:T(8,128)(2,1)} %collective-permute-done.36.refs_0_.refs_4_), channel_id=1, source_target_pairs={{0,2},{2,4},{4,6},{6,7},{7,5},{5,3},{3,1},{1,0},{8,10},{10,12},{12... | collective-permute-start | bytes 2359304 | tf_op jit(solution)/shard_map/ppermute | solution.py:635
  226.0 33.7 %collective-permute-start.40 = (bf16[3,256,512]{2,1,0:T(8,128)(2,1)}, bf16[3,256,512]{2,1,0:T(8,128)(2,1)}, u32[]{:S(2)}, u32[]{:S(2)}) collective-permute-start(bf16[3,256,512]{2,1,0:T(8,128)(2,1)} %collective-permute-done.39.refs_1_.refs_5_), channel_id=1, source_target_pairs={{0,1},{2,0},{4,2},{6,4},{7,6},{5,7},{3,5},{1,3},{8,9},{10,8},{12,1... | collective-permute-start | bytes 2359304 | tf_op jit(solution)/shard_map/ppermute | solution.py:635
  230.3 2.7 collective-permute-start.25
  233.9 4.9 %collective-permute-start.26 = (f32[256,1]{1,0:T(8,128)S(1)}, f32[256,1]{1,0:T(8,128)S(1)}, u32[]{:S(2)}, u32[]{:S(2)}) collective-permute-start(f32[256,1]{1,0:T(8,128)S(1)} %add.31), channel_id=1, source_target_pairs={{0,16},{8,24},{16,0},{24,8},{1,17},{9,25},{17,1},{25,9},{2,18},{10... | collective-permute-start | bytes 3080 | tf_op jit(solution)/shard_map/ppermute | solution.py:638
  242.2 4.8 %copy-start.6 = (bf16[3,256,512]{2,1,0:T(8,128)(2,1)S(1)}, bf16[3,256,512]{2,1,0:T(8,128)(2,1)}, u32[]{:S(2)}) copy-start(bf16[3,256,512]{2,1,0:T(8,128)(2,1)} %copy-done.5) | copy-start | bytes 2359300
  242.2 4.8 %copy-start.8 = (bf16[3,256,512]{2,1,0:T(8,128)(2,1)S(1)}, bf16[3,256,512]{2,1,0:T(8,128)(2,1)}, u32[]{:S(2)}) copy-start(bf16[3,256,512]{2,1,0:T(8,128)(2,1)} %copy-done.7) | copy-start | bytes 2359300
  242.2 4.8 %copy-start.10 = (bf16[3,256,512]{2,1,0:T(8,128)(2,1)S(1)}, bf16[3,256,512]{2,1,0:T(8,128)(2,1)}, u32[]{:S(2)}) copy-start(bf16[3,256,512]{2,1,0:T(8,128)(2,1)} %copy-done.9) | copy-start | bytes 2359300
  245.1 23.4 %collective-permute-start.33 = (bf16[3,128,512]{2,1,0:T(8,128)(2,1)S(1)}, bf16[3,128,512]{2,1,0:T(8,128)(2,1)S(1)}, u32[]{:S(2)}, u32[]{:S(2)}) collective-permute-start(bf16[3,128,512]{2,1,0:T(8,128)(2,1)S(1)} %get-tuple-element.104), channel_id=1, source_target_pairs={{0,2},{2,4},{4,6},{6,7},{7,5},{5,3},{3,1},{1,0},{8,10},{10,12},{12... | collective-permute-start | bytes 1179656 | tf_op jit(solution)/shard_map/ppermute | solution.py:635
  246.8 21.7 %collective-permute-start.34 = (bf16[3,128,512]{2,1,0:T(8,128)(2,1)S(1)}, bf16[3,128,512]{2,1,0:T(8,128)(2,1)S(1)}, u32[]{:S(2)}, u32[]{:S(2)}) collective-permute-start(bf16[3,128,512]{2,1,0:T(8,128)(2,1)S(1)} %get-tuple-element.105), channel_id=1, source_target_pairs={{0,1},{2,0},{4,2},{6,4},{7,6},{5,7},{3,5},{1,3},{8,9},{10,8},{12,1... | collective-permute-start | bytes 1179656 | tf_op jit(solution)/shard_map/ppermute | solution.py:635
  261.1 15.5 %collective-permute-start.41 = (bf16[3,128,512]{2,1,0:T(8,128)(2,1)S(1)}, bf16[3,128,512]{2,1,0:T(8,128)(2,1)S(1)}, u32[]{:S(2)}, u32[]{:S(2)}) collective-permute-start(bf16[3,128,512]{2,1,0:T(8,128)(2,1)S(1)} %get-tuple-element.119), channel_id=1, source_target_pairs={{0,2},{2,4},{4,6},{6,7},{7,5},{5,3},{3,1},{1,0},{8,10},{10,12},{12... | collective-permute-start | bytes 1179656 | tf_op jit(solution)/shard_map/ppermute | solution.py:635
  263.6 13.0 %collective-permute-start.42 = (bf16[3,128,512]{2,1,0:T(8,128)(2,1)S(1)}, bf16[3,128,512]{2,1,0:T(8,128)(2,1)S(1)}, u32[]{:S(2)}, u32[]{:S(2)}) collective-permute-start(bf16[3,128,512]{2,1,0:T(8,128)(2,1)S(1)} %get-tuple-element.120), channel_id=1, source_target_pairs={{0,1},{2,0},{4,2},{6,4},{7,6},{5,7},{3,5},{1,3},{8,9},{10,8},{12,1... | collective-permute-start | bytes 1179656 | tf_op jit(solution)/shard_map/ppermute | solution.py:635
  266.0 3.1 copy-start.20
  268.4 1.8 copy-start.14
  268.4 2.0 copy-start.17
  278.3 3.2 %collective-permute-start.47 = (bf16[4,128,512]{2,1,0:T(8,128)(2,1)S(1)}, bf16[4,128,512]{2,1,0:T(8,128)(2,1)S(1)}, u32[]{:S(2)}, u32[]{:S(2)}) collective-permute-start(bf16[4,128,512]{2,1,0:T(8,128)(2,1)S(1)} %get-tuple-element.135), channel_id=1, source_target_pairs={{0,8},{8,0},{16,24},{24,16},{1,9},{9,1},{17,25},{25,17},{2,10},{10... | collective-permute-start | bytes 1572872 | tf_op jit(solution)/shard_map/ppermute | solution.py:638
  280.0 3.5 %collective-permute-start.43 = (bf16[4,128,512]{2,1,0:T(8,128)(2,1)S(1)}, bf16[4,128,512]{2,1,0:T(8,128)(2,1)S(1)}, u32[]{:S(2)}, u32[]{:S(2)}) collective-permute-start(bf16[4,128,512]{2,1,0:T(8,128)(2,1)S(1)} %get-tuple-element.127), channel_id=1, source_target_pairs={{0,8},{8,0},{16,24},{24,16},{1,9},{9,1},{17,25},{25,17},{2,10},{10... | collective-permute-start | bytes 1572872 | tf_op jit(solution)/shard_map/ppermute | solution.py:638
  282.1 8.5 %collective-permute-start.48 = (bf16[2,128,512]{2,1,0:T(8,128)(2,1)S(1)}, bf16[2,128,512]{2,1,0:T(8,128)(2,1)S(1)}, u32[]{:S(2)}, u32[]{:S(2)}) collective-permute-start(bf16[2,128,512]{2,1,0:T(8,128)(2,1)S(1)} %get-tuple-element.137), channel_id=1, source_target_pairs={{0,16},{8,24},{16,0},{24,8},{1,17},{9,25},{17,1},{25,9},{2,18},{10... | collective-permute-start | bytes 786440 | tf_op jit(solution)/shard_map/ppermute | solution.py:638
  284.0 14.1 %collective-permute-start.44 = (bf16[2,128,512]{2,1,0:T(8,128)(2,1)S(1)}, bf16[2,128,512]{2,1,0:T(8,128)(2,1)S(1)}, u32[]{:S(2)}, u32[]{:S(2)}) collective-permute-start(bf16[2,128,512]{2,1,0:T(8,128)(2,1)S(1)} %get-tuple-element.129), channel_id=1, source_target_pairs={{0,16},{8,24},{16,0},{24,8},{1,17},{9,25},{17,1},{25,9},{2,18},{10... | collective-permute-start | bytes 786440 | tf_op jit(solution)/shard_map/ppermute | solution.py:638
  284.4 18.9 %copy-start.22 = (bf16[256,512]{1,0:T(8,128)(2,1)S(1)}, bf16[256,512]{1,0:T(8,128)(2,1)}, u32[]{:S(2)}) copy-start(bf16[256,512]{1,0:T(8,128)(2,1)} %copy-done.21) | copy-start | bytes 786436
  284.4 30.4 %copy-start.24 = (f32[256,128]{1,0:T(8,128)S(1)}, f32[256,128]{1,0:T(8,128)}, u32[]{:S(2)}) copy-start(f32[256,128]{1,0:T(8,128)} %copy-done.23) | copy-start | bytes 393220
  290.7 24.1 %copy-start.3 = (bf16[256,4096]{1,0:T(8,128)(2,1)S(1)}, bf16[256,4096]{1,0:T(8,128)(2,1)}, u32[]{:S(2)}) copy-start(bf16[256,4096]{1,0:T(8,128)(2,1)} %tokens.3) | copy-start | bytes 6291460
  291.3 12.9 %collective-permute-start.49 = (bf16[128,512]{1,0:T(8,128)(2,1)S(1)}, bf16[128,512]{1,0:T(8,128)(2,1)S(1)}, u32[]{:S(2)}, u32[]{:S(2)}) collective-permute-start(bf16[128,512]{1,0:T(8,128)(2,1)S(1)} %get-tuple-element.138), channel_id=1, source_target_pairs={{0,0},{1,1},{2,8},{3,9},{4,16},{5,17},{6,24},{7,25},{8,4},{9,5},{1... | collective-permute-start | bytes 393224 | tf_op jit(solution)/shard_map/ppermute | solution.py:696
  297.4 14.6 %collective-permute-start.50 = (bf16[128,512]{1,0:T(8,128)(2,1)S(1)}, bf16[128,512]{1,0:T(8,128)(2,1)S(1)}, u32[]{:S(2)}, u32[]{:S(2)}) collective-permute-start(bf16[128,512]{1,0:T(8,128)(2,1)S(1)} %get-tuple-element.139), channel_id=1, source_target_pairs={{0,1},{1,0},{2,9},{3,8},{4,17},{5,16},{6,25},{7,24},{8,5},{9,4},{1... | collective-permute-start | bytes 393224 | tf_op jit(solution)/shard_map/ppermute | solution.py:696
  298.8 14.0 %collective-permute-start.45 = (bf16[128,512]{1,0:T(8,128)(2,1)S(1)}, bf16[128,512]{1,0:T(8,128)(2,1)S(1)}, u32[]{:S(2)}, u32[]{:S(2)}) collective-permute-start(bf16[128,512]{1,0:T(8,128)(2,1)S(1)} %get-tuple-element.133), channel_id=1, source_target_pairs={{0,0},{1,1},{2,8},{3,9},{4,16},{5,17},{6,24},{7,25},{8,4},{9,5},{1... | collective-permute-start | bytes 393224 | tf_op jit(solution)/shard_map/ppermute | solution.py:696
  302.6 12.2 %collective-permute-start.46 = (bf16[128,512]{1,0:T(8,128)(2,1)S(1)}, bf16[128,512]{1,0:T(8,128)(2,1)S(1)}, u32[]{:S(2)}, u32[]{:S(2)}) collective-permute-start(bf16[128,512]{1,0:T(8,128)(2,1)S(1)} %get-tuple-element.134), channel_id=1, source_target_pairs={{0,1},{1,0},{2,9},{3,8},{4,17},{5,16},{6,25},{7,24},{8,5},{9,4},{1... | collective-permute-start | bytes 393224 | tf_op jit(solution)/shard_map/ppermute | solution.py:696
  (15 other events, 14.6 us)

commit v15 on v14

--- a/solution.py
+++ b/solution.py
@@ -554,24 +554,26 @@
     )(idx, keep, came)
 
 
-def order_kernel(column, idx, keep, came, *outs):
+def order_kernel(column, idx, keep_0, came_0, keep_1, came_1, *outs):
+    half = keep_0.shape[1]
     for turn, out in enumerate(outs):
         block = idx[column + turn]
-        out[...] = (keep[block] + came[block].astype(jnp.float32)).astype(jnp.bfloat16)
-
-
-def order_sum(idx, column, keep, came, ties):
+        out[:half] = (keep_0[block] + came_0[block].astype(jnp.float32)).astype(jnp.bfloat16)
+        out[half:] = (keep_1[block] + came_1[block].astype(jnp.float32)).astype(jnp.bfloat16)
+
+
+def order_sum(idx, column, halves, ties):
     whole = pl.BlockSpec(memory_space=pltpu.VMEM)
-    count = keep.shape[0]
-    return pl.pallas_call(
-        tied(functools.partial(order_kernel, column), 3, len(ties)),
-        in_specs=[pl.BlockSpec(memory_space=pltpu.SMEM), whole, whole, *tie_specs(ties)],
+    count, rows, depth = halves[0].shape
+    return pl.pallas_call(
+        tied(functools.partial(order_kernel, column), 5, len(ties)),
+        in_specs=[pl.BlockSpec(memory_space=pltpu.SMEM), *[whole] * 4, *tie_specs(ties)],
         out_specs=[whole] * count,
-        out_shape=[jax.ShapeDtypeStruct(keep.shape[1:], jnp.bfloat16)] * count,
+        out_shape=[jax.ShapeDtypeStruct((2 * rows, depth), jnp.bfloat16)] * count,
         compiler_params=pltpu.CompilerParams(vmem_limit_bytes=4 * MIB),
-        cost_estimate=cost(0, 8 * count * keep.shape[1] * keep.shape[2]),
+        cost_estimate=cost(0, 16 * count * rows * depth),
         name="order_sum",
-    )(idx, keep, came, *ties)
+    )(idx, *halves, *ties)
 
 
 def finish_kernel(column, width, idx, tokens, gain, inverse, dots, *refs):
@@ -676,14 +678,14 @@
         dots = dots + swap(dots, bit)
         bit *= 2
 
-    def sum_nodes(keep, send, ties):
+    def sum_nodes(keep, send):
         column = 4 * size + 1
         bit = 1
         while 2 * bit < nodes:
             keep, send = split_sum(idx, column, group, keep, swap(send, bit))
             column += 1
             bit *= 2
-        return order_sum(idx, column, keep, swap(send, bit), ties)
+        return keep, swap(send, bit)
 
     def relocate(blocks):
         came = []
@@ -720,9 +722,9 @@
         idx, turned, lasts, gathered[1][-2:], terms[1], [done]
     )
     grads, done = grads_chunk(rows_turned, gathered[1], grads, [keep_1], 1, wide, columns)
-    first, second = sum_nodes(keep_0, send_0, [done]), sum_nodes(keep_1, send_1, [done])
-    came = [*relocate(first), *relocate(second)]
+    halves = [*sum_nodes(keep_0, send_0), *sum_nodes(keep_1, send_1)]
     column = idx.shape[0] - 1 - group
+    came = relocate(order_sum(idx, column - group, halves, [done]))
     d_tokens = finish(
         idx, column, tokens, norm_gain[None], inverse_rms, dots, came, width // nodes
     )

time: 317 us -> 321 us (1.013)
  the two profiles are of different devices: /device:TPU:1 before, /device:TPU:2 now
where the time goes in v15:
time: 321 us; the launch traced here: 316 us
  waiting for transfers between devices  162 us (50%)
  Pallas kernels  65.7 us (20%)
  starting transfers between devices  61.9 us (19%)
  local copies, waits for them, and re-layouts  18.4 us (6%)
  other arithmetic  6.83 us (2%)
    ppermute x39, waiting for transfers between devices, shift(): return lax.ppermute(array, 'local', moves)  135 us
    ppermute x39, starting transfers between devices, shift(): return lax.ppermute(array, 'local', moves)  54.2 us
    unnamed x56, local copies, waits for them, and re-layouts  15.5 us
    pallas_call x2, Pallas kernels, attention(): pl.pallas_call(attention_kernel, grid_spec=pltpu.PrefetchScalarGridSpec(n...  14.4 us
    ppermute x2, waiting for transfers between devices, relocate(): came.append(lax.ppermute(block, ('node', 'local'), moves))  13.8 us
    ppermute x8, waiting for transfers between devices, swap(): return lax.ppermute(array, 'node', [(n, n ^ bit) for n in range(nodes)])  12.9 us
    pallas_call x7, Pallas kernels, term_step(): pl.pallas_call(kernel, in_specs=[whole] * (1 + count + len(befores)), out...  12.8 us
    pallas_call x2, Pallas kernels, grads_chunk(): pl.pallas_call(tied(grads_kernel, 1 + len(pieces), len(ties)), grid=(3,),...  12.5 us
  transfers between devices with their start and end apart: 49, of which 30 were waited for; matrix products, arithmetic and copies ran while one was open for 3% of the time, Pallas kernels for 19%

profile of v15, /device:TPU:2, one launch (start us, length us, event | category | flops | bytes accessed | tf_op | source)
XLA Modules:
  0.0 315.7 jit_solution(16272455468063823220)
XLA Ops:
  2.0 1.6 copy-done.2
  3.6 1.4 normed_blocks.1
  5.1 4.6 %collective-permute-start.6 = (bf16[256,256]{1,0:T(8,128)(2,1)S(1)}, bf16[256,256]{1,0:T(8,128)(2,1)S(1)}, u32[]{:S(2)}, u32[]{:S(2)}) collective-permute-start(bf16[256,256]{1,0:T(8,128)(2,1)S(1)} %get-tuple-element.77), channel_id=1, source_target_pairs={{0,7},{2,5},{4,3},{6,1},{7,0},{5,2},{3,4},{1,6},{8,15},{10,13},{12... | collective-permute-start | bytes 393224 | tf_op jit(solution)/shard_map/ppermute | solution.py:637
  9.7 4.5 %collective-permute-done.6.mine.mine_far = bf16[256,256]{1,0:T(8,128)(2,1)S(1)} collective-permute-done((bf16[256,256]{1,0:T(8,128)(2,1)S(1)}, bf16[256,256]{1,0:T(8,128)(2,1)S(1)}, u32[]{:S(2)}, u32[]{:S(2)}) %collective-permute-start.6) | collective-permute-done | bytes 131104 | tf_op jit(solution)/shard_map/ppermute | solution.py:637
  14.7 3.5 %collective-permute-start.2 = (bf16[256,256]{1,0:T(8,128)(2,1)S(1)}, bf16[256,256]{1,0:T(8,128)(2,1)S(1)}, u32[]{:S(2)}, u32[]{:S(2)}) collective-permute-start(bf16[256,256]{1,0:T(8,128)(2,1)S(1)} %get-tuple-element.73), channel_id=1, source_target_pairs={{0,4},{2,6},{4,7},{6,5},{7,3},{5,1},{3,0},{1,2},{8,12},{10,14},{12... | collective-permute-start | bytes 393224 | tf_op jit(solution)/shard_map/ppermute | solution.py:637
  19.4 1.7 collective-permute-start.4
  21.1 2.1 collective-permute-start.5
  23.2 1.9 copy-done.4
  26.9 1.9 sum_first.1
  28.8 4.6 %collective-permute-done.3.refs_4_ = bf16[256,256]{1,0:T(8,128)(2,1)S(1)} collective-permute-done((bf16[256,256]{1,0:T(8,128)(2,1)S(1)}, bf16[256,256]{1,0:T(8,128)(2,1)S(1)}, u32[]{:S(2)}, u32[]{:S(2)}) %collective-permute-start.3) | collective-permute-done | bytes 131104 | tf_op jit(solution)/shard_map/ppermute | solution.py:637
  34.7 3.1 collective-permute-start.10
  37.9 2.0 collective-permute-start.18
  39.9 7.9 %collective-permute-done.9.refs_7_ = bf16[3,128,512]{2,1,0:T(8,128)(2,1)S(1)} collective-permute-done((bf16[3,128,512]{2,1,0:T(8,128)(2,1)S(1)}, bf16[3,128,512]{2,1,0:T(8,128)(2,1)S(1)}, u32[]{:S(2)}, u32[]{:S(2)}) %collective-permute-start.9) | collective-permute-done | bytes 393248 | tf_op jit(solution)/shard_map/ppermute | solution.py:637
  47.8 2.1 sum_step.6
  49.8 3.1 collective-permute-start.11
  53.0 3.2 %collective-permute-done.17.refs_7_ = bf16[3,128,512]{2,1,0:T(8,128)(2,1)S(1)} collective-permute-done((bf16[3,128,512]{2,1,0:T(8,128)(2,1)S(1)}, bf16[3,128,512]{2,1,0:T(8,128)(2,1)S(1)}, u32[]{:S(2)}, u32[]{:S(2)}) %collective-permute-start.17) | collective-permute-done | bytes 393248 | tf_op jit(solution)/shard_map/ppermute | solution.py:637
  56.2 2.1 sum_step.9
  58.2 3.1 collective-permute-start.19
  61.4 11.6 %collective-permute-done.11.refs_7_ = bf16[3,256,512]{2,1,0:T(8,128)(2,1)S(1)} collective-permute-done((bf16[3,256,512]{2,1,0:T(8,128)(2,1)S(1)}, bf16[3,256,512]{2,1,0:T(8,128)(2,1)S(1)}, u32[]{:S(2)}, u32[]{:S(2)}) %collective-permute-start.11) | collective-permute-done | bytes 786464 | tf_op jit(solution)/shard_map/ppermute | solution.py:637
  73.5 2.1 sum_step.7
  75.6 2.7 collective-permute-start.13
  78.2 11.6 %collective-permute-done.19.refs_7_ = bf16[3,256,512]{2,1,0:T(8,128)(2,1)S(1)} collective-permute-done((bf16[3,256,512]{2,1,0:T(8,128)(2,1)S(1)}, bf16[3,256,512]{2,1,0:T(8,128)(2,1)S(1)}, u32[]{:S(2)}, u32[]{:S(2)}) %collective-permute-start.19) | collective-permute-done | bytes 786464 | tf_op jit(solution)/shard_map/ppermute | solution.py:637
  90.3 2.1 sum_step.10
  92.4 2.7 collective-permute-start.21
  96.3 10.4 %collective-permute-done.13.refs_7_ = bf16[3,256,512]{2,1,0:T(8,128)(2,1)S(1)} collective-permute-done((bf16[3,256,512]{2,1,0:T(8,128)(2,1)S(1)}, bf16[3,256,512]{2,1,0:T(8,128)(2,1)S(1)}, u32[]{:S(2)}, u32[]{:S(2)}) %collective-permute-start.13) | collective-permute-done | bytes 786464 | tf_op jit(solution)/shard_map/ppermute | solution.py:637
  107.2 2.1 sum_step.8
  109.3 2.7 collective-permute-start.15
  112.0 11.6 %collective-permute-done.21.refs_7_ = bf16[3,256,512]{2,1,0:T(8,128)(2,1)S(1)} collective-permute-done((bf16[3,256,512]{2,1,0:T(8,128)(2,1)S(1)}, bf16[3,256,512]{2,1,0:T(8,128)(2,1)S(1)}, u32[]{:S(2)}, u32[]{:S(2)}) %collective-permute-start.21) | collective-permute-done | bytes 786464 | tf_op jit(solution)/shard_map/ppermute | solution.py:637
  124.1 2.1 sum_step.11
  126.1 2.7 collective-permute-start.23
  129.5 10.9 %collective-permute-done.15.from_left = bf16[3,256,512]{2,1,0:T(8,128)(2,1)S(1)} collective-permute-done((bf16[3,256,512]{2,1,0:T(8,128)(2,1)S(1)}, bf16[3,256,512]{2,1,0:T(8,128)(2,1)S(1)}, u32[]{:S(2)}, u32[]{:S(2)}) %collective-permute-start.15) | collective-permute-done | bytes 786464 | tf_op jit(solution)/shard_map/ppermute | solution.py:637
  140.9 7.2 %attention.2 = (bf16[256,512]{1,0:T(8,128)(2,1)S(1)}, f32[256,128]{1,0:T(8,128)S(1)}, bf16[3,256,512]{2,1,0:T(8,128)(2,1)S(1)}) custom-call(s32[39]{0:T(128)S(1)} %dynamic-slice_bitcast_fusion.idx.refs_0_, bf16[7,256,256]{2,1,0:T(8,128)(2,1)S(1)} %stack.1.refs_1_.refs_3_.mine, bf16[7,256,256]{2,1,0:T(8,128)(2,1)S(1)} %collective-permute-done.8.refs_2_.refs_4_.other, ...), custom_call_target="tpu_custom_call" | custom-call | flops 402653184 | bytes 3145728 | tf_op jit(solution)/shard_map/attention/pallas_call | solution.py:394
  148.7 2.6 collective-permute-start.27
  151.4 5.9 %collective-permute-done.23.from_left = bf16[3,256,512]{2,1,0:T(8,128)(2,1)S(1)} collective-permute-done((bf16[3,256,512]{2,1,0:T(8,128)(2,1)S(1)}, bf16[3,256,512]{2,1,0:T(8,128)(2,1)S(1)}, u32[]{:S(2)}, u32[]{:S(2)}) %collective-permute-start.23) | collective-permute-done | bytes 786464 | tf_op jit(solution)/shard_map/ppermute | solution.py:637
  157.8 7.2 %attention.3 = (bf16[256,512]{1,0:T(8,128)(2,1)S(1)}, f32[256,128]{1,0:T(8,128)S(1)}, bf16[3,256,512]{2,1,0:T(8,128)(2,1)S(1)}) custom-call(s32[39]{0:T(128)S(1)} %dynamic-slice_bitcast_fusion.idx.refs_0_, bf16[7,256,256]{2,1,0:T(8,128)(2,1)S(1)} %stack.1.refs_1_.refs_3_.mine, bf16[7,256,256]{2,1,0:T(8,128)(2,1)S(1)} %collective-permute-done.8.refs_2_.refs_4_.other, ...), custom_call_target="tpu_custom_call" | custom-call | flops 402653184 | bytes 3145728 | tf_op jit(solution)/shard_map/attention/pallas_call | solution.py:394
  166.4 2.6 collective-permute-start.35
  170.0 4.2 %collective-permute-done.27.refs_1_.refs_2_ = bf16[3,256,512]{2,1,0:T(8,128)(2,1)S(1)} collective-permute-done((bf16[3,256,512]{2,1,0:T(8,128)(2,1)S(1)}, bf16[3,256,512]{2,1,0:T(8,128)(2,1)S(1)}, u32[]{:S(2)}, u32[]{:S(2)}) %collective-permute-start.27) | collective-permute-done | bytes 786464 | tf_op jit(solution)/shard_map/ppermute | solution.py:637
  175.5 1.6 collective-permute-start.31
  178.0 13.0 %collective-permute-done.35.refs_1_.refs_2_ = bf16[3,256,512]{2,1,0:T(8,128)(2,1)S(1)} collective-permute-done((bf16[3,256,512]{2,1,0:T(8,128)(2,1)S(1)}, bf16[3,256,512]{2,1,0:T(8,128)(2,1)S(1)}, u32[]{:S(2)}, u32[]{:S(2)}) %collective-permute-start.35) | collective-permute-done | bytes 786464 | tf_op jit(solution)/shard_map/ppermute | solution.py:637
  192.3 1.6 collective-permute-start.39
  194.8 13.2 %collective-permute-done.28.refs_0_.refs_4_ = bf16[3,256,512]{2,1,0:T(8,128)(2,1)} collective-permute-done((bf16[3,256,512]{2,1,0:T(8,128)(2,1)S(1)}, bf16[3,256,512]{2,1,0:T(8,128)(2,1)}, u32[]{:S(2)}, u32[]{:S(2)}) %collective-permute-start.28) | collective-permute-done | bytes 786464 | tf_op jit(solution)/shard_map/ppermute | solution.py:637
  208.4 1.6 collective-permute-start.32
  210.0 14.8 %collective-permute-done.36.refs_0_.refs_4_ = bf16[3,256,512]{2,1,0:T(8,128)(2,1)} collective-permute-done((bf16[3,256,512]{2,1,0:T(8,128)(2,1)S(1)}, bf16[3,256,512]{2,1,0:T(8,128)(2,1)}, u32[]{:S(2)}, u32[]{:S(2)}) %collective-permute-start.36) | collective-permute-done | bytes 786464 | tf_op jit(solution)/shard_map/ppermute | solution.py:637
  225.3 1.6 collective-permute-start.40
  226.9 1.6 reduce_sum.18
  228.4 1.6 reduce_sum.19
  232.6 1.6 collective-permute-done.25
  235.7 5.0 %collective-permute-done.26 = f32[256,1]{1,0:T(8,128)S(1)} collective-permute-done((f32[256,1]{1,0:T(8,128)S(1)}, f32[256,1]{1,0:T(8,128)S(1)}, u32[]{:S(2)}, u32[]{:S(2)}) %collective-permute-start.26) | collective-permute-done | bytes 1056 | tf_op jit(solution)/shard_map/ppermute | solution.py:640
  245.5 1.4 halve.2
  250.6 2.3 term_step.10
  253.0 2.3 term_step.11
  255.3 3.2 %collective-permute-done.37.refs_0_.refs_6_ = bf16[3,256,512]{2,1,0:T(8,128)(2,1)} collective-permute-done((bf16[3,256,512]{2,1,0:T(8,128)(2,1)}, bf16[3,256,512]{2,1,0:T(8,128)(2,1)}, u32[]{:S(2)}, u32[]{:S(2)}) %collective-permute-start.37) | collective-permute-done | bytes 786464 | tf_op jit(solution)/shard_map/ppermute | solution.py:637
  260.4 2.7 collective-permute-start.41
  263.1 2.3 term_step.12
  265.5 2.4 term_step.13
  269.9 6.3 %grads.2 = (f32[3,512,1024]{2,1,0:T(8,128)}, f32[8,128]{1,0:T(8,128)S(1)}) custom-call(bf16[512,2048]{1,0:T(8,128)(2,1)S(1)} %copy-done.1, bf16[3,256,512]{2,1,0:T(8,128)(2,1)S(1)} %copy-done.14, bf16[3,256,512]{2,1,0:T(8,128)(2,1)S(1)} %copy-done.17, bf16[3,256,512]{2,1,0:T(8,128)(2,1)S(1)} %copy-done.20, ...), custom_call_target="tpu_custom_call" | custom-call | flops 3221225472 | bytes 9437184 | tf_op jit(solution)/shard_map/grads/pallas_call | solution.py:438
  276.2 1.6 term_last.1
  281.7 1.6 collective-permute-start.44
  283.2 6.3 %grads.3 = (f32[3,512,1024]{2,1,0:T(8,128)}, f32[8,128]{1,0:T(8,128)S(1)}) custom-call(bf16[512,2048]{1,0:T(8,128)(2,1)S(1)} %copy-done.1, bf16[3,256,512]{2,1,0:T(8,128)(2,1)S(1)} %copy-done.6, bf16[3,256,512]{2,1,0:T(8,128)(2,1)S(1)} %copy-done.8, bf16[3,256,512]{2,1,0:T(8,128)(2,1)S(1)} %copy-done.10, ...), custom_call_target="tpu_custom_call", output_to_operand_aliasing={{0}: (10, {})} | custom-call | flops 3221225472 | bytes 9437184 | tf_op jit(solution)/shard_map/grads/pallas_call | solution.py:438
  289.6 4.8 %collective-permute-done.44.refs_2_ = bf16[2,128,512]{2,1,0:T(8,128)(2,1)S(1)} collective-permute-done((bf16[2,128,512]{2,1,0:T(8,128)(2,1)S(1)}, bf16[2,128,512]{2,1,0:T(8,128)(2,1)S(1)}, u32[]{:S(2)}, u32[]{:S(2)}) %collective-permute-start.44) | collective-permute-done | bytes 262176 | tf_op jit(solution)/shard_map/ppermute | solution.py:640
  295.1 3.9 %collective-permute-start.47 = (bf16[256,512]{1,0:T(8,128)(2,1)S(1)}, bf16[256,512]{1,0:T(8,128)(2,1)S(1)}, u32[]{:S(2)}, u32[]{:S(2)}) collective-permute-start(bf16[256,512]{1,0:T(8,128)(2,1)S(1)} %get-tuple-element.134), channel_id=1, source_target_pairs={{0,0},{1,1},{2,8},{3,9},{4,16},{5,17},{6,24},{7,25},{8,4},{9,5},{1... | collective-permute-start | bytes 786440 | tf_op jit(solution)/shard_map/ppermute | solution.py:698
  300.3 8.2 %collective-permute-done.47.refs_0_ = bf16[256,512]{1,0:T(8,128)(2,1)S(1)} collective-permute-done((bf16[256,512]{1,0:T(8,128)(2,1)S(1)}, bf16[256,512]{1,0:T(8,128)(2,1)S(1)}, u32[]{:S(2)}, u32[]{:S(2)}) %collective-permute-start.47) | collective-permute-done | bytes 262176 | tf_op jit(solution)/shard_map/ppermute | solution.py:698
  308.5 5.6 %collective-permute-done.48.refs_1_ = bf16[256,512]{1,0:T(8,128)(2,1)S(1)} collective-permute-done((bf16[256,512]{1,0:T(8,128)(2,1)S(1)}, bf16[256,512]{1,0:T(8,128)(2,1)S(1)}, u32[]{:S(2)}, u32[]{:S(2)}) %collective-permute-start.48) | collective-permute-done | bytes 262176 | tf_op jit(solution)/shard_map/ppermute | solution.py:698
  314.0 1.7 finish.1
  (132 shorter events, 41.4 us)
Async XLA Ops:
  3.6 154.1 %copy-start.25 = (s32[39]{0:T(128)}, s32[39]{0:T(128)S(1)}, u32[]{:S(2)}) copy-start(s32[39]{0:T(128)S(1)} %dynamic-slice_bitcast_fusion.idx.refs_0_) | copy-start | bytes 472
  5.1 9.1 %collective-permute-start.6 = (bf16[256,256]{1,0:T(8,128)(2,1)S(1)}, bf16[256,256]{1,0:T(8,128)(2,1)S(1)}, u32[]{:S(2)}, u32[]{:S(2)}) collective-permute-start(bf16[256,256]{1,0:T(8,128)(2,1)S(1)} %get-tuple-element.77), channel_id=1, source_target_pairs={{0,7},{2,5},{4,3},{6,1},{7,0},{5,2},{3,4},{1,6},{8,15},{10,13},{12... | collective-permute-start | bytes 393224 | tf_op jit(solution)/shard_map/ppermute | solution.py:637
  9.7 9.7 %collective-permute-start = (bf16[256,256]{1,0:T(8,128)(2,1)S(1)}, bf16[256,256]{1,0:T(8,128)(2,1)S(1)}, u32[]{:S(2)}, u32[]{:S(2)}) collective-permute-start(bf16[256,256]{1,0:T(8,128)(2,1)S(1)} %get-tuple-element.71), channel_id=1, source_target_pairs={{0,2},{2,4},{4,6},{6,7},{7,5},{5,3},{3,1},{1,0},{8,10},{10,12},{12... | collective-permute-start | bytes 393224 | tf_op jit(solution)/shard_map/ppermute | solution.py:637
  14.2 6.9 %collective-permute-start.7 = (bf16[256,256]{1,0:T(8,128)(2,1)S(1)}, bf16[256,256]{1,0:T(8,128)(2,1)S(1)}, u32[]{:S(2)}, u32[]{:S(2)}) collective-permute-start(bf16[256,256]{1,0:T(8,128)(2,1)S(1)} %collective-permute-done.6.mine.mine_far), channel_id=1, source_target_pairs={{0,8},{8,0},{16,24},{24,16},{1,9},{9,1},{17,25},{25,17},{2,10},{10... | collective-permute-start | bytes 393224 | tf_op jit(solution)/shard_map/ppermute | solution.py:640
  14.2 14.6 %collective-permute-start.1 = (bf16[256,256]{1,0:T(8,128)(2,1)S(1)}, bf16[256,256]{1,0:T(8,128)(2,1)S(1)}, u32[]{:S(2)}, u32[]{:S(2)}) collective-permute-start(bf16[256,256]{1,0:T(8,128)(2,1)S(1)} %get-tuple-element.72), channel_id=1, source_target_pairs={{0,1},{2,0},{4,2},{6,4},{7,6},{5,7},{3,5},{1,3},{8,9},{10,8},{12,1... | collective-permute-start | bytes 393224 | tf_op jit(solution)/shard_map/ppermute | solution.py:637
  14.7 14.1 %collective-permute-start.2 = (bf16[256,256]{1,0:T(8,128)(2,1)S(1)}, bf16[256,256]{1,0:T(8,128)(2,1)S(1)}, u32[]{:S(2)}, u32[]{:S(2)}) collective-permute-start(bf16[256,256]{1,0:T(8,128)(2,1)S(1)} %get-tuple-element.73), channel_id=1, source_target_pairs={{0,4},{2,6},{4,7},{6,5},{7,3},{5,1},{3,0},{1,2},{8,12},{10,14},{12... | collective-permute-start | bytes 393224 | tf_op jit(solution)/shard_map/ppermute | solution.py:637
  18.1 15.3 %collective-permute-start.3 = (bf16[256,256]{1,0:T(8,128)(2,1)S(1)}, bf16[256,256]{1,0:T(8,128)(2,1)S(1)}, u32[]{:S(2)}, u32[]{:S(2)}) collective-permute-start(bf16[256,256]{1,0:T(8,128)(2,1)S(1)} %get-tuple-element.74), channel_id=1, source_target_pairs={{0,3},{2,1},{4,0},{6,2},{7,4},{5,6},{3,7},{1,5},{8,11},{10,9},{12,... | collective-permute-start | bytes 393224 | tf_op jit(solution)/shard_map/ppermute | solution.py:637
  19.4 15.2 %collective-permute-start.4 = (bf16[256,256]{1,0:T(8,128)(2,1)S(1)}, bf16[256,256]{1,0:T(8,128)(2,1)S(1)}, u32[]{:S(2)}, u32[]{:S(2)}) collective-permute-start(bf16[256,256]{1,0:T(8,128)(2,1)S(1)} %get-tuple-element.75), channel_id=1, source_target_pairs={{0,6},{2,7},{4,5},{6,3},{7,1},{5,0},{3,2},{1,4},{8,14},{10,15},{12... | collective-permute-start | bytes 393224 | tf_op jit(solution)/shard_map/ppermute | solution.py:637
  21.1 13.4 %collective-permute-start.5 = (bf16[256,256]{1,0:T(8,128)(2,1)S(1)}, bf16[256,256]{1,0:T(8,128)(2,1)S(1)}, u32[]{:S(2)}, u32[]{:S(2)}) collective-permute-start(bf16[256,256]{1,0:T(8,128)(2,1)S(1)} %get-tuple-element.76), channel_id=1, source_target_pairs={{0,5},{2,3},{4,1},{6,0},{7,2},{5,4},{3,6},{1,7},{8,13},{10,11},{12... | collective-permute-start | bytes 393224 | tf_op jit(solution)/shard_map/ppermute | solution.py:637
  23.2 1.9 copy-start.4
  34.6 13.2 %collective-permute-start.8 = (bf16[7,256,256]{2,1,0:T(8,128)(2,1)S(1)}, bf16[7,256,256]{2,1,0:T(8,128)(2,1)S(1)}, u32[]{:S(2)}, u32[]{:S(2)}) collective-permute-start(bf16[7,256,256]{2,1,0:T(8,128)(2,1)S(1)} %stack.1.refs_1_.refs_3_.mine), channel_id=1, source_target_pairs={{0,8},{8,0},{16,24},{24,16},{1,9},{9,1},{17,25},{25,17},{2,10},{10... | collective-permute-start | bytes 2752520 | tf_op jit(solution)/shard_map/ppermute | solution.py:640
  34.7 13.1 %collective-permute-start.9 = (bf16[3,128,512]{2,1,0:T(8,128)(2,1)S(1)}, bf16[3,128,512]{2,1,0:T(8,128)(2,1)S(1)}, u32[]{:S(2)}, u32[]{:S(2)}) collective-permute-start(bf16[3,128,512]{2,1,0:T(8,128)(2,1)S(1)} %get-tuple-element.79.refs_7_), channel_id=1, source_target_pairs={{0,2},{2,4},{4,6},{6,7},{7,5},{5,3},{3,1},{1,0},{8,10},{10,12},{12... | collective-permute-start | bytes 1179656 | tf_op jit(solution)/shard_map/ppermute | solution.py:637
  34.7 13.0 %collective-permute-start.10 = (bf16[3,128,512]{2,1,0:T(8,128)(2,1)S(1)}, bf16[3,128,512]{2,1,0:T(8,128)(2,1)S(1)}, u32[]{:S(2)}, u32[]{:S(2)}) collective-permute-start(bf16[3,128,512]{2,1,0:T(8,128)(2,1)S(1)} %get-tuple-element.80), channel_id=1, source_target_pairs={{0,1},{2,0},{4,2},{6,4},{7,6},{5,7},{3,5},{1,3},{8,9},{10,8},{12,1... | collective-permute-start | bytes 1179656 | tf_op jit(solution)/shard_map/ppermute | solution.py:637
  37.9 18.3 %collective-permute-start.17 = (bf16[3,128,512]{2,1,0:T(8,128)(2,1)S(1)}, bf16[3,128,512]{2,1,0:T(8,128)(2,1)S(1)}, u32[]{:S(2)}, u32[]{:S(2)}) collective-permute-start(bf16[3,128,512]{2,1,0:T(8,128)(2,1)S(1)} %get-tuple-element.88), channel_id=1, source_target_pairs={{0,2},{2,4},{4,6},{6,7},{7,5},{5,3},{3,1},{1,0},{8,10},{10,12},{12... | collective-permute-start | bytes 1179656 | tf_op jit(solution)/shard_map/ppermute | solution.py:637
  37.9 18.3 %collective-permute-start.18 = (bf16[3,128,512]{2,1,0:T(8,128)(2,1)S(1)}, bf16[3,128,512]{2,1,0:T(8,128)(2,1)S(1)}, u32[]{:S(2)}, u32[]{:S(2)}) collective-permute-start(bf16[3,128,512]{2,1,0:T(8,128)(2,1)S(1)} %get-tuple-element.89), channel_id=1, source_target_pairs={{0,1},{2,0},{4,2},{6,4},{7,6},{5,7},{3,5},{1,3},{8,9},{10,8},{12,1... | collective-permute-start | bytes 1179656 | tf_op jit(solution)/shard_map/ppermute | solution.py:637
  49.8 23.2 %collective-permute-start.11 = (bf16[3,256,512]{2,1,0:T(8,128)(2,1)S(1)}, bf16[3,256,512]{2,1,0:T(8,128)(2,1)S(1)}, u32[]{:S(2)}, u32[]{:S(2)}) collective-permute-start(bf16[3,256,512]{2,1,0:T(8,128)(2,1)S(1)} %get-tuple-element.81), channel_id=1, source_target_pairs={{0,2},{2,4},{4,6},{6,7},{7,5},{5,3},{3,1},{1,0},{8,10},{10,12},{12... | collective-permute-start | bytes 2359304 | tf_op jit(solution)/shard_map/ppermute | solution.py:637
  53.0 20.5 %collective-permute-start.12 = (bf16[3,256,512]{2,1,0:T(8,128)(2,1)S(1)}, bf16[3,256,512]{2,1,0:T(8,128)(2,1)S(1)}, u32[]{:S(2)}, u32[]{:S(2)}) collective-permute-start(bf16[3,256,512]{2,1,0:T(8,128)(2,1)S(1)} %get-tuple-element.82), channel_id=1, source_target_pairs={{0,1},{2,0},{4,2},{6,4},{7,6},{5,7},{3,5},{1,3},{8,9},{10,8},{12,1... | collective-permute-start | bytes 2359304 | tf_op jit(solution)/shard_map/ppermute | solution.py:637
  58.2 31.6 %collective-permute-start.19 = (bf16[3,256,512]{2,1,0:T(8,128)(2,1)S(1)}, bf16[3,256,512]{2,1,0:T(8,128)(2,1)S(1)}, u32[]{:S(2)}, u32[]{:S(2)}) collective-permute-start(bf16[3,256,512]{2,1,0:T(8,128)(2,1)S(1)} %get-tuple-element.90), channel_id=1, source_target_pairs={{0,2},{2,4},{4,6},{6,7},{7,5},{5,3},{3,1},{1,0},{8,10},{10,12},{12... | collective-permute-start | bytes 2359304 | tf_op jit(solution)/shard_map/ppermute | solution.py:637
  61.4 29.0 %collective-permute-start.20 = (bf16[3,256,512]{2,1,0:T(8,128)(2,1)S(1)}, bf16[3,256,512]{2,1,0:T(8,128)(2,1)S(1)}, u32[]{:S(2)}, u32[]{:S(2)}) collective-permute-start(bf16[3,256,512]{2,1,0:T(8,128)(2,1)S(1)} %get-tuple-element.91), channel_id=1, source_target_pairs={{0,1},{2,0},{4,2},{6,4},{7,6},{5,7},{3,5},{1,3},{8,9},{10,8},{12,1... | collective-permute-start | bytes 2359304 | tf_op jit(solution)/shard_map/ppermute | solution.py:637
  75.6 31.2 %collective-permute-start.13 = (bf16[3,256,512]{2,1,0:T(8,128)(2,1)S(1)}, bf16[3,256,512]{2,1,0:T(8,128)(2,1)S(1)}, u32[]{:S(2)}, u32[]{:S(2)}) collective-permute-start(bf16[3,256,512]{2,1,0:T(8,128)(2,1)S(1)} %get-tuple-element.83), channel_id=1, source_target_pairs={{0,2},{2,4},{4,6},{6,7},{7,5},{5,3},{3,1},{1,0},{8,10},{10,12},{12... | collective-permute-start | bytes 2359304 | tf_op jit(solution)/shard_map/ppermute | solution.py:637
  78.2 29.0 %collective-permute-start.14 = (bf16[3,256,512]{2,1,0:T(8,128)(2,1)S(1)}, bf16[3,256,512]{2,1,0:T(8,128)(2,1)S(1)}, u32[]{:S(2)}, u32[]{:S(2)}) collective-permute-start(bf16[3,256,512]{2,1,0:T(8,128)(2,1)S(1)} %get-tuple-element.84), channel_id=1, source_target_pairs={{0,1},{2,0},{4,2},{6,4},{7,6},{5,7},{3,5},{1,3},{8,9},{10,8},{12,1... | collective-permute-start | bytes 2359304 | tf_op jit(solution)/shard_map/ppermute | solution.py:637
  92.4 31.2 %collective-permute-start.21 = (bf16[3,256,512]{2,1,0:T(8,128)(2,1)S(1)}, bf16[3,256,512]{2,1,0:T(8,128)(2,1)S(1)}, u32[]{:S(2)}, u32[]{:S(2)}) collective-permute-start(bf16[3,256,512]{2,1,0:T(8,128)(2,1)S(1)} %get-tuple-element.92), channel_id=1, source_target_pairs={{0,2},{2,4},{4,6},{6,7},{7,5},{5,3},{3,1},{1,0},{8,10},{10,12},{12... | collective-permute-start | bytes 2359304 | tf_op jit(solution)/shard_map/ppermute | solution.py:637
  95.1 29.0 %collective-permute-start.22 = (bf16[3,256,512]{2,1,0:T(8,128)(2,1)S(1)}, bf16[3,256,512]{2,1,0:T(8,128)(2,1)S(1)}, u32[]{:S(2)}, u32[]{:S(2)}) collective-permute-start(bf16[3,256,512]{2,1,0:T(8,128)(2,1)S(1)} %get-tuple-element.93), channel_id=1, source_target_pairs={{0,1},{2,0},{4,2},{6,4},{7,6},{5,7},{3,5},{1,3},{8,9},{10,8},{12,1... | collective-permute-start | bytes 2359304 | tf_op jit(solution)/shard_map/ppermute | solution.py:637
  96.3 27.8 %copy-start = (bf16[512,2048]{1,0:T(8,128)(2,1)}, bf16[512,2048]{1,0:T(8,128)(2,1)S(1)}, u32[]{:S(2)}) copy-start(bf16[512,2048]{1,0:T(8,128)(2,1)S(1)} %turn.1.refs_9_.refs_0_) | copy-start | bytes 6291460
  109.3 31.2 %collective-permute-start.15 = (bf16[3,256,512]{2,1,0:T(8,128)(2,1)S(1)}, bf16[3,256,512]{2,1,0:T(8,128)(2,1)S(1)}, u32[]{:S(2)}, u32[]{:S(2)}) collective-permute-start(bf16[3,256,512]{2,1,0:T(8,128)(2,1)S(1)} %get-tuple-element.85), channel_id=1, source_target_pairs={{0,2},{2,4},{4,6},{6,7},{7,5},{5,3},{3,1},{1,0},{8,10},{10,12},{12... | collective-permute-start | bytes 2359304 | tf_op jit(solution)/shard_map/ppermute | solution.py:637
  111.9 29.0 %copy-start.11 = (bf16[256,1024]{1,0:T(8,128)(2,1)S(1)}, bf16[256,1024]{1,0:T(8,128)(2,1)}, u32[]{:S(2)}) copy-start(bf16[256,1024]{1,0:T(8,128)(2,1)} %d_out.3) | copy-start | bytes 1572868
  112.0 29.0 %collective-permute-start.16 = (bf16[3,256,512]{2,1,0:T(8,128)(2,1)S(1)}, bf16[3,256,512]{2,1,0:T(8,128)(2,1)S(1)}, u32[]{:S(2)}, u32[]{:S(2)}) collective-permute-start(bf16[3,256,512]{2,1,0:T(8,128)(2,1)S(1)} %get-tuple-element.86), channel_id=1, source_target_pairs={{0,1},{2,0},{4,2},{6,4},{7,6},{5,7},{3,5},{1,3},{8,9},{10,8},{12,1... | collective-permute-start | bytes 2359304 | tf_op jit(solution)/shard_map/ppermute | solution.py:637
  126.1 31.2 %collective-permute-start.23 = (bf16[3,256,512]{2,1,0:T(8,128)(2,1)S(1)}, bf16[3,256,512]{2,1,0:T(8,128)(2,1)S(1)}, u32[]{:S(2)}, u32[]{:S(2)}) collective-permute-start(bf16[3,256,512]{2,1,0:T(8,128)(2,1)S(1)} %get-tuple-element.94), channel_id=1, source_target_pairs={{0,2},{2,4},{4,6},{6,7},{7,5},{5,3},{3,1},{1,0},{8,10},{10,12},{12... | collective-permute-start | bytes 2359304 | tf_op jit(solution)/shard_map/ppermute | solution.py:637
  128.8 29.0 %collective-permute-start.24 = (bf16[3,256,512]{2,1,0:T(8,128)(2,1)S(1)}, bf16[3,256,512]{2,1,0:T(8,128)(2,1)S(1)}, u32[]{:S(2)}, u32[]{:S(2)}) collective-permute-start(bf16[3,256,512]{2,1,0:T(8,128)(2,1)S(1)} %get-tuple-element.95), channel_id=1, source_target_pairs={{0,1},{2,0},{4,2},{6,4},{7,6},{5,7},{3,5},{1,3},{8,9},{10,8},{12,1... | collective-permute-start | bytes 2359304 | tf_op jit(solution)/shard_map/ppermute | solution.py:637
  148.7 16.3 %copy-start.12 = (bf16[3,256,512]{2,1,0:T(8,128)(2,1)}, bf16[3,256,512]{2,1,0:T(8,128)(2,1)S(1)}, u32[]{:S(2)}) copy-start(bf16[3,256,512]{2,1,0:T(8,128)(2,1)S(1)} %get-tuple-element.101.refs_0_.refs_1_) | copy-start | bytes 2359300
  148.7 25.4 %collective-permute-start.27 = (bf16[3,256,512]{2,1,0:T(8,128)(2,1)S(1)}, bf16[3,256,512]{2,1,0:T(8,128)(2,1)S(1)}, u32[]{:S(2)}, u32[]{:S(2)}) collective-permute-start(bf16[3,256,512]{2,1,0:T(8,128)(2,1)S(1)} %get-tuple-element.101.refs_0_.refs_1_), channel_id=1, source_target_pairs={{0,2},{2,4},{4,6},{6,7},{7,5},{5,3},{3,1},{1,0},{8,10},{10,12},{12... | collective-permute-start | bytes 2359304 | tf_op jit(solution)/shard_map/ppermute | solution.py:637
  151.4 24.1 %collective-permute-start.30 = (bf16[3,256,512]{2,1,0:T(8,128)(2,1)S(1)}, bf16[3,256,512]{2,1,0:T(8,128)(2,1)S(1)}, u32[]{:S(2)}, u32[]{:S(2)}) collective-permute-start(bf16[3,256,512]{2,1,0:T(8,128)(2,1)S(1)} %get-tuple-element.101.refs_0_.refs_1_), channel_id=1, source_target_pairs={{0,1},{2,0},{4,2},{6,4},{7,6},{5,7},{3,5},{1,3},{8,9},{10,8},{12,1... | collective-permute-start | bytes 2359304 | tf_op jit(solution)/shard_map/ppermute | solution.py:637
  166.4 24.6 %collective-permute-start.35 = (bf16[3,256,512]{2,1,0:T(8,128)(2,1)S(1)}, bf16[3,256,512]{2,1,0:T(8,128)(2,1)S(1)}, u32[]{:S(2)}, u32[]{:S(2)}) collective-permute-start(bf16[3,256,512]{2,1,0:T(8,128)(2,1)S(1)} %get-tuple-element.106.refs_0_.refs_1_), channel_id=1, source_target_pairs={{0,2},{2,4},{4,6},{6,7},{7,5},{5,3},{3,1},{1,0},{8,10},{10,12},{12... | collective-permute-start | bytes 2359304 | tf_op jit(solution)/shard_map/ppermute | solution.py:637
  169.0 23.3 %collective-permute-start.38 = (bf16[3,256,512]{2,1,0:T(8,128)(2,1)S(1)}, bf16[3,256,512]{2,1,0:T(8,128)(2,1)S(1)}, u32[]{:S(2)}, u32[]{:S(2)}) collective-permute-start(bf16[3,256,512]{2,1,0:T(8,128)(2,1)S(1)} %get-tuple-element.106.refs_0_.refs_1_), channel_id=1, source_target_pairs={{0,1},{2,0},{4,2},{6,4},{7,6},{5,7},{3,5},{1,3},{8,9},{10,8},{12,1... | collective-permute-start | bytes 2359304 | tf_op jit(solution)/shard_map/ppermute | solution.py:637
  174.1 33.8 %collective-permute-start.28 = (bf16[3,256,512]{2,1,0:T(8,128)(2,1)S(1)}, bf16[3,256,512]{2,1,0:T(8,128)(2,1)}, u32[]{:S(2)}, u32[]{:S(2)}) collective-permute-start(bf16[3,256,512]{2,1,0:T(8,128)(2,1)S(1)} %collective-permute-done.27.refs_1_.refs_2_), channel_id=1, source_target_pairs={{0,2},{2,4},{4,6},{6,7},{7,5},{5,3},{3,1},{1,0},{8,10},{10,12},{12... | collective-permute-start | bytes 2359304 | tf_op jit(solution)/shard_map/ppermute | solution.py:637
  175.5 33.0 %collective-permute-start.31 = (bf16[3,256,512]{2,1,0:T(8,128)(2,1)S(1)}, bf16[3,256,512]{2,1,0:T(8,128)(2,1)}, u32[]{:S(2)}, u32[]{:S(2)}) collective-permute-start(bf16[3,256,512]{2,1,0:T(8,128)(2,1)S(1)} %collective-permute-done.30.refs_2_.refs_3_), channel_id=1, source_target_pairs={{0,1},{2,0},{4,2},{6,4},{7,6},{5,7},{3,5},{1,3},{8,9},{10,8},{12,1... | collective-permute-start | bytes 2359304 | tf_op jit(solution)/shard_map/ppermute | solution.py:637
  191.0 33.8 %collective-permute-start.36 = (bf16[3,256,512]{2,1,0:T(8,128)(2,1)S(1)}, bf16[3,256,512]{2,1,0:T(8,128)(2,1)}, u32[]{:S(2)}, u32[]{:S(2)}) collective-permute-start(bf16[3,256,512]{2,1,0:T(8,128)(2,1)S(1)} %collective-permute-done.35.refs_1_.refs_2_), channel_id=1, source_target_pairs={{0,2},{2,4},{4,6},{6,7},{7,5},{5,3},{3,1},{1,0},{8,10},{10,12},{12... | collective-permute-start | bytes 2359304 | tf_op jit(solution)/shard_map/ppermute | solution.py:637
  192.3 33.0 %collective-permute-start.39 = (bf16[3,256,512]{2,1,0:T(8,128)(2,1)S(1)}, bf16[3,256,512]{2,1,0:T(8,128)(2,1)}, u32[]{:S(2)}, u32[]{:S(2)}) collective-permute-start(bf16[3,256,512]{2,1,0:T(8,128)(2,1)S(1)} %collective-permute-done.38.refs_2_.refs_3_), channel_id=1, source_target_pairs={{0,1},{2,0},{4,2},{6,4},{7,6},{5,7},{3,5},{1,3},{8,9},{10,8},{12,1... | collective-permute-start | bytes 2359304 | tf_op jit(solution)/shard_map/ppermute | solution.py:637
  208.0 37.6 %collective-permute-start.29 = (bf16[3,256,512]{2,1,0:T(8,128)(2,1)}, bf16[3,256,512]{2,1,0:T(8,128)(2,1)}, u32[]{:S(2)}, u32[]{:S(2)}) collective-permute-start(bf16[3,256,512]{2,1,0:T(8,128)(2,1)} %collective-permute-done.28.refs_0_.refs_4_), channel_id=1, source_target_pairs={{0,2},{2,4},{4,6},{6,7},{7,5},{5,3},{3,1},{1,0},{8,10},{10,12},{12... | collective-permute-start | bytes 2359304 | tf_op jit(solution)/shard_map/ppermute | solution.py:637
  208.4 37.1 %collective-permute-start.32 = (bf16[3,256,512]{2,1,0:T(8,128)(2,1)}, bf16[3,256,512]{2,1,0:T(8,128)(2,1)}, u32[]{:S(2)}, u32[]{:S(2)}) collective-permute-start(bf16[3,256,512]{2,1,0:T(8,128)(2,1)} %collective-permute-done.31.refs_1_.refs_5_), channel_id=1, source_target_pairs={{0,1},{2,0},{4,2},{6,4},{7,6},{5,7},{3,5},{1,3},{8,9},{10,8},{12,1... | collective-permute-start | bytes 2359304 | tf_op jit(solution)/shard_map/ppermute | solution.py:637
  224.8 33.7 %collective-permute-start.37 = (bf16[3,256,512]{2,1,0:T(8,128)(2,1)}, bf16[3,256,512]{2,1,0:T(8,128)(2,1)}, u32[]{:S(2)}, u32[]{:S(2)}) collective-permute-start(bf16[3,256,512]{2,1,0:T(8,128)(2,1)} %collective-permute-done.36.refs_0_.refs_4_), channel_id=1, source_target_pairs={{0,2},{2,4},{4,6},{6,7},{7,5},{5,3},{3,1},{1,0},{8,10},{10,12},{12... | collective-permute-start | bytes 2359304 | tf_op jit(solution)/shard_map/ppermute | solution.py:637
  225.3 33.7 %collective-permute-start.40 = (bf16[3,256,512]{2,1,0:T(8,128)(2,1)}, bf16[3,256,512]{2,1,0:T(8,128)(2,1)}, u32[]{:S(2)}, u32[]{:S(2)}) collective-permute-start(bf16[3,256,512]{2,1,0:T(8,128)(2,1)} %collective-permute-done.39.refs_1_.refs_5_), channel_id=1, source_target_pairs={{0,1},{2,0},{4,2},{6,4},{7,6},{5,7},{3,5},{1,3},{8,9},{10,8},{12,1... | collective-permute-start | bytes 2359304 | tf_op jit(solution)/shard_map/ppermute | solution.py:637
  232.6 1.6 collective-permute-start.25
  235.1 5.6 %collective-permute-start.26 = (f32[256,1]{1,0:T(8,128)S(1)}, f32[256,1]{1,0:T(8,128)S(1)}, u32[]{:S(2)}, u32[]{:S(2)}) collective-permute-start(f32[256,1]{1,0:T(8,128)S(1)} %add.31), channel_id=1, source_target_pairs={{0,16},{8,24},{16,0},{24,8},{1,17},{9,25},{17,1},{25,9},{2,18},{10... | collective-permute-start | bytes 3080 | tf_op jit(solution)/shard_map/ppermute | solution.py:640
  244.1 5.1 %copy-start.6 = (bf16[3,256,512]{2,1,0:T(8,128)(2,1)S(1)}, bf16[3,256,512]{2,1,0:T(8,128)(2,1)}, u32[]{:S(2)}) copy-start(bf16[3,256,512]{2,1,0:T(8,128)(2,1)} %copy-done.5) | copy-start | bytes 2359300
  244.1 5.1 %copy-start.8 = (bf16[3,256,512]{2,1,0:T(8,128)(2,1)S(1)}, bf16[3,256,512]{2,1,0:T(8,128)(2,1)}, u32[]{:S(2)}) copy-start(bf16[3,256,512]{2,1,0:T(8,128)(2,1)} %copy-done.7) | copy-start | bytes 2359300
  244.1 5.1 %copy-start.10 = (bf16[3,256,512]{2,1,0:T(8,128)(2,1)S(1)}, bf16[3,256,512]{2,1,0:T(8,128)(2,1)}, u32[]{:S(2)}) copy-start(bf16[3,256,512]{2,1,0:T(8,128)(2,1)} %copy-done.9) | copy-start | bytes 2359300
  247.0 20.9 %collective-permute-start.33 = (bf16[3,128,512]{2,1,0:T(8,128)(2,1)S(1)}, bf16[3,128,512]{2,1,0:T(8,128)(2,1)S(1)}, u32[]{:S(2)}, u32[]{:S(2)}) collective-permute-start(bf16[3,128,512]{2,1,0:T(8,128)(2,1)S(1)} %get-tuple-element.102), channel_id=1, source_target_pairs={{0,2},{2,4},{4,6},{6,7},{7,5},{5,3},{3,1},{1,0},{8,10},{10,12},{12... | collective-permute-start | bytes 1179656 | tf_op jit(solution)/shard_map/ppermute | solution.py:637
  248.3 19.7 %collective-permute-start.34 = (bf16[3,128,512]{2,1,0:T(8,128)(2,1)S(1)}, bf16[3,128,512]{2,1,0:T(8,128)(2,1)S(1)}, u32[]{:S(2)}, u32[]{:S(2)}) collective-permute-start(bf16[3,128,512]{2,1,0:T(8,128)(2,1)S(1)} %get-tuple-element.103), channel_id=1, source_target_pairs={{0,1},{2,0},{4,2},{6,4},{7,6},{5,7},{3,5},{1,3},{8,9},{10,8},{12,1... | collective-permute-start | bytes 1179656 | tf_op jit(solution)/shard_map/ppermute | solution.py:637
  260.4 15.7 %collective-permute-start.41 = (bf16[3,128,512]{2,1,0:T(8,128)(2,1)S(1)}, bf16[3,128,512]{2,1,0:T(8,128)(2,1)S(1)}, u32[]{:S(2)}, u32[]{:S(2)}) collective-permute-start(bf16[3,128,512]{2,1,0:T(8,128)(2,1)S(1)} %get-tuple-element.117), channel_id=1, source_target_pairs={{0,2},{2,4},{4,6},{6,7},{7,5},{5,3},{3,1},{1,0},{8,10},{10,12},{12... | collective-permute-start | bytes 1179656 | tf_op jit(solution)/shard_map/ppermute | solution.py:637
  263.1 13.0 %collective-permute-start.42 = (bf16[3,128,512]{2,1,0:T(8,128)(2,1)S(1)}, bf16[3,128,512]{2,1,0:T(8,128)(2,1)S(1)}, u32[]{:S(2)}, u32[]{:S(2)}) collective-permute-start(bf16[3,128,512]{2,1,0:T(8,128)(2,1)S(1)} %get-tuple-element.118), channel_id=1, source_target_pairs={{0,1},{2,0},{4,2},{6,4},{7,6},{5,7},{3,5},{1,3},{8,9},{10,8},{12,1... | collective-permute-start | bytes 1179656 | tf_op jit(solution)/shard_map/ppermute | solution.py:637
  265.4 3.1 copy-start.20
  267.9 1.6 copy-start.1
  267.9 1.8 copy-start.14
  267.9 2.0 copy-start.17
  269.9 6.3 %copy-start.26 = (s32[39]{0:T(128)S(1)}, s32[39]{0:T(128)}, u32[]{:S(2)}) copy-start(s32[39]{0:T(128)} %copy-done.25) | copy-start | bytes 472
  277.8 2.0 collective-permute-start.45
  277.9 3.1 collective-permute-start.43
  280.4 9.2 %collective-permute-start.46 = (bf16[2,128,512]{2,1,0:T(8,128)(2,1)S(1)}, bf16[2,128,512]{2,1,0:T(8,128)(2,1)S(1)}, u32[]{:S(2)}, u32[]{:S(2)}) collective-permute-start(bf16[2,128,512]{2,1,0:T(8,128)(2,1)S(1)} %get-tuple-element.131), channel_id=1, source_target_pairs={{0,16},{8,24},{16,0},{24,8},{1,17},{9,25},{17,1},{25,9},{2,18},{10... | collective-permute-start | bytes 786440 | tf_op jit(solution)/shard_map/ppermute | solution.py:640
  281.7 12.8 %collective-permute-start.44 = (bf16[2,128,512]{2,1,0:T(8,128)(2,1)S(1)}, bf16[2,128,512]{2,1,0:T(8,128)(2,1)S(1)}, u32[]{:S(2)}, u32[]{:S(2)}) collective-permute-start(bf16[2,128,512]{2,1,0:T(8,128)(2,1)S(1)} %get-tuple-element.127), channel_id=1, source_target_pairs={{0,16},{8,24},{16,0},{24,8},{1,17},{9,25},{17,1},{25,9},{2,18},{10... | collective-permute-start | bytes 786440 | tf_op jit(solution)/shard_map/ppermute | solution.py:640
  283.2 16.2 %copy-start.22 = (bf16[256,512]{1,0:T(8,128)(2,1)S(1)}, bf16[256,512]{1,0:T(8,128)(2,1)}, u32[]{:S(2)}) copy-start(bf16[256,512]{1,0:T(8,128)(2,1)} %copy-done.21) | copy-start | bytes 786436
  289.5 24.5 %copy-start.3 = (bf16[256,4096]{1,0:T(8,128)(2,1)S(1)}, bf16[256,4096]{1,0:T(8,128)(2,1)}, u32[]{:S(2)}) copy-start(bf16[256,4096]{1,0:T(8,128)(2,1)} %tokens.3) | copy-start | bytes 6291460
  295.1 13.4 %collective-permute-start.47 = (bf16[256,512]{1,0:T(8,128)(2,1)S(1)}, bf16[256,512]{1,0:T(8,128)(2,1)S(1)}, u32[]{:S(2)}, u32[]{:S(2)}) collective-permute-start(bf16[256,512]{1,0:T(8,128)(2,1)S(1)} %get-tuple-element.134), channel_id=1, source_target_pairs={{0,0},{1,1},{2,8},{3,9},{4,16},{5,17},{6,24},{7,25},{8,4},{9,5},{1... | collective-permute-start | bytes 786440 | tf_op jit(solution)/shard_map/ppermute | solution.py:698
  299.0 15.0 %collective-permute-start.48 = (bf16[256,512]{1,0:T(8,128)(2,1)S(1)}, bf16[256,512]{1,0:T(8,128)(2,1)S(1)}, u32[]{:S(2)}, u32[]{:S(2)}) collective-permute-start(bf16[256,512]{1,0:T(8,128)(2,1)S(1)} %get-tuple-element.135), channel_id=1, source_target_pairs={{0,1},{1,0},{2,9},{3,8},{4,17},{5,16},{6,25},{7,24},{8,5},{9,4},{1... | collective-permute-start | bytes 786440 | tf_op jit(solution)/shard_map/ppermute | solution.py:698
  (13 other events, 12.3 us)
